TPU v7x, 32 devices: a whole 2x2x4 slice. The times are simulated.
32 devices in a mesh: seg: 4 (over z), grp: 8 (over y, x, core).
Axes of the slice: x: 2, y: 2, z: 4, core: 2. Of those that a mesh axis runs over, the one named last changes fastest.
Arguments:
- frames_in: bfloat16 [32, 32, 120, 128], P(('seg', 'grp')), may hold values from -6 to 6
- spatial_weight: bfloat16 [9, 128, 128], replicated, may hold values from -0.1875 to 0.1875
- temporal_weight: bfloat16 [2, 5, 128, 128], replicated, may hold values from -0.25 to 0.25
- uniting_weight: bfloat16 [2, 128, 128], replicated, may hold values from -0.375 to 0.375
- key_index: int32 [4], replicated, may hold values from 0 to 7
- dilation: int32 [2], replicated, may hold values from 1 to 8, as said below
- cotangent: bfloat16 [32, 32, 120, 128], P(('seg', 'grp')), may hold values from -6 to 6
Outputs:
- united: bfloat16 [32, 32, 120, 128], P(('seg', 'grp'))
- grad_frames: bfloat16 [32, 32, 120, 128], P(('seg', 'grp'))
- grad_spatial: float32 [9, 128, 128], replicated
- grad_temporal: float32 [2, 5, 128, 128], replicated
- grad_uniting: float32 [2, 128, 128], replicated
Inputs may be any that keep to these rules, and one draw needn't show every extreme that they name: `key_index`: position of a segment's keyframe within its 8 frames. Exactly one layer uses dilation 8; the others use less.
All inputs are finite; a program needn't handle non-finite values.
Results may differ from a plain program's by a relative error of at most 0.0095.
Values may be sent and summed in bfloat16 or wider, within the bound.
No kernel may reach another device: no remote copies, remote signals or barrier semaphores. Data moves between devices by JAX's collectives and lax.ppermute only.
A program may use at most 128 MiB of HBM per device.

v0:
```python
import jax
import jax.numpy as jnp
from jax import lax
from jax.sharding import PartitionSpec as P

LAYERS = 2
DMAX = 8


def from_root(value, axis, root):
    mine = lax.axis_index(axis) == root
    return lax.psum(jnp.where(mine, value, jnp.zeros_like(value)), axis)


def silu_grad(value):
    sigma = jax.nn.sigmoid(value)
    return sigma * (1.0 + value * (1.0 - sigma))


def inner(left, right):
    return lax.dot_general(
        left, right, (((0,), (0,)), ((), ())), preferred_element_type=jnp.float32
    )


def spatial_forward(frames, kernel):
    count, rows, cols, chans = frames.shape
    padded = jnp.pad(frames, ((0, 0), (1, 1), (1, 1), (0, 0)))
    total = jnp.zeros((count * rows * cols, chans), jnp.float32)
    for row_tap in range(3):
        for col_tap in range(3):
            piece = padded[:, row_tap : row_tap + rows, col_tap : col_tap + cols, :].reshape(
                -1, chans
            )
            total = total + jnp.dot(
                piece, kernel[3 * row_tap + col_tap], preferred_element_type=jnp.float32
            )
    return total.reshape(frames.shape)


def spatial_back(grads, kernel):
    count, rows, cols, chans = grads.shape
    padded = jnp.pad(grads, ((0, 0), (1, 1), (1, 1), (0, 0)))
    total = jnp.zeros((count * rows * cols, chans), jnp.float32)
    for row_tap in range(3):
        for col_tap in range(3):
            piece = padded[
                :, 2 - row_tap : 2 - row_tap + rows, 2 - col_tap : 2 - col_tap + cols, :
            ].reshape(-1, chans)
            total = total + jnp.dot(
                piece, kernel[3 * row_tap + col_tap].T, preferred_element_type=jnp.float32
            )
    return total.reshape(grads.shape)


def spatial_wgrad(frames, grads):
    count, rows, cols, chans = frames.shape
    padded = jnp.pad(frames, ((0, 0), (1, 1), (1, 1), (0, 0)))
    flat_grads = grads.reshape(-1, chans)
    result = []
    for row_tap in range(3):
        for col_tap in range(3):
            piece = padded[:, row_tap : row_tap + rows, col_tap : col_tap + cols, :].reshape(
                -1, chans
            )
            result.append(inner(piece, flat_grads))
    return jnp.stack(result)


def shifted(values, offset):
    padded = jnp.pad(values, ((2 * DMAX, 2 * DMAX), (0, 0), (0, 0)))
    start = 2 * DMAX + offset
    return lax.dynamic_slice_in_dim(padded, start, values.shape[0], 0)


def temporal_forward(acts, kernel, step_size):
    chans = acts.shape[2]
    total = jnp.zeros((acts.shape[0] * acts.shape[1], chans), jnp.float32)
    for tap in range(5):
        piece = shifted(acts, (tap - 2) * step_size).reshape(-1, chans)
        total = total + jnp.dot(piece, kernel[tap], preferred_element_type=jnp.float32)
    return total.reshape(acts.shape)


def temporal_back(grads, kernel, step_size):
    chans = grads.shape[2]
    total = jnp.zeros((grads.shape[0] * grads.shape[1], chans), jnp.float32)
    for tap in range(5):
        piece = shifted(grads, (2 - tap) * step_size).reshape(-1, chans)
        total = total + jnp.dot(piece, kernel[tap].T, preferred_element_type=jnp.float32)
    return total.reshape(grads.shape)


def temporal_wgrad(acts, grads, step_size):
    chans = acts.shape[2]
    flat_grads = grads.reshape(-1, chans)
    return jnp.stack(
        [
            inner(shifted(acts, (tap - 2) * step_size).reshape(-1, chans), flat_grads)
            for tap in range(5)
        ]
    )


def to_pixels(flat):
    return lax.all_to_all(flat, ("seg", "grp"), split_axis=1, concat_axis=0, tiled=True)


def to_frames(blocks):
    return lax.all_to_all(blocks, ("seg", "grp"), split_axis=0, concat_axis=1, tiled=True)


def local(
    frames_in, spatial_weight, temporal_weight, uniting_weight, key_index, dilation, cotangent
):
    local_frames, rows, cols, chans = frames_in.shape
    pixels = rows * cols
    seg_count = lax.axis_size("seg")
    pre_spatial = spatial_forward(frames_in, spatial_weight)
    act_zero = jax.nn.silu(pre_spatial).astype(jnp.bfloat16).reshape(local_frames, pixels, chans)
    cot_local = cotangent.reshape(local_frames, pixels, chans)
    act_blocks = to_pixels(act_zero)
    cot_blocks = lax.all_to_all(cot_local, ("seg", "grp"), split_axis=1, concat_axis=0, tiled=True)
    acts = [act_blocks]
    total_frames = acts[0].shape[0]
    block = acts[0].shape[1]
    seg_frames = total_frames // seg_count
    pres = []
    for layer in range(LAYERS):
        pre = temporal_forward(acts[-1], temporal_weight[layer], dilation[layer])
        pres.append(pre)
        acts.append(jax.nn.silu(pre).astype(jnp.bfloat16))
    feat = acts[-1]
    feat_seg = feat.reshape(seg_count, seg_frames, block, chans)
    positions = jnp.arange(seg_frames, dtype=jnp.int32)
    onehot = positions[None, :] == key_index[:, None]
    keys = jnp.einsum(
        "ns,nspc->npc", onehot.astype(jnp.bfloat16), feat_seg, preferred_element_type=jnp.float32
    ).astype(jnp.bfloat16)
    key_full = jnp.broadcast_to(keys[:, None], feat_seg.shape).reshape(-1, chans)
    feat_flat = feat.reshape(-1, chans)
    feat_time = to_frames(feat)
    seg_here = key_index[lax.axis_index("seg")]
    owner = seg_here // local_frames
    local_pos = seg_here % local_frames
    panel = lax.dynamic_index_in_dim(feat_time, local_pos, 0, keepdims=False)
    key_panel = from_root(panel, "grp", owner)
    key_part = jnp.dot(key_panel, uniting_weight[1], preferred_element_type=jnp.float32)
    main_part = jnp.dot(
        feat_time.reshape(-1, chans), uniting_weight[0], preferred_element_type=jnp.float32
    )
    united = (main_part.reshape(local_frames, pixels, chans) + key_part[None]).astype(jnp.bfloat16)
    cot_flat = cot_blocks.reshape(-1, chans)
    grad_feat = jnp.dot(cot_flat, uniting_weight[0].T, preferred_element_type=jnp.float32)
    seg_cot = jnp.sum(
        cot_blocks.reshape(seg_count, seg_frames, block, chans).astype(jnp.float32), axis=1
    )
    key_term = jnp.dot(
        seg_cot.reshape(-1, chans),
        uniting_weight[1].T.astype(jnp.float32),
        precision=lax.Precision.HIGHEST,
    ).reshape(seg_count, 1, block, chans)
    placed = onehot.astype(jnp.float32)[:, :, None, None] * key_term
    grad_feat = grad_feat.reshape(seg_count, seg_frames, block, chans) + placed
    grad_feat = grad_feat.reshape(total_frames, block, chans)
    grad_uniting = jnp.stack([inner(feat_flat, cot_flat), inner(key_full, cot_flat)])
    grad_pre = (grad_feat * silu_grad(pres[-1])).astype(jnp.bfloat16)
    tgrads = [None] * LAYERS
    grad_act0 = None
    for layer in range(LAYERS - 1, -1, -1):
        tgrads[layer] = temporal_wgrad(acts[layer], grad_pre, dilation[layer])
        grad_act = temporal_back(grad_pre, temporal_weight[layer], dilation[layer])
        if layer > 0:
            grad_pre = (grad_act * silu_grad(pres[layer - 1])).astype(jnp.bfloat16)
        else:
            grad_act0 = grad_act.astype(jnp.bfloat16)
    grad_time = to_frames(grad_act0).reshape(frames_in.shape)
    grad_spre = (grad_time.astype(jnp.float32) * silu_grad(pre_spatial)).astype(jnp.bfloat16)
    grad_frames = spatial_back(grad_spre, spatial_weight).astype(jnp.bfloat16)
    grad_spatial = spatial_wgrad(frames_in, grad_spre)
    summed = lax.psum((grad_spatial, jnp.stack(tgrads), grad_uniting), ("seg", "grp"))
    scale = 1.0 / jnp.sqrt(jnp.float32(total_frames * pixels))
    return (
        united.reshape(frames_in.shape),
        grad_frames,
        summed[0] * scale,
        summed[1] * scale,
        summed[2] * scale,
    )


def solution(mesh):
    placed = (
        P(("seg", "grp"), None, None, None),
        P(),
        P(),
        P(),
        P(),
        P(),
        P(("seg", "grp"), None, None, None),
    )
    return jax.shard_map(
        local,
        mesh=mesh,
        in_specs=placed,
        out_specs=(
            P(("seg", "grp"), None, None, None),
            P(("seg", "grp"), None, None, None),
            P(),
            P(),
            P(),
        ),
        check_vma=False,
    )
```

profile of v0, /device:TPU:0, one launch (start us, length us, event | category | flops | bytes accessed | tf_op | source)
XLA Modules:
  0.0 413.0 jit_solution(11193187069494379591)
XLA Ops:
  7.2 9.1 %copy.34 = bf16[1,3840,128]{2,0,1:T(2,128)(2,1)S(1)} copy(bf16[1,3840,128]{2,1,0:T(8,128)(2,1)} %bitcast.470) | data formatting | bytes 1966080 | tf_op jit(solution)/shard_map/reshape | solution.py:121
  16.8 21.0 %reduce = bf16[3840,128]{1,0:T(8,128)(2,1)S(1)} reduce(bf16[3840,1,128]{2,1,0:T(2,128)(2,1)S(1)} %bitcast.435, bf16[]{:T(256)} %broadcast.83), dimensions={1}, to_apply=%bitcast.417.reduce_sub_computation | reduce | bytes 1966082
  37.8 1.2 reshape.485
  39.0 7.8 %all-to-all-start.2 = ((bf16[32,2,7680]{2,1,0:T(2,128)(2,1)}), bf16[32,2,7680]{2,1,0:T(2,128)(2,1)S(1)}, u32[]{:S(2)}, u32[]{:S(2)}) async-start(bf16[32,2,7680]{2,1,0:T(2,128)(2,1)} %reshape.485), calls=%async_computation.2 | async-start | bytes 1966080 | tf_op jit(solution)/shard_map/all_to_all | solution.py:123
  46.9 2.5 pad_slice_fusion.8
  53.6 16.0 %copy.35 = bf16[1,3840,128]{2,0,1:T(2,128)(2,1)} copy(bf16[1,3840,128]{2,1,0:T(8,128)(2,1)S(1)} %fusion.40) | data formatting | bytes 1966080 | tf_op jit(solution)/shard_map/convert_element_type | solution.py:120
  69.6 23.2 %reduce.1 = bf16[3840,128]{1,0:T(8,128)(2,1)} reduce(bf16[3840,1,128]{2,1,0:T(2,128)(2,1)} %bitcast.436, bf16[]{:T(256)} %broadcast.83), dimensions={1}, to_apply=%bitcast.418.reduce_sub_computation | reduce | bytes 1966082
  92.8 3.1 reshape.483
  95.9 6.1 %all-to-all-start = ((bf16[32,2,7680]{2,1,0:T(2,128)(2,1)}), bf16[32,2,7680]{2,1,0:T(2,128)(2,1)}, u32[]{:S(2)}, u32[]{:S(2)}) async-start(bf16[32,2,7680]{2,1,0:T(2,128)(2,1)} %reshape.483), calls=%async_computation | async-start | bytes 1966080 | tf_op jit(solution)/shard_map/all_to_all | solution.py:106
  110.9 3.2 reshape.486
  114.1 1.7 copy.26
  116.0 10.8 %all-to-all-done = bf16[32,2,7680]{2,1,0:T(2,128)(2,1)} async-done(((bf16[32,2,7680]{2,1,0:T(2,128)(2,1)}), bf16[32,2,7680]{2,1,0:T(2,128)(2,1)}, u32[]{:S(2)}, u32[]{:S(2)}) %all-to-all-start) | async-done | bytes 983072 | tf_op jit(solution)/shard_map/all_to_all | solution.py:106
  126.8 5.8 %reshape.484 = bf16[3840,1,128]{2,1,0:T(2,128)(2,1)} reshape(bf16[32,2,7680]{2,1,0:T(2,128)(2,1)} %all-to-all-done) | data formatting | bytes 1966080
  132.6 1.7 copy.24
  134.3 1.8 pad_dynamic-slice_fusion.12
  139.2 1.8 pad_dynamic-slice_fusion.8
  145.0 1.9 fusion.5
  147.4 2.2 pad_dynamic-slice_fusion.4
  151.3 1.8 multiply_convert_fusion.4
  153.9 1.1 fusion.15
  155.0 3.2 pad_dynamic-slice_fusion
  162.3 3.9 all-to-all-start.1
  166.2 2.4 fusion.14
  173.9 1.4 fusion.1
  176.5 14.5 %all-to-all-done.1 = bf16[32,120,128]{2,1,0:T(8,128)(2,1)} async-done(((bf16[32,120,128]{2,1,0:T(8,128)(2,1)}), bf16[32,120,128]{2,1,0:T(8,128)(2,1)}, u32[]{:S(2)}, u32[]{:S(2)}) %all-to-all-start.1) | async-done | bytes 983072 | tf_op jit(solution)/shard_map/all_to_all | solution.py:110
  191.0 3.7 all-to-all-start.3
  195.5 2.7 fusion.13
  198.2 1.1 fusion.12
  200.4 1.9 pad_maximum_fusion
  202.2 2.2 broadcast_select_fusion
  204.5 15.1 %all-to-all-done.3 = bf16[32,120,128]{2,1,0:T(8,128)(2,1)} async-done(((bf16[32,120,128]{2,1,0:T(8,128)(2,1)}), bf16[32,120,128]{2,1,0:T(8,128)(2,1)}, u32[]{:S(2)}, u32[]{:S(2)}) %all-to-all-start.3) | async-done | bytes 983072 | tf_op jit(solution)/shard_map/all_to_all | solution.py:110
  219.6 2.0 multiply_convert_fusion.3
  221.6 1.1 fusion.24
  223.8 1.1 fusion.22
  228.2 1.1 fusion.18
  230.4 3.5 pad_slice_fusion
  235.5 1.9 fusion.3
  238.3 1.7 convolution_add_fusion.2
  240.0 1.1 fusion.16
  241.1 2.0 convolution_add_fusion.1
  243.1 3.0 fusion.45
  246.1 1.4 fusion.2
  247.5 15.5 %all-reduce.10.cloned.1.call-done = bf16[3840,128]{1,0:T(8,128)(2,1)} async-done(((bf16[3840,128]{1,0:T(8,128)(2,1)}), bf16[3840,128]{1,0:T(8,128)(2,1)}) %all-reduce.10.cloned.1.call-update) | async-done | bytes 983056 | tf_op jit(solution)/shard_map/psum | solution.py:12
  263.0 3.2 fusion
  266.2 134.2 %all-reduce.12.cloned.1.call-done = (f32[9,128,128]{2,1,0:T(8,128)}, f32[2,5,128,128]{3,2,1,0:T(8,128)}, f32[2,128,128]{2,1,0:T(8,128)}) async-done(((f32[9,128,128]{2,1,0:T(8,128)}, f32[2,5,128,128]{3,2,1,0:T(8,128)}, f32[2,128,128]{2,1,0:T(8,128)}), (f32[9,128,128]{2,1,0:T(8,128)}, f32[2,5,128,128]{3,2,1,0:T(8,128)}, f32[2,128,128]{2,1,0:T(8,128)})) %all-reduce.12.cloned.1.call-update) | async-done | bytes 1376272 | tf_op jit(solution)/shard_map/psum | solution.py:181
  400.4 1.9 broadcast_multiply_fusion.1
  402.4 1.6 broadcast_multiply_fusion.2
  403.9 2.0 broadcast_multiply_fusion
  (122 shorter events, 36.7 us)
Async XLA Ops:
  37.8 9.0 %copy-start.3 = (bf16[1,32,120,128]{3,2,1,0:T(8,128)(2,1)S(1)}, bf16[1,32,120,128]{3,2,1,0:T(8,128)(2,1)}, u32[]{:S(2)}) copy-start(bf16[1,32,120,128]{3,2,1,0:T(8,128)(2,1)} %param.7) | copy-start | bytes 2949124
  39.0 56.8 %all-to-all-start.2 = ((bf16[32,2,7680]{2,1,0:T(2,128)(2,1)}), bf16[32,2,7680]{2,1,0:T(2,128)(2,1)S(1)}, u32[]{:S(2)}, u32[]{:S(2)}) async-start(bf16[32,2,7680]{2,1,0:T(2,128)(2,1)} %reshape.485), calls=%async_computation.2 | async-start | bytes 1966080 | tf_op jit(solution)/shard_map/all_to_all | solution.py:123
  46.9 2.5 copy-start.18
  92.8 9.2 %copy-start.26 = (s32[2]{0:T(128)S(1)}, s32[2]{0:T(128)}, u32[]{:S(2)}) copy-start(s32[2]{0:T(128)} %param.12) | copy-start | bytes 28
  92.8 16.3 %copy-start.27 = (s32[4]{0:T(128)S(1)}, s32[4]{0:T(128)}, u32[]{:S(2)}) copy-start(s32[4]{0:T(128)} %param.11) | copy-start | bytes 52
  95.9 30.9 %all-to-all-start = ((bf16[32,2,7680]{2,1,0:T(2,128)(2,1)}), bf16[32,2,7680]{2,1,0:T(2,128)(2,1)}, u32[]{:S(2)}, u32[]{:S(2)}) async-start(bf16[32,2,7680]{2,1,0:T(2,128)(2,1)} %reshape.483), calls=%async_computation | async-start | bytes 1966080 | tf_op jit(solution)/shard_map/all_to_all | solution.py:106
  115.8 26.3 %copy-start.1 = (bf16[1,3840,128]{2,1,0:T(8,128)(2,1)}, bf16[1,3840,128]{2,1,0:T(8,128)(2,1)S(1)}, u32[]{:S(2)}) copy-start(bf16[1,3840,128]{2,1,0:T(8,128)(2,1)S(1)} %copy.26) | copy-start | bytes 2949124
  134.2 2.7 copy-start
  134.3 1.9 copy-start.19
  136.1 1.0 copy-start.7
  136.1 1.4 copy-start.5
  136.1 1.8 copy-start.13
  141.0 0.8 copy-start.23
  141.0 1.1 copy-start.25
  145.0 13.2 %copy-start.8 = (f32[3840,128]{1,0:T(8,128)}, f32[3840,128]{1,0:T(8,128)S(1)}, u32[]{:S(2)}) copy-start(f32[3840,128]{1,0:T(8,128)S(1)} %get-tuple-element.51) | copy-start | bytes 5898244
  159.1 0.7 copy-start.24
  161.6 0.7 copy-start.21
  162.3 28.7 %all-to-all-start.1 = ((bf16[32,120,128]{2,1,0:T(8,128)(2,1)}), bf16[32,120,128]{2,1,0:T(8,128)(2,1)}, u32[]{:S(2)}, u32[]{:S(2)}) async-start(bf16[32,120,128]{2,1,0:T(8,128)(2,1)} %get-tuple-element.11), calls=%async_computation.1 | async-start | bytes 1966080 | tf_op jit(solution)/shard_map/all_to_all | solution.py:110
  166.2 2.4 copy-start.15
  166.2 2.4 copy-start.20
  168.6 1.2 copy-start.2
  169.0 1.3 copy-start.12
  170.3 1.2 copy-start.10
  171.5 1.2 copy-start.11
  172.7 1.2 copy-start.16
  173.9 1.9 copy-start.9
  191.0 28.6 %all-to-all-start.3 = ((bf16[32,120,128]{2,1,0:T(8,128)(2,1)}), bf16[32,120,128]{2,1,0:T(8,128)(2,1)}, u32[]{:S(2)}, u32[]{:S(2)}) async-start(bf16[32,120,128]{2,1,0:T(8,128)(2,1)} %bitcast.466), calls=%async_computation.3 | async-start | bytes 1966080 | tf_op jit(solution)/shard_map/all_to_all | solution.py:110
  194.8 68.3 %all-reduce.10.cloned.1.call-start = ((), (), s32[]{:S(2)}) async-start(), calls=%async_computation.4 | async-start | bytes 1966080 | tf_op jit(solution)/shard_map/psum | solution.py:12
  194.8 3.4 copy-start.6
  195.5 3.8 copy-start.14
  198.2 2.2 copy-start.22
  204.5 196.0 %all-reduce.12.cloned.1.call-start = ((), (), s32[]{:S(2)}) async-start(), calls=%async_computation.5 | async-start | bytes 2752512 | tf_op jit(solution)/shard_map/psum | solution.py:181
  219.6 2.0 copy-start.4
  243.1 3.0 copy-start.17
Sparse Core Ops, SparseCore 0:
  204.6 58.3 all-reduce.9
  269.3 131.0 all-reduce.11
where the time goes:
time: 420 us; the launch traced here: 413 us
  waiting for transfers between devices  190 us (45%)
  other arithmetic  63.8 us (15%)
  local copies, waits for them, and re-layouts  63.7 us (15%)
  matrix products  51.7 us (12%)
  between operations  22 us (5%)
  starting transfers between devices  21.6 us (5%)
    psum x1, waiting for transfers between devices, local(): lax.psum((grad_spatial, jnp.stack(tgrads), grad_uniting), ('seg', 'grp'))  134 us
    unnamed x2, other arithmetic  44.2 us
    all_to_all x2, waiting for transfers between devices, to_frames(): lax.all_to_all(blocks, ('seg', 'grp'), split_axis=0, concat_axis=1, tiled...  29.5 us
    unnamed x63, local copies, waits for them, and re-layouts  22.3 us
    dot_general x21, matrix products, inner(): lax.dot_general(left, right, (((0,), (0,)), ((), ())), preferred_element_...  21.7 us
    convert_element_type x1, local copies, waits for them, and re-layouts, local(): jax.nn.silu(pre_spatial).astype(jnp.bfloat16)  16 us
    psum x1, waiting for transfers between devices, from_root(): return lax.psum(jnp.where(mine, value, jnp.zeros_like(value)), axis)  15.5 us
    all_to_all x1, waiting for transfers between devices, to_pixels(): lax.all_to_all(flat, ('seg', 'grp'), split_axis=1, concat_axis=0, tiled=T...  10.8 us
  transfers between devices with their start and end apart: 6, of which 5 were waited for; matrix products, arithmetic and copies ran while one was open for 25% of the time, Pallas kernels for 0%

commit v1 on v0

v1 whole, which is shorter than its diff:
```python
import functools

import jax
import jax.numpy as jnp
from jax import lax
from jax.experimental import pallas as pl
from jax.experimental.pallas import tpu as pltpu
from jax.sharding import PartitionSpec as P

LAYERS = 2
TAPS = 5
DMAX = 8
HALO = 2 * DMAX
AXES = ("seg", "grp")
BF16 = jnp.bfloat16
F32 = jnp.float32
VMEM_LIMIT = 48 * 1024 * 1024


def round_up(value, step):
    return -(-value // step) * step


def silu_parts(value):
    sigma = 0.5 * jnp.tanh(0.5 * value) + 0.5
    act = value * sigma
    return act, sigma + act * (1.0 - sigma)


def mm(left, right):
    return jnp.dot(left, right, preferred_element_type=F32)


def mm_nt(left, right):
    return lax.dot_general(left, right, (((1,), (1,)), ((), ())), preferred_element_type=F32)


def mm_tn(left, right):
    return lax.dot_general(left, right, (((0,), (0,)), ((), ())), preferred_element_type=F32)


def three_parts(value):
    high = value.astype(BF16)
    rest = value - high.astype(F32)
    middle = rest.astype(BF16)
    return high, middle, (rest - middle.astype(F32)).astype(BF16)


def call(kernel, outs, scratch, flops, moved, smem, args):
    specs = [pl.BlockSpec(memory_space=pltpu.SMEM)] * smem
    specs += [pl.BlockSpec(memory_space=pltpu.VMEM)] * (len(args) - smem)
    return pl.pallas_call(
        kernel,
        out_shape=[jax.ShapeDtypeStruct(shape, kind) for shape, kind in outs],
        in_specs=specs,
        out_specs=[pl.BlockSpec(memory_space=pltpu.VMEM)] * len(outs),
        scratch_shapes=scratch,
        compiler_params=pltpu.CompilerParams(vmem_limit_bytes=VMEM_LIMIT),
        cost_estimate=pl.CostEstimate(flops=flops, bytes_accessed=moved, transcendentals=0),
    )(*args)


def roll_rows(value, shift):
    return pltpu.roll(value, shift % value.shape[0], 0)


def spatial_fwd_kernel(rows_step, x_ref, w_ref, act_ref, slope_ref, xs):
    rows, cols, ch = x_ref.shape
    wide = xs.shape[1]
    xs[...] = jnp.zeros(xs.shape, xs.dtype)
    xs[1 : rows + 1, :cols, :] = x_ref[...]
    weight = jnp.concatenate(
        [jnp.concatenate([w_ref[3 * a + b] for b in range(3)], axis=1) for a in range(3)], axis=0
    )
    flat = rows_step * wide
    for step in range(rows // rows_step):
        at = step * rows_step
        left = jnp.concatenate(
            [xs[at + a : at + a + rows_step].reshape(flat, ch) for a in range(3)], axis=1
        )
        y = mm(left, weight)
        pre = y[:, ch : 2 * ch] + roll_rows(y[:, :ch], 1) + roll_rows(y[:, 2 * ch :], -1)
        act, slope = silu_parts(pre)
        act_ref[at : at + rows_step] = act.astype(BF16).reshape(rows_step, wide, ch)[:, :cols]
        slope_ref[at : at + rows_step] = slope.reshape(rows_step, wide, ch)


def spatial_bwd_kernel(rows_step, x_ref, w_ref, grad_ref, slope_ref, back_ref, wgrad_ref, gs):
    rows, cols, ch = x_ref.shape
    wide = gs.shape[1]
    gs[...] = jnp.zeros(gs.shape, gs.dtype)
    gs[1 : rows + 1, :cols, :] = (
        grad_ref[...].astype(F32) * slope_ref[:, :cols, :]
    ).astype(BF16)
    weight = jnp.concatenate(
        [
            jnp.concatenate([w_ref[3 * a + b].astype(F32).T.astype(BF16) for b in range(3)], axis=1)
            for a in range(3)
        ],
        axis=0,
    )
    flat = rows_step * wide
    pad = jnp.zeros((rows_step, wide - cols, ch), F32)
    total = jnp.zeros((3 * ch, 3 * ch), F32)
    for step in range(rows // rows_step):
        at = step * rows_step
        grads = jnp.concatenate(
            [gs[at + 2 - a : at + 2 - a + rows_step].reshape(flat, ch) for a in range(3)], axis=1
        )
        y = mm(grads, weight)
        back = y[:, ch : 2 * ch] + roll_rows(y[:, :ch], -1) + roll_rows(y[:, 2 * ch :], 1)
        back_ref[at : at + rows_step] = back.astype(BF16).reshape(rows_step, wide, ch)[:, :cols]
        x = jnp.concatenate([x_ref[at : at + rows_step].astype(F32), pad], axis=1).reshape(flat, ch)
        x_cat = jnp.concatenate([roll_rows(x, 1), x, roll_rows(x, -1)], axis=1).astype(BF16)
        total = total + mm_tn(x_cat, grads)
    for a in range(3):
        for b in range(3):
            wgrad_ref[3 * a + b] = total[b * ch : (b + 1) * ch, a * ch : (a + 1) * ch]


def fill_frames(pad_ref, value_ref):
    frames, block, ch = value_ref.shape
    pad_ref[...] = jnp.zeros(pad_ref.shape, pad_ref.dtype)
    pad_ref[HALO : HALO + frames, :block, :] = value_ref[...]


def clear_halo(pad_ref, frames):
    zeros = jnp.zeros((HALO,) + pad_ref.shape[1:], pad_ref.dtype)
    pad_ref[:HALO] = zeros
    pad_ref[HALO + frames :] = zeros


def taps_of(pad_ref, at, count, step_size, sign):
    high, ch = pad_ref.shape[1:]
    pieces = [
        pad_ref[pl.ds(HALO + at + sign * (k - 2) * step_size, count)].reshape(count * high, ch)
        for k in range(TAPS)
    ]
    return jnp.concatenate(pieces, axis=1)


def temporal_fwd_kernel(
    step_frames, dil_ref, key_ref, act_ref, tw_ref, uw_ref,
    united_ref, a0, a1, feat, slope0, slope1,
):
    frames, block, ch = act_ref.shape
    high = a0.shape[1]
    fill_frames(a0, act_ref)
    clear_halo(a1, frames)
    for layer, (source, target, slopes) in enumerate(((a0, a1, slope0), (a1, feat, slope1))):
        step_size = dil_ref[layer]
        weight = jnp.concatenate([tw_ref[layer, k] for k in range(TAPS)], axis=0)
        first = HALO if layer == 0 else 0
        for at in range(0, frames, step_frames):
            pre = mm(taps_of(source, at, step_frames, step_size, 1), weight)
            act, slope = silu_parts(pre)
            target[first + at : first + at + step_frames] = act.astype(BF16).reshape(
                step_frames, high, ch
            )
            slopes[at : at + step_frames] = slope.reshape(step_frames, high, ch)
    segs = key_ref.shape[0]
    seg_frames = frames // segs
    for seg in range(segs):
        key_part = mm(feat[seg * seg_frames + key_ref[seg]], uw_ref[1])
        main = mm(
            feat[seg * seg_frames : (seg + 1) * seg_frames].reshape(seg_frames * high, ch), uw_ref[0]
        ).reshape(seg_frames, high, ch)
        united_ref[seg * seg_frames : (seg + 1) * seg_frames] = (main + key_part[None]).astype(BF16)[
            :, :block
        ]


def temporal_bwd_kernel(
    step_frames, dil_ref, key_ref, cot_ref, tw_ref, uw_ref, slope0, slope1,
    grad_ref, cots, g0, g1, seg_cot, grad_feat,
):
    frames, block, ch = cot_ref.shape
    high = cots.shape[1]
    segs = key_ref.shape[0]
    seg_frames = frames // segs
    cots[...] = jnp.zeros(cots.shape, cots.dtype)
    cots[:, :block, :] = cot_ref[...]
    clear_halo(g0, frames)
    clear_halo(g1, frames)
    for seg in range(segs):
        low, top = seg * seg_frames, (seg + 1) * seg_frames
        mine = cots[low:top]
        total = jnp.sum(mine.astype(F32), axis=0)
        seg_cot[seg] = total
        grad_feat[low:top] = mm_nt(mine.reshape(seg_frames * high, ch), uw_ref[0]).reshape(
            seg_frames, high, ch
        )
        key_term = sum(mm_nt(part, uw_ref[1]) for part in three_parts(total))
        here = low + key_ref[seg]
        grad_feat[here] = grad_feat[here] + key_term
        g1[HALO + low : HALO + top] = (grad_feat[low:top] * slope1[low:top]).astype(BF16)
    for layer, source in ((1, g1), (0, g0)):
        step_size = dil_ref[layer]
        weight = jnp.concatenate([tw_ref[layer, k].astype(F32).T.astype(BF16) for k in range(TAPS)], axis=0)
        for at in range(0, frames, step_frames):
            grad = mm(taps_of(source, at, step_frames, step_size, -1), weight).reshape(
                step_frames, high, ch
            )
            if layer == 1:
                g0[HALO + at : HALO + at + step_frames] = (
                    grad * slope0[at : at + step_frames]
                ).astype(BF16)
            else:
                grad_ref[at : at + step_frames] = grad.astype(BF16)[:, :block]


def temporal_wgrad_kernel(
    step_frames, dil_ref, key_ref, a0, a1, feat, g0, g1, cots, seg_cot, out_ref
):
    frames, high, ch = feat.shape
    segs = key_ref.shape[0]
    seg_frames = frames // segs
    rows = step_frames * high
    for layer, acts, grads in ((0, a0, g0), (1, a1, g1)):
        total = jnp.zeros((TAPS * ch, ch), F32)
        for at in range(0, frames, step_frames):
            total = total + mm_tn(
                taps_of(acts, at, step_frames, dil_ref[layer], 1),
                grads[HALO + at : HALO + at + step_frames].reshape(rows, ch),
            )
        out_ref[layer * TAPS : (layer + 1) * TAPS] = total.reshape(TAPS, ch, ch).astype(out_ref.dtype)
    total = jnp.zeros((ch, ch), F32)
    for at in range(0, frames, step_frames):
        total = total + mm_tn(
            feat[at : at + step_frames].reshape(rows, ch),
            cots[at : at + step_frames].reshape(rows, ch),
        )
    out_ref[LAYERS * TAPS] = total.astype(out_ref.dtype)
    total = jnp.zeros((ch, ch), F32)
    for seg in range(segs):
        key = feat[seg * seg_frames + key_ref[seg]]
        total = total + sum(mm_tn(key, part) for part in three_parts(seg_cot[seg]))
    out_ref[LAYERS * TAPS + 1] = total.astype(out_ref.dtype)


def exchange(blocks):
    return lax.all_to_all(blocks, AXES, split_axis=0, concat_axis=0, tiled=True)


def reduce_everywhere(parts, devices):
    count, ch, _ = parts.shape
    pieces = exchange(parts.astype(BF16).reshape(devices, count * ch // devices, ch))
    mine = jnp.sum(pieces.astype(F32), axis=0)
    return lax.all_gather(mine, AXES, axis=0, tiled=True).reshape(count, ch, ch)


def local(
    frames_in, spatial_weight, temporal_weight, uniting_weight, key_index, dilation, cotangent
):
    held, rows, cols, ch = frames_in.shape
    pixels = rows * cols
    devices = lax.axis_size("seg") * lax.axis_size("grp")
    frames = held * devices
    block = pixels // devices
    wide = round_up(cols + 1, 16)
    high = round_up(block, 16)
    rows_step = next(n for n in (4, 2, 1) if rows % n == 0)
    step_frames = max(n for n in range(1, frames + 1) if frames % n == 0 and n * high <= 512)

    def to_pixels(values):
        split = values.reshape(held, devices, block, ch).swapaxes(0, 1)
        return exchange(split.reshape(devices * held, block, ch))

    def to_frames(blocks):
        got = exchange(blocks).reshape(devices, held, block, ch).swapaxes(0, 1)
        return got.reshape(held, rows, cols, ch)

    cot_blocks = to_pixels(cotangent)

    spatial = [
        call(
            functools.partial(spatial_fwd_kernel, rows_step),
            [((rows, cols, ch), BF16), ((rows, wide, ch), F32)],
            [pltpu.VMEM((rows + 2, wide, ch), BF16)],
            2 * 9 * pixels * ch * ch,
            pixels * ch * 8,
            0,
            (frames_in[i], spatial_weight),
        )
        for i in range(held)
    ]
    act_blocks = to_pixels(jnp.stack([act for act, _ in spatial]))

    padded = ((frames + 2 * HALO, high, ch), BF16)
    whole = (frames, high, ch)
    united_blocks, a0, a1, feat, slope0, slope1 = call(
        functools.partial(temporal_fwd_kernel, step_frames),
        [((frames, block, ch), BF16), padded, padded, (whole, BF16), (whole, F32), (whole, F32)],
        [],
        2 * 11 * frames * block * ch * ch,
        frames * block * ch * 18,
        2,
        (dilation, key_index, act_blocks, temporal_weight, uniting_weight),
    )
    grad_blocks, cots, g0, g1, seg_cot = call(
        functools.partial(temporal_bwd_kernel, step_frames),
        [
            ((frames, block, ch), BF16),
            (whole, BF16),
            padded,
            padded,
            ((key_index.shape[0], high, ch), F32),
        ],
        [pltpu.VMEM(whole, F32)],
        2 * 11 * frames * block * ch * ch,
        frames * block * ch * 18,
        2,
        (dilation, key_index, cot_blocks, temporal_weight, uniting_weight, slope0, slope1),
    )
    grad_time = to_frames(grad_blocks)
    united = to_frames(united_blocks)
    (tgrads,) = call(
        functools.partial(temporal_wgrad_kernel, step_frames),
        [((LAYERS * TAPS + 2, ch, ch), F32)],
        [],
        2 * 12 * frames * block * ch * ch,
        frames * block * ch * 14,
        2,
        (dilation, key_index, a0, a1, feat, g0, g1, cots, seg_cot),
    )
    back = [
        call(
            functools.partial(spatial_bwd_kernel, rows_step),
            [((rows, cols, ch), BF16), ((9, ch, ch), F32)],
            [pltpu.VMEM((rows + 2, wide, ch), BF16)],
            2 * 18 * pixels * ch * ch,
            pixels * ch * 10,
            0,
            (frames_in[i], spatial_weight, grad_time[i], spatial[i][1]),
        )
        for i in range(held)
    ]
    scale = 1.0 / jnp.sqrt(jnp.float32(frames * pixels))
    summed_time = reduce_everywhere(tgrads, devices) * scale
    summed_space = reduce_everywhere(sum(grad for _, grad in back), devices) * scale
    return (
        united,
        jnp.stack([grad for grad, _ in back]),
        summed_space,
        summed_time[: LAYERS * TAPS].reshape(LAYERS, TAPS, ch, ch),
        summed_time[LAYERS * TAPS :],
    )


def solution(mesh):
    frame_spec = P(AXES, None, None, None)
    return jax.shard_map(
        local,
        mesh=mesh,
        in_specs=(frame_spec, P(), P(), P(), P(), P(), frame_spec),
        out_specs=(frame_spec, frame_spec, P(), P(), P()),
        check_vma=False,
    )
```

time: 420 us -> 245 us (0.58); the launches traced: 413 us -> 245 us
  blocking collectives: 0 us -> 159 us
  waiting for transfers between devices: 190 us -> 31.6 us
  other arithmetic: 63.8 us -> 1.35 us
  matrix products: 51.7 us -> 0 us
  local copies, waits for them, and re-layouts: 63.7 us -> 12.8 us
  Pallas kernels: 0 us -> 28 us
  between operations: 22 us -> 0.78 us
  starting transfers between devices: 21.6 us -> 11.3 us
    psum x2 -> x0, waiting for transfers between devices: 150 us -> none  [the longest x1 134 us: local(): lax.psum((grad_spatial, jnp.stack(tgrads), grad_uniting), ('seg', 'grp'))]
    all_gather x0 -> x2, blocking collectives: none -> 82.8 us  [reduce_everywhere(): return lax.all_gather(mine, AXES, axis=0, tiled=True).reshape(count, ch, ch)]
    all_to_all x0 -> x3, blocking collectives: none -> 76 us  [exchange(): return lax.all_to_all(blocks, AXES, split_axis=0, concat_axis=0, tiled=True)]
    dot_general x64 -> x0, matrix products: 51.7 us -> none  [the longest x21 21.7 us: inner(): lax.dot_general(left, right, (((0,), (0,)), ((), ())), preferred_element_...]
    unnamed x2 -> x0, other arithmetic: 44.2 us -> none
    pallas_call x0 -> x5, Pallas kernels: none -> 28 us  [call(): pl.pallas_call(kernel, out_shape=[jax.ShapeDtypeStruct(shape, kind) for s...]
    convert_element_type x1 -> x0, local copies, waits for them, and re-layouts: 16 us -> none  [local(): jax.nn.silu(pre_spatial).astype(jnp.bfloat16)]
    unnamed x63 -> x29, local copies, waits for them, and re-layouts: 22.3 us -> 9.57 us
  transfers between devices with their start and end apart: 6 -> 3, of which waited for: 5 -> 2; matrix products, arithmetic and copies ran while one was open for 25% -> 1% of each run, Pallas kernels for 0% -> 5%
where the time goes in v1:
time: 245 us
  blocking collectives  159 us (65%)
  waiting for transfers between devices  31.6 us (13%)
  Pallas kernels  28 us (11%)
  local copies, waits for them, and re-layouts  12.8 us (5%)
  starting transfers between devices  11.3 us (5%)
    all_gather x2, blocking collectives, reduce_everywhere(): return lax.all_gather(mine, AXES, axis=0, tiled=True).reshape(count, ch, ch)  82.8 us
    all_to_all x3, blocking collectives, exchange(): return lax.all_to_all(blocks, AXES, split_axis=0, concat_axis=0, tiled=True)  76 us
    all_to_all x3, waiting for transfers between devices, exchange(): return lax.all_to_all(blocks, AXES, split_axis=0, concat_axis=0, tiled=True)  31.6 us
    pallas_call x5, Pallas kernels, call(): pl.pallas_call(kernel, out_shape=[jax.ShapeDtypeStruct(shape, kind) for s...  28 us
    all_to_all x3, starting transfers between devices, exchange(): return lax.all_to_all(blocks, AXES, split_axis=0, concat_axis=0, tiled=True)  11.3 us
    unnamed x29, local copies, waits for them, and re-layouts  9.57 us
  transfers between devices with their start and end apart: 3, of which 2 were waited for; matrix products, arithmetic and copies ran while one was open for 1% of the time, Pallas kernels for 5%

profile of v1, /device:TPU:0, one launch (start us, length us, event | category | flops | bytes accessed | tf_op | source)
XLA Modules:
  0.0 244.7 jit_solution(15382744948054349195)
XLA Ops:
  0.6 0.0 copy-start.8
  0.6 1.2 copy-done.8
  1.8 0.0 copy-start.10
  1.8 1.0 copy-done.10
  2.8 2.3 shard_map.110
  5.1 0.0 copy-start.12
  5.1 1.3 copy-done.12
  6.4 0.0 copy-start.4
  6.4 0.0 copy-start.5
  6.4 0.0 copy-start.6
  6.4 32.0 %all_to_all.30.act_ref = bf16[32,120,128]{2,1,0:T(8,128)(2,1)} all-to-all(bf16[32,120,128]{2,1,0:T(8,128)(2,1)S(1)} %get-tuple-element.20), channel_id=1, replica_groups=mesh['seg'=4,'grp'=8] {'seg','grp'}, dimensions={0} | all-to-all | bytes 1966080 | tf_op jit(solution)/shard_map/all_to_all | solution.py:242
  38.5 3.8 %all-to-all-start.2 = ((bf16[32,120,128]{2,1,0:T(8,128)(2,1)}), bf16[32,120,128]{2,1,0:T(8,128)(2,1)S(1)}, u32[]{:S(2)}, u32[]{:S(2)}) async-start(bf16[32,120,128]{2,1,0:T(8,128)(2,1)} %bitcast.2), calls=%async_computation.2 | async-start | bytes 1966080 | tf_op jit(solution)/shard_map/all_to_all | solution.py:242
  42.3 0.0 copy-done.4
  42.3 0.0 copy-done.5
  42.3 0.0 copy-done.6
  42.3 0.0 copy-done.7
  42.3 0.0 copy-start.3
  42.3 1.2 copy-done.3
  43.5 7.2 %shard_map.111 = (bf16[32,120,128]{2,1,0:T(8,128)(2,1)}, bf16[64,128,128]{2,1,0:T(8,128)(2,1)S(1)}, bf16[64,128,128]{2,1,0:T(8,128)(2,1)}, bf16[32,128,128]{2,1,...) custom-call(s32[2]{0:T(128)S(1)} %copy-done.6, s32[4]{0:T(128)S(1)} %copy-done.7, ...), custom_call_target="tpu_custom_call" | custom-call | flops 1384120320 | bytes 8847360 | tf_op jit(solution)/shard_map/pallas_call | solution.py:52
  50.8 1.0 copy-done.1
  51.8 15.2 %all-to-all-done.2.cot_ref = bf16[32,120,128]{2,1,0:T(8,128)(2,1)S(1)} async-done(((bf16[32,120,128]{2,1,0:T(8,128)(2,1)}), bf16[32,120,128]{2,1,0:T(8,128)(2,1)S(1)}, u32[]{:S(2)}, u32[]{:S(2)}) %all-to-all-start.2) | async-done | bytes 983072 | tf_op jit(solution)/shard_map/all_to_all | solution.py:242
  66.9 7.7 %shard_map.112 = (bf16[32,120,128]{2,1,0:T(8,128)(2,1)S(1)}, bf16[32,128,128]{2,1,0:T(8,128)(2,1)S(1)}, bf16[64,128,128]{2,1,0:T(8,128)(2,1)S(1)}, bf16[64,128,128]{2,1,0:T(8,128)(2,1)}, f32[4,128,128]{2,1,0:T(8,128)S(1)}) custom-call(s32[2]{0:T(128)S(1)} %copy-done.6, s32[4]{0:T(128)S(1)} %copy-done.7, bf16[32,120,128]{2,1,0:T(8,128)(2,1)S(1)} %all-to-all-done.2.cot_ref, ...), custom_call_target="tpu_custom_call" | custom-call | flops 1384120320 | bytes 8847360 | tf_op jit(solution)/shard_map/pallas_call | solution.py:52
  74.6 1.4 copy-done
  76.0 0.0 copy-done.2
  76.0 6.2 %shard_map.114 = f32[12,128,128]{2,1,0:T(8,128)S(1)} custom-call(s32[2]{0:T(128)S(1)} %copy-done.6, s32[4]{0:T(128)S(1)} %copy-done.7, bf16[64,128,128]{2,1,0:T(8,128)(2,1)S(1)} %get-tuple-element.28.a0, bf16[64,128,128]{2,1,0:T(8,128)(2,1)} %get-tuple-element.29.a1, bf16[32,128,128]{2,1,0:T(8,128)(2,1)S(1)} %copy-done.2, bf16[64,128,128]{2,1,0:T(8,128)(2,1)} %copy-done, ...), custom_call_target="tpu_custom_call" | custom-call | flops 1509949440 | bytes 6881280 | tf_op jit(solution)/shard_map/pallas_call | solution.py:52
  82.2 0.1 convert_element_type.14
  82.2 16.7 %all_to_all.31 = bf16[32,48,128]{2,1,0:T(8,128)(2,1)} all-to-all(bf16[32,48,128]{2,1,0:T(8,128)(2,1)S(1)} %bitcast.11), channel_id=1, replica_groups=mesh['seg'=4,'grp'=8] {'seg','grp'}, dimensions={0} | all-to-all | bytes 786432 | tf_op jit(solution)/shard_map/all_to_all | solution.py:242
  99.0 27.3 %all_to_all.32.grad_ref = bf16[32,120,128]{2,1,0:T(8,128)(2,1)S(1)} all-to-all(bf16[32,120,128]{2,1,0:T(8,128)(2,1)S(1)} %get-tuple-element.24), channel_id=1, replica_groups=mesh['seg'=4,'grp'=8] {'seg','grp'}, dimensions={0} | all-to-all | bytes 1966080 | tf_op jit(solution)/shard_map/all_to_all | solution.py:242
  126.2 3.8 %all-to-all-start.1 = ((bf16[32,120,128]{2,1,0:T(8,128)(2,1)}), bf16[32,120,128]{2,1,0:T(8,128)(2,1)S(1)}, u32[]{:S(2)}, u32[]{:S(2)}) async-start(bf16[32,120,128]{2,1,0:T(8,128)(2,1)} %get-tuple-element.21), calls=%async_computation.1 | async-start | bytes 1966080 | tf_op jit(solution)/shard_map/all_to_all | solution.py:242
  130.1 1.1 convert_reduce_fusion
  131.1 0.0 copy-done.9
  131.1 0.0 copy-done.11
  131.1 0.0 copy-start.13
  131.2 1.6 copy-done.13
  132.7 4.7 %shard_map.113 = (bf16[32,120,128]{2,1,0:T(8,128)(2,1)}, f32[9,128,128]{2,1,0:T(8,128)S(1)}) custom-call(bf16[32,120,128]{2,1,0:T(8,128)(2,1)S(1)} %bitcast.9, bf16[9,128,128]{2,1,0:T(8,128)(2,1)S(1)} %copy-done.11, bf16[32,120,128]{2,1,0:T(8,128)(2,1)S(1)} %all_to_all.32.grad_ref, f32[32,128,128]{2,1,0:T(8,128)S(1)} %copy-done.13), custom_call_target="tpu_custom_call" | custom-call | flops 2264924160 | bytes 4915200 | tf_op jit(solution)/shard_map/pallas_call | solution.py:52
  137.5 0.8 reshape.28
  138.2 16.4 %all-to-all-done.1 = bf16[32,120,128]{2,1,0:T(8,128)(2,1)S(1)} async-done(((bf16[32,120,128]{2,1,0:T(8,128)(2,1)}), bf16[32,120,128]{2,1,0:T(8,128)(2,1)S(1)}, u32[]{:S(2)}, u32[]{:S(2)}) %all-to-all-start.1) | async-done | bytes 983072 | tf_op jit(solution)/shard_map/all_to_all | solution.py:242
  154.7 3.6 %all-to-all-start.4 = ((bf16[32,36,128]{2,1,0:T(8,128)(2,1)}), bf16[32,36,128]{2,1,0:T(8,128)(2,1)S(1)}, u32[]{:S(2)}, u32[]{:S(2)}) async-start(bf16[32,36,128]{2,1,0:T(8,128)(2,1)} %reshape.28), calls=%async_computation.4 | async-start | bytes 655360 | tf_op jit(solution)/shard_map/all_to_all | solution.py:242
  158.3 44.0 %all_gather.7 = f32[1536,128]{1,0:T(8,128)S(1)} all-gather(f32[48,128]{1,0:T(8,128)S(1)} %convert_reduce_fusion), channel_id=1, replica_groups=mesh['seg'=4,'grp'=8] {'seg','grp'}, dimensions={0}, use_global_device_ids=true | all-gather | bytes 811008 | tf_op jit(solution)/shard_map/all_gather | solution.py:249
  202.3 0.1 broadcast_multiply_fusion
  202.4 0.7 slice.14
  203.1 0.9 slice.13
  203.9 0.0 all-to-all-done.4
  204.0 0.1 convert_reduce_fusion.1
  204.0 38.8 %all-gather = f32[32,36,128]{2,1,0:T(8,128)S(1)} all-gather(f32[1,36,128]{2,1,0:T(8,128)S(1)} %bitcast.14), channel_id=1, replica_groups=mesh['seg'=4,'grp'=8] {'seg','grp'}, dimensions={0}, use_global_device_ids=true | all-gather | bytes 608256 | tf_op jit(solution)/shard_map/all_gather | solution.py:249
  242.8 0.1 broadcast_multiply_fusion.1
  242.9 0.9 mul.18
  243.7 0.9 copy.13
  (7 shorter events, 0.1 us)
Async XLA Ops:
  0.6 1.2 copy-start.8
  1.8 1.0 copy-start.10
  5.1 1.3 copy-start.12
  6.4 35.9 %copy-start.4 = (bf16[2,5,128,128]{3,2,1,0:T(8,128)(2,1)S(1)}, bf16[2,5,128,128]{3,2,1,0:T(8,128)(2,1)}, u32[]{:S(2)}) copy-start(bf16[2,5,128,128]{3,2,1,0:T(8,128)(2,1)} %tw_ref.3) | copy-start | bytes 983044
  6.4 35.9 %copy-start.5 = (bf16[2,128,128]{2,1,0:T(8,128)(2,1)S(1)}, bf16[2,128,128]{2,1,0:T(8,128)(2,1)}, u32[]{:S(2)}) copy-start(bf16[2,128,128]{2,1,0:T(8,128)(2,1)} %uw_ref.3) | copy-start | bytes 196612
  6.4 35.9 %copy-start.6 = (s32[2]{0:T(128)S(1)}, s32[2]{0:T(128)}, u32[]{:S(2)}) copy-start(s32[2]{0:T(128)} %dil_ref.5) | copy-start | bytes 28
  6.4 35.9 %copy-start.7 = (s32[4]{0:T(128)S(1)}, s32[4]{0:T(128)}, u32[]{:S(2)}) copy-start(s32[4]{0:T(128)} %key_ref.5) | copy-start | bytes 52
  38.5 28.5 %all-to-all-start.2 = ((bf16[32,120,128]{2,1,0:T(8,128)(2,1)}), bf16[32,120,128]{2,1,0:T(8,128)(2,1)S(1)}, u32[]{:S(2)}, u32[]{:S(2)}) async-start(bf16[32,120,128]{2,1,0:T(8,128)(2,1)} %bitcast.2), calls=%async_computation.2 | async-start | bytes 1966080 | tf_op jit(solution)/shard_map/all_to_all | solution.py:242
  42.3 1.2 copy-start.3
  50.8 1.0 copy-start.1
  66.9 9.1 %copy-start.2 = (bf16[32,128,128]{2,1,0:T(8,128)(2,1)S(1)}, bf16[32,128,128]{2,1,0:T(8,128)(2,1)}, u32[]{:S(2)}) copy-start(bf16[32,128,128]{2,1,0:T(8,128)(2,1)} %copy-done.1) | copy-start | bytes 3145732
  74.6 1.4 copy-start
  98.9 32.2 %copy-start.9 = (bf16[1,32,120,128]{3,2,1,0:T(8,128)(2,1)S(1)}, bf16[1,32,120,128]{3,2,1,0:T(8,128)(2,1)}, u32[]{:S(2)}) copy-start(bf16[1,32,120,128]{3,2,1,0:T(8,128)(2,1)} %param.7) | copy-start | bytes 2949124
  99.0 32.2 %copy-start.11 = (bf16[9,128,128]{2,1,0:T(8,128)(2,1)S(1)}, bf16[9,128,128]{2,1,0:T(8,128)(2,1)}, u32[]{:S(2)}) copy-start(bf16[9,128,128]{2,1,0:T(8,128)(2,1)} %w_ref.3) | copy-start | bytes 884740
  126.2 28.5 %all-to-all-start.1 = ((bf16[32,120,128]{2,1,0:T(8,128)(2,1)}), bf16[32,120,128]{2,1,0:T(8,128)(2,1)S(1)}, u32[]{:S(2)}, u32[]{:S(2)}) async-start(bf16[32,120,128]{2,1,0:T(8,128)(2,1)} %get-tuple-element.21), calls=%async_computation.1 | async-start | bytes 1966080 | tf_op jit(solution)/shard_map/all_to_all | solution.py:242
  131.1 1.6 copy-start.13
  154.7 49.3 %all-to-all-start.4 = ((bf16[32,36,128]{2,1,0:T(8,128)(2,1)}), bf16[32,36,128]{2,1,0:T(8,128)(2,1)S(1)}, u32[]{:S(2)}, u32[]{:S(2)}) async-start(bf16[32,36,128]{2,1,0:T(8,128)(2,1)} %reshape.28), calls=%async_computation.4 | async-start | bytes 655360 | tf_op jit(solution)/shard_map/all_to_all | solution.py:242

commit v2 on v1

--- a/solution.py
+++ b/solution.py
@@ -122,6 +122,17 @@
     frames, block, ch = value_ref.shape
     pad_ref[...] = jnp.zeros(pad_ref.shape, pad_ref.dtype)
     pad_ref[HALO : HALO + frames, :block, :] = value_ref[...]
+
+
+def place_of(here_ref, turns, peers, turn, peer):
+    return lax.rem(here_ref[0] + (turns - turn), turns) * peers + jnp.bitwise_xor(here_ref[1], peer)
+
+
+def order_kernel(here_ref, got_ref, out_ref):
+    peers, turns = got_ref.shape[:2]
+    for peer in range(peers):
+        for turn in range(turns):
+            out_ref[place_of(here_ref, turns, peers, turn, peer)] = got_ref[peer, turn]
 
 
 def clear_halo(pad_ref, frames):
@@ -171,15 +182,17 @@
 
 
 def temporal_bwd_kernel(
-    step_frames, dil_ref, key_ref, cot_ref, tw_ref, uw_ref, slope0, slope1,
+    step_frames, here_ref, dil_ref, key_ref, cot_ref, tw_ref, uw_ref, slope0, slope1,
     grad_ref, cots, g0, g1, seg_cot, grad_feat,
 ):
-    frames, block, ch = cot_ref.shape
-    high = cots.shape[1]
+    turns, peers, block, ch = cot_ref.shape
+    frames, high, _ = cots.shape
     segs = key_ref.shape[0]
     seg_frames = frames // segs
     cots[...] = jnp.zeros(cots.shape, cots.dtype)
-    cots[:, :block, :] = cot_ref[...]
+    for turn in range(turns):
+        for peer in range(peers):
+            cots[place_of(here_ref, turns, peers, turn, peer), :block, :] = cot_ref[turn, peer]
     clear_halo(g0, frames)
     clear_halo(g1, frames)
     for seg in range(segs):
@@ -245,8 +258,50 @@
 def reduce_everywhere(parts, devices):
     count, ch, _ = parts.shape
     pieces = exchange(parts.astype(BF16).reshape(devices, count * ch // devices, ch))
-    mine = jnp.sum(pieces.astype(F32), axis=0)
-    return lax.all_gather(mine, AXES, axis=0, tiled=True).reshape(count, ch, ch)
+    mine = jnp.sum(pieces.astype(F32), axis=0).astype(BF16)
+    return exchange(jnp.broadcast_to(mine, pieces.shape)).reshape(count, ch, ch).astype(F32)
+
+
+def flip(value, peer):
+    size = lax.axis_size("grp")
+    return lax.ppermute(value, "grp", [(i, i ^ peer) for i in range(size)])
+
+
+def turn_by(value, turn):
+    size = lax.axis_size("seg")
+    return lax.ppermute(value, "seg", [(i, (i + turn) % size) for i in range(size)])
+
+
+def pick(values, index):
+    return lax.dynamic_index_in_dim(values, index, 0, keepdims=False)
+
+
+def spread_grp_first(values):
+    turns, peers = values.shape[:2]
+    seg, grp = lax.axis_index("seg"), lax.axis_index("grp")
+    near = []
+    for peer in range(peers):
+        mine = lax.dynamic_index_in_dim(values, grp ^ peer, 1, keepdims=False)
+        near.append(flip(mine, peer) if peer else mine)
+    far = []
+    for turn in range(turns):
+        mine = jnp.stack([pick(part, lax.rem(seg + turn, turns)) for part in near])
+        far.append(turn_by(mine, turn) if turn else mine)
+    return jnp.stack(far)
+
+
+def spread_seg_first(values):
+    turns, peers = values.shape[:2]
+    seg, grp = lax.axis_index("seg"), lax.axis_index("grp")
+    far = []
+    for turn in range(turns):
+        mine = pick(values, lax.rem(seg + turn, turns))
+        far.append(turn_by(mine, turn) if turn else mine)
+    near = []
+    for peer in range(peers):
+        mine = jnp.stack([pick(part, grp ^ peer) for part in far])
+        near.append(flip(mine, peer) if peer else mine)
+    return jnp.stack(near)
 
 
 def local(
@@ -270,7 +325,9 @@
         got = exchange(blocks).reshape(devices, held, block, ch).swapaxes(0, 1)
         return got.reshape(held, rows, cols, ch)
 
-    cot_blocks = to_pixels(cotangent)
+    segs, peers = lax.axis_size("seg"), lax.axis_size("grp")
+    here = jnp.stack([lax.axis_index("seg"), lax.axis_index("grp")]).astype(jnp.int32)
+    cot_blocks = spread_grp_first(cotangent.reshape(segs, peers, block, ch))
 
     spatial = [
         call(
@@ -309,11 +366,19 @@
         [pltpu.VMEM(whole, F32)],
         2 * 11 * frames * block * ch * ch,
         frames * block * ch * 18,
-        2,
-        (dilation, key_index, cot_blocks, temporal_weight, uniting_weight, slope0, slope1),
+        3,
+        (here, dilation, key_index, cot_blocks, temporal_weight, uniting_weight, slope0, slope1),
     )
     grad_time = to_frames(grad_blocks)
-    united = to_frames(united_blocks)
+    (united,) = call(
+        order_kernel,
+        [((devices, block, ch), BF16)],
+        [],
+        0,
+        pixels * ch * 4,
+        1,
+        (here, spread_seg_first(united_blocks.reshape(segs, peers, block, ch))),
+    )
     (tgrads,) = call(
         functools.partial(temporal_wgrad_kernel, step_frames),
         [((LAYERS * TAPS + 2, ch, ch), F32)],
@@ -336,14 +401,14 @@
         for i in range(held)
     ]
     scale = 1.0 / jnp.sqrt(jnp.float32(frames * pixels))
-    summed_time = reduce_everywhere(tgrads, devices) * scale
-    summed_space = reduce_everywhere(sum(grad for _, grad in back), devices) * scale
+    space_grads = sum(grad for _, grad in back)
+    summed = reduce_everywhere(jnp.concatenate([space_grads, tgrads]), devices) * scale
     return (
-        united,
+        united.reshape(frames_in.shape),
         jnp.stack([grad for grad, _ in back]),
-        summed_space,
-        summed_time[: LAYERS * TAPS].reshape(LAYERS, TAPS, ch, ch),
-        summed_time[LAYERS * TAPS :],
+        summed[:9],
+        summed[9 : 9 + LAYERS * TAPS].reshape(LAYERS, TAPS, ch, ch),
+        summed[9 + LAYERS * TAPS :],
     )
 
 

time: 245 us -> 191 us (0.78)
  blocking collectives: 159 us -> 0 us
  waiting for transfers between devices: 31.6 us -> 77.7 us
  starting transfers between devices: 11.3 us -> 54.4 us
  local copies, waits for them, and re-layouts: 12.8 us -> 26.5 us
    all_gather x2 -> x0, blocking collectives: 82.8 us -> none  [reduce_everywhere(): return lax.all_gather(mine, AXES, axis=0, tiled=True).reshape(count, ch, ch)]
    all_to_all x3 -> x0, blocking collectives: 76 us -> none  [exchange(): return lax.all_to_all(blocks, AXES, split_axis=0, concat_axis=0, tiled=True)]
    ppermute x0 -> x20, waiting for transfers between devices: none -> 57.8 us  [the longest x6 30.6 us: turn_by(): lax.ppermute(value, 'seg', [(i, (i + turn) % size) for i in range(size)])]
    ppermute x0 -> x20, starting transfers between devices: none -> 26.7 us  [the longest x14 16.6 us: flip(): return lax.ppermute(value, 'grp', [(i, i ^ peer) for i in range(size)])]
    all_to_all x3 -> x4, starting transfers between devices: 11.3 us -> 27.7 us  [exchange(): return lax.all_to_all(blocks, AXES, split_axis=0, concat_axis=0, tiled=True)]
    all_to_all x3 -> x4, waiting for transfers between devices: 31.6 us -> 19.8 us  [exchange(): return lax.all_to_all(blocks, AXES, split_axis=0, concat_axis=0, tiled=True)]
    unnamed x29 -> x69, local copies, waits for them, and re-layouts: 9.57 us -> 15.6 us
    dynamic_slice x0 -> x4, local copies, waits for them, and re-layouts: none -> 3.46 us  [pick(): return lax.dynamic_index_in_dim(values, index, 0, keepdims=False)]
  transfers between devices with their start and end apart: 3 -> 24, of which waited for: 2 -> 9; matrix products, arithmetic and copies ran while one was open for 1% -> 5% of each run, Pallas kernels for 5% -> 7%
where the time goes in v2:
time: 191 us; the launch traced here: 190 us
  waiting for transfers between devices  77.7 us (41%)
  starting transfers between devices  54.4 us (28%)
  Pallas kernels  29.8 us (16%)
  local copies, waits for them, and re-layouts  26.5 us (14%)
    ppermute x6, waiting for transfers between devices, turn_by(): lax.ppermute(value, 'seg', [(i, (i + turn) % size) for i in range(size)])  30.6 us
    pallas_call x6, Pallas kernels, call(): pl.pallas_call(kernel, out_shape=[jax.ShapeDtypeStruct(shape, kind) for s...  29.8 us
    all_to_all x4, starting transfers between devices, exchange(): return lax.all_to_all(blocks, AXES, split_axis=0, concat_axis=0, tiled=True)  27.7 us
    ppermute x14, waiting for transfers between devices, flip(): return lax.ppermute(value, 'grp', [(i, i ^ peer) for i in range(size)])  27.3 us
    all_to_all x4, waiting for transfers between devices, exchange(): return lax.all_to_all(blocks, AXES, split_axis=0, concat_axis=0, tiled=True)  19.8 us
    ppermute x14, starting transfers between devices, flip(): return lax.ppermute(value, 'grp', [(i, i ^ peer) for i in range(size)])  16.6 us
    unnamed x69, local copies, waits for them, and re-layouts  15.6 us
    ppermute x6, starting transfers between devices, turn_by(): lax.ppermute(value, 'seg', [(i, (i + turn) % size) for i in range(size)])  10.1 us
  transfers between devices with their start and end apart: 24, of which 9 were waited for; matrix products, arithmetic and copies ran while one was open for 5% of the time, Pallas kernels for 7%

profile of v2, /device:TPU:0, one launch (start us, length us, event | category | flops | bytes accessed | tf_op | source)
XLA Modules:
  0.0 190.3 jit_solution(12547117492516814457)
XLA Ops:
  0.6 1.2 copy-done.15
  1.8 1.0 copy-done.17
  2.8 3.2 %shard_map.110 = (bf16[32,120,128]{2,1,0:T(8,128)(2,1)}, f32[32,128,128]{2,1,0:T(8,128)S(1)}) custom-call(bf16[32,120,128]{2,1,0:T(8,128)(2,1)S(1)} %bitcast.84, bf16[9,128,128]{2,1,0:T(8,128)(2,1)S(1)} %copy-done.17), custom_call_target="tpu_custom_call" | custom-call | flops 1132462080 | bytes 3932160 | tf_op jit(solution)/shard_map/pallas_call | solution.py:52
  6.0 1.3 copy-done.19
  7.4 7.3 %all-to-all-start = ((bf16[32,120,128]{2,1,0:T(8,128)(2,1)}), bf16[32,120,128]{2,1,0:T(8,128)(2,1)S(1)}, u32[]{:S(2)}, u32[]{:S(2)}) async-start(bf16[32,120,128]{2,1,0:T(8,128)(2,1)} %get-tuple-element.20), calls=%async_computation | async-start | bytes 1966080 | tf_op jit(solution)/shard_map/all_to_all | solution.py:255
  15.8 2.5 %collective-permute-start.16 = (bf16[4,120,128]{2,1,0:T(8,128)(2,1)S(1)}, bf16[4,120,128]{2,1,0:T(8,128)(2,1)S(1)}, u32[]{:S(2)}, u32[]{:S(2)}) collective-permute-start(bf16[4,120,128]{2,1,0:T(8,128)(2,1)S(1)} %get-tuple-element.39), channel_id=1, source_target_pairs={{0,7},{1,6},{2,5},{3,4},{4,3},{5,2},{6,1},{7,0},{8,15},{9,14},{10,... | collective-permute-start | bytes 368648 | tf_op jit(solution)/shard_map/ppermute | solution.py:267
  18.7 1.5 collective-permute-start.11
  20.5 1.1 collective-permute-start.14
  21.7 13.4 %collective-permute-done.11 = bf16[4,120,128]{2,1,0:T(8,128)(2,1)S(1)} collective-permute-done((bf16[4,120,128]{2,1,0:T(8,128)(2,1)}, bf16[4,120,128]{2,1,0:T(8,128)(2,1)S(1)}, u32[]{:S(2)}, u32[]{:S(2)}) %collective-permute-start.11) | collective-permute-done | bytes 122912 | tf_op jit(solution)/shard_map/ppermute | solution.py:267
  35.1 1.3 collective-permute-start.13
  36.5 5.5 %collective-permute-done.13 = bf16[4,120,128]{2,1,0:T(8,128)(2,1)S(1)} collective-permute-done((bf16[4,120,128]{2,1,0:T(8,128)(2,1)}, bf16[4,120,128]{2,1,0:T(8,128)(2,1)S(1)}, u32[]{:S(2)}, u32[]{:S(2)}) %collective-permute-start.13) | collective-permute-done | bytes 122912 | tf_op jit(solution)/shard_map/ppermute | solution.py:267
  42.1 4.3 %collective-permute-start.19 = (bf16[8,120,128]{2,1,0:T(8,128)(2,1)S(1)}, bf16[8,120,128]{2,1,0:T(8,128)(2,1)S(1)}, u32[]{:S(2)}, u32[]{:S(2)}) collective-permute-start(bf16[8,120,128]{2,1,0:T(8,128)(2,1)S(1)} %get-tuple-element.82), channel_id=1, source_target_pairs={{0,24},{8,0},{16,8},{24,16},{1,25},{9,1},{17,9},{25,17},{2,26},{10... | collective-permute-start | bytes 737288 | tf_op jit(solution)/shard_map/ppermute | solution.py:272
  46.5 1.0 collective-permute-start.17
  47.6 5.3 %collective-permute-done.19 = bf16[8,120,128]{2,1,0:T(8,128)(2,1)S(1)} collective-permute-done((bf16[8,120,128]{2,1,0:T(8,128)(2,1)S(1)}, bf16[8,120,128]{2,1,0:T(8,128)(2,1)S(1)}, u32[]{:S(2)}, u32[]{:S(2)}) %collective-permute-start.19) | collective-permute-done | bytes 245792 | tf_op jit(solution)/shard_map/ppermute | solution.py:272
  52.9 14.3 %collective-permute-done.18 = bf16[8,120,128]{2,1,0:T(8,128)(2,1)S(1)} collective-permute-done((bf16[8,120,128]{2,1,0:T(8,128)(2,1)S(1)}, bf16[8,120,128]{2,1,0:T(8,128)(2,1)S(1)}, u32[]{:S(2)}, u32[]{:S(2)}) %collective-permute-start.18) | collective-permute-done | bytes 245792 | tf_op jit(solution)/shard_map/ppermute | solution.py:272
  67.3 0.9 copy-done.5
  68.3 1.2 copy-done.6
  69.5 6.6 %shard_map.111 = (bf16[32,120,128]{2,1,0:T(8,128)(2,1)S(1)}, bf16[64,128,128]{2,1,0:T(8,128)(2,1)S(1)}, bf16[64,128,128]{2,1,0:T(8,128)(2,1)}, bf16[32,128,128]{...) custom-call(s32[2]{0:T(128)S(1)} %copy-done.13, s32[4]{0:T(128)S(1)} %copy-done.14, ...), custom_call_target="tpu_custom_call" | custom-call | flops 1384120320 | bytes 8847360 | tf_op jit(solution)/shard_map/pallas_call | solution.py:52
  76.1 1.0 copy-done.1
  77.1 0.9 copy-done.8
  78.1 7.6 %shard_map.113 = (bf16[32,120,128]{2,1,0:T(8,128)(2,1)S(1)}, bf16[32,128,128]{2,1,0:T(8,128)(2,1)S(1)}, bf16[64,128,128]{2,1,0:T(8,128)(2,1)S(1)}, bf16[64,128,128]{2,1,0:T(8,128)(2,1)}, f32[4,128,128]{2,1,0:T(8,128)S(1)}) custom-call(s32[2]{0:T(128)S(1)} %pad_add_fusion.here_ref, s32[2]{0:T(128)S(1)} %copy-done.13, s32[4]{0:T(128)S(1)} %copy-done.14, ...), custom_call_target="tpu_custom_call" | custom-call | flops 1384120320 | bytes 8847360 | tf_op jit(solution)/shard_map/pallas_call | solution.py:52
  85.7 1.4 copy-done
  87.1 1.0 copy-done.3
  88.0 0.9 copy-done.7
  89.7 3.3 %all-to-all-start.1 = ((bf16[32,120,128]{2,1,0:T(8,128)(2,1)}), bf16[32,120,128]{2,1,0:T(8,128)(2,1)S(1)}, u32[]{:S(2)}, u32[]{:S(2)}) async-start(bf16[32,120,128]{2,1,0:T(8,128)(2,1)} %copy-done.7), calls=%async_computation.1 | async-start | bytes 1966080 | tf_op jit(solution)/shard_map/all_to_all | solution.py:255
  93.1 2.1 %dynamic-slice_bitcast_fusion.2 = (bf16[8,120,128]{2,1,0:T(8,128)(2,1)S(1)}, bf16[8,120,128]{2,1,0:T(8,128)(2,1)}, bf16[8,120,128]{2,1,0:T(8,128)(2,1)}) fusion(bf16[4,8,120,128]{3,2,1,0:T(8,128)(2,1)} %bitcast.82, s32[]{:T(128)S(6)} %select_n.132, s32[]{:T(128)S(6)} %select_n.134, s32[]{:T(128)S(6)} %select_n.133), kind=kLoop, calls=%fused_computation.5 | loop fusion | bytes 1474572 | tf_op jit(solution)/shard_map/jit(dynamic_index_in_dim)/squeeze | solution.py:276
  95.2 1.8 collective-permute-start
  96.9 2.1 %collective-permute-start.2 = (bf16[8,120,128]{2,1,0:T(8,128)(2,1)}, bf16[8,120,128]{2,1,0:T(8,128)(2,1)}, u32[]{:S(2)}, u32[]{:S(2)}) collective-permute-start(bf16[8,120,128]{2,1,0:T(8,128)(2,1)} %get-tuple-element.55), channel_id=1, source_target_pairs={{0,24},{8,0},{16,8},{24,16},{1,25},{9,1},{17,9},{25,17},{2,26},{10... | collective-permute-start | bytes 737288 | tf_op jit(solution)/shard_map/ppermute | solution.py:272
  99.9 1.2 copy-done.2
  101.1 6.1 %shard_map.115 = f32[12,128,128]{2,1,0:T(8,128)S(1)} custom-call(s32[2]{0:T(128)S(1)} %copy-done.13, s32[4]{0:T(128)S(1)} %copy-done.14, bf16[64,128,128]{2,1,0:T(8,128)(2,1)S(1)} %get-tuple-element.28.a0, bf16[64,128,128]{2,1,0:T(8,128)(2,1)} %get-tuple-element.29.a1, bf16[32,128,128]{2,1,0:T(8,128)(2,1)S(1)} %copy-done.2, bf16[64,128,128]{2,1,0:T(8,128)(2,1)} %copy-done, ...), custom_call_target="tpu_custom_call" | custom-call | flops 1509949440 | bytes 6881280 | tf_op jit(solution)/shard_map/pallas_call | solution.py:52
  107.3 1.0 dynamic-slice_bitcast_fusion.10
  108.3 10.9 %collective-permute-done = bf16[8,120,128]{2,1,0:T(8,128)(2,1)S(1)} collective-permute-done((bf16[8,120,128]{2,1,0:T(8,128)(2,1)S(1)}, bf16[8,120,128]{2,1,0:T(8,128)(2,1)S(1)}, u32[]{:S(2)}, u32[]{:S(2)}) %collective-permute-start) | collective-permute-done | bytes 245792 | tf_op jit(solution)/shard_map/ppermute | solution.py:272
  119.9 3.7 %all-to-all-done.1.grad_ref = bf16[32,120,128]{2,1,0:T(8,128)(2,1)S(1)} async-done(((bf16[32,120,128]{2,1,0:T(8,128)(2,1)}), bf16[32,120,128]{2,1,0:T(8,128)(2,1)S(1)}, u32[]{:S(2)}, u32[]{:S(2)}) %all-to-all-start.1) | async-done | bytes 983072 | tf_op jit(solution)/shard_map/all_to_all | solution.py:255
  123.6 1.6 copy-done.20
  125.2 4.7 %shard_map.114 = (bf16[32,120,128]{2,1,0:T(8,128)(2,1)}, f32[9,128,128]{2,1,0:T(8,128)S(1)}) custom-call(bf16[32,120,128]{2,1,0:T(8,128)(2,1)S(1)} %bitcast.85, bf16[9,128,128]{2,1,0:T(8,128)(2,1)S(1)} %copy-done.18, bf16[32,120,128]{2,1,0:T(8,128)(2,1)S(1)} %all-to-all-done.1.grad_ref, f32[32,128,128]{2,1,0:T(8,128)S(1)} %copy-done.20), custom_call_target="tpu_custom_call" | custom-call | flops 2264924160 | bytes 4915200 | tf_op jit(solution)/shard_map/pallas_call | solution.py:52
  130.0 1.0 convert_element_type.11
  131.0 13.5 %all-to-all-start.2 = ((bf16[32,84,128]{2,1,0:T(8,128)(2,1)}), bf16[32,84,128]{2,1,0:T(8,128)(2,1)S(1)}, u32[]{:S(2)}, u32[]{:S(2)}) async-start(bf16[32,84,128]{2,1,0:T(8,128)(2,1)} %convert_element_type.11), calls=%async_computation.2 | async-start | bytes 1441792 | tf_op jit(solution)/shard_map/all_to_all | solution.py:255
  146.7 1.7 collective-permute-start.4
  148.6 1.7 collective-permute-start.6
  150.7 2.6 %collective-permute-start.8 = (bf16[4,120,128]{2,1,0:T(8,128)(2,1)S(1)}, bf16[4,120,128]{2,1,0:T(8,128)(2,1)}, u32[]{:S(2)}, u32[]{:S(2)}) collective-permute-start(bf16[4,120,128]{2,1,0:T(8,128)(2,1)S(1)} %pad_maximum_fusion.7), channel_id=1, source_target_pairs={{0,6},{1,7},{2,4},{3,5},{4,2},{5,3},{6,0},{7,1},{8,14},{9,15},{10,... | collective-permute-start | bytes 368648 | tf_op jit(solution)/shard_map/ppermute | solution.py:267
  153.3 10.5 %all-to-all-done.2 = bf16[32,84,128]{2,1,0:T(8,128)(2,1)S(1)} async-done(((bf16[32,84,128]{2,1,0:T(8,128)(2,1)}), bf16[32,84,128]{2,1,0:T(8,128)(2,1)S(1)}, u32[]{:S(2)}, u32[]{:S(2)}) %all-to-all-start.2) | async-done | bytes 688160 | tf_op jit(solution)/shard_map/all_to_all | solution.py:255
  164.0 1.0 broadcast_in_dim.3
  165.0 3.5 %all-to-all-start.3 = ((bf16[32,84,128]{2,1,0:T(8,128)(2,1)}), bf16[32,84,128]{2,1,0:T(8,128)(2,1)S(1)}, u32[]{:S(2)}, u32[]{:S(2)}) async-start(bf16[32,84,128]{2,1,0:T(8,128)(2,1)} %broadcast_in_dim.3), calls=%async_computation.3 | async-start | bytes 1441792 | tf_op jit(solution)/shard_map/all_to_all | solution.py:255
  168.5 2.5 %collective-permute-start.9 = (bf16[4,120,128]{2,1,0:T(8,128)(2,1)S(1)}, bf16[4,120,128]{2,1,0:T(8,128)(2,1)S(1)}, u32[]{:S(2)}, u32[]{:S(2)}) collective-permute-start(bf16[4,120,128]{2,1,0:T(8,128)(2,1)S(1)} %pad_maximum_fusion.8), channel_id=1, source_target_pairs={{0,7},{1,6},{2,5},{3,4},{4,3},{5,2},{6,1},{7,0},{8,15},{9,14},{10,... | collective-permute-start | bytes 368648 | tf_op jit(solution)/shard_map/ppermute | solution.py:267
  171.1 0.9 bitcast_dynamic-update-slice_fusion.1
  172.0 8.4 %collective-permute-done.9 = bf16[4,120,128]{2,1,0:T(8,128)(2,1)S(1)} collective-permute-done((bf16[4,120,128]{2,1,0:T(8,128)(2,1)S(1)}, bf16[4,120,128]{2,1,0:T(8,128)(2,1)S(1)}, u32[]{:S(2)}, u32[]{:S(2)}) %collective-permute-start.9) | collective-permute-done | bytes 122912 | tf_op jit(solution)/shard_map/ppermute | solution.py:267
  180.4 1.6 shard_map.112
  182.0 5.7 %all-to-all-done.3 = bf16[32,84,128]{2,1,0:T(8,128)(2,1)S(1)} async-done(((bf16[32,84,128]{2,1,0:T(8,128)(2,1)}), bf16[32,84,128]{2,1,0:T(8,128)(2,1)S(1)}, u32[]{:S(2)}, u32[]{:S(2)}) %all-to-all-start.3) | async-done | bytes 688160 | tf_op jit(solution)/shard_map/all_to_all | solution.py:255
  (104 shorter events, 10.1 us)
Async XLA Ops:
  0.6 1.2 copy-start.15
  1.8 1.0 copy-start.17
  2.8 11.9 %copy-start.21 = (bf16[1,32,120,128]{3,2,1,0:T(8,128)(2,1)S(1)}, bf16[1,32,120,128]{3,2,1,0:T(8,128)(2,1)}, u32[]{:S(2)}) copy-start(bf16[1,32,120,128]{3,2,1,0:T(8,128)(2,1)} %param.13) | copy-start | bytes 2949124
  6.0 1.3 copy-start.19
  7.4 60.0 %all-to-all-start = ((bf16[32,120,128]{2,1,0:T(8,128)(2,1)}), bf16[32,120,128]{2,1,0:T(8,128)(2,1)S(1)}, u32[]{:S(2)}, u32[]{:S(2)}) async-start(bf16[32,120,128]{2,1,0:T(8,128)(2,1)} %get-tuple-element.20), calls=%async_computation | async-start | bytes 1966080 | tf_op jit(solution)/shard_map/all_to_all | solution.py:255
  15.5 52.8 %copy-start.9 = (bf16[2,5,128,128]{3,2,1,0:T(8,128)(2,1)S(1)}, bf16[2,5,128,128]{3,2,1,0:T(8,128)(2,1)}, u32[]{:S(2)}) copy-start(bf16[2,5,128,128]{3,2,1,0:T(8,128)(2,1)} %tw_ref.3) | copy-start | bytes 983044
  15.5 52.8 %copy-start.12 = (bf16[2,128,128]{2,1,0:T(8,128)(2,1)S(1)}, bf16[2,128,128]{2,1,0:T(8,128)(2,1)}, u32[]{:S(2)}) copy-start(bf16[2,128,128]{2,1,0:T(8,128)(2,1)} %uw_ref.3) | copy-start | bytes 196612
  15.5 52.8 %copy-start.13 = (s32[2]{0:T(128)S(1)}, s32[2]{0:T(128)}, u32[]{:S(2)}) copy-start(s32[2]{0:T(128)} %dil_ref.5) | copy-start | bytes 28
  15.5 52.8 %copy-start.14 = (s32[4]{0:T(128)S(1)}, s32[4]{0:T(128)}, u32[]{:S(2)}) copy-start(s32[4]{0:T(128)} %key_ref.5) | copy-start | bytes 52
  15.5 5.0 %collective-permute-start.10 = (bf16[4,120,128]{2,1,0:T(8,128)(2,1)S(1)}, bf16[4,120,128]{2,1,0:T(8,128)(2,1)S(1)}, u32[]{:S(2)}, u32[]{:S(2)}) collective-permute-start(bf16[4,120,128]{2,1,0:T(8,128)(2,1)S(1)} %get-tuple-element.42), channel_id=1, source_target_pairs={{0,1},{1,0},{2,3},{3,2},{4,5},{5,4},{6,7},{7,6},{8,9},{9,8},{10,11... | collective-permute-start | bytes 368648 | tf_op jit(solution)/shard_map/ppermute | solution.py:267
  15.8 26.3 %collective-permute-start.16 = (bf16[4,120,128]{2,1,0:T(8,128)(2,1)S(1)}, bf16[4,120,128]{2,1,0:T(8,128)(2,1)S(1)}, u32[]{:S(2)}, u32[]{:S(2)}) collective-permute-start(bf16[4,120,128]{2,1,0:T(8,128)(2,1)S(1)} %get-tuple-element.39), channel_id=1, source_target_pairs={{0,7},{1,6},{2,5},{3,4},{4,3},{5,2},{6,1},{7,0},{8,15},{9,14},{10,... | collective-permute-start | bytes 368648 | tf_op jit(solution)/shard_map/ppermute | solution.py:267
  18.4 18.1 %collective-permute-start.12 = (bf16[4,120,128]{2,1,0:T(8,128)(2,1)}, bf16[4,120,128]{2,1,0:T(8,128)(2,1)S(1)}, u32[]{:S(2)}, u32[]{:S(2)}) collective-permute-start(bf16[4,120,128]{2,1,0:T(8,128)(2,1)} %get-tuple-element.40), channel_id=1, source_target_pairs={{0,3},{1,2},{2,1},{3,0},{4,7},{5,6},{6,5},{7,4},{8,11},{9,10},{10,... | collective-permute-start | bytes 368648 | tf_op jit(solution)/shard_map/ppermute | solution.py:267
  18.7 16.4 %collective-permute-start.11 = (bf16[4,120,128]{2,1,0:T(8,128)(2,1)}, bf16[4,120,128]{2,1,0:T(8,128)(2,1)S(1)}, u32[]{:S(2)}, u32[]{:S(2)}) collective-permute-start(bf16[4,120,128]{2,1,0:T(8,128)(2,1)} %get-tuple-element.41), channel_id=1, source_target_pairs={{0,2},{1,3},{2,0},{3,1},{4,6},{5,7},{6,4},{7,5},{8,10},{9,11},{10,... | collective-permute-start | bytes 368648 | tf_op jit(solution)/shard_map/ppermute | solution.py:267
  20.2 21.9 %collective-permute-start.15 = (bf16[4,120,128]{2,1,0:T(8,128)(2,1)S(1)}, bf16[4,120,128]{2,1,0:T(8,128)(2,1)S(1)}, u32[]{:S(2)}, u32[]{:S(2)}) collective-permute-start(bf16[4,120,128]{2,1,0:T(8,128)(2,1)S(1)} %get-tuple-element.43), channel_id=1, source_target_pairs={{0,6},{1,7},{2,4},{3,5},{4,2},{5,3},{6,0},{7,1},{8,14},{9,15},{10,... | collective-permute-start | bytes 368648 | tf_op jit(solution)/shard_map/ppermute | solution.py:267
  20.5 21.5 %collective-permute-start.14 = (bf16[4,120,128]{2,1,0:T(8,128)(2,1)S(1)}, bf16[4,120,128]{2,1,0:T(8,128)(2,1)S(1)}, u32[]{:S(2)}, u32[]{:S(2)}) collective-permute-start(bf16[4,120,128]{2,1,0:T(8,128)(2,1)S(1)} %get-tuple-element.44), channel_id=1, source_target_pairs={{0,5},{1,4},{2,7},{3,6},{4,1},{5,0},{6,3},{7,2},{8,13},{9,12},{10,... | collective-permute-start | bytes 368648 | tf_op jit(solution)/shard_map/ppermute | solution.py:267
  35.1 6.9 %collective-permute-start.13 = (bf16[4,120,128]{2,1,0:T(8,128)(2,1)}, bf16[4,120,128]{2,1,0:T(8,128)(2,1)S(1)}, u32[]{:S(2)}, u32[]{:S(2)}) collective-permute-start(bf16[4,120,128]{2,1,0:T(8,128)(2,1)} %get-tuple-element.45), channel_id=1, source_target_pairs={{0,4},{1,5},{2,6},{3,7},{4,0},{5,1},{6,2},{7,3},{8,12},{9,13},{10,... | collective-permute-start | bytes 368648 | tf_op jit(solution)/shard_map/ppermute | solution.py:267
  42.1 10.8 %collective-permute-start.19 = (bf16[8,120,128]{2,1,0:T(8,128)(2,1)S(1)}, bf16[8,120,128]{2,1,0:T(8,128)(2,1)S(1)}, u32[]{:S(2)}, u32[]{:S(2)}) collective-permute-start(bf16[8,120,128]{2,1,0:T(8,128)(2,1)S(1)} %get-tuple-element.82), channel_id=1, source_target_pairs={{0,24},{8,0},{16,8},{24,16},{1,25},{9,1},{17,9},{25,17},{2,26},{10... | collective-permute-start | bytes 737288 | tf_op jit(solution)/shard_map/ppermute | solution.py:272
  46.5 20.7 %collective-permute-start.18 = (bf16[8,120,128]{2,1,0:T(8,128)(2,1)S(1)}, bf16[8,120,128]{2,1,0:T(8,128)(2,1)S(1)}, u32[]{:S(2)}, u32[]{:S(2)}) collective-permute-start(bf16[8,120,128]{2,1,0:T(8,128)(2,1)S(1)} %get-tuple-element.83), channel_id=1, source_target_pairs={{0,16},{8,24},{16,0},{24,8},{1,17},{9,25},{17,1},{25,9},{2,18},{10... | collective-permute-start | bytes 737288 | tf_op jit(solution)/shard_map/ppermute | solution.py:272
  46.5 20.7 %collective-permute-start.17 = (bf16[8,120,128]{2,1,0:T(8,128)(2,1)S(1)}, bf16[8,120,128]{2,1,0:T(8,128)(2,1)S(1)}, u32[]{:S(2)}, u32[]{:S(2)}) collective-permute-start(bf16[8,120,128]{2,1,0:T(8,128)(2,1)S(1)} %get-tuple-element.84), channel_id=1, source_target_pairs={{0,8},{8,16},{16,24},{24,0},{1,9},{9,17},{17,25},{25,1},{2,10},{10... | collective-permute-start | bytes 737288 | tf_op jit(solution)/shard_map/ppermute | solution.py:272
  68.3 1.2 copy-start.6
  76.1 1.0 copy-start.1
  85.7 1.4 copy-start
  87.1 1.0 copy-start.3
  89.7 10.2 %copy-start.11 = (f32[4,128,128]{2,1,0:T(8,128)S(1)}, f32[4,128,128]{2,1,0:T(8,128)}, u32[]{:S(2)}) copy-start(f32[4,128,128]{2,1,0:T(8,128)} %copy-done.10) | copy-start | bytes 786436
  89.7 33.9 %all-to-all-start.1 = ((bf16[32,120,128]{2,1,0:T(8,128)(2,1)}), bf16[32,120,128]{2,1,0:T(8,128)(2,1)S(1)}, u32[]{:S(2)}, u32[]{:S(2)}) async-start(bf16[32,120,128]{2,1,0:T(8,128)(2,1)} %copy-done.7), calls=%async_computation.1 | async-start | bytes 1966080 | tf_op jit(solution)/shard_map/all_to_all | solution.py:255
  93.1 6.8 %copy-start.4 = (bf16[32,128,128]{2,1,0:T(8,128)(2,1)S(1)}, bf16[32,128,128]{2,1,0:T(8,128)(2,1)}, u32[]{:S(2)}) copy-start(bf16[32,128,128]{2,1,0:T(8,128)(2,1)} %copy-done.3) | copy-start | bytes 3145732
  95.2 24.1 %collective-permute-start = (bf16[8,120,128]{2,1,0:T(8,128)(2,1)S(1)}, bf16[8,120,128]{2,1,0:T(8,128)(2,1)S(1)}, u32[]{:S(2)}, u32[]{:S(2)}) collective-permute-start(bf16[8,120,128]{2,1,0:T(8,128)(2,1)S(1)} %get-tuple-element.54), channel_id=1, source_target_pairs={{0,8},{8,16},{16,24},{24,0},{1,9},{9,17},{17,25},{25,1},{2,10},{10... | collective-permute-start | bytes 737288 | tf_op jit(solution)/shard_map/ppermute | solution.py:272
  96.9 47.6 %collective-permute-start.2 = (bf16[8,120,128]{2,1,0:T(8,128)(2,1)}, bf16[8,120,128]{2,1,0:T(8,128)(2,1)}, u32[]{:S(2)}, u32[]{:S(2)}) collective-permute-start(bf16[8,120,128]{2,1,0:T(8,128)(2,1)} %get-tuple-element.55), channel_id=1, source_target_pairs={{0,24},{8,0},{16,8},{24,16},{1,25},{9,1},{17,9},{25,17},{2,26},{10... | collective-permute-start | bytes 737288 | tf_op jit(solution)/shard_map/ppermute | solution.py:272
  99.0 46.5 %collective-permute-start.1 = (bf16[8,120,128]{2,1,0:T(8,128)(2,1)}, bf16[8,120,128]{2,1,0:T(8,128)(2,1)}, u32[]{:S(2)}, u32[]{:S(2)}) collective-permute-start(bf16[8,120,128]{2,1,0:T(8,128)(2,1)} %get-tuple-element.56), channel_id=1, source_target_pairs={{0,16},{8,24},{16,0},{24,8},{1,17},{9,25},{17,1},{25,9},{2,18},{10... | collective-permute-start | bytes 737288 | tf_op jit(solution)/shard_map/ppermute | solution.py:272
  99.9 1.2 copy-start.2
  107.3 16.3 %copy-start.16 = (bf16[1,32,120,128]{3,2,1,0:T(8,128)(2,1)S(1)}, bf16[1,32,120,128]{3,2,1,0:T(8,128)(2,1)}, u32[]{:S(2)}) copy-start(bf16[1,32,120,128]{3,2,1,0:T(8,128)(2,1)} %param.7) | copy-start | bytes 2949124
  107.3 16.3 %copy-start.18 = (bf16[9,128,128]{2,1,0:T(8,128)(2,1)S(1)}, bf16[9,128,128]{2,1,0:T(8,128)(2,1)}, u32[]{:S(2)}) copy-start(bf16[9,128,128]{2,1,0:T(8,128)(2,1)} %w_ref.3) | copy-start | bytes 884740
  123.6 1.6 copy-start.20
  130.0 16.8 %copy-start.27 = (bf16[1,120,128]{2,1,0:T(8,128)(2,1)S(1)}, bf16[1,120,128]{2,1,0:T(8,128)(2,1)}, u32[]{:S(2)}) copy-start(bf16[1,120,128]{2,1,0:T(8,128)(2,1)} %get-tuple-element.62) | copy-start | bytes 92164
  130.0 18.5 %copy-start.26 = (bf16[1,120,128]{2,1,0:T(8,128)(2,1)S(1)}, bf16[1,120,128]{2,1,0:T(8,128)(2,1)}, u32[]{:S(2)}) copy-start(bf16[1,120,128]{2,1,0:T(8,128)(2,1)} %get-tuple-element.61) | copy-start | bytes 92164
  130.0 18.6 %copy-start.25 = (bf16[1,120,128]{2,1,0:T(8,128)(2,1)S(1)}, bf16[1,120,128]{2,1,0:T(8,128)(2,1)}, u32[]{:S(2)}) copy-start(bf16[1,120,128]{2,1,0:T(8,128)(2,1)} %get-tuple-element.60) | copy-start | bytes 92164
  130.0 20.4 %copy-start.24 = (bf16[1,120,128]{2,1,0:T(8,128)(2,1)S(1)}, bf16[1,120,128]{2,1,0:T(8,128)(2,1)}, u32[]{:S(2)}) copy-start(bf16[1,120,128]{2,1,0:T(8,128)(2,1)} %get-tuple-element.59) | copy-start | bytes 92164
  131.0 19.6 %copy-start.23 = (bf16[1,120,128]{2,1,0:T(8,128)(2,1)S(1)}, bf16[1,120,128]{2,1,0:T(8,128)(2,1)}, u32[]{:S(2)}) copy-start(bf16[1,120,128]{2,1,0:T(8,128)(2,1)} %get-tuple-element.57) | copy-start | bytes 92164
  131.0 19.6 %copy-start.22 = (bf16[1,120,128]{2,1,0:T(8,128)(2,1)S(1)}, bf16[1,120,128]{2,1,0:T(8,128)(2,1)}, u32[]{:S(2)}) copy-start(bf16[1,120,128]{2,1,0:T(8,128)(2,1)} %get-tuple-element.58) | copy-start | bytes 92164
  131.0 32.9 %all-to-all-start.2 = ((bf16[32,84,128]{2,1,0:T(8,128)(2,1)}), bf16[32,84,128]{2,1,0:T(8,128)(2,1)S(1)}, u32[]{:S(2)}, u32[]{:S(2)}) async-start(bf16[32,84,128]{2,1,0:T(8,128)(2,1)} %convert_element_type.11), calls=%async_computation.2 | async-start | bytes 1441792 | tf_op jit(solution)/shard_map/all_to_all | solution.py:255
  146.4 4.3 %collective-permute-start.3 = (bf16[4,120,128]{2,1,0:T(8,128)(2,1)S(1)}, bf16[4,120,128]{2,1,0:T(8,128)(2,1)S(1)}, u32[]{:S(2)}, u32[]{:S(2)}) collective-permute-start(bf16[4,120,128]{2,1,0:T(8,128)(2,1)S(1)} %pad_maximum_fusion.2), channel_id=1, source_target_pairs={{0,1},{1,0},{2,3},{3,2},{4,5},{5,4},{6,7},{7,6},{8,9},{9,8},{10,11... | collective-permute-start | bytes 368648 | tf_op jit(solution)/shard_map/ppermute | solution.py:267
  146.7 21.7 %collective-permute-start.4 = (bf16[4,120,128]{2,1,0:T(8,128)(2,1)S(1)}, bf16[4,120,128]{2,1,0:T(8,128)(2,1)S(1)}, u32[]{:S(2)}, u32[]{:S(2)}) collective-permute-start(bf16[4,120,128]{2,1,0:T(8,128)(2,1)S(1)} %pad_maximum_fusion.3), channel_id=1, source_target_pairs={{0,2},{1,3},{2,0},{3,1},{4,6},{5,7},{6,4},{7,5},{8,10},{9,11},{10,... | collective-permute-start | bytes 368648 | tf_op jit(solution)/shard_map/ppermute | solution.py:267
  148.5 22.5 %collective-permute-start.5 = (bf16[4,120,128]{2,1,0:T(8,128)(2,1)S(1)}, bf16[4,120,128]{2,1,0:T(8,128)(2,1)S(1)}, u32[]{:S(2)}, u32[]{:S(2)}) collective-permute-start(bf16[4,120,128]{2,1,0:T(8,128)(2,1)S(1)} %pad_maximum_fusion.4), channel_id=1, source_target_pairs={{0,3},{1,2},{2,1},{3,0},{4,7},{5,6},{6,5},{7,4},{8,11},{9,10},{10,... | collective-permute-start | bytes 368648 | tf_op jit(solution)/shard_map/ppermute | solution.py:267
  148.6 22.4 %collective-permute-start.6 = (bf16[4,120,128]{2,1,0:T(8,128)(2,1)S(1)}, bf16[4,120,128]{2,1,0:T(8,128)(2,1)S(1)}, u32[]{:S(2)}, u32[]{:S(2)}) collective-permute-start(bf16[4,120,128]{2,1,0:T(8,128)(2,1)S(1)} %pad_maximum_fusion.5), channel_id=1, source_target_pairs={{0,4},{1,5},{2,6},{3,7},{4,0},{5,1},{6,2},{7,3},{8,12},{9,13},{10,... | collective-permute-start | bytes 368648 | tf_op jit(solution)/shard_map/ppermute | solution.py:267
  150.4 20.7 %collective-permute-start.7 = (bf16[4,120,128]{2,1,0:T(8,128)(2,1)S(1)}, bf16[4,120,128]{2,1,0:T(8,128)(2,1)S(1)}, u32[]{:S(2)}, u32[]{:S(2)}) collective-permute-start(bf16[4,120,128]{2,1,0:T(8,128)(2,1)S(1)} %pad_maximum_fusion.6), channel_id=1, source_target_pairs={{0,5},{1,4},{2,7},{3,6},{4,1},{5,0},{6,3},{7,2},{8,13},{9,12},{10,... | collective-permute-start | bytes 368648 | tf_op jit(solution)/shard_map/ppermute | solution.py:267
  150.7 20.4 %collective-permute-start.8 = (bf16[4,120,128]{2,1,0:T(8,128)(2,1)S(1)}, bf16[4,120,128]{2,1,0:T(8,128)(2,1)}, u32[]{:S(2)}, u32[]{:S(2)}) collective-permute-start(bf16[4,120,128]{2,1,0:T(8,128)(2,1)S(1)} %pad_maximum_fusion.7), channel_id=1, source_target_pairs={{0,6},{1,7},{2,4},{3,5},{4,2},{5,3},{6,0},{7,1},{8,14},{9,15},{10,... | collective-permute-start | bytes 368648 | tf_op jit(solution)/shard_map/ppermute | solution.py:267
  165.0 22.7 %all-to-all-start.3 = ((bf16[32,84,128]{2,1,0:T(8,128)(2,1)}), bf16[32,84,128]{2,1,0:T(8,128)(2,1)S(1)}, u32[]{:S(2)}, u32[]{:S(2)}) async-start(bf16[32,84,128]{2,1,0:T(8,128)(2,1)} %broadcast_in_dim.3), calls=%async_computation.3 | async-start | bytes 1441792 | tf_op jit(solution)/shard_map/all_to_all | solution.py:255
  168.5 11.9 %collective-permute-start.9 = (bf16[4,120,128]{2,1,0:T(8,128)(2,1)S(1)}, bf16[4,120,128]{2,1,0:T(8,128)(2,1)S(1)}, u32[]{:S(2)}, u32[]{:S(2)}) collective-permute-start(bf16[4,120,128]{2,1,0:T(8,128)(2,1)S(1)} %pad_maximum_fusion.8), channel_id=1, source_target_pairs={{0,7},{1,6},{2,5},{3,4},{4,3},{5,2},{6,1},{7,0},{8,15},{9,14},{10,... | collective-permute-start | bytes 368648 | tf_op jit(solution)/shard_map/ppermute | solution.py:267
  (4 other events, 3.5 us)

commit v3 on v1

v3 whole, which is shorter than its diff:
```python
import functools

import jax
import jax.numpy as jnp
from jax import lax
from jax.experimental import pallas as pl
from jax.experimental.pallas import tpu as pltpu
from jax.sharding import PartitionSpec as P

LAYERS = 2
TAPS = 5
DMAX = 8
HALO = 2 * DMAX
AXES = ("seg", "grp")
BF16 = jnp.bfloat16
F32 = jnp.float32
VMEM_LIMIT = 32 * 1024 * 1024


def round_up(value, step):
    return -(-value // step) * step


def silu_parts(value):
    sigma = 0.5 * jnp.tanh(0.5 * value) + 0.5
    act = value * sigma
    return act, sigma + act * (1.0 - sigma)


def mm(left, right):
    return jnp.dot(left, right, preferred_element_type=F32)


def mm_nt(left, right):
    return lax.dot_general(left, right, (((1,), (1,)), ((), ())), preferred_element_type=F32)


def mm_tn(left, right):
    return lax.dot_general(left, right, (((0,), (0,)), ((), ())), preferred_element_type=F32)


def three_parts(value):
    high = value.astype(BF16)
    rest = value - high.astype(F32)
    middle = rest.astype(BF16)
    return high, middle, (rest - middle.astype(F32)).astype(BF16)


def call(kernel, outs, scratch, flops, moved, smem, args):
    specs = [pl.BlockSpec(memory_space=pltpu.SMEM)] * smem
    specs += [pl.BlockSpec(memory_space=pltpu.VMEM)] * (len(args) - smem)
    return pl.pallas_call(
        kernel,
        out_shape=[jax.ShapeDtypeStruct(shape, kind) for shape, kind in outs],
        in_specs=specs,
        out_specs=[pl.BlockSpec(memory_space=pltpu.VMEM)] * len(outs),
        scratch_shapes=scratch,
        compiler_params=pltpu.CompilerParams(vmem_limit_bytes=VMEM_LIMIT),
        cost_estimate=pl.CostEstimate(flops=flops, bytes_accessed=moved, transcendentals=0),
    )(*args)


def roll_rows(value, shift):
    return pltpu.roll(value, shift % value.shape[0], 0)


def spatial_fwd_kernel(rows_step, x_ref, w_ref, cot_ref, send_ref, slope_ref, xs):
    rows, cols, ch = x_ref.shape
    wide = xs.shape[1]
    send_ref[:, 1] = cot_ref[...]
    xs[...] = jnp.zeros(xs.shape, xs.dtype)
    xs[1 : rows + 1, :cols, :] = x_ref[...]
    weight = jnp.concatenate(
        [jnp.concatenate([w_ref[3 * a + b] for b in range(3)], axis=1) for a in range(3)], axis=0
    )
    flat = rows_step * wide
    for step in range(rows // rows_step):
        at = step * rows_step
        left = jnp.concatenate(
            [xs[at + a : at + a + rows_step].reshape(flat, ch) for a in range(3)], axis=1
        )
        y = mm(left, weight)
        pre = y[:, ch : 2 * ch] + roll_rows(y[:, :ch], 1) + roll_rows(y[:, 2 * ch :], -1)
        act, slope = silu_parts(pre)
        send_ref[at : at + rows_step, 0] = act.astype(BF16).reshape(rows_step, wide, ch)[:, :cols]
        slope_ref[at : at + rows_step] = slope.reshape(rows_step, wide, ch)


def columns_kernel(rows_step, x_ref, cat_ref):
    rows, cols, ch = x_ref.shape
    wide = cat_ref.shape[0] // rows
    flat = rows_step * wide
    pad = jnp.zeros((rows_step, wide - cols, ch), F32)
    for at in range(0, rows, rows_step):
        x = jnp.concatenate([x_ref[at : at + rows_step].astype(F32), pad], axis=1).reshape(flat, ch)
        x_cat = jnp.concatenate([roll_rows(x, 1), x, roll_rows(x, -1)], axis=1)
        cat_ref[at * wide : at * wide + flat] = x_cat.astype(BF16)


def taps_up(gs, at, rows_step):
    wide, ch = gs.shape[1:]
    return jnp.concatenate(
        [gs[at + 2 - a : at + 2 - a + rows_step].reshape(rows_step * wide, ch) for a in range(3)],
        axis=1,
    )


def spatial_wgrad_kernel(rows_step, scale, got_ref, slope_ref, cat_ref, gs, united_ref, wgrad_ref):
    rows, _, cols, ch = got_ref.shape
    wide = gs.shape[1]
    gs[...] = jnp.zeros(gs.shape, gs.dtype)
    gs[1 : rows + 1, :cols, :] = (
        got_ref[:, 0].astype(F32) * slope_ref[:, :cols, :]
    ).astype(BF16)
    flat = rows_step * wide
    total = jnp.zeros((3 * ch, 3 * ch), F32)
    for at in range(0, rows, rows_step):
        total = total + mm_tn(cat_ref[at * wide : at * wide + flat], taps_up(gs, at, rows_step))
    for a in range(3):
        for b in range(3):
            piece = total[b * ch : (b + 1) * ch, a * ch : (a + 1) * ch] * scale
            wgrad_ref[3 * a + b] = piece.astype(wgrad_ref.dtype)
    united_ref[...] = got_ref[:, 1]


def spatial_back_kernel(rows_step, w_ref, gs, back_ref):
    rows, cols, ch = back_ref.shape
    wide = gs.shape[1]
    weight = jnp.concatenate(
        [
            jnp.concatenate([w_ref[3 * a + b].astype(F32).T.astype(BF16) for b in range(3)], axis=1)
            for a in range(3)
        ],
        axis=0,
    )
    for at in range(0, rows, rows_step):
        y = mm(taps_up(gs, at, rows_step), weight)
        back = y[:, ch : 2 * ch] + roll_rows(y[:, :ch], -1) + roll_rows(y[:, 2 * ch :], 1)
        back_ref[at : at + rows_step] = back.astype(BF16).reshape(rows_step, wide, ch)[:, :cols]


def clear_halo(pad_ref, frames):
    zeros = jnp.zeros((HALO,) + pad_ref.shape[1:], pad_ref.dtype)
    pad_ref[:HALO] = zeros
    pad_ref[HALO + frames :] = zeros


def taps_of(pad_ref, at, count, step_size, sign):
    high, ch = pad_ref.shape[1:]
    pieces = [
        pad_ref[pl.ds(HALO + at + sign * (k - 2) * step_size, count)].reshape(count * high, ch)
        for k in range(TAPS)
    ]
    return jnp.concatenate(pieces, axis=1)


def temporal_kernel(
    step_frames, dil_ref, key_ref, got_ref, tw_ref, uw_ref,
    send_ref, a0, a1, feat, cots, g0, g1, seg_cot, slope0, slope1, grad_feat,
):
    frames, _, block, ch = got_ref.shape
    high = feat.shape[1]
    segs = key_ref.shape[0]
    seg_frames = frames // segs
    for ref in (a0, a1, g0, g1):
        clear_halo(ref, frames)
    a0[HALO : HALO + frames] = jnp.zeros((frames, high, ch), BF16)
    a0[HALO : HALO + frames, :block, :] = got_ref[:, 0]
    cots[...] = jnp.zeros(cots.shape, cots.dtype)
    cots[:, :block, :] = got_ref[:, 1]
    for layer, (source, target, slopes) in enumerate(((a0, a1, slope0), (a1, feat, slope1))):
        step_size = dil_ref[layer]
        weight = jnp.concatenate([tw_ref[layer, k] for k in range(TAPS)], axis=0)
        first = HALO if layer == 0 else 0
        for at in range(0, frames, step_frames):
            pre = mm(taps_of(source, at, step_frames, step_size, 1), weight)
            act, slope = silu_parts(pre)
            target[first + at : first + at + step_frames] = act.astype(BF16).reshape(
                step_frames, high, ch
            )
            slopes[at : at + step_frames] = slope.reshape(step_frames, high, ch)
    for seg in range(segs):
        low, top = seg * seg_frames, (seg + 1) * seg_frames
        here = low + key_ref[seg]
        key_part = mm(feat[here], uw_ref[1])
        main = mm(feat[low:top].reshape(seg_frames * high, ch), uw_ref[0]).reshape(
            seg_frames, high, ch
        )
        send_ref[low:top, 1] = (main + key_part[None]).astype(BF16)[:, :block]
        mine = cots[low:top]
        total = jnp.sum(mine.astype(F32), axis=0)
        seg_cot[seg] = total
        grad_feat[low:top] = mm_nt(mine.reshape(seg_frames * high, ch), uw_ref[0]).reshape(
            seg_frames, high, ch
        )
        key_term = sum(mm_nt(part, uw_ref[1]) for part in three_parts(total))
        grad_feat[here] = grad_feat[here] + key_term
        g1[HALO + low : HALO + top] = (grad_feat[low:top] * slope1[low:top]).astype(BF16)
    for layer, source in ((1, g1), (0, g0)):
        step_size = dil_ref[layer]
        weight = jnp.concatenate(
            [tw_ref[layer, k].astype(F32).T.astype(BF16) for k in range(TAPS)], axis=0
        )
        for at in range(0, frames, step_frames):
            grad = mm(taps_of(source, at, step_frames, step_size, -1), weight).reshape(
                step_frames, high, ch
            )
            if layer == 1:
                g0[HALO + at : HALO + at + step_frames] = (
                    grad * slope0[at : at + step_frames]
                ).astype(BF16)
            else:
                send_ref[at : at + step_frames, 0] = grad.astype(BF16)[:, :block]


def temporal_wgrad_kernel(
    step_frames, scale, dil_ref, key_ref, a0, a1, feat, g0, g1, cots, seg_cot, out_ref
):
    frames, high, ch = feat.shape
    segs = key_ref.shape[0]
    seg_frames = frames // segs
    rows = step_frames * high
    for layer, acts, grads in ((0, a0, g0), (1, a1, g1)):
        total = jnp.zeros((TAPS * ch, ch), F32)
        for at in range(0, frames, step_frames):
            total = total + mm_tn(
                taps_of(acts, at, step_frames, dil_ref[layer], 1),
                grads[HALO + at : HALO + at + step_frames].reshape(rows, ch),
            )
        out_ref[layer * TAPS : (layer + 1) * TAPS] = total.reshape(TAPS, ch, ch) * scale
    total = jnp.zeros((ch, ch), F32)
    for at in range(0, frames, step_frames):
        total = total + mm_tn(
            feat[at : at + step_frames].reshape(rows, ch),
            cots[at : at + step_frames].reshape(rows, ch),
        )
    out_ref[LAYERS * TAPS] = total * scale
    total = jnp.zeros((ch, ch), F32)
    for seg in range(segs):
        key = feat[seg * seg_frames + key_ref[seg]]
        total = total + sum(mm_tn(key, part) for part in three_parts(seg_cot[seg]))
    out_ref[LAYERS * TAPS + 1] = total * scale


def exchange(blocks):
    return lax.all_to_all(blocks, AXES, split_axis=0, concat_axis=0, tiled=True)


def reduce_everywhere(parts, devices):
    count, ch, _ = parts.shape
    pieces = exchange(parts.reshape(devices, count * ch // devices, ch))
    mine = jnp.sum(pieces.astype(F32), axis=0).astype(BF16)
    return exchange(jnp.broadcast_to(mine, pieces.shape)).reshape(count, ch, ch).astype(F32)


def local(
    frames_in, spatial_weight, temporal_weight, uniting_weight, key_index, dilation, cotangent
):
    held, rows, cols, ch = frames_in.shape
    assert held == 1
    pixels = rows * cols
    devices = lax.axis_size("seg") * lax.axis_size("grp")
    frames = held * devices
    block = pixels // devices
    split = cols // block
    wide = round_up(cols + 1, 16)
    high = round_up(block, 16)
    rows_step = next(n for n in (4, 2, 1) if rows % n == 0)
    step_frames = max(n for n in range(1, frames + 1) if frames % n == 0 and n * high <= 512)
    scale = float((frames * pixels) ** -0.5)

    send, space_slope = call(
        functools.partial(spatial_fwd_kernel, rows_step),
        [((rows, 2, cols, ch), BF16), ((rows, wide, ch), F32)],
        [pltpu.VMEM((rows + 2, wide, ch), BF16)],
        2 * 9 * pixels * ch * ch,
        pixels * ch * 12,
        0,
        (frames_in[0], spatial_weight, cotangent[0]),
    )
    send = send.reshape(rows, 2, split, block, ch).swapaxes(1, 2).reshape(devices, 2, block, ch)
    got = exchange(send)

    padded = ((frames + 2 * HALO, high, ch), BF16)
    whole = (frames, high, ch)
    send, a0, a1, feat, cots, g0, g1, seg_cot = call(
        functools.partial(temporal_kernel, step_frames),
        [
            ((frames, 2, block, ch), BF16),
            padded,
            padded,
            (whole, BF16),
            (whole, BF16),
            padded,
            padded,
            ((key_index.shape[0], high, ch), F32),
        ],
        [pltpu.VMEM(whole, F32)] * 3,
        2 * 22 * frames * block * ch * ch,
        frames * block * ch * 18,
        2,
        (dilation, key_index, got, temporal_weight, uniting_weight),
    )
    got = exchange(send)
    (time_grads,) = call(
        functools.partial(temporal_wgrad_kernel, step_frames, scale),
        [((LAYERS * TAPS + 2, ch, ch), F32)],
        [],
        2 * 12 * frames * block * ch * ch,
        frames * block * ch * 14,
        2,
        (dilation, key_index, a0, a1, feat, g0, g1, cots, seg_cot),
    )
    (x_cat,) = call(
        functools.partial(columns_kernel, rows_step),
        [((rows * wide, 3 * ch), BF16)],
        [],
        0,
        pixels * ch * 8,
        0,
        (frames_in[0],),
    )
    got = got.reshape(rows, split, 2, block, ch).swapaxes(1, 2).reshape(rows, 2, cols, ch)
    gs, united, space_grads = call(
        functools.partial(spatial_wgrad_kernel, rows_step, scale),
        [((rows + 2, wide, ch), BF16), ((rows, cols, ch), BF16), ((9, ch, ch), BF16)],
        [],
        2 * 9 * pixels * ch * ch,
        pixels * ch * 18,
        0,
        (got, space_slope, x_cat),
    )
    (back,) = call(
        functools.partial(spatial_back_kernel, rows_step),
        [((rows, cols, ch), BF16)],
        [],
        2 * 9 * pixels * ch * ch,
        pixels * ch * 4,
        0,
        (spatial_weight, gs),
    )
    time_grads = lax.psum(time_grads, AXES)
    return (
        united[None],
        back[None],
        reduce_everywhere(space_grads, devices),
        time_grads[: LAYERS * TAPS].reshape(LAYERS, TAPS, ch, ch),
        time_grads[LAYERS * TAPS :],
    )


def solution(mesh):
    frame_spec = P(AXES, None, None, None)
    return jax.shard_map(
        local,
        mesh=mesh,
        in_specs=(frame_spec, P(), P(), P(), P(), P(), frame_spec),
        out_specs=(frame_spec, frame_spec, P(), P(), P()),
        check_vma=False,
    )
```

time: 245 us -> 319 us (1.30)
  waiting for transfers between devices: 31.6 us -> 175 us
  blocking collectives: 159 us -> 68.8 us
  local copies, waits for them, and re-layouts: 12.8 us -> 29.1 us
  between operations: 0.78 us -> 14.1 us
  starting transfers between devices: 11.3 us -> 6.55 us
    psum x0 -> x1, waiting for transfers between devices: none -> 130 us  [local(): time_grads = lax.psum(time_grads, AXES)]
    all_gather x2 -> x0, blocking collectives: 82.8 us -> none  [reduce_everywhere(): return lax.all_gather(mine, AXES, axis=0, tiled=True).reshape(count, ch, ch)]
    unnamed x29 -> x54, local copies, waits for them, and re-layouts: 9.57 us -> 23.9 us
    all_to_all x3 -> x2, waiting for transfers between devices: 31.6 us -> 44.2 us  [exchange(): return lax.all_to_all(blocks, AXES, split_axis=0, concat_axis=0, tiled=True)]
    all_to_all x3 -> x2, blocking collectives: 76 us -> 68.8 us  [exchange(): return lax.all_to_all(blocks, AXES, split_axis=0, concat_axis=0, tiled=True)]
    all_to_all x3 -> x2, starting transfers between devices: 11.3 us -> 6.5 us  [exchange(): return lax.all_to_all(blocks, AXES, split_axis=0, concat_axis=0, tiled=True)]
    pallas_call x5 -> x6, Pallas kernels: 28 us -> 25.4 us  [call(): pl.pallas_call(kernel, out_shape=[jax.ShapeDtypeStruct(shape, kind) for s...]
  transfers between devices with their start and end apart: 3 -> 3, of which waited for: 2 -> 2; matrix products, arithmetic and copies ran while one was open for 1% -> 1% of each run, Pallas kernels for 5% -> 3%
where the time goes in v3:
time: 319 us
  waiting for transfers between devices  175 us (55%)
  blocking collectives  68.8 us (22%)
  local copies, waits for them, and re-layouts  29.1 us (9%)
  Pallas kernels  25.4 us (8%)
  between operations  14.1 us (4%)
  starting transfers between devices  6.55 us (2%)
    psum x1, waiting for transfers between devices, local(): time_grads = lax.psum(time_grads, AXES)  130 us
    all_to_all x2, blocking collectives, exchange(): return lax.all_to_all(blocks, AXES, split_axis=0, concat_axis=0, tiled=True)  68.8 us
    all_to_all x2, waiting for transfers between devices, exchange(): return lax.all_to_all(blocks, AXES, split_axis=0, concat_axis=0, tiled=True)  44.2 us
    pallas_call x6, Pallas kernels, call(): pl.pallas_call(kernel, out_shape=[jax.ShapeDtypeStruct(shape, kind) for s...  25.4 us
    unnamed x54, local copies, waits for them, and re-layouts  23.9 us
    all_to_all x2, starting transfers between devices, exchange(): return lax.all_to_all(blocks, AXES, split_axis=0, concat_axis=0, tiled=True)  6.5 us
  transfers between devices with their start and end apart: 3, of which 2 were waited for; matrix products, arithmetic and copies ran while one was open for 1% of the time, Pallas kernels for 3%

profile of v3, /device:TPU:0, one launch (start us, length us, event | category | flops | bytes accessed | tf_op | source)
XLA Modules:
  0.0 318.7 jit_solution(16872745064365593029)
XLA Ops:
  7.2 0.0 copy-start.14
  7.2 1.2 copy-done.14
  8.4 1.2 copy-done.22
  9.6 1.0 copy-done.24
  10.5 2.4 shard_map.110
  12.9 0.0 copy-start
  12.9 1.4 copy-done
  14.3 53.0 %all_to_all.20.got_ref = bf16[32,2,120,128]{3,2,1,0:T(8,128)(2,1)S(1)} all-to-all(bf16[32,2,120,128]{3,2,1,0:T(8,128)(2,1)S(1)} %get-tuple-element.18), channel_id=1, replica_groups=mesh['seg'=4,'grp'=8] {'seg','grp'}, dimensions={0} | all-to-all | bytes 3932160 | tf_op jit(solution)/shard_map/all_to_all | solution.py:246
  67.3 0.0 copy-done.18
  67.3 0.0 copy-done.19
  67.3 0.0 copy-done.23
  67.3 0.0 copy-done.26
  67.3 10.0 %shard_map.111 = (bf16[32,2,120,128]{3,2,1,0:T(8,128)(2,1)}, bf16[64,128,128]{2,1,0:T(8,128)(2,1)S(1)}, bf16[64,128,128]{2,1,0:T(8,128)(2,1)S(1)}, bf16[32,128,1...) custom-call(s32[2]{0:T(128)S(1)} %copy-done.18, ...), custom_call_target="tpu_custom_call" | custom-call | flops 2768240640 | bytes 8847360 | tf_op jit(solution)/shard_map/pallas_call | solution.py:52
  77.4 1.3 copy-done.2
  78.7 1.3 copy-done.4
  80.0 1.4 copy-done.6
  81.4 1.4 copy-done.8
  82.8 1.0 copy-done.10
  83.8 1.0 copy-done.12
  84.8 0.7 copy-done.16
  85.5 3.9 %all-to-all-start.1 = ((bf16[32,2,120,128]{3,2,1,0:T(8,128)(2,1)}), bf16[32,2,120,128]{3,2,1,0:T(8,128)(2,1)}, u32[]{:S(2)}, u32[]{:S(2)}) async-start(bf16[32,2,120,128]{3,2,1,0:T(8,128)(2,1)} %get-tuple-element.19), calls=%async_computation.1 | async-start | bytes 3932160 | tf_op jit(solution)/shard_map/all_to_all | solution.py:246
  89.4 0.0 copy-start.15
  89.4 1.2 copy-done.15
  90.6 0.5 shard_map.112.cat_ref
  91.1 44.2 %all-to-all-done.1.got_ref = bf16[32,2,120,128]{3,2,1,0:T(8,128)(2,1)} async-done(((bf16[32,2,120,128]{3,2,1,0:T(8,128)(2,1)}), bf16[32,2,120,128]{3,2,1,0:T(8,128)(2,1)}, u32[]{:S(2)}, u32[]{:S(2)}) %all-to-all-start.1) | async-done | bytes 1966112 | tf_op jit(solution)/shard_map/all_to_all | solution.py:246
  135.3 1.6 copy-done.1
  136.9 4.6 %shard_map.113 = (bf16[34,128,128]{2,1,0:T(8,128)(2,1)S(1)}, bf16[32,120,128]{2,1,0:T(8,128)(2,1)}, bf16[9,128,128]{2,1,0:T(8,128)(2,1)S(1)}) custom-call(bf16[32,2,120,128]{3,2,1,0:T(8,128)(2,1)} %all-to-all-done.1.got_ref, f32[32,128,128]{2,1,0:T(8,128)S(1)} %copy-done.1, bf16[4096,384]{1,0:T(8,128)(2,1)S(1)} %shard_map.112.cat_ref), custom_call_target="tpu_custom_call" | custom-call | flops 1132462080 | bytes 8847360 | tf_op jit(solution)/shard_map/pallas_call | solution.py:52
  141.5 1.1 copy-done.20
  142.5 0.1 reshape.19
  142.6 15.8 %all_to_all.21 = bf16[32,36,128]{2,1,0:T(8,128)(2,1)S(1)} all-to-all(bf16[32,36,128]{2,1,0:T(8,128)(2,1)S(1)} %reshape.19), channel_id=1, replica_groups=mesh['seg'=4,'grp'=8] {'seg','grp'}, dimensions={0} | all-to-all | bytes 589824 | tf_op jit(solution)/shard_map/all_to_all | solution.py:246
  158.4 0.1 reduce_sum.12
  158.4 0.8 broadcast_in_dim.11
  159.2 2.6 all-to-all-start.3
  161.8 0.0 all-reduce.2.cloned.1.call-start
  161.8 0.0 copy-done.3
  161.9 1.6 copy-done.5
  163.5 1.6 copy-done.7
  165.0 1.6 copy-done.9
  166.6 1.2 copy-done.11
  167.9 1.2 copy-done.13
  169.1 4.7 %shard_map.115 = f32[12,128,128]{2,1,0:T(8,128)} custom-call(s32[2]{0:T(128)S(1)} %copy-done.18, s32[4]{0:T(128)S(1)} %copy-done.19, bf16[64,128,128]{2,1,0:T(8,128)(2,1)S(1)} %copy-done.3, bf16[64,128,128]{2,1,0:T(8,128)(2,1)S(1)} %copy-done.5, bf16[32,128,128]{2,1,0:T(8,128)(2,1)S(1)} %copy-done.11, bf16[64,128,128]{2,1,0:T(8,128)(2,1)S(1)} %copy-done.7, ...), custom_call_target="tpu_custom_call" | custom-call | flops 1509949440 | bytes 6881280 | tf_op jit(solution)/shard_map/pallas_call | solution.py:52
  173.8 0.0 all-reduce.2.cloned.1.call-update
  173.8 130.4 %all-reduce.2.cloned.1.call-done = f32[12,128,128]{2,1,0:T(8,128)} async-done(((f32[12,128,128]{2,1,0:T(8,128)}), f32[12,128,128]{2,1,0:T(8,128)}) %all-reduce.2.cloned.1.call-update) | async-done | bytes 786448 | tf_op jit(solution)/shard_map/psum | solution.py:342
  304.2 2.0 slice.8
  306.2 1.6 slice.9
  307.8 3.1 shard_map.114
  310.9 0.0 all-to-all-done.3
  310.9 0.9 reshape.21
  (27 shorter events, 0.0 us)
Async XLA Ops:
  7.2 1.2 copy-start.14
  8.4 1.2 copy-start.22
  9.6 1.0 copy-start.24
  12.9 1.4 copy-start
  14.3 53.0 %copy-start.18 = (s32[2]{0:T(128)S(1)}, s32[2]{0:T(128)}, u32[]{:S(2)}) copy-start(s32[2]{0:T(128)} %dil_ref.3) | copy-start | bytes 28
  14.3 53.0 %copy-start.19 = (s32[4]{0:T(128)S(1)}, s32[4]{0:T(128)}, u32[]{:S(2)}) copy-start(s32[4]{0:T(128)} %key_ref.3) | copy-start | bytes 52
  14.3 53.0 %copy-start.23 = (bf16[2,5,128,128]{3,2,1,0:T(8,128)(2,1)S(1)}, bf16[2,5,128,128]{3,2,1,0:T(8,128)(2,1)}, u32[]{:S(2)}) copy-start(bf16[2,5,128,128]{3,2,1,0:T(8,128)(2,1)} %tw_ref.1) | copy-start | bytes 983044
  14.3 53.0 %copy-start.26 = (bf16[2,128,128]{2,1,0:T(8,128)(2,1)S(1)}, bf16[2,128,128]{2,1,0:T(8,128)(2,1)}, u32[]{:S(2)}) copy-start(bf16[2,128,128]{2,1,0:T(8,128)(2,1)} %uw_ref.1) | copy-start | bytes 196612
  77.4 1.3 copy-start.2
  78.7 1.3 copy-start.4
  80.0 1.4 copy-start.6
  81.4 1.4 copy-start.8
  82.8 1.0 copy-start.10
  83.8 1.0 copy-start.12
  84.8 0.7 copy-start.16
  85.5 49.8 %all-to-all-start.1 = ((bf16[32,2,120,128]{3,2,1,0:T(8,128)(2,1)}), bf16[32,2,120,128]{3,2,1,0:T(8,128)(2,1)}, u32[]{:S(2)}, u32[]{:S(2)}) async-start(bf16[32,2,120,128]{3,2,1,0:T(8,128)(2,1)} %get-tuple-element.19), calls=%async_computation.1 | async-start | bytes 3932160 | tf_op jit(solution)/shard_map/all_to_all | solution.py:246
  89.4 1.2 copy-start.15
  135.3 1.6 copy-start.1
  141.5 1.1 copy-start.20
  142.5 19.3 %copy-start.3 = (bf16[64,128,128]{2,1,0:T(8,128)(2,1)S(1)}, bf16[64,128,128]{2,1,0:T(8,128)(2,1)}, u32[]{:S(2)}) copy-start(bf16[64,128,128]{2,1,0:T(8,128)(2,1)} %copy-done.2) | copy-start | bytes 6291460
  142.5 19.3 %copy-start.17 = (f32[4,128,128]{2,1,0:T(8,128)S(1)}, f32[4,128,128]{2,1,0:T(8,128)}, u32[]{:S(2)}) copy-start(f32[4,128,128]{2,1,0:T(8,128)} %copy-done.16) | copy-start | bytes 786436
  159.2 151.7 %all-to-all-start.3 = ((bf16[32,36,128]{2,1,0:T(8,128)(2,1)}), bf16[32,36,128]{2,1,0:T(8,128)(2,1)S(1)}, u32[]{:S(2)}, u32[]{:S(2)}) async-start(bf16[32,36,128]{2,1,0:T(8,128)(2,1)} %broadcast_in_dim.11), calls=%async_computation.3 | async-start | bytes 655360 | tf_op jit(solution)/shard_map/all_to_all | solution.py:246
  161.8 142.5 %all-reduce.2.cloned.1.call-start = ((), (), s32[]{:S(2)}) async-start(), calls=%async_computation.4 | async-start | bytes 1572864 | tf_op jit(solution)/shard_map/psum | solution.py:342
  161.9 1.6 copy-start.5
  163.5 1.6 copy-start.7
  165.0 1.6 copy-start.9
  166.6 1.2 copy-start.11
  167.9 1.2 copy-start.13
  173.8 134.0 %copy-start.21 = (bf16[34,128,128]{2,1,0:T(8,128)(2,1)S(1)}, bf16[34,128,128]{2,1,0:T(8,128)(2,1)}, u32[]{:S(2)}) copy-start(bf16[34,128,128]{2,1,0:T(8,128)(2,1)} %copy-done.20) | copy-start | bytes 3342340
  173.8 134.0 %copy-start.25 = (bf16[9,128,128]{2,1,0:T(8,128)(2,1)S(1)}, bf16[9,128,128]{2,1,0:T(8,128)(2,1)}, u32[]{:S(2)}) copy-start(bf16[9,128,128]{2,1,0:T(8,128)(2,1)} %w_ref.3) | copy-start | bytes 884740
Sparse Core Ops, SparseCore 0:
  173.9 130.2 all-reduce.1

commit v4 on v3

v4 whole, which is shorter than its diff:
```python
import functools

import jax
import jax.numpy as jnp
from jax import lax
from jax.experimental import pallas as pl
from jax.experimental.pallas import tpu as pltpu
from jax.sharding import PartitionSpec as P

LAYERS = 2
TAPS = 5
DMAX = 8
HALO = 2 * DMAX
AXES = ("seg", "grp")
BF16 = jnp.bfloat16
F32 = jnp.float32
VMEM_LIMIT = 32 * 1024 * 1024


def round_up(value, step):
    return -(-value // step) * step


def silu_parts(value):
    sigma = 0.5 * jnp.tanh(0.5 * value) + 0.5
    act = value * sigma
    return act, sigma + act * (1.0 - sigma)


def mm(left, right):
    return jnp.dot(left, right, preferred_element_type=F32)


def mm_nt(left, right):
    return lax.dot_general(left, right, (((1,), (1,)), ((), ())), preferred_element_type=F32)


def mm_tn(left, right):
    return lax.dot_general(left, right, (((0,), (0,)), ((), ())), preferred_element_type=F32)


def three_parts(value):
    high = value.astype(BF16)
    rest = value - high.astype(F32)
    middle = rest.astype(BF16)
    return high, middle, (rest - middle.astype(F32)).astype(BF16)


VMEM = pl.BlockSpec(memory_space=pltpu.VMEM)
SMEM = pl.BlockSpec(memory_space=pltpu.SMEM)
ANY = pl.BlockSpec(memory_space=pl.ANY)


def call(kernel, outs, scratch, flops, moved, args):
    return pl.pallas_call(
        kernel,
        out_shape=[jax.ShapeDtypeStruct(shape, kind) for shape, kind, _ in outs],
        in_specs=[spec for _, spec in args],
        out_specs=[spec for _, _, spec in outs],
        scratch_shapes=scratch,
        compiler_params=pltpu.CompilerParams(vmem_limit_bytes=VMEM_LIMIT),
        cost_estimate=pl.CostEstimate(flops=flops, bytes_accessed=moved, transcendentals=0),
    )(*[value for value, _ in args])


def roll_rows(value, shift):
    return pltpu.roll(value, shift % value.shape[0], 0)


def spatial_fwd_kernel(
    rows_step, x_hbm, w_ref, cot_hbm, send_ref, slope_hbm, x_in, xs, slopes, in_sems, cot_sem, out_sems
):
    rows, cols, ch = x_in.shape
    wide = xs.shape[1]
    steps = rows // rows_step

    def part(step):
        return pl.ds(step * rows_step, rows_step)

    loads = [
        pltpu.make_async_copy(x_hbm.at[part(n)], x_in.at[part(n)], in_sems.at[n]) for n in range(steps)
    ]
    stores = [
        pltpu.make_async_copy(slopes.at[part(n)], slope_hbm.at[part(n)], out_sems.at[n])
        for n in range(steps)
    ]
    for load in loads:
        load.start()
    cot_copy = pltpu.make_async_copy(cot_hbm, send_ref.at[:, 1], cot_sem.at[0])
    cot_copy.start()
    xs[0] = jnp.zeros((wide, ch), BF16)
    xs[rows + 1] = jnp.zeros((wide, ch), BF16)
    weight = jnp.concatenate(
        [jnp.concatenate([w_ref[3 * a + b] for b in range(3)], axis=1) for a in range(3)], axis=0
    )
    flat = rows_step * wide

    def bring(step):
        loads[step].wait()
        at = step * rows_step
        xs[1 + at : 1 + at + rows_step] = jnp.zeros((rows_step, wide, ch), BF16)
        xs[1 + at : 1 + at + rows_step, :cols, :] = x_in[at : at + rows_step]

    bring(0)
    for step in range(steps):
        if step + 1 < steps:
            bring(step + 1)
        at = step * rows_step
        left = jnp.concatenate(
            [xs[at + a : at + a + rows_step].reshape(flat, ch) for a in range(3)], axis=1
        )
        y = mm(left, weight)
        pre = y[:, ch : 2 * ch] + roll_rows(y[:, :ch], 1) + roll_rows(y[:, 2 * ch :], -1)
        act, slope = silu_parts(pre)
        send_ref[at : at + rows_step, 0] = act.astype(BF16).reshape(rows_step, wide, ch)[:, :cols]
        slopes[at : at + rows_step] = slope.reshape(rows_step, wide, ch)
        stores[step].start()
    cot_copy.wait()
    for store in stores:
        store.wait()


def hand_out(here_ref, total_ref, pieces):
    for peer, piece in enumerate(pieces):
        piece[...] = total_ref[jnp.bitwise_xor(here_ref[1], peer)].astype(piece.dtype)


def columns_kernel(rows_step, x_ref, cat_ref):
    rows, cols, ch = x_ref.shape
    wide = cat_ref.shape[0] // rows
    flat = rows_step * wide
    pad = jnp.zeros((rows_step, wide - cols, ch), F32)
    for at in range(0, rows, rows_step):
        x = jnp.concatenate([x_ref[at : at + rows_step].astype(F32), pad], axis=1).reshape(flat, ch)
        x_cat = jnp.concatenate([roll_rows(x, 1), x, roll_rows(x, -1)], axis=1)
        cat_ref[at * wide : at * wide + flat] = x_cat.astype(BF16)


def taps_up(gs, at, rows_step):
    wide, ch = gs.shape[1:]
    return jnp.concatenate(
        [gs[at + 2 - a : at + 2 - a + rows_step].reshape(rows_step * wide, ch) for a in range(3)],
        axis=1,
    )


def spatial_wgrad_kernel(
    rows_step, scale, here_ref, got_ref, slope_ref, cat_ref, gs, *rest
):
    pieces, total_ref = rest[:-1], rest[-1]
    rows, cols, ch = got_ref.shape
    wide = gs.shape[1]
    gs[0] = jnp.zeros((wide, ch), BF16)
    gs[rows + 1] = jnp.zeros((wide, ch), BF16)
    for at in range(0, rows, rows_step):
        gs[1 + at : 1 + at + rows_step] = jnp.zeros((rows_step, wide, ch), BF16)
        gs[1 + at : 1 + at + rows_step, :cols, :] = (
            got_ref[at : at + rows_step].astype(F32) * slope_ref[at : at + rows_step, :cols, :]
        ).astype(BF16)
    flat = rows_step * wide
    total = jnp.zeros((3 * ch, 3 * ch), F32)
    for at in range(0, rows, rows_step):
        total = total + mm_tn(cat_ref[at * wide : at * wide + flat], taps_up(gs, at, rows_step))
    total_ref[...] = (
        jnp.concatenate(
            [
                total[b * ch : (b + 1) * ch, a * ch : (a + 1) * ch]
                for a in range(3)
                for b in range(3)
            ],
            axis=0,
        )
        * scale
    ).reshape(total_ref.shape)
    hand_out(here_ref, total_ref, pieces)


def spatial_back_kernel(rows_step, w_ref, gs, back_ref):
    rows, cols, ch = back_ref.shape
    wide = gs.shape[1]
    weight = jnp.concatenate(
        [
            jnp.concatenate([w_ref[3 * a + b].astype(F32).T.astype(BF16) for b in range(3)], axis=1)
            for a in range(3)
        ],
        axis=0,
    )
    for at in range(0, rows, rows_step):
        y = mm(taps_up(gs, at, rows_step), weight)
        back = y[:, ch : 2 * ch] + roll_rows(y[:, :ch], -1) + roll_rows(y[:, 2 * ch :], 1)
        back_ref[at : at + rows_step] = back.astype(BF16).reshape(rows_step, wide, ch)[:, :cols]


def clear_halo(pad_ref, frames):
    zeros = jnp.zeros((HALO,) + pad_ref.shape[1:], pad_ref.dtype)
    pad_ref[:HALO] = zeros
    pad_ref[HALO + frames :] = zeros


def taps_of(pad_ref, at, count, step_size, sign):
    high, ch = pad_ref.shape[1:]
    pieces = [
        pad_ref[pl.ds(HALO + at + sign * (k - 2) * step_size, count)].reshape(count * high, ch)
        for k in range(TAPS)
    ]
    return jnp.concatenate(pieces, axis=1)


def temporal_kernel(
    step_frames, dil_ref, key_ref, got_ref, tw_ref, uw_ref,
    grad_ref, united_ref, a1_hbm, feat_hbm, g1_hbm, g0_hbm,
    a0, a1, feat, cots, g0, g1, slope0, slope1, grad_feat, sems,
):
    frames, _, block, ch = got_ref.shape
    high = feat.shape[1]
    segs = key_ref.shape[0]
    seg_frames = frames // segs
    inside = pl.ds(HALO, frames)
    copies = [
        pltpu.make_async_copy(source, target, sems.at[n])
        for n, (source, target) in enumerate(
            (
                (a1.at[inside], a1_hbm),
                (feat, feat_hbm),
                (g1.at[inside], g1_hbm),
                (g0.at[inside], g0_hbm),
            )
        )
    ]
    for ref in (a0, a1, g0, g1):
        clear_halo(ref, frames)
    a0[HALO : HALO + frames] = jnp.zeros((frames, high, ch), BF16)
    a0[HALO : HALO + frames, :block, :] = got_ref[:, 0]
    cots[...] = jnp.zeros(cots.shape, cots.dtype)
    cots[:, :block, :] = got_ref[:, 1]
    for layer, (source, target, slopes) in enumerate(((a0, a1, slope0), (a1, feat, slope1))):
        step_size = dil_ref[layer]
        weight = jnp.concatenate([tw_ref[layer, k] for k in range(TAPS)], axis=0)
        first = HALO if layer == 0 else 0
        for at in range(0, frames, step_frames):
            pre = mm(taps_of(source, at, step_frames, step_size, 1), weight)
            act, slope = silu_parts(pre)
            target[first + at : first + at + step_frames] = act.astype(BF16).reshape(
                step_frames, high, ch
            )
            slopes[at : at + step_frames] = slope.reshape(step_frames, high, ch)
        copies[layer].start()
    for seg in range(segs):
        low, top = seg * seg_frames, (seg + 1) * seg_frames
        here = low + key_ref[seg]
        key_part = mm(feat[here], uw_ref[1])
        main = mm(feat[low:top].reshape(seg_frames * high, ch), uw_ref[0]).reshape(
            seg_frames, high, ch
        )
        united_ref[low:top] = (main + key_part[None]).astype(BF16)[:, :block]
        mine = cots[low:top]
        total = jnp.sum(mine.astype(F32), axis=0)
        grad_feat[low:top] = mm_nt(mine.reshape(seg_frames * high, ch), uw_ref[0]).reshape(
            seg_frames, high, ch
        )
        key_term = sum(mm_nt(part, uw_ref[1]) for part in three_parts(total))
        grad_feat[here] = grad_feat[here] + key_term
        g1[HALO + low : HALO + top] = (grad_feat[low:top] * slope1[low:top]).astype(BF16)
    for layer, source in ((1, g1), (0, g0)):
        copies[3 - layer].start()
        step_size = dil_ref[layer]
        weight = jnp.concatenate(
            [tw_ref[layer, k].astype(F32).T.astype(BF16) for k in range(TAPS)], axis=0
        )
        for at in range(0, frames, step_frames):
            grad = mm(taps_of(source, at, step_frames, step_size, -1), weight).reshape(
                step_frames, high, ch
            )
            if layer == 1:
                g0[HALO + at : HALO + at + step_frames] = (
                    grad * slope0[at : at + step_frames]
                ).astype(BF16)
            else:
                grad_ref[at : at + step_frames] = grad.astype(BF16)[:, :block]
    for copy in copies:
        copy.wait()


def temporal_wgrad_kernel(
    step_frames, scale, here_ref, dil_ref, key_ref, got_ref, a1_ref, feat, g0, g1, *rest
):
    pieces, (a0, a1, cots, total_ref) = rest[:-4], rest[-4:]
    frames, high, ch = feat.shape
    block = got_ref.shape[2]
    segs = key_ref.shape[0]
    seg_frames = frames // segs
    rows = step_frames * high
    clear_halo(a0, frames)
    clear_halo(a1, frames)
    a0[HALO : HALO + frames] = jnp.zeros((frames, high, ch), BF16)
    a0[HALO : HALO + frames, :block, :] = got_ref[:, 0]
    a1[HALO : HALO + frames] = a1_ref[...]
    cots[...] = jnp.zeros(cots.shape, cots.dtype)
    cots[:, :block, :] = got_ref[:, 1]
    totals = []
    for layer, acts, grads in ((0, a0, g0), (1, a1, g1)):
        total = jnp.zeros((TAPS * ch, ch), F32)
        for at in range(0, frames, step_frames):
            total = total + mm_tn(
                taps_of(acts, at, step_frames, dil_ref[layer], 1),
                grads[at : at + step_frames].reshape(rows, ch),
            )
        totals.append(total)
    total = jnp.zeros((ch, ch), F32)
    for at in range(0, frames, step_frames):
        total = total + mm_tn(
            feat[at : at + step_frames].reshape(rows, ch),
            cots[at : at + step_frames].reshape(rows, ch),
        )
    keyed = jnp.zeros((ch, ch), F32)
    for seg in range(segs):
        low, top = seg * seg_frames, (seg + 1) * seg_frames
        key = feat[low + key_ref[seg]]
        seg_cot = jnp.sum(cots[low:top].astype(F32), axis=0)
        keyed = keyed + sum(mm_tn(key, part) for part in three_parts(seg_cot))
    peers = len(pieces)
    split = LAYERS * TAPS * ch // peers
    total_ref[:, :split] = (jnp.concatenate(totals, axis=0) * scale).reshape(peers, split, ch)
    total_ref[:, split:] = (jnp.concatenate([total, keyed], axis=0) * scale).reshape(
        peers, 2 * ch // peers, ch
    )
    hand_out(here_ref, total_ref, pieces)


def sum_kernel(*refs):
    refs[-1][...] = sum(ref[...].astype(F32) for ref in refs[:-1]).astype(refs[-1].dtype)


def join_kernel(first_ref, *refs):
    out_ref = refs[-1]
    split = first_ref.shape[0]
    out_ref[:split] = first_ref[...]
    out_ref[split:] = sum(ref[...].astype(F32) for ref in refs[:-1]).astype(out_ref.dtype)


def deal_kernel(here_ref, *refs):
    pieces, outs = refs[:-3], refs[-3:]
    for peer, piece in enumerate(pieces):
        place = jnp.bitwise_xor(here_ref[1], peer)
        at = 0
        for out_ref in outs:
            count = out_ref.shape[1]
            out_ref[place] = piece[at : at + count].astype(F32)
            at += count


def exchange(blocks):
    return lax.all_to_all(blocks, AXES, split_axis=0, concat_axis=0, tiled=True)


def flip(value, peer):
    size = lax.axis_size("grp")
    return lax.ppermute(value, "grp", [(i, i ^ peer) for i in range(size)])


def turn_by(value, turn):
    size = lax.axis_size("seg")
    return lax.ppermute(value, "seg", [(i, (i + turn) % size) for i in range(size)])


def sum_of(parts):
    shape = parts[0].shape
    return call(
        sum_kernel, [(shape, BF16, VMEM)], [], 0, len(parts) * 2 * shape[0] * shape[1],
        [(part, VMEM) for part in parts],
    )[0]


def reduce_in_grp(pieces):
    return sum_of([flip(piece, peer) if peer else piece for peer, piece in enumerate(pieces)])


def all_turns(value):
    return [turn_by(value, turn) if turn else value for turn in range(lax.axis_size("seg"))]


def local(
    frames_in, spatial_weight, temporal_weight, uniting_weight, key_index, dilation, cotangent
):
    held, rows, cols, ch = frames_in.shape
    assert held == 1
    pixels = rows * cols
    peers = lax.axis_size("grp")
    devices = lax.axis_size("seg") * peers
    frames = held * devices
    block = pixels // devices
    split = cols // block
    wide = round_up(cols + 1, 16)
    high = round_up(block, 16)
    rows_step = next(n for n in (4, 2, 1) if rows % n == 0)
    steps = rows // rows_step
    step_frames = max(n for n in range(1, frames + 1) if frames % n == 0 and n * high <= 512)
    scale = float((frames * pixels) ** -0.5)
    here = jnp.stack([lax.axis_index("seg"), lax.axis_index("grp")]).astype(jnp.int32)
    space_rows, time_rows, unite_rows = (n * ch // peers for n in (9, LAYERS * TAPS, 2))

    send, space_slope = call(
        functools.partial(spatial_fwd_kernel, rows_step),
        [((rows, 2, cols, ch), BF16, VMEM), ((rows, wide, ch), F32, ANY)],
        [
            pltpu.VMEM((rows, cols, ch), BF16),
            pltpu.VMEM((rows + 2, wide, ch), BF16),
            pltpu.VMEM((rows, wide, ch), F32),
            pltpu.SemaphoreType.DMA((steps,)),
            pltpu.SemaphoreType.DMA((1,)),
            pltpu.SemaphoreType.DMA((steps,)),
        ],
        2 * 9 * pixels * ch * ch,
        pixels * ch * 12,
        [(frames_in[0], ANY), (spatial_weight, VMEM), (cotangent[0], ANY)],
    )
    send = send.reshape(rows, 2, split, block, ch).swapaxes(1, 2).reshape(devices, 2, block, ch)
    got = exchange(send)

    padded = (frames + 2 * HALO, high, ch)
    whole = (frames, high, ch)
    grad_send, united_send, a1, feat, g1, g0 = call(
        functools.partial(temporal_kernel, step_frames),
        [((frames, block, ch), BF16, VMEM)] * 2 + [(whole, BF16, ANY)] * 4,
        [
            pltpu.VMEM(padded, BF16),
            pltpu.VMEM(padded, BF16),
            pltpu.VMEM(whole, BF16),
            pltpu.VMEM(whole, BF16),
            pltpu.VMEM(padded, BF16),
            pltpu.VMEM(padded, BF16),
            pltpu.VMEM(whole, F32),
            pltpu.VMEM(whole, F32),
            pltpu.VMEM(whole, F32),
            pltpu.SemaphoreType.DMA((4,)),
        ],
        2 * 22 * frames * block * ch * ch,
        frames * block * ch * 18,
        [
            (dilation, SMEM), (key_index, SMEM), (got, VMEM),
            (temporal_weight, VMEM), (uniting_weight, VMEM),
        ],
    )
    grad_time = exchange(grad_send).reshape(rows, cols, ch)
    time_pieces = call(
        functools.partial(temporal_wgrad_kernel, step_frames, scale),
        [((time_rows + unite_rows, ch), BF16, VMEM)] * peers,
        [
            pltpu.VMEM(padded, BF16),
            pltpu.VMEM(padded, BF16),
            pltpu.VMEM(whole, BF16),
            pltpu.VMEM((peers, time_rows + unite_rows, ch), F32),
        ],
        2 * 12 * frames * block * ch * ch,
        frames * block * ch * 14,
        [
            (here, SMEM), (dilation, SMEM), (key_index, SMEM), (got, VMEM),
            (a1, VMEM), (feat, VMEM), (g0, VMEM), (g1, VMEM),
        ],
    )
    time_sum = sum_of(all_turns(reduce_in_grp(time_pieces)))
    (x_cat,) = call(
        functools.partial(columns_kernel, rows_step),
        [((rows * wide, 3 * ch), BF16, VMEM)],
        [],
        0,
        pixels * ch * 8,
        [(frames_in[0], VMEM)],
    )
    gs, *space_pieces = call(
        functools.partial(spatial_wgrad_kernel, rows_step, scale),
        [((rows + 2, wide, ch), BF16, VMEM)] + [((space_rows, ch), BF16, VMEM)] * peers,
        [pltpu.VMEM((peers, space_rows, ch), F32)],
        2 * 9 * pixels * ch * ch,
        pixels * ch * 18,
        [(here, SMEM), (grad_time, VMEM), (space_slope, VMEM), (x_cat, VMEM)],
    )
    united_send, space_pieces[0] = lax.optimization_barrier((united_send, space_pieces[0]))
    united = exchange(united_send)
    (back,) = call(
        functools.partial(spatial_back_kernel, rows_step),
        [((rows, cols, ch), BF16, VMEM)],
        [],
        2 * 9 * pixels * ch * ch,
        pixels * ch * 4,
        [(spatial_weight, VMEM), (gs, VMEM)],
    )
    space_parts = all_turns(reduce_in_grp(space_pieces))
    (piece,) = call(
        join_kernel,
        [((time_rows + unite_rows + space_rows, ch), BF16, VMEM)],
        [],
        0,
        10 * space_rows * ch,
        [(time_sum, VMEM)] + [(part, VMEM) for part in space_parts],
    )
    grads = call(
        deal_kernel,
        [((peers, count, ch), F32, VMEM) for count in (time_rows, unite_rows, space_rows)],
        [],
        0,
        6 * 21 * ch * ch,
        [(here, SMEM)] + [(flip(piece, peer) if peer else piece, VMEM) for peer in range(peers)],
    )
    return (
        united.reshape(frames_in.shape),
        back[None],
        grads[2].reshape(9, ch, ch),
        grads[0].reshape(LAYERS, TAPS, ch, ch),
        grads[1].reshape(2, ch, ch),
    )


def solution(mesh):
    frame_spec = P(AXES, None, None, None)
    return jax.shard_map(
        local,
        mesh=mesh,
        in_specs=(frame_spec, P(), P(), P(), P(), P(), frame_spec),
        out_specs=(frame_spec, frame_spec, P(), P(), P()),
        check_vma=False,
    )
```

time: 319 us -> 172 us (0.54)
  waiting for transfers between devices: 175 us -> 33 us
  starting transfers between devices: 6.55 us -> 35.4 us
  blocking collectives: 68.8 us -> 53 us
  between operations: 14.1 us -> 0.86 us
  local copies, waits for them, and re-layouts: 29.1 us -> 20.6 us
  Pallas kernels: 25.4 us -> 28.9 us
    psum x1 -> x0, waiting for transfers between devices: 130 us -> none  [local(): time_grads = lax.psum(time_grads, AXES)]
    ppermute x0 -> x27, starting transfers between devices: none -> 27.7 us  [the longest x21 21.7 us: flip(): return lax.ppermute(value, 'grp', [(i, i ^ peer) for i in range(size)])]
    all_to_all x2, waiting for transfers between devices: 44.2 us -> 22.8 us  [exchange(): return lax.all_to_all(blocks, AXES, split_axis=0, concat_axis=0, tiled=True)]
    all_to_all x2 -> x1, blocking collectives: 68.8 us -> 53 us  [exchange(): return lax.all_to_all(blocks, AXES, split_axis=0, concat_axis=0, tiled=True)]
    ppermute x0 -> x27, waiting for transfers between devices: none -> 10.2 us  [the longest x6 5.71 us: turn_by(): lax.ppermute(value, 'seg', [(i, (i + turn) % size) for i in range(size)])]
    slice x2 -> x0, local copies, waits for them, and re-layouts: 3.54 us -> none  [the longest x1 1.97 us: local(): time_grads[:LAYERS * TAPS].reshape(LAYERS, TAPS, ch, ch)]
    pallas_call x6 -> x11, Pallas kernels: 25.4 us -> 28.9 us  [call(): pl.pallas_call(kernel, out_shape=[jax.ShapeDtypeStruct(shape, kind) for s...]
    unnamed x54 -> x49, local copies, waits for them, and re-layouts: 23.9 us -> 20.6 us
  transfers between devices with their start and end apart: 3 -> 29, of which waited for: 2 -> 11; matrix products, arithmetic and copies ran while one was open for 1% -> 0% of each run, Pallas kernels for 3% -> 6%
where the time goes in v4:
time: 172 us
  blocking collectives  53 us (31%)
  starting transfers between devices  35.4 us (21%)
  waiting for transfers between devices  33 us (19%)
  Pallas kernels  28.9 us (17%)
  local copies, waits for them, and re-layouts  20.6 us (12%)
    all_to_all x1, blocking collectives, exchange(): return lax.all_to_all(blocks, AXES, split_axis=0, concat_axis=0, tiled=True)  53 us
    pallas_call x11, Pallas kernels, call(): pl.pallas_call(kernel, out_shape=[jax.ShapeDtypeStruct(shape, kind) for s...  28.9 us
    all_to_all x2, waiting for transfers between devices, exchange(): return lax.all_to_all(blocks, AXES, split_axis=0, concat_axis=0, tiled=True)  22.8 us
    ppermute x21, starting transfers between devices, flip(): return lax.ppermute(value, 'grp', [(i, i ^ peer) for i in range(size)])  21.7 us
    unnamed x49, local copies, waits for them, and re-layouts  20.6 us
    all_to_all x2, starting transfers between devices, exchange(): return lax.all_to_all(blocks, AXES, split_axis=0, concat_axis=0, tiled=True)  7.65 us
    ppermute x6, starting transfers between devices, turn_by(): lax.ppermute(value, 'seg', [(i, (i + turn) % size) for i in range(size)])  6 us
    ppermute x6, waiting for transfers between devices, turn_by(): lax.ppermute(value, 'seg', [(i, (i + turn) % size) for i in range(size)])  5.71 us
  transfers between devices with their start and end apart: 29, of which 11 were waited for; matrix products, arithmetic and copies ran while one was open for 0% of the time, Pallas kernels for 6%

profile of v4, /device:TPU:0, one launch (start us, length us, event | category | flops | bytes accessed | tf_op | source)
XLA Modules:
  0.0 171.8 jit_solution(15302127948345302640)
XLA Ops:
  0.6 1.2 copy-done.13
  1.8 1.2 copy-done.19
  3.0 1.0 copy-done.21
  4.0 5.4 %shard_map.110 = (bf16[32,2,120,128]{3,2,1,0:T(8,128)(2,1)S(1)}, f32[32,128,128]{2,1,0:T(8,128)S(1)}) custom-call(bf16[32,120,128]{2,1,0:T(8,128)(2,1)S(1)} %bitcast.9, bf16[9,128,128]{2,1,0:T(8,128)(2,1)S(1)} %copy-done.21, bf16[32,120,128]{2,1,0:T(8,128)(2,1)S(1)} %bitcast.11), custom_call_target="tpu_custom_call" | custom-call | flops 1132462080 | bytes 5898240 | tf_op jit(solution)/shard_map/pallas_call | solution.py:55
  9.4 1.3 copy-done.2
  10.7 53.0 %all_to_all.15.got_ref = bf16[32,2,120,128]{3,2,1,0:T(8,128)(2,1)S(1)} all-to-all(bf16[32,2,120,128]{3,2,1,0:T(8,128)(2,1)S(1)} %get-tuple-element.35), channel_id=1, replica_groups=mesh['seg'=4,'grp'=8] {'seg','grp'}, dimensions={0} | all-to-all | bytes 3932160 | tf_op jit(solution)/shard_map/all_to_all | solution.py:353
  63.8 10.2 %shard_map.111 = (bf16[32,120,128]{2,1,0:T(8,128)(2,1)}, bf16[32,120,128]{2,1,0:T(8,128)(2,1)S(1)}, bf16[32,128,128]{2,1,0:T(8,128)(2,1)S(1)}, bf16[32,128,128]{...) custom-call(s32[2]{0:T(128)S(1)} %copy-done.15, s32[4]{0:T(128)S(1)} %copy-done.16, ...), custom_call_target="tpu_custom_call" | custom-call | flops 2768240640 | bytes 8847360 | tf_op jit(solution)/shard_map/pallas_call | solution.py:55
  74.0 1.0 copy-done.4
  75.0 1.0 copy-done.6
  76.0 1.0 copy-done.8
  77.0 1.0 copy-done.10
  78.0 0.9 copy-done.12
  78.9 3.9 %all-to-all-start.1 = ((bf16[32,120,128]{2,1,0:T(8,128)(2,1)}), bf16[32,120,128]{2,1,0:T(8,128)(2,1)}, u32[]{:S(2)}, u32[]{:S(2)}) async-start(bf16[32,120,128]{2,1,0:T(8,128)(2,1)} %get-tuple-element.37), calls=%async_computation.1 | async-start | bytes 1966080 | tf_op jit(solution)/shard_map/all_to_all | solution.py:353
  82.9 1.2 copy-done.14
  84.7 22.8 %all-to-all-done.1.got_ref = bf16[32,120,128]{2,1,0:T(8,128)(2,1)} async-done(((bf16[32,120,128]{2,1,0:T(8,128)(2,1)}), bf16[32,120,128]{2,1,0:T(8,128)(2,1)}, u32[]{:S(2)}, u32[]{:S(2)}) %all-to-all-start.1) | async-done | bytes 983072 | tf_op jit(solution)/shard_map/all_to_all | solution.py:353
  107.5 1.6 copy-done.3
  109.1 3.3 %shard_map.113 = (bf16[34,128,128]{2,1,0:T(8,128)(2,1)S(1)}, bf16[144,128]{1,0:T(8,128)(2,1)S(1)}, bf16[144,128]{1,0:T(8,128)(2,1)S(1)}, bf16[144,128]{1,0:T(8,1...) custom-call(s32[2]{0:T(128)S(1)} %pad_add_fusion.here_ref, ...), custom_call_target="tpu_custom_call" | custom-call | flops 1132462080 | bytes 8847360 | tf_op jit(solution)/shard_map/pallas_call | solution.py:55
  112.4 1.0 copy-done.17
  113.5 3.7 %all-to-all-start.2 = ((bf16[32,120,128]{2,1,0:T(8,128)(2,1)}), bf16[32,120,128]{2,1,0:T(8,128)(2,1)}, u32[]{:S(2)}, u32[]{:S(2)}) async-start(bf16[32,120,128]{2,1,0:T(8,128)(2,1)} %copy-done.12), calls=%async_computation.2 | async-start | bytes 1966080 | tf_op jit(solution)/shard_map/all_to_all | solution.py:353
  117.2 1.2 copy-done.5
  118.4 1.2 copy-done.7
  119.7 1.2 copy-done.9
  120.9 1.2 copy-done.11
  122.1 4.5 %shard_map.115 = (bf16[192,128]{1,0:T(8,128)(2,1)S(1)}, bf16[192,128]{1,0:T(8,128)(2,1)S(1)}, bf16[192,128]{1,0:T(8,128)(2,1)S(1)}, bf16[192,128]{1,0:T(8,128)(2...) custom-call(s32[2]{0:T(128)S(1)} %pad_add_fusion.here_ref, ...), custom_call_target="tpu_custom_call" | custom-call | flops 1509949440 | bytes 6881280 | tf_op jit(solution)/shard_map/pallas_call | solution.py:55
  126.9 1.7 collective-permute-start.1
  128.6 1.7 collective-permute-start.3
  130.4 2.6 %collective-permute-start.5 = (bf16[192,128]{1,0:T(8,128)(2,1)S(1)}, bf16[192,128]{1,0:T(8,128)(2,1)S(1)}, u32[]{:S(2)}, u32[]{:S(2)}) collective-permute-start(bf16[192,128]{1,0:T(8,128)(2,1)S(1)} %get-tuple-element.52), channel_id=1, source_target_pairs={{0,6},{1,7},{2,4},{3,5},{4,2},{5,3},{6,0},{7,1},{8,14},{9,15},{10,... | collective-permute-start | bytes 147464 | tf_op jit(solution)/shard_map/ppermute | solution.py:358
  133.4 1.3 collective-permute-start.10
  135.2 1.4 collective-permute-done.4.refs_5_
  136.6 2.3 %collective-permute-start.12 = (bf16[144,128]{1,0:T(8,128)(2,1)S(1)}, bf16[144,128]{1,0:T(8,128)(2,1)S(1)}, u32[]{:S(2)}, u32[]{:S(2)}) collective-permute-start(bf16[144,128]{1,0:T(8,128)(2,1)S(1)} %get-tuple-element.57), channel_id=1, source_target_pairs={{0,3},{1,2},{2,1},{3,0},{4,7},{5,6},{6,5},{7,4},{8,11},{9,10},{10,... | collective-permute-start | bytes 110600 | tf_op jit(solution)/shard_map/ppermute | solution.py:358
  138.9 1.7 collective-permute-start.14
  140.6 1.9 %collective-permute-start.9 = (bf16[192,128]{1,0:T(8,128)(2,1)S(1)}, bf16[192,128]{1,0:T(8,128)(2,1)S(1)}, u32[]{:S(2)}, u32[]{:S(2)}) collective-permute-start(bf16[192,128]{1,0:T(8,128)(2,1)S(1)} %shard_map.116.refs_0_), channel_id=1, source_target_pairs={{0,24},{8,0},{16,8},{24,16},{1,25},{9,1},{17,9},{25,17},{2,26},{10... | collective-permute-start | bytes 147464 | tf_op jit(solution)/shard_map/ppermute | solution.py:363
  142.6 1.5 collective-permute-start.15
  144.0 2.6 %collective-permute-start.16 = (bf16[144,128]{1,0:T(8,128)(2,1)S(1)}, bf16[144,128]{1,0:T(8,128)(2,1)S(1)}, u32[]{:S(2)}, u32[]{:S(2)}) collective-permute-start(bf16[144,128]{1,0:T(8,128)(2,1)S(1)} %get-tuple-element.61), channel_id=1, source_target_pairs={{0,7},{1,6},{2,5},{3,4},{4,3},{5,2},{6,1},{7,0},{8,15},{9,14},{10,... | collective-permute-start | bytes 110600 | tf_op jit(solution)/shard_map/ppermute | solution.py:358
  146.6 1.1 collective-permute-start.7
  147.7 1.0 collective-permute-done.16.refs_7_
  148.7 1.9 %collective-permute-start.19 = (bf16[144,128]{1,0:T(8,128)(2,1)S(1)}, bf16[144,128]{1,0:T(8,128)(2,1)S(1)}, u32[]{:S(2)}, u32[]{:S(2)}) collective-permute-start(bf16[144,128]{1,0:T(8,128)(2,1)S(1)} %shard_map.118.refs_0_), channel_id=1, source_target_pairs={{0,24},{8,0},{16,8},{24,16},{1,25},{9,1},{17,9},{25,17},{2,26},{10... | collective-permute-start | bytes 110600 | tf_op jit(solution)/shard_map/ppermute | solution.py:363
  150.6 1.1 collective-permute-start.18
  151.7 0.8 collective-permute-done.8.refs_2_
  153.5 2.7 %collective-permute-done.18.refs_2_ = bf16[144,128]{1,0:T(8,128)(2,1)S(1)} collective-permute-done((bf16[144,128]{1,0:T(8,128)(2,1)S(1)}, bf16[144,128]{1,0:T(8,128)(2,1)S(1)}, u32[]{:S(2)}, u32[]{:S(2)}) %collective-permute-start.18) | collective-permute-done | bytes 36896 | tf_op jit(solution)/shard_map/ppermute | solution.py:363
  156.2 1.2 collective-permute-done.17.refs_1_
  157.5 1.3 collective-permute-start.25
  158.9 1.3 collective-permute-start.24
  160.1 1.8 %collective-permute-start.23 = (bf16[336,128]{1,0:T(8,128)(2,1)S(1)}, bf16[336,128]{1,0:T(8,128)(2,1)S(1)}, u32[]{:S(2)}, u32[]{:S(2)}) collective-permute-start(bf16[336,128]{1,0:T(8,128)(2,1)S(1)} %shard_map.119.refs_0_), channel_id=1, source_target_pairs={{0,4},{1,5},{2,6},{3,7},{4,0},{5,1},{6,2},{7,3},{8,12},{9,13},{10,... | collective-permute-start | bytes 258056 | tf_op jit(solution)/shard_map/ppermute | solution.py:358
  161.9 0.8 collective-permute-done.26.refs_7_
  164.1 3.1 %shard_map.114 = bf16[32,120,128]{2,1,0:T(8,128)(2,1)} custom-call(bf16[9,128,128]{2,1,0:T(8,128)(2,1)S(1)} %copy-done.22, bf16[34,128,128]{2,1,0:T(8,128)(2,1)S(1)} %copy-done.18), custom_call_target="tpu_custom_call" | custom-call | flops 1132462080 | bytes 1966080 | tf_op jit(solution)/shard_map/pallas_call | solution.py:55
  167.9 1.7 shard_map.120
  169.6 2.2 %copy.13 = bf16[1,32,120,128]{3,2,1,0:T(8,128)(2,1)} copy(bf16[1,32,120,128]{3,2,1,0:T(8,128)(2,1)} %bitcast.4) | data formatting | bytes 1966080
  (72 shorter events, 5.3 us)
Async XLA Ops:
  0.6 1.2 copy-start.13
  1.8 1.2 copy-start.19
  9.4 1.4 copy-start.2
  10.7 53.0 %copy-start.15 = (s32[2]{0:T(128)S(1)}, s32[2]{0:T(128)}, u32[]{:S(2)}) copy-start(s32[2]{0:T(128)} %dil_ref.3) | copy-start | bytes 28
  10.7 53.0 %copy-start.16 = (s32[4]{0:T(128)S(1)}, s32[4]{0:T(128)}, u32[]{:S(2)}) copy-start(s32[4]{0:T(128)} %key_ref.3) | copy-start | bytes 52
  10.7 53.0 %copy-start.20 = (bf16[2,5,128,128]{3,2,1,0:T(8,128)(2,1)S(1)}, bf16[2,5,128,128]{3,2,1,0:T(8,128)(2,1)}, u32[]{:S(2)}) copy-start(bf16[2,5,128,128]{3,2,1,0:T(8,128)(2,1)} %tw_ref.1) | copy-start | bytes 983044
  10.7 53.0 %copy-start.23 = (bf16[2,128,128]{2,1,0:T(8,128)(2,1)S(1)}, bf16[2,128,128]{2,1,0:T(8,128)(2,1)}, u32[]{:S(2)}) copy-start(bf16[2,128,128]{2,1,0:T(8,128)(2,1)} %uw_ref.1) | copy-start | bytes 196612
  63.8 10.2 %copy-start = (bf16[32,2,120,128]{3,2,1,0:T(8,128)(2,1)}, bf16[32,2,120,128]{3,2,1,0:T(8,128)(2,1)S(1)}, u32[]{:S(2)}) copy-start(bf16[32,2,120,128]{3,2,1,0:T(8,128)(2,1)S(1)} %all_to_all.15.got_ref) | copy-start | bytes 5898244
  76.0 1.0 copy-start.8
  78.9 28.6 %all-to-all-start.1 = ((bf16[32,120,128]{2,1,0:T(8,128)(2,1)}), bf16[32,120,128]{2,1,0:T(8,128)(2,1)}, u32[]{:S(2)}, u32[]{:S(2)}) async-start(bf16[32,120,128]{2,1,0:T(8,128)(2,1)} %get-tuple-element.37), calls=%async_computation.1 | async-start | bytes 1966080 | tf_op jit(solution)/shard_map/all_to_all | solution.py:353
  82.9 1.2 copy-start.14
  107.5 1.6 copy-start.3
  112.4 1.1 copy-start.17
  113.5 3.7 %copy-start.1 = (bf16[32,2,120,128]{3,2,1,0:T(8,128)(2,1)S(1)}, bf16[32,2,120,128]{3,2,1,0:T(8,128)(2,1)}, u32[]{:S(2)}) copy-start(bf16[32,2,120,128]{3,2,1,0:T(8,128)(2,1)} %copy-done) | copy-start | bytes 5898244
  113.5 56.1 %all-to-all-start.2 = ((bf16[32,120,128]{2,1,0:T(8,128)(2,1)}), bf16[32,120,128]{2,1,0:T(8,128)(2,1)}, u32[]{:S(2)}, u32[]{:S(2)}) async-start(bf16[32,120,128]{2,1,0:T(8,128)(2,1)} %copy-done.12), calls=%async_computation.2 | async-start | bytes 1966080 | tf_op jit(solution)/shard_map/all_to_all | solution.py:353
  117.2 1.2 copy-start.5
  118.4 1.2 copy-start.7
  119.7 1.2 copy-start.9
  120.9 1.2 copy-start.11
  122.1 42.0 %copy-start.18 = (bf16[34,128,128]{2,1,0:T(8,128)(2,1)S(1)}, bf16[34,128,128]{2,1,0:T(8,128)(2,1)}, u32[]{:S(2)}) copy-start(bf16[34,128,128]{2,1,0:T(8,128)(2,1)} %copy-done.17) | copy-start | bytes 3342340
  122.1 42.0 %copy-start.22 = (bf16[9,128,128]{2,1,0:T(8,128)(2,1)S(1)}, bf16[9,128,128]{2,1,0:T(8,128)(2,1)}, u32[]{:S(2)}) copy-start(bf16[9,128,128]{2,1,0:T(8,128)(2,1)} %w_ref.3) | copy-start | bytes 884740
  126.6 3.7 %collective-permute-start = (bf16[192,128]{1,0:T(8,128)(2,1)S(1)}, bf16[192,128]{1,0:T(8,128)(2,1)S(1)}, u32[]{:S(2)}, u32[]{:S(2)}) collective-permute-start(bf16[192,128]{1,0:T(8,128)(2,1)S(1)} %get-tuple-element.47), channel_id=1, source_target_pairs={{0,1},{1,0},{2,3},{3,2},{4,5},{5,4},{6,7},{7,6},{8,9},{9,8},{10,11... | collective-permute-start | bytes 147464 | tf_op jit(solution)/shard_map/ppermute | solution.py:358
  126.9 6.1 %collective-permute-start.1 = (bf16[192,128]{1,0:T(8,128)(2,1)S(1)}, bf16[192,128]{1,0:T(8,128)(2,1)S(1)}, u32[]{:S(2)}, u32[]{:S(2)}) collective-permute-start(bf16[192,128]{1,0:T(8,128)(2,1)S(1)} %get-tuple-element.48), channel_id=1, source_target_pairs={{0,2},{1,3},{2,0},{3,1},{4,6},{5,7},{6,4},{7,5},{8,10},{9,11},{10,... | collective-permute-start | bytes 147464 | tf_op jit(solution)/shard_map/ppermute | solution.py:358
  128.5 4.9 %collective-permute-start.2 = (bf16[192,128]{1,0:T(8,128)(2,1)S(1)}, bf16[192,128]{1,0:T(8,128)(2,1)S(1)}, u32[]{:S(2)}, u32[]{:S(2)}) collective-permute-start(bf16[192,128]{1,0:T(8,128)(2,1)S(1)} %get-tuple-element.49), channel_id=1, source_target_pairs={{0,3},{1,2},{2,1},{3,0},{4,7},{5,6},{6,5},{7,4},{8,11},{9,10},{10,... | collective-permute-start | bytes 147464 | tf_op jit(solution)/shard_map/ppermute | solution.py:358
  128.6 6.2 %collective-permute-start.3 = (bf16[192,128]{1,0:T(8,128)(2,1)S(1)}, bf16[192,128]{1,0:T(8,128)(2,1)S(1)}, u32[]{:S(2)}, u32[]{:S(2)}) collective-permute-start(bf16[192,128]{1,0:T(8,128)(2,1)S(1)} %get-tuple-element.50), channel_id=1, source_target_pairs={{0,4},{1,5},{2,6},{3,7},{4,0},{5,1},{6,2},{7,3},{8,12},{9,13},{10,... | collective-permute-start | bytes 147464 | tf_op jit(solution)/shard_map/ppermute | solution.py:358
  130.2 6.4 %collective-permute-start.4 = (bf16[192,128]{1,0:T(8,128)(2,1)S(1)}, bf16[192,128]{1,0:T(8,128)(2,1)S(1)}, u32[]{:S(2)}, u32[]{:S(2)}) collective-permute-start(bf16[192,128]{1,0:T(8,128)(2,1)S(1)} %get-tuple-element.51), channel_id=1, source_target_pairs={{0,5},{1,4},{2,7},{3,6},{4,1},{5,0},{6,3},{7,2},{8,13},{9,12},{10,... | collective-permute-start | bytes 147464 | tf_op jit(solution)/shard_map/ppermute | solution.py:358
  130.4 8.5 %collective-permute-start.5 = (bf16[192,128]{1,0:T(8,128)(2,1)S(1)}, bf16[192,128]{1,0:T(8,128)(2,1)S(1)}, u32[]{:S(2)}, u32[]{:S(2)}) collective-permute-start(bf16[192,128]{1,0:T(8,128)(2,1)S(1)} %get-tuple-element.52), channel_id=1, source_target_pairs={{0,6},{1,7},{2,4},{3,5},{4,2},{5,3},{6,0},{7,1},{8,14},{9,15},{10,... | collective-permute-start | bytes 147464 | tf_op jit(solution)/shard_map/ppermute | solution.py:358
  132.9 5.9 %collective-permute-start.6 = (bf16[192,128]{1,0:T(8,128)(2,1)S(1)}, bf16[192,128]{1,0:T(8,128)(2,1)S(1)}, u32[]{:S(2)}, u32[]{:S(2)}) collective-permute-start(bf16[192,128]{1,0:T(8,128)(2,1)S(1)} %get-tuple-element.53), channel_id=1, source_target_pairs={{0,7},{1,6},{2,5},{3,4},{4,3},{5,2},{6,1},{7,0},{8,15},{9,14},{10,... | collective-permute-start | bytes 147464 | tf_op jit(solution)/shard_map/ppermute | solution.py:358
  133.4 7.2 %collective-permute-start.10 = (bf16[144,128]{1,0:T(8,128)(2,1)S(1)}, bf16[144,128]{1,0:T(8,128)(2,1)S(1)}, u32[]{:S(2)}, u32[]{:S(2)}) collective-permute-start(bf16[144,128]{1,0:T(8,128)(2,1)S(1)} %get-tuple-element.55), channel_id=1, source_target_pairs={{0,1},{1,0},{2,3},{3,2},{4,5},{5,4},{6,7},{7,6},{8,9},{9,8},{10,11... | collective-permute-start | bytes 110600 | tf_op jit(solution)/shard_map/ppermute | solution.py:358
  134.7 7.8 %collective-permute-start.11 = (bf16[144,128]{1,0:T(8,128)(2,1)S(1)}, bf16[144,128]{1,0:T(8,128)(2,1)S(1)}, u32[]{:S(2)}, u32[]{:S(2)}) collective-permute-start(bf16[144,128]{1,0:T(8,128)(2,1)S(1)} %get-tuple-element.56), channel_id=1, source_target_pairs={{0,2},{1,3},{2,0},{3,1},{4,6},{5,7},{6,4},{7,5},{8,10},{9,11},{10,... | collective-permute-start | bytes 110600 | tf_op jit(solution)/shard_map/ppermute | solution.py:358
  136.6 7.4 %collective-permute-start.12 = (bf16[144,128]{1,0:T(8,128)(2,1)S(1)}, bf16[144,128]{1,0:T(8,128)(2,1)S(1)}, u32[]{:S(2)}, u32[]{:S(2)}) collective-permute-start(bf16[144,128]{1,0:T(8,128)(2,1)S(1)} %get-tuple-element.57), channel_id=1, source_target_pairs={{0,3},{1,2},{2,1},{3,0},{4,7},{5,6},{6,5},{7,4},{8,11},{9,10},{10,... | collective-permute-start | bytes 110600 | tf_op jit(solution)/shard_map/ppermute | solution.py:358
  138.9 7.7 %collective-permute-start.13 = (bf16[144,128]{1,0:T(8,128)(2,1)S(1)}, bf16[144,128]{1,0:T(8,128)(2,1)S(1)}, u32[]{:S(2)}, u32[]{:S(2)}) collective-permute-start(bf16[144,128]{1,0:T(8,128)(2,1)S(1)} %get-tuple-element.58), channel_id=1, source_target_pairs={{0,4},{1,5},{2,6},{3,7},{4,0},{5,1},{6,2},{7,3},{8,12},{9,13},{10,... | collective-permute-start | bytes 110600 | tf_op jit(solution)/shard_map/ppermute | solution.py:358
  138.9 7.7 %collective-permute-start.14 = (bf16[144,128]{1,0:T(8,128)(2,1)S(1)}, bf16[144,128]{1,0:T(8,128)(2,1)S(1)}, u32[]{:S(2)}, u32[]{:S(2)}) collective-permute-start(bf16[144,128]{1,0:T(8,128)(2,1)S(1)} %get-tuple-element.59), channel_id=1, source_target_pairs={{0,5},{1,4},{2,7},{3,6},{4,1},{5,0},{6,3},{7,2},{8,13},{9,12},{10,... | collective-permute-start | bytes 110600 | tf_op jit(solution)/shard_map/ppermute | solution.py:358
  140.6 11.0 %collective-permute-start.9 = (bf16[192,128]{1,0:T(8,128)(2,1)S(1)}, bf16[192,128]{1,0:T(8,128)(2,1)S(1)}, u32[]{:S(2)}, u32[]{:S(2)}) collective-permute-start(bf16[192,128]{1,0:T(8,128)(2,1)S(1)} %shard_map.116.refs_0_), channel_id=1, source_target_pairs={{0,24},{8,0},{16,8},{24,16},{1,25},{9,1},{17,9},{25,17},{2,26},{10... | collective-permute-start | bytes 147464 | tf_op jit(solution)/shard_map/ppermute | solution.py:363
  142.6 5.1 %collective-permute-start.15 = (bf16[144,128]{1,0:T(8,128)(2,1)S(1)}, bf16[144,128]{1,0:T(8,128)(2,1)S(1)}, u32[]{:S(2)}, u32[]{:S(2)}) collective-permute-start(bf16[144,128]{1,0:T(8,128)(2,1)S(1)} %get-tuple-element.60), channel_id=1, source_target_pairs={{0,6},{1,7},{2,4},{3,5},{4,2},{5,3},{6,0},{7,1},{8,14},{9,15},{10,... | collective-permute-start | bytes 110600 | tf_op jit(solution)/shard_map/ppermute | solution.py:358
  144.0 4.6 %collective-permute-start.16 = (bf16[144,128]{1,0:T(8,128)(2,1)S(1)}, bf16[144,128]{1,0:T(8,128)(2,1)S(1)}, u32[]{:S(2)}, u32[]{:S(2)}) collective-permute-start(bf16[144,128]{1,0:T(8,128)(2,1)S(1)} %get-tuple-element.61), channel_id=1, source_target_pairs={{0,7},{1,6},{2,5},{3,4},{4,3},{5,2},{6,1},{7,0},{8,15},{9,14},{10,... | collective-permute-start | bytes 110600 | tf_op jit(solution)/shard_map/ppermute | solution.py:358
  146.6 5.8 %collective-permute-start.8 = (bf16[192,128]{1,0:T(8,128)(2,1)S(1)}, bf16[192,128]{1,0:T(8,128)(2,1)S(1)}, u32[]{:S(2)}, u32[]{:S(2)}) collective-permute-start(bf16[192,128]{1,0:T(8,128)(2,1)S(1)} %shard_map.116.refs_0_), channel_id=1, source_target_pairs={{0,16},{8,24},{16,0},{24,8},{1,17},{9,25},{17,1},{25,9},{2,18},{10... | collective-permute-start | bytes 147464 | tf_op jit(solution)/shard_map/ppermute | solution.py:363
  146.6 6.3 %collective-permute-start.7 = (bf16[192,128]{1,0:T(8,128)(2,1)S(1)}, bf16[192,128]{1,0:T(8,128)(2,1)S(1)}, u32[]{:S(2)}, u32[]{:S(2)}) collective-permute-start(bf16[192,128]{1,0:T(8,128)(2,1)S(1)} %shard_map.116.refs_0_), channel_id=1, source_target_pairs={{0,8},{8,16},{16,24},{24,0},{1,9},{9,17},{17,25},{25,1},{2,10},{10... | collective-permute-start | bytes 147464 | tf_op jit(solution)/shard_map/ppermute | solution.py:363
  148.7 4.9 %collective-permute-start.19 = (bf16[144,128]{1,0:T(8,128)(2,1)S(1)}, bf16[144,128]{1,0:T(8,128)(2,1)S(1)}, u32[]{:S(2)}, u32[]{:S(2)}) collective-permute-start(bf16[144,128]{1,0:T(8,128)(2,1)S(1)} %shard_map.118.refs_0_), channel_id=1, source_target_pairs={{0,24},{8,0},{16,8},{24,16},{1,25},{9,1},{17,9},{25,17},{2,26},{10... | collective-permute-start | bytes 110600 | tf_op jit(solution)/shard_map/ppermute | solution.py:363
  150.6 5.6 %collective-permute-start.18 = (bf16[144,128]{1,0:T(8,128)(2,1)S(1)}, bf16[144,128]{1,0:T(8,128)(2,1)S(1)}, u32[]{:S(2)}, u32[]{:S(2)}) collective-permute-start(bf16[144,128]{1,0:T(8,128)(2,1)S(1)} %shard_map.118.refs_0_), channel_id=1, source_target_pairs={{0,16},{8,24},{16,0},{24,8},{1,17},{9,25},{17,1},{25,9},{2,18},{10... | collective-permute-start | bytes 110600 | tf_op jit(solution)/shard_map/ppermute | solution.py:363
  151.7 5.8 %collective-permute-start.17 = (bf16[144,128]{1,0:T(8,128)(2,1)S(1)}, bf16[144,128]{1,0:T(8,128)(2,1)S(1)}, u32[]{:S(2)}, u32[]{:S(2)}) collective-permute-start(bf16[144,128]{1,0:T(8,128)(2,1)S(1)} %shard_map.118.refs_0_), channel_id=1, source_target_pairs={{0,8},{8,16},{16,24},{24,0},{1,9},{9,17},{17,25},{25,1},{2,10},{10... | collective-permute-start | bytes 110600 | tf_op jit(solution)/shard_map/ppermute | solution.py:363
  157.5 5.3 %collective-permute-start.26 = (bf16[336,128]{1,0:T(8,128)(2,1)S(1)}, bf16[336,128]{1,0:T(8,128)(2,1)S(1)}, u32[]{:S(2)}, u32[]{:S(2)}) collective-permute-start(bf16[336,128]{1,0:T(8,128)(2,1)S(1)} %shard_map.119.refs_0_), channel_id=1, source_target_pairs={{0,7},{1,6},{2,5},{3,4},{4,3},{5,2},{6,1},{7,0},{8,15},{9,14},{10,... | collective-permute-start | bytes 258056 | tf_op jit(solution)/shard_map/ppermute | solution.py:358
  157.5 6.4 %collective-permute-start.25 = (bf16[336,128]{1,0:T(8,128)(2,1)S(1)}, bf16[336,128]{1,0:T(8,128)(2,1)S(1)}, u32[]{:S(2)}, u32[]{:S(2)}) collective-permute-start(bf16[336,128]{1,0:T(8,128)(2,1)S(1)} %shard_map.119.refs_0_), channel_id=1, source_target_pairs={{0,6},{1,7},{2,4},{3,5},{4,2},{5,3},{6,0},{7,1},{8,14},{9,15},{10,... | collective-permute-start | bytes 258056 | tf_op jit(solution)/shard_map/ppermute | solution.py:358
  158.9 8.4 %collective-permute-start.24 = (bf16[336,128]{1,0:T(8,128)(2,1)S(1)}, bf16[336,128]{1,0:T(8,128)(2,1)S(1)}, u32[]{:S(2)}, u32[]{:S(2)}) collective-permute-start(bf16[336,128]{1,0:T(8,128)(2,1)S(1)} %shard_map.119.refs_0_), channel_id=1, source_target_pairs={{0,5},{1,4},{2,7},{3,6},{4,1},{5,0},{6,3},{7,2},{8,13},{9,12},{10,... | collective-permute-start | bytes 258056 | tf_op jit(solution)/shard_map/ppermute | solution.py:358
  160.1 7.7 %collective-permute-start.23 = (bf16[336,128]{1,0:T(8,128)(2,1)S(1)}, bf16[336,128]{1,0:T(8,128)(2,1)S(1)}, u32[]{:S(2)}, u32[]{:S(2)}) collective-permute-start(bf16[336,128]{1,0:T(8,128)(2,1)S(1)} %shard_map.119.refs_0_), channel_id=1, source_target_pairs={{0,4},{1,5},{2,6},{3,7},{4,0},{5,1},{6,2},{7,3},{8,12},{9,13},{10,... | collective-permute-start | bytes 258056 | tf_op jit(solution)/shard_map/ppermute | solution.py:358
  161.9 5.9 %collective-permute-start.22 = (bf16[336,128]{1,0:T(8,128)(2,1)S(1)}, bf16[336,128]{1,0:T(8,128)(2,1)S(1)}, u32[]{:S(2)}, u32[]{:S(2)}) collective-permute-start(bf16[336,128]{1,0:T(8,128)(2,1)S(1)} %shard_map.119.refs_0_), channel_id=1, source_target_pairs={{0,3},{1,2},{2,1},{3,0},{4,7},{5,6},{6,5},{7,4},{8,11},{9,10},{10,... | collective-permute-start | bytes 258056 | tf_op jit(solution)/shard_map/ppermute | solution.py:358
  162.7 5.1 %collective-permute-start.21 = (bf16[336,128]{1,0:T(8,128)(2,1)S(1)}, bf16[336,128]{1,0:T(8,128)(2,1)S(1)}, u32[]{:S(2)}, u32[]{:S(2)}) collective-permute-start(bf16[336,128]{1,0:T(8,128)(2,1)S(1)} %shard_map.119.refs_0_), channel_id=1, source_target_pairs={{0,2},{1,3},{2,0},{3,1},{4,6},{5,7},{6,4},{7,5},{8,10},{9,11},{10,... | collective-permute-start | bytes 258056 | tf_op jit(solution)/shard_map/ppermute | solution.py:358
  164.0 3.9 %collective-permute-start.20 = (bf16[336,128]{1,0:T(8,128)(2,1)S(1)}, bf16[336,128]{1,0:T(8,128)(2,1)S(1)}, u32[]{:S(2)}, u32[]{:S(2)}) collective-permute-start(bf16[336,128]{1,0:T(8,128)(2,1)S(1)} %shard_map.119.refs_0_), channel_id=1, source_target_pairs={{0,1},{1,0},{2,3},{3,2},{4,5},{5,4},{6,7},{7,6},{8,9},{9,8},{10,11... | collective-permute-start | bytes 258056 | tf_op jit(solution)/shard_map/ppermute | solution.py:358
  (5 other events, 4.9 us)

commit v5 on v4

--- a/solution.py
+++ b/solution.py
@@ -14,7 +14,8 @@
 AXES = ("seg", "grp")
 BF16 = jnp.bfloat16
 F32 = jnp.float32
-VMEM_LIMIT = 32 * 1024 * 1024
+BIG_VMEM = 60 * 1024 * 1024
+SMALL_VMEM = 16 * 1024 * 1024
 
 
 def round_up(value, step):
@@ -48,17 +49,17 @@
 
 VMEM = pl.BlockSpec(memory_space=pltpu.VMEM)
 SMEM = pl.BlockSpec(memory_space=pltpu.SMEM)
-ANY = pl.BlockSpec(memory_space=pl.ANY)
-
-
-def call(kernel, outs, scratch, flops, moved, args):
+HBM = pl.BlockSpec(memory_space=pltpu.HBM)
+
+
+def call(kernel, outs, scratch, flops, moved, args, vmem=BIG_VMEM):
     return pl.pallas_call(
         kernel,
         out_shape=[jax.ShapeDtypeStruct(shape, kind) for shape, kind, _ in outs],
         in_specs=[spec for _, spec in args],
         out_specs=[spec for _, _, spec in outs],
         scratch_shapes=scratch,
-        compiler_params=pltpu.CompilerParams(vmem_limit_bytes=VMEM_LIMIT),
+        compiler_params=pltpu.CompilerParams(vmem_limit_bytes=vmem),
         cost_estimate=pl.CostEstimate(flops=flops, bytes_accessed=moved, transcendentals=0),
     )(*[value for value, _ in args])
 
@@ -68,7 +69,8 @@
 
 
 def spatial_fwd_kernel(
-    rows_step, x_hbm, w_ref, cot_hbm, send_ref, slope_hbm, x_in, xs, slopes, in_sems, cot_sem, out_sems
+    rows_step, x_hbm, w_ref, cot_hbm, send_hbm, slope_hbm,
+    x_in, xs, acts, slopes, in_sems, cot_sem, act_sems, out_sems,
 ):
     rows, cols, ch = x_in.shape
     wide = xs.shape[1]
@@ -81,12 +83,15 @@
         pltpu.make_async_copy(x_hbm.at[part(n)], x_in.at[part(n)], in_sems.at[n]) for n in range(steps)
     ]
     stores = [
-        pltpu.make_async_copy(slopes.at[part(n)], slope_hbm.at[part(n)], out_sems.at[n])
+        (
+            pltpu.make_async_copy(acts.at[part(n)], send_hbm.at[part(n), 0], act_sems.at[n]),
+            pltpu.make_async_copy(slopes.at[part(n)], slope_hbm.at[part(n)], out_sems.at[n]),
+        )
         for n in range(steps)
     ]
     for load in loads:
         load.start()
-    cot_copy = pltpu.make_async_copy(cot_hbm, send_ref.at[:, 1], cot_sem.at[0])
+    cot_copy = pltpu.make_async_copy(cot_hbm, send_hbm.at[:, 1], cot_sem.at[0])
     cot_copy.start()
     xs[0] = jnp.zeros((wide, ch), BF16)
     xs[rows + 1] = jnp.zeros((wide, ch), BF16)
@@ -112,12 +117,14 @@
         y = mm(left, weight)
         pre = y[:, ch : 2 * ch] + roll_rows(y[:, :ch], 1) + roll_rows(y[:, 2 * ch :], -1)
         act, slope = silu_parts(pre)
-        send_ref[at : at + rows_step, 0] = act.astype(BF16).reshape(rows_step, wide, ch)[:, :cols]
+        acts[at : at + rows_step] = act.astype(BF16).reshape(rows_step, wide, ch)[:, :cols]
         slopes[at : at + rows_step] = slope.reshape(rows_step, wide, ch)
-        stores[step].start()
+        for store in stores[step]:
+            store.start()
     cot_copy.wait()
-    for store in stores:
-        store.wait()
+    for pair in stores:
+        for store in pair:
+            store.wait()
 
 
 def hand_out(here_ref, total_ref, pieces):
@@ -145,21 +152,54 @@
 
 
 def spatial_wgrad_kernel(
-    rows_step, scale, here_ref, got_ref, slope_ref, cat_ref, gs, *rest
+    rows_step, scale, here_ref, got_hbm, slope_hbm, cat_hbm, gs_hbm, *rest
 ):
-    pieces, total_ref = rest[:-1], rest[-1]
-    rows, cols, ch = got_ref.shape
+    pieces = rest[:-9]
+    got, slopes, gs, cat_ref, total_ref, got_sems, slope_sems, cat_sems, gs_sems = rest[-9:]
+    rows, cols, ch = got.shape
     wide = gs.shape[1]
+    steps = rows // rows_step
+    flat = rows_step * wide
+
+    def part(step, first=0):
+        return pl.ds(first + step * rows_step, rows_step)
+
+    loads = [
+        (
+            pltpu.make_async_copy(got_hbm.at[part(n)], got.at[part(n)], got_sems.at[n]),
+            pltpu.make_async_copy(slope_hbm.at[part(n)], slopes.at[part(n)], slope_sems.at[n]),
+            pltpu.make_async_copy(
+                cat_hbm.at[pl.ds(n * flat, flat)], cat_ref.at[pl.ds(n * flat, flat)], cat_sems.at[n]
+            ),
+        )
+        for n in range(steps)
+    ]
+    for pair in loads:
+        for load in pair:
+            load.start()
+    stores = [
+        pltpu.make_async_copy(gs.at[part(n, 1)], gs_hbm.at[part(n)], gs_sems.at[n])
+        for n in range(steps)
+    ]
     gs[0] = jnp.zeros((wide, ch), BF16)
     gs[rows + 1] = jnp.zeros((wide, ch), BF16)
-    for at in range(0, rows, rows_step):
+
+    def bring(step):
+        for load in loads[step]:
+            load.wait()
+        at = step * rows_step
         gs[1 + at : 1 + at + rows_step] = jnp.zeros((rows_step, wide, ch), BF16)
         gs[1 + at : 1 + at + rows_step, :cols, :] = (
-            got_ref[at : at + rows_step].astype(F32) * slope_ref[at : at + rows_step, :cols, :]
+            got[at : at + rows_step].astype(F32) * slopes[at : at + rows_step, :cols, :]
         ).astype(BF16)
-    flat = rows_step * wide
+        stores[step].start()
+
     total = jnp.zeros((3 * ch, 3 * ch), F32)
-    for at in range(0, rows, rows_step):
+    bring(0)
+    for step in range(steps):
+        if step + 1 < steps:
+            bring(step + 1)
+        at = step * rows_step
         total = total + mm_tn(cat_ref[at * wide : at * wide + flat], taps_up(gs, at, rows_step))
     total_ref[...] = (
         jnp.concatenate(
@@ -173,11 +213,23 @@
         * scale
     ).reshape(total_ref.shape)
     hand_out(here_ref, total_ref, pieces)
-
-
-def spatial_back_kernel(rows_step, w_ref, gs, back_ref):
+    for store in stores:
+        store.wait()
+
+
+def spatial_back_kernel(rows_step, w_ref, gs_hbm, back_hbm, gs, back_ref, sem, out_sems):
     rows, cols, ch = back_ref.shape
+    stores = [
+        pltpu.make_async_copy(
+            back_ref.at[pl.ds(at, rows_step)], back_hbm.at[pl.ds(at, rows_step)], out_sems.at[n]
+        )
+        for n, at in enumerate(range(0, rows, rows_step))
+    ]
     wide = gs.shape[1]
+    load = pltpu.make_async_copy(gs_hbm, gs.at[pl.ds(1, rows)], sem.at[0])
+    load.start()
+    gs[0] = jnp.zeros((wide, ch), BF16)
+    gs[rows + 1] = jnp.zeros((wide, ch), BF16)
     weight = jnp.concatenate(
         [
             jnp.concatenate([w_ref[3 * a + b].astype(F32).T.astype(BF16) for b in range(3)], axis=1)
@@ -185,10 +237,14 @@
         ],
         axis=0,
     )
-    for at in range(0, rows, rows_step):
+    load.wait()
+    for n, at in enumerate(range(0, rows, rows_step)):
         y = mm(taps_up(gs, at, rows_step), weight)
         back = y[:, ch : 2 * ch] + roll_rows(y[:, :ch], -1) + roll_rows(y[:, 2 * ch :], 1)
         back_ref[at : at + rows_step] = back.astype(BF16).reshape(rows_step, wide, ch)[:, :cols]
+        stores[n].start()
+    for store in stores:
+        store.wait()
 
 
 def clear_halo(pad_ref, frames):
@@ -207,12 +263,25 @@
 
 
 def temporal_kernel(
-    step_frames, dil_ref, key_ref, got_ref, tw_ref, uw_ref,
-    grad_ref, united_ref, a1_hbm, feat_hbm, g1_hbm, g0_hbm,
-    a0, a1, feat, cots, g0, g1, slope0, slope1, grad_feat, sems,
+    step_frames, dil_ref, key_ref, got_hbm, tw_ref, uw_ref,
+    grad_hbm, united_hbm, a0_hbm, cots_hbm, a1_hbm, feat_hbm, g1_hbm, g0_hbm,
+    a0, a1, feat, cots, g0, g1, slope0, slope1, grad_feat, united_ref, act_ref, cot_ref, grad_ref,
+    sems, in_sems, out_sems,
 ):
-    frames, _, block, ch = got_ref.shape
+    frames, block, ch = act_ref.shape
     high = feat.shape[1]
+    loads = [
+        pltpu.make_async_copy(got_hbm.at[:, n], ref, in_sems.at[n])
+        for n, ref in enumerate((act_ref, cot_ref))
+    ]
+    for load in loads:
+        load.start()
+    stores = [
+        pltpu.make_async_copy(
+            grad_ref.at[pl.ds(at, step_frames)], grad_hbm.at[pl.ds(at, step_frames)], out_sems.at[n]
+        )
+        for n, at in enumerate(range(0, frames, step_frames))
+    ]
     segs = key_ref.shape[0]
     seg_frames = frames // segs
     inside = pl.ds(HALO, frames)
@@ -224,15 +293,19 @@
                 (feat, feat_hbm),
                 (g1.at[inside], g1_hbm),
                 (g0.at[inside], g0_hbm),
+                (a0.at[inside], a0_hbm),
+                (cots, cots_hbm),
+                (united_ref, united_hbm),
             )
         )
     ]
     for ref in (a0, a1, g0, g1):
         clear_halo(ref, frames)
     a0[HALO : HALO + frames] = jnp.zeros((frames, high, ch), BF16)
-    a0[HALO : HALO + frames, :block, :] = got_ref[:, 0]
     cots[...] = jnp.zeros(cots.shape, cots.dtype)
-    cots[:, :block, :] = got_ref[:, 1]
+    loads[0].wait()
+    a0[HALO : HALO + frames, :block, :] = act_ref[...]
+    copies[4].start()
     for layer, (source, target, slopes) in enumerate(((a0, a1, slope0), (a1, feat, slope1))):
         step_size = dil_ref[layer]
         weight = jnp.concatenate([tw_ref[layer, k] for k in range(TAPS)], axis=0)
@@ -245,6 +318,9 @@
             )
             slopes[at : at + step_frames] = slope.reshape(step_frames, high, ch)
         copies[layer].start()
+    loads[1].wait()
+    cots[:, :block, :] = cot_ref[...]
+    copies[5].start()
     for seg in range(segs):
         low, top = seg * seg_frames, (seg + 1) * seg_frames
         here = low + key_ref[seg]
@@ -261,13 +337,14 @@
         key_term = sum(mm_nt(part, uw_ref[1]) for part in three_parts(total))
         grad_feat[here] = grad_feat[here] + key_term
         g1[HALO + low : HALO + top] = (grad_feat[low:top] * slope1[low:top]).astype(BF16)
+    copies[6].start()
     for layer, source in ((1, g1), (0, g0)):
         copies[3 - layer].start()
         step_size = dil_ref[layer]
         weight = jnp.concatenate(
             [tw_ref[layer, k].astype(F32).T.astype(BF16) for k in range(TAPS)], axis=0
         )
-        for at in range(0, frames, step_frames):
+        for n, at in enumerate(range(0, frames, step_frames)):
             grad = mm(taps_of(source, at, step_frames, step_size, -1), weight).reshape(
                 step_frames, high, ch
             )
@@ -277,28 +354,42 @@
                 ).astype(BF16)
             else:
                 grad_ref[at : at + step_frames] = grad.astype(BF16)[:, :block]
-    for copy in copies:
+                stores[n].start()
+    for copy in copies + stores:
         copy.wait()
 
 
 def temporal_wgrad_kernel(
-    step_frames, scale, here_ref, dil_ref, key_ref, got_ref, a1_ref, feat, g0, g1, *rest
+    step_frames, scale, here_ref, dil_ref, key_ref,
+    a0_hbm, g0_hbm, a1_hbm, g1_hbm, feat_hbm, cots_hbm, *rest
 ):
-    pieces, (a0, a1, cots, total_ref) = rest[:-4], rest[-4:]
+    pieces, (a0, g0, a1, g1, feat, cots, total_ref, sems) = rest[:-8], rest[-8:]
     frames, high, ch = feat.shape
-    block = got_ref.shape[2]
     segs = key_ref.shape[0]
     seg_frames = frames // segs
     rows = step_frames * high
+    inside = pl.ds(HALO, frames)
+    copies = [
+        pltpu.make_async_copy(source, target, sems.at[n])
+        for n, (source, target) in enumerate(
+            (
+                (a0_hbm, a0.at[inside]),
+                (g0_hbm, g0),
+                (a1_hbm, a1.at[inside]),
+                (g1_hbm, g1),
+                (feat_hbm, feat),
+                (cots_hbm, cots),
+            )
+        )
+    ]
+    for copy in copies:
+        copy.start()
     clear_halo(a0, frames)
     clear_halo(a1, frames)
-    a0[HALO : HALO + frames] = jnp.zeros((frames, high, ch), BF16)
-    a0[HALO : HALO + frames, :block, :] = got_ref[:, 0]
-    a1[HALO : HALO + frames] = a1_ref[...]
-    cots[...] = jnp.zeros(cots.shape, cots.dtype)
-    cots[:, :block, :] = got_ref[:, 1]
     totals = []
     for layer, acts, grads in ((0, a0, g0), (1, a1, g1)):
+        copies[2 * layer].wait()
+        copies[2 * layer + 1].wait()
         total = jnp.zeros((TAPS * ch, ch), F32)
         for at in range(0, frames, step_frames):
             total = total + mm_tn(
@@ -306,6 +397,8 @@
                 grads[at : at + step_frames].reshape(rows, ch),
             )
         totals.append(total)
+    copies[4].wait()
+    copies[5].wait()
     total = jnp.zeros((ch, ch), F32)
     for at in range(0, frames, step_frames):
         total = total + mm_tn(
@@ -339,7 +432,10 @@
 
 
 def deal_kernel(here_ref, *refs):
-    pieces, outs = refs[:-3], refs[-3:]
+    united_hbm, *pieces = refs[:-5]
+    *outs, united_out, sem = refs[-5:]
+    copy = pltpu.make_async_copy(united_hbm, united_out, sem.at[0])
+    copy.start()
     for peer, piece in enumerate(pieces):
         place = jnp.bitwise_xor(here_ref[1], peer)
         at = 0
@@ -347,6 +443,7 @@
             count = out_ref.shape[1]
             out_ref[place] = piece[at : at + count].astype(F32)
             at += count
+    copy.wait()
 
 
 def exchange(blocks):
@@ -367,7 +464,7 @@
     shape = parts[0].shape
     return call(
         sum_kernel, [(shape, BF16, VMEM)], [], 0, len(parts) * 2 * shape[0] * shape[1],
-        [(part, VMEM) for part in parts],
+        [(part, VMEM) for part in parts], SMALL_VMEM,
     )[0]
 
 
@@ -401,27 +498,29 @@
 
     send, space_slope = call(
         functools.partial(spatial_fwd_kernel, rows_step),
-        [((rows, 2, cols, ch), BF16, VMEM), ((rows, wide, ch), F32, ANY)],
+        [((rows, 2, cols, ch), BF16, HBM), ((rows, wide, ch), F32, HBM)],
         [
             pltpu.VMEM((rows, cols, ch), BF16),
             pltpu.VMEM((rows + 2, wide, ch), BF16),
+            pltpu.VMEM((rows, cols, ch), BF16),
             pltpu.VMEM((rows, wide, ch), F32),
             pltpu.SemaphoreType.DMA((steps,)),
             pltpu.SemaphoreType.DMA((1,)),
             pltpu.SemaphoreType.DMA((steps,)),
+            pltpu.SemaphoreType.DMA((steps,)),
         ],
         2 * 9 * pixels * ch * ch,
         pixels * ch * 12,
-        [(frames_in[0], ANY), (spatial_weight, VMEM), (cotangent[0], ANY)],
+        [(frames_in[0], HBM), (spatial_weight, VMEM), (cotangent[0], HBM)],
     )
     send = send.reshape(rows, 2, split, block, ch).swapaxes(1, 2).reshape(devices, 2, block, ch)
     got = exchange(send)
 
     padded = (frames + 2 * HALO, high, ch)
     whole = (frames, high, ch)
-    grad_send, united_send, a1, feat, g1, g0 = call(
+    grad_send, united_send, a0, cots, a1, feat, g1, g0 = call(
         functools.partial(temporal_kernel, step_frames),
-        [((frames, block, ch), BF16, VMEM)] * 2 + [(whole, BF16, ANY)] * 4,
+        [((frames, block, ch), BF16, HBM)] * 2 + [(whole, BF16, HBM)] * 6,
         [
             pltpu.VMEM(padded, BF16),
             pltpu.VMEM(padded, BF16),
@@ -432,12 +531,18 @@
             pltpu.VMEM(whole, F32),
             pltpu.VMEM(whole, F32),
             pltpu.VMEM(whole, F32),
-            pltpu.SemaphoreType.DMA((4,)),
+            pltpu.VMEM((frames, block, ch), BF16),
+            pltpu.VMEM((frames, block, ch), BF16),
+            pltpu.VMEM((frames, block, ch), BF16),
+            pltpu.VMEM((frames, block, ch), BF16),
+            pltpu.SemaphoreType.DMA((7,)),
+            pltpu.SemaphoreType.DMA((2,)),
+            pltpu.SemaphoreType.DMA((frames // step_frames,)),
         ],
         2 * 22 * frames * block * ch * ch,
         frames * block * ch * 18,
         [
-            (dilation, SMEM), (key_index, SMEM), (got, VMEM),
+            (dilation, SMEM), (key_index, SMEM), (got, HBM),
             (temporal_weight, VMEM), (uniting_weight, VMEM),
         ],
     )
@@ -447,18 +552,23 @@
         [((time_rows + unite_rows, ch), BF16, VMEM)] * peers,
         [
             pltpu.VMEM(padded, BF16),
+            pltpu.VMEM(whole, BF16),
             pltpu.VMEM(padded, BF16),
             pltpu.VMEM(whole, BF16),
+            pltpu.VMEM(whole, BF16),
+            pltpu.VMEM(whole, BF16),
             pltpu.VMEM((peers, time_rows + unite_rows, ch), F32),
+            pltpu.SemaphoreType.DMA((6,)),
         ],
         2 * 12 * frames * block * ch * ch,
         frames * block * ch * 14,
         [
-            (here, SMEM), (dilation, SMEM), (key_index, SMEM), (got, VMEM),
-            (a1, VMEM), (feat, VMEM), (g0, VMEM), (g1, VMEM),
+            (here, SMEM), (dilation, SMEM), (key_index, SMEM),
+            (a0, HBM), (g0, HBM), (a1, HBM), (g1, HBM), (feat, HBM), (cots, HBM),
         ],
     )
-    time_sum = sum_of(all_turns(reduce_in_grp(time_pieces)))
+    time_sum = reduce_in_grp(time_pieces)
+    time_sum, grad_time = lax.optimization_barrier((time_sum, grad_time))
     (x_cat,) = call(
         functools.partial(columns_kernel, rows_step),
         [((rows * wide, 3 * ch), BF16, VMEM)],
@@ -469,38 +579,55 @@
     )
     gs, *space_pieces = call(
         functools.partial(spatial_wgrad_kernel, rows_step, scale),
-        [((rows + 2, wide, ch), BF16, VMEM)] + [((space_rows, ch), BF16, VMEM)] * peers,
-        [pltpu.VMEM((peers, space_rows, ch), F32)],
+        [((rows, wide, ch), BF16, HBM)] + [((space_rows, ch), BF16, VMEM)] * peers,
+        [
+            pltpu.VMEM((rows, cols, ch), BF16),
+            pltpu.VMEM((rows, wide, ch), F32),
+            pltpu.VMEM((rows + 2, wide, ch), BF16),
+            pltpu.VMEM((rows * wide, 3 * ch), BF16),
+            pltpu.VMEM((peers, space_rows, ch), F32),
+        ]
+        + [pltpu.SemaphoreType.DMA((steps,))] * 4,
         2 * 9 * pixels * ch * ch,
         pixels * ch * 18,
-        [(here, SMEM), (grad_time, VMEM), (space_slope, VMEM), (x_cat, VMEM)],
+        [(here, SMEM), (grad_time, HBM), (space_slope, HBM), (x_cat, HBM)],
     )
     united_send, space_pieces[0] = lax.optimization_barrier((united_send, space_pieces[0]))
     united = exchange(united_send)
     (back,) = call(
         functools.partial(spatial_back_kernel, rows_step),
-        [((rows, cols, ch), BF16, VMEM)],
-        [],
+        [((rows, cols, ch), BF16, HBM)],
+        [
+            pltpu.VMEM((rows + 2, wide, ch), BF16),
+            pltpu.VMEM((rows, cols, ch), BF16),
+            pltpu.SemaphoreType.DMA((1,)),
+            pltpu.SemaphoreType.DMA((steps,)),
+        ],
         2 * 9 * pixels * ch * ch,
         pixels * ch * 4,
-        [(spatial_weight, VMEM), (gs, VMEM)],
-    )
-    space_parts = all_turns(reduce_in_grp(space_pieces))
-    (piece,) = call(
+        [(spatial_weight, VMEM), (gs, HBM)],
+    )
+    space_parts = [flip(part, peer) if peer else part for peer, part in enumerate(space_pieces)]
+    (plane,) = call(
         join_kernel,
         [((time_rows + unite_rows + space_rows, ch), BF16, VMEM)],
         [],
         0,
-        10 * space_rows * ch,
+        2 * (peers + 10) * space_rows * ch,
         [(time_sum, VMEM)] + [(part, VMEM) for part in space_parts],
-    )
-    grads = call(
+        SMALL_VMEM,
+    )
+    piece = sum_of(all_turns(plane))
+    *grads, united = call(
         deal_kernel,
-        [((peers, count, ch), F32, VMEM) for count in (time_rows, unite_rows, space_rows)],
-        [],
+        [((peers, count, ch), F32, VMEM) for count in (time_rows, unite_rows, space_rows)]
+        + [((frames, block, ch), BF16, HBM)],
+        [pltpu.SemaphoreType.DMA((1,))],
         0,
         6 * 21 * ch * ch,
-        [(here, SMEM)] + [(flip(piece, peer) if peer else piece, VMEM) for peer in range(peers)],
+        [(here, SMEM), (united, HBM)]
+        + [(flip(piece, peer) if peer else piece, VMEM) for peer in range(peers)],
+        SMALL_VMEM,
     )
     return (
         united.reshape(frames_in.shape),

time: 172 us -> 183 us (1.064)
  Pallas kernels: 28.9 us -> 70 us
  local copies, waits for them, and re-layouts: 20.6 us -> 1.72 us
  waiting for transfers between devices: 33 us -> 19.5 us
    pallas_call x11 -> x10, Pallas kernels: 28.9 us -> 70 us  [call(): pl.pallas_call(kernel, out_shape=[jax.ShapeDtypeStruct(shape, kind) for s...]
    all_to_all x2, waiting for transfers between devices: 22.8 us -> 3.46 us  [exchange(): return lax.all_to_all(blocks, AXES, split_axis=0, concat_axis=0, tiled=True)]
    unnamed x49 -> x8, local copies, waits for them, and re-layouts: 20.6 us -> 1.72 us
    ppermute x21, waiting for transfers between devices: 4.49 us -> 8.41 us  [flip(): return lax.ppermute(value, 'grp', [(i, i ^ peer) for i in range(size)])]
    ppermute x21, starting transfers between devices: 21.7 us -> 24.2 us  [flip(): return lax.ppermute(value, 'grp', [(i, i ^ peer) for i in range(size)])]
    ppermute x6 -> x3, waiting for transfers between devices: 5.71 us -> 7.63 us  [turn_by(): lax.ppermute(value, 'seg', [(i, (i + turn) % size) for i in range(size)])]
    ppermute x6 -> x3, starting transfers between devices: 6 us -> 4.36 us  [turn_by(): lax.ppermute(value, 'seg', [(i, (i + turn) % size) for i in range(size)])]
  transfers between devices with their start and end apart: 29 -> 26, of which waited for: 11 -> 8; matrix products, arithmetic and copies ran while one was open for 0% -> 0% of each run, Pallas kernels for 6% -> 10%
where the time goes in v5:
time: 183 us; the launch traced here: 182 us
  Pallas kernels  70 us (38%)
  blocking collectives  53.3 us (29%)
  starting transfers between devices  36 us (20%)
  waiting for transfers between devices  19.5 us (11%)
    pallas_call x10, Pallas kernels, call(): pl.pallas_call(kernel, out_shape=[jax.ShapeDtypeStruct(shape, kind) for s...  70 us
    all_to_all x1, blocking collectives, exchange(): return lax.all_to_all(blocks, AXES, split_axis=0, concat_axis=0, tiled=True)  53.3 us
    ppermute x21, starting transfers between devices, flip(): return lax.ppermute(value, 'grp', [(i, i ^ peer) for i in range(size)])  24.2 us
    ppermute x21, waiting for transfers between devices, flip(): return lax.ppermute(value, 'grp', [(i, i ^ peer) for i in range(size)])  8.41 us
    ppermute x3, waiting for transfers between devices, turn_by(): lax.ppermute(value, 'seg', [(i, (i + turn) % size) for i in range(size)])  7.63 us
    all_to_all x2, starting transfers between devices, exchange(): return lax.all_to_all(blocks, AXES, split_axis=0, concat_axis=0, tiled=True)  7.43 us
    ppermute x3, starting transfers between devices, turn_by(): lax.ppermute(value, 'seg', [(i, (i + turn) % size) for i in range(size)])  4.36 us
  transfers between devices with their start and end apart: 26, of which 8 were waited for; matrix products, arithmetic and copies ran while one was open for 0% of the time, Pallas kernels for 10%

profile of v5, /device:TPU:0, one launch (start us, length us, event | category | flops | bytes accessed | tf_op | source)
XLA Modules:
  0.0 182.2 jit_solution(5325921591830408492)
XLA Ops:
  0.6 32.1 %shard_map.110 = (bf16[32,2,120,128]{3,2,1,0:T(8,128)(2,1)}, f32[32,128,128]{2,1,0:T(8,128)}) custom-call(bf16[32,120,128]{2,1,0:T(8,128)(2,1)} %bitcast.9, bf16[9,128,128]{2,1,0:T(8,128)(2,1)} %w_ref.3, bf16[32,120,128]{2,1,0:T(8,128)(2,1)} %bitcast.11), custom_call_target="tpu_custom_call" | custom-call | flops 1132462080 | bytes 5898240 | tf_op jit(solution)/shard_map/pallas_call | solution.py:56
  32.7 53.3 %all_to_all.15.got_hbm = bf16[32,2,120,128]{3,2,1,0:T(8,128)(2,1)} all-to-all(bf16[32,2,120,128]{3,2,1,0:T(8,128)(2,1)} %get-tuple-element.40), channel_id=1, replica_groups=mesh['seg'=4,'grp'=8] {'seg','grp'}, dimensions={0} | all-to-all | bytes 3932160 | tf_op jit(solution)/shard_map/all_to_all | solution.py:450
  86.1 11.6 %shard_map.111 = (bf16[32,120,128]{2,1,0:T(8,128)(2,1)}, bf16[32,120,128]{2,1,0:T(8,128)(2,1)}, bf16[32,128,128]{2,1,0:T(8,128)(2,1)}, bf16[32,128,128]{2,1,0:T(...) custom-call(s32[2]{0:T(128)} %dil_ref.3, ...), custom_call_target="tpu_custom_call" | custom-call | flops 2768240640 | bytes 8847360 | tf_op jit(solution)/shard_map/pallas_call | solution.py:56
  97.7 3.8 %all-to-all-start.1 = ((bf16[32,120,128]{2,1,0:T(8,128)(2,1)}), bf16[32,120,128]{2,1,0:T(8,128)(2,1)S(1)}, u32[]{:S(2)}, u32[]{:S(2)}) async-start(bf16[32,120,128]{2,1,0:T(8,128)(2,1)} %get-tuple-element.56), calls=%async_computation.1 | async-start | bytes 1966080 | tf_op jit(solution)/shard_map/all_to_all | solution.py:450
  101.5 0.7 pad_add_fusion.here_ref
  102.2 9.3 %shard_map.112 = (bf16[192,128]{1,0:T(8,128)(2,1)}, bf16[192,128]{1,0:T(8,128)(2,1)}, bf16[192,128]{1,0:T(8,128)(2,1)}, bf16[192,128]{1,0:T(8,128)(2,1)}, bf16[1...) custom-call(s32[2]{0:T(128)} %pad_add_fusion.here_ref, ...), custom_call_target="tpu_custom_call" | custom-call | flops 1509949440 | bytes 6881280 | tf_op jit(solution)/shard_map/pallas_call | solution.py:56
  111.5 0.0 copy-start
  111.5 0.1 collective-permute-start
  111.7 1.7 collective-permute-start.1
  113.3 0.1 collective-permute-start.2
  113.5 1.6 collective-permute-start.3
  115.0 0.1 collective-permute-start.4
  115.2 2.6 %collective-permute-start.5 = (bf16[192,128]{1,0:T(8,128)(2,1)}, bf16[192,128]{1,0:T(8,128)(2,1)S(1)}, u32[]{:S(2)}, u32[]{:S(2)}) collective-permute-start(bf16[192,128]{1,0:T(8,128)(2,1)} %get-tuple-element.54), channel_id=1, source_target_pairs={{0,6},{1,7},{2,4},{3,5},{4,2},{5,3},{6,0},{7,1},{8,14},{9,15},{10,... | collective-permute-start | bytes 147464 | tf_op jit(solution)/shard_map/ppermute | solution.py:455
  117.7 0.0 collective-permute-done.1.refs_2_
  117.8 0.4 collective-permute-start.6
  118.1 3.4 %shard_map.114.cat_hbm = bf16[4096,384]{1,0:T(8,128)(2,1)} custom-call(bf16[32,120,128]{2,1,0:T(8,128)(2,1)} %bitcast.10), custom_call_target="tpu_custom_call" | custom-call | bytes 3932160 | tf_op jit(solution)/shard_map/pallas_call | solution.py:56
  121.6 0.0 collective-permute-done.2.refs_3_
  121.6 0.0 collective-permute-done.3.refs_4_
  121.6 1.1 collective-permute-done.6.refs_7_
  122.7 0.1 shard_map.113.first_ref
  122.7 3.5 %all-to-all-done.1.got_hbm = bf16[32,120,128]{2,1,0:T(8,128)(2,1)S(1)} async-done(((bf16[32,120,128]{2,1,0:T(8,128)(2,1)}), bf16[32,120,128]{2,1,0:T(8,128)(2,1)S(1)}, u32[]{:S(2)}, u32[]{:S(2)}) %all-to-all-start.1) | async-done | bytes 983072 | tf_op jit(solution)/shard_map/all_to_all | solution.py:450
  126.2 0.9 copy-done.3
  127.1 5.8 %shard_map.115 = (bf16[32,128,128]{2,1,0:T(8,128)(2,1)}, bf16[144,128]{1,0:T(8,128)(2,1)}, bf16[144,128]{1,0:T(8,128)(2,1)}, bf16[144,128]{1,0:T(8,128)(2,1)}, b...) custom-call(s32[2]{0:T(128)} %pad_add_fusion.here_ref, ...), custom_call_target="tpu_custom_call" | custom-call | flops 1132462080 | bytes 8847360 | tf_op jit(solution)/shard_map/pallas_call | solution.py:56
  133.0 3.6 %all-to-all-start.2 = ((bf16[32,120,128]{2,1,0:T(8,128)(2,1)}), bf16[32,120,128]{2,1,0:T(8,128)(2,1)S(1)}, u32[]{:S(2)}, u32[]{:S(2)}) async-start(bf16[32,120,128]{2,1,0:T(8,128)(2,1)} %get-tuple-element.60), calls=%async_computation.2 | async-start | bytes 1966080 | tf_op jit(solution)/shard_map/all_to_all | solution.py:450
  136.6 1.8 %collective-permute-start.10 = (bf16[144,128]{1,0:T(8,128)(2,1)}, bf16[144,128]{1,0:T(8,128)(2,1)S(1)}, u32[]{:S(2)}, u32[]{:S(2)}) collective-permute-start(bf16[144,128]{1,0:T(8,128)(2,1)} %get-tuple-element.66), channel_id=1, source_target_pairs={{0,4},{1,5},{2,6},{3,7},{4,0},{5,1},{6,2},{7,3},{8,12},{9,13},{10,... | collective-permute-start | bytes 110600 | tf_op jit(solution)/shard_map/ppermute | solution.py:455
  138.4 2.4 %collective-permute-start.12 = (bf16[144,128]{1,0:T(8,128)(2,1)}, bf16[144,128]{1,0:T(8,128)(2,1)S(1)}, u32[]{:S(2)}, u32[]{:S(2)}) collective-permute-start(bf16[144,128]{1,0:T(8,128)(2,1)} %get-tuple-element.68), channel_id=1, source_target_pairs={{0,6},{1,7},{2,4},{3,5},{4,2},{5,3},{6,0},{7,1},{8,14},{9,15},{10,... | collective-permute-start | bytes 110600 | tf_op jit(solution)/shard_map/ppermute | solution.py:455
  140.8 0.3 collective-permute-start.13
  141.1 0.4 collective-permute-start.7
  141.5 3.6 %collective-permute-done.10.refs_4_ = bf16[144,128]{1,0:T(8,128)(2,1)S(1)} collective-permute-done((bf16[144,128]{1,0:T(8,128)(2,1)}, bf16[144,128]{1,0:T(8,128)(2,1)S(1)}, u32[]{:S(2)}, u32[]{:S(2)}) %collective-permute-start.10) | collective-permute-done | bytes 36896 | tf_op jit(solution)/shard_map/ppermute | solution.py:455
  145.1 6.0 %collective-permute-start.8 = (bf16[144,128]{1,0:T(8,128)(2,1)}, bf16[144,128]{1,0:T(8,128)(2,1)S(1)}, u32[]{:S(2)}, u32[]{:S(2)}) collective-permute-start(bf16[144,128]{1,0:T(8,128)(2,1)} %get-tuple-element.64), channel_id=1, source_target_pairs={{0,2},{1,3},{2,0},{3,1},{4,6},{5,7},{6,4},{7,5},{8,10},{9,11},{10,... | collective-permute-start | bytes 110600 | tf_op jit(solution)/shard_map/ppermute | solution.py:455
  151.1 0.1 collective-permute-start.9
  151.2 2.7 %collective-permute-done.8.refs_2_ = bf16[144,128]{1,0:T(8,128)(2,1)S(1)} collective-permute-done((bf16[144,128]{1,0:T(8,128)(2,1)}, bf16[144,128]{1,0:T(8,128)(2,1)S(1)}, u32[]{:S(2)}, u32[]{:S(2)}) %collective-permute-start.8) | collective-permute-done | bytes 36896 | tf_op jit(solution)/shard_map/ppermute | solution.py:455
  153.8 0.8 collective-permute-done.9.refs_3_
  154.7 0.8 copy-done.1
  155.5 1.3 collective-permute-start.14
  156.8 3.1 %collective-permute-start.15 = (bf16[336,128]{1,0:T(8,128)(2,1)S(1)}, bf16[336,128]{1,0:T(8,128)(2,1)S(1)}, u32[]{:S(2)}, u32[]{:S(2)}) collective-permute-start(bf16[336,128]{1,0:T(8,128)(2,1)S(1)} %shard_map.116.refs_0_), channel_id=1, source_target_pairs={{0,16},{8,24},{16,0},{24,8},{1,17},{9,25},{17,1},{25,9},{2,18},{10... | collective-permute-start | bytes 258056 | tf_op jit(solution)/shard_map/ppermute | solution.py:460
  159.8 3.0 %collective-permute-done.14.refs_1_ = bf16[336,128]{1,0:T(8,128)(2,1)S(1)} collective-permute-done((bf16[336,128]{1,0:T(8,128)(2,1)S(1)}, bf16[336,128]{1,0:T(8,128)(2,1)S(1)}, u32[]{:S(2)}, u32[]{:S(2)}) %collective-permute-start.14) | collective-permute-done | bytes 86048 | tf_op jit(solution)/shard_map/ppermute | solution.py:460
  162.8 4.7 %collective-permute-done.15.refs_2_ = bf16[336,128]{1,0:T(8,128)(2,1)S(1)} collective-permute-done((bf16[336,128]{1,0:T(8,128)(2,1)S(1)}, bf16[336,128]{1,0:T(8,128)(2,1)S(1)}, u32[]{:S(2)}, u32[]{:S(2)}) %collective-permute-start.15) | collective-permute-done | bytes 86048 | tf_op jit(solution)/shard_map/ppermute | solution.py:460
  167.5 0.1 collective-permute-start.17
  167.6 1.5 collective-permute-start.18
  169.1 0.4 collective-permute-start.19
  169.5 1.4 collective-permute-start.20
  170.9 0.3 collective-permute-start.21
  171.2 2.3 %collective-permute-start.22 = (bf16[336,128]{1,0:T(8,128)(2,1)S(1)}, bf16[336,128]{1,0:T(8,128)(2,1)S(1)}, u32[]{:S(2)}, u32[]{:S(2)}) collective-permute-start(bf16[336,128]{1,0:T(8,128)(2,1)S(1)} %shard_map.117.refs_1_), channel_id=1, source_target_pairs={{0,6},{1,7},{2,4},{3,5},{4,2},{5,3},{6,0},{7,1},{8,14},{9,15},{10,... | collective-permute-start | bytes 258056 | tf_op jit(solution)/shard_map/ppermute | solution.py:455
  173.5 0.6 collective-permute-start.23
  174.2 5.0 %shard_map.119 = bf16[32,120,128]{2,1,0:T(8,128)(2,1)} custom-call(bf16[9,128,128]{2,1,0:T(8,128)(2,1)} %w_ref.3, bf16[32,128,128]{2,1,0:T(8,128)(2,1)} %get-tuple-element.71.gs_hbm), custom_call_target="tpu_custom_call" | custom-call | flops 1132462080 | bytes 1966080 | tf_op jit(solution)/shard_map/pallas_call | solution.py:56
  179.2 0.2 collective-permute-done.21.refs_6_
  179.4 2.6 %shard_map.118 = (f32[8,160,128]{2,1,0:T(8,128)}, f32[8,32,128]{2,1,0:T(8,128)}, f32[8,144,128]{2,1,0:T(8,128)}, bf16[32,120,128]{2,1,0:T(8,128)(2,1)}) custom-call(s32[2]{0:T(128)S(1)} %copy-done.2, bf16[32,120,128]{2,1,0:T(8,128)(2,1)S(1)} %all-to-all-done.2.refs_0_, bf16[336,128]{1,0:T(8,128)(2,1)S(1)} %shard_map.117.refs_1_, ...), custom_call_target="tpu_custom_call" | custom-call | bytes 2064384 | tf_op jit(solution)/shard_map/pallas_call | solution.py:56
  (24 shorter events, 0.2 us)
Async XLA Ops:
  97.7 28.5 %all-to-all-start.1 = ((bf16[32,120,128]{2,1,0:T(8,128)(2,1)}), bf16[32,120,128]{2,1,0:T(8,128)(2,1)S(1)}, u32[]{:S(2)}, u32[]{:S(2)}) async-start(bf16[32,120,128]{2,1,0:T(8,128)(2,1)} %get-tuple-element.56), calls=%async_computation.1 | async-start | bytes 1966080 | tf_op jit(solution)/shard_map/all_to_all | solution.py:450
  111.5 11.2 %copy-start = (bf16[192,128]{1,0:T(8,128)(2,1)S(1)}, bf16[192,128]{1,0:T(8,128)(2,1)}, u32[]{:S(2)}) copy-start(bf16[192,128]{1,0:T(8,128)(2,1)} %get-tuple-element.48.refs_0_) | copy-start | bytes 147460
  111.5 3.6 %collective-permute-start = (bf16[192,128]{1,0:T(8,128)(2,1)}, bf16[192,128]{1,0:T(8,128)(2,1)S(1)}, u32[]{:S(2)}, u32[]{:S(2)}) collective-permute-start(bf16[192,128]{1,0:T(8,128)(2,1)} %get-tuple-element.49), channel_id=1, source_target_pairs={{0,1},{1,0},{2,3},{3,2},{4,5},{5,4},{6,7},{7,6},{8,9},{9,8},{10,11... | collective-permute-start | bytes 147464 | tf_op jit(solution)/shard_map/ppermute | solution.py:455
  111.7 6.1 %collective-permute-start.1 = (bf16[192,128]{1,0:T(8,128)(2,1)}, bf16[192,128]{1,0:T(8,128)(2,1)S(1)}, u32[]{:S(2)}, u32[]{:S(2)}) collective-permute-start(bf16[192,128]{1,0:T(8,128)(2,1)} %get-tuple-element.50), channel_id=1, source_target_pairs={{0,2},{1,3},{2,0},{3,1},{4,6},{5,7},{6,4},{7,5},{8,10},{9,11},{10,... | collective-permute-start | bytes 147464 | tf_op jit(solution)/shard_map/ppermute | solution.py:455
  113.3 8.2 %collective-permute-start.2 = (bf16[192,128]{1,0:T(8,128)(2,1)}, bf16[192,128]{1,0:T(8,128)(2,1)S(1)}, u32[]{:S(2)}, u32[]{:S(2)}) collective-permute-start(bf16[192,128]{1,0:T(8,128)(2,1)} %get-tuple-element.51), channel_id=1, source_target_pairs={{0,3},{1,2},{2,1},{3,0},{4,7},{5,6},{6,5},{7,4},{8,11},{9,10},{10,... | collective-permute-start | bytes 147464 | tf_op jit(solution)/shard_map/ppermute | solution.py:455
  113.5 8.1 %collective-permute-start.3 = (bf16[192,128]{1,0:T(8,128)(2,1)}, bf16[192,128]{1,0:T(8,128)(2,1)S(1)}, u32[]{:S(2)}, u32[]{:S(2)}) collective-permute-start(bf16[192,128]{1,0:T(8,128)(2,1)} %get-tuple-element.52), channel_id=1, source_target_pairs={{0,4},{1,5},{2,6},{3,7},{4,0},{5,1},{6,2},{7,3},{8,12},{9,13},{10,... | collective-permute-start | bytes 147464 | tf_op jit(solution)/shard_map/ppermute | solution.py:455
  115.0 6.5 %collective-permute-start.4 = (bf16[192,128]{1,0:T(8,128)(2,1)}, bf16[192,128]{1,0:T(8,128)(2,1)S(1)}, u32[]{:S(2)}, u32[]{:S(2)}) collective-permute-start(bf16[192,128]{1,0:T(8,128)(2,1)} %get-tuple-element.53), channel_id=1, source_target_pairs={{0,5},{1,4},{2,7},{3,6},{4,1},{5,0},{6,3},{7,2},{8,13},{9,12},{10,... | collective-permute-start | bytes 147464 | tf_op jit(solution)/shard_map/ppermute | solution.py:455
  115.2 6.4 %collective-permute-start.5 = (bf16[192,128]{1,0:T(8,128)(2,1)}, bf16[192,128]{1,0:T(8,128)(2,1)S(1)}, u32[]{:S(2)}, u32[]{:S(2)}) collective-permute-start(bf16[192,128]{1,0:T(8,128)(2,1)} %get-tuple-element.54), channel_id=1, source_target_pairs={{0,6},{1,7},{2,4},{3,5},{4,2},{5,3},{6,0},{7,1},{8,14},{9,15},{10,... | collective-permute-start | bytes 147464 | tf_op jit(solution)/shard_map/ppermute | solution.py:455
  117.8 4.9 %collective-permute-start.6 = (bf16[192,128]{1,0:T(8,128)(2,1)}, bf16[192,128]{1,0:T(8,128)(2,1)S(1)}, u32[]{:S(2)}, u32[]{:S(2)}) collective-permute-start(bf16[192,128]{1,0:T(8,128)(2,1)} %get-tuple-element.55), channel_id=1, source_target_pairs={{0,7},{1,6},{2,5},{3,4},{4,3},{5,2},{6,1},{7,0},{8,15},{9,14},{10,... | collective-permute-start | bytes 147464 | tf_op jit(solution)/shard_map/ppermute | solution.py:455
  126.2 0.9 copy-start.3
  133.0 46.5 %all-to-all-start.2 = ((bf16[32,120,128]{2,1,0:T(8,128)(2,1)}), bf16[32,120,128]{2,1,0:T(8,128)(2,1)S(1)}, u32[]{:S(2)}, u32[]{:S(2)}) async-start(bf16[32,120,128]{2,1,0:T(8,128)(2,1)} %get-tuple-element.60), calls=%async_computation.2 | async-start | bytes 1966080 | tf_op jit(solution)/shard_map/all_to_all | solution.py:450
  136.6 8.5 %collective-permute-start.10 = (bf16[144,128]{1,0:T(8,128)(2,1)}, bf16[144,128]{1,0:T(8,128)(2,1)S(1)}, u32[]{:S(2)}, u32[]{:S(2)}) collective-permute-start(bf16[144,128]{1,0:T(8,128)(2,1)} %get-tuple-element.66), channel_id=1, source_target_pairs={{0,4},{1,5},{2,6},{3,7},{4,0},{5,1},{6,2},{7,3},{8,12},{9,13},{10,... | collective-permute-start | bytes 110600 | tf_op jit(solution)/shard_map/ppermute | solution.py:455
  138.4 12.6 %collective-permute-start.11 = (bf16[144,128]{1,0:T(8,128)(2,1)}, bf16[144,128]{1,0:T(8,128)(2,1)S(1)}, u32[]{:S(2)}, u32[]{:S(2)}) collective-permute-start(bf16[144,128]{1,0:T(8,128)(2,1)} %get-tuple-element.67), channel_id=1, source_target_pairs={{0,5},{1,4},{2,7},{3,6},{4,1},{5,0},{6,3},{7,2},{8,13},{9,12},{10,... | collective-permute-start | bytes 110600 | tf_op jit(solution)/shard_map/ppermute | solution.py:455
  138.4 12.7 %collective-permute-start.12 = (bf16[144,128]{1,0:T(8,128)(2,1)}, bf16[144,128]{1,0:T(8,128)(2,1)S(1)}, u32[]{:S(2)}, u32[]{:S(2)}) collective-permute-start(bf16[144,128]{1,0:T(8,128)(2,1)} %get-tuple-element.68), channel_id=1, source_target_pairs={{0,6},{1,7},{2,4},{3,5},{4,2},{5,3},{6,0},{7,1},{8,14},{9,15},{10,... | collective-permute-start | bytes 110600 | tf_op jit(solution)/shard_map/ppermute | solution.py:455
  140.8 10.3 %collective-permute-start.13 = (bf16[144,128]{1,0:T(8,128)(2,1)}, bf16[144,128]{1,0:T(8,128)(2,1)S(1)}, u32[]{:S(2)}, u32[]{:S(2)}) collective-permute-start(bf16[144,128]{1,0:T(8,128)(2,1)} %get-tuple-element.69), channel_id=1, source_target_pairs={{0,7},{1,6},{2,5},{3,4},{4,3},{5,2},{6,1},{7,0},{8,15},{9,14},{10,... | collective-permute-start | bytes 110600 | tf_op jit(solution)/shard_map/ppermute | solution.py:455
  141.1 10.1 %collective-permute-start.7 = (bf16[144,128]{1,0:T(8,128)(2,1)}, bf16[144,128]{1,0:T(8,128)(2,1)S(1)}, u32[]{:S(2)}, u32[]{:S(2)}) collective-permute-start(bf16[144,128]{1,0:T(8,128)(2,1)} %get-tuple-element.63), channel_id=1, source_target_pairs={{0,1},{1,0},{2,3},{3,2},{4,5},{5,4},{6,7},{7,6},{8,9},{9,8},{10,11... | collective-permute-start | bytes 110600 | tf_op jit(solution)/shard_map/ppermute | solution.py:455
  145.1 8.8 %collective-permute-start.8 = (bf16[144,128]{1,0:T(8,128)(2,1)}, bf16[144,128]{1,0:T(8,128)(2,1)S(1)}, u32[]{:S(2)}, u32[]{:S(2)}) collective-permute-start(bf16[144,128]{1,0:T(8,128)(2,1)} %get-tuple-element.64), channel_id=1, source_target_pairs={{0,2},{1,3},{2,0},{3,1},{4,6},{5,7},{6,4},{7,5},{8,10},{9,11},{10,... | collective-permute-start | bytes 110600 | tf_op jit(solution)/shard_map/ppermute | solution.py:455
  151.1 3.6 %collective-permute-start.9 = (bf16[144,128]{1,0:T(8,128)(2,1)}, bf16[144,128]{1,0:T(8,128)(2,1)S(1)}, u32[]{:S(2)}, u32[]{:S(2)}) collective-permute-start(bf16[144,128]{1,0:T(8,128)(2,1)} %get-tuple-element.65), channel_id=1, source_target_pairs={{0,3},{1,2},{2,1},{3,0},{4,7},{5,6},{6,5},{7,4},{8,11},{9,10},{10,... | collective-permute-start | bytes 110600 | tf_op jit(solution)/shard_map/ppermute | solution.py:455
  154.7 0.8 copy-start.1
  155.5 7.3 %collective-permute-start.14 = (bf16[336,128]{1,0:T(8,128)(2,1)S(1)}, bf16[336,128]{1,0:T(8,128)(2,1)S(1)}, u32[]{:S(2)}, u32[]{:S(2)}) collective-permute-start(bf16[336,128]{1,0:T(8,128)(2,1)S(1)} %shard_map.116.refs_0_), channel_id=1, source_target_pairs={{0,8},{8,16},{16,24},{24,0},{1,9},{9,17},{17,25},{25,1},{2,10},{10... | collective-permute-start | bytes 258056 | tf_op jit(solution)/shard_map/ppermute | solution.py:460
  156.8 10.7 %collective-permute-start.15 = (bf16[336,128]{1,0:T(8,128)(2,1)S(1)}, bf16[336,128]{1,0:T(8,128)(2,1)S(1)}, u32[]{:S(2)}, u32[]{:S(2)}) collective-permute-start(bf16[336,128]{1,0:T(8,128)(2,1)S(1)} %shard_map.116.refs_0_), channel_id=1, source_target_pairs={{0,16},{8,24},{16,0},{24,8},{1,17},{9,25},{17,1},{25,9},{2,18},{10... | collective-permute-start | bytes 258056 | tf_op jit(solution)/shard_map/ppermute | solution.py:460
  159.8 7.6 %collective-permute-start.16 = (bf16[336,128]{1,0:T(8,128)(2,1)S(1)}, bf16[336,128]{1,0:T(8,128)(2,1)S(1)}, u32[]{:S(2)}, u32[]{:S(2)}) collective-permute-start(bf16[336,128]{1,0:T(8,128)(2,1)S(1)} %shard_map.116.refs_0_), channel_id=1, source_target_pairs={{0,24},{8,0},{16,8},{24,16},{1,25},{9,1},{17,9},{25,17},{2,26},{10... | collective-permute-start | bytes 258056 | tf_op jit(solution)/shard_map/ppermute | solution.py:460
  167.5 11.9 %copy-start.2 = (s32[2]{0:T(128)S(1)}, s32[2]{0:T(128)}, u32[]{:S(2)}) copy-start(s32[2]{0:T(128)} %pad_add_fusion.here_ref) | copy-start | bytes 28
  167.5 3.6 %collective-permute-start.17 = (bf16[336,128]{1,0:T(8,128)(2,1)S(1)}, bf16[336,128]{1,0:T(8,128)(2,1)S(1)}, u32[]{:S(2)}, u32[]{:S(2)}) collective-permute-start(bf16[336,128]{1,0:T(8,128)(2,1)S(1)} %shard_map.117.refs_1_), channel_id=1, source_target_pairs={{0,1},{1,0},{2,3},{3,2},{4,5},{5,4},{6,7},{7,6},{8,9},{9,8},{10,11... | collective-permute-start | bytes 258056 | tf_op jit(solution)/shard_map/ppermute | solution.py:455
  167.6 5.9 %collective-permute-start.18 = (bf16[336,128]{1,0:T(8,128)(2,1)S(1)}, bf16[336,128]{1,0:T(8,128)(2,1)S(1)}, u32[]{:S(2)}, u32[]{:S(2)}) collective-permute-start(bf16[336,128]{1,0:T(8,128)(2,1)S(1)} %shard_map.117.refs_1_), channel_id=1, source_target_pairs={{0,2},{1,3},{2,0},{3,1},{4,6},{5,7},{6,4},{7,5},{8,10},{9,11},{10,... | collective-permute-start | bytes 258056 | tf_op jit(solution)/shard_map/ppermute | solution.py:455
  169.1 10.1 %collective-permute-start.19 = (bf16[336,128]{1,0:T(8,128)(2,1)S(1)}, bf16[336,128]{1,0:T(8,128)(2,1)S(1)}, u32[]{:S(2)}, u32[]{:S(2)}) collective-permute-start(bf16[336,128]{1,0:T(8,128)(2,1)S(1)} %shard_map.117.refs_1_), channel_id=1, source_target_pairs={{0,3},{1,2},{2,1},{3,0},{4,7},{5,6},{6,5},{7,4},{8,11},{9,10},{10,... | collective-permute-start | bytes 258056 | tf_op jit(solution)/shard_map/ppermute | solution.py:455
  169.5 9.7 %collective-permute-start.20 = (bf16[336,128]{1,0:T(8,128)(2,1)S(1)}, bf16[336,128]{1,0:T(8,128)(2,1)S(1)}, u32[]{:S(2)}, u32[]{:S(2)}) collective-permute-start(bf16[336,128]{1,0:T(8,128)(2,1)S(1)} %shard_map.117.refs_1_), channel_id=1, source_target_pairs={{0,4},{1,5},{2,6},{3,7},{4,0},{5,1},{6,2},{7,3},{8,12},{9,13},{10,... | collective-permute-start | bytes 258056 | tf_op jit(solution)/shard_map/ppermute | solution.py:455
  170.9 8.5 %collective-permute-start.21 = (bf16[336,128]{1,0:T(8,128)(2,1)S(1)}, bf16[336,128]{1,0:T(8,128)(2,1)S(1)}, u32[]{:S(2)}, u32[]{:S(2)}) collective-permute-start(bf16[336,128]{1,0:T(8,128)(2,1)S(1)} %shard_map.117.refs_1_), channel_id=1, source_target_pairs={{0,5},{1,4},{2,7},{3,6},{4,1},{5,0},{6,3},{7,2},{8,13},{9,12},{10,... | collective-permute-start | bytes 258056 | tf_op jit(solution)/shard_map/ppermute | solution.py:455
  171.2 8.2 %collective-permute-start.22 = (bf16[336,128]{1,0:T(8,128)(2,1)S(1)}, bf16[336,128]{1,0:T(8,128)(2,1)S(1)}, u32[]{:S(2)}, u32[]{:S(2)}) collective-permute-start(bf16[336,128]{1,0:T(8,128)(2,1)S(1)} %shard_map.117.refs_1_), channel_id=1, source_target_pairs={{0,6},{1,7},{2,4},{3,5},{4,2},{5,3},{6,0},{7,1},{8,14},{9,15},{10,... | collective-permute-start | bytes 258056 | tf_op jit(solution)/shard_map/ppermute | solution.py:455
  173.5 5.9 %collective-permute-start.23 = (bf16[336,128]{1,0:T(8,128)(2,1)S(1)}, bf16[336,128]{1,0:T(8,128)(2,1)S(1)}, u32[]{:S(2)}, u32[]{:S(2)}) collective-permute-start(bf16[336,128]{1,0:T(8,128)(2,1)S(1)} %shard_map.117.refs_1_), channel_id=1, source_target_pairs={{0,7},{1,6},{2,5},{3,4},{4,3},{5,2},{6,1},{7,0},{8,15},{9,14},{10,... | collective-permute-start | bytes 258056 | tf_op jit(solution)/shard_map/ppermute | solution.py:455

commit v6 on v5

--- a/solution.py
+++ b/solution.py
@@ -15,6 +15,7 @@
 BF16 = jnp.bfloat16
 F32 = jnp.float32
 BIG_VMEM = 60 * 1024 * 1024
+MID_VMEM = 24 * 1024 * 1024
 SMALL_VMEM = 16 * 1024 * 1024
 
 
@@ -70,7 +71,7 @@
 
 def spatial_fwd_kernel(
     rows_step, x_hbm, w_ref, cot_hbm, send_hbm, slope_hbm,
-    x_in, xs, acts, slopes, in_sems, cot_sem, act_sems, out_sems,
+    x_in, xs, sends, slopes, in_sems, cot_sems, send_sems, out_sems,
 ):
     rows, cols, ch = x_in.shape
     wide = xs.shape[1]
@@ -84,15 +85,18 @@
     ]
     stores = [
         (
-            pltpu.make_async_copy(acts.at[part(n)], send_hbm.at[part(n), 0], act_sems.at[n]),
+            pltpu.make_async_copy(sends.at[part(n)], send_hbm.at[part(n)], send_sems.at[n]),
             pltpu.make_async_copy(slopes.at[part(n)], slope_hbm.at[part(n)], out_sems.at[n]),
         )
         for n in range(steps)
     ]
-    for load in loads:
-        load.start()
-    cot_copy = pltpu.make_async_copy(cot_hbm, send_hbm.at[:, 1], cot_sem.at[0])
-    cot_copy.start()
+    cot_loads = [
+        pltpu.make_async_copy(cot_hbm.at[part(n)], sends.at[part(n), 1], cot_sems.at[n])
+        for n in range(steps)
+    ]
+    for n in range(steps):
+        loads[n].start()
+        cot_loads[n].start()
     xs[0] = jnp.zeros((wide, ch), BF16)
     xs[rows + 1] = jnp.zeros((wide, ch), BF16)
     weight = jnp.concatenate(
@@ -117,11 +121,11 @@
         y = mm(left, weight)
         pre = y[:, ch : 2 * ch] + roll_rows(y[:, :ch], 1) + roll_rows(y[:, 2 * ch :], -1)
         act, slope = silu_parts(pre)
-        acts[at : at + rows_step] = act.astype(BF16).reshape(rows_step, wide, ch)[:, :cols]
-        slopes[at : at + rows_step] = slope.reshape(rows_step, wide, ch)
+        sends[at : at + rows_step, 0] = act.astype(BF16).reshape(rows_step, wide, ch)[:, :cols]
+        slopes[at : at + rows_step] = slope.astype(BF16).reshape(rows_step, wide, ch)
+        cot_loads[step].wait()
         for store in stores[step]:
             store.start()
-    cot_copy.wait()
     for pair in stores:
         for store in pair:
             store.wait()
@@ -132,15 +136,16 @@
         piece[...] = total_ref[jnp.bitwise_xor(here_ref[1], peer)].astype(piece.dtype)
 
 
-def columns_kernel(rows_step, x_ref, cat_ref):
+def columns_kernel(rows_step, x_ref, slope_ref, cat_ref, near_ref):
     rows, cols, ch = x_ref.shape
-    wide = cat_ref.shape[0] // rows
+    wide = cat_ref.shape[1] // rows
     flat = rows_step * wide
     pad = jnp.zeros((rows_step, wide - cols, ch), F32)
     for at in range(0, rows, rows_step):
         x = jnp.concatenate([x_ref[at : at + rows_step].astype(F32), pad], axis=1).reshape(flat, ch)
         x_cat = jnp.concatenate([roll_rows(x, 1), x, roll_rows(x, -1)], axis=1)
-        cat_ref[at * wide : at * wide + flat] = x_cat.astype(BF16)
+        cat_ref[:, at * wide : at * wide + flat] = x_cat.T.astype(BF16)
+    near_ref[...] = slope_ref[...]
 
 
 def taps_up(gs, at, rows_step):
@@ -152,55 +157,23 @@
 
 
 def spatial_wgrad_kernel(
-    rows_step, scale, here_ref, got_hbm, slope_hbm, cat_hbm, gs_hbm, *rest
+    rows_step, scale, here_ref, got_ref, slope_ref, cat_ref, gs, *rest
 ):
-    pieces = rest[:-9]
-    got, slopes, gs, cat_ref, total_ref, got_sems, slope_sems, cat_sems, gs_sems = rest[-9:]
-    rows, cols, ch = got.shape
+    pieces, total_ref = rest[:-1], rest[-1]
+    rows, cols, ch = got_ref.shape
     wide = gs.shape[1]
-    steps = rows // rows_step
     flat = rows_step * wide
-
-    def part(step, first=0):
-        return pl.ds(first + step * rows_step, rows_step)
-
-    loads = [
-        (
-            pltpu.make_async_copy(got_hbm.at[part(n)], got.at[part(n)], got_sems.at[n]),
-            pltpu.make_async_copy(slope_hbm.at[part(n)], slopes.at[part(n)], slope_sems.at[n]),
-            pltpu.make_async_copy(
-                cat_hbm.at[pl.ds(n * flat, flat)], cat_ref.at[pl.ds(n * flat, flat)], cat_sems.at[n]
-            ),
-        )
-        for n in range(steps)
-    ]
-    for pair in loads:
-        for load in pair:
-            load.start()
-    stores = [
-        pltpu.make_async_copy(gs.at[part(n, 1)], gs_hbm.at[part(n)], gs_sems.at[n])
-        for n in range(steps)
-    ]
     gs[0] = jnp.zeros((wide, ch), BF16)
     gs[rows + 1] = jnp.zeros((wide, ch), BF16)
-
-    def bring(step):
-        for load in loads[step]:
-            load.wait()
-        at = step * rows_step
+    for at in range(0, rows, rows_step):
         gs[1 + at : 1 + at + rows_step] = jnp.zeros((rows_step, wide, ch), BF16)
         gs[1 + at : 1 + at + rows_step, :cols, :] = (
-            got[at : at + rows_step].astype(F32) * slopes[at : at + rows_step, :cols, :]
+            got_ref[at : at + rows_step].astype(F32)
+            * slope_ref[at : at + rows_step, :cols, :].astype(F32)
         ).astype(BF16)
-        stores[step].start()
-
     total = jnp.zeros((3 * ch, 3 * ch), F32)
-    bring(0)
-    for step in range(steps):
-        if step + 1 < steps:
-            bring(step + 1)
-        at = step * rows_step
-        total = total + mm_tn(cat_ref[at * wide : at * wide + flat], taps_up(gs, at, rows_step))
+    for at in range(0, rows, rows_step):
+        total = total + mm(cat_ref[:, at * wide : at * wide + flat], taps_up(gs, at, rows_step))
     total_ref[...] = (
         jnp.concatenate(
             [
@@ -213,23 +186,11 @@
         * scale
     ).reshape(total_ref.shape)
     hand_out(here_ref, total_ref, pieces)
-    for store in stores:
-        store.wait()
-
-
-def spatial_back_kernel(rows_step, w_ref, gs_hbm, back_hbm, gs, back_ref, sem, out_sems):
+
+
+def spatial_back_kernel(rows_step, w_ref, gs, back_ref):
     rows, cols, ch = back_ref.shape
-    stores = [
-        pltpu.make_async_copy(
-            back_ref.at[pl.ds(at, rows_step)], back_hbm.at[pl.ds(at, rows_step)], out_sems.at[n]
-        )
-        for n, at in enumerate(range(0, rows, rows_step))
-    ]
     wide = gs.shape[1]
-    load = pltpu.make_async_copy(gs_hbm, gs.at[pl.ds(1, rows)], sem.at[0])
-    load.start()
-    gs[0] = jnp.zeros((wide, ch), BF16)
-    gs[rows + 1] = jnp.zeros((wide, ch), BF16)
     weight = jnp.concatenate(
         [
             jnp.concatenate([w_ref[3 * a + b].astype(F32).T.astype(BF16) for b in range(3)], axis=1)
@@ -237,14 +198,10 @@
         ],
         axis=0,
     )
-    load.wait()
-    for n, at in enumerate(range(0, rows, rows_step)):
+    for at in range(0, rows, rows_step):
         y = mm(taps_up(gs, at, rows_step), weight)
         back = y[:, ch : 2 * ch] + roll_rows(y[:, :ch], -1) + roll_rows(y[:, 2 * ch :], 1)
         back_ref[at : at + rows_step] = back.astype(BF16).reshape(rows_step, wide, ch)[:, :cols]
-        stores[n].start()
-    for store in stores:
-        store.wait()
 
 
 def clear_halo(pad_ref, frames):
@@ -498,14 +455,14 @@
 
     send, space_slope = call(
         functools.partial(spatial_fwd_kernel, rows_step),
-        [((rows, 2, cols, ch), BF16, HBM), ((rows, wide, ch), F32, HBM)],
+        [((rows, 2, cols, ch), BF16, HBM), ((rows, wide, ch), BF16, HBM)],
         [
             pltpu.VMEM((rows, cols, ch), BF16),
             pltpu.VMEM((rows + 2, wide, ch), BF16),
-            pltpu.VMEM((rows, cols, ch), BF16),
-            pltpu.VMEM((rows, wide, ch), F32),
+            pltpu.VMEM((rows, 2, cols, ch), BF16),
+            pltpu.VMEM((rows, wide, ch), BF16),
             pltpu.SemaphoreType.DMA((steps,)),
-            pltpu.SemaphoreType.DMA((1,)),
+            pltpu.SemaphoreType.DMA((steps,)),
             pltpu.SemaphoreType.DMA((steps,)),
             pltpu.SemaphoreType.DMA((steps,)),
         ],
@@ -569,44 +526,36 @@
     )
     time_sum = reduce_in_grp(time_pieces)
     time_sum, grad_time = lax.optimization_barrier((time_sum, grad_time))
-    (x_cat,) = call(
+    x_cat, space_slope = call(
         functools.partial(columns_kernel, rows_step),
-        [((rows * wide, 3 * ch), BF16, VMEM)],
+        [((3 * ch, rows * wide), BF16, VMEM), ((rows, wide, ch), BF16, VMEM)],
         [],
         0,
-        pixels * ch * 8,
-        [(frames_in[0], VMEM)],
+        pixels * ch * 12,
+        [(frames_in[0], VMEM), (space_slope, VMEM)],
+        MID_VMEM,
     )
     gs, *space_pieces = call(
         functools.partial(spatial_wgrad_kernel, rows_step, scale),
-        [((rows, wide, ch), BF16, HBM)] + [((space_rows, ch), BF16, VMEM)] * peers,
-        [
-            pltpu.VMEM((rows, cols, ch), BF16),
-            pltpu.VMEM((rows, wide, ch), F32),
-            pltpu.VMEM((rows + 2, wide, ch), BF16),
-            pltpu.VMEM((rows * wide, 3 * ch), BF16),
-            pltpu.VMEM((peers, space_rows, ch), F32),
-        ]
-        + [pltpu.SemaphoreType.DMA((steps,))] * 4,
+        [((rows + 2, wide, ch), BF16, VMEM)] + [((space_rows, ch), BF16, VMEM)] * peers,
+        [pltpu.VMEM((peers, space_rows, ch), F32)],
         2 * 9 * pixels * ch * ch,
         pixels * ch * 18,
-        [(here, SMEM), (grad_time, HBM), (space_slope, HBM), (x_cat, HBM)],
+        [(here, SMEM), (grad_time, VMEM), (space_slope, VMEM), (x_cat, VMEM)],
+        MID_VMEM,
     )
     united_send, space_pieces[0] = lax.optimization_barrier((united_send, space_pieces[0]))
     united = exchange(united_send)
     (back,) = call(
         functools.partial(spatial_back_kernel, rows_step),
-        [((rows, cols, ch), BF16, HBM)],
-        [
-            pltpu.VMEM((rows + 2, wide, ch), BF16),
-            pltpu.VMEM((rows, cols, ch), BF16),
-            pltpu.SemaphoreType.DMA((1,)),
-            pltpu.SemaphoreType.DMA((steps,)),
-        ],
+        [((rows, cols, ch), BF16, VMEM)],
+        [],
         2 * 9 * pixels * ch * ch,
         pixels * ch * 4,
-        [(spatial_weight, VMEM), (gs, HBM)],
-    )
+        [(spatial_weight, VMEM), (gs, VMEM)],
+        MID_VMEM,
+    )
+    space_pieces[0], back = lax.optimization_barrier((space_pieces[0], back))
     space_parts = [flip(part, peer) if peer else part for peer, part in enumerate(space_pieces)]
     (plane,) = call(
         join_kernel,

time: 183 us -> 156 us (0.85)
  Pallas kernels: 70 us -> 37.2 us
  local copies, waits for them, and re-layouts: 1.72 us -> 5.77 us
    pallas_call x10, Pallas kernels: 70 us -> 37.2 us  [call(): pl.pallas_call(kernel, out_shape=[jax.ShapeDtypeStruct(shape, kind) for s...]
    unnamed x8 -> x18, local copies, waits for them, and re-layouts: 1.72 us -> 5.77 us
  transfers between devices with their start and end apart: 26 -> 26, of which waited for: 8 -> 8; matrix products, arithmetic and copies ran while one was open for 0% -> 0% of each run, Pallas kernels for 10% -> 9%
where the time goes in v6:
time: 156 us; the launch traced here: 155 us
  blocking collectives  53.3 us (34%)
  Pallas kernels  37.2 us (24%)
  starting transfers between devices  36.7 us (24%)
  waiting for transfers between devices  21 us (13%)
  local copies, waits for them, and re-layouts  5.77 us (4%)
    all_to_all x1, blocking collectives, exchange(): return lax.all_to_all(blocks, AXES, split_axis=0, concat_axis=0, tiled=True)  53.3 us
    pallas_call x10, Pallas kernels, call(): pl.pallas_call(kernel, out_shape=[jax.ShapeDtypeStruct(shape, kind) for s...  37.2 us
    ppermute x21, starting transfers between devices, flip(): return lax.ppermute(value, 'grp', [(i, i ^ peer) for i in range(size)])  24.2 us
    ppermute x21, waiting for transfers between devices, flip(): return lax.ppermute(value, 'grp', [(i, i ^ peer) for i in range(size)])  9.73 us
    ppermute x3, waiting for transfers between devices, turn_by(): lax.ppermute(value, 'seg', [(i, (i + turn) % size) for i in range(size)])  7.81 us
    all_to_all x2, starting transfers between devices, exchange(): return lax.all_to_all(blocks, AXES, split_axis=0, concat_axis=0, tiled=True)  7.43 us
    unnamed x18, local copies, waits for them, and re-layouts  5.77 us
    ppermute x3, starting transfers between devices, turn_by(): lax.ppermute(value, 'seg', [(i, (i + turn) % size) for i in range(size)])  5.11 us
  transfers between devices with their start and end apart: 26, of which 8 were waited for; matrix products, arithmetic and copies ran while one was open for 0% of the time, Pallas kernels for 9%

profile of v6, /device:TPU:0, one launch (start us, length us, event | category | flops | bytes accessed | tf_op | source)
XLA Modules:
  0.0 155.5 jit_solution(3550256425038585533)
XLA Ops:
  0.6 6.7 %shard_map.110 = (bf16[32,2,120,128]{3,2,1,0:T(8,128)(2,1)}, bf16[32,128,128]{2,1,0:T(8,128)(2,1)}) custom-call(bf16[32,120,128]{2,1,0:T(8,128)(2,1)} %bitcast.9, bf16[9,128,128]{2,1,0:T(8,128)(2,1)} %w_ref.3, bf16[32,120,128]{2,1,0:T(8,128)(2,1)} %bitcast.11), custom_call_target="tpu_custom_call" | custom-call | flops 1132462080 | bytes 5898240 | tf_op jit(solution)/shard_map/pallas_call | solution.py:57
  7.4 53.3 %all_to_all.15.got_hbm = bf16[32,2,120,128]{3,2,1,0:T(8,128)(2,1)} all-to-all(bf16[32,2,120,128]{3,2,1,0:T(8,128)(2,1)} %get-tuple-element.44), channel_id=1, replica_groups=mesh['seg'=4,'grp'=8] {'seg','grp'}, dimensions={0} | all-to-all | bytes 3932160 | tf_op jit(solution)/shard_map/all_to_all | solution.py:407
  60.7 11.6 %shard_map.111 = (bf16[32,120,128]{2,1,0:T(8,128)(2,1)}, bf16[32,120,128]{2,1,0:T(8,128)(2,1)}, bf16[32,128,128]{2,1,0:T(8,128)(2,1)}, bf16[32,128,128]{2,1,0:T(...) custom-call(s32[2]{0:T(128)} %dil_ref.3, ...), custom_call_target="tpu_custom_call" | custom-call | flops 2768240640 | bytes 8847360 | tf_op jit(solution)/shard_map/pallas_call | solution.py:57
  72.3 3.8 %all-to-all-start.1 = ((bf16[32,120,128]{2,1,0:T(8,128)(2,1)}), bf16[32,120,128]{2,1,0:T(8,128)(2,1)S(1)}, u32[]{:S(2)}, u32[]{:S(2)}) async-start(bf16[32,120,128]{2,1,0:T(8,128)(2,1)} %get-tuple-element.60), calls=%async_computation.1 | async-start | bytes 1966080 | tf_op jit(solution)/shard_map/all_to_all | solution.py:407
  76.1 0.6 pad_add_fusion.here_ref
  76.6 9.4 %shard_map.112 = (bf16[192,128]{1,0:T(8,128)(2,1)}, bf16[192,128]{1,0:T(8,128)(2,1)}, bf16[192,128]{1,0:T(8,128)(2,1)}, bf16[192,128]{1,0:T(8,128)(2,1)}, bf16[1...) custom-call(s32[2]{0:T(128)} %pad_add_fusion.here_ref, ...), custom_call_target="tpu_custom_call" | custom-call | flops 1509949440 | bytes 6881280 | tf_op jit(solution)/shard_map/pallas_call | solution.py:57
  86.1 0.1 collective-permute-start
  86.2 1.7 %collective-permute-start.1 = (bf16[192,128]{1,0:T(8,128)(2,1)}, bf16[192,128]{1,0:T(8,128)(2,1)S(1)}, u32[]{:S(2)}, u32[]{:S(2)}) collective-permute-start(bf16[192,128]{1,0:T(8,128)(2,1)} %get-tuple-element.54), channel_id=1, source_target_pairs={{0,2},{1,3},{2,0},{3,1},{4,6},{5,7},{6,4},{7,5},{8,10},{9,11},{10,... | collective-permute-start | bytes 147464 | tf_op jit(solution)/shard_map/ppermute | solution.py:412
  87.9 0.1 collective-permute-start.2
  88.0 1.6 %collective-permute-start.3 = (bf16[192,128]{1,0:T(8,128)(2,1)}, bf16[192,128]{1,0:T(8,128)(2,1)S(1)}, u32[]{:S(2)}, u32[]{:S(2)}) collective-permute-start(bf16[192,128]{1,0:T(8,128)(2,1)} %get-tuple-element.56), channel_id=1, source_target_pairs={{0,4},{1,5},{2,6},{3,7},{4,0},{5,1},{6,2},{7,3},{8,12},{9,13},{10,... | collective-permute-start | bytes 147464 | tf_op jit(solution)/shard_map/ppermute | solution.py:412
  89.6 0.1 collective-permute-start.4
  89.7 2.6 %collective-permute-start.5 = (bf16[192,128]{1,0:T(8,128)(2,1)}, bf16[192,128]{1,0:T(8,128)(2,1)S(1)}, u32[]{:S(2)}, u32[]{:S(2)}) collective-permute-start(bf16[192,128]{1,0:T(8,128)(2,1)} %get-tuple-element.58), channel_id=1, source_target_pairs={{0,6},{1,7},{2,4},{3,5},{4,2},{5,3},{6,0},{7,1},{8,14},{9,15},{10,... | collective-permute-start | bytes 147464 | tf_op jit(solution)/shard_map/ppermute | solution.py:412
  92.3 0.3 collective-permute-start.6
  92.7 1.2 copy-done.3
  93.9 1.0 shard_map.114
  94.9 1.6 %copy-done = bf16[384,4096]{1,0:T(8,128)(2,1)} copy-done((bf16[384,4096]{1,0:T(8,128)(2,1)}, bf16[384,4096]{1,0:T(8,128)(2,1)S(1)}, u32[]{:S(2)}) %copy-start) | copy-done | bytes 3145752
  96.5 0.7 collective-permute-done.6.refs_7_
  97.3 0.1 shard_map.113.first_ref
  97.3 3.4 %all-to-all-done.1.got_ref = bf16[32,120,128]{2,1,0:T(8,128)(2,1)S(1)} async-done(((bf16[32,120,128]{2,1,0:T(8,128)(2,1)}), bf16[32,120,128]{2,1,0:T(8,128)(2,1)S(1)}, u32[]{:S(2)}, u32[]{:S(2)}) %all-to-all-start.1) | async-done | bytes 983072 | tf_op jit(solution)/shard_map/all_to_all | solution.py:407
  100.7 1.9 %copy-done.1 = bf16[384,4096]{1,0:T(8,128)(2,1)S(1)} copy-done((bf16[384,4096]{1,0:T(8,128)(2,1)S(1)}, bf16[384,4096]{1,0:T(8,128)(2,1)}, u32[]{:S(2)}) %copy-start.1) | copy-done | bytes 3145752
  102.6 2.6 %shard_map.115 = (bf16[34,128,128]{2,1,0:T(8,128)(2,1)S(1)}, bf16[144,128]{1,0:T(8,128)(2,1)S(1)}, bf16[144,128]{1,0:T(8,128)(2,1)S(1)}, bf16[144,128]{1,0:T(8,1...) custom-call(s32[2]{0:T(128)S(1)} %copy-done.5, ...), custom_call_target="tpu_custom_call" | custom-call | flops 1132462080 | bytes 8847360 | tf_op jit(solution)/shard_map/pallas_call | solution.py:57
  105.3 1.0 copy-done.6
  106.3 3.6 %all-to-all-start.2 = ((bf16[32,120,128]{2,1,0:T(8,128)(2,1)}), bf16[32,120,128]{2,1,0:T(8,128)(2,1)S(1)}, u32[]{:S(2)}, u32[]{:S(2)}) async-start(bf16[32,120,128]{2,1,0:T(8,128)(2,1)} %get-tuple-element.66), calls=%async_computation.2 | async-start | bytes 1966080 | tf_op jit(solution)/shard_map/all_to_all | solution.py:407
  109.9 1.8 %collective-permute-start.10 = (bf16[144,128]{1,0:T(8,128)(2,1)S(1)}, bf16[144,128]{1,0:T(8,128)(2,1)S(1)}, u32[]{:S(2)}, u32[]{:S(2)}) collective-permute-start(bf16[144,128]{1,0:T(8,128)(2,1)S(1)} %get-tuple-element.74), channel_id=1, source_target_pairs={{0,4},{1,5},{2,6},{3,7},{4,0},{5,1},{6,2},{7,3},{8,12},{9,13},{10,... | collective-permute-start | bytes 110600 | tf_op jit(solution)/shard_map/ppermute | solution.py:412
  111.8 2.4 %collective-permute-start.12 = (bf16[144,128]{1,0:T(8,128)(2,1)S(1)}, bf16[144,128]{1,0:T(8,128)(2,1)S(1)}, u32[]{:S(2)}, u32[]{:S(2)}) collective-permute-start(bf16[144,128]{1,0:T(8,128)(2,1)S(1)} %get-tuple-element.76), channel_id=1, source_target_pairs={{0,6},{1,7},{2,4},{3,5},{4,2},{5,3},{6,0},{7,1},{8,14},{9,15},{10,... | collective-permute-start | bytes 110600 | tf_op jit(solution)/shard_map/ppermute | solution.py:412
  114.2 0.3 collective-permute-start.13
  114.5 0.4 collective-permute-start.7
  114.8 3.6 %collective-permute-done.10.refs_4_ = bf16[144,128]{1,0:T(8,128)(2,1)S(1)} collective-permute-done((bf16[144,128]{1,0:T(8,128)(2,1)S(1)}, bf16[144,128]{1,0:T(8,128)(2,1)S(1)}, u32[]{:S(2)}, u32[]{:S(2)}) %collective-permute-start.10) | collective-permute-done | bytes 36896 | tf_op jit(solution)/shard_map/ppermute | solution.py:412
  118.4 6.0 %collective-permute-start.8 = (bf16[144,128]{1,0:T(8,128)(2,1)S(1)}, bf16[144,128]{1,0:T(8,128)(2,1)S(1)}, u32[]{:S(2)}, u32[]{:S(2)}) collective-permute-start(bf16[144,128]{1,0:T(8,128)(2,1)S(1)} %get-tuple-element.72), channel_id=1, source_target_pairs={{0,2},{1,3},{2,0},{3,1},{4,6},{5,7},{6,4},{7,5},{8,10},{9,11},{10,... | collective-permute-start | bytes 110600 | tf_op jit(solution)/shard_map/ppermute | solution.py:412
  124.4 0.1 collective-permute-start.9
  124.5 3.1 %shard_map.116 = bf16[32,120,128]{2,1,0:T(8,128)(2,1)} custom-call(bf16[9,128,128]{2,1,0:T(8,128)(2,1)S(1)} %copy-done.8, bf16[34,128,128]{2,1,0:T(8,128)(2,1)S(1)} %copy-done.7), custom_call_target="tpu_custom_call" | custom-call | flops 1132462080 | bytes 1966080 | tf_op jit(solution)/shard_map/pallas_call | solution.py:57
  127.7 0.1 collective-permute-done.9.refs_3_
  127.8 0.1 shard_map.117.refs_0_
  127.9 1.4 collective-permute-start.14
  129.2 3.0 %collective-permute-start.15 = (bf16[336,128]{1,0:T(8,128)(2,1)S(1)}, bf16[336,128]{1,0:T(8,128)(2,1)S(1)}, u32[]{:S(2)}, u32[]{:S(2)}) collective-permute-start(bf16[336,128]{1,0:T(8,128)(2,1)S(1)} %shard_map.117.refs_0_), channel_id=1, source_target_pairs={{0,16},{8,24},{16,0},{24,8},{1,17},{9,25},{17,1},{25,9},{2,18},{10... | collective-permute-start | bytes 258056 | tf_op jit(solution)/shard_map/ppermute | solution.py:417
  132.2 0.8 collective-permute-start.16
  133.0 2.2 %collective-permute-done.14.refs_1_ = bf16[336,128]{1,0:T(8,128)(2,1)S(1)} collective-permute-done((bf16[336,128]{1,0:T(8,128)(2,1)S(1)}, bf16[336,128]{1,0:T(8,128)(2,1)S(1)}, u32[]{:S(2)}, u32[]{:S(2)}) %collective-permute-start.14) | collective-permute-done | bytes 86048 | tf_op jit(solution)/shard_map/ppermute | solution.py:417
  135.1 5.6 %collective-permute-done.15.refs_2_ = bf16[336,128]{1,0:T(8,128)(2,1)S(1)} collective-permute-done((bf16[336,128]{1,0:T(8,128)(2,1)S(1)}, bf16[336,128]{1,0:T(8,128)(2,1)S(1)}, u32[]{:S(2)}, u32[]{:S(2)}) %collective-permute-start.15) | collective-permute-done | bytes 86048 | tf_op jit(solution)/shard_map/ppermute | solution.py:417
  140.8 0.1 collective-permute-start.17
  140.9 1.5 collective-permute-start.18
  142.4 0.3 collective-permute-start.19
  142.8 1.5 collective-permute-start.20
  144.2 0.2 collective-permute-start.21
  144.5 2.4 %collective-permute-start.22 = (bf16[336,128]{1,0:T(8,128)(2,1)S(1)}, bf16[336,128]{1,0:T(8,128)(2,1)S(1)}, u32[]{:S(2)}, u32[]{:S(2)}) collective-permute-start(bf16[336,128]{1,0:T(8,128)(2,1)S(1)} %shard_map.118.refs_1_), channel_id=1, source_target_pairs={{0,6},{1,7},{2,4},{3,5},{4,2},{5,3},{6,0},{7,1},{8,14},{9,15},{10,... | collective-permute-start | bytes 258056 | tf_op jit(solution)/shard_map/ppermute | solution.py:412
  146.9 0.6 collective-permute-start.23
  147.5 0.4 collective-permute-done.20.refs_5_
  147.9 4.9 %collective-permute-done.21.refs_6_ = bf16[336,128]{1,0:T(8,128)(2,1)S(1)} collective-permute-done((bf16[336,128]{1,0:T(8,128)(2,1)S(1)}, bf16[336,128]{1,0:T(8,128)(2,1)S(1)}, u32[]{:S(2)}, u32[]{:S(2)}) %collective-permute-start.21) | collective-permute-done | bytes 86048 | tf_op jit(solution)/shard_map/ppermute | solution.py:412
  152.8 2.6 %shard_map.119 = (f32[8,160,128]{2,1,0:T(8,128)}, f32[8,32,128]{2,1,0:T(8,128)}, f32[8,144,128]{2,1,0:T(8,128)}, bf16[32,120,128]{2,1,0:T(8,128)(2,1)}) custom-call(s32[2]{0:T(128)S(1)} %copy-done.5, bf16[32,120,128]{2,1,0:T(8,128)(2,1)S(1)} %all-to-all-done.2.refs_0_, bf16[336,128]{1,0:T(8,128)(2,1)S(1)} %shard_map.118.refs_1_, ...), custom_call_target="tpu_custom_call" | custom-call | bytes 2064384 | tf_op jit(solution)/shard_map/pallas_call | solution.py:57
  (34 shorter events, 0.1 us)
Async XLA Ops:
  72.3 28.5 %all-to-all-start.1 = ((bf16[32,120,128]{2,1,0:T(8,128)(2,1)}), bf16[32,120,128]{2,1,0:T(8,128)(2,1)S(1)}, u32[]{:S(2)}, u32[]{:S(2)}) async-start(bf16[32,120,128]{2,1,0:T(8,128)(2,1)} %get-tuple-element.60), calls=%async_computation.1 | async-start | bytes 1966080 | tf_op jit(solution)/shard_map/all_to_all | solution.py:407
  76.6 16.0 %copy-start.2 = (bf16[32,128,128]{2,1,0:T(8,128)(2,1)S(1)}, bf16[32,128,128]{2,1,0:T(8,128)(2,1)}, u32[]{:S(2)}) copy-start(bf16[32,128,128]{2,1,0:T(8,128)(2,1)} %get-tuple-element.62.slope_ref) | copy-start | bytes 3145732
  86.1 14.6 %copy-start.5 = (s32[2]{0:T(128)S(1)}, s32[2]{0:T(128)}, u32[]{:S(2)}) copy-start(s32[2]{0:T(128)} %pad_add_fusion.here_ref) | copy-start | bytes 28
  86.1 3.6 %collective-permute-start = (bf16[192,128]{1,0:T(8,128)(2,1)}, bf16[192,128]{1,0:T(8,128)(2,1)S(1)}, u32[]{:S(2)}, u32[]{:S(2)}) collective-permute-start(bf16[192,128]{1,0:T(8,128)(2,1)} %get-tuple-element.53), channel_id=1, source_target_pairs={{0,1},{1,0},{2,3},{3,2},{4,5},{5,4},{6,7},{7,6},{8,9},{9,8},{10,11... | collective-permute-start | bytes 147464 | tf_op jit(solution)/shard_map/ppermute | solution.py:412
  86.2 6.1 %collective-permute-start.1 = (bf16[192,128]{1,0:T(8,128)(2,1)}, bf16[192,128]{1,0:T(8,128)(2,1)S(1)}, u32[]{:S(2)}, u32[]{:S(2)}) collective-permute-start(bf16[192,128]{1,0:T(8,128)(2,1)} %get-tuple-element.54), channel_id=1, source_target_pairs={{0,2},{1,3},{2,0},{3,1},{4,6},{5,7},{6,4},{7,5},{8,10},{9,11},{10,... | collective-permute-start | bytes 147464 | tf_op jit(solution)/shard_map/ppermute | solution.py:412
  87.9 8.6 %collective-permute-start.2 = (bf16[192,128]{1,0:T(8,128)(2,1)}, bf16[192,128]{1,0:T(8,128)(2,1)S(1)}, u32[]{:S(2)}, u32[]{:S(2)}) collective-permute-start(bf16[192,128]{1,0:T(8,128)(2,1)} %get-tuple-element.55), channel_id=1, source_target_pairs={{0,3},{1,2},{2,1},{3,0},{4,7},{5,6},{6,5},{7,4},{8,11},{9,10},{10,... | collective-permute-start | bytes 147464 | tf_op jit(solution)/shard_map/ppermute | solution.py:412
  88.0 8.5 %collective-permute-start.3 = (bf16[192,128]{1,0:T(8,128)(2,1)}, bf16[192,128]{1,0:T(8,128)(2,1)S(1)}, u32[]{:S(2)}, u32[]{:S(2)}) collective-permute-start(bf16[192,128]{1,0:T(8,128)(2,1)} %get-tuple-element.56), channel_id=1, source_target_pairs={{0,4},{1,5},{2,6},{3,7},{4,0},{5,1},{6,2},{7,3},{8,12},{9,13},{10,... | collective-permute-start | bytes 147464 | tf_op jit(solution)/shard_map/ppermute | solution.py:412
  89.6 6.9 %collective-permute-start.4 = (bf16[192,128]{1,0:T(8,128)(2,1)}, bf16[192,128]{1,0:T(8,128)(2,1)S(1)}, u32[]{:S(2)}, u32[]{:S(2)}) collective-permute-start(bf16[192,128]{1,0:T(8,128)(2,1)} %get-tuple-element.57), channel_id=1, source_target_pairs={{0,5},{1,4},{2,7},{3,6},{4,1},{5,0},{6,3},{7,2},{8,13},{9,12},{10,... | collective-permute-start | bytes 147464 | tf_op jit(solution)/shard_map/ppermute | solution.py:412
  89.7 6.8 %collective-permute-start.5 = (bf16[192,128]{1,0:T(8,128)(2,1)}, bf16[192,128]{1,0:T(8,128)(2,1)S(1)}, u32[]{:S(2)}, u32[]{:S(2)}) collective-permute-start(bf16[192,128]{1,0:T(8,128)(2,1)} %get-tuple-element.58), channel_id=1, source_target_pairs={{0,6},{1,7},{2,4},{3,5},{4,2},{5,3},{6,0},{7,1},{8,14},{9,15},{10,... | collective-permute-start | bytes 147464 | tf_op jit(solution)/shard_map/ppermute | solution.py:412
  92.3 4.9 %collective-permute-start.6 = (bf16[192,128]{1,0:T(8,128)(2,1)}, bf16[192,128]{1,0:T(8,128)(2,1)S(1)}, u32[]{:S(2)}, u32[]{:S(2)}) collective-permute-start(bf16[192,128]{1,0:T(8,128)(2,1)} %get-tuple-element.59), channel_id=1, source_target_pairs={{0,7},{1,6},{2,5},{3,4},{4,3},{5,2},{6,1},{7,0},{8,15},{9,14},{10,... | collective-permute-start | bytes 147464 | tf_op jit(solution)/shard_map/ppermute | solution.py:412
  92.7 1.2 copy-start.3
  93.9 3.4 %copy-start.4 = (bf16[192,128]{1,0:T(8,128)(2,1)S(1)}, bf16[192,128]{1,0:T(8,128)(2,1)}, u32[]{:S(2)}) copy-start(bf16[192,128]{1,0:T(8,128)(2,1)} %get-tuple-element.52.refs_0_) | copy-start | bytes 147460
  94.8 1.6 %copy-start = (bf16[384,4096]{1,0:T(8,128)(2,1)}, bf16[384,4096]{1,0:T(8,128)(2,1)S(1)}, u32[]{:S(2)}) copy-start(bf16[384,4096]{1,0:T(8,128)(2,1)S(1)} %get-tuple-element.64.cat_ref) | copy-start | bytes 9437188
  100.7 1.9 %copy-start.1 = (bf16[384,4096]{1,0:T(8,128)(2,1)S(1)}, bf16[384,4096]{1,0:T(8,128)(2,1)}, u32[]{:S(2)}) copy-start(bf16[384,4096]{1,0:T(8,128)(2,1)} %copy-done) | copy-start | bytes 9437188
  105.3 1.0 copy-start.6
  106.3 18.2 %copy-start.8 = (bf16[9,128,128]{2,1,0:T(8,128)(2,1)S(1)}, bf16[9,128,128]{2,1,0:T(8,128)(2,1)}, u32[]{:S(2)}) copy-start(bf16[9,128,128]{2,1,0:T(8,128)(2,1)} %w_ref.3) | copy-start | bytes 884740
  106.3 18.2 %copy-start.7 = (bf16[34,128,128]{2,1,0:T(8,128)(2,1)S(1)}, bf16[34,128,128]{2,1,0:T(8,128)(2,1)}, u32[]{:S(2)}) copy-start(bf16[34,128,128]{2,1,0:T(8,128)(2,1)} %copy-done.6) | copy-start | bytes 3342340
  106.3 46.4 %all-to-all-start.2 = ((bf16[32,120,128]{2,1,0:T(8,128)(2,1)}), bf16[32,120,128]{2,1,0:T(8,128)(2,1)S(1)}, u32[]{:S(2)}, u32[]{:S(2)}) async-start(bf16[32,120,128]{2,1,0:T(8,128)(2,1)} %get-tuple-element.66), calls=%async_computation.2 | async-start | bytes 1966080 | tf_op jit(solution)/shard_map/all_to_all | solution.py:407
  109.9 8.5 %collective-permute-start.10 = (bf16[144,128]{1,0:T(8,128)(2,1)S(1)}, bf16[144,128]{1,0:T(8,128)(2,1)S(1)}, u32[]{:S(2)}, u32[]{:S(2)}) collective-permute-start(bf16[144,128]{1,0:T(8,128)(2,1)S(1)} %get-tuple-element.74), channel_id=1, source_target_pairs={{0,4},{1,5},{2,6},{3,7},{4,0},{5,1},{6,2},{7,3},{8,12},{9,13},{10,... | collective-permute-start | bytes 110600 | tf_op jit(solution)/shard_map/ppermute | solution.py:412
  111.8 12.6 %collective-permute-start.11 = (bf16[144,128]{1,0:T(8,128)(2,1)S(1)}, bf16[144,128]{1,0:T(8,128)(2,1)S(1)}, u32[]{:S(2)}, u32[]{:S(2)}) collective-permute-start(bf16[144,128]{1,0:T(8,128)(2,1)S(1)} %get-tuple-element.75), channel_id=1, source_target_pairs={{0,5},{1,4},{2,7},{3,6},{4,1},{5,0},{6,3},{7,2},{8,13},{9,12},{10,... | collective-permute-start | bytes 110600 | tf_op jit(solution)/shard_map/ppermute | solution.py:412
  111.8 15.9 %collective-permute-start.12 = (bf16[144,128]{1,0:T(8,128)(2,1)S(1)}, bf16[144,128]{1,0:T(8,128)(2,1)S(1)}, u32[]{:S(2)}, u32[]{:S(2)}) collective-permute-start(bf16[144,128]{1,0:T(8,128)(2,1)S(1)} %get-tuple-element.76), channel_id=1, source_target_pairs={{0,6},{1,7},{2,4},{3,5},{4,2},{5,3},{6,0},{7,1},{8,14},{9,15},{10,... | collective-permute-start | bytes 110600 | tf_op jit(solution)/shard_map/ppermute | solution.py:412
  114.2 13.5 %collective-permute-start.13 = (bf16[144,128]{1,0:T(8,128)(2,1)S(1)}, bf16[144,128]{1,0:T(8,128)(2,1)S(1)}, u32[]{:S(2)}, u32[]{:S(2)}) collective-permute-start(bf16[144,128]{1,0:T(8,128)(2,1)S(1)} %get-tuple-element.77), channel_id=1, source_target_pairs={{0,7},{1,6},{2,5},{3,4},{4,3},{5,2},{6,1},{7,0},{8,15},{9,14},{10,... | collective-permute-start | bytes 110600 | tf_op jit(solution)/shard_map/ppermute | solution.py:412
  114.5 13.2 %collective-permute-start.7 = (bf16[144,128]{1,0:T(8,128)(2,1)S(1)}, bf16[144,128]{1,0:T(8,128)(2,1)S(1)}, u32[]{:S(2)}, u32[]{:S(2)}) collective-permute-start(bf16[144,128]{1,0:T(8,128)(2,1)S(1)} %get-tuple-element.71), channel_id=1, source_target_pairs={{0,1},{1,0},{2,3},{3,2},{4,5},{5,4},{6,7},{7,6},{8,9},{9,8},{10,11... | collective-permute-start | bytes 110600 | tf_op jit(solution)/shard_map/ppermute | solution.py:412
  118.4 9.2 %collective-permute-start.8 = (bf16[144,128]{1,0:T(8,128)(2,1)S(1)}, bf16[144,128]{1,0:T(8,128)(2,1)S(1)}, u32[]{:S(2)}, u32[]{:S(2)}) collective-permute-start(bf16[144,128]{1,0:T(8,128)(2,1)S(1)} %get-tuple-element.72), channel_id=1, source_target_pairs={{0,2},{1,3},{2,0},{3,1},{4,6},{5,7},{6,4},{7,5},{8,10},{9,11},{10,... | collective-permute-start | bytes 110600 | tf_op jit(solution)/shard_map/ppermute | solution.py:412
  124.4 3.4 %collective-permute-start.9 = (bf16[144,128]{1,0:T(8,128)(2,1)S(1)}, bf16[144,128]{1,0:T(8,128)(2,1)S(1)}, u32[]{:S(2)}, u32[]{:S(2)}) collective-permute-start(bf16[144,128]{1,0:T(8,128)(2,1)S(1)} %get-tuple-element.73), channel_id=1, source_target_pairs={{0,3},{1,2},{2,1},{3,0},{4,7},{5,6},{6,5},{7,4},{8,11},{9,10},{10,... | collective-permute-start | bytes 110600 | tf_op jit(solution)/shard_map/ppermute | solution.py:412
  127.9 7.3 %collective-permute-start.14 = (bf16[336,128]{1,0:T(8,128)(2,1)S(1)}, bf16[336,128]{1,0:T(8,128)(2,1)S(1)}, u32[]{:S(2)}, u32[]{:S(2)}) collective-permute-start(bf16[336,128]{1,0:T(8,128)(2,1)S(1)} %shard_map.117.refs_0_), channel_id=1, source_target_pairs={{0,8},{8,16},{16,24},{24,0},{1,9},{9,17},{17,25},{25,1},{2,10},{10... | collective-permute-start | bytes 258056 | tf_op jit(solution)/shard_map/ppermute | solution.py:417
  129.2 11.6 %collective-permute-start.15 = (bf16[336,128]{1,0:T(8,128)(2,1)S(1)}, bf16[336,128]{1,0:T(8,128)(2,1)S(1)}, u32[]{:S(2)}, u32[]{:S(2)}) collective-permute-start(bf16[336,128]{1,0:T(8,128)(2,1)S(1)} %shard_map.117.refs_0_), channel_id=1, source_target_pairs={{0,16},{8,24},{16,0},{24,8},{1,17},{9,25},{17,1},{25,9},{2,18},{10... | collective-permute-start | bytes 258056 | tf_op jit(solution)/shard_map/ppermute | solution.py:417
  132.2 8.6 %collective-permute-start.16 = (bf16[336,128]{1,0:T(8,128)(2,1)S(1)}, bf16[336,128]{1,0:T(8,128)(2,1)S(1)}, u32[]{:S(2)}, u32[]{:S(2)}) collective-permute-start(bf16[336,128]{1,0:T(8,128)(2,1)S(1)} %shard_map.117.refs_0_), channel_id=1, source_target_pairs={{0,24},{8,0},{16,8},{24,16},{1,25},{9,1},{17,9},{25,17},{2,26},{10... | collective-permute-start | bytes 258056 | tf_op jit(solution)/shard_map/ppermute | solution.py:417
  140.8 3.6 %collective-permute-start.17 = (bf16[336,128]{1,0:T(8,128)(2,1)S(1)}, bf16[336,128]{1,0:T(8,128)(2,1)S(1)}, u32[]{:S(2)}, u32[]{:S(2)}) collective-permute-start(bf16[336,128]{1,0:T(8,128)(2,1)S(1)} %shard_map.118.refs_1_), channel_id=1, source_target_pairs={{0,1},{1,0},{2,3},{3,2},{4,5},{5,4},{6,7},{7,6},{8,9},{9,8},{10,11... | collective-permute-start | bytes 258056 | tf_op jit(solution)/shard_map/ppermute | solution.py:412
  140.9 6.0 %collective-permute-start.18 = (bf16[336,128]{1,0:T(8,128)(2,1)S(1)}, bf16[336,128]{1,0:T(8,128)(2,1)S(1)}, u32[]{:S(2)}, u32[]{:S(2)}) collective-permute-start(bf16[336,128]{1,0:T(8,128)(2,1)S(1)} %shard_map.118.refs_1_), channel_id=1, source_target_pairs={{0,2},{1,3},{2,0},{3,1},{4,6},{5,7},{6,4},{7,5},{8,10},{9,11},{10,... | collective-permute-start | bytes 258056 | tf_op jit(solution)/shard_map/ppermute | solution.py:412
  142.4 5.1 %collective-permute-start.19 = (bf16[336,128]{1,0:T(8,128)(2,1)S(1)}, bf16[336,128]{1,0:T(8,128)(2,1)S(1)}, u32[]{:S(2)}, u32[]{:S(2)}) collective-permute-start(bf16[336,128]{1,0:T(8,128)(2,1)S(1)} %shard_map.118.refs_1_), channel_id=1, source_target_pairs={{0,3},{1,2},{2,1},{3,0},{4,7},{5,6},{6,5},{7,4},{8,11},{9,10},{10,... | collective-permute-start | bytes 258056 | tf_op jit(solution)/shard_map/ppermute | solution.py:412
  142.8 5.1 %collective-permute-start.20 = (bf16[336,128]{1,0:T(8,128)(2,1)S(1)}, bf16[336,128]{1,0:T(8,128)(2,1)S(1)}, u32[]{:S(2)}, u32[]{:S(2)}) collective-permute-start(bf16[336,128]{1,0:T(8,128)(2,1)S(1)} %shard_map.118.refs_1_), channel_id=1, source_target_pairs={{0,4},{1,5},{2,6},{3,7},{4,0},{5,1},{6,2},{7,3},{8,12},{9,13},{10,... | collective-permute-start | bytes 258056 | tf_op jit(solution)/shard_map/ppermute | solution.py:412
  144.2 8.5 %collective-permute-start.21 = (bf16[336,128]{1,0:T(8,128)(2,1)S(1)}, bf16[336,128]{1,0:T(8,128)(2,1)S(1)}, u32[]{:S(2)}, u32[]{:S(2)}) collective-permute-start(bf16[336,128]{1,0:T(8,128)(2,1)S(1)} %shard_map.118.refs_1_), channel_id=1, source_target_pairs={{0,5},{1,4},{2,7},{3,6},{4,1},{5,0},{6,3},{7,2},{8,13},{9,12},{10,... | collective-permute-start | bytes 258056 | tf_op jit(solution)/shard_map/ppermute | solution.py:412
  144.5 8.3 %collective-permute-start.22 = (bf16[336,128]{1,0:T(8,128)(2,1)S(1)}, bf16[336,128]{1,0:T(8,128)(2,1)S(1)}, u32[]{:S(2)}, u32[]{:S(2)}) collective-permute-start(bf16[336,128]{1,0:T(8,128)(2,1)S(1)} %shard_map.118.refs_1_), channel_id=1, source_target_pairs={{0,6},{1,7},{2,4},{3,5},{4,2},{5,3},{6,0},{7,1},{8,14},{9,15},{10,... | collective-permute-start | bytes 258056 | tf_op jit(solution)/shard_map/ppermute | solution.py:412
  146.9 5.9 %collective-permute-start.23 = (bf16[336,128]{1,0:T(8,128)(2,1)S(1)}, bf16[336,128]{1,0:T(8,128)(2,1)S(1)}, u32[]{:S(2)}, u32[]{:S(2)}) collective-permute-start(bf16[336,128]{1,0:T(8,128)(2,1)S(1)} %shard_map.118.refs_1_), channel_id=1, source_target_pairs={{0,7},{1,6},{2,5},{3,4},{4,3},{5,2},{6,1},{7,0},{8,15},{9,14},{10,... | collective-permute-start | bytes 258056 | tf_op jit(solution)/shard_map/ppermute | solution.py:412

commit v7 on v6

--- a/solution.py
+++ b/solution.py
@@ -69,9 +69,36 @@
     return pltpu.roll(value, shift % value.shape[0], 0)
 
 
+def spatial_pre(xs, weight, at, rows_step):
+    wide, ch = xs.shape[1:]
+    flat = rows_step * wide
+    left = jnp.concatenate(
+        [xs[at + a : at + a + rows_step].reshape(flat, ch) for a in range(3)], axis=1
+    )
+    y = mm(left, weight)
+    return y[:, ch : 2 * ch] + roll_rows(y[:, :ch], 1) + roll_rows(y[:, 2 * ch :], -1)
+
+
+def forward_weight(w_ref):
+    return jnp.concatenate(
+        [jnp.concatenate([w_ref[3 * a + b] for b in range(3)], axis=1) for a in range(3)], axis=0
+    )
+
+
+def clear_ends(ref):
+    last = ref.shape[0] - 1
+    ref[0] = jnp.zeros(ref.shape[1:], ref.dtype)
+    ref[last] = jnp.zeros(ref.shape[1:], ref.dtype)
+
+
+def put_rows(ref, at, value):
+    count, cols, ch = value.shape
+    ref[1 + at : 1 + at + count] = jnp.zeros((count,) + ref.shape[1:], ref.dtype)
+    ref[1 + at : 1 + at + count, :cols, :] = value
+
+
 def spatial_fwd_kernel(
-    rows_step, x_hbm, w_ref, cot_hbm, send_hbm, slope_hbm,
-    x_in, xs, sends, slopes, in_sems, cot_sems, send_sems, out_sems,
+    rows_step, x_hbm, w_ref, cot_hbm, send_hbm, x_in, xs, sends, in_sems, cot_sems, send_sems
 ):
     rows, cols, ch = x_in.shape
     wide = xs.shape[1]
@@ -83,69 +110,53 @@
     loads = [
         pltpu.make_async_copy(x_hbm.at[part(n)], x_in.at[part(n)], in_sems.at[n]) for n in range(steps)
     ]
-    stores = [
-        (
-            pltpu.make_async_copy(sends.at[part(n)], send_hbm.at[part(n)], send_sems.at[n]),
-            pltpu.make_async_copy(slopes.at[part(n)], slope_hbm.at[part(n)], out_sems.at[n]),
-        )
-        for n in range(steps)
-    ]
     cot_loads = [
         pltpu.make_async_copy(cot_hbm.at[part(n)], sends.at[part(n), 1], cot_sems.at[n])
         for n in range(steps)
     ]
-    for n in range(steps):
-        loads[n].start()
-        cot_loads[n].start()
-    xs[0] = jnp.zeros((wide, ch), BF16)
-    xs[rows + 1] = jnp.zeros((wide, ch), BF16)
-    weight = jnp.concatenate(
-        [jnp.concatenate([w_ref[3 * a + b] for b in range(3)], axis=1) for a in range(3)], axis=0
-    )
-    flat = rows_step * wide
+    stores = [
+        pltpu.make_async_copy(sends.at[part(n)], send_hbm.at[part(n)], send_sems.at[n])
+        for n in range(steps)
+    ]
+    for load in loads + cot_loads:
+        load.start()
+    clear_ends(xs)
+    weight = forward_weight(w_ref)
 
     def bring(step):
         loads[step].wait()
         at = step * rows_step
-        xs[1 + at : 1 + at + rows_step] = jnp.zeros((rows_step, wide, ch), BF16)
-        xs[1 + at : 1 + at + rows_step, :cols, :] = x_in[at : at + rows_step]
+        put_rows(xs, at, x_in[at : at + rows_step])
 
     bring(0)
     for step in range(steps):
         if step + 1 < steps:
             bring(step + 1)
         at = step * rows_step
-        left = jnp.concatenate(
-            [xs[at + a : at + a + rows_step].reshape(flat, ch) for a in range(3)], axis=1
-        )
-        y = mm(left, weight)
-        pre = y[:, ch : 2 * ch] + roll_rows(y[:, :ch], 1) + roll_rows(y[:, 2 * ch :], -1)
-        act, slope = silu_parts(pre)
+        act, _ = silu_parts(spatial_pre(xs, weight, at, rows_step))
         sends[at : at + rows_step, 0] = act.astype(BF16).reshape(rows_step, wide, ch)[:, :cols]
-        slopes[at : at + rows_step] = slope.astype(BF16).reshape(rows_step, wide, ch)
         cot_loads[step].wait()
-        for store in stores[step]:
-            store.start()
-    for pair in stores:
-        for store in pair:
-            store.wait()
+        stores[step].start()
+    for store in stores:
+        store.wait()
+
+
+def spatial_slope_kernel(rows_step, x_ref, w_ref, slope_ref, xs):
+    rows, cols, ch = x_ref.shape
+    wide = xs.shape[1]
+    clear_ends(xs)
+    put_rows(xs, 0, x_ref[...])
+    weight = forward_weight(w_ref)
+    for at in range(0, rows, rows_step):
+        _, slope = silu_parts(spatial_pre(xs, weight, at, rows_step))
+        slope_ref[at : at + rows_step] = (
+            slope.astype(BF16).reshape(rows_step, wide, ch)[:, :cols]
+        )
 
 
 def hand_out(here_ref, total_ref, pieces):
     for peer, piece in enumerate(pieces):
         piece[...] = total_ref[jnp.bitwise_xor(here_ref[1], peer)].astype(piece.dtype)
-
-
-def columns_kernel(rows_step, x_ref, slope_ref, cat_ref, near_ref):
-    rows, cols, ch = x_ref.shape
-    wide = cat_ref.shape[1] // rows
-    flat = rows_step * wide
-    pad = jnp.zeros((rows_step, wide - cols, ch), F32)
-    for at in range(0, rows, rows_step):
-        x = jnp.concatenate([x_ref[at : at + rows_step].astype(F32), pad], axis=1).reshape(flat, ch)
-        x_cat = jnp.concatenate([roll_rows(x, 1), x, roll_rows(x, -1)], axis=1)
-        cat_ref[:, at * wide : at * wide + flat] = x_cat.T.astype(BF16)
-    near_ref[...] = slope_ref[...]
 
 
 def taps_up(gs, at, rows_step):
@@ -156,24 +167,26 @@
     )
 
 
-def spatial_wgrad_kernel(
-    rows_step, scale, here_ref, got_ref, slope_ref, cat_ref, gs, *rest
-):
-    pieces, total_ref = rest[:-1], rest[-1]
+def fill_grads(rows_step, gs, got_ref, slope_ref):
+    clear_ends(gs)
+    for at in range(0, got_ref.shape[0], rows_step):
+        grads = got_ref[at : at + rows_step].astype(F32)
+        slopes = slope_ref[at : at + rows_step].astype(F32)
+        put_rows(gs, at, (grads * slopes).astype(BF16))
+
+
+def spatial_wgrad_kernel(rows_step, scale, here_ref, got_ref, slope_ref, x_ref, *rest):
+    pieces, (gs, total_ref) = rest[:-2], rest[-2:]
     rows, cols, ch = got_ref.shape
     wide = gs.shape[1]
     flat = rows_step * wide
-    gs[0] = jnp.zeros((wide, ch), BF16)
-    gs[rows + 1] = jnp.zeros((wide, ch), BF16)
-    for at in range(0, rows, rows_step):
-        gs[1 + at : 1 + at + rows_step] = jnp.zeros((rows_step, wide, ch), BF16)
-        gs[1 + at : 1 + at + rows_step, :cols, :] = (
-            got_ref[at : at + rows_step].astype(F32)
-            * slope_ref[at : at + rows_step, :cols, :].astype(F32)
-        ).astype(BF16)
+    pad = jnp.zeros((rows_step, wide - cols, ch), F32)
+    fill_grads(rows_step, gs, got_ref, slope_ref)
     total = jnp.zeros((3 * ch, 3 * ch), F32)
     for at in range(0, rows, rows_step):
-        total = total + mm(cat_ref[:, at * wide : at * wide + flat], taps_up(gs, at, rows_step))
+        x = jnp.concatenate([x_ref[at : at + rows_step].astype(F32), pad], axis=1).reshape(flat, ch)
+        x_cat = jnp.concatenate([roll_rows(x, 1), x, roll_rows(x, -1)], axis=1)
+        total = total + mm(x_cat.T.astype(BF16), taps_up(gs, at, rows_step))
     total_ref[...] = (
         jnp.concatenate(
             [
@@ -188,7 +201,7 @@
     hand_out(here_ref, total_ref, pieces)
 
 
-def spatial_back_kernel(rows_step, w_ref, gs, back_ref):
+def spatial_back_kernel(rows_step, w_ref, got_ref, slope_ref, back_ref, gs):
     rows, cols, ch = back_ref.shape
     wide = gs.shape[1]
     weight = jnp.concatenate(
@@ -198,6 +211,7 @@
         ],
         axis=0,
     )
+    fill_grads(rows_step, gs, got_ref, slope_ref)
     for at in range(0, rows, rows_step):
         y = mm(taps_up(gs, at, rows_step), weight)
         back = y[:, ch : 2 * ch] + roll_rows(y[:, :ch], -1) + roll_rows(y[:, 2 * ch :], 1)
@@ -453,25 +467,33 @@
     here = jnp.stack([lax.axis_index("seg"), lax.axis_index("grp")]).astype(jnp.int32)
     space_rows, time_rows, unite_rows = (n * ch // peers for n in (9, LAYERS * TAPS, 2))
 
-    send, space_slope = call(
+    (send,) = call(
         functools.partial(spatial_fwd_kernel, rows_step),
-        [((rows, 2, cols, ch), BF16, HBM), ((rows, wide, ch), BF16, HBM)],
+        [((rows, 2, cols, ch), BF16, HBM)],
         [
             pltpu.VMEM((rows, cols, ch), BF16),
             pltpu.VMEM((rows + 2, wide, ch), BF16),
             pltpu.VMEM((rows, 2, cols, ch), BF16),
-            pltpu.VMEM((rows, wide, ch), BF16),
-            pltpu.SemaphoreType.DMA((steps,)),
             pltpu.SemaphoreType.DMA((steps,)),
             pltpu.SemaphoreType.DMA((steps,)),
             pltpu.SemaphoreType.DMA((steps,)),
         ],
         2 * 9 * pixels * ch * ch,
-        pixels * ch * 12,
+        pixels * ch * 8,
         [(frames_in[0], HBM), (spatial_weight, VMEM), (cotangent[0], HBM)],
     )
+    send, frame = lax.optimization_barrier((send, frames_in[0]))
     send = send.reshape(rows, 2, split, block, ch).swapaxes(1, 2).reshape(devices, 2, block, ch)
     got = exchange(send)
+    (space_slope,) = call(
+        functools.partial(spatial_slope_kernel, rows_step),
+        [((rows, cols, ch), BF16, VMEM)],
+        [pltpu.VMEM((rows + 2, wide, ch), BF16)],
+        2 * 9 * pixels * ch * ch,
+        pixels * ch * 4,
+        [(frame, VMEM), (spatial_weight, VMEM)],
+    )
+    got, space_slope = lax.optimization_barrier((got, space_slope))
 
     padded = (frames + 2 * HALO, high, ch)
     whole = (frames, high, ch)
@@ -526,35 +548,27 @@
     )
     time_sum = reduce_in_grp(time_pieces)
     time_sum, grad_time = lax.optimization_barrier((time_sum, grad_time))
-    x_cat, space_slope = call(
-        functools.partial(columns_kernel, rows_step),
-        [((3 * ch, rows * wide), BF16, VMEM), ((rows, wide, ch), BF16, VMEM)],
-        [],
-        0,
-        pixels * ch * 12,
-        [(frames_in[0], VMEM), (space_slope, VMEM)],
+    united_send, grad_time = lax.optimization_barrier((united_send, grad_time))
+    united = exchange(united_send)
+    space_pieces = call(
+        functools.partial(spatial_wgrad_kernel, rows_step, scale),
+        [((space_rows, ch), BF16, VMEM)] * peers,
+        [pltpu.VMEM((rows + 2, wide, ch), BF16), pltpu.VMEM((peers, space_rows, ch), F32)],
+        2 * 9 * pixels * ch * ch,
+        pixels * ch * 8,
+        [(here, SMEM), (grad_time, VMEM), (space_slope, VMEM), (frame, VMEM)],
         MID_VMEM,
     )
-    gs, *space_pieces = call(
-        functools.partial(spatial_wgrad_kernel, rows_step, scale),
-        [((rows + 2, wide, ch), BF16, VMEM)] + [((space_rows, ch), BF16, VMEM)] * peers,
-        [pltpu.VMEM((peers, space_rows, ch), F32)],
-        2 * 9 * pixels * ch * ch,
-        pixels * ch * 18,
-        [(here, SMEM), (grad_time, VMEM), (space_slope, VMEM), (x_cat, VMEM)],
-        MID_VMEM,
-    )
-    united_send, space_pieces[0] = lax.optimization_barrier((united_send, space_pieces[0]))
-    united = exchange(united_send)
     (back,) = call(
         functools.partial(spatial_back_kernel, rows_step),
         [((rows, cols, ch), BF16, VMEM)],
-        [],
+        [pltpu.VMEM((rows + 2, wide, ch), BF16)],
         2 * 9 * pixels * ch * ch,
-        pixels * ch * 4,
-        [(spatial_weight, VMEM), (gs, VMEM)],
+        pixels * ch * 6,
+        [(spatial_weight, VMEM), (grad_time, VMEM), (space_slope, VMEM)],
         MID_VMEM,
     )
+    space_pieces = list(space_pieces)
     space_pieces[0], back = lax.optimization_barrier((space_pieces[0], back))
     space_parts = [flip(part, peer) if peer else part for peer, part in enumerate(space_pieces)]
     (plane,) = call(

time: 156 us -> 152 us (0.974)
  blocking collectives: 53.3 us -> 0 us
  waiting for transfers between devices: 21 us -> 62.9 us
  starting transfers between devices: 36.7 us -> 43 us
  Pallas kernels: 37.2 us -> 40.8 us
  local copies, waits for them, and re-layouts: 5.77 us -> 3.33 us
    all_to_all x1 -> x0, blocking collectives: 53.3 us -> none  [exchange(): return lax.all_to_all(blocks, AXES, split_axis=0, concat_axis=0, tiled=True)]
    all_to_all x2 -> x3, waiting for transfers between devices: 3.42 us -> 44 us  [exchange(): return lax.all_to_all(blocks, AXES, split_axis=0, concat_axis=0, tiled=True)]
    all_to_all x2 -> x3, starting transfers between devices: 7.43 us -> 15.3 us  [exchange(): return lax.all_to_all(blocks, AXES, split_axis=0, concat_axis=0, tiled=True)]
    pallas_call x10, Pallas kernels: 37.2 us -> 40.8 us  [call(): pl.pallas_call(kernel, out_shape=[jax.ShapeDtypeStruct(shape, kind) for s...]
    unnamed x18 -> x14, local copies, waits for them, and re-layouts: 5.77 us -> 3.33 us
    ppermute x21, waiting for transfers between devices: 9.73 us -> 11.3 us  [flip(): return lax.ppermute(value, 'grp', [(i, i ^ peer) for i in range(size)])]
  transfers between devices with their start and end apart: 26 -> 27, of which waited for: 8 -> 9; matrix products, arithmetic and copies ran while one was open for 0% -> 0% of each run, Pallas kernels for 9% -> 13%
where the time goes in v7:
time: 152 us
  waiting for transfers between devices  62.9 us (41%)
  starting transfers between devices  43 us (28%)
  Pallas kernels  40.8 us (27%)
  local copies, waits for them, and re-layouts  3.33 us (2%)
    all_to_all x3, waiting for transfers between devices, exchange(): return lax.all_to_all(blocks, AXES, split_axis=0, concat_axis=0, tiled=True)  44 us
    pallas_call x10, Pallas kernels, call(): pl.pallas_call(kernel, out_shape=[jax.ShapeDtypeStruct(shape, kind) for s...  40.8 us
    ppermute x21, starting transfers between devices, flip(): return lax.ppermute(value, 'grp', [(i, i ^ peer) for i in range(size)])  22.7 us
    all_to_all x3, starting transfers between devices, exchange(): return lax.all_to_all(blocks, AXES, split_axis=0, concat_axis=0, tiled=True)  15.3 us
    ppermute x21, waiting for transfers between devices, flip(): return lax.ppermute(value, 'grp', [(i, i ^ peer) for i in range(size)])  11.3 us
    ppermute x3, waiting for transfers between devices, turn_by(): lax.ppermute(value, 'seg', [(i, (i + turn) % size) for i in range(size)])  7.61 us
    ppermute x3, starting transfers between devices, turn_by(): lax.ppermute(value, 'seg', [(i, (i + turn) % size) for i in range(size)])  5.07 us
    unnamed x14, local copies, waits for them, and re-layouts  3.33 us
  transfers between devices with their start and end apart: 27, of which 9 were waited for; matrix products, arithmetic and copies ran while one was open for 0% of the time, Pallas kernels for 13%

profile of v7, /device:TPU:0, one launch (start us, length us, event | category | flops | bytes accessed | tf_op | source)
XLA Modules:
  0.0 151.6 jit_solution(14133950034470737196)
XLA Ops:
  0.6 6.6 %shard_map.110 = bf16[32,2,120,128]{3,2,1,0:T(8,128)(2,1)} custom-call(bf16[32,120,128]{2,1,0:T(8,128)(2,1)} %bitcast.9, bf16[9,128,128]{2,1,0:T(8,128)(2,1)} %w_ref.5, bf16[32,120,128]{2,1,0:T(8,128)(2,1)} %bitcast.12), custom_call_target="tpu_custom_call" | custom-call | flops 1132462080 | bytes 3932160 | tf_op jit(solution)/shard_map/pallas_call | solution.py:57
  7.2 7.5 %all-to-all-start = ((bf16[32,2,120,128]{3,2,1,0:T(8,128)(2,1)}), bf16[32,2,120,128]{3,2,1,0:T(8,128)(2,1)S(1)}, u32[]{:S(2)}, u32[]{:S(2)}) async-start(bf16[32,2,120,128]{3,2,1,0:T(8,128)(2,1)} %shard_map.110), calls=%async_computation | async-start | bytes 3932160 | tf_op jit(solution)/shard_map/all_to_all | solution.py:421
  14.7 4.6 %shard_map.111.slope_ref = bf16[32,120,128]{2,1,0:T(8,128)(2,1)} custom-call(bf16[32,120,128]{2,1,0:T(8,128)(2,1)} %bitcast.10, bf16[9,128,128]{2,1,0:T(8,128)(2,1)} %w_ref.5), custom_call_target="tpu_custom_call" | custom-call | flops 1132462080 | bytes 1966080 | tf_op jit(solution)/shard_map/pallas_call | solution.py:57
  19.3 41.3 %all-to-all-done.got_hbm = bf16[32,2,120,128]{3,2,1,0:T(8,128)(2,1)S(1)} async-done(((bf16[32,2,120,128]{3,2,1,0:T(8,128)(2,1)}), bf16[32,2,120,128]{3,2,1,0:T(8,128)(2,1)S(1)}, u32[]{:S(2)}, u32[]{:S(2)}) %all-to-all-start) | async-done | bytes 1966112 | tf_op jit(solution)/shard_map/all_to_all | solution.py:421
  60.6 1.3 copy-done.6
  61.9 11.7 %shard_map.112 = (bf16[32,120,128]{2,1,0:T(8,128)(2,1)}, bf16[32,120,128]{2,1,0:T(8,128)(2,1)}, bf16[32,128,128]{2,1,0:T(8,128)(2,1)}, bf16[32,128,128]{2,1,0:T(...) custom-call(s32[2]{0:T(128)} %dil_ref.3, ...), custom_call_target="tpu_custom_call" | custom-call | flops 2768240640 | bytes 8847360 | tf_op jit(solution)/shard_map/pallas_call | solution.py:57
  73.6 4.2 %all-to-all-start.1 = ((bf16[32,120,128]{2,1,0:T(8,128)(2,1)}), bf16[32,120,128]{2,1,0:T(8,128)(2,1)S(1)}, u32[]{:S(2)}, u32[]{:S(2)}) async-start(bf16[32,120,128]{2,1,0:T(8,128)(2,1)} %get-tuple-element.61), calls=%async_computation.1 | async-start | bytes 1966080 | tf_op jit(solution)/shard_map/all_to_all | solution.py:421
  77.8 0.6 pad_add_fusion.here_ref
  78.4 9.4 %shard_map.113 = (bf16[192,128]{1,0:T(8,128)(2,1)}, bf16[192,128]{1,0:T(8,128)(2,1)}, bf16[192,128]{1,0:T(8,128)(2,1)}, bf16[192,128]{1,0:T(8,128)(2,1)}, bf16[1...) custom-call(s32[2]{0:T(128)} %pad_add_fusion.here_ref, ...), custom_call_target="tpu_custom_call" | custom-call | flops 1509949440 | bytes 6881280 | tf_op jit(solution)/shard_map/pallas_call | solution.py:57
  87.8 0.1 collective-permute-start
  87.9 1.7 %collective-permute-start.1 = (bf16[192,128]{1,0:T(8,128)(2,1)}, bf16[192,128]{1,0:T(8,128)(2,1)S(1)}, u32[]{:S(2)}, u32[]{:S(2)}) collective-permute-start(bf16[192,128]{1,0:T(8,128)(2,1)} %get-tuple-element.55), channel_id=1, source_target_pairs={{0,2},{1,3},{2,0},{3,1},{4,6},{5,7},{6,4},{7,5},{8,10},{9,11},{10,... | collective-permute-start | bytes 147464 | tf_op jit(solution)/shard_map/ppermute | solution.py:426
  89.6 0.2 collective-permute-start.2
  89.8 1.5 %collective-permute-start.3 = (bf16[192,128]{1,0:T(8,128)(2,1)}, bf16[192,128]{1,0:T(8,128)(2,1)S(1)}, u32[]{:S(2)}, u32[]{:S(2)}) collective-permute-start(bf16[192,128]{1,0:T(8,128)(2,1)} %get-tuple-element.57), channel_id=1, source_target_pairs={{0,4},{1,5},{2,6},{3,7},{4,0},{5,1},{6,2},{7,3},{8,12},{9,13},{10,... | collective-permute-start | bytes 147464 | tf_op jit(solution)/shard_map/ppermute | solution.py:426
  91.3 0.2 collective-permute-start.4
  91.5 2.5 %collective-permute-start.5 = (bf16[192,128]{1,0:T(8,128)(2,1)}, bf16[192,128]{1,0:T(8,128)(2,1)S(1)}, u32[]{:S(2)}, u32[]{:S(2)}) collective-permute-start(bf16[192,128]{1,0:T(8,128)(2,1)} %get-tuple-element.59), channel_id=1, source_target_pairs={{0,6},{1,7},{2,4},{3,5},{4,2},{5,3},{6,0},{7,1},{8,14},{9,15},{10,... | collective-permute-start | bytes 147464 | tf_op jit(solution)/shard_map/ppermute | solution.py:426
  94.0 0.4 collective-permute-start.6
  94.4 2.4 %collective-permute-done.4.refs_5_ = bf16[192,128]{1,0:T(8,128)(2,1)S(1)} collective-permute-done((bf16[192,128]{1,0:T(8,128)(2,1)}, bf16[192,128]{1,0:T(8,128)(2,1)S(1)}, u32[]{:S(2)}, u32[]{:S(2)}) %collective-permute-start.4) | collective-permute-done | bytes 49184 | tf_op jit(solution)/shard_map/ppermute | solution.py:426
  96.9 2.1 %collective-permute-done.6.refs_7_ = bf16[192,128]{1,0:T(8,128)(2,1)S(1)} collective-permute-done((bf16[192,128]{1,0:T(8,128)(2,1)}, bf16[192,128]{1,0:T(8,128)(2,1)S(1)}, u32[]{:S(2)}, u32[]{:S(2)}) %collective-permute-start.6) | collective-permute-done | bytes 49184 | tf_op jit(solution)/shard_map/ppermute | solution.py:426
  98.9 0.8 copy-done.2
  99.7 0.1 shard_map.114.first_ref
  99.8 2.7 %all-to-all-done.1.got_ref = bf16[32,120,128]{2,1,0:T(8,128)(2,1)S(1)} async-done(((bf16[32,120,128]{2,1,0:T(8,128)(2,1)}), bf16[32,120,128]{2,1,0:T(8,128)(2,1)S(1)}, u32[]{:S(2)}, u32[]{:S(2)}) %all-to-all-start.1) | async-done | bytes 983072 | tf_op jit(solution)/shard_map/all_to_all | solution.py:421
  102.4 3.6 %all-to-all-start.2 = ((bf16[32,120,128]{2,1,0:T(8,128)(2,1)}), bf16[32,120,128]{2,1,0:T(8,128)(2,1)S(1)}, u32[]{:S(2)}, u32[]{:S(2)}) async-start(bf16[32,120,128]{2,1,0:T(8,128)(2,1)} %get-tuple-element.63), calls=%async_computation.2 | async-start | bytes 1966080 | tf_op jit(solution)/shard_map/all_to_all | solution.py:421
  106.1 1.2 copy-done.4
  107.3 2.6 %shard_map.115 = (bf16[144,128]{1,0:T(8,128)(2,1)S(1)}, bf16[144,128]{1,0:T(8,128)(2,1)S(1)}, bf16[144,128]{1,0:T(8,128)(2,1)S(1)}, bf16[144,128]{1,0:T(8,128)(2...) custom-call(s32[2]{0:T(128)S(1)} %copy-done.3, ...), custom_call_target="tpu_custom_call" | custom-call | flops 1132462080 | bytes 3932160 | tf_op jit(solution)/shard_map/pallas_call | solution.py:57
  109.9 1.8 %collective-permute-start.10 = (bf16[144,128]{1,0:T(8,128)(2,1)S(1)}, bf16[144,128]{1,0:T(8,128)(2,1)S(1)}, u32[]{:S(2)}, u32[]{:S(2)}) collective-permute-start(bf16[144,128]{1,0:T(8,128)(2,1)S(1)} %get-tuple-element.72), channel_id=1, source_target_pairs={{0,4},{1,5},{2,6},{3,7},{4,0},{5,1},{6,2},{7,3},{8,12},{9,13},{10,... | collective-permute-start | bytes 110600 | tf_op jit(solution)/shard_map/ppermute | solution.py:426
  111.8 2.4 %collective-permute-start.12 = (bf16[144,128]{1,0:T(8,128)(2,1)S(1)}, bf16[144,128]{1,0:T(8,128)(2,1)S(1)}, u32[]{:S(2)}, u32[]{:S(2)}) collective-permute-start(bf16[144,128]{1,0:T(8,128)(2,1)S(1)} %get-tuple-element.74), channel_id=1, source_target_pairs={{0,6},{1,7},{2,4},{3,5},{4,2},{5,3},{6,0},{7,1},{8,14},{9,15},{10,... | collective-permute-start | bytes 110600 | tf_op jit(solution)/shard_map/ppermute | solution.py:426
  114.2 0.3 collective-permute-start.13
  114.4 0.4 collective-permute-start.7
  114.8 2.3 %collective-permute-start.8 = (bf16[144,128]{1,0:T(8,128)(2,1)S(1)}, bf16[144,128]{1,0:T(8,128)(2,1)S(1)}, u32[]{:S(2)}, u32[]{:S(2)}) collective-permute-start(bf16[144,128]{1,0:T(8,128)(2,1)S(1)} %get-tuple-element.70), channel_id=1, source_target_pairs={{0,2},{1,3},{2,0},{3,1},{4,6},{5,7},{6,4},{7,5},{8,10},{9,11},{10,... | collective-permute-start | bytes 110600 | tf_op jit(solution)/shard_map/ppermute | solution.py:426
  117.1 1.5 %collective-permute-done.11.refs_5_ = bf16[144,128]{1,0:T(8,128)(2,1)S(1)} collective-permute-done((bf16[144,128]{1,0:T(8,128)(2,1)S(1)}, bf16[144,128]{1,0:T(8,128)(2,1)S(1)}, u32[]{:S(2)}, u32[]{:S(2)}) %collective-permute-start.11) | collective-permute-done | bytes 36896 | tf_op jit(solution)/shard_map/ppermute | solution.py:426
  118.6 2.3 %collective-permute-start.9 = (bf16[144,128]{1,0:T(8,128)(2,1)S(1)}, bf16[144,128]{1,0:T(8,128)(2,1)S(1)}, u32[]{:S(2)}, u32[]{:S(2)}) collective-permute-start(bf16[144,128]{1,0:T(8,128)(2,1)S(1)} %get-tuple-element.71), channel_id=1, source_target_pairs={{0,3},{1,2},{2,1},{3,0},{4,7},{5,6},{6,5},{7,4},{8,11},{9,10},{10,... | collective-permute-start | bytes 110600 | tf_op jit(solution)/shard_map/ppermute | solution.py:426
  120.9 3.2 %shard_map.116 = bf16[32,120,128]{2,1,0:T(8,128)(2,1)} custom-call(bf16[9,128,128]{2,1,0:T(8,128)(2,1)S(1)} %copy-done.1, bf16[32,120,128]{2,1,0:T(8,128)(2,1)S(1)} %all-to-all-done.1.got_ref, bf16[32,120,128]{2,1,0:T(8,128)(2,1)S(1)} %copy-done.5), custom_call_target="tpu_custom_call" | custom-call | flops 1132462080 | bytes 2949120 | tf_op jit(solution)/shard_map/pallas_call | solution.py:57
  124.2 0.1 shard_map.117.refs_0_
  124.2 0.1 collective-permute-start.14
  124.3 4.1 %collective-permute-start.15 = (bf16[336,128]{1,0:T(8,128)(2,1)S(1)}, bf16[336,128]{1,0:T(8,128)(2,1)S(1)}, u32[]{:S(2)}, u32[]{:S(2)}) collective-permute-start(bf16[336,128]{1,0:T(8,128)(2,1)S(1)} %shard_map.117.refs_0_), channel_id=1, source_target_pairs={{0,16},{8,24},{16,0},{24,8},{1,17},{9,25},{17,1},{25,9},{2,18},{10... | collective-permute-start | bytes 258056 | tf_op jit(solution)/shard_map/ppermute | solution.py:431
  128.3 0.9 collective-permute-start.16
  129.3 2.2 %collective-permute-done.14.refs_1_ = bf16[336,128]{1,0:T(8,128)(2,1)S(1)} collective-permute-done((bf16[336,128]{1,0:T(8,128)(2,1)S(1)}, bf16[336,128]{1,0:T(8,128)(2,1)S(1)}, u32[]{:S(2)}, u32[]{:S(2)}) %collective-permute-start.14) | collective-permute-done | bytes 86048 | tf_op jit(solution)/shard_map/ppermute | solution.py:431
  131.5 5.4 %collective-permute-done.15.refs_2_ = bf16[336,128]{1,0:T(8,128)(2,1)S(1)} collective-permute-done((bf16[336,128]{1,0:T(8,128)(2,1)S(1)}, bf16[336,128]{1,0:T(8,128)(2,1)S(1)}, u32[]{:S(2)}, u32[]{:S(2)}) %collective-permute-start.15) | collective-permute-done | bytes 86048 | tf_op jit(solution)/shard_map/ppermute | solution.py:431
  137.0 0.1 collective-permute-start.17
  137.0 1.5 %collective-permute-start.18 = (bf16[336,128]{1,0:T(8,128)(2,1)S(1)}, bf16[336,128]{1,0:T(8,128)(2,1)S(1)}, u32[]{:S(2)}, u32[]{:S(2)}) collective-permute-start(bf16[336,128]{1,0:T(8,128)(2,1)S(1)} %shard_map.118.refs_1_), channel_id=1, source_target_pairs={{0,2},{1,3},{2,0},{3,1},{4,6},{5,7},{6,4},{7,5},{8,10},{9,11},{10,... | collective-permute-start | bytes 258056 | tf_op jit(solution)/shard_map/ppermute | solution.py:426
  138.6 0.3 collective-permute-start.19
  138.9 1.5 collective-permute-start.20
  140.4 0.2 collective-permute-start.21
  140.6 2.4 %collective-permute-start.22 = (bf16[336,128]{1,0:T(8,128)(2,1)S(1)}, bf16[336,128]{1,0:T(8,128)(2,1)S(1)}, u32[]{:S(2)}, u32[]{:S(2)}) collective-permute-start(bf16[336,128]{1,0:T(8,128)(2,1)S(1)} %shard_map.118.refs_1_), channel_id=1, source_target_pairs={{0,6},{1,7},{2,4},{3,5},{4,2},{5,3},{6,0},{7,1},{8,14},{9,15},{10,... | collective-permute-start | bytes 258056 | tf_op jit(solution)/shard_map/ppermute | solution.py:426
  143.0 0.6 collective-permute-start.23
  143.6 0.4 collective-permute-done.20.refs_5_
  144.0 4.9 %collective-permute-done.21.refs_6_ = bf16[336,128]{1,0:T(8,128)(2,1)S(1)} collective-permute-done((bf16[336,128]{1,0:T(8,128)(2,1)S(1)}, bf16[336,128]{1,0:T(8,128)(2,1)S(1)}, u32[]{:S(2)}, u32[]{:S(2)}) %collective-permute-start.21) | collective-permute-done | bytes 86048 | tf_op jit(solution)/shard_map/ppermute | solution.py:426
  148.9 2.6 %shard_map.119 = (f32[8,160,128]{2,1,0:T(8,128)}, f32[8,32,128]{2,1,0:T(8,128)}, f32[8,144,128]{2,1,0:T(8,128)}, bf16[32,120,128]{2,1,0:T(8,128)(2,1)}) custom-call(s32[2]{0:T(128)S(1)} %copy-done.3, bf16[32,120,128]{2,1,0:T(8,128)(2,1)S(1)} %all-to-all-done.2.refs_0_, bf16[336,128]{1,0:T(8,128)(2,1)S(1)} %shard_map.118.refs_1_, ...), custom_call_target="tpu_custom_call" | custom-call | bytes 2064384 | tf_op jit(solution)/shard_map/pallas_call | solution.py:57
  (31 shorter events, 0.1 us)
Async XLA Ops:
  7.2 53.4 %all-to-all-start = ((bf16[32,2,120,128]{3,2,1,0:T(8,128)(2,1)}), bf16[32,2,120,128]{3,2,1,0:T(8,128)(2,1)S(1)}, u32[]{:S(2)}, u32[]{:S(2)}) async-start(bf16[32,2,120,128]{3,2,1,0:T(8,128)(2,1)} %shard_map.110), calls=%async_computation | async-start | bytes 3932160 | tf_op jit(solution)/shard_map/all_to_all | solution.py:421
  60.6 1.3 copy-start.6
  73.6 28.8 %all-to-all-start.1 = ((bf16[32,120,128]{2,1,0:T(8,128)(2,1)}), bf16[32,120,128]{2,1,0:T(8,128)(2,1)S(1)}, u32[]{:S(2)}, u32[]{:S(2)}) async-start(bf16[32,120,128]{2,1,0:T(8,128)(2,1)} %get-tuple-element.61), calls=%async_computation.1 | async-start | bytes 1966080 | tf_op jit(solution)/shard_map/all_to_all | solution.py:421
  78.4 27.6 %copy-start.3 = (s32[2]{0:T(128)S(1)}, s32[2]{0:T(128)}, u32[]{:S(2)}) copy-start(s32[2]{0:T(128)} %pad_add_fusion.here_ref) | copy-start | bytes 28
  87.8 18.3 %copy-start = (bf16[1,32,120,128]{3,2,1,0:T(8,128)(2,1)S(1)}, bf16[1,32,120,128]{3,2,1,0:T(8,128)(2,1)}, u32[]{:S(2)}) copy-start(bf16[1,32,120,128]{3,2,1,0:T(8,128)(2,1)} %param.7) | copy-start | bytes 2949124
  87.8 3.6 %collective-permute-start = (bf16[192,128]{1,0:T(8,128)(2,1)}, bf16[192,128]{1,0:T(8,128)(2,1)S(1)}, u32[]{:S(2)}, u32[]{:S(2)}) collective-permute-start(bf16[192,128]{1,0:T(8,128)(2,1)} %get-tuple-element.54), channel_id=1, source_target_pairs={{0,1},{1,0},{2,3},{3,2},{4,5},{5,4},{6,7},{7,6},{8,9},{9,8},{10,11... | collective-permute-start | bytes 147464 | tf_op jit(solution)/shard_map/ppermute | solution.py:426
  87.9 6.1 %collective-permute-start.1 = (bf16[192,128]{1,0:T(8,128)(2,1)}, bf16[192,128]{1,0:T(8,128)(2,1)S(1)}, u32[]{:S(2)}, u32[]{:S(2)}) collective-permute-start(bf16[192,128]{1,0:T(8,128)(2,1)} %get-tuple-element.55), channel_id=1, source_target_pairs={{0,2},{1,3},{2,0},{3,1},{4,6},{5,7},{6,4},{7,5},{8,10},{9,11},{10,... | collective-permute-start | bytes 147464 | tf_op jit(solution)/shard_map/ppermute | solution.py:426
  89.6 4.8 %collective-permute-start.2 = (bf16[192,128]{1,0:T(8,128)(2,1)}, bf16[192,128]{1,0:T(8,128)(2,1)S(1)}, u32[]{:S(2)}, u32[]{:S(2)}) collective-permute-start(bf16[192,128]{1,0:T(8,128)(2,1)} %get-tuple-element.56), channel_id=1, source_target_pairs={{0,3},{1,2},{2,1},{3,0},{4,7},{5,6},{6,5},{7,4},{8,11},{9,10},{10,... | collective-permute-start | bytes 147464 | tf_op jit(solution)/shard_map/ppermute | solution.py:426
  89.8 4.7 %collective-permute-start.3 = (bf16[192,128]{1,0:T(8,128)(2,1)}, bf16[192,128]{1,0:T(8,128)(2,1)S(1)}, u32[]{:S(2)}, u32[]{:S(2)}) collective-permute-start(bf16[192,128]{1,0:T(8,128)(2,1)} %get-tuple-element.57), channel_id=1, source_target_pairs={{0,4},{1,5},{2,6},{3,7},{4,0},{5,1},{6,2},{7,3},{8,12},{9,13},{10,... | collective-permute-start | bytes 147464 | tf_op jit(solution)/shard_map/ppermute | solution.py:426
  91.3 5.6 %collective-permute-start.4 = (bf16[192,128]{1,0:T(8,128)(2,1)}, bf16[192,128]{1,0:T(8,128)(2,1)S(1)}, u32[]{:S(2)}, u32[]{:S(2)}) collective-permute-start(bf16[192,128]{1,0:T(8,128)(2,1)} %get-tuple-element.58), channel_id=1, source_target_pairs={{0,5},{1,4},{2,7},{3,6},{4,1},{5,0},{6,3},{7,2},{8,13},{9,12},{10,... | collective-permute-start | bytes 147464 | tf_op jit(solution)/shard_map/ppermute | solution.py:426
  91.5 5.4 %collective-permute-start.5 = (bf16[192,128]{1,0:T(8,128)(2,1)}, bf16[192,128]{1,0:T(8,128)(2,1)S(1)}, u32[]{:S(2)}, u32[]{:S(2)}) collective-permute-start(bf16[192,128]{1,0:T(8,128)(2,1)} %get-tuple-element.59), channel_id=1, source_target_pairs={{0,6},{1,7},{2,4},{3,5},{4,2},{5,3},{6,0},{7,1},{8,14},{9,15},{10,... | collective-permute-start | bytes 147464 | tf_op jit(solution)/shard_map/ppermute | solution.py:426
  94.0 4.9 %collective-permute-start.6 = (bf16[192,128]{1,0:T(8,128)(2,1)}, bf16[192,128]{1,0:T(8,128)(2,1)S(1)}, u32[]{:S(2)}, u32[]{:S(2)}) collective-permute-start(bf16[192,128]{1,0:T(8,128)(2,1)} %get-tuple-element.60), channel_id=1, source_target_pairs={{0,7},{1,6},{2,5},{3,4},{4,3},{5,2},{6,1},{7,0},{8,15},{9,14},{10,... | collective-permute-start | bytes 147464 | tf_op jit(solution)/shard_map/ppermute | solution.py:426
  98.9 0.8 copy-start.2
  102.4 46.4 %all-to-all-start.2 = ((bf16[32,120,128]{2,1,0:T(8,128)(2,1)}), bf16[32,120,128]{2,1,0:T(8,128)(2,1)S(1)}, u32[]{:S(2)}, u32[]{:S(2)}) async-start(bf16[32,120,128]{2,1,0:T(8,128)(2,1)} %get-tuple-element.63), calls=%async_computation.2 | async-start | bytes 1966080 | tf_op jit(solution)/shard_map/all_to_all | solution.py:421
  106.1 1.2 copy-start.4
  107.3 13.6 %copy-start.1 = (bf16[9,128,128]{2,1,0:T(8,128)(2,1)S(1)}, bf16[9,128,128]{2,1,0:T(8,128)(2,1)}, u32[]{:S(2)}) copy-start(bf16[9,128,128]{2,1,0:T(8,128)(2,1)} %w_ref.5) | copy-start | bytes 884740
  107.3 13.6 %copy-start.5 = (bf16[32,120,128]{2,1,0:T(8,128)(2,1)S(1)}, bf16[32,120,128]{2,1,0:T(8,128)(2,1)}, u32[]{:S(2)}) copy-start(bf16[32,120,128]{2,1,0:T(8,128)(2,1)} %shard_map.111.slope_ref) | copy-start | bytes 2949124
  109.9 4.9 %collective-permute-start.10 = (bf16[144,128]{1,0:T(8,128)(2,1)S(1)}, bf16[144,128]{1,0:T(8,128)(2,1)S(1)}, u32[]{:S(2)}, u32[]{:S(2)}) collective-permute-start(bf16[144,128]{1,0:T(8,128)(2,1)S(1)} %get-tuple-element.72), channel_id=1, source_target_pairs={{0,4},{1,5},{2,6},{3,7},{4,0},{5,1},{6,2},{7,3},{8,12},{9,13},{10,... | collective-permute-start | bytes 110600 | tf_op jit(solution)/shard_map/ppermute | solution.py:426
  111.8 6.9 %collective-permute-start.11 = (bf16[144,128]{1,0:T(8,128)(2,1)S(1)}, bf16[144,128]{1,0:T(8,128)(2,1)S(1)}, u32[]{:S(2)}, u32[]{:S(2)}) collective-permute-start(bf16[144,128]{1,0:T(8,128)(2,1)S(1)} %get-tuple-element.73), channel_id=1, source_target_pairs={{0,5},{1,4},{2,7},{3,6},{4,1},{5,0},{6,3},{7,2},{8,13},{9,12},{10,... | collective-permute-start | bytes 110600 | tf_op jit(solution)/shard_map/ppermute | solution.py:426
  111.8 12.4 %collective-permute-start.12 = (bf16[144,128]{1,0:T(8,128)(2,1)S(1)}, bf16[144,128]{1,0:T(8,128)(2,1)S(1)}, u32[]{:S(2)}, u32[]{:S(2)}) collective-permute-start(bf16[144,128]{1,0:T(8,128)(2,1)S(1)} %get-tuple-element.74), channel_id=1, source_target_pairs={{0,6},{1,7},{2,4},{3,5},{4,2},{5,3},{6,0},{7,1},{8,14},{9,15},{10,... | collective-permute-start | bytes 110600 | tf_op jit(solution)/shard_map/ppermute | solution.py:426
  114.2 10.0 %collective-permute-start.13 = (bf16[144,128]{1,0:T(8,128)(2,1)S(1)}, bf16[144,128]{1,0:T(8,128)(2,1)S(1)}, u32[]{:S(2)}, u32[]{:S(2)}) collective-permute-start(bf16[144,128]{1,0:T(8,128)(2,1)S(1)} %get-tuple-element.75), channel_id=1, source_target_pairs={{0,7},{1,6},{2,5},{3,4},{4,3},{5,2},{6,1},{7,0},{8,15},{9,14},{10,... | collective-permute-start | bytes 110600 | tf_op jit(solution)/shard_map/ppermute | solution.py:426
  114.4 9.7 %collective-permute-start.7 = (bf16[144,128]{1,0:T(8,128)(2,1)S(1)}, bf16[144,128]{1,0:T(8,128)(2,1)S(1)}, u32[]{:S(2)}, u32[]{:S(2)}) collective-permute-start(bf16[144,128]{1,0:T(8,128)(2,1)S(1)} %get-tuple-element.69), channel_id=1, source_target_pairs={{0,1},{1,0},{2,3},{3,2},{4,5},{5,4},{6,7},{7,6},{8,9},{9,8},{10,11... | collective-permute-start | bytes 110600 | tf_op jit(solution)/shard_map/ppermute | solution.py:426
  114.8 9.3 %collective-permute-start.8 = (bf16[144,128]{1,0:T(8,128)(2,1)S(1)}, bf16[144,128]{1,0:T(8,128)(2,1)S(1)}, u32[]{:S(2)}, u32[]{:S(2)}) collective-permute-start(bf16[144,128]{1,0:T(8,128)(2,1)S(1)} %get-tuple-element.70), channel_id=1, source_target_pairs={{0,2},{1,3},{2,0},{3,1},{4,6},{5,7},{6,4},{7,5},{8,10},{9,11},{10,... | collective-permute-start | bytes 110600 | tf_op jit(solution)/shard_map/ppermute | solution.py:426
  118.6 5.5 %collective-permute-start.9 = (bf16[144,128]{1,0:T(8,128)(2,1)S(1)}, bf16[144,128]{1,0:T(8,128)(2,1)S(1)}, u32[]{:S(2)}, u32[]{:S(2)}) collective-permute-start(bf16[144,128]{1,0:T(8,128)(2,1)S(1)} %get-tuple-element.71), channel_id=1, source_target_pairs={{0,3},{1,2},{2,1},{3,0},{4,7},{5,6},{6,5},{7,4},{8,11},{9,10},{10,... | collective-permute-start | bytes 110600 | tf_op jit(solution)/shard_map/ppermute | solution.py:426
  124.2 7.3 %collective-permute-start.14 = (bf16[336,128]{1,0:T(8,128)(2,1)S(1)}, bf16[336,128]{1,0:T(8,128)(2,1)S(1)}, u32[]{:S(2)}, u32[]{:S(2)}) collective-permute-start(bf16[336,128]{1,0:T(8,128)(2,1)S(1)} %shard_map.117.refs_0_), channel_id=1, source_target_pairs={{0,8},{8,16},{16,24},{24,0},{1,9},{9,17},{17,25},{25,1},{2,10},{10... | collective-permute-start | bytes 258056 | tf_op jit(solution)/shard_map/ppermute | solution.py:431
  124.3 12.6 %collective-permute-start.15 = (bf16[336,128]{1,0:T(8,128)(2,1)S(1)}, bf16[336,128]{1,0:T(8,128)(2,1)S(1)}, u32[]{:S(2)}, u32[]{:S(2)}) collective-permute-start(bf16[336,128]{1,0:T(8,128)(2,1)S(1)} %shard_map.117.refs_0_), channel_id=1, source_target_pairs={{0,16},{8,24},{16,0},{24,8},{1,17},{9,25},{17,1},{25,9},{2,18},{10... | collective-permute-start | bytes 258056 | tf_op jit(solution)/shard_map/ppermute | solution.py:431
  128.3 8.6 %collective-permute-start.16 = (bf16[336,128]{1,0:T(8,128)(2,1)S(1)}, bf16[336,128]{1,0:T(8,128)(2,1)S(1)}, u32[]{:S(2)}, u32[]{:S(2)}) collective-permute-start(bf16[336,128]{1,0:T(8,128)(2,1)S(1)} %shard_map.117.refs_0_), channel_id=1, source_target_pairs={{0,24},{8,0},{16,8},{24,16},{1,25},{9,1},{17,9},{25,17},{2,26},{10... | collective-permute-start | bytes 258056 | tf_op jit(solution)/shard_map/ppermute | solution.py:431
  137.0 3.6 %collective-permute-start.17 = (bf16[336,128]{1,0:T(8,128)(2,1)S(1)}, bf16[336,128]{1,0:T(8,128)(2,1)S(1)}, u32[]{:S(2)}, u32[]{:S(2)}) collective-permute-start(bf16[336,128]{1,0:T(8,128)(2,1)S(1)} %shard_map.118.refs_1_), channel_id=1, source_target_pairs={{0,1},{1,0},{2,3},{3,2},{4,5},{5,4},{6,7},{7,6},{8,9},{9,8},{10,11... | collective-permute-start | bytes 258056 | tf_op jit(solution)/shard_map/ppermute | solution.py:426
  137.0 6.0 %collective-permute-start.18 = (bf16[336,128]{1,0:T(8,128)(2,1)S(1)}, bf16[336,128]{1,0:T(8,128)(2,1)S(1)}, u32[]{:S(2)}, u32[]{:S(2)}) collective-permute-start(bf16[336,128]{1,0:T(8,128)(2,1)S(1)} %shard_map.118.refs_1_), channel_id=1, source_target_pairs={{0,2},{1,3},{2,0},{3,1},{4,6},{5,7},{6,4},{7,5},{8,10},{9,11},{10,... | collective-permute-start | bytes 258056 | tf_op jit(solution)/shard_map/ppermute | solution.py:426
  138.6 5.1 %collective-permute-start.19 = (bf16[336,128]{1,0:T(8,128)(2,1)S(1)}, bf16[336,128]{1,0:T(8,128)(2,1)S(1)}, u32[]{:S(2)}, u32[]{:S(2)}) collective-permute-start(bf16[336,128]{1,0:T(8,128)(2,1)S(1)} %shard_map.118.refs_1_), channel_id=1, source_target_pairs={{0,3},{1,2},{2,1},{3,0},{4,7},{5,6},{6,5},{7,4},{8,11},{9,10},{10,... | collective-permute-start | bytes 258056 | tf_op jit(solution)/shard_map/ppermute | solution.py:426
  138.9 5.1 %collective-permute-start.20 = (bf16[336,128]{1,0:T(8,128)(2,1)S(1)}, bf16[336,128]{1,0:T(8,128)(2,1)S(1)}, u32[]{:S(2)}, u32[]{:S(2)}) collective-permute-start(bf16[336,128]{1,0:T(8,128)(2,1)S(1)} %shard_map.118.refs_1_), channel_id=1, source_target_pairs={{0,4},{1,5},{2,6},{3,7},{4,0},{5,1},{6,2},{7,3},{8,12},{9,13},{10,... | collective-permute-start | bytes 258056 | tf_op jit(solution)/shard_map/ppermute | solution.py:426
  140.4 8.5 %collective-permute-start.21 = (bf16[336,128]{1,0:T(8,128)(2,1)S(1)}, bf16[336,128]{1,0:T(8,128)(2,1)S(1)}, u32[]{:S(2)}, u32[]{:S(2)}) collective-permute-start(bf16[336,128]{1,0:T(8,128)(2,1)S(1)} %shard_map.118.refs_1_), channel_id=1, source_target_pairs={{0,5},{1,4},{2,7},{3,6},{4,1},{5,0},{6,3},{7,2},{8,13},{9,12},{10,... | collective-permute-start | bytes 258056 | tf_op jit(solution)/shard_map/ppermute | solution.py:426
  140.6 8.3 %collective-permute-start.22 = (bf16[336,128]{1,0:T(8,128)(2,1)S(1)}, bf16[336,128]{1,0:T(8,128)(2,1)S(1)}, u32[]{:S(2)}, u32[]{:S(2)}) collective-permute-start(bf16[336,128]{1,0:T(8,128)(2,1)S(1)} %shard_map.118.refs_1_), channel_id=1, source_target_pairs={{0,6},{1,7},{2,4},{3,5},{4,2},{5,3},{6,0},{7,1},{8,14},{9,15},{10,... | collective-permute-start | bytes 258056 | tf_op jit(solution)/shard_map/ppermute | solution.py:426
  143.0 5.9 %collective-permute-start.23 = (bf16[336,128]{1,0:T(8,128)(2,1)S(1)}, bf16[336,128]{1,0:T(8,128)(2,1)S(1)}, u32[]{:S(2)}, u32[]{:S(2)}) collective-permute-start(bf16[336,128]{1,0:T(8,128)(2,1)S(1)} %shard_map.118.refs_1_), channel_id=1, source_target_pairs={{0,7},{1,6},{2,5},{3,4},{4,3},{5,2},{6,1},{7,0},{8,15},{9,14},{10,... | collective-permute-start | bytes 258056 | tf_op jit(solution)/shard_map/ppermute | solution.py:426

commit v8 on v7

--- a/solution.py
+++ b/solution.py
@@ -170,14 +170,14 @@
 def fill_grads(rows_step, gs, got_ref, slope_ref):
     clear_ends(gs)
     for at in range(0, got_ref.shape[0], rows_step):
-        grads = got_ref[at : at + rows_step].astype(F32)
+        grads = got_ref[at : at + rows_step, 0].astype(F32)
         slopes = slope_ref[at : at + rows_step].astype(F32)
         put_rows(gs, at, (grads * slopes).astype(BF16))
 
 
 def spatial_wgrad_kernel(rows_step, scale, here_ref, got_ref, slope_ref, x_ref, *rest):
     pieces, (gs, total_ref) = rest[:-2], rest[-2:]
-    rows, cols, ch = got_ref.shape
+    rows, _, cols, ch = got_ref.shape
     wide = gs.shape[1]
     flat = rows_step * wide
     pad = jnp.zeros((rows_step, wide - cols, ch), F32)
@@ -201,7 +201,7 @@
     hand_out(here_ref, total_ref, pieces)
 
 
-def spatial_back_kernel(rows_step, w_ref, got_ref, slope_ref, back_ref, gs):
+def spatial_back_kernel(rows_step, w_ref, got_ref, slope_ref, back_ref, united_ref, gs):
     rows, cols, ch = back_ref.shape
     wide = gs.shape[1]
     weight = jnp.concatenate(
@@ -216,6 +216,7 @@
         y = mm(taps_up(gs, at, rows_step), weight)
         back = y[:, ch : 2 * ch] + roll_rows(y[:, :ch], -1) + roll_rows(y[:, 2 * ch :], 1)
         back_ref[at : at + rows_step] = back.astype(BF16).reshape(rows_step, wide, ch)[:, :cols]
+    united_ref[...] = got_ref[:, 1]
 
 
 def clear_halo(pad_ref, frames):
@@ -235,7 +236,7 @@
 
 def temporal_kernel(
     step_frames, dil_ref, key_ref, got_hbm, tw_ref, uw_ref,
-    grad_hbm, united_hbm, a0_hbm, cots_hbm, a1_hbm, feat_hbm, g1_hbm, g0_hbm,
+    send_hbm, a0_hbm, cots_hbm, a1_hbm, feat_hbm, g1_hbm, g0_hbm,
     a0, a1, feat, cots, g0, g1, slope0, slope1, grad_feat, united_ref, act_ref, cot_ref, grad_ref,
     sems, in_sems, out_sems,
 ):
@@ -249,7 +250,7 @@
         load.start()
     stores = [
         pltpu.make_async_copy(
-            grad_ref.at[pl.ds(at, step_frames)], grad_hbm.at[pl.ds(at, step_frames)], out_sems.at[n]
+            grad_ref.at[pl.ds(at, step_frames)], send_hbm.at[pl.ds(at, step_frames), 0], out_sems.at[n]
         )
         for n, at in enumerate(range(0, frames, step_frames))
     ]
@@ -266,7 +267,7 @@
                 (g0.at[inside], g0_hbm),
                 (a0.at[inside], a0_hbm),
                 (cots, cots_hbm),
-                (united_ref, united_hbm),
+                (united_ref, send_hbm.at[:, 1]),
             )
         )
     ]
@@ -395,26 +396,13 @@
     refs[-1][...] = sum(ref[...].astype(F32) for ref in refs[:-1]).astype(refs[-1].dtype)
 
 
-def join_kernel(first_ref, *refs):
-    out_ref = refs[-1]
-    split = first_ref.shape[0]
-    out_ref[:split] = first_ref[...]
-    out_ref[split:] = sum(ref[...].astype(F32) for ref in refs[:-1]).astype(out_ref.dtype)
-
-
-def deal_kernel(here_ref, *refs):
-    united_hbm, *pieces = refs[:-5]
-    *outs, united_out, sem = refs[-5:]
-    copy = pltpu.make_async_copy(united_hbm, united_out, sem.at[0])
-    copy.start()
+def deal_kernel(here_ref, time_ref, *refs):
+    pieces, (time_out, unite_out, space_out) = refs[:-3], refs[-3:]
+    split = time_out.shape[1]
+    time_out[...] = time_ref[:, :split].astype(F32)
+    unite_out[...] = time_ref[:, split:].astype(F32)
     for peer, piece in enumerate(pieces):
-        place = jnp.bitwise_xor(here_ref[1], peer)
-        at = 0
-        for out_ref in outs:
-            count = out_ref.shape[1]
-            out_ref[place] = piece[at : at + count].astype(F32)
-            at += count
-    copy.wait()
+        space_out[jnp.bitwise_xor(here_ref[1], peer)] = piece[...].astype(F32)
 
 
 def exchange(blocks):
@@ -497,9 +485,9 @@
 
     padded = (frames + 2 * HALO, high, ch)
     whole = (frames, high, ch)
-    grad_send, united_send, a0, cots, a1, feat, g1, g0 = call(
+    send, a0, cots, a1, feat, g1, g0 = call(
         functools.partial(temporal_kernel, step_frames),
-        [((frames, block, ch), BF16, HBM)] * 2 + [(whole, BF16, HBM)] * 6,
+        [((frames, 2, block, ch), BF16, HBM)] + [(whole, BF16, HBM)] * 6,
         [
             pltpu.VMEM(padded, BF16),
             pltpu.VMEM(padded, BF16),
@@ -525,7 +513,8 @@
             (temporal_weight, VMEM), (uniting_weight, VMEM),
         ],
     )
-    grad_time = exchange(grad_send).reshape(rows, cols, ch)
+    got = exchange(send).reshape(rows, split, 2, block, ch).swapaxes(1, 2)
+    got = got.reshape(rows, 2, cols, ch)
     time_pieces = call(
         functools.partial(temporal_wgrad_kernel, step_frames, scale),
         [((time_rows + unite_rows, ch), BF16, VMEM)] * peers,
@@ -546,49 +535,37 @@
             (a0, HBM), (g0, HBM), (a1, HBM), (g1, HBM), (feat, HBM), (cots, HBM),
         ],
     )
-    time_sum = reduce_in_grp(time_pieces)
-    time_sum, grad_time = lax.optimization_barrier((time_sum, grad_time))
-    united_send, grad_time = lax.optimization_barrier((united_send, grad_time))
-    united = exchange(united_send)
+    time_piece = sum_of(all_turns(reduce_in_grp(time_pieces)))
+    time_grads = lax.all_gather(time_piece, "grp", axis=0)
+    _, got = lax.optimization_barrier((time_piece, got))
     space_pieces = call(
         functools.partial(spatial_wgrad_kernel, rows_step, scale),
         [((space_rows, ch), BF16, VMEM)] * peers,
         [pltpu.VMEM((rows + 2, wide, ch), BF16), pltpu.VMEM((peers, space_rows, ch), F32)],
         2 * 9 * pixels * ch * ch,
         pixels * ch * 8,
-        [(here, SMEM), (grad_time, VMEM), (space_slope, VMEM), (frame, VMEM)],
+        [(here, SMEM), (got, VMEM), (space_slope, VMEM), (frame, VMEM)],
         MID_VMEM,
     )
-    (back,) = call(
+    back, united = call(
         functools.partial(spatial_back_kernel, rows_step),
-        [((rows, cols, ch), BF16, VMEM)],
+        [((rows, cols, ch), BF16, VMEM)] * 2,
         [pltpu.VMEM((rows + 2, wide, ch), BF16)],
         2 * 9 * pixels * ch * ch,
-        pixels * ch * 6,
-        [(spatial_weight, VMEM), (grad_time, VMEM), (space_slope, VMEM)],
+        pixels * ch * 10,
+        [(spatial_weight, VMEM), (got, VMEM), (space_slope, VMEM)],
         MID_VMEM,
     )
     space_pieces = list(space_pieces)
     space_pieces[0], back = lax.optimization_barrier((space_pieces[0], back))
-    space_parts = [flip(part, peer) if peer else part for peer, part in enumerate(space_pieces)]
-    (plane,) = call(
-        join_kernel,
-        [((time_rows + unite_rows + space_rows, ch), BF16, VMEM)],
+    piece = sum_of(all_turns(reduce_in_grp(space_pieces)))
+    grads = call(
+        deal_kernel,
+        [((peers, count, ch), F32, VMEM) for count in (time_rows, unite_rows, space_rows)],
         [],
         0,
-        2 * (peers + 10) * space_rows * ch,
-        [(time_sum, VMEM)] + [(part, VMEM) for part in space_parts],
-        SMALL_VMEM,
-    )
-    piece = sum_of(all_turns(plane))
-    *grads, united = call(
-        deal_kernel,
-        [((peers, count, ch), F32, VMEM) for count in (time_rows, unite_rows, space_rows)]
-        + [((frames, block, ch), BF16, HBM)],
-        [pltpu.SemaphoreType.DMA((1,))],
-        0,
         6 * 21 * ch * ch,
-        [(here, SMEM), (united, HBM)]
+        [(here, SMEM), (time_grads, VMEM)]
         + [(flip(piece, peer) if peer else piece, VMEM) for peer in range(peers)],
         SMALL_VMEM,
     )

time: 152 us -> 165 us (1.086)
  waiting for transfers between devices: 62.9 us -> 73.3 us
  blocking collectives: 0 us -> 9.03 us
  starting transfers between devices: 43 us -> 38.8 us
  Pallas kernels: 40.8 us -> 39.1 us
    ppermute x3 -> x6, waiting for transfers between devices: 7.61 us -> 22.6 us  [turn_by(): lax.ppermute(value, 'seg', [(i, (i + turn) % size) for i in range(size)])]
    all_gather x0 -> x1, blocking collectives: none -> 9.03 us  [local(): time_grads = lax.all_gather(time_piece, 'grp', axis=0)]
    all_to_all x3 -> x2, starting transfers between devices: 15.3 us -> 11.7 us  [exchange(): return lax.all_to_all(blocks, AXES, split_axis=0, concat_axis=0, tiled=True)]
    ppermute x21, starting transfers between devices: 22.7 us -> 19.4 us  [flip(): return lax.ppermute(value, 'grp', [(i, i ^ peer) for i in range(size)])]
    ppermute x3 -> x6, starting transfers between devices: 5.07 us -> 7.75 us  [turn_by(): lax.ppermute(value, 'seg', [(i, (i + turn) % size) for i in range(size)])]
    all_to_all x3 -> x2, waiting for transfers between devices: 44 us -> 41.4 us  [exchange(): return lax.all_to_all(blocks, AXES, split_axis=0, concat_axis=0, tiled=True)]
    ppermute x21, waiting for transfers between devices: 11.3 us -> 9.22 us  [flip(): return lax.ppermute(value, 'grp', [(i, i ^ peer) for i in range(size)])]
    pallas_call x10 -> x11, Pallas kernels: 40.8 us -> 39.1 us  [call(): pl.pallas_call(kernel, out_shape=[jax.ShapeDtypeStruct(shape, kind) for s...]
  transfers between devices with their start and end apart: 27 -> 29, of which waited for: 9 -> 13; matrix products, arithmetic and copies ran while one was open for 0% -> 0% of each run, Pallas kernels for 13% -> 11%
where the time goes in v8:
time: 165 us
  waiting for transfers between devices  73.3 us (44%)
  Pallas kernels  39.1 us (24%)
  starting transfers between devices  38.8 us (24%)
  blocking collectives  9.03 us (5%)
  local copies, waits for them, and re-layouts  3.31 us (2%)
    all_to_all x2, waiting for transfers between devices, exchange(): return lax.all_to_all(blocks, AXES, split_axis=0, concat_axis=0, tiled=True)  41.4 us
    pallas_call x11, Pallas kernels, call(): pl.pallas_call(kernel, out_shape=[jax.ShapeDtypeStruct(shape, kind) for s...  39.1 us
    ppermute x6, waiting for transfers between devices, turn_by(): lax.ppermute(value, 'seg', [(i, (i + turn) % size) for i in range(size)])  22.6 us
    ppermute x21, starting transfers between devices, flip(): return lax.ppermute(value, 'grp', [(i, i ^ peer) for i in range(size)])  19.4 us
    all_to_all x2, starting transfers between devices, exchange(): return lax.all_to_all(blocks, AXES, split_axis=0, concat_axis=0, tiled=True)  11.7 us
    ppermute x21, waiting for transfers between devices, flip(): return lax.ppermute(value, 'grp', [(i, i ^ peer) for i in range(size)])  9.22 us
    all_gather x1, blocking collectives, local(): time_grads = lax.all_gather(time_piece, 'grp', axis=0)  9.03 us
    ppermute x6, starting transfers between devices, turn_by(): lax.ppermute(value, 'seg', [(i, (i + turn) % size) for i in range(size)])  7.75 us
  transfers between devices with their start and end apart: 29, of which 13 were waited for; matrix products, arithmetic and copies ran while one was open for 0% of the time, Pallas kernels for 11%

profile of v8, /device:TPU:0, one launch (start us, length us, event | category | flops | bytes accessed | tf_op | source)
XLA Modules:
  0.0 164.9 jit_solution(9144068547555365089)
XLA Ops:
  0.6 6.6 %shard_map.110 = bf16[32,2,120,128]{3,2,1,0:T(8,128)(2,1)} custom-call(bf16[32,120,128]{2,1,0:T(8,128)(2,1)} %bitcast.11, bf16[9,128,128]{2,1,0:T(8,128)(2,1)} %w_ref.5, bf16[32,120,128]{2,1,0:T(8,128)(2,1)} %bitcast.14), custom_call_target="tpu_custom_call" | custom-call | flops 1132462080 | bytes 3932160 | tf_op jit(solution)/shard_map/pallas_call | solution.py:57
  7.2 7.5 %all-to-all-start = ((bf16[32,2,120,128]{3,2,1,0:T(8,128)(2,1)}), bf16[32,2,120,128]{3,2,1,0:T(8,128)(2,1)S(1)}, u32[]{:S(2)}, u32[]{:S(2)}) async-start(bf16[32,2,120,128]{3,2,1,0:T(8,128)(2,1)} %shard_map.110), calls=%async_computation | async-start | bytes 3932160 | tf_op jit(solution)/shard_map/all_to_all | solution.py:409
  14.7 4.5 %shard_map.111.slope_ref = bf16[32,120,128]{2,1,0:T(8,128)(2,1)} custom-call(bf16[32,120,128]{2,1,0:T(8,128)(2,1)} %bitcast.12, bf16[9,128,128]{2,1,0:T(8,128)(2,1)} %w_ref.5), custom_call_target="tpu_custom_call" | custom-call | flops 1132462080 | bytes 1966080 | tf_op jit(solution)/shard_map/pallas_call | solution.py:57
  19.2 41.4 %all-to-all-done.got_hbm = bf16[32,2,120,128]{3,2,1,0:T(8,128)(2,1)S(1)} async-done(((bf16[32,2,120,128]{3,2,1,0:T(8,128)(2,1)}), bf16[32,2,120,128]{3,2,1,0:T(8,128)(2,1)S(1)}, u32[]{:S(2)}, u32[]{:S(2)}) %all-to-all-start) | async-done | bytes 1966112 | tf_op jit(solution)/shard_map/all_to_all | solution.py:409
  60.6 1.3 copy-done.5
  61.9 10.6 %shard_map.112 = (bf16[32,2,120,128]{3,2,1,0:T(8,128)(2,1)}, bf16[32,128,128]{2,1,0:T(8,128)(2,1)}, bf16[32,128,128]{2,1,0:T(8,128)(2,1)}, bf16[32,128,128]{2,1,...) custom-call(s32[2]{0:T(128)} %dil_ref.3, s32[4]{0:T(128)} %key_ref.3, ...), custom_call_target="tpu_custom_call" | custom-call | flops 2768240640 | bytes 8847360 | tf_op jit(solution)/shard_map/pallas_call | solution.py:57
  72.5 4.2 %all-to-all-start.1 = ((bf16[32,2,120,128]{3,2,1,0:T(8,128)(2,1)}), bf16[32,2,120,128]{3,2,1,0:T(8,128)(2,1)S(1)}, u32[]{:S(2)}, u32[]{:S(2)}) async-start(bf16[32,2,120,128]{3,2,1,0:T(8,128)(2,1)} %get-tuple-element.57), calls=%async_computation.1 | async-start | bytes 3932160 | tf_op jit(solution)/shard_map/all_to_all | solution.py:409
  76.7 0.6 pad_add_fusion.here_ref
  77.2 9.4 %shard_map.113 = (bf16[192,128]{1,0:T(8,128)(2,1)}, bf16[192,128]{1,0:T(8,128)(2,1)}, bf16[192,128]{1,0:T(8,128)(2,1)}, bf16[192,128]{1,0:T(8,128)(2,1)}, bf16[1...) custom-call(s32[2]{0:T(128)} %pad_add_fusion.here_ref, ...), custom_call_target="tpu_custom_call" | custom-call | flops 1509949440 | bytes 6881280 | tf_op jit(solution)/shard_map/pallas_call | solution.py:57
  86.8 1.7 %collective-permute-start.1 = (bf16[192,128]{1,0:T(8,128)(2,1)}, bf16[192,128]{1,0:T(8,128)(2,1)S(1)}, u32[]{:S(2)}, u32[]{:S(2)}) collective-permute-start(bf16[192,128]{1,0:T(8,128)(2,1)} %get-tuple-element.51), channel_id=1, source_target_pairs={{0,2},{1,3},{2,0},{3,1},{4,6},{5,7},{6,4},{7,5},{8,10},{9,11},{10,... | collective-permute-start | bytes 147464 | tf_op jit(solution)/shard_map/ppermute | solution.py:414
  88.5 0.2 collective-permute-start.2
  88.6 1.5 collective-permute-start.3
  90.3 2.5 %collective-permute-start.5 = (bf16[192,128]{1,0:T(8,128)(2,1)}, bf16[192,128]{1,0:T(8,128)(2,1)S(1)}, u32[]{:S(2)}, u32[]{:S(2)}) collective-permute-start(bf16[192,128]{1,0:T(8,128)(2,1)} %get-tuple-element.55), channel_id=1, source_target_pairs={{0,6},{1,7},{2,4},{3,5},{4,2},{5,3},{6,0},{7,1},{8,14},{9,15},{10,... | collective-permute-start | bytes 147464 | tf_op jit(solution)/shard_map/ppermute | solution.py:414
  92.9 0.6 collective-permute-start.6
  93.5 0.6 collective-permute-done.2.refs_3_
  94.1 1.6 collective-permute-done.3.refs_4_
  95.7 2.1 %collective-permute-done.4.refs_5_ = bf16[192,128]{1,0:T(8,128)(2,1)S(1)} collective-permute-done((bf16[192,128]{1,0:T(8,128)(2,1)}, bf16[192,128]{1,0:T(8,128)(2,1)S(1)}, u32[]{:S(2)}, u32[]{:S(2)}) %collective-permute-start.4) | collective-permute-done | bytes 49184 | tf_op jit(solution)/shard_map/ppermute | solution.py:414
  97.9 2.3 %collective-permute-done.5.refs_6_ = bf16[192,128]{1,0:T(8,128)(2,1)S(1)} collective-permute-done((bf16[192,128]{1,0:T(8,128)(2,1)}, bf16[192,128]{1,0:T(8,128)(2,1)S(1)}, u32[]{:S(2)}, u32[]{:S(2)}) %collective-permute-start.5) | collective-permute-done | bytes 49184 | tf_op jit(solution)/shard_map/ppermute | solution.py:414
  100.2 2.2 %collective-permute-done.6.refs_7_ = bf16[192,128]{1,0:T(8,128)(2,1)S(1)} collective-permute-done((bf16[192,128]{1,0:T(8,128)(2,1)}, bf16[192,128]{1,0:T(8,128)(2,1)S(1)}, u32[]{:S(2)}, u32[]{:S(2)}) %collective-permute-start.6) | collective-permute-done | bytes 49184 | tf_op jit(solution)/shard_map/ppermute | solution.py:414
  102.3 0.8 copy-done.2
  103.3 3.2 %collective-permute-start.8 = (bf16[192,128]{1,0:T(8,128)(2,1)S(1)}, bf16[192,128]{1,0:T(8,128)(2,1)S(1)}, u32[]{:S(2)}, u32[]{:S(2)}) collective-permute-start(bf16[192,128]{1,0:T(8,128)(2,1)S(1)} %shard_map.114.refs_0_), channel_id=1, source_target_pairs={{0,16},{8,24},{16,0},{24,8},{1,17},{9,25},{17,1},{25,9},{2,18},{10... | collective-permute-start | bytes 147464 | tf_op jit(solution)/shard_map/ppermute | solution.py:419
  106.5 0.6 collective-permute-start.9
  107.1 7.3 %collective-permute-done.7.refs_1_ = bf16[192,128]{1,0:T(8,128)(2,1)S(1)} collective-permute-done((bf16[192,128]{1,0:T(8,128)(2,1)S(1)}, bf16[192,128]{1,0:T(8,128)(2,1)S(1)}, u32[]{:S(2)}, u32[]{:S(2)}) %collective-permute-start.7) | collective-permute-done | bytes 49184 | tf_op jit(solution)/shard_map/ppermute | solution.py:419
  114.3 11.9 %collective-permute-done.8.refs_2_ = bf16[192,128]{1,0:T(8,128)(2,1)S(1)} collective-permute-done((bf16[192,128]{1,0:T(8,128)(2,1)S(1)}, bf16[192,128]{1,0:T(8,128)(2,1)S(1)}, u32[]{:S(2)}, u32[]{:S(2)}) %collective-permute-start.8) | collective-permute-done | bytes 49184 | tf_op jit(solution)/shard_map/ppermute | solution.py:419
  126.3 1.2 copy-done.4
  127.5 2.6 %shard_map.117 = (bf16[144,128]{1,0:T(8,128)(2,1)S(1)}, bf16[144,128]{1,0:T(8,128)(2,1)S(1)}, bf16[144,128]{1,0:T(8,128)(2,1)S(1)}, bf16[144,128]{1,0:T(8,128)(2...) custom-call(s32[2]{0:T(128)S(1)} %copy-done.3, ...), custom_call_target="tpu_custom_call" | custom-call | flops 1132462080 | bytes 3932160 | tf_op jit(solution)/shard_map/pallas_call | solution.py:57
  130.3 1.4 collective-permute-start.11
  131.6 0.5 collective-permute-start.12
  132.1 1.2 collective-permute-start.13
  133.4 0.5 collective-permute-start.14
  133.8 2.2 %collective-permute-start.15 = (bf16[144,128]{1,0:T(8,128)(2,1)S(1)}, bf16[144,128]{1,0:T(8,128)(2,1)S(1)}, u32[]{:S(2)}, u32[]{:S(2)}) collective-permute-start(bf16[144,128]{1,0:T(8,128)(2,1)S(1)} %get-tuple-element.70), channel_id=1, source_target_pairs={{0,6},{1,7},{2,4},{3,5},{4,2},{5,3},{6,0},{7,1},{8,14},{9,15},{10,... | collective-permute-start | bytes 110600 | tf_op jit(solution)/shard_map/ppermute | solution.py:414
  136.0 0.5 collective-permute-start.16
  136.5 3.6 %shard_map.116 = (bf16[32,120,128]{2,1,0:T(8,128)(2,1)}, bf16[32,120,128]{2,1,0:T(8,128)(2,1)}) custom-call(bf16[9,128,128]{2,1,0:T(8,128)(2,1)S(1)} %copy-done.1, bf16[32,2,120,128]{3,2,1,0:T(8,128)(2,1)S(1)} %all-to-all-done.1.got_ref, bf16[32,120,128]{2,1,0:T(8,128)(2,1)S(1)} %copy-done.4), custom_call_target="tpu_custom_call" | custom-call | flops 1132462080 | bytes 4915200 | tf_op jit(solution)/shard_map/pallas_call | solution.py:57
  140.1 0.3 collective-permute-done.16.refs_7_
  140.4 1.2 collective-permute-start.17
  141.6 2.0 %collective-permute-start.18 = (bf16[144,128]{1,0:T(8,128)(2,1)S(1)}, bf16[144,128]{1,0:T(8,128)(2,1)S(1)}, u32[]{:S(2)}, u32[]{:S(2)}) collective-permute-start(bf16[144,128]{1,0:T(8,128)(2,1)S(1)} %shard_map.118.refs_0_), channel_id=1, source_target_pairs={{0,16},{8,24},{16,0},{24,8},{1,17},{9,25},{17,1},{25,9},{2,18},{10... | collective-permute-start | bytes 110600 | tf_op jit(solution)/shard_map/ppermute | solution.py:419
  143.6 0.7 collective-permute-start.19
  144.3 2.2 %collective-permute-done.17.refs_1_ = bf16[144,128]{1,0:T(8,128)(2,1)S(1)} collective-permute-done((bf16[144,128]{1,0:T(8,128)(2,1)S(1)}, bf16[144,128]{1,0:T(8,128)(2,1)S(1)}, u32[]{:S(2)}, u32[]{:S(2)}) %collective-permute-start.17) | collective-permute-done | bytes 36896 | tf_op jit(solution)/shard_map/ppermute | solution.py:419
  146.5 1.0 collective-permute-done.18.refs_2_
  147.5 0.3 collective-permute-done.19.refs_3_
  147.9 1.0 collective-permute-start.21
  148.9 0.8 collective-permute-start.22
  149.7 1.0 collective-permute-start.23
  150.7 0.7 collective-permute-start.24
  151.4 2.0 %collective-permute-start.25 = (bf16[144,128]{1,0:T(8,128)(2,1)S(1)}, bf16[144,128]{1,0:T(8,128)(2,1)S(1)}, u32[]{:S(2)}, u32[]{:S(2)}) collective-permute-start(bf16[144,128]{1,0:T(8,128)(2,1)S(1)} %shard_map.119.refs_0_), channel_id=1, source_target_pairs={{0,6},{1,7},{2,4},{3,5},{4,2},{5,3},{6,0},{7,1},{8,14},{9,15},{10,... | collective-permute-start | bytes 110600 | tf_op jit(solution)/shard_map/ppermute | solution.py:414
  153.5 0.7 collective-permute-start.26
  154.1 9.0 %all-gather = bf16[1536,128]{1,0:T(8,128)(2,1)S(1)} all-gather(bf16[192,128]{1,0:T(8,128)(2,1)S(1)} %shard_map.115), channel_id=2, replica_groups=mesh['seg'=4,'grp'=8] {'grp'}, dimensions={0}, use_global_device_ids=true | all-gather | bytes 442368 | tf_op jit(solution)/shard_map/all_gather | solution.py:539
  163.2 1.7 %shard_map.120 = (f32[8,160,128]{2,1,0:T(8,128)}, f32[8,32,128]{2,1,0:T(8,128)}, f32[8,144,128]{2,1,0:T(8,128)}) custom-call(s32[2]{0:T(128)S(1)} %copy-done.3, bf16[8,192,128]{2,1,0:T(8,128)(2,1)S(1)} %bitcast.10, bf16[144,128]{1,0:T(8,128)(2,1)S(1)} %shard_map.119.refs_0_, bf16[144,128]{1,0:T(8,128)(2,1)S(1)} %collective-permute-done.20.refs_1_, ...), custom_call_target="tpu_custom_call" | custom-call | bytes 2064384 | tf_op jit(solution)/shard_map/pallas_call | solution.py:57
  (35 shorter events, 0.7 us)
Async XLA Ops:
  7.2 53.4 %all-to-all-start = ((bf16[32,2,120,128]{3,2,1,0:T(8,128)(2,1)}), bf16[32,2,120,128]{3,2,1,0:T(8,128)(2,1)S(1)}, u32[]{:S(2)}, u32[]{:S(2)}) async-start(bf16[32,2,120,128]{3,2,1,0:T(8,128)(2,1)} %shard_map.110), calls=%async_computation | async-start | bytes 3932160 | tf_op jit(solution)/shard_map/all_to_all | solution.py:409
  60.6 1.3 copy-start.5
  72.5 53.8 %all-to-all-start.1 = ((bf16[32,2,120,128]{3,2,1,0:T(8,128)(2,1)}), bf16[32,2,120,128]{3,2,1,0:T(8,128)(2,1)S(1)}, u32[]{:S(2)}, u32[]{:S(2)}) async-start(bf16[32,2,120,128]{3,2,1,0:T(8,128)(2,1)} %get-tuple-element.57), calls=%async_computation.1 | async-start | bytes 3932160 | tf_op jit(solution)/shard_map/all_to_all | solution.py:409
  77.2 49.1 %copy-start = (bf16[1,32,120,128]{3,2,1,0:T(8,128)(2,1)S(1)}, bf16[1,32,120,128]{3,2,1,0:T(8,128)(2,1)}, u32[]{:S(2)}) copy-start(bf16[1,32,120,128]{3,2,1,0:T(8,128)(2,1)} %param.7) | copy-start | bytes 2949124
  77.2 49.1 %copy-start.3 = (s32[2]{0:T(128)S(1)}, s32[2]{0:T(128)}, u32[]{:S(2)}) copy-start(s32[2]{0:T(128)} %pad_add_fusion.here_ref) | copy-start | bytes 28
  86.7 3.6 %collective-permute-start = (bf16[192,128]{1,0:T(8,128)(2,1)}, bf16[192,128]{1,0:T(8,128)(2,1)S(1)}, u32[]{:S(2)}, u32[]{:S(2)}) collective-permute-start(bf16[192,128]{1,0:T(8,128)(2,1)} %get-tuple-element.50), channel_id=1, source_target_pairs={{0,1},{1,0},{2,3},{3,2},{4,5},{5,4},{6,7},{7,6},{8,9},{9,8},{10,11... | collective-permute-start | bytes 147464 | tf_op jit(solution)/shard_map/ppermute | solution.py:414
  86.8 6.1 %collective-permute-start.1 = (bf16[192,128]{1,0:T(8,128)(2,1)}, bf16[192,128]{1,0:T(8,128)(2,1)S(1)}, u32[]{:S(2)}, u32[]{:S(2)}) collective-permute-start(bf16[192,128]{1,0:T(8,128)(2,1)} %get-tuple-element.51), channel_id=1, source_target_pairs={{0,2},{1,3},{2,0},{3,1},{4,6},{5,7},{6,4},{7,5},{8,10},{9,11},{10,... | collective-permute-start | bytes 147464 | tf_op jit(solution)/shard_map/ppermute | solution.py:414
  88.5 5.6 %collective-permute-start.2 = (bf16[192,128]{1,0:T(8,128)(2,1)}, bf16[192,128]{1,0:T(8,128)(2,1)S(1)}, u32[]{:S(2)}, u32[]{:S(2)}) collective-permute-start(bf16[192,128]{1,0:T(8,128)(2,1)} %get-tuple-element.52), channel_id=1, source_target_pairs={{0,3},{1,2},{2,1},{3,0},{4,7},{5,6},{6,5},{7,4},{8,11},{9,10},{10,... | collective-permute-start | bytes 147464 | tf_op jit(solution)/shard_map/ppermute | solution.py:414
  88.6 7.1 %collective-permute-start.3 = (bf16[192,128]{1,0:T(8,128)(2,1)}, bf16[192,128]{1,0:T(8,128)(2,1)S(1)}, u32[]{:S(2)}, u32[]{:S(2)}) collective-permute-start(bf16[192,128]{1,0:T(8,128)(2,1)} %get-tuple-element.53), channel_id=1, source_target_pairs={{0,4},{1,5},{2,6},{3,7},{4,0},{5,1},{6,2},{7,3},{8,12},{9,13},{10,... | collective-permute-start | bytes 147464 | tf_op jit(solution)/shard_map/ppermute | solution.py:414
  90.2 7.7 %collective-permute-start.4 = (bf16[192,128]{1,0:T(8,128)(2,1)}, bf16[192,128]{1,0:T(8,128)(2,1)S(1)}, u32[]{:S(2)}, u32[]{:S(2)}) collective-permute-start(bf16[192,128]{1,0:T(8,128)(2,1)} %get-tuple-element.54), channel_id=1, source_target_pairs={{0,5},{1,4},{2,7},{3,6},{4,1},{5,0},{6,3},{7,2},{8,13},{9,12},{10,... | collective-permute-start | bytes 147464 | tf_op jit(solution)/shard_map/ppermute | solution.py:414
  90.3 9.9 %collective-permute-start.5 = (bf16[192,128]{1,0:T(8,128)(2,1)}, bf16[192,128]{1,0:T(8,128)(2,1)S(1)}, u32[]{:S(2)}, u32[]{:S(2)}) collective-permute-start(bf16[192,128]{1,0:T(8,128)(2,1)} %get-tuple-element.55), channel_id=1, source_target_pairs={{0,6},{1,7},{2,4},{3,5},{4,2},{5,3},{6,0},{7,1},{8,14},{9,15},{10,... | collective-permute-start | bytes 147464 | tf_op jit(solution)/shard_map/ppermute | solution.py:414
  92.9 9.4 %collective-permute-start.6 = (bf16[192,128]{1,0:T(8,128)(2,1)}, bf16[192,128]{1,0:T(8,128)(2,1)S(1)}, u32[]{:S(2)}, u32[]{:S(2)}) collective-permute-start(bf16[192,128]{1,0:T(8,128)(2,1)} %get-tuple-element.56), channel_id=1, source_target_pairs={{0,7},{1,6},{2,5},{3,4},{4,3},{5,2},{6,1},{7,0},{8,15},{9,14},{10,... | collective-permute-start | bytes 147464 | tf_op jit(solution)/shard_map/ppermute | solution.py:414
  102.3 0.8 copy-start.2
  103.2 11.1 %collective-permute-start.7 = (bf16[192,128]{1,0:T(8,128)(2,1)S(1)}, bf16[192,128]{1,0:T(8,128)(2,1)S(1)}, u32[]{:S(2)}, u32[]{:S(2)}) collective-permute-start(bf16[192,128]{1,0:T(8,128)(2,1)S(1)} %shard_map.114.refs_0_), channel_id=1, source_target_pairs={{0,8},{8,16},{16,24},{24,0},{1,9},{9,17},{17,25},{25,1},{2,10},{10... | collective-permute-start | bytes 147464 | tf_op jit(solution)/shard_map/ppermute | solution.py:419
  103.3 23.0 %collective-permute-start.8 = (bf16[192,128]{1,0:T(8,128)(2,1)S(1)}, bf16[192,128]{1,0:T(8,128)(2,1)S(1)}, u32[]{:S(2)}, u32[]{:S(2)}) collective-permute-start(bf16[192,128]{1,0:T(8,128)(2,1)S(1)} %shard_map.114.refs_0_), channel_id=1, source_target_pairs={{0,16},{8,24},{16,0},{24,8},{1,17},{9,25},{17,1},{25,9},{2,18},{10... | collective-permute-start | bytes 147464 | tf_op jit(solution)/shard_map/ppermute | solution.py:419
  106.5 19.7 %collective-permute-start.9 = (bf16[192,128]{1,0:T(8,128)(2,1)S(1)}, bf16[192,128]{1,0:T(8,128)(2,1)S(1)}, u32[]{:S(2)}, u32[]{:S(2)}) collective-permute-start(bf16[192,128]{1,0:T(8,128)(2,1)S(1)} %shard_map.114.refs_0_), channel_id=1, source_target_pairs={{0,24},{8,0},{16,8},{24,16},{1,25},{9,1},{17,9},{25,17},{2,26},{10... | collective-permute-start | bytes 147464 | tf_op jit(solution)/shard_map/ppermute | solution.py:419
  126.3 10.3 %copy-start.1 = (bf16[9,128,128]{2,1,0:T(8,128)(2,1)S(1)}, bf16[9,128,128]{2,1,0:T(8,128)(2,1)}, u32[]{:S(2)}) copy-start(bf16[9,128,128]{2,1,0:T(8,128)(2,1)} %w_ref.5) | copy-start | bytes 884740
  126.3 1.2 copy-start.4
  130.2 3.6 %collective-permute-start.10 = (bf16[144,128]{1,0:T(8,128)(2,1)S(1)}, bf16[144,128]{1,0:T(8,128)(2,1)S(1)}, u32[]{:S(2)}, u32[]{:S(2)}) collective-permute-start(bf16[144,128]{1,0:T(8,128)(2,1)S(1)} %get-tuple-element.65), channel_id=1, source_target_pairs={{0,1},{1,0},{2,3},{3,2},{4,5},{5,4},{6,7},{7,6},{8,9},{9,8},{10,11... | collective-permute-start | bytes 110600 | tf_op jit(solution)/shard_map/ppermute | solution.py:414
  130.3 5.8 %collective-permute-start.11 = (bf16[144,128]{1,0:T(8,128)(2,1)S(1)}, bf16[144,128]{1,0:T(8,128)(2,1)S(1)}, u32[]{:S(2)}, u32[]{:S(2)}) collective-permute-start(bf16[144,128]{1,0:T(8,128)(2,1)S(1)} %get-tuple-element.66), channel_id=1, source_target_pairs={{0,2},{1,3},{2,0},{3,1},{4,6},{5,7},{6,4},{7,5},{8,10},{9,11},{10,... | collective-permute-start | bytes 110600 | tf_op jit(solution)/shard_map/ppermute | solution.py:414
  131.6 8.5 %collective-permute-start.12 = (bf16[144,128]{1,0:T(8,128)(2,1)S(1)}, bf16[144,128]{1,0:T(8,128)(2,1)S(1)}, u32[]{:S(2)}, u32[]{:S(2)}) collective-permute-start(bf16[144,128]{1,0:T(8,128)(2,1)S(1)} %get-tuple-element.67), channel_id=1, source_target_pairs={{0,3},{1,2},{2,1},{3,0},{4,7},{5,6},{6,5},{7,4},{8,11},{9,10},{10,... | collective-permute-start | bytes 110600 | tf_op jit(solution)/shard_map/ppermute | solution.py:414
  132.1 8.0 %collective-permute-start.13 = (bf16[144,128]{1,0:T(8,128)(2,1)S(1)}, bf16[144,128]{1,0:T(8,128)(2,1)S(1)}, u32[]{:S(2)}, u32[]{:S(2)}) collective-permute-start(bf16[144,128]{1,0:T(8,128)(2,1)S(1)} %get-tuple-element.68), channel_id=1, source_target_pairs={{0,4},{1,5},{2,6},{3,7},{4,0},{5,1},{6,2},{7,3},{8,12},{9,13},{10,... | collective-permute-start | bytes 110600 | tf_op jit(solution)/shard_map/ppermute | solution.py:414
  133.4 6.7 %collective-permute-start.14 = (bf16[144,128]{1,0:T(8,128)(2,1)S(1)}, bf16[144,128]{1,0:T(8,128)(2,1)S(1)}, u32[]{:S(2)}, u32[]{:S(2)}) collective-permute-start(bf16[144,128]{1,0:T(8,128)(2,1)S(1)} %get-tuple-element.69), channel_id=1, source_target_pairs={{0,5},{1,4},{2,7},{3,6},{4,1},{5,0},{6,3},{7,2},{8,13},{9,12},{10,... | collective-permute-start | bytes 110600 | tf_op jit(solution)/shard_map/ppermute | solution.py:414
  133.8 6.3 %collective-permute-start.15 = (bf16[144,128]{1,0:T(8,128)(2,1)S(1)}, bf16[144,128]{1,0:T(8,128)(2,1)S(1)}, u32[]{:S(2)}, u32[]{:S(2)}) collective-permute-start(bf16[144,128]{1,0:T(8,128)(2,1)S(1)} %get-tuple-element.70), channel_id=1, source_target_pairs={{0,6},{1,7},{2,4},{3,5},{4,2},{5,3},{6,0},{7,1},{8,14},{9,15},{10,... | collective-permute-start | bytes 110600 | tf_op jit(solution)/shard_map/ppermute | solution.py:414
  136.0 4.3 %collective-permute-start.16 = (bf16[144,128]{1,0:T(8,128)(2,1)S(1)}, bf16[144,128]{1,0:T(8,128)(2,1)S(1)}, u32[]{:S(2)}, u32[]{:S(2)}) collective-permute-start(bf16[144,128]{1,0:T(8,128)(2,1)S(1)} %get-tuple-element.71), channel_id=1, source_target_pairs={{0,7},{1,6},{2,5},{3,4},{4,3},{5,2},{6,1},{7,0},{8,15},{9,14},{10,... | collective-permute-start | bytes 110600 | tf_op jit(solution)/shard_map/ppermute | solution.py:414
  140.4 6.0 %collective-permute-start.17 = (bf16[144,128]{1,0:T(8,128)(2,1)S(1)}, bf16[144,128]{1,0:T(8,128)(2,1)S(1)}, u32[]{:S(2)}, u32[]{:S(2)}) collective-permute-start(bf16[144,128]{1,0:T(8,128)(2,1)S(1)} %shard_map.118.refs_0_), channel_id=1, source_target_pairs={{0,8},{8,16},{16,24},{24,0},{1,9},{9,17},{17,25},{25,1},{2,10},{10... | collective-permute-start | bytes 110600 | tf_op jit(solution)/shard_map/ppermute | solution.py:419
  141.6 5.9 %collective-permute-start.18 = (bf16[144,128]{1,0:T(8,128)(2,1)S(1)}, bf16[144,128]{1,0:T(8,128)(2,1)S(1)}, u32[]{:S(2)}, u32[]{:S(2)}) collective-permute-start(bf16[144,128]{1,0:T(8,128)(2,1)S(1)} %shard_map.118.refs_0_), channel_id=1, source_target_pairs={{0,16},{8,24},{16,0},{24,8},{1,17},{9,25},{17,1},{25,9},{2,18},{10... | collective-permute-start | bytes 110600 | tf_op jit(solution)/shard_map/ppermute | solution.py:419
  143.6 4.1 %collective-permute-start.19 = (bf16[144,128]{1,0:T(8,128)(2,1)S(1)}, bf16[144,128]{1,0:T(8,128)(2,1)S(1)}, u32[]{:S(2)}, u32[]{:S(2)}) collective-permute-start(bf16[144,128]{1,0:T(8,128)(2,1)S(1)} %shard_map.118.refs_0_), channel_id=1, source_target_pairs={{0,24},{8,0},{16,8},{24,16},{1,25},{9,1},{17,9},{25,17},{2,26},{10... | collective-permute-start | bytes 110600 | tf_op jit(solution)/shard_map/ppermute | solution.py:419
  147.8 3.6 %collective-permute-start.20 = (bf16[144,128]{1,0:T(8,128)(2,1)S(1)}, bf16[144,128]{1,0:T(8,128)(2,1)S(1)}, u32[]{:S(2)}, u32[]{:S(2)}) collective-permute-start(bf16[144,128]{1,0:T(8,128)(2,1)S(1)} %shard_map.119.refs_0_), channel_id=1, source_target_pairs={{0,1},{1,0},{2,3},{3,2},{4,5},{5,4},{6,7},{7,6},{8,9},{9,8},{10,11... | collective-permute-start | bytes 110600 | tf_op jit(solution)/shard_map/ppermute | solution.py:414
  147.9 5.6 %collective-permute-start.21 = (bf16[144,128]{1,0:T(8,128)(2,1)S(1)}, bf16[144,128]{1,0:T(8,128)(2,1)S(1)}, u32[]{:S(2)}, u32[]{:S(2)}) collective-permute-start(bf16[144,128]{1,0:T(8,128)(2,1)S(1)} %shard_map.119.refs_0_), channel_id=1, source_target_pairs={{0,2},{1,3},{2,0},{3,1},{4,6},{5,7},{6,4},{7,5},{8,10},{9,11},{10,... | collective-permute-start | bytes 110600 | tf_op jit(solution)/shard_map/ppermute | solution.py:414
  148.9 14.3 %collective-permute-start.22 = (bf16[144,128]{1,0:T(8,128)(2,1)S(1)}, bf16[144,128]{1,0:T(8,128)(2,1)S(1)}, u32[]{:S(2)}, u32[]{:S(2)}) collective-permute-start(bf16[144,128]{1,0:T(8,128)(2,1)S(1)} %shard_map.119.refs_0_), channel_id=1, source_target_pairs={{0,3},{1,2},{2,1},{3,0},{4,7},{5,6},{6,5},{7,4},{8,11},{9,10},{10,... | collective-permute-start | bytes 110600 | tf_op jit(solution)/shard_map/ppermute | solution.py:414
  149.7 13.4 %collective-permute-start.23 = (bf16[144,128]{1,0:T(8,128)(2,1)S(1)}, bf16[144,128]{1,0:T(8,128)(2,1)S(1)}, u32[]{:S(2)}, u32[]{:S(2)}) collective-permute-start(bf16[144,128]{1,0:T(8,128)(2,1)S(1)} %shard_map.119.refs_0_), channel_id=1, source_target_pairs={{0,4},{1,5},{2,6},{3,7},{4,0},{5,1},{6,2},{7,3},{8,12},{9,13},{10,... | collective-permute-start | bytes 110600 | tf_op jit(solution)/shard_map/ppermute | solution.py:414
  150.7 12.5 %collective-permute-start.24 = (bf16[144,128]{1,0:T(8,128)(2,1)S(1)}, bf16[144,128]{1,0:T(8,128)(2,1)S(1)}, u32[]{:S(2)}, u32[]{:S(2)}) collective-permute-start(bf16[144,128]{1,0:T(8,128)(2,1)S(1)} %shard_map.119.refs_0_), channel_id=1, source_target_pairs={{0,5},{1,4},{2,7},{3,6},{4,1},{5,0},{6,3},{7,2},{8,13},{9,12},{10,... | collective-permute-start | bytes 110600 | tf_op jit(solution)/shard_map/ppermute | solution.py:414
  151.4 11.7 %collective-permute-start.25 = (bf16[144,128]{1,0:T(8,128)(2,1)S(1)}, bf16[144,128]{1,0:T(8,128)(2,1)S(1)}, u32[]{:S(2)}, u32[]{:S(2)}) collective-permute-start(bf16[144,128]{1,0:T(8,128)(2,1)S(1)} %shard_map.119.refs_0_), channel_id=1, source_target_pairs={{0,6},{1,7},{2,4},{3,5},{4,2},{5,3},{6,0},{7,1},{8,14},{9,15},{10,... | collective-permute-start | bytes 110600 | tf_op jit(solution)/shard_map/ppermute | solution.py:414
  153.5 9.7 %collective-permute-start.26 = (bf16[144,128]{1,0:T(8,128)(2,1)S(1)}, bf16[144,128]{1,0:T(8,128)(2,1)S(1)}, u32[]{:S(2)}, u32[]{:S(2)}) collective-permute-start(bf16[144,128]{1,0:T(8,128)(2,1)S(1)} %shard_map.119.refs_0_), channel_id=1, source_target_pairs={{0,7},{1,6},{2,5},{3,4},{4,3},{5,2},{6,1},{7,0},{8,15},{9,14},{10,... | collective-permute-start | bytes 110600 | tf_op jit(solution)/shard_map/ppermute | solution.py:414

commit v9 on v7

--- a/solution.py
+++ b/solution.py
@@ -98,7 +98,7 @@
 
 
 def spatial_fwd_kernel(
-    rows_step, x_hbm, w_ref, cot_hbm, send_hbm, x_in, xs, sends, in_sems, cot_sems, send_sems
+    rows_step, x_hbm, w_hbm, act_hbm, x_in, w_ref, xs, acts, in_sems, w_sem, out_sems
 ):
     rows, cols, ch = x_in.shape
     wide = xs.shape[1]
@@ -110,18 +110,15 @@
     loads = [
         pltpu.make_async_copy(x_hbm.at[part(n)], x_in.at[part(n)], in_sems.at[n]) for n in range(steps)
     ]
-    cot_loads = [
-        pltpu.make_async_copy(cot_hbm.at[part(n)], sends.at[part(n), 1], cot_sems.at[n])
+    stores = [
+        pltpu.make_async_copy(acts.at[part(n)], act_hbm.at[part(n)], out_sems.at[n])
         for n in range(steps)
     ]
-    stores = [
-        pltpu.make_async_copy(sends.at[part(n)], send_hbm.at[part(n)], send_sems.at[n])
-        for n in range(steps)
-    ]
-    for load in loads + cot_loads:
+    w_load = pltpu.make_async_copy(w_hbm, w_ref, w_sem.at[0])
+    w_load.start()
+    for load in loads:
         load.start()
     clear_ends(xs)
-    weight = forward_weight(w_ref)
 
     def bring(step):
         loads[step].wait()
@@ -129,13 +126,14 @@
         put_rows(xs, at, x_in[at : at + rows_step])
 
     bring(0)
+    w_load.wait()
+    weight = forward_weight(w_ref)
     for step in range(steps):
         if step + 1 < steps:
             bring(step + 1)
         at = step * rows_step
         act, _ = silu_parts(spatial_pre(xs, weight, at, rows_step))
-        sends[at : at + rows_step, 0] = act.astype(BF16).reshape(rows_step, wide, ch)[:, :cols]
-        cot_loads[step].wait()
+        acts[at : at + rows_step] = act.astype(BF16).reshape(rows_step, wide, ch)[:, :cols]
         stores[step].start()
     for store in stores:
         store.wait()
@@ -218,6 +216,10 @@
         back_ref[at : at + rows_step] = back.astype(BF16).reshape(rows_step, wide, ch)[:, :cols]
 
 
+def place_of(here_ref, turns, peers, turn, peer):
+    return lax.rem(here_ref[0] + (turns - turn), turns) * peers + jnp.bitwise_xor(here_ref[1], peer)
+
+
 def clear_halo(pad_ref, frames):
     zeros = jnp.zeros((HALO,) + pad_ref.shape[1:], pad_ref.dtype)
     pad_ref[:HALO] = zeros
@@ -234,18 +236,25 @@
 
 
 def temporal_kernel(
-    step_frames, dil_ref, key_ref, got_hbm, tw_ref, uw_ref,
-    grad_hbm, united_hbm, a0_hbm, cots_hbm, a1_hbm, feat_hbm, g1_hbm, g0_hbm,
-    a0, a1, feat, cots, g0, g1, slope0, slope1, grad_feat, united_ref, act_ref, cot_ref, grad_ref,
-    sems, in_sems, out_sems,
+    step_frames, here_ref, dil_ref, key_ref, act_hbm, tw_hbm, uw_hbm, *rest
 ):
+    cot_parts = rest[:-27]
+    (
+        grad_hbm, united_hbm, a0_hbm, cots_hbm, a1_hbm, feat_hbm, g1_hbm, g0_hbm,
+        a0, a1, feat, cots, g0, g1, slope0, slope1, grad_feat, united_ref, act_ref, cot_ref, grad_ref,
+        tw_ref, uw_ref, sems, in_sems, out_sems, cot_sems,
+    ) = rest[len(cot_parts) :]
     frames, block, ch = act_ref.shape
     high = feat.shape[1]
+    peers, turns = cot_ref.shape[:2]
     loads = [
-        pltpu.make_async_copy(got_hbm.at[:, n], ref, in_sems.at[n])
-        for n, ref in enumerate((act_ref, cot_ref))
-    ]
-    for load in loads:
+        pltpu.make_async_copy(source, ref, in_sems.at[n])
+        for n, (source, ref) in enumerate(((act_hbm, act_ref), (tw_hbm, tw_ref), (uw_hbm, uw_ref)))
+    ]
+    cot_loads = [
+        pltpu.make_async_copy(part, cot_ref.at[n], cot_sems.at[n]) for n, part in enumerate(cot_parts)
+    ]
+    for load in loads + cot_loads:
         load.start()
     stores = [
         pltpu.make_async_copy(
@@ -277,6 +286,8 @@
     loads[0].wait()
     a0[HALO : HALO + frames, :block, :] = act_ref[...]
     copies[4].start()
+    loads[1].wait()
+    loads[2].wait()
     for layer, (source, target, slopes) in enumerate(((a0, a1, slope0), (a1, feat, slope1))):
         step_size = dil_ref[layer]
         weight = jnp.concatenate([tw_ref[layer, k] for k in range(TAPS)], axis=0)
@@ -289,8 +300,10 @@
             )
             slopes[at : at + step_frames] = slope.reshape(step_frames, high, ch)
         copies[layer].start()
-    loads[1].wait()
-    cots[:, :block, :] = cot_ref[...]
+    for peer in range(peers):
+        cot_loads[peer].wait()
+        for turn in range(turns):
+            cots[place_of(here_ref, turns, peers, turn, peer), :block, :] = cot_ref[peer, turn]
     copies[5].start()
     for seg in range(segs):
         low, top = seg * seg_frames, (seg + 1) * seg_frames
@@ -402,18 +415,15 @@
     out_ref[split:] = sum(ref[...].astype(F32) for ref in refs[:-1]).astype(out_ref.dtype)
 
 
-def deal_kernel(here_ref, *refs):
-    united_hbm, *pieces = refs[:-5]
-    *outs, united_out, sem = refs[-5:]
+def deal_kernel(pieces_ref, united_hbm, *refs):
+    *outs, united_out, sem = refs
     copy = pltpu.make_async_copy(united_hbm, united_out, sem.at[0])
     copy.start()
-    for peer, piece in enumerate(pieces):
-        place = jnp.bitwise_xor(here_ref[1], peer)
-        at = 0
-        for out_ref in outs:
-            count = out_ref.shape[1]
-            out_ref[place] = piece[at : at + count].astype(F32)
-            at += count
+    at = 0
+    for out_ref in outs:
+        count = out_ref.shape[1]
+        out_ref[...] = pieces_ref[:, at : at + count].astype(F32)
+        at += count
     copy.wait()
 
 
@@ -429,6 +439,29 @@
 def turn_by(value, turn):
     size = lax.axis_size("seg")
     return lax.ppermute(value, "seg", [(i, (i + turn) % size) for i in range(size)])
+
+
+def pick(values, index):
+    return lax.dynamic_index_in_dim(values, index, 0, keepdims=False)
+
+
+def spread_in_seg(values):
+    size = lax.axis_size("seg")
+    seg = lax.axis_index("seg")
+    far = []
+    for turn in range(size):
+        mine = pick(values, lax.rem(seg + turn, size))
+        far.append(turn_by(mine, turn) if turn else mine)
+    return far
+
+
+def spread_in_grp(far):
+    grp = lax.axis_index("grp")
+    near = []
+    for peer in range(lax.axis_size("grp")):
+        mine = jnp.stack([pick(part, grp ^ peer) for part in far])
+        near.append(flip(mine, peer) if peer else mine)
+    return near
 
 
 def sum_of(parts):
@@ -467,24 +500,26 @@
     here = jnp.stack([lax.axis_index("seg"), lax.axis_index("grp")]).astype(jnp.int32)
     space_rows, time_rows, unite_rows = (n * ch // peers for n in (9, LAYERS * TAPS, 2))
 
+    cot_far = spread_in_seg(cotangent.reshape(-1, peers, block, ch))
     (send,) = call(
         functools.partial(spatial_fwd_kernel, rows_step),
-        [((rows, 2, cols, ch), BF16, HBM)],
+        [((rows, cols, ch), BF16, HBM)],
         [
             pltpu.VMEM((rows, cols, ch), BF16),
+            pltpu.VMEM(spatial_weight.shape, BF16),
             pltpu.VMEM((rows + 2, wide, ch), BF16),
-            pltpu.VMEM((rows, 2, cols, ch), BF16),
+            pltpu.VMEM((rows, cols, ch), BF16),
             pltpu.SemaphoreType.DMA((steps,)),
-            pltpu.SemaphoreType.DMA((steps,)),
+            pltpu.SemaphoreType.DMA((1,)),
             pltpu.SemaphoreType.DMA((steps,)),
         ],
         2 * 9 * pixels * ch * ch,
-        pixels * ch * 8,
-        [(frames_in[0], HBM), (spatial_weight, VMEM), (cotangent[0], HBM)],
-    )
-    send, frame = lax.optimization_barrier((send, frames_in[0]))
-    send = send.reshape(rows, 2, split, block, ch).swapaxes(1, 2).reshape(devices, 2, block, ch)
-    got = exchange(send)
+        pixels * ch * 4,
+        [(frames_in[0], HBM), (spatial_weight, HBM)],
+    )
+    send, frame, cot_far[1] = lax.optimization_barrier((send, frames_in[0], cot_far[1]))
+    got = exchange(send.reshape(devices, block, ch))
+    cot_near = spread_in_grp(cot_far)
     (space_slope,) = call(
         functools.partial(spatial_slope_kernel, rows_step),
         [((rows, cols, ch), BF16, VMEM)],
@@ -512,18 +547,22 @@
             pltpu.VMEM(whole, F32),
             pltpu.VMEM((frames, block, ch), BF16),
             pltpu.VMEM((frames, block, ch), BF16),
+            pltpu.VMEM((peers, devices // peers, block, ch), BF16),
             pltpu.VMEM((frames, block, ch), BF16),
-            pltpu.VMEM((frames, block, ch), BF16),
+            pltpu.VMEM(temporal_weight.shape, BF16),
+            pltpu.VMEM(uniting_weight.shape, BF16),
             pltpu.SemaphoreType.DMA((7,)),
-            pltpu.SemaphoreType.DMA((2,)),
+            pltpu.SemaphoreType.DMA((3,)),
             pltpu.SemaphoreType.DMA((frames // step_frames,)),
+            pltpu.SemaphoreType.DMA((peers,)),
         ],
         2 * 22 * frames * block * ch * ch,
         frames * block * ch * 18,
         [
-            (dilation, SMEM), (key_index, SMEM), (got, HBM),
-            (temporal_weight, VMEM), (uniting_weight, VMEM),
-        ],
+            (here, SMEM), (dilation, SMEM), (key_index, SMEM), (got, HBM),
+            (temporal_weight, HBM), (uniting_weight, HBM),
+        ]
+        + [(part, HBM) for part in cot_near],
     )
     grad_time = exchange(grad_send).reshape(rows, cols, ch)
     time_pieces = call(
@@ -588,8 +627,7 @@
         [pltpu.SemaphoreType.DMA((1,))],
         0,
         6 * 21 * ch * ch,
-        [(here, SMEM), (united, HBM)]
-        + [(flip(piece, peer) if peer else piece, VMEM) for peer in range(peers)],
+        [(lax.all_gather(piece, "grp", axis=0), VMEM), (united, HBM)],
         SMALL_VMEM,
     )
     return (

time: 152 us -> 163 us (1.072)
  blocking collectives: 0 us -> 10.2 us
  waiting for transfers between devices: 62.9 us -> 55 us
  starting transfers between devices: 43 us -> 50.3 us
  local copies, waits for them, and re-layouts: 3.33 us -> 5.57 us
    all_to_all x3, waiting for transfers between devices: 44 us -> 3.11 us  [exchange(): return lax.all_to_all(blocks, AXES, split_axis=0, concat_axis=0, tiled=True)]
    ppermute x3 -> x6, waiting for transfers between devices: 7.61 us -> 43.9 us  [turn_by(): lax.ppermute(value, 'seg', [(i, (i + turn) % size) for i in range(size)])]
    all_gather x0 -> x1, blocking collectives: none -> 10.2 us  [local(): lax.all_gather(piece, 'grp', axis=0)]
    ppermute x3 -> x6, starting transfers between devices: 5.07 us -> 12.7 us  [turn_by(): lax.ppermute(value, 'seg', [(i, (i + turn) % size) for i in range(size)])]
    ppermute x21, waiting for transfers between devices: 11.3 us -> 8.05 us  [flip(): return lax.ppermute(value, 'grp', [(i, i ^ peer) for i in range(size)])]
    unnamed x14 -> x28, local copies, waits for them, and re-layouts: 3.33 us -> 3.34 us
  transfers between devices with their start and end apart: 27 -> 30, of which waited for: 9 -> 10; matrix products, arithmetic and copies ran while one was open for 0% -> 1% of each run, Pallas kernels for 13% -> 16%
where the time goes in v9:
time: 163 us
  waiting for transfers between devices  55 us (34%)
  starting transfers between devices  50.3 us (31%)
  Pallas kernels  39.2 us (24%)
  blocking collectives  10.2 us (6%)
  local copies, waits for them, and re-layouts  5.57 us (3%)
    ppermute x6, waiting for transfers between devices, turn_by(): lax.ppermute(value, 'seg', [(i, (i + turn) % size) for i in range(size)])  43.9 us
    pallas_call x10, Pallas kernels, call(): pl.pallas_call(kernel, out_shape=[jax.ShapeDtypeStruct(shape, kind) for s...  39.2 us
    ppermute x21, starting transfers between devices, flip(): return lax.ppermute(value, 'grp', [(i, i ^ peer) for i in range(size)])  21.2 us
    all_to_all x3, starting transfers between devices, exchange(): return lax.all_to_all(blocks, AXES, split_axis=0, concat_axis=0, tiled=True)  16.4 us
    ppermute x6, starting transfers between devices, turn_by(): lax.ppermute(value, 'seg', [(i, (i + turn) % size) for i in range(size)])  12.7 us
    all_gather x1, blocking collectives, local(): lax.all_gather(piece, 'grp', axis=0)  10.2 us
    ppermute x21, waiting for transfers between devices, flip(): return lax.ppermute(value, 'grp', [(i, i ^ peer) for i in range(size)])  8.05 us
    unnamed x28, local copies, waits for them, and re-layouts  3.34 us
  transfers between devices with their start and end apart: 30, of which 10 were waited for; matrix products, arithmetic and copies ran while one was open for 1% of the time, Pallas kernels for 16%

profile of v9, /device:TPU:0, one launch (start us, length us, event | category | flops | bytes accessed | tf_op | source)
XLA Modules:
  0.0 162.8 jit_solution(5484749195050858965)
XLA Ops:
  0.7 1.2 dynamic-slice_bitcast_fusion.1
  1.9 3.1 %collective-permute-start = (bf16[8,120,128]{2,1,0:T(8,128)(2,1)S(1)}, bf16[8,120,128]{2,1,0:T(8,128)(2,1)S(1)}, u32[]{:S(2)}, u32[]{:S(2)}) collective-permute-start(bf16[8,120,128]{2,1,0:T(8,128)(2,1)S(1)} %get-tuple-element.93), channel_id=1, source_target_pairs={{0,8},{8,16},{16,24},{24,0},{1,9},{9,17},{17,25},{25,1},{2,10},{10... | collective-permute-start | bytes 737288 | tf_op jit(solution)/shard_map/ppermute | solution.py:441
  5.0 5.6 %shard_map.110 = bf16[32,120,128]{2,1,0:T(8,128)(2,1)} custom-call(bf16[32,120,128]{2,1,0:T(8,128)(2,1)} %bitcast.33, bf16[9,128,128]{2,1,0:T(8,128)(2,1)} %w_ref.3), custom_call_target="tpu_custom_call" | custom-call | flops 1132462080 | bytes 1966080 | tf_op jit(solution)/shard_map/pallas_call | solution.py:57
  10.5 2.4 %collective-permute-done = bf16[8,120,128]{2,1,0:T(8,128)(2,1)S(1)} collective-permute-done((bf16[8,120,128]{2,1,0:T(8,128)(2,1)S(1)}, bf16[8,120,128]{2,1,0:T(8,128)(2,1)S(1)}, u32[]{:S(2)}, u32[]{:S(2)}) %collective-permute-start) | collective-permute-done | bytes 245792 | tf_op jit(solution)/shard_map/ppermute | solution.py:441
  13.0 4.0 %all-to-all-start = ((bf16[32,120,128]{2,1,0:T(8,128)(2,1)}), bf16[32,120,128]{2,1,0:T(8,128)(2,1)S(1)}, u32[]{:S(2)}, u32[]{:S(2)}) async-start(bf16[32,120,128]{2,1,0:T(8,128)(2,1)} %shard_map.110), calls=%async_computation | async-start | bytes 1966080 | tf_op jit(solution)/shard_map/all_to_all | solution.py:431
  16.9 2.7 %collective-permute-start.1 = (bf16[8,120,128]{2,1,0:T(8,128)(2,1)S(1)}, bf16[8,120,128]{2,1,0:T(8,128)(2,1)S(1)}, u32[]{:S(2)}, u32[]{:S(2)}) collective-permute-start(bf16[8,120,128]{2,1,0:T(8,128)(2,1)S(1)} %get-tuple-element.91), channel_id=1, source_target_pairs={{0,16},{8,24},{16,0},{24,8},{1,17},{9,25},{17,1},{25,9},{2,18},{10... | collective-permute-start | bytes 737288 | tf_op jit(solution)/shard_map/ppermute | solution.py:441
  19.7 1.5 collective-permute-start.2
  21.1 0.9 dynamic-slice_bitcast_fusion.3
  22.0 0.6 pad_add_fusion.here_ref
  22.7 30.1 %collective-permute-done.1 = bf16[8,120,128]{2,1,0:T(8,128)(2,1)S(1)} collective-permute-done((bf16[8,120,128]{2,1,0:T(8,128)(2,1)S(1)}, bf16[8,120,128]{2,1,0:T(8,128)(2,1)S(1)}, u32[]{:S(2)}, u32[]{:S(2)}) %collective-permute-start.1) | collective-permute-done | bytes 245792 | tf_op jit(solution)/shard_map/ppermute | solution.py:441
  53.0 1.6 collective-permute-start.4
  54.6 0.4 collective-permute-start.5
  55.0 1.5 collective-permute-start.6
  56.9 2.5 %collective-permute-start.8 = (bf16[4,120,128]{2,1,0:T(8,128)(2,1)S(1)}, bf16[4,120,128]{2,1,0:T(8,128)(2,1)S(1)}, u32[]{:S(2)}, u32[]{:S(2)}) collective-permute-start(bf16[4,120,128]{2,1,0:T(8,128)(2,1)S(1)} %pad_maximum_fusion.6), channel_id=1, source_target_pairs={{0,6},{1,7},{2,4},{3,5},{4,2},{5,3},{6,0},{7,1},{8,14},{9,15},{10,... | collective-permute-start | bytes 368648 | tf_op jit(solution)/shard_map/ppermute | solution.py:436
  59.4 1.1 collective-permute-start.9
  60.5 4.5 %shard_map.111.slope_ref = bf16[32,120,128]{2,1,0:T(8,128)(2,1)} custom-call(bf16[32,120,128]{2,1,0:T(8,128)(2,1)} %bitcast.34, bf16[9,128,128]{2,1,0:T(8,128)(2,1)} %w_ref.3), custom_call_target="tpu_custom_call" | custom-call | flops 1132462080 | bytes 1966080 | tf_op jit(solution)/shard_map/pallas_call | solution.py:57
  65.0 0.7 pad_maximum_fusion.rest_0_
  65.7 2.2 %collective-permute-done.7.rest_5_ = bf16[4,120,128]{2,1,0:T(8,128)(2,1)S(1)} collective-permute-done((bf16[4,120,128]{2,1,0:T(8,128)(2,1)S(1)}, bf16[4,120,128]{2,1,0:T(8,128)(2,1)S(1)}, u32[]{:S(2)}, u32[]{:S(2)}) %collective-permute-start.7) | collective-permute-done | bytes 122912 | tf_op jit(solution)/shard_map/ppermute | solution.py:436
  67.9 0.6 copy-done.11
  68.6 0.6 copy-done.13
  69.2 11.8 %shard_map.112 = (bf16[32,120,128]{2,1,0:T(8,128)(2,1)}, bf16[32,120,128]{2,1,0:T(8,128)(2,1)}, bf16[32,128,128]{2,1,0:T(8,128)(2,1)}, bf16[32,128,128]{2,1,0:T(...) custom-call(s32[2]{0:T(128)} %pad_add_fusion.here_ref, ...), custom_call_target="tpu_custom_call" | custom-call | flops 2768240640 | bytes 8847360 | tf_op jit(solution)/shard_map/pallas_call | solution.py:57
  81.1 8.8 %all-to-all-start.1 = ((bf16[32,120,128]{2,1,0:T(8,128)(2,1)}), bf16[32,120,128]{2,1,0:T(8,128)(2,1)S(1)}, u32[]{:S(2)}, u32[]{:S(2)}) async-start(bf16[32,120,128]{2,1,0:T(8,128)(2,1)} %get-tuple-element.62), calls=%async_computation.1 | async-start | bytes 1966080 | tf_op jit(solution)/shard_map/all_to_all | solution.py:431
  89.8 9.3 %shard_map.113 = (bf16[192,128]{1,0:T(8,128)(2,1)}, bf16[192,128]{1,0:T(8,128)(2,1)}, bf16[192,128]{1,0:T(8,128)(2,1)}, bf16[192,128]{1,0:T(8,128)(2,1)}, bf16[1...) custom-call(s32[2]{0:T(128)} %pad_add_fusion.here_ref, ...), custom_call_target="tpu_custom_call" | custom-call | flops 1509949440 | bytes 6881280 | tf_op jit(solution)/shard_map/pallas_call | solution.py:57
  99.3 1.7 %collective-permute-start.11 = (bf16[192,128]{1,0:T(8,128)(2,1)}, bf16[192,128]{1,0:T(8,128)(2,1)S(1)}, u32[]{:S(2)}, u32[]{:S(2)}) collective-permute-start(bf16[192,128]{1,0:T(8,128)(2,1)} %get-tuple-element.56), channel_id=1, source_target_pairs={{0,2},{1,3},{2,0},{3,1},{4,6},{5,7},{6,4},{7,5},{8,10},{9,11},{10,... | collective-permute-start | bytes 147464 | tf_op jit(solution)/shard_map/ppermute | solution.py:436
  101.1 1.5 collective-permute-start.13
  102.8 2.5 %collective-permute-start.15 = (bf16[192,128]{1,0:T(8,128)(2,1)}, bf16[192,128]{1,0:T(8,128)(2,1)S(1)}, u32[]{:S(2)}, u32[]{:S(2)}) collective-permute-start(bf16[192,128]{1,0:T(8,128)(2,1)} %get-tuple-element.60), channel_id=1, source_target_pairs={{0,6},{1,7},{2,4},{3,5},{4,2},{5,3},{6,0},{7,1},{8,14},{9,15},{10,... | collective-permute-start | bytes 147464 | tf_op jit(solution)/shard_map/ppermute | solution.py:436
  105.4 0.7 collective-permute-start.16
  106.1 0.3 collective-permute-done.13.refs_4_
  106.4 2.9 %collective-permute-done.14.refs_5_ = bf16[192,128]{1,0:T(8,128)(2,1)S(1)} collective-permute-done((bf16[192,128]{1,0:T(8,128)(2,1)}, bf16[192,128]{1,0:T(8,128)(2,1)S(1)}, u32[]{:S(2)}, u32[]{:S(2)}) %collective-permute-start.14) | collective-permute-done | bytes 49184 | tf_op jit(solution)/shard_map/ppermute | solution.py:436
  109.3 1.2 collective-permute-done.16.refs_7_
  110.5 0.8 copy-done
  111.4 3.1 %all-to-all-done.1.got_ref = bf16[32,120,128]{2,1,0:T(8,128)(2,1)S(1)} async-done(((bf16[32,120,128]{2,1,0:T(8,128)(2,1)}), bf16[32,120,128]{2,1,0:T(8,128)(2,1)S(1)}, u32[]{:S(2)}, u32[]{:S(2)}) %all-to-all-start.1) | async-done | bytes 983072 | tf_op jit(solution)/shard_map/all_to_all | solution.py:431
  114.5 3.6 %all-to-all-start.2 = ((bf16[32,120,128]{2,1,0:T(8,128)(2,1)}), bf16[32,120,128]{2,1,0:T(8,128)(2,1)S(1)}, u32[]{:S(2)}, u32[]{:S(2)}) async-start(bf16[32,120,128]{2,1,0:T(8,128)(2,1)} %get-tuple-element.77), calls=%async_computation.2 | async-start | bytes 1966080 | tf_op jit(solution)/shard_map/all_to_all | solution.py:431
  118.1 1.2 copy-done.4
  119.3 2.6 %shard_map.115 = (bf16[144,128]{1,0:T(8,128)(2,1)S(1)}, bf16[144,128]{1,0:T(8,128)(2,1)S(1)}, bf16[144,128]{1,0:T(8,128)(2,1)S(1)}, bf16[144,128]{1,0:T(8,128)(2...) custom-call(s32[2]{0:T(128)S(1)} %copy-done.1, ...), custom_call_target="tpu_custom_call" | custom-call | flops 1132462080 | bytes 3932160 | tf_op jit(solution)/shard_map/pallas_call | solution.py:57
  121.9 0.3 collective-permute-start.17
  122.3 1.7 %collective-permute-start.18 = (bf16[144,128]{1,0:T(8,128)(2,1)S(1)}, bf16[144,128]{1,0:T(8,128)(2,1)S(1)}, u32[]{:S(2)}, u32[]{:S(2)}) collective-permute-start(bf16[144,128]{1,0:T(8,128)(2,1)S(1)} %get-tuple-element.71), channel_id=1, source_target_pairs={{0,2},{1,3},{2,0},{3,1},{4,6},{5,7},{6,4},{7,5},{8,10},{9,11},{10,... | collective-permute-start | bytes 110600 | tf_op jit(solution)/shard_map/ppermute | solution.py:436
  123.9 1.7 %collective-permute-start.20 = (bf16[144,128]{1,0:T(8,128)(2,1)S(1)}, bf16[144,128]{1,0:T(8,128)(2,1)S(1)}, u32[]{:S(2)}, u32[]{:S(2)}) collective-permute-start(bf16[144,128]{1,0:T(8,128)(2,1)S(1)} %get-tuple-element.73), channel_id=1, source_target_pairs={{0,4},{1,5},{2,6},{3,7},{4,0},{5,1},{6,2},{7,3},{8,12},{9,13},{10,... | collective-permute-start | bytes 110600 | tf_op jit(solution)/shard_map/ppermute | solution.py:436
  125.8 2.6 %collective-permute-start.22 = (bf16[144,128]{1,0:T(8,128)(2,1)S(1)}, bf16[144,128]{1,0:T(8,128)(2,1)S(1)}, u32[]{:S(2)}, u32[]{:S(2)}) collective-permute-start(bf16[144,128]{1,0:T(8,128)(2,1)S(1)} %get-tuple-element.75), channel_id=1, source_target_pairs={{0,6},{1,7},{2,4},{3,5},{4,2},{5,3},{6,0},{7,1},{8,14},{9,15},{10,... | collective-permute-start | bytes 110600 | tf_op jit(solution)/shard_map/ppermute | solution.py:436
  128.4 0.5 collective-permute-start.23
  128.9 3.2 %shard_map.116 = bf16[32,120,128]{2,1,0:T(8,128)(2,1)} custom-call(bf16[9,128,128]{2,1,0:T(8,128)(2,1)S(1)} %copy-done.3, bf16[32,120,128]{2,1,0:T(8,128)(2,1)S(1)} %all-to-all-done.1.got_ref, bf16[32,120,128]{2,1,0:T(8,128)(2,1)S(1)} %copy-done.5), custom_call_target="tpu_custom_call" | custom-call | flops 1132462080 | bytes 2949120 | tf_op jit(solution)/shard_map/pallas_call | solution.py:57
  132.1 1.4 collective-permute-done.23.refs_7_
  133.6 4.7 %collective-permute-start.26 = (bf16[336,128]{1,0:T(8,128)(2,1)S(1)}, bf16[336,128]{1,0:T(8,128)(2,1)S(1)}, u32[]{:S(2)}, u32[]{:S(2)}) collective-permute-start(bf16[336,128]{1,0:T(8,128)(2,1)S(1)} %shard_map.117.refs_0_), channel_id=1, source_target_pairs={{0,24},{8,0},{16,8},{24,16},{1,25},{9,1},{17,9},{25,17},{2,26},{10... | collective-permute-start | bytes 258056 | tf_op jit(solution)/shard_map/ppermute | solution.py:441
  138.3 0.6 collective-permute-start.24
  139.0 2.3 %collective-permute-done.26.refs_3_ = bf16[336,128]{1,0:T(8,128)(2,1)S(1)} collective-permute-done((bf16[336,128]{1,0:T(8,128)(2,1)S(1)}, bf16[336,128]{1,0:T(8,128)(2,1)S(1)}, u32[]{:S(2)}, u32[]{:S(2)}) %collective-permute-start.26) | collective-permute-done | bytes 86048 | tf_op jit(solution)/shard_map/ppermute | solution.py:441
  141.3 9.0 %collective-permute-done.25.refs_2_ = bf16[336,128]{1,0:T(8,128)(2,1)S(1)} collective-permute-done((bf16[336,128]{1,0:T(8,128)(2,1)S(1)}, bf16[336,128]{1,0:T(8,128)(2,1)S(1)}, u32[]{:S(2)}, u32[]{:S(2)}) %collective-permute-start.25) | collective-permute-done | bytes 86048 | tf_op jit(solution)/shard_map/ppermute | solution.py:441
  150.3 10.2 %all-gather = bf16[2688,128]{1,0:T(8,128)(2,1)S(1)} all-gather(bf16[336,128]{1,0:T(8,128)(2,1)S(1)} %shard_map.118), channel_id=2, replica_groups=mesh['seg'=4,'grp'=8] {'grp'}, dimensions={0}, use_global_device_ids=true | all-gather | bytes 774144 | tf_op jit(solution)/shard_map/all_gather | solution.py:630
  160.6 2.0 %shard_map.119 = (f32[8,160,128]{2,1,0:T(8,128)}, f32[8,32,128]{2,1,0:T(8,128)}, f32[8,144,128]{2,1,0:T(8,128)}, bf16[32,120,128]{2,1,0:T(8,128)(2,1)}) custom-call(bf16[8,336,128]{2,1,0:T(8,128)(2,1)S(1)} %bitcast.32, bf16[32,120,128]{2,1,0:T(8,128)(2,1)S(1)} %all-to-all-done.2.united_hbm), custom_call_target="tpu_custom_call" | custom-call | bytes 2064384 | tf_op jit(solution)/shard_map/pallas_call | solution.py:57
  (65 shorter events, 1.4 us)
Async XLA Ops:
  1.9 11.1 %collective-permute-start = (bf16[8,120,128]{2,1,0:T(8,128)(2,1)S(1)}, bf16[8,120,128]{2,1,0:T(8,128)(2,1)S(1)}, u32[]{:S(2)}, u32[]{:S(2)}) collective-permute-start(bf16[8,120,128]{2,1,0:T(8,128)(2,1)S(1)} %get-tuple-element.93), channel_id=1, source_target_pairs={{0,8},{8,16},{16,24},{24,0},{1,9},{9,17},{17,25},{25,1},{2,10},{10... | collective-permute-start | bytes 737288 | tf_op jit(solution)/shard_map/ppermute | solution.py:441
  13.0 52.7 %all-to-all-start = ((bf16[32,120,128]{2,1,0:T(8,128)(2,1)}), bf16[32,120,128]{2,1,0:T(8,128)(2,1)S(1)}, u32[]{:S(2)}, u32[]{:S(2)}) async-start(bf16[32,120,128]{2,1,0:T(8,128)(2,1)} %shard_map.110), calls=%async_computation | async-start | bytes 1966080 | tf_op jit(solution)/shard_map/all_to_all | solution.py:431
  16.9 35.8 %collective-permute-start.1 = (bf16[8,120,128]{2,1,0:T(8,128)(2,1)S(1)}, bf16[8,120,128]{2,1,0:T(8,128)(2,1)S(1)}, u32[]{:S(2)}, u32[]{:S(2)}) collective-permute-start(bf16[8,120,128]{2,1,0:T(8,128)(2,1)S(1)} %get-tuple-element.91), channel_id=1, source_target_pairs={{0,16},{8,24},{16,0},{24,8},{1,17},{9,25},{17,1},{25,9},{2,18},{10... | collective-permute-start | bytes 737288 | tf_op jit(solution)/shard_map/ppermute | solution.py:441
  19.7 33.1 %collective-permute-start.2 = (bf16[8,120,128]{2,1,0:T(8,128)(2,1)S(1)}, bf16[8,120,128]{2,1,0:T(8,128)(2,1)S(1)}, u32[]{:S(2)}, u32[]{:S(2)}) collective-permute-start(bf16[8,120,128]{2,1,0:T(8,128)(2,1)S(1)} %get-tuple-element.92), channel_id=1, source_target_pairs={{0,24},{8,0},{16,8},{24,16},{1,25},{9,1},{17,9},{25,17},{2,26},{10... | collective-permute-start | bytes 737288 | tf_op jit(solution)/shard_map/ppermute | solution.py:441
  52.9 4.0 %collective-permute-start.3 = (bf16[4,120,128]{2,1,0:T(8,128)(2,1)S(1)}, bf16[4,120,128]{2,1,0:T(8,128)(2,1)S(1)}, u32[]{:S(2)}, u32[]{:S(2)}) collective-permute-start(bf16[4,120,128]{2,1,0:T(8,128)(2,1)S(1)} %pad_maximum_fusion.1), channel_id=1, source_target_pairs={{0,1},{1,0},{2,3},{3,2},{4,5},{5,4},{6,7},{7,6},{8,9},{9,8},{10,11... | collective-permute-start | bytes 368648 | tf_op jit(solution)/shard_map/ppermute | solution.py:436
  53.0 6.4 %collective-permute-start.4 = (bf16[4,120,128]{2,1,0:T(8,128)(2,1)S(1)}, bf16[4,120,128]{2,1,0:T(8,128)(2,1)S(1)}, u32[]{:S(2)}, u32[]{:S(2)}) collective-permute-start(bf16[4,120,128]{2,1,0:T(8,128)(2,1)S(1)} %pad_maximum_fusion.2), channel_id=1, source_target_pairs={{0,2},{1,3},{2,0},{3,1},{4,6},{5,7},{6,4},{7,5},{8,10},{9,11},{10,... | collective-permute-start | bytes 368648 | tf_op jit(solution)/shard_map/ppermute | solution.py:436
  54.6 11.1 %collective-permute-start.5 = (bf16[4,120,128]{2,1,0:T(8,128)(2,1)S(1)}, bf16[4,120,128]{2,1,0:T(8,128)(2,1)S(1)}, u32[]{:S(2)}, u32[]{:S(2)}) collective-permute-start(bf16[4,120,128]{2,1,0:T(8,128)(2,1)S(1)} %pad_maximum_fusion.3), channel_id=1, source_target_pairs={{0,3},{1,2},{2,1},{3,0},{4,7},{5,6},{6,5},{7,4},{8,11},{9,10},{10,... | collective-permute-start | bytes 368648 | tf_op jit(solution)/shard_map/ppermute | solution.py:436
  55.0 10.7 %collective-permute-start.6 = (bf16[4,120,128]{2,1,0:T(8,128)(2,1)S(1)}, bf16[4,120,128]{2,1,0:T(8,128)(2,1)S(1)}, u32[]{:S(2)}, u32[]{:S(2)}) collective-permute-start(bf16[4,120,128]{2,1,0:T(8,128)(2,1)S(1)} %pad_maximum_fusion.4), channel_id=1, source_target_pairs={{0,4},{1,5},{2,6},{3,7},{4,0},{5,1},{6,2},{7,3},{8,12},{9,13},{10,... | collective-permute-start | bytes 368648 | tf_op jit(solution)/shard_map/ppermute | solution.py:436
  56.6 11.3 %collective-permute-start.7 = (bf16[4,120,128]{2,1,0:T(8,128)(2,1)S(1)}, bf16[4,120,128]{2,1,0:T(8,128)(2,1)S(1)}, u32[]{:S(2)}, u32[]{:S(2)}) collective-permute-start(bf16[4,120,128]{2,1,0:T(8,128)(2,1)S(1)} %pad_maximum_fusion.5), channel_id=1, source_target_pairs={{0,5},{1,4},{2,7},{3,6},{4,1},{5,0},{6,3},{7,2},{8,13},{9,12},{10,... | collective-permute-start | bytes 368648 | tf_op jit(solution)/shard_map/ppermute | solution.py:436
  56.9 8.1 %copy-start.7 = (bf16[4,120,128]{2,1,0:T(8,128)(2,1)}, bf16[4,120,128]{2,1,0:T(8,128)(2,1)S(1)}, u32[]{:S(2)}) copy-start(bf16[4,120,128]{2,1,0:T(8,128)(2,1)S(1)} %collective-permute-done.3.rest_1_) | copy-start | bytes 368644
  56.9 11.0 %collective-permute-start.8 = (bf16[4,120,128]{2,1,0:T(8,128)(2,1)S(1)}, bf16[4,120,128]{2,1,0:T(8,128)(2,1)S(1)}, u32[]{:S(2)}, u32[]{:S(2)}) collective-permute-start(bf16[4,120,128]{2,1,0:T(8,128)(2,1)S(1)} %pad_maximum_fusion.6), channel_id=1, source_target_pairs={{0,6},{1,7},{2,4},{3,5},{4,2},{5,3},{6,0},{7,1},{8,14},{9,15},{10,... | collective-permute-start | bytes 368648 | tf_op jit(solution)/shard_map/ppermute | solution.py:436
  59.4 5.6 %copy-start.8 = (bf16[4,120,128]{2,1,0:T(8,128)(2,1)}, bf16[4,120,128]{2,1,0:T(8,128)(2,1)S(1)}, u32[]{:S(2)}) copy-start(bf16[4,120,128]{2,1,0:T(8,128)(2,1)S(1)} %collective-permute-done.4.rest_2_) | copy-start | bytes 368644
  59.4 8.5 %collective-permute-start.9 = (bf16[4,120,128]{2,1,0:T(8,128)(2,1)S(1)}, bf16[4,120,128]{2,1,0:T(8,128)(2,1)S(1)}, u32[]{:S(2)}, u32[]{:S(2)}) collective-permute-start(bf16[4,120,128]{2,1,0:T(8,128)(2,1)S(1)} %pad_maximum_fusion.7), channel_id=1, source_target_pairs={{0,7},{1,6},{2,5},{3,4},{4,3},{5,2},{6,1},{7,0},{8,15},{9,14},{10,... | collective-permute-start | bytes 368648 | tf_op jit(solution)/shard_map/ppermute | solution.py:436
  65.7 2.2 %copy-start.6 = (bf16[32,120,128]{2,1,0:T(8,128)(2,1)}, bf16[32,120,128]{2,1,0:T(8,128)(2,1)S(1)}, u32[]{:S(2)}) copy-start(bf16[32,120,128]{2,1,0:T(8,128)(2,1)S(1)} %all-to-all-done.act_hbm) | copy-start | bytes 2949124
  65.7 2.2 %copy-start.9 = (bf16[4,120,128]{2,1,0:T(8,128)(2,1)}, bf16[4,120,128]{2,1,0:T(8,128)(2,1)S(1)}, u32[]{:S(2)}) copy-start(bf16[4,120,128]{2,1,0:T(8,128)(2,1)S(1)} %collective-permute-done.5.rest_3_) | copy-start | bytes 368644
  65.7 2.2 %copy-start.10 = (bf16[4,120,128]{2,1,0:T(8,128)(2,1)}, bf16[4,120,128]{2,1,0:T(8,128)(2,1)S(1)}, u32[]{:S(2)}) copy-start(bf16[4,120,128]{2,1,0:T(8,128)(2,1)S(1)} %collective-permute-done.6.rest_4_) | copy-start | bytes 368644
  67.9 0.7 copy-start.11
  67.9 0.7 copy-start.12
  68.6 0.6 copy-start.13
  81.1 33.4 %all-to-all-start.1 = ((bf16[32,120,128]{2,1,0:T(8,128)(2,1)}), bf16[32,120,128]{2,1,0:T(8,128)(2,1)S(1)}, u32[]{:S(2)}, u32[]{:S(2)}) async-start(bf16[32,120,128]{2,1,0:T(8,128)(2,1)} %get-tuple-element.62), calls=%async_computation.1 | async-start | bytes 1966080 | tf_op jit(solution)/shard_map/all_to_all | solution.py:431
  99.2 3.6 %collective-permute-start.10 = (bf16[192,128]{1,0:T(8,128)(2,1)}, bf16[192,128]{1,0:T(8,128)(2,1)S(1)}, u32[]{:S(2)}, u32[]{:S(2)}) collective-permute-start(bf16[192,128]{1,0:T(8,128)(2,1)} %get-tuple-element.55), channel_id=1, source_target_pairs={{0,1},{1,0},{2,3},{3,2},{4,5},{5,4},{6,7},{7,6},{8,9},{9,8},{10,11... | collective-permute-start | bytes 147464 | tf_op jit(solution)/shard_map/ppermute | solution.py:436
  99.3 6.1 %collective-permute-start.11 = (bf16[192,128]{1,0:T(8,128)(2,1)}, bf16[192,128]{1,0:T(8,128)(2,1)S(1)}, u32[]{:S(2)}, u32[]{:S(2)}) collective-permute-start(bf16[192,128]{1,0:T(8,128)(2,1)} %get-tuple-element.56), channel_id=1, source_target_pairs={{0,2},{1,3},{2,0},{3,1},{4,6},{5,7},{6,4},{7,5},{8,10},{9,11},{10,... | collective-permute-start | bytes 147464 | tf_op jit(solution)/shard_map/ppermute | solution.py:436
  101.0 5.2 %collective-permute-start.12 = (bf16[192,128]{1,0:T(8,128)(2,1)}, bf16[192,128]{1,0:T(8,128)(2,1)S(1)}, u32[]{:S(2)}, u32[]{:S(2)}) collective-permute-start(bf16[192,128]{1,0:T(8,128)(2,1)} %get-tuple-element.57), channel_id=1, source_target_pairs={{0,3},{1,2},{2,1},{3,0},{4,7},{5,6},{6,5},{7,4},{8,11},{9,10},{10,... | collective-permute-start | bytes 147464 | tf_op jit(solution)/shard_map/ppermute | solution.py:436
  101.1 5.3 %collective-permute-start.13 = (bf16[192,128]{1,0:T(8,128)(2,1)}, bf16[192,128]{1,0:T(8,128)(2,1)S(1)}, u32[]{:S(2)}, u32[]{:S(2)}) collective-permute-start(bf16[192,128]{1,0:T(8,128)(2,1)} %get-tuple-element.58), channel_id=1, source_target_pairs={{0,4},{1,5},{2,6},{3,7},{4,0},{5,1},{6,2},{7,3},{8,12},{9,13},{10,... | collective-permute-start | bytes 147464 | tf_op jit(solution)/shard_map/ppermute | solution.py:436
  102.7 6.7 %collective-permute-start.14 = (bf16[192,128]{1,0:T(8,128)(2,1)}, bf16[192,128]{1,0:T(8,128)(2,1)S(1)}, u32[]{:S(2)}, u32[]{:S(2)}) collective-permute-start(bf16[192,128]{1,0:T(8,128)(2,1)} %get-tuple-element.59), channel_id=1, source_target_pairs={{0,5},{1,4},{2,7},{3,6},{4,1},{5,0},{6,3},{7,2},{8,13},{9,12},{10,... | collective-permute-start | bytes 147464 | tf_op jit(solution)/shard_map/ppermute | solution.py:436
  102.8 6.5 %collective-permute-start.15 = (bf16[192,128]{1,0:T(8,128)(2,1)}, bf16[192,128]{1,0:T(8,128)(2,1)S(1)}, u32[]{:S(2)}, u32[]{:S(2)}) collective-permute-start(bf16[192,128]{1,0:T(8,128)(2,1)} %get-tuple-element.60), channel_id=1, source_target_pairs={{0,6},{1,7},{2,4},{3,5},{4,2},{5,3},{6,0},{7,1},{8,14},{9,15},{10,... | collective-permute-start | bytes 147464 | tf_op jit(solution)/shard_map/ppermute | solution.py:436
  105.4 5.1 %collective-permute-start.16 = (bf16[192,128]{1,0:T(8,128)(2,1)}, bf16[192,128]{1,0:T(8,128)(2,1)S(1)}, u32[]{:S(2)}, u32[]{:S(2)}) collective-permute-start(bf16[192,128]{1,0:T(8,128)(2,1)} %get-tuple-element.61), channel_id=1, source_target_pairs={{0,7},{1,6},{2,5},{3,4},{4,3},{5,2},{6,1},{7,0},{8,15},{9,14},{10,... | collective-permute-start | bytes 147464 | tf_op jit(solution)/shard_map/ppermute | solution.py:436
  110.5 0.8 copy-start
  114.5 3.6 %copy-start.1 = (s32[2]{0:T(128)S(1)}, s32[2]{0:T(128)}, u32[]{:S(2)}) copy-start(s32[2]{0:T(128)} %pad_add_fusion.here_ref) | copy-start | bytes 28
  114.5 3.6 %copy-start.2 = (bf16[1,32,120,128]{3,2,1,0:T(8,128)(2,1)S(1)}, bf16[1,32,120,128]{3,2,1,0:T(8,128)(2,1)}, u32[]{:S(2)}) copy-start(bf16[1,32,120,128]{3,2,1,0:T(8,128)(2,1)} %param.7) | copy-start | bytes 2949124
  114.5 46.1 %all-to-all-start.2 = ((bf16[32,120,128]{2,1,0:T(8,128)(2,1)}), bf16[32,120,128]{2,1,0:T(8,128)(2,1)S(1)}, u32[]{:S(2)}, u32[]{:S(2)}) async-start(bf16[32,120,128]{2,1,0:T(8,128)(2,1)} %get-tuple-element.77), calls=%async_computation.2 | async-start | bytes 1966080 | tf_op jit(solution)/shard_map/all_to_all | solution.py:431
  118.1 1.2 copy-start.4
  119.3 9.5 %copy-start.3 = (bf16[9,128,128]{2,1,0:T(8,128)(2,1)S(1)}, bf16[9,128,128]{2,1,0:T(8,128)(2,1)}, u32[]{:S(2)}) copy-start(bf16[9,128,128]{2,1,0:T(8,128)(2,1)} %w_ref.3) | copy-start | bytes 884740
  119.3 9.5 %copy-start.5 = (bf16[32,120,128]{2,1,0:T(8,128)(2,1)S(1)}, bf16[32,120,128]{2,1,0:T(8,128)(2,1)}, u32[]{:S(2)}) copy-start(bf16[32,120,128]{2,1,0:T(8,128)(2,1)} %shard_map.111.slope_ref) | copy-start | bytes 2949124
  121.9 3.8 %collective-permute-start.17 = (bf16[144,128]{1,0:T(8,128)(2,1)S(1)}, bf16[144,128]{1,0:T(8,128)(2,1)S(1)}, u32[]{:S(2)}, u32[]{:S(2)}) collective-permute-start(bf16[144,128]{1,0:T(8,128)(2,1)S(1)} %get-tuple-element.70), channel_id=1, source_target_pairs={{0,1},{1,0},{2,3},{3,2},{4,5},{5,4},{6,7},{7,6},{8,9},{9,8},{10,11... | collective-permute-start | bytes 110600 | tf_op jit(solution)/shard_map/ppermute | solution.py:436
  122.3 6.1 %collective-permute-start.18 = (bf16[144,128]{1,0:T(8,128)(2,1)S(1)}, bf16[144,128]{1,0:T(8,128)(2,1)S(1)}, u32[]{:S(2)}, u32[]{:S(2)}) collective-permute-start(bf16[144,128]{1,0:T(8,128)(2,1)S(1)} %get-tuple-element.71), channel_id=1, source_target_pairs={{0,2},{1,3},{2,0},{3,1},{4,6},{5,7},{6,4},{7,5},{8,10},{9,11},{10,... | collective-permute-start | bytes 110600 | tf_op jit(solution)/shard_map/ppermute | solution.py:436
  123.9 8.1 %collective-permute-start.19 = (bf16[144,128]{1,0:T(8,128)(2,1)S(1)}, bf16[144,128]{1,0:T(8,128)(2,1)S(1)}, u32[]{:S(2)}, u32[]{:S(2)}) collective-permute-start(bf16[144,128]{1,0:T(8,128)(2,1)S(1)} %get-tuple-element.72), channel_id=1, source_target_pairs={{0,3},{1,2},{2,1},{3,0},{4,7},{5,6},{6,5},{7,4},{8,11},{9,10},{10,... | collective-permute-start | bytes 110600 | tf_op jit(solution)/shard_map/ppermute | solution.py:436
  123.9 8.1 %collective-permute-start.20 = (bf16[144,128]{1,0:T(8,128)(2,1)S(1)}, bf16[144,128]{1,0:T(8,128)(2,1)S(1)}, u32[]{:S(2)}, u32[]{:S(2)}) collective-permute-start(bf16[144,128]{1,0:T(8,128)(2,1)S(1)} %get-tuple-element.73), channel_id=1, source_target_pairs={{0,4},{1,5},{2,6},{3,7},{4,0},{5,1},{6,2},{7,3},{8,12},{9,13},{10,... | collective-permute-start | bytes 110600 | tf_op jit(solution)/shard_map/ppermute | solution.py:436
  125.6 6.4 %collective-permute-start.21 = (bf16[144,128]{1,0:T(8,128)(2,1)S(1)}, bf16[144,128]{1,0:T(8,128)(2,1)S(1)}, u32[]{:S(2)}, u32[]{:S(2)}) collective-permute-start(bf16[144,128]{1,0:T(8,128)(2,1)S(1)} %get-tuple-element.74), channel_id=1, source_target_pairs={{0,5},{1,4},{2,7},{3,6},{4,1},{5,0},{6,3},{7,2},{8,13},{9,12},{10,... | collective-permute-start | bytes 110600 | tf_op jit(solution)/shard_map/ppermute | solution.py:436
  125.8 6.4 %collective-permute-start.22 = (bf16[144,128]{1,0:T(8,128)(2,1)S(1)}, bf16[144,128]{1,0:T(8,128)(2,1)S(1)}, u32[]{:S(2)}, u32[]{:S(2)}) collective-permute-start(bf16[144,128]{1,0:T(8,128)(2,1)S(1)} %get-tuple-element.75), channel_id=1, source_target_pairs={{0,6},{1,7},{2,4},{3,5},{4,2},{5,3},{6,0},{7,1},{8,14},{9,15},{10,... | collective-permute-start | bytes 110600 | tf_op jit(solution)/shard_map/ppermute | solution.py:436
  128.4 5.2 %collective-permute-start.23 = (bf16[144,128]{1,0:T(8,128)(2,1)S(1)}, bf16[144,128]{1,0:T(8,128)(2,1)S(1)}, u32[]{:S(2)}, u32[]{:S(2)}) collective-permute-start(bf16[144,128]{1,0:T(8,128)(2,1)S(1)} %get-tuple-element.76), channel_id=1, source_target_pairs={{0,7},{1,6},{2,5},{3,4},{4,3},{5,2},{6,1},{7,0},{8,15},{9,14},{10,... | collective-permute-start | bytes 110600 | tf_op jit(solution)/shard_map/ppermute | solution.py:436
  133.6 7.7 %collective-permute-start.26 = (bf16[336,128]{1,0:T(8,128)(2,1)S(1)}, bf16[336,128]{1,0:T(8,128)(2,1)S(1)}, u32[]{:S(2)}, u32[]{:S(2)}) collective-permute-start(bf16[336,128]{1,0:T(8,128)(2,1)S(1)} %shard_map.117.refs_0_), channel_id=1, source_target_pairs={{0,24},{8,0},{16,8},{24,16},{1,25},{9,1},{17,9},{25,17},{2,26},{10... | collective-permute-start | bytes 258056 | tf_op jit(solution)/shard_map/ppermute | solution.py:441
  138.3 12.0 %collective-permute-start.25 = (bf16[336,128]{1,0:T(8,128)(2,1)S(1)}, bf16[336,128]{1,0:T(8,128)(2,1)S(1)}, u32[]{:S(2)}, u32[]{:S(2)}) collective-permute-start(bf16[336,128]{1,0:T(8,128)(2,1)S(1)} %shard_map.117.refs_0_), channel_id=1, source_target_pairs={{0,16},{8,24},{16,0},{24,8},{1,17},{9,25},{17,1},{25,9},{2,18},{10... | collective-permute-start | bytes 258056 | tf_op jit(solution)/shard_map/ppermute | solution.py:441
  138.3 12.0 %collective-permute-start.24 = (bf16[336,128]{1,0:T(8,128)(2,1)S(1)}, bf16[336,128]{1,0:T(8,128)(2,1)S(1)}, u32[]{:S(2)}, u32[]{:S(2)}) collective-permute-start(bf16[336,128]{1,0:T(8,128)(2,1)S(1)} %shard_map.117.refs_0_), channel_id=1, source_target_pairs={{0,8},{8,16},{16,24},{24,0},{1,9},{9,17},{17,25},{25,1},{2,10},{10... | collective-permute-start | bytes 258056 | tf_op jit(solution)/shard_map/ppermute | solution.py:441

commit v10 on v7

--- a/solution.py
+++ b/solution.py
@@ -15,6 +15,7 @@
 BF16 = jnp.bfloat16
 F32 = jnp.float32
 BIG_VMEM = 60 * 1024 * 1024
+TIME_VMEM = 55 * 1024 * 1024
 MID_VMEM = 24 * 1024 * 1024
 SMALL_VMEM = 16 * 1024 * 1024
 
@@ -98,7 +99,8 @@
 
 
 def spatial_fwd_kernel(
-    rows_step, x_hbm, w_ref, cot_hbm, send_hbm, x_in, xs, sends, in_sems, cot_sems, send_sems
+    rows_step, x_hbm, w_hbm, cot_hbm, send_hbm,
+    x_in, w_ref, xs, sends, in_sems, w_sem, cot_sems, send_sems,
 ):
     rows, cols, ch = x_in.shape
     wide = xs.shape[1]
@@ -118,10 +120,10 @@
         pltpu.make_async_copy(sends.at[part(n)], send_hbm.at[part(n)], send_sems.at[n])
         for n in range(steps)
     ]
-    for load in loads + cot_loads:
+    w_load = pltpu.make_async_copy(w_hbm, w_ref, w_sem.at[0])
+    for load in [loads[0], w_load] + loads[1:] + cot_loads:
         load.start()
     clear_ends(xs)
-    weight = forward_weight(w_ref)
 
     def bring(step):
         loads[step].wait()
@@ -129,6 +131,8 @@
         put_rows(xs, at, x_in[at : at + rows_step])
 
     bring(0)
+    w_load.wait()
+    weight = forward_weight(w_ref)
     for step in range(steps):
         if step + 1 < steps:
             bring(step + 1)
@@ -234,16 +238,16 @@
 
 
 def temporal_kernel(
-    step_frames, dil_ref, key_ref, got_hbm, tw_ref, uw_ref,
-    grad_hbm, united_hbm, a0_hbm, cots_hbm, a1_hbm, feat_hbm, g1_hbm, g0_hbm,
-    a0, a1, feat, cots, g0, g1, slope0, slope1, grad_feat, united_ref, act_ref, cot_ref, grad_ref,
+    step_frames, dil_ref, key_ref, got_ref, tw_hbm, uw_hbm,
+    grad_hbm, united_hbm, kept_hbm,
+    a0, a1, feat, cots, g0, g1, slope0, slope1, united_ref, grad_ref, tw_ref, uw_ref,
     sems, in_sems, out_sems,
 ):
-    frames, block, ch = act_ref.shape
+    frames, _, block, ch = got_ref.shape
     high = feat.shape[1]
     loads = [
-        pltpu.make_async_copy(got_hbm.at[:, n], ref, in_sems.at[n])
-        for n, ref in enumerate((act_ref, cot_ref))
+        pltpu.make_async_copy(source, ref, in_sems.at[n])
+        for n, (source, ref) in enumerate(((tw_hbm, tw_ref), (uw_hbm, uw_ref)))
     ]
     for load in loads:
         load.start()
@@ -260,12 +264,12 @@
         pltpu.make_async_copy(source, target, sems.at[n])
         for n, (source, target) in enumerate(
             (
-                (a1.at[inside], a1_hbm),
-                (feat, feat_hbm),
-                (g1.at[inside], g1_hbm),
-                (g0.at[inside], g0_hbm),
-                (a0.at[inside], a0_hbm),
-                (cots, cots_hbm),
+                (a1.at[inside], kept_hbm.at[0]),
+                (feat, kept_hbm.at[1]),
+                (g1.at[inside], kept_hbm.at[2]),
+                (g0.at[inside], kept_hbm.at[3]),
+                (a0.at[inside], kept_hbm.at[4]),
+                (cots, kept_hbm.at[5]),
                 (united_ref, united_hbm),
             )
         )
@@ -274,9 +278,10 @@
         clear_halo(ref, frames)
     a0[HALO : HALO + frames] = jnp.zeros((frames, high, ch), BF16)
     cots[...] = jnp.zeros(cots.shape, cots.dtype)
-    loads[0].wait()
-    a0[HALO : HALO + frames, :block, :] = act_ref[...]
+    a0[HALO : HALO + frames, :block, :] = got_ref[:, 0]
     copies[4].start()
+    for load in loads:
+        load.wait()
     for layer, (source, target, slopes) in enumerate(((a0, a1, slope0), (a1, feat, slope1))):
         step_size = dil_ref[layer]
         weight = jnp.concatenate([tw_ref[layer, k] for k in range(TAPS)], axis=0)
@@ -289,8 +294,7 @@
             )
             slopes[at : at + step_frames] = slope.reshape(step_frames, high, ch)
         copies[layer].start()
-    loads[1].wait()
-    cots[:, :block, :] = cot_ref[...]
+    cots[:, :block, :] = got_ref[:, 1]
     copies[5].start()
     for seg in range(segs):
         low, top = seg * seg_frames, (seg + 1) * seg_frames
@@ -302,12 +306,13 @@
         united_ref[low:top] = (main + key_part[None]).astype(BF16)[:, :block]
         mine = cots[low:top]
         total = jnp.sum(mine.astype(F32), axis=0)
-        grad_feat[low:top] = mm_nt(mine.reshape(seg_frames * high, ch), uw_ref[0]).reshape(
+        key_term = sum(mm_nt(part, uw_ref[1]) for part in three_parts(total))
+        grad_feat = mm_nt(mine.reshape(seg_frames * high, ch), uw_ref[0]).reshape(
             seg_frames, high, ch
         )
-        key_term = sum(mm_nt(part, uw_ref[1]) for part in three_parts(total))
-        grad_feat[here] = grad_feat[here] + key_term
-        g1[HALO + low : HALO + top] = (grad_feat[low:top] * slope1[low:top]).astype(BF16)
+        for n in range(seg_frames):
+            grad = grad_feat[n] + jnp.where(key_ref[seg] == n, key_term, 0.0)
+            g1[HALO + low + n] = (grad * slope1[low + n]).astype(BF16)
     copies[6].start()
     for layer, source in ((1, g1), (0, g0)):
         copies[3 - layer].start()
@@ -332,7 +337,7 @@
 
 def temporal_wgrad_kernel(
     step_frames, scale, here_ref, dil_ref, key_ref,
-    a0_hbm, g0_hbm, a1_hbm, g1_hbm, feat_hbm, cots_hbm, *rest
+    kept_hbm, *rest
 ):
     pieces, (a0, g0, a1, g1, feat, cots, total_ref, sems) = rest[:-8], rest[-8:]
     frames, high, ch = feat.shape
@@ -344,12 +349,12 @@
         pltpu.make_async_copy(source, target, sems.at[n])
         for n, (source, target) in enumerate(
             (
-                (a0_hbm, a0.at[inside]),
-                (g0_hbm, g0),
-                (a1_hbm, a1.at[inside]),
-                (g1_hbm, g1),
-                (feat_hbm, feat),
-                (cots_hbm, cots),
+                (kept_hbm.at[4], a0.at[inside]),
+                (kept_hbm.at[3], g0),
+                (kept_hbm.at[0], a1.at[inside]),
+                (kept_hbm.at[2], g1),
+                (kept_hbm.at[1], feat),
+                (kept_hbm.at[5], cots),
             )
         )
     ]
@@ -391,6 +396,10 @@
     hand_out(here_ref, total_ref, pieces)
 
 
+def copy_kernel(from_ref, to_ref):
+    to_ref[...] = from_ref[...]
+
+
 def sum_kernel(*refs):
     refs[-1][...] = sum(ref[...].astype(F32) for ref in refs[:-1]).astype(refs[-1].dtype)
 
@@ -402,18 +411,15 @@
     out_ref[split:] = sum(ref[...].astype(F32) for ref in refs[:-1]).astype(out_ref.dtype)
 
 
-def deal_kernel(here_ref, *refs):
-    united_hbm, *pieces = refs[:-5]
-    *outs, united_out, sem = refs[-5:]
+def deal_kernel(pieces_ref, united_hbm, *refs):
+    *outs, united_out, sem = refs
     copy = pltpu.make_async_copy(united_hbm, united_out, sem.at[0])
     copy.start()
-    for peer, piece in enumerate(pieces):
-        place = jnp.bitwise_xor(here_ref[1], peer)
-        at = 0
-        for out_ref in outs:
-            count = out_ref.shape[1]
-            out_ref[place] = piece[at : at + count].astype(F32)
-            at += count
+    at = 0
+    for out_ref in outs:
+        count = out_ref.shape[1]
+        out_ref[...] = pieces_ref[:, at : at + count].astype(F32)
+        at += count
     copy.wait()
 
 
@@ -462,7 +468,10 @@
     high = round_up(block, 16)
     rows_step = next(n for n in (4, 2, 1) if rows % n == 0)
     steps = rows // rows_step
-    step_frames = max(n for n in range(1, frames + 1) if frames % n == 0 and n * high <= 512)
+    step_frames, narrow_step = (
+        max(n for n in range(1, frames + 1) if frames % n == 0 and n * high <= most)
+        for most in (512, 256)
+    )
     scale = float((frames * pixels) ** -0.5)
     here = jnp.stack([lax.axis_index("seg"), lax.axis_index("grp")]).astype(jnp.int32)
     space_rows, time_rows, unite_rows = (n * ch // peers for n in (9, LAYERS * TAPS, 2))
@@ -472,15 +481,17 @@
         [((rows, 2, cols, ch), BF16, HBM)],
         [
             pltpu.VMEM((rows, cols, ch), BF16),
+            pltpu.VMEM(spatial_weight.shape, BF16),
             pltpu.VMEM((rows + 2, wide, ch), BF16),
             pltpu.VMEM((rows, 2, cols, ch), BF16),
             pltpu.SemaphoreType.DMA((steps,)),
+            pltpu.SemaphoreType.DMA((1,)),
             pltpu.SemaphoreType.DMA((steps,)),
             pltpu.SemaphoreType.DMA((steps,)),
         ],
         2 * 9 * pixels * ch * ch,
         pixels * ch * 8,
-        [(frames_in[0], HBM), (spatial_weight, VMEM), (cotangent[0], HBM)],
+        [(frames_in[0], HBM), (spatial_weight, HBM), (cotangent[0], HBM)],
     )
     send, frame = lax.optimization_barrier((send, frames_in[0]))
     send = send.reshape(rows, 2, split, block, ch).swapaxes(1, 2).reshape(devices, 2, block, ch)
@@ -497,9 +508,9 @@
 
     padded = (frames + 2 * HALO, high, ch)
     whole = (frames, high, ch)
-    grad_send, united_send, a0, cots, a1, feat, g1, g0 = call(
-        functools.partial(temporal_kernel, step_frames),
-        [((frames, block, ch), BF16, HBM)] * 2 + [(whole, BF16, HBM)] * 6,
+    grad_send, united_send, kept = call(
+        functools.partial(temporal_kernel, narrow_step),
+        [((frames, block, ch), BF16, HBM)] * 2 + [((6,) + whole, BF16, HBM)],
         [
             pltpu.VMEM(padded, BF16),
             pltpu.VMEM(padded, BF16),
@@ -509,21 +520,21 @@
             pltpu.VMEM(padded, BF16),
             pltpu.VMEM(whole, F32),
             pltpu.VMEM(whole, F32),
-            pltpu.VMEM(whole, F32),
             pltpu.VMEM((frames, block, ch), BF16),
             pltpu.VMEM((frames, block, ch), BF16),
-            pltpu.VMEM((frames, block, ch), BF16),
-            pltpu.VMEM((frames, block, ch), BF16),
+            pltpu.VMEM(temporal_weight.shape, BF16),
+            pltpu.VMEM(uniting_weight.shape, BF16),
             pltpu.SemaphoreType.DMA((7,)),
             pltpu.SemaphoreType.DMA((2,)),
-            pltpu.SemaphoreType.DMA((frames // step_frames,)),
+            pltpu.SemaphoreType.DMA((frames // narrow_step,)),
         ],
         2 * 22 * frames * block * ch * ch,
         frames * block * ch * 18,
         [
-            (dilation, SMEM), (key_index, SMEM), (got, HBM),
-            (temporal_weight, VMEM), (uniting_weight, VMEM),
+            (dilation, SMEM), (key_index, SMEM), (got, VMEM),
+            (temporal_weight, HBM), (uniting_weight, HBM),
         ],
+        TIME_VMEM,
     )
     grad_time = exchange(grad_send).reshape(rows, cols, ch)
     time_pieces = call(
@@ -543,11 +554,20 @@
         frames * block * ch * 14,
         [
             (here, SMEM), (dilation, SMEM), (key_index, SMEM),
-            (a0, HBM), (g0, HBM), (a1, HBM), (g1, HBM), (feat, HBM), (cots, HBM),
+            (kept, HBM),
         ],
     )
+    (space_slope,) = call(
+        copy_kernel,
+        [((rows, cols, ch), BF16, VMEM)],
+        [],
+        0,
+        pixels * ch * 4,
+        [(space_slope, VMEM)],
+        MID_VMEM,
+    )
     time_sum = reduce_in_grp(time_pieces)
-    time_sum, grad_time = lax.optimization_barrier((time_sum, grad_time))
+    time_sum, space_slope, grad_time = lax.optimization_barrier((time_sum, space_slope, grad_time))
     united_send, grad_time = lax.optimization_barrier((united_send, grad_time))
     united = exchange(united_send)
     space_pieces = call(
@@ -588,8 +608,7 @@
         [pltpu.SemaphoreType.DMA((1,))],
         0,
         6 * 21 * ch * ch,
-        [(here, SMEM), (united, HBM)]
-        + [(flip(piece, peer) if peer else piece, VMEM) for peer in range(peers)],
+        [(lax.all_gather(piece, "grp", axis=0), VMEM), (united, HBM)],
         SMALL_VMEM,
     )
     return (

time: 152 us -> 150 us (0.987)
  blocking collectives: 0 us -> 10.2 us
  starting transfers between devices: 43 us -> 36.1 us
  waiting for transfers between devices: 62.9 us -> 57.5 us
    all_gather x0 -> x1, blocking collectives: none -> 10.2 us  [local(): lax.all_gather(piece, 'grp', axis=0)]
    ppermute x21 -> x14, starting transfers between devices: 22.7 us -> 15.8 us  [flip(): return lax.ppermute(value, 'grp', [(i, i ^ peer) for i in range(size)])]
    ppermute x21 -> x14, waiting for transfers between devices: 11.3 us -> 5.29 us  [flip(): return lax.ppermute(value, 'grp', [(i, i ^ peer) for i in range(size)])]
    pallas_call x10 -> x11, Pallas kernels: 40.8 us -> 40.5 us  [call(): pl.pallas_call(kernel, out_shape=[jax.ShapeDtypeStruct(shape, kind) for s...]
    unnamed x14 -> x18, local copies, waits for them, and re-layouts: 3.33 us -> 3.53 us
  transfers between devices with their start and end apart: 27 -> 20, of which waited for: 9 -> 7; matrix products, arithmetic and copies ran while one was open for 0% -> 0% of each run, Pallas kernels for 13% -> 13%
where the time goes in v10:
time: 150 us
  waiting for transfers between devices  57.5 us (38%)
  Pallas kernels  40.5 us (27%)
  starting transfers between devices  36.1 us (24%)
  blocking collectives  10.2 us (7%)
  local copies, waits for them, and re-layouts  3.53 us (2%)
    all_to_all x3, waiting for transfers between devices, exchange(): return lax.all_to_all(blocks, AXES, split_axis=0, concat_axis=0, tiled=True)  44.6 us
    pallas_call x11, Pallas kernels, call(): pl.pallas_call(kernel, out_shape=[jax.ShapeDtypeStruct(shape, kind) for s...  40.5 us
    ppermute x14, starting transfers between devices, flip(): return lax.ppermute(value, 'grp', [(i, i ^ peer) for i in range(size)])  15.8 us
    all_to_all x3, starting transfers between devices, exchange(): return lax.all_to_all(blocks, AXES, split_axis=0, concat_axis=0, tiled=True)  15.3 us
    all_gather x1, blocking collectives, local(): lax.all_gather(piece, 'grp', axis=0)  10.2 us
    ppermute x3, waiting for transfers between devices, turn_by(): lax.ppermute(value, 'seg', [(i, (i + turn) % size) for i in range(size)])  7.63 us
    ppermute x14, waiting for transfers between devices, flip(): return lax.ppermute(value, 'grp', [(i, i ^ peer) for i in range(size)])  5.29 us
    ppermute x3, starting transfers between devices, turn_by(): lax.ppermute(value, 'seg', [(i, (i + turn) % size) for i in range(size)])  5.06 us
  transfers between devices with their start and end apart: 20, of which 7 were waited for; matrix products, arithmetic and copies ran while one was open for 0% of the time, Pallas kernels for 13%

profile of v10, /device:TPU:0, one launch (start us, length us, event | category | flops | bytes accessed | tf_op | source)
XLA Modules:
  0.0 149.6 jit_solution(1273010204079065977)
XLA Ops:
  0.6 6.2 %shard_map.110 = bf16[32,2,120,128]{3,2,1,0:T(8,128)(2,1)} custom-call(bf16[32,120,128]{2,1,0:T(8,128)(2,1)} %bitcast.11, bf16[9,128,128]{2,1,0:T(8,128)(2,1)} %w_ref.3, bf16[32,120,128]{2,1,0:T(8,128)(2,1)} %bitcast.14), custom_call_target="tpu_custom_call" | custom-call | flops 1132462080 | bytes 3932160 | tf_op jit(solution)/shard_map/pallas_call | solution.py:58
  6.8 7.5 %all-to-all-start = ((bf16[32,2,120,128]{3,2,1,0:T(8,128)(2,1)}), bf16[32,2,120,128]{3,2,1,0:T(8,128)(2,1)S(1)}, u32[]{:S(2)}, u32[]{:S(2)}) async-start(bf16[32,2,120,128]{3,2,1,0:T(8,128)(2,1)} %shard_map.110), calls=%async_computation | async-start | bytes 3932160 | tf_op jit(solution)/shard_map/all_to_all | solution.py:427
  14.3 4.6 %shard_map.111.from_ref = bf16[32,120,128]{2,1,0:T(8,128)(2,1)} custom-call(bf16[32,120,128]{2,1,0:T(8,128)(2,1)} %bitcast.12, bf16[9,128,128]{2,1,0:T(8,128)(2,1)} %w_ref.3), custom_call_target="tpu_custom_call" | custom-call | flops 1132462080 | bytes 1966080 | tf_op jit(solution)/shard_map/pallas_call | solution.py:58
  18.9 41.3 %all-to-all-done.got_ref = bf16[32,2,120,128]{3,2,1,0:T(8,128)(2,1)S(1)} async-done(((bf16[32,2,120,128]{3,2,1,0:T(8,128)(2,1)}), bf16[32,2,120,128]{3,2,1,0:T(8,128)(2,1)S(1)}, u32[]{:S(2)}, u32[]{:S(2)}) %all-to-all-start) | async-done | bytes 1966112 | tf_op jit(solution)/shard_map/all_to_all | solution.py:427
  60.2 1.4 copy-done.8
  61.6 12.2 %shard_map.112 = (bf16[32,120,128]{2,1,0:T(8,128)(2,1)}, bf16[32,120,128]{2,1,0:T(8,128)(2,1)}, bf16[6,32,128,128]{3,2,1,0:T(8,128)(2,1)}) custom-call(s32[2]{0:T(128)} %dil_ref.3, s32[4]{0:T(128)} %key_ref.3, bf16[32,2,120,128]{3,2,1,0:T(8,128)(2,1)} %copy-done.8, bf16[2,5,128,128]{3,2,1,0:T(8,128)(2,1)} %tw_hbm.1, bf16[2,128,128]{2,1,0:T(8,128)(2,1)} %uw_hbm.1), custom_call_target="tpu_custom_call" | custom-call | flops 2768240640 | bytes 8847360 | tf_op jit(solution)/shard_map/pallas_call | solution.py:58
  73.8 4.2 %all-to-all-start.1 = ((bf16[32,120,128]{2,1,0:T(8,128)(2,1)}), bf16[32,120,128]{2,1,0:T(8,128)(2,1)S(1)}, u32[]{:S(2)}, u32[]{:S(2)}) async-start(bf16[32,120,128]{2,1,0:T(8,128)(2,1)} %get-tuple-element.52), calls=%async_computation.1 | async-start | bytes 1966080 | tf_op jit(solution)/shard_map/all_to_all | solution.py:427
  78.0 0.7 pad_add_fusion.here_ref
  78.7 9.4 %shard_map.113 = (bf16[192,128]{1,0:T(8,128)(2,1)}, bf16[192,128]{1,0:T(8,128)(2,1)}, bf16[192,128]{1,0:T(8,128)(2,1)}, bf16[192,128]{1,0:T(8,128)(2,1)}, bf16[1...) custom-call(s32[2]{0:T(128)} %pad_add_fusion.here_ref, ...), custom_call_target="tpu_custom_call" | custom-call | flops 1509949440 | bytes 6881280 | tf_op jit(solution)/shard_map/pallas_call | solution.py:58
  88.1 0.0 copy-start.6
  88.1 0.1 collective-permute-start
  88.2 1.7 %collective-permute-start.1 = (bf16[192,128]{1,0:T(8,128)(2,1)}, bf16[192,128]{1,0:T(8,128)(2,1)S(1)}, u32[]{:S(2)}, u32[]{:S(2)}) collective-permute-start(bf16[192,128]{1,0:T(8,128)(2,1)} %get-tuple-element.45), channel_id=1, source_target_pairs={{0,2},{1,3},{2,0},{3,1},{4,6},{5,7},{6,4},{7,5},{8,10},{9,11},{10,... | collective-permute-start | bytes 147464 | tf_op jit(solution)/shard_map/ppermute | solution.py:432
  89.9 0.2 collective-permute-start.2
  90.1 1.5 %collective-permute-start.3 = (bf16[192,128]{1,0:T(8,128)(2,1)}, bf16[192,128]{1,0:T(8,128)(2,1)S(1)}, u32[]{:S(2)}, u32[]{:S(2)}) collective-permute-start(bf16[192,128]{1,0:T(8,128)(2,1)} %get-tuple-element.47), channel_id=1, source_target_pairs={{0,4},{1,5},{2,6},{3,7},{4,0},{5,1},{6,2},{7,3},{8,12},{9,13},{10,... | collective-permute-start | bytes 147464 | tf_op jit(solution)/shard_map/ppermute | solution.py:432
  91.6 0.2 collective-permute-start.4
  91.8 0.0 collective-permute-done.refs_1_
  91.8 2.5 %collective-permute-start.5 = (bf16[192,128]{1,0:T(8,128)(2,1)}, bf16[192,128]{1,0:T(8,128)(2,1)S(1)}, u32[]{:S(2)}, u32[]{:S(2)}) collective-permute-start(bf16[192,128]{1,0:T(8,128)(2,1)} %get-tuple-element.49), channel_id=1, source_target_pairs={{0,6},{1,7},{2,4},{3,5},{4,2},{5,3},{6,0},{7,1},{8,14},{9,15},{10,... | collective-permute-start | bytes 147464 | tf_op jit(solution)/shard_map/ppermute | solution.py:432
  94.3 0.0 collective-permute-done.1.refs_2_
  94.3 0.2 collective-permute-start.6
  94.5 0.1 shard_map.115.slope_ref
  94.6 1.0 copy-done.1
  95.5 0.0 collective-permute-done.2.refs_3_
  95.5 0.0 collective-permute-done.3.refs_4_
  95.5 1.6 %collective-permute-done.4.refs_5_ = bf16[192,128]{1,0:T(8,128)(2,1)S(1)} collective-permute-done((bf16[192,128]{1,0:T(8,128)(2,1)}, bf16[192,128]{1,0:T(8,128)(2,1)S(1)}, u32[]{:S(2)}, u32[]{:S(2)}) %collective-permute-start.4) | collective-permute-done | bytes 49184 | tf_op jit(solution)/shard_map/ppermute | solution.py:432
  97.2 0.0 collective-permute-done.5.refs_6_
  97.2 2.1 %collective-permute-done.6.refs_7_ = bf16[192,128]{1,0:T(8,128)(2,1)S(1)} collective-permute-done((bf16[192,128]{1,0:T(8,128)(2,1)}, bf16[192,128]{1,0:T(8,128)(2,1)S(1)}, u32[]{:S(2)}, u32[]{:S(2)}) %collective-permute-start.6) | collective-permute-done | bytes 49184 | tf_op jit(solution)/shard_map/ppermute | solution.py:432
  99.3 0.1 shard_map.114.first_ref
  99.3 3.3 %all-to-all-done.1.got_ref = bf16[32,120,128]{2,1,0:T(8,128)(2,1)S(1)} async-done(((bf16[32,120,128]{2,1,0:T(8,128)(2,1)}), bf16[32,120,128]{2,1,0:T(8,128)(2,1)S(1)}, u32[]{:S(2)}, u32[]{:S(2)}) %all-to-all-start.1) | async-done | bytes 983072 | tf_op jit(solution)/shard_map/all_to_all | solution.py:427
  102.6 3.6 %all-to-all-start.2 = ((bf16[32,120,128]{2,1,0:T(8,128)(2,1)}), bf16[32,120,128]{2,1,0:T(8,128)(2,1)S(1)}, u32[]{:S(2)}, u32[]{:S(2)}) async-start(bf16[32,120,128]{2,1,0:T(8,128)(2,1)} %get-tuple-element.67), calls=%async_computation.2 | async-start | bytes 1966080 | tf_op jit(solution)/shard_map/all_to_all | solution.py:427
  106.3 1.2 copy-done.2
  107.5 2.6 %shard_map.116 = (bf16[144,128]{1,0:T(8,128)(2,1)S(1)}, bf16[144,128]{1,0:T(8,128)(2,1)S(1)}, bf16[144,128]{1,0:T(8,128)(2,1)S(1)}, bf16[144,128]{1,0:T(8,128)(2...) custom-call(s32[2]{0:T(128)S(1)} %copy-done.7, ...), custom_call_target="tpu_custom_call" | custom-call | flops 1132462080 | bytes 3932160 | tf_op jit(solution)/shard_map/pallas_call | solution.py:58
  110.1 1.8 %collective-permute-start.10 = (bf16[144,128]{1,0:T(8,128)(2,1)S(1)}, bf16[144,128]{1,0:T(8,128)(2,1)S(1)}, u32[]{:S(2)}, u32[]{:S(2)}) collective-permute-start(bf16[144,128]{1,0:T(8,128)(2,1)S(1)} %get-tuple-element.63), channel_id=1, source_target_pairs={{0,4},{1,5},{2,6},{3,7},{4,0},{5,1},{6,2},{7,3},{8,12},{9,13},{10,... | collective-permute-start | bytes 110600 | tf_op jit(solution)/shard_map/ppermute | solution.py:432
  111.9 0.0 collective-permute-start.11
  111.9 2.4 %collective-permute-start.12 = (bf16[144,128]{1,0:T(8,128)(2,1)S(1)}, bf16[144,128]{1,0:T(8,128)(2,1)S(1)}, u32[]{:S(2)}, u32[]{:S(2)}) collective-permute-start(bf16[144,128]{1,0:T(8,128)(2,1)S(1)} %get-tuple-element.65), channel_id=1, source_target_pairs={{0,6},{1,7},{2,4},{3,5},{4,2},{5,3},{6,0},{7,1},{8,14},{9,15},{10,... | collective-permute-start | bytes 110600 | tf_op jit(solution)/shard_map/ppermute | solution.py:432
  114.3 0.3 collective-permute-start.13
  114.6 0.3 collective-permute-start.7
  115.0 2.3 %collective-permute-start.8 = (bf16[144,128]{1,0:T(8,128)(2,1)S(1)}, bf16[144,128]{1,0:T(8,128)(2,1)S(1)}, u32[]{:S(2)}, u32[]{:S(2)}) collective-permute-start(bf16[144,128]{1,0:T(8,128)(2,1)S(1)} %get-tuple-element.61), channel_id=1, source_target_pairs={{0,2},{1,3},{2,0},{3,1},{4,6},{5,7},{6,4},{7,5},{8,10},{9,11},{10,... | collective-permute-start | bytes 110600 | tf_op jit(solution)/shard_map/ppermute | solution.py:432
  117.3 1.5 %collective-permute-done.11.refs_5_ = bf16[144,128]{1,0:T(8,128)(2,1)S(1)} collective-permute-done((bf16[144,128]{1,0:T(8,128)(2,1)S(1)}, bf16[144,128]{1,0:T(8,128)(2,1)S(1)}, u32[]{:S(2)}, u32[]{:S(2)}) %collective-permute-start.11) | collective-permute-done | bytes 36896 | tf_op jit(solution)/shard_map/ppermute | solution.py:432
  118.8 2.3 %collective-permute-start.9 = (bf16[144,128]{1,0:T(8,128)(2,1)S(1)}, bf16[144,128]{1,0:T(8,128)(2,1)S(1)}, u32[]{:S(2)}, u32[]{:S(2)}) collective-permute-start(bf16[144,128]{1,0:T(8,128)(2,1)S(1)} %get-tuple-element.62), channel_id=1, source_target_pairs={{0,3},{1,2},{2,1},{3,0},{4,7},{5,6},{6,5},{7,4},{8,11},{9,10},{10,... | collective-permute-start | bytes 110600 | tf_op jit(solution)/shard_map/ppermute | solution.py:432
  121.1 3.2 %shard_map.117 = bf16[32,120,128]{2,1,0:T(8,128)(2,1)} custom-call(bf16[9,128,128]{2,1,0:T(8,128)(2,1)S(1)} %copy-done.5, bf16[32,120,128]{2,1,0:T(8,128)(2,1)S(1)} %all-to-all-done.1.got_ref, bf16[32,120,128]{2,1,0:T(8,128)(2,1)S(1)} %copy-done.3), custom_call_target="tpu_custom_call" | custom-call | flops 1132462080 | bytes 2949120 | tf_op jit(solution)/shard_map/pallas_call | solution.py:58
  124.3 0.1 shard_map.118.refs_0_
  124.4 0.1 collective-permute-start.14
  124.4 4.0 %collective-permute-start.15 = (bf16[336,128]{1,0:T(8,128)(2,1)S(1)}, bf16[336,128]{1,0:T(8,128)(2,1)S(1)}, u32[]{:S(2)}, u32[]{:S(2)}) collective-permute-start(bf16[336,128]{1,0:T(8,128)(2,1)S(1)} %shard_map.118.refs_0_), channel_id=1, source_target_pairs={{0,16},{8,24},{16,0},{24,8},{1,17},{9,25},{17,1},{25,9},{2,18},{10... | collective-permute-start | bytes 258056 | tf_op jit(solution)/shard_map/ppermute | solution.py:437
  128.5 1.0 collective-permute-start.16
  129.4 2.2 %collective-permute-done.14.refs_1_ = bf16[336,128]{1,0:T(8,128)(2,1)S(1)} collective-permute-done((bf16[336,128]{1,0:T(8,128)(2,1)S(1)}, bf16[336,128]{1,0:T(8,128)(2,1)S(1)}, u32[]{:S(2)}, u32[]{:S(2)}) %collective-permute-start.14) | collective-permute-done | bytes 86048 | tf_op jit(solution)/shard_map/ppermute | solution.py:437
  131.7 5.4 %collective-permute-done.15.refs_2_ = bf16[336,128]{1,0:T(8,128)(2,1)S(1)} collective-permute-done((bf16[336,128]{1,0:T(8,128)(2,1)S(1)}, bf16[336,128]{1,0:T(8,128)(2,1)S(1)}, u32[]{:S(2)}, u32[]{:S(2)}) %collective-permute-start.15) | collective-permute-done | bytes 86048 | tf_op jit(solution)/shard_map/ppermute | solution.py:437
  137.1 10.2 %all-gather = bf16[2688,128]{1,0:T(8,128)(2,1)S(1)} all-gather(bf16[336,128]{1,0:T(8,128)(2,1)S(1)} %shard_map.119), channel_id=2, replica_groups=mesh['seg'=4,'grp'=8] {'grp'}, dimensions={0}, use_global_device_ids=true | all-gather | bytes 774144 | tf_op jit(solution)/shard_map/all_gather | solution.py:611
  147.4 2.0 %shard_map.120 = (f32[8,160,128]{2,1,0:T(8,128)}, f32[8,32,128]{2,1,0:T(8,128)}, f32[8,144,128]{2,1,0:T(8,128)}, bf16[32,120,128]{2,1,0:T(8,128)(2,1)}) custom-call(bf16[8,336,128]{2,1,0:T(8,128)(2,1)S(1)} %bitcast.10, bf16[32,120,128]{2,1,0:T(8,128)(2,1)S(1)} %all-to-all-done.2.united_hbm), custom_call_target="tpu_custom_call" | custom-call | bytes 2064384 | tf_op jit(solution)/shard_map/pallas_call | solution.py:58
  (23 shorter events, 0.1 us)
Async XLA Ops:
  6.8 53.4 %all-to-all-start = ((bf16[32,2,120,128]{3,2,1,0:T(8,128)(2,1)}), bf16[32,2,120,128]{3,2,1,0:T(8,128)(2,1)S(1)}, u32[]{:S(2)}, u32[]{:S(2)}) async-start(bf16[32,2,120,128]{3,2,1,0:T(8,128)(2,1)} %shard_map.110), calls=%async_computation | async-start | bytes 3932160 | tf_op jit(solution)/shard_map/all_to_all | solution.py:427
  60.2 1.4 copy-start.8
  73.8 28.8 %all-to-all-start.1 = ((bf16[32,120,128]{2,1,0:T(8,128)(2,1)}), bf16[32,120,128]{2,1,0:T(8,128)(2,1)S(1)}, u32[]{:S(2)}, u32[]{:S(2)}) async-start(bf16[32,120,128]{2,1,0:T(8,128)(2,1)} %get-tuple-element.52), calls=%async_computation.1 | async-start | bytes 1966080 | tf_op jit(solution)/shard_map/all_to_all | solution.py:427
  78.7 15.8 %copy-start.4 = (bf16[32,120,128]{2,1,0:T(8,128)(2,1)S(1)}, bf16[32,120,128]{2,1,0:T(8,128)(2,1)}, u32[]{:S(2)}) copy-start(bf16[32,120,128]{2,1,0:T(8,128)(2,1)} %shard_map.111.from_ref) | copy-start | bytes 2949124
  88.1 11.2 %copy-start.6 = (bf16[192,128]{1,0:T(8,128)(2,1)S(1)}, bf16[192,128]{1,0:T(8,128)(2,1)}, u32[]{:S(2)}) copy-start(bf16[192,128]{1,0:T(8,128)(2,1)} %get-tuple-element.43.refs_0_) | copy-start | bytes 147460
  88.1 3.6 %collective-permute-start = (bf16[192,128]{1,0:T(8,128)(2,1)}, bf16[192,128]{1,0:T(8,128)(2,1)S(1)}, u32[]{:S(2)}, u32[]{:S(2)}) collective-permute-start(bf16[192,128]{1,0:T(8,128)(2,1)} %get-tuple-element.44), channel_id=1, source_target_pairs={{0,1},{1,0},{2,3},{3,2},{4,5},{5,4},{6,7},{7,6},{8,9},{9,8},{10,11... | collective-permute-start | bytes 147464 | tf_op jit(solution)/shard_map/ppermute | solution.py:432
  88.2 6.1 %collective-permute-start.1 = (bf16[192,128]{1,0:T(8,128)(2,1)}, bf16[192,128]{1,0:T(8,128)(2,1)S(1)}, u32[]{:S(2)}, u32[]{:S(2)}) collective-permute-start(bf16[192,128]{1,0:T(8,128)(2,1)} %get-tuple-element.45), channel_id=1, source_target_pairs={{0,2},{1,3},{2,0},{3,1},{4,6},{5,7},{6,4},{7,5},{8,10},{9,11},{10,... | collective-permute-start | bytes 147464 | tf_op jit(solution)/shard_map/ppermute | solution.py:432
  89.9 5.6 %collective-permute-start.2 = (bf16[192,128]{1,0:T(8,128)(2,1)}, bf16[192,128]{1,0:T(8,128)(2,1)S(1)}, u32[]{:S(2)}, u32[]{:S(2)}) collective-permute-start(bf16[192,128]{1,0:T(8,128)(2,1)} %get-tuple-element.46), channel_id=1, source_target_pairs={{0,3},{1,2},{2,1},{3,0},{4,7},{5,6},{6,5},{7,4},{8,11},{9,10},{10,... | collective-permute-start | bytes 147464 | tf_op jit(solution)/shard_map/ppermute | solution.py:432
  90.1 5.5 %collective-permute-start.3 = (bf16[192,128]{1,0:T(8,128)(2,1)}, bf16[192,128]{1,0:T(8,128)(2,1)S(1)}, u32[]{:S(2)}, u32[]{:S(2)}) collective-permute-start(bf16[192,128]{1,0:T(8,128)(2,1)} %get-tuple-element.47), channel_id=1, source_target_pairs={{0,4},{1,5},{2,6},{3,7},{4,0},{5,1},{6,2},{7,3},{8,12},{9,13},{10,... | collective-permute-start | bytes 147464 | tf_op jit(solution)/shard_map/ppermute | solution.py:432
  91.6 5.5 %collective-permute-start.4 = (bf16[192,128]{1,0:T(8,128)(2,1)}, bf16[192,128]{1,0:T(8,128)(2,1)S(1)}, u32[]{:S(2)}, u32[]{:S(2)}) collective-permute-start(bf16[192,128]{1,0:T(8,128)(2,1)} %get-tuple-element.48), channel_id=1, source_target_pairs={{0,5},{1,4},{2,7},{3,6},{4,1},{5,0},{6,3},{7,2},{8,13},{9,12},{10,... | collective-permute-start | bytes 147464 | tf_op jit(solution)/shard_map/ppermute | solution.py:432
  91.8 5.4 %collective-permute-start.5 = (bf16[192,128]{1,0:T(8,128)(2,1)}, bf16[192,128]{1,0:T(8,128)(2,1)S(1)}, u32[]{:S(2)}, u32[]{:S(2)}) collective-permute-start(bf16[192,128]{1,0:T(8,128)(2,1)} %get-tuple-element.49), channel_id=1, source_target_pairs={{0,6},{1,7},{2,4},{3,5},{4,2},{5,3},{6,0},{7,1},{8,14},{9,15},{10,... | collective-permute-start | bytes 147464 | tf_op jit(solution)/shard_map/ppermute | solution.py:432
  94.3 11.9 %copy-start = (bf16[1,32,120,128]{3,2,1,0:T(8,128)(2,1)S(1)}, bf16[1,32,120,128]{3,2,1,0:T(8,128)(2,1)}, u32[]{:S(2)}) copy-start(bf16[1,32,120,128]{3,2,1,0:T(8,128)(2,1)} %param.7) | copy-start | bytes 2949124
  94.3 11.9 %copy-start.7 = (s32[2]{0:T(128)S(1)}, s32[2]{0:T(128)}, u32[]{:S(2)}) copy-start(s32[2]{0:T(128)} %pad_add_fusion.here_ref) | copy-start | bytes 28
  94.3 5.0 %collective-permute-start.6 = (bf16[192,128]{1,0:T(8,128)(2,1)}, bf16[192,128]{1,0:T(8,128)(2,1)S(1)}, u32[]{:S(2)}, u32[]{:S(2)}) collective-permute-start(bf16[192,128]{1,0:T(8,128)(2,1)} %get-tuple-element.50), channel_id=1, source_target_pairs={{0,7},{1,6},{2,5},{3,4},{4,3},{5,2},{6,1},{7,0},{8,15},{9,14},{10,... | collective-permute-start | bytes 147464 | tf_op jit(solution)/shard_map/ppermute | solution.py:432
  94.6 1.0 copy-start.1
  102.6 44.8 %all-to-all-start.2 = ((bf16[32,120,128]{2,1,0:T(8,128)(2,1)}), bf16[32,120,128]{2,1,0:T(8,128)(2,1)S(1)}, u32[]{:S(2)}, u32[]{:S(2)}) async-start(bf16[32,120,128]{2,1,0:T(8,128)(2,1)} %get-tuple-element.67), calls=%async_computation.2 | async-start | bytes 1966080 | tf_op jit(solution)/shard_map/all_to_all | solution.py:427
  106.3 1.2 copy-start.2
  107.5 13.6 %copy-start.3 = (bf16[32,120,128]{2,1,0:T(8,128)(2,1)S(1)}, bf16[32,120,128]{2,1,0:T(8,128)(2,1)}, u32[]{:S(2)}) copy-start(bf16[32,120,128]{2,1,0:T(8,128)(2,1)} %copy-done.1) | copy-start | bytes 2949124
  107.5 13.6 %copy-start.5 = (bf16[9,128,128]{2,1,0:T(8,128)(2,1)S(1)}, bf16[9,128,128]{2,1,0:T(8,128)(2,1)}, u32[]{:S(2)}) copy-start(bf16[9,128,128]{2,1,0:T(8,128)(2,1)} %w_ref.3) | copy-start | bytes 884740
  110.1 4.9 %collective-permute-start.10 = (bf16[144,128]{1,0:T(8,128)(2,1)S(1)}, bf16[144,128]{1,0:T(8,128)(2,1)S(1)}, u32[]{:S(2)}, u32[]{:S(2)}) collective-permute-start(bf16[144,128]{1,0:T(8,128)(2,1)S(1)} %get-tuple-element.63), channel_id=1, source_target_pairs={{0,4},{1,5},{2,6},{3,7},{4,0},{5,1},{6,2},{7,3},{8,12},{9,13},{10,... | collective-permute-start | bytes 110600 | tf_op jit(solution)/shard_map/ppermute | solution.py:432
  111.9 6.9 %collective-permute-start.11 = (bf16[144,128]{1,0:T(8,128)(2,1)S(1)}, bf16[144,128]{1,0:T(8,128)(2,1)S(1)}, u32[]{:S(2)}, u32[]{:S(2)}) collective-permute-start(bf16[144,128]{1,0:T(8,128)(2,1)S(1)} %get-tuple-element.64), channel_id=1, source_target_pairs={{0,5},{1,4},{2,7},{3,6},{4,1},{5,0},{6,3},{7,2},{8,13},{9,12},{10,... | collective-permute-start | bytes 110600 | tf_op jit(solution)/shard_map/ppermute | solution.py:432
  111.9 12.4 %collective-permute-start.12 = (bf16[144,128]{1,0:T(8,128)(2,1)S(1)}, bf16[144,128]{1,0:T(8,128)(2,1)S(1)}, u32[]{:S(2)}, u32[]{:S(2)}) collective-permute-start(bf16[144,128]{1,0:T(8,128)(2,1)S(1)} %get-tuple-element.65), channel_id=1, source_target_pairs={{0,6},{1,7},{2,4},{3,5},{4,2},{5,3},{6,0},{7,1},{8,14},{9,15},{10,... | collective-permute-start | bytes 110600 | tf_op jit(solution)/shard_map/ppermute | solution.py:432
  114.3 10.0 %collective-permute-start.13 = (bf16[144,128]{1,0:T(8,128)(2,1)S(1)}, bf16[144,128]{1,0:T(8,128)(2,1)S(1)}, u32[]{:S(2)}, u32[]{:S(2)}) collective-permute-start(bf16[144,128]{1,0:T(8,128)(2,1)S(1)} %get-tuple-element.66), channel_id=1, source_target_pairs={{0,7},{1,6},{2,5},{3,4},{4,3},{5,2},{6,1},{7,0},{8,15},{9,14},{10,... | collective-permute-start | bytes 110600 | tf_op jit(solution)/shard_map/ppermute | solution.py:432
  114.6 9.7 %collective-permute-start.7 = (bf16[144,128]{1,0:T(8,128)(2,1)S(1)}, bf16[144,128]{1,0:T(8,128)(2,1)S(1)}, u32[]{:S(2)}, u32[]{:S(2)}) collective-permute-start(bf16[144,128]{1,0:T(8,128)(2,1)S(1)} %get-tuple-element.60), channel_id=1, source_target_pairs={{0,1},{1,0},{2,3},{3,2},{4,5},{5,4},{6,7},{7,6},{8,9},{9,8},{10,11... | collective-permute-start | bytes 110600 | tf_op jit(solution)/shard_map/ppermute | solution.py:432
  115.0 9.3 %collective-permute-start.8 = (bf16[144,128]{1,0:T(8,128)(2,1)S(1)}, bf16[144,128]{1,0:T(8,128)(2,1)S(1)}, u32[]{:S(2)}, u32[]{:S(2)}) collective-permute-start(bf16[144,128]{1,0:T(8,128)(2,1)S(1)} %get-tuple-element.61), channel_id=1, source_target_pairs={{0,2},{1,3},{2,0},{3,1},{4,6},{5,7},{6,4},{7,5},{8,10},{9,11},{10,... | collective-permute-start | bytes 110600 | tf_op jit(solution)/shard_map/ppermute | solution.py:432
  118.8 5.5 %collective-permute-start.9 = (bf16[144,128]{1,0:T(8,128)(2,1)S(1)}, bf16[144,128]{1,0:T(8,128)(2,1)S(1)}, u32[]{:S(2)}, u32[]{:S(2)}) collective-permute-start(bf16[144,128]{1,0:T(8,128)(2,1)S(1)} %get-tuple-element.62), channel_id=1, source_target_pairs={{0,3},{1,2},{2,1},{3,0},{4,7},{5,6},{6,5},{7,4},{8,11},{9,10},{10,... | collective-permute-start | bytes 110600 | tf_op jit(solution)/shard_map/ppermute | solution.py:432
  124.4 7.3 %collective-permute-start.14 = (bf16[336,128]{1,0:T(8,128)(2,1)S(1)}, bf16[336,128]{1,0:T(8,128)(2,1)S(1)}, u32[]{:S(2)}, u32[]{:S(2)}) collective-permute-start(bf16[336,128]{1,0:T(8,128)(2,1)S(1)} %shard_map.118.refs_0_), channel_id=1, source_target_pairs={{0,8},{8,16},{16,24},{24,0},{1,9},{9,17},{17,25},{25,1},{2,10},{10... | collective-permute-start | bytes 258056 | tf_op jit(solution)/shard_map/ppermute | solution.py:437
  124.4 12.6 %collective-permute-start.15 = (bf16[336,128]{1,0:T(8,128)(2,1)S(1)}, bf16[336,128]{1,0:T(8,128)(2,1)S(1)}, u32[]{:S(2)}, u32[]{:S(2)}) collective-permute-start(bf16[336,128]{1,0:T(8,128)(2,1)S(1)} %shard_map.118.refs_0_), channel_id=1, source_target_pairs={{0,16},{8,24},{16,0},{24,8},{1,17},{9,25},{17,1},{25,9},{2,18},{10... | collective-permute-start | bytes 258056 | tf_op jit(solution)/shard_map/ppermute | solution.py:437
  128.5 8.6 %collective-permute-start.16 = (bf16[336,128]{1,0:T(8,128)(2,1)S(1)}, bf16[336,128]{1,0:T(8,128)(2,1)S(1)}, u32[]{:S(2)}, u32[]{:S(2)}) collective-permute-start(bf16[336,128]{1,0:T(8,128)(2,1)S(1)} %shard_map.118.refs_0_), channel_id=1, source_target_pairs={{0,24},{8,0},{16,8},{24,16},{1,25},{9,1},{17,9},{25,17},{2,26},{10... | collective-permute-start | bytes 258056 | tf_op jit(solution)/shard_map/ppermute | solution.py:437

commit v11 on v10

--- a/solution.py
+++ b/solution.py
@@ -15,8 +15,8 @@
 BF16 = jnp.bfloat16
 F32 = jnp.float32
 BIG_VMEM = 60 * 1024 * 1024
-TIME_VMEM = 55 * 1024 * 1024
-MID_VMEM = 24 * 1024 * 1024
+MID_VMEM = 40 * 1024 * 1024
+SPARE = 28
 SMALL_VMEM = 16 * 1024 * 1024
 
 
@@ -94,58 +94,56 @@
 
 def put_rows(ref, at, value):
     count, cols, ch = value.shape
-    ref[1 + at : 1 + at + count] = jnp.zeros((count,) + ref.shape[1:], ref.dtype)
+    ref[1 + at : 1 + at + count, cols:, :] = jnp.zeros((count, ref.shape[1] - cols, ch), ref.dtype)
     ref[1 + at : 1 + at + count, :cols, :] = value
 
 
 def spatial_fwd_kernel(
     rows_step, x_hbm, w_hbm, cot_hbm, send_hbm,
-    x_in, w_ref, xs, sends, in_sems, w_sem, cot_sems, send_sems,
+    x_in, w_ref, xs, sends, in_sems, w_sem, cot_sem, send_sems,
 ):
     rows, cols, ch = x_in.shape
     wide = xs.shape[1]
-    steps = rows // rows_step
-
-    def part(step):
-        return pl.ds(step * rows_step, rows_step)
+    parts = in_sems.shape[0]
+    many = rows // parts
+
+    def part(n):
+        return pl.ds(n * many, many)
 
     loads = [
-        pltpu.make_async_copy(x_hbm.at[part(n)], x_in.at[part(n)], in_sems.at[n]) for n in range(steps)
-    ]
-    cot_loads = [
-        pltpu.make_async_copy(cot_hbm.at[part(n)], sends.at[part(n), 1], cot_sems.at[n])
-        for n in range(steps)
+        pltpu.make_async_copy(x_hbm.at[part(n)], x_in.at[part(n)], in_sems.at[n]) for n in range(parts)
     ]
     stores = [
         pltpu.make_async_copy(sends.at[part(n)], send_hbm.at[part(n)], send_sems.at[n])
-        for n in range(steps)
+        for n in range(parts)
     ]
     w_load = pltpu.make_async_copy(w_hbm, w_ref, w_sem.at[0])
-    for load in [loads[0], w_load] + loads[1:] + cot_loads:
+    cot_load = pltpu.make_async_copy(cot_hbm, sends.at[:, 1], cot_sem.at[0])
+    for load in [loads[0], w_load] + loads[1:] + [cot_load]:
         load.start()
     clear_ends(xs)
 
-    def bring(step):
-        loads[step].wait()
-        at = step * rows_step
-        put_rows(xs, at, x_in[at : at + rows_step])
+    def bring(n):
+        loads[n].wait()
+        put_rows(xs, n * many, x_in[n * many : (n + 1) * many])
 
     bring(0)
     w_load.wait()
     weight = forward_weight(w_ref)
-    for step in range(steps):
-        if step + 1 < steps:
-            bring(step + 1)
-        at = step * rows_step
-        act, _ = silu_parts(spatial_pre(xs, weight, at, rows_step))
-        sends[at : at + rows_step, 0] = act.astype(BF16).reshape(rows_step, wide, ch)[:, :cols]
-        cot_loads[step].wait()
-        stores[step].start()
+    for n in range(parts):
+        if n + 1 < parts:
+            bring(n + 1)
+        for at in range(n * many, (n + 1) * many, rows_step):
+            act, _ = silu_parts(spatial_pre(xs, weight, at, rows_step))
+            sends[at : at + rows_step, 0] = act.astype(BF16).reshape(rows_step, wide, ch)[:, :cols]
+        if n == 0:
+            cot_load.wait()
+        stores[n].start()
     for store in stores:
         store.wait()
 
 
-def spatial_slope_kernel(rows_step, x_ref, w_ref, slope_ref, xs):
+def spatial_slope_kernel(rows_step, x_ref, w_ref, slope_hbm, xs, slopes, sem):
     rows, cols, ch = x_ref.shape
     wide = xs.shape[1]
     clear_ends(xs)
@@ -153,9 +151,10 @@
     weight = forward_weight(w_ref)
     for at in range(0, rows, rows_step):
         _, slope = silu_parts(spatial_pre(xs, weight, at, rows_step))
-        slope_ref[at : at + rows_step] = (
-            slope.astype(BF16).reshape(rows_step, wide, ch)[:, :cols]
-        )
+        slopes[at : at + rows_step] = slope.astype(BF16).reshape(rows_step, wide, ch)[:, :cols]
+    store = pltpu.make_async_copy(slopes, slope_hbm.at[0], sem.at[0])
+    store.start()
+    store.wait()
 
 
 def hand_out(here_ref, total_ref, pieces):
@@ -179,18 +178,23 @@
         put_rows(gs, at, (grads * slopes).astype(BF16))
 
 
-def spatial_wgrad_kernel(rows_step, scale, here_ref, got_ref, slope_ref, x_ref, *rest):
-    pieces, (gs, total_ref) = rest[:-2], rest[-2:]
+def spatial_wgrad_kernel(rows_step, scale, here_ref, got_ref, slope_hbm, x_ref, *rest):
+    pieces, (gs, slopes, cat_ref, total_ref, sem) = rest[:-5], rest[-5:]
     rows, cols, ch = got_ref.shape
     wide = gs.shape[1]
     flat = rows_step * wide
+    load = pltpu.make_async_copy(slope_hbm.at[0], slopes, sem.at[0])
+    load.start()
     pad = jnp.zeros((rows_step, wide - cols, ch), F32)
-    fill_grads(rows_step, gs, got_ref, slope_ref)
-    total = jnp.zeros((3 * ch, 3 * ch), F32)
     for at in range(0, rows, rows_step):
         x = jnp.concatenate([x_ref[at : at + rows_step].astype(F32), pad], axis=1).reshape(flat, ch)
         x_cat = jnp.concatenate([roll_rows(x, 1), x, roll_rows(x, -1)], axis=1)
-        total = total + mm(x_cat.T.astype(BF16), taps_up(gs, at, rows_step))
+        cat_ref[:, at * wide : at * wide + flat] = x_cat.T.astype(BF16)
+    load.wait()
+    fill_grads(rows_step, gs, got_ref, slopes)
+    total = jnp.zeros((3 * ch, 3 * ch), F32)
+    for at in range(0, rows, rows_step):
+        total = total + mm(cat_ref[:, at * wide : at * wide + flat], taps_up(gs, at, rows_step))
     total_ref[...] = (
         jnp.concatenate(
             [
@@ -205,9 +209,11 @@
     hand_out(here_ref, total_ref, pieces)
 
 
-def spatial_back_kernel(rows_step, w_ref, got_ref, slope_ref, back_ref, gs):
+def spatial_back_kernel(rows_step, w_ref, got_ref, slope_hbm, back_ref, gs, slopes, sem):
     rows, cols, ch = back_ref.shape
     wide = gs.shape[1]
+    load = pltpu.make_async_copy(slope_hbm.at[0], slopes, sem.at[0])
+    load.start()
     weight = jnp.concatenate(
         [
             jnp.concatenate([w_ref[3 * a + b].astype(F32).T.astype(BF16) for b in range(3)], axis=1)
@@ -215,7 +221,8 @@
         ],
         axis=0,
     )
-    fill_grads(rows_step, gs, got_ref, slope_ref)
+    load.wait()
+    fill_grads(rows_step, gs, got_ref, slopes)
     for at in range(0, rows, rows_step):
         y = mm(taps_up(gs, at, rows_step), weight)
         back = y[:, ch : 2 * ch] + roll_rows(y[:, :ch], -1) + roll_rows(y[:, 2 * ch :], 1)
@@ -239,7 +246,7 @@
 
 def temporal_kernel(
     step_frames, dil_ref, key_ref, got_ref, tw_hbm, uw_hbm,
-    grad_hbm, united_hbm, kept_hbm,
+    grad_hbm, kept_hbm, united_hbm,
     a0, a1, feat, cots, g0, g1, slope0, slope1, united_ref, grad_ref, tw_ref, uw_ref,
     sems, in_sems, out_sems,
 ):
@@ -270,14 +277,16 @@
                 (g0.at[inside], kept_hbm.at[3]),
                 (a0.at[inside], kept_hbm.at[4]),
                 (cots, kept_hbm.at[5]),
-                (united_ref, united_hbm),
+                (united_ref, united_hbm.at[0]),
             )
         )
     ]
     for ref in (a0, a1, g0, g1):
         clear_halo(ref, frames)
-    a0[HALO : HALO + frames] = jnp.zeros((frames, high, ch), BF16)
-    cots[...] = jnp.zeros(cots.shape, cots.dtype)
+    if high > block:
+        pad = jnp.zeros((frames, high - block, ch), BF16)
+        a0[HALO : HALO + frames, block:, :] = pad
+        cots[:, block:, :] = pad
     a0[HALO : HALO + frames, :block, :] = got_ref[:, 0]
     copies[4].start()
     for load in loads:
@@ -337,9 +346,9 @@
 
 def temporal_wgrad_kernel(
     step_frames, scale, here_ref, dil_ref, key_ref,
-    kept_hbm, *rest
+    kept_hbm, united_kept, united_hbm, *rest
 ):
-    pieces, (a0, g0, a1, g1, feat, cots, total_ref, sems) = rest[:-8], rest[-8:]
+    pieces, (a0, g0, a1, g1, feat, cots, united, total_ref, sems) = rest[:-9], rest[-9:]
     frames, high, ch = feat.shape
     segs = key_ref.shape[0]
     seg_frames = frames // segs
@@ -355,6 +364,7 @@
                 (kept_hbm.at[2], g1),
                 (kept_hbm.at[1], feat),
                 (kept_hbm.at[5], cots),
+                (united_kept.at[0], united),
             )
         )
     ]
@@ -373,8 +383,10 @@
                 grads[at : at + step_frames].reshape(rows, ch),
             )
         totals.append(total)
-    copies[4].wait()
-    copies[5].wait()
+    for copy in copies[4:]:
+        copy.wait()
+    united_copy = pltpu.make_async_copy(united, united_hbm, sems.at[len(copies)])
+    united_copy.start()
     total = jnp.zeros((ch, ch), F32)
     for at in range(0, frames, step_frames):
         total = total + mm_tn(
@@ -394,10 +406,7 @@
         peers, 2 * ch // peers, ch
     )
     hand_out(here_ref, total_ref, pieces)
-
-
-def copy_kernel(from_ref, to_ref):
-    to_ref[...] = from_ref[...]
+    united_copy.wait()
 
 
 def sum_kernel(*refs):
@@ -412,15 +421,18 @@
 
 
 def deal_kernel(pieces_ref, united_hbm, *refs):
-    *outs, united_out, sem = refs
-    copy = pltpu.make_async_copy(united_hbm, united_out, sem.at[0])
-    copy.start()
+    outs_hbm, united_out, outs, sems = refs[:3], refs[3], refs[4:7], refs[7]
+    copies = [pltpu.make_async_copy(united_hbm, united_out, sems.at[3])]
+    copies[0].start()
     at = 0
-    for out_ref in outs:
+    for n, out_ref in enumerate(outs):
         count = out_ref.shape[1]
         out_ref[...] = pieces_ref[:, at : at + count].astype(F32)
+        copies.append(pltpu.make_async_copy(out_ref, outs_hbm[n], sems.at[n]))
+        copies[-1].start()
         at += count
-    copy.wait()
+    for copy in copies:
+        copy.wait()
 
 
 def exchange(blocks):
@@ -467,7 +479,7 @@
     wide = round_up(cols + 1, 16)
     high = round_up(block, 16)
     rows_step = next(n for n in (4, 2, 1) if rows % n == 0)
-    steps = rows // rows_step
+    parts = next(n for n in (4, 2, 1) if rows % (n * rows_step) == 0)
     step_frames, narrow_step = (
         max(n for n in range(1, frames + 1) if frames % n == 0 and n * high <= most)
         for most in (512, 256)
@@ -484,10 +496,10 @@
             pltpu.VMEM(spatial_weight.shape, BF16),
             pltpu.VMEM((rows + 2, wide, ch), BF16),
             pltpu.VMEM((rows, 2, cols, ch), BF16),
-            pltpu.SemaphoreType.DMA((steps,)),
+            pltpu.SemaphoreType.DMA((parts,)),
             pltpu.SemaphoreType.DMA((1,)),
-            pltpu.SemaphoreType.DMA((steps,)),
-            pltpu.SemaphoreType.DMA((steps,)),
+            pltpu.SemaphoreType.DMA((1,)),
+            pltpu.SemaphoreType.DMA((parts,)),
         ],
         2 * 9 * pixels * ch * ch,
         pixels * ch * 8,
@@ -498,8 +510,12 @@
     got = exchange(send)
     (space_slope,) = call(
         functools.partial(spatial_slope_kernel, rows_step),
-        [((rows, cols, ch), BF16, VMEM)],
-        [pltpu.VMEM((rows + 2, wide, ch), BF16)],
+        [((SPARE, rows, cols, ch), BF16, HBM)],
+        [
+            pltpu.VMEM((rows + 2, wide, ch), BF16),
+            pltpu.VMEM((rows, cols, ch), BF16),
+            pltpu.SemaphoreType.DMA((1,)),
+        ],
         2 * 9 * pixels * ch * ch,
         pixels * ch * 4,
         [(frame, VMEM), (spatial_weight, VMEM)],
@@ -508,9 +524,13 @@
 
     padded = (frames + 2 * HALO, high, ch)
     whole = (frames, high, ch)
-    grad_send, united_send, kept = call(
+    grad_send, kept, united_kept = call(
         functools.partial(temporal_kernel, narrow_step),
-        [((frames, block, ch), BF16, HBM)] * 2 + [((6,) + whole, BF16, HBM)],
+        [
+            ((frames, block, ch), BF16, HBM),
+            ((SPARE,) + whole, BF16, HBM),
+            ((SPARE, frames, block, ch), BF16, HBM),
+        ],
         [
             pltpu.VMEM(padded, BF16),
             pltpu.VMEM(padded, BF16),
@@ -534,12 +554,13 @@
             (dilation, SMEM), (key_index, SMEM), (got, VMEM),
             (temporal_weight, HBM), (uniting_weight, HBM),
         ],
-        TIME_VMEM,
+        MID_VMEM,
     )
     grad_time = exchange(grad_send).reshape(rows, cols, ch)
-    time_pieces = call(
+    united_send, *time_pieces = call(
         functools.partial(temporal_wgrad_kernel, step_frames, scale),
-        [((time_rows + unite_rows, ch), BF16, VMEM)] * peers,
+        [((frames, block, ch), BF16, HBM)]
+        + [((time_rows + unite_rows, ch), BF16, VMEM)] * peers,
         [
             pltpu.VMEM(padded, BF16),
             pltpu.VMEM(whole, BF16),
@@ -547,49 +568,49 @@
             pltpu.VMEM(whole, BF16),
             pltpu.VMEM(whole, BF16),
             pltpu.VMEM(whole, BF16),
+            pltpu.VMEM((frames, block, ch), BF16),
             pltpu.VMEM((peers, time_rows + unite_rows, ch), F32),
-            pltpu.SemaphoreType.DMA((6,)),
+            pltpu.SemaphoreType.DMA((8,)),
         ],
         2 * 12 * frames * block * ch * ch,
         frames * block * ch * 14,
         [
             (here, SMEM), (dilation, SMEM), (key_index, SMEM),
-            (kept, HBM),
-        ],
-    )
-    (space_slope,) = call(
-        copy_kernel,
-        [((rows, cols, ch), BF16, VMEM)],
-        [],
-        0,
-        pixels * ch * 4,
-        [(space_slope, VMEM)],
-        MID_VMEM,
+            (kept, HBM), (united_kept, HBM),
+        ],
     )
     time_sum = reduce_in_grp(time_pieces)
-    time_sum, space_slope, grad_time = lax.optimization_barrier((time_sum, space_slope, grad_time))
+    time_sum, grad_time = lax.optimization_barrier((time_sum, grad_time))
     united_send, grad_time = lax.optimization_barrier((united_send, grad_time))
     united = exchange(united_send)
     space_pieces = call(
         functools.partial(spatial_wgrad_kernel, rows_step, scale),
         [((space_rows, ch), BF16, VMEM)] * peers,
-        [pltpu.VMEM((rows + 2, wide, ch), BF16), pltpu.VMEM((peers, space_rows, ch), F32)],
+        [
+            pltpu.VMEM((rows + 2, wide, ch), BF16),
+            pltpu.VMEM((rows, cols, ch), BF16),
+            pltpu.VMEM((3 * ch, rows * wide), BF16),
+            pltpu.VMEM((peers, space_rows, ch), F32),
+            pltpu.SemaphoreType.DMA((1,)),
+        ],
         2 * 9 * pixels * ch * ch,
         pixels * ch * 8,
-        [(here, SMEM), (grad_time, VMEM), (space_slope, VMEM), (frame, VMEM)],
+        [(here, SMEM), (grad_time, VMEM), (space_slope, HBM), (frame, VMEM)],
         MID_VMEM,
     )
     (back,) = call(
         functools.partial(spatial_back_kernel, rows_step),
         [((rows, cols, ch), BF16, VMEM)],
-        [pltpu.VMEM((rows + 2, wide, ch), BF16)],
+        [
+            pltpu.VMEM((rows + 2, wide, ch), BF16),
+            pltpu.VMEM((rows, cols, ch), BF16),
+            pltpu.SemaphoreType.DMA((1,)),
+        ],
         2 * 9 * pixels * ch * ch,
         pixels * ch * 6,
-        [(spatial_weight, VMEM), (grad_time, VMEM), (space_slope, VMEM)],
+        [(spatial_weight, VMEM), (grad_time, VMEM), (space_slope, HBM)],
         MID_VMEM,
     )
-    space_pieces = list(space_pieces)
-    space_pieces[0], back = lax.optimization_barrier((space_pieces[0], back))
     space_parts = [flip(part, peer) if peer else part for peer, part in enumerate(space_pieces)]
     (plane,) = call(
         join_kernel,
@@ -600,12 +621,15 @@
         [(time_sum, VMEM)] + [(part, VMEM) for part in space_parts],
         SMALL_VMEM,
     )
-    piece = sum_of(all_turns(plane))
+    turned = all_turns(plane)
+    turned[0], back = lax.optimization_barrier((turned[0], back))
+    piece = sum_of(turned)
     *grads, united = call(
         deal_kernel,
-        [((peers, count, ch), F32, VMEM) for count in (time_rows, unite_rows, space_rows)]
+        [((peers, count, ch), F32, HBM) for count in (time_rows, unite_rows, space_rows)]
         + [((frames, block, ch), BF16, HBM)],
-        [pltpu.SemaphoreType.DMA((1,))],
+        [pltpu.VMEM((peers, count, ch), F32) for count in (time_rows, unite_rows, space_rows)]
+        + [pltpu.SemaphoreType.DMA((4,))],
         0,
         6 * 21 * ch * ch,
         [(lax.all_gather(piece, "grp", axis=0), VMEM), (united, HBM)],

time: 150 us -> 146 us (0.973)
  local copies, waits for them, and re-layouts: 3.53 us -> 0.83 us
  starting transfers between devices: 36.1 us -> 33.9 us
    ppermute x14, waiting for transfers between devices: 5.29 us -> 10.4 us  [flip(): return lax.ppermute(value, 'grp', [(i, i ^ peer) for i in range(size)])]
    ppermute x3, waiting for transfers between devices: 7.63 us -> 4.35 us  [turn_by(): lax.ppermute(value, 'seg', [(i, (i + turn) % size) for i in range(size)])]
    ppermute x14, starting transfers between devices: 15.8 us -> 12.7 us  [flip(): return lax.ppermute(value, 'grp', [(i, i ^ peer) for i in range(size)])]
    unnamed x18 -> x16, local copies, waits for them, and re-layouts: 3.53 us -> 0.83 us
    pallas_call x11 -> x10, Pallas kernels: 40.5 us -> 40.4 us  [call(): pl.pallas_call(kernel, out_shape=[jax.ShapeDtypeStruct(shape, kind) for s...]
  transfers between devices with their start and end apart: 20 -> 20, of which waited for: 7 -> 10; matrix products, arithmetic and copies ran while one was open for 0% -> 0% of each run, Pallas kernels for 13% -> 16%
where the time goes in v11:
time: 146 us; the launch traced here: 145 us
  waiting for transfers between devices  58.1 us (40%)
  Pallas kernels  40.4 us (28%)
  starting transfers between devices  33.9 us (23%)
  blocking collectives  10.2 us (7%)
    all_to_all x3, waiting for transfers between devices, exchange(): return lax.all_to_all(blocks, AXES, split_axis=0, concat_axis=0, tiled=True)  43.3 us
    pallas_call x10, Pallas kernels, call(): pl.pallas_call(kernel, out_shape=[jax.ShapeDtypeStruct(shape, kind) for s...  40.4 us
    all_to_all x3, starting transfers between devices, exchange(): return lax.all_to_all(blocks, AXES, split_axis=0, concat_axis=0, tiled=True)  15.3 us
    ppermute x14, starting transfers between devices, flip(): return lax.ppermute(value, 'grp', [(i, i ^ peer) for i in range(size)])  12.7 us
    ppermute x14, waiting for transfers between devices, flip(): return lax.ppermute(value, 'grp', [(i, i ^ peer) for i in range(size)])  10.4 us
    all_gather x1, blocking collectives, local(): lax.all_gather(piece, 'grp', axis=0)  10.2 us
    ppermute x3, starting transfers between devices, turn_by(): lax.ppermute(value, 'seg', [(i, (i + turn) % size) for i in range(size)])  5.91 us
    ppermute x3, waiting for transfers between devices, turn_by(): lax.ppermute(value, 'seg', [(i, (i + turn) % size) for i in range(size)])  4.35 us
  transfers between devices with their start and end apart: 20, of which 10 were waited for; matrix products, arithmetic and copies ran while one was open for 0% of the time, Pallas kernels for 16%

profile of v11, /device:TPU:0, one launch (start us, length us, event | category | flops | bytes accessed | tf_op | source)
XLA Modules:
  0.0 145.1 jit_solution(4005077833635896077)
XLA Ops:
  0.6 0.0 copy-start.5
  0.7 0.0 copy-start.4
  0.7 4.8 %shard_map.110 = bf16[32,2,120,128]{3,2,1,0:T(8,128)(2,1)} custom-call(bf16[32,120,128]{2,1,0:T(8,128)(2,1)} %bitcast.10, bf16[9,128,128]{2,1,0:T(8,128)(2,1)} %w_ref.3, bf16[32,120,128]{2,1,0:T(8,128)(2,1)} %bitcast.14), custom_call_target="tpu_custom_call" | custom-call | flops 1132462080 | bytes 3932160 | tf_op jit(solution)/shard_map/pallas_call | solution.py:58
  5.5 7.5 %all-to-all-start = ((bf16[32,2,120,128]{3,2,1,0:T(8,128)(2,1)}), bf16[32,2,120,128]{3,2,1,0:T(8,128)(2,1)S(1)}, u32[]{:S(2)}, u32[]{:S(2)}) async-start(bf16[32,2,120,128]{3,2,1,0:T(8,128)(2,1)} %shard_map.110), calls=%async_computation | async-start | bytes 3932160 | tf_op jit(solution)/shard_map/all_to_all | solution.py:439
  13.0 4.4 %shard_map.111.slope_hbm = bf16[28,32,120,128]{3,2,1,0:T(8,128)(2,1)} custom-call(bf16[32,120,128]{2,1,0:T(8,128)(2,1)} %bitcast.11, bf16[9,128,128]{2,1,0:T(8,128)(2,1)} %w_ref.3), custom_call_target="tpu_custom_call" | custom-call | flops 1132462080 | bytes 1966080 | tf_op jit(solution)/shard_map/pallas_call | solution.py:58
  17.4 41.5 %all-to-all-done.got_ref = bf16[32,2,120,128]{3,2,1,0:T(8,128)(2,1)S(1)} async-done(((bf16[32,2,120,128]{3,2,1,0:T(8,128)(2,1)}), bf16[32,2,120,128]{3,2,1,0:T(8,128)(2,1)S(1)}, u32[]{:S(2)}, u32[]{:S(2)}) %all-to-all-start) | async-done | bytes 1966112 | tf_op jit(solution)/shard_map/all_to_all | solution.py:439
  58.9 11.1 %shard_map.112 = (bf16[32,120,128]{2,1,0:T(8,128)(2,1)}, bf16[28,32,128,128]{3,2,1,0:T(8,128)(2,1)}, bf16[28,32,120,128]{3,2,1,0:T(8,128)(2,1)}) custom-call(s32[2]{0:T(128)S(1)} %copy-done.4, s32[4]{0:T(128)S(1)} %copy-done.5, bf16[32,2,120,128]{3,2,1,0:T(8,128)(2,1)S(1)} %all-to-all-done.got_ref, bf16[2,5,128,128]{3,2,1,0:T(8,128)(2,1)S(1)} %copy-done.6, ...), custom_call_target="tpu_custom_call" | custom-call | flops 2768240640 | bytes 8847360 | tf_op jit(solution)/shard_map/pallas_call | solution.py:58
  70.0 4.2 %all-to-all-start.1 = ((bf16[32,120,128]{2,1,0:T(8,128)(2,1)}), bf16[32,120,128]{2,1,0:T(8,128)(2,1)S(1)}, u32[]{:S(2)}, u32[]{:S(2)}) async-start(bf16[32,120,128]{2,1,0:T(8,128)(2,1)} %get-tuple-element.52), calls=%async_computation.1 | async-start | bytes 1966080 | tf_op jit(solution)/shard_map/all_to_all | solution.py:439
  74.2 0.7 pad_add_fusion.here_ref
  74.8 9.8 %shard_map.113 = (bf16[32,120,128]{2,1,0:T(8,128)(2,1)}, bf16[192,128]{1,0:T(8,128)(2,1)}, bf16[192,128]{1,0:T(8,128)(2,1)}, bf16[192,128]{1,0:T(8,128)(2,1)}, b...) custom-call(s32[2]{0:T(128)} %pad_add_fusion.here_ref, ...), custom_call_target="tpu_custom_call" | custom-call | flops 1509949440 | bytes 6881280 | tf_op jit(solution)/shard_map/pallas_call | solution.py:58
  84.6 0.0 copy-start.1
  84.7 0.1 collective-permute-start
  84.8 1.7 %collective-permute-start.1 = (bf16[192,128]{1,0:T(8,128)(2,1)}, bf16[192,128]{1,0:T(8,128)(2,1)S(1)}, u32[]{:S(2)}, u32[]{:S(2)}) collective-permute-start(bf16[192,128]{1,0:T(8,128)(2,1)} %get-tuple-element.46), channel_id=1, source_target_pairs={{0,2},{1,3},{2,0},{3,1},{4,6},{5,7},{6,4},{7,5},{8,10},{9,11},{10,... | collective-permute-start | bytes 147464 | tf_op jit(solution)/shard_map/ppermute | solution.py:444
  86.4 0.2 collective-permute-start.2
  86.6 1.5 %collective-permute-start.3 = (bf16[192,128]{1,0:T(8,128)(2,1)}, bf16[192,128]{1,0:T(8,128)(2,1)S(1)}, u32[]{:S(2)}, u32[]{:S(2)}) collective-permute-start(bf16[192,128]{1,0:T(8,128)(2,1)} %get-tuple-element.48), channel_id=1, source_target_pairs={{0,4},{1,5},{2,6},{3,7},{4,0},{5,1},{6,2},{7,3},{8,12},{9,13},{10,... | collective-permute-start | bytes 147464 | tf_op jit(solution)/shard_map/ppermute | solution.py:444
  88.1 0.2 collective-permute-start.4
  88.3 0.0 collective-permute-done.refs_1_
  88.3 2.5 %collective-permute-start.5 = (bf16[192,128]{1,0:T(8,128)(2,1)}, bf16[192,128]{1,0:T(8,128)(2,1)S(1)}, u32[]{:S(2)}, u32[]{:S(2)}) collective-permute-start(bf16[192,128]{1,0:T(8,128)(2,1)} %get-tuple-element.50), channel_id=1, source_target_pairs={{0,6},{1,7},{2,4},{3,5},{4,2},{5,3},{6,0},{7,1},{8,14},{9,15},{10,... | collective-permute-start | bytes 147464 | tf_op jit(solution)/shard_map/ppermute | solution.py:444
  90.8 0.2 collective-permute-start.6
  91.0 0.3 collective-permute-done.2.refs_3_
  91.2 0.0 collective-permute-done.3.refs_4_
  91.2 2.4 %collective-permute-done.4.refs_5_ = bf16[192,128]{1,0:T(8,128)(2,1)S(1)} collective-permute-done((bf16[192,128]{1,0:T(8,128)(2,1)}, bf16[192,128]{1,0:T(8,128)(2,1)S(1)}, u32[]{:S(2)}, u32[]{:S(2)}) %collective-permute-start.4) | collective-permute-done | bytes 49184 | tf_op jit(solution)/shard_map/ppermute | solution.py:444
  93.6 2.5 %collective-permute-done.6.refs_7_ = bf16[192,128]{1,0:T(8,128)(2,1)S(1)} collective-permute-done((bf16[192,128]{1,0:T(8,128)(2,1)}, bf16[192,128]{1,0:T(8,128)(2,1)S(1)}, u32[]{:S(2)}, u32[]{:S(2)}) %collective-permute-start.6) | collective-permute-done | bytes 49184 | tf_op jit(solution)/shard_map/ppermute | solution.py:444
  96.1 0.8 copy-done.2
  96.9 0.1 shard_map.114.first_ref
  97.0 1.8 %all-to-all-done.1.got_ref = bf16[32,120,128]{2,1,0:T(8,128)(2,1)S(1)} async-done(((bf16[32,120,128]{2,1,0:T(8,128)(2,1)}), bf16[32,120,128]{2,1,0:T(8,128)(2,1)S(1)}, u32[]{:S(2)}, u32[]{:S(2)}) %all-to-all-start.1) | async-done | bytes 983072 | tf_op jit(solution)/shard_map/all_to_all | solution.py:439
  98.8 3.6 %all-to-all-start.2 = ((bf16[32,120,128]{2,1,0:T(8,128)(2,1)}), bf16[32,120,128]{2,1,0:T(8,128)(2,1)S(1)}, u32[]{:S(2)}, u32[]{:S(2)}) async-start(bf16[32,120,128]{2,1,0:T(8,128)(2,1)} %get-tuple-element.67), calls=%async_computation.2 | async-start | bytes 1966080 | tf_op jit(solution)/shard_map/all_to_all | solution.py:439
  102.4 4.5 %shard_map.115 = (bf16[144,128]{1,0:T(8,128)(2,1)S(1)}, bf16[144,128]{1,0:T(8,128)(2,1)S(1)}, bf16[144,128]{1,0:T(8,128)(2,1)S(1)}, bf16[144,128]{1,0:T(8,128)(2...) custom-call(s32[2]{0:T(128)S(1)} %copy-done.3, ...), custom_call_target="tpu_custom_call" | custom-call | flops 1132462080 | bytes 3932160 | tf_op jit(solution)/shard_map/pallas_call | solution.py:58
  106.9 1.8 %collective-permute-start.10 = (bf16[144,128]{1,0:T(8,128)(2,1)S(1)}, bf16[144,128]{1,0:T(8,128)(2,1)S(1)}, u32[]{:S(2)}, u32[]{:S(2)}) collective-permute-start(bf16[144,128]{1,0:T(8,128)(2,1)S(1)} %get-tuple-element.62), channel_id=1, source_target_pairs={{0,4},{1,5},{2,6},{3,7},{4,0},{5,1},{6,2},{7,3},{8,12},{9,13},{10,... | collective-permute-start | bytes 110600 | tf_op jit(solution)/shard_map/ppermute | solution.py:444
  108.7 0.0 collective-permute-start.11
  108.7 2.4 %collective-permute-start.12 = (bf16[144,128]{1,0:T(8,128)(2,1)S(1)}, bf16[144,128]{1,0:T(8,128)(2,1)S(1)}, u32[]{:S(2)}, u32[]{:S(2)}) collective-permute-start(bf16[144,128]{1,0:T(8,128)(2,1)S(1)} %get-tuple-element.64), channel_id=1, source_target_pairs={{0,6},{1,7},{2,4},{3,5},{4,2},{5,3},{6,0},{7,1},{8,14},{9,15},{10,... | collective-permute-start | bytes 110600 | tf_op jit(solution)/shard_map/ppermute | solution.py:444
  111.1 0.3 collective-permute-start.13
  111.4 0.4 collective-permute-start.7
  111.8 0.0 collective-permute-done.10.refs_4_
  111.8 1.5 %collective-permute-start.8 = (bf16[144,128]{1,0:T(8,128)(2,1)S(1)}, bf16[144,128]{1,0:T(8,128)(2,1)S(1)}, u32[]{:S(2)}, u32[]{:S(2)}) collective-permute-start(bf16[144,128]{1,0:T(8,128)(2,1)S(1)} %get-tuple-element.60), channel_id=1, source_target_pairs={{0,2},{1,3},{2,0},{3,1},{4,6},{5,7},{6,4},{7,5},{8,10},{9,11},{10,... | collective-permute-start | bytes 110600 | tf_op jit(solution)/shard_map/ppermute | solution.py:444
  113.3 1.7 %collective-permute-done.11.refs_5_ = bf16[144,128]{1,0:T(8,128)(2,1)S(1)} collective-permute-done((bf16[144,128]{1,0:T(8,128)(2,1)S(1)}, bf16[144,128]{1,0:T(8,128)(2,1)S(1)}, u32[]{:S(2)}, u32[]{:S(2)}) %collective-permute-start.11) | collective-permute-done | bytes 36896 | tf_op jit(solution)/shard_map/ppermute | solution.py:444
  115.0 0.0 collective-permute-start.9
  115.0 0.0 collective-permute-done.12.refs_6_
  115.0 1.9 %collective-permute-done.13.refs_7_ = bf16[144,128]{1,0:T(8,128)(2,1)S(1)} collective-permute-done((bf16[144,128]{1,0:T(8,128)(2,1)S(1)}, bf16[144,128]{1,0:T(8,128)(2,1)S(1)}, u32[]{:S(2)}, u32[]{:S(2)}) %collective-permute-start.13) | collective-permute-done | bytes 36896 | tf_op jit(solution)/shard_map/ppermute | solution.py:444
  116.9 0.3 collective-permute-done.8.refs_2_
  117.2 1.4 collective-permute-done.9.refs_3_
  118.6 1.3 collective-permute-start.14
  119.9 4.4 %collective-permute-start.15 = (bf16[336,128]{1,0:T(8,128)(2,1)S(1)}, bf16[336,128]{1,0:T(8,128)(2,1)S(1)}, u32[]{:S(2)}, u32[]{:S(2)}) collective-permute-start(bf16[336,128]{1,0:T(8,128)(2,1)S(1)} %shard_map.116.refs_0_), channel_id=1, source_target_pairs={{0,16},{8,24},{16,0},{24,8},{1,17},{9,25},{17,1},{25,9},{2,18},{10... | collective-permute-start | bytes 258056 | tf_op jit(solution)/shard_map/ppermute | solution.py:449
  124.4 0.2 collective-permute-start.16
  124.5 4.3 %shard_map.117 = bf16[32,120,128]{2,1,0:T(8,128)(2,1)} custom-call(bf16[9,128,128]{2,1,0:T(8,128)(2,1)S(1)} %copy-done.1, bf16[32,120,128]{2,1,0:T(8,128)(2,1)S(1)} %all-to-all-done.1.got_ref, bf16[28,32,120,128]{3,2,1,0:T(8,128)(2,1)} %shard_map.111.slope_hbm), custom_call_target="tpu_custom_call" | custom-call | flops 1132462080 | bytes 2949120 | tf_op jit(solution)/shard_map/pallas_call | solution.py:58
  128.9 4.3 %collective-permute-done.15.refs_2_ = bf16[336,128]{1,0:T(8,128)(2,1)S(1)} collective-permute-done((bf16[336,128]{1,0:T(8,128)(2,1)S(1)}, bf16[336,128]{1,0:T(8,128)(2,1)S(1)}, u32[]{:S(2)}, u32[]{:S(2)}) %collective-permute-start.15) | collective-permute-done | bytes 86048 | tf_op jit(solution)/shard_map/ppermute | solution.py:449
  133.3 10.2 %all-gather = bf16[2688,128]{1,0:T(8,128)(2,1)S(1)} all-gather(bf16[336,128]{1,0:T(8,128)(2,1)S(1)} %shard_map.118), channel_id=2, replica_groups=mesh['seg'=4,'grp'=8] {'grp'}, dimensions={0}, use_global_device_ids=true | all-gather | bytes 774144 | tf_op jit(solution)/shard_map/all_gather | solution.py:635
  143.5 1.4 shard_map.119
  (20 shorter events, 0.1 us)
Async XLA Ops:
  0.6 58.2 %copy-start.7 = (bf16[2,128,128]{2,1,0:T(8,128)(2,1)S(1)}, bf16[2,128,128]{2,1,0:T(8,128)(2,1)}, u32[]{:S(2)}) copy-start(bf16[2,128,128]{2,1,0:T(8,128)(2,1)} %uw_hbm.1) | copy-start | bytes 196612
  0.6 58.2 %copy-start.5 = (s32[4]{0:T(128)S(1)}, s32[4]{0:T(128)}, u32[]{:S(2)}) copy-start(s32[4]{0:T(128)} %key_ref.3) | copy-start | bytes 52
  0.7 58.2 %copy-start.4 = (s32[2]{0:T(128)S(1)}, s32[2]{0:T(128)}, u32[]{:S(2)}) copy-start(s32[2]{0:T(128)} %dil_ref.3) | copy-start | bytes 28
  0.7 58.2 %copy-start.6 = (bf16[2,5,128,128]{3,2,1,0:T(8,128)(2,1)S(1)}, bf16[2,5,128,128]{3,2,1,0:T(8,128)(2,1)}, u32[]{:S(2)}) copy-start(bf16[2,5,128,128]{3,2,1,0:T(8,128)(2,1)} %tw_hbm.1) | copy-start | bytes 983044
  5.5 53.4 %all-to-all-start = ((bf16[32,2,120,128]{3,2,1,0:T(8,128)(2,1)}), bf16[32,2,120,128]{3,2,1,0:T(8,128)(2,1)S(1)}, u32[]{:S(2)}, u32[]{:S(2)}) async-start(bf16[32,2,120,128]{3,2,1,0:T(8,128)(2,1)} %shard_map.110), calls=%async_computation | async-start | bytes 3932160 | tf_op jit(solution)/shard_map/all_to_all | solution.py:439
  70.0 28.8 %all-to-all-start.1 = ((bf16[32,120,128]{2,1,0:T(8,128)(2,1)}), bf16[32,120,128]{2,1,0:T(8,128)(2,1)S(1)}, u32[]{:S(2)}, u32[]{:S(2)}) async-start(bf16[32,120,128]{2,1,0:T(8,128)(2,1)} %get-tuple-element.52), calls=%async_computation.1 | async-start | bytes 1966080 | tf_op jit(solution)/shard_map/all_to_all | solution.py:439
  74.8 27.6 %copy-start = (bf16[1,32,120,128]{3,2,1,0:T(8,128)(2,1)S(1)}, bf16[1,32,120,128]{3,2,1,0:T(8,128)(2,1)}, u32[]{:S(2)}) copy-start(bf16[1,32,120,128]{3,2,1,0:T(8,128)(2,1)} %param.7) | copy-start | bytes 2949124
  74.8 27.6 %copy-start.3 = (s32[2]{0:T(128)S(1)}, s32[2]{0:T(128)}, u32[]{:S(2)}) copy-start(s32[2]{0:T(128)} %pad_add_fusion.here_ref) | copy-start | bytes 28
  84.6 39.9 %copy-start.1 = (bf16[9,128,128]{2,1,0:T(8,128)(2,1)S(1)}, bf16[9,128,128]{2,1,0:T(8,128)(2,1)}, u32[]{:S(2)}) copy-start(bf16[9,128,128]{2,1,0:T(8,128)(2,1)} %w_ref.3) | copy-start | bytes 884740
  84.7 3.6 %collective-permute-start = (bf16[192,128]{1,0:T(8,128)(2,1)}, bf16[192,128]{1,0:T(8,128)(2,1)S(1)}, u32[]{:S(2)}, u32[]{:S(2)}) collective-permute-start(bf16[192,128]{1,0:T(8,128)(2,1)} %get-tuple-element.45), channel_id=1, source_target_pairs={{0,1},{1,0},{2,3},{3,2},{4,5},{5,4},{6,7},{7,6},{8,9},{9,8},{10,11... | collective-permute-start | bytes 147464 | tf_op jit(solution)/shard_map/ppermute | solution.py:444
  84.8 6.1 %collective-permute-start.1 = (bf16[192,128]{1,0:T(8,128)(2,1)}, bf16[192,128]{1,0:T(8,128)(2,1)S(1)}, u32[]{:S(2)}, u32[]{:S(2)}) collective-permute-start(bf16[192,128]{1,0:T(8,128)(2,1)} %get-tuple-element.46), channel_id=1, source_target_pairs={{0,2},{1,3},{2,0},{3,1},{4,6},{5,7},{6,4},{7,5},{8,10},{9,11},{10,... | collective-permute-start | bytes 147464 | tf_op jit(solution)/shard_map/ppermute | solution.py:444
  86.4 4.8 %collective-permute-start.2 = (bf16[192,128]{1,0:T(8,128)(2,1)}, bf16[192,128]{1,0:T(8,128)(2,1)S(1)}, u32[]{:S(2)}, u32[]{:S(2)}) collective-permute-start(bf16[192,128]{1,0:T(8,128)(2,1)} %get-tuple-element.47), channel_id=1, source_target_pairs={{0,3},{1,2},{2,1},{3,0},{4,7},{5,6},{6,5},{7,4},{8,11},{9,10},{10,... | collective-permute-start | bytes 147464 | tf_op jit(solution)/shard_map/ppermute | solution.py:444
  86.6 4.7 %collective-permute-start.3 = (bf16[192,128]{1,0:T(8,128)(2,1)}, bf16[192,128]{1,0:T(8,128)(2,1)S(1)}, u32[]{:S(2)}, u32[]{:S(2)}) collective-permute-start(bf16[192,128]{1,0:T(8,128)(2,1)} %get-tuple-element.48), channel_id=1, source_target_pairs={{0,4},{1,5},{2,6},{3,7},{4,0},{5,1},{6,2},{7,3},{8,12},{9,13},{10,... | collective-permute-start | bytes 147464 | tf_op jit(solution)/shard_map/ppermute | solution.py:444
  88.1 5.5 %collective-permute-start.4 = (bf16[192,128]{1,0:T(8,128)(2,1)}, bf16[192,128]{1,0:T(8,128)(2,1)S(1)}, u32[]{:S(2)}, u32[]{:S(2)}) collective-permute-start(bf16[192,128]{1,0:T(8,128)(2,1)} %get-tuple-element.49), channel_id=1, source_target_pairs={{0,5},{1,4},{2,7},{3,6},{4,1},{5,0},{6,3},{7,2},{8,13},{9,12},{10,... | collective-permute-start | bytes 147464 | tf_op jit(solution)/shard_map/ppermute | solution.py:444
  88.3 5.3 %collective-permute-start.5 = (bf16[192,128]{1,0:T(8,128)(2,1)}, bf16[192,128]{1,0:T(8,128)(2,1)S(1)}, u32[]{:S(2)}, u32[]{:S(2)}) collective-permute-start(bf16[192,128]{1,0:T(8,128)(2,1)} %get-tuple-element.50), channel_id=1, source_target_pairs={{0,6},{1,7},{2,4},{3,5},{4,2},{5,3},{6,0},{7,1},{8,14},{9,15},{10,... | collective-permute-start | bytes 147464 | tf_op jit(solution)/shard_map/ppermute | solution.py:444
  90.8 5.3 %collective-permute-start.6 = (bf16[192,128]{1,0:T(8,128)(2,1)}, bf16[192,128]{1,0:T(8,128)(2,1)S(1)}, u32[]{:S(2)}, u32[]{:S(2)}) collective-permute-start(bf16[192,128]{1,0:T(8,128)(2,1)} %get-tuple-element.51), channel_id=1, source_target_pairs={{0,7},{1,6},{2,5},{3,4},{4,3},{5,2},{6,1},{7,0},{8,15},{9,14},{10,... | collective-permute-start | bytes 147464 | tf_op jit(solution)/shard_map/ppermute | solution.py:444
  96.1 0.8 copy-start.2
  98.8 44.8 %all-to-all-start.2 = ((bf16[32,120,128]{2,1,0:T(8,128)(2,1)}), bf16[32,120,128]{2,1,0:T(8,128)(2,1)S(1)}, u32[]{:S(2)}, u32[]{:S(2)}) async-start(bf16[32,120,128]{2,1,0:T(8,128)(2,1)} %get-tuple-element.67), calls=%async_computation.2 | async-start | bytes 1966080 | tf_op jit(solution)/shard_map/all_to_all | solution.py:439
  106.9 4.9 %collective-permute-start.10 = (bf16[144,128]{1,0:T(8,128)(2,1)S(1)}, bf16[144,128]{1,0:T(8,128)(2,1)S(1)}, u32[]{:S(2)}, u32[]{:S(2)}) collective-permute-start(bf16[144,128]{1,0:T(8,128)(2,1)S(1)} %get-tuple-element.62), channel_id=1, source_target_pairs={{0,4},{1,5},{2,6},{3,7},{4,0},{5,1},{6,2},{7,3},{8,12},{9,13},{10,... | collective-permute-start | bytes 110600 | tf_op jit(solution)/shard_map/ppermute | solution.py:444
  108.7 6.2 %collective-permute-start.11 = (bf16[144,128]{1,0:T(8,128)(2,1)S(1)}, bf16[144,128]{1,0:T(8,128)(2,1)S(1)}, u32[]{:S(2)}, u32[]{:S(2)}) collective-permute-start(bf16[144,128]{1,0:T(8,128)(2,1)S(1)} %get-tuple-element.63), channel_id=1, source_target_pairs={{0,5},{1,4},{2,7},{3,6},{4,1},{5,0},{6,3},{7,2},{8,13},{9,12},{10,... | collective-permute-start | bytes 110600 | tf_op jit(solution)/shard_map/ppermute | solution.py:444
  108.7 6.2 %collective-permute-start.12 = (bf16[144,128]{1,0:T(8,128)(2,1)S(1)}, bf16[144,128]{1,0:T(8,128)(2,1)S(1)}, u32[]{:S(2)}, u32[]{:S(2)}) collective-permute-start(bf16[144,128]{1,0:T(8,128)(2,1)S(1)} %get-tuple-element.64), channel_id=1, source_target_pairs={{0,6},{1,7},{2,4},{3,5},{4,2},{5,3},{6,0},{7,1},{8,14},{9,15},{10,... | collective-permute-start | bytes 110600 | tf_op jit(solution)/shard_map/ppermute | solution.py:444
  111.1 5.7 %collective-permute-start.13 = (bf16[144,128]{1,0:T(8,128)(2,1)S(1)}, bf16[144,128]{1,0:T(8,128)(2,1)S(1)}, u32[]{:S(2)}, u32[]{:S(2)}) collective-permute-start(bf16[144,128]{1,0:T(8,128)(2,1)S(1)} %get-tuple-element.65), channel_id=1, source_target_pairs={{0,7},{1,6},{2,5},{3,4},{4,3},{5,2},{6,1},{7,0},{8,15},{9,14},{10,... | collective-permute-start | bytes 110600 | tf_op jit(solution)/shard_map/ppermute | solution.py:444
  111.4 5.4 %collective-permute-start.7 = (bf16[144,128]{1,0:T(8,128)(2,1)S(1)}, bf16[144,128]{1,0:T(8,128)(2,1)S(1)}, u32[]{:S(2)}, u32[]{:S(2)}) collective-permute-start(bf16[144,128]{1,0:T(8,128)(2,1)S(1)} %get-tuple-element.59), channel_id=1, source_target_pairs={{0,1},{1,0},{2,3},{3,2},{4,5},{5,4},{6,7},{7,6},{8,9},{9,8},{10,11... | collective-permute-start | bytes 110600 | tf_op jit(solution)/shard_map/ppermute | solution.py:444
  111.8 5.4 %collective-permute-start.8 = (bf16[144,128]{1,0:T(8,128)(2,1)S(1)}, bf16[144,128]{1,0:T(8,128)(2,1)S(1)}, u32[]{:S(2)}, u32[]{:S(2)}) collective-permute-start(bf16[144,128]{1,0:T(8,128)(2,1)S(1)} %get-tuple-element.60), channel_id=1, source_target_pairs={{0,2},{1,3},{2,0},{3,1},{4,6},{5,7},{6,4},{7,5},{8,10},{9,11},{10,... | collective-permute-start | bytes 110600 | tf_op jit(solution)/shard_map/ppermute | solution.py:444
  115.0 3.6 %collective-permute-start.9 = (bf16[144,128]{1,0:T(8,128)(2,1)S(1)}, bf16[144,128]{1,0:T(8,128)(2,1)S(1)}, u32[]{:S(2)}, u32[]{:S(2)}) collective-permute-start(bf16[144,128]{1,0:T(8,128)(2,1)S(1)} %get-tuple-element.61), channel_id=1, source_target_pairs={{0,3},{1,2},{2,1},{3,0},{4,7},{5,6},{6,5},{7,4},{8,11},{9,10},{10,... | collective-permute-start | bytes 110600 | tf_op jit(solution)/shard_map/ppermute | solution.py:444
  118.6 10.3 %collective-permute-start.14 = (bf16[336,128]{1,0:T(8,128)(2,1)S(1)}, bf16[336,128]{1,0:T(8,128)(2,1)S(1)}, u32[]{:S(2)}, u32[]{:S(2)}) collective-permute-start(bf16[336,128]{1,0:T(8,128)(2,1)S(1)} %shard_map.116.refs_0_), channel_id=1, source_target_pairs={{0,8},{8,16},{16,24},{24,0},{1,9},{9,17},{17,25},{25,1},{2,10},{10... | collective-permute-start | bytes 258056 | tf_op jit(solution)/shard_map/ppermute | solution.py:449
  119.9 13.3 %collective-permute-start.15 = (bf16[336,128]{1,0:T(8,128)(2,1)S(1)}, bf16[336,128]{1,0:T(8,128)(2,1)S(1)}, u32[]{:S(2)}, u32[]{:S(2)}) collective-permute-start(bf16[336,128]{1,0:T(8,128)(2,1)S(1)} %shard_map.116.refs_0_), channel_id=1, source_target_pairs={{0,16},{8,24},{16,0},{24,8},{1,17},{9,25},{17,1},{25,9},{2,18},{10... | collective-permute-start | bytes 258056 | tf_op jit(solution)/shard_map/ppermute | solution.py:449
  124.4 8.9 %collective-permute-start.16 = (bf16[336,128]{1,0:T(8,128)(2,1)S(1)}, bf16[336,128]{1,0:T(8,128)(2,1)S(1)}, u32[]{:S(2)}, u32[]{:S(2)}) collective-permute-start(bf16[336,128]{1,0:T(8,128)(2,1)S(1)} %shard_map.116.refs_0_), channel_id=1, source_target_pairs={{0,24},{8,0},{16,8},{24,16},{1,25},{9,1},{17,9},{25,17},{2,26},{10... | collective-permute-start | bytes 258056 | tf_op jit(solution)/shard_map/ppermute | solution.py:449

commit v12 on v11

--- a/solution.py
+++ b/solution.py
@@ -186,15 +186,21 @@
     load = pltpu.make_async_copy(slope_hbm.at[0], slopes, sem.at[0])
     load.start()
     pad = jnp.zeros((rows_step, wide - cols, ch), F32)
-    for at in range(0, rows, rows_step):
+
+    def columns(at):
         x = jnp.concatenate([x_ref[at : at + rows_step].astype(F32), pad], axis=1).reshape(flat, ch)
         x_cat = jnp.concatenate([roll_rows(x, 1), x, roll_rows(x, -1)], axis=1)
-        cat_ref[:, at * wide : at * wide + flat] = x_cat.T.astype(BF16)
+        return x_cat.T.astype(BF16)
+
+    early = cat_ref.shape[1] // flat
+    for n in range(early):
+        cat_ref[:, n * flat : (n + 1) * flat] = columns(n * rows_step)
     load.wait()
     fill_grads(rows_step, gs, got_ref, slopes)
     total = jnp.zeros((3 * ch, 3 * ch), F32)
-    for at in range(0, rows, rows_step):
-        total = total + mm(cat_ref[:, at * wide : at * wide + flat], taps_up(gs, at, rows_step))
+    for n, at in enumerate(range(0, rows, rows_step)):
+        cat = cat_ref[:, n * flat : (n + 1) * flat] if n < early else columns(at)
+        total = total + mm(cat, taps_up(gs, at, rows_step))
     total_ref[...] = (
         jnp.concatenate(
             [
@@ -245,19 +251,12 @@
 
 
 def temporal_kernel(
-    step_frames, dil_ref, key_ref, got_ref, tw_hbm, uw_hbm,
+    step_frames, dil_ref, key_ref, got_ref, tw_ref, uw_ref,
     grad_hbm, kept_hbm, united_hbm,
-    a0, a1, feat, cots, g0, g1, slope0, slope1, united_ref, grad_ref, tw_ref, uw_ref,
-    sems, in_sems, out_sems,
+    a0, a1, feat, cots, g0, g1, slope0, slope1, united_ref, grad_ref, sems, out_sems,
 ):
     frames, _, block, ch = got_ref.shape
     high = feat.shape[1]
-    loads = [
-        pltpu.make_async_copy(source, ref, in_sems.at[n])
-        for n, (source, ref) in enumerate(((tw_hbm, tw_ref), (uw_hbm, uw_ref)))
-    ]
-    for load in loads:
-        load.start()
     stores = [
         pltpu.make_async_copy(
             grad_ref.at[pl.ds(at, step_frames)], grad_hbm.at[pl.ds(at, step_frames)], out_sems.at[n]
@@ -275,9 +274,7 @@
                 (feat, kept_hbm.at[1]),
                 (g1.at[inside], kept_hbm.at[2]),
                 (g0.at[inside], kept_hbm.at[3]),
-                (a0.at[inside], kept_hbm.at[4]),
-                (cots, kept_hbm.at[5]),
-                (united_ref, united_hbm.at[0]),
+                (united_ref, united_hbm),
             )
         )
     ]
@@ -288,9 +285,6 @@
         a0[HALO : HALO + frames, block:, :] = pad
         cots[:, block:, :] = pad
     a0[HALO : HALO + frames, :block, :] = got_ref[:, 0]
-    copies[4].start()
-    for load in loads:
-        load.wait()
     for layer, (source, target, slopes) in enumerate(((a0, a1, slope0), (a1, feat, slope1))):
         step_size = dil_ref[layer]
         weight = jnp.concatenate([tw_ref[layer, k] for k in range(TAPS)], axis=0)
@@ -304,7 +298,6 @@
             slopes[at : at + step_frames] = slope.reshape(step_frames, high, ch)
         copies[layer].start()
     cots[:, :block, :] = got_ref[:, 1]
-    copies[5].start()
     for seg in range(segs):
         low, top = seg * seg_frames, (seg + 1) * seg_frames
         here = low + key_ref[seg]
@@ -322,7 +315,7 @@
         for n in range(seg_frames):
             grad = grad_feat[n] + jnp.where(key_ref[seg] == n, key_term, 0.0)
             g1[HALO + low + n] = (grad * slope1[low + n]).astype(BF16)
-    copies[6].start()
+    copies[4].start()
     for layer, source in ((1, g1), (0, g0)):
         copies[3 - layer].start()
         step_size = dil_ref[layer]
@@ -345,37 +338,33 @@
 
 
 def temporal_wgrad_kernel(
-    step_frames, scale, here_ref, dil_ref, key_ref,
-    kept_hbm, united_kept, united_hbm, *rest
+    step_frames, scale, here_ref, dil_ref, key_ref, got_ref, kept_hbm, *rest
 ):
-    pieces, (a0, g0, a1, g1, feat, cots, united, total_ref, sems) = rest[:-9], rest[-9:]
+    pieces, (a0, g0, a1, g1, feat, cots, total_ref, sems) = rest[:-8], rest[-8:]
     frames, high, ch = feat.shape
+    block = got_ref.shape[2]
     segs = key_ref.shape[0]
     seg_frames = frames // segs
     rows = step_frames * high
     inside = pl.ds(HALO, frames)
     copies = [
-        pltpu.make_async_copy(source, target, sems.at[n])
-        for n, (source, target) in enumerate(
-            (
-                (kept_hbm.at[4], a0.at[inside]),
-                (kept_hbm.at[3], g0),
-                (kept_hbm.at[0], a1.at[inside]),
-                (kept_hbm.at[2], g1),
-                (kept_hbm.at[1], feat),
-                (kept_hbm.at[5], cots),
-                (united_kept.at[0], united),
-            )
-        )
+        pltpu.make_async_copy(kept_hbm.at[n], target, sems.at[n])
+        for n, target in ((3, g0), (0, a1.at[inside]), (2, g1), (1, feat))
     ]
     for copy in copies:
         copy.start()
     clear_halo(a0, frames)
     clear_halo(a1, frames)
+    if high > block:
+        pad = jnp.zeros((frames, high - block, ch), BF16)
+        a0[HALO : HALO + frames, block:, :] = pad
+        cots[:, block:, :] = pad
+    a0[HALO : HALO + frames, :block, :] = got_ref[:, 0]
+    cots[:, :block, :] = got_ref[:, 1]
     totals = []
     for layer, acts, grads in ((0, a0, g0), (1, a1, g1)):
-        copies[2 * layer].wait()
-        copies[2 * layer + 1].wait()
+        for copy in copies[1:3] if layer else copies[:1]:
+            copy.wait()
         total = jnp.zeros((TAPS * ch, ch), F32)
         for at in range(0, frames, step_frames):
             total = total + mm_tn(
@@ -383,10 +372,7 @@
                 grads[at : at + step_frames].reshape(rows, ch),
             )
         totals.append(total)
-    for copy in copies[4:]:
-        copy.wait()
-    united_copy = pltpu.make_async_copy(united, united_hbm, sems.at[len(copies)])
-    united_copy.start()
+    copies[3].wait()
     total = jnp.zeros((ch, ch), F32)
     for at in range(0, frames, step_frames):
         total = total + mm_tn(
@@ -406,18 +392,18 @@
         peers, 2 * ch // peers, ch
     )
     hand_out(here_ref, total_ref, pieces)
-    united_copy.wait()
 
 
 def sum_kernel(*refs):
     refs[-1][...] = sum(ref[...].astype(F32) for ref in refs[:-1]).astype(refs[-1].dtype)
 
 
-def join_kernel(first_ref, *refs):
-    out_ref = refs[-1]
-    split = first_ref.shape[0]
-    out_ref[:split] = first_ref[...]
-    out_ref[split:] = sum(ref[...].astype(F32) for ref in refs[:-1]).astype(out_ref.dtype)
+def join_kernel(*refs):
+    *parts, out_ref = refs
+    half = len(parts) // 2
+    split = parts[0].shape[0]
+    out_ref[:split] = sum(ref[...].astype(F32) for ref in parts[:half]).astype(out_ref.dtype)
+    out_ref[split:] = sum(ref[...].astype(F32) for ref in parts[half:]).astype(out_ref.dtype)
 
 
 def deal_kernel(pieces_ref, united_hbm, *refs):
@@ -479,11 +465,9 @@
     wide = round_up(cols + 1, 16)
     high = round_up(block, 16)
     rows_step = next(n for n in (4, 2, 1) if rows % n == 0)
+    steps = rows // rows_step
     parts = next(n for n in (4, 2, 1) if rows % (n * rows_step) == 0)
-    step_frames, narrow_step = (
-        max(n for n in range(1, frames + 1) if frames % n == 0 and n * high <= most)
-        for most in (512, 256)
-    )
+    step_frames = max(n for n in range(1, frames + 1) if frames % n == 0 and n * high <= 512)
     scale = float((frames * pixels) ** -0.5)
     here = jnp.stack([lax.axis_index("seg"), lax.axis_index("grp")]).astype(jnp.int32)
     space_rows, time_rows, unite_rows = (n * ch // peers for n in (9, LAYERS * TAPS, 2))
@@ -524,12 +508,12 @@
 
     padded = (frames + 2 * HALO, high, ch)
     whole = (frames, high, ch)
-    grad_send, kept, united_kept = call(
-        functools.partial(temporal_kernel, narrow_step),
+    grad_send, kept, united_send = call(
+        functools.partial(temporal_kernel, step_frames),
         [
             ((frames, block, ch), BF16, HBM),
             ((SPARE,) + whole, BF16, HBM),
-            ((SPARE, frames, block, ch), BF16, HBM),
+            ((frames, block, ch), BF16, HBM),
         ],
         [
             pltpu.VMEM(padded, BF16),
@@ -542,25 +526,21 @@
             pltpu.VMEM(whole, F32),
             pltpu.VMEM((frames, block, ch), BF16),
             pltpu.VMEM((frames, block, ch), BF16),
-            pltpu.VMEM(temporal_weight.shape, BF16),
-            pltpu.VMEM(uniting_weight.shape, BF16),
-            pltpu.SemaphoreType.DMA((7,)),
-            pltpu.SemaphoreType.DMA((2,)),
-            pltpu.SemaphoreType.DMA((frames // narrow_step,)),
+            pltpu.SemaphoreType.DMA((5,)),
+            pltpu.SemaphoreType.DMA((frames // step_frames,)),
         ],
         2 * 22 * frames * block * ch * ch,
         frames * block * ch * 18,
         [
             (dilation, SMEM), (key_index, SMEM), (got, VMEM),
-            (temporal_weight, HBM), (uniting_weight, HBM),
+            (temporal_weight, VMEM), (uniting_weight, VMEM),
         ],
         MID_VMEM,
     )
     grad_time = exchange(grad_send).reshape(rows, cols, ch)
-    united_send, *time_pieces = call(
+    time_pieces = call(
         functools.partial(temporal_wgrad_kernel, step_frames, scale),
-        [((frames, block, ch), BF16, HBM)]
-        + [((time_rows + unite_rows, ch), BF16, VMEM)] * peers,
+        [((time_rows + unite_rows, ch), BF16, VMEM)] * peers,
         [
             pltpu.VMEM(padded, BF16),
             pltpu.VMEM(whole, BF16),
@@ -568,28 +548,27 @@
             pltpu.VMEM(whole, BF16),
             pltpu.VMEM(whole, BF16),
             pltpu.VMEM(whole, BF16),
-            pltpu.VMEM((frames, block, ch), BF16),
             pltpu.VMEM((peers, time_rows + unite_rows, ch), F32),
-            pltpu.SemaphoreType.DMA((8,)),
+            pltpu.SemaphoreType.DMA((4,)),
         ],
         2 * 12 * frames * block * ch * ch,
         frames * block * ch * 14,
         [
-            (here, SMEM), (dilation, SMEM), (key_index, SMEM),
-            (kept, HBM), (united_kept, HBM),
-        ],
-    )
-    time_sum = reduce_in_grp(time_pieces)
-    time_sum, grad_time = lax.optimization_barrier((time_sum, grad_time))
+            (here, SMEM), (dilation, SMEM), (key_index, SMEM), (got, VMEM), (kept, HBM),
+        ],
+        MID_VMEM,
+    )
+    time_turned = all_turns(reduce_in_grp(time_pieces))
     united_send, grad_time = lax.optimization_barrier((united_send, grad_time))
     united = exchange(united_send)
+    *time_turned, grad_time = lax.optimization_barrier((*time_turned, grad_time))
     space_pieces = call(
         functools.partial(spatial_wgrad_kernel, rows_step, scale),
         [((space_rows, ch), BF16, VMEM)] * peers,
         [
             pltpu.VMEM((rows + 2, wide, ch), BF16),
             pltpu.VMEM((rows, cols, ch), BF16),
-            pltpu.VMEM((3 * ch, rows * wide), BF16),
+            pltpu.VMEM((3 * ch, min(3, steps) * rows_step * wide), BF16),
             pltpu.VMEM((peers, space_rows, ch), F32),
             pltpu.SemaphoreType.DMA((1,)),
         ],
@@ -611,19 +590,17 @@
         [(spatial_weight, VMEM), (grad_time, VMEM), (space_slope, HBM)],
         MID_VMEM,
     )
-    space_parts = [flip(part, peer) if peer else part for peer, part in enumerate(space_pieces)]
-    (plane,) = call(
+    turned = all_turns(reduce_in_grp(space_pieces))
+    turned[0], back = lax.optimization_barrier((turned[0], back))
+    (piece,) = call(
         join_kernel,
         [((time_rows + unite_rows + space_rows, ch), BF16, VMEM)],
         [],
         0,
-        2 * (peers + 10) * space_rows * ch,
-        [(time_sum, VMEM)] + [(part, VMEM) for part in space_parts],
+        2 * 4 * 21 * ch * ch,
+        [(part, VMEM) for part in time_turned + turned],
         SMALL_VMEM,
     )
-    turned = all_turns(plane)
-    turned[0], back = lax.optimization_barrier((turned[0], back))
-    piece = sum_of(turned)
     *grads, united = call(
         deal_kernel,
         [((peers, count, ch), F32, HBM) for count in (time_rows, unite_rows, space_rows)]

time: 146 us -> 168 us (1.15)
  blocking collectives: 10.2 us -> 38 us
  waiting for transfers between devices: 58.1 us -> 53.6 us
  local copies, waits for them, and re-layouts: 0.83 us -> 2.55 us
    all_to_all x0 -> x1, blocking collectives: none -> 28.6 us  [exchange(): return lax.all_to_all(blocks, AXES, split_axis=0, concat_axis=0, tiled=True)]
    all_to_all x3 -> x2, starting transfers between devices: 15.3 us -> 11.3 us  [exchange(): return lax.all_to_all(blocks, AXES, split_axis=0, concat_axis=0, tiled=True)]
    ppermute x14, waiting for transfers between devices: 10.4 us -> 7.12 us  [flip(): return lax.ppermute(value, 'grp', [(i, i ^ peer) for i in range(size)])]
    ppermute x3 -> x6, starting transfers between devices: 5.91 us -> 9.13 us  [turn_by(): lax.ppermute(value, 'seg', [(i, (i + turn) % size) for i in range(size)])]
    all_to_all x3 -> x2, waiting for transfers between devices: 43.3 us -> 41.5 us  [exchange(): return lax.all_to_all(blocks, AXES, split_axis=0, concat_axis=0, tiled=True)]
    unnamed x16 -> x18, local copies, waits for them, and re-layouts: 0.83 us -> 2.55 us
    ppermute x3 -> x6, waiting for transfers between devices: 4.35 us -> 5.01 us  [turn_by(): lax.ppermute(value, 'seg', [(i, (i + turn) % size) for i in range(size)])]
  transfers between devices with their start and end apart: 20 -> 22, of which waited for: 10 -> 8; matrix products, arithmetic and copies ran while one was open for 0% -> 0% of each run, Pallas kernels for 16% -> 12%
where the time goes in v12:
time: 168 us
  waiting for transfers between devices  53.6 us (32%)
  Pallas kernels  38.8 us (23%)
  blocking collectives  38 us (23%)
  starting transfers between devices  33.5 us (20%)
  local copies, waits for them, and re-layouts  2.55 us (2%)
    all_to_all x2, waiting for transfers between devices, exchange(): return lax.all_to_all(blocks, AXES, split_axis=0, concat_axis=0, tiled=True)  41.5 us
    pallas_call x10, Pallas kernels, call(): pl.pallas_call(kernel, out_shape=[jax.ShapeDtypeStruct(shape, kind) for s...  38.8 us
    all_to_all x1, blocking collectives, exchange(): return lax.all_to_all(blocks, AXES, split_axis=0, concat_axis=0, tiled=True)  28.6 us
    ppermute x14, starting transfers between devices, flip(): return lax.ppermute(value, 'grp', [(i, i ^ peer) for i in range(size)])  13.1 us
    all_to_all x2, starting transfers between devices, exchange(): return lax.all_to_all(blocks, AXES, split_axis=0, concat_axis=0, tiled=True)  11.3 us
    all_gather x1, blocking collectives, local(): lax.all_gather(piece, 'grp', axis=0)  9.38 us
    ppermute x6, starting transfers between devices, turn_by(): lax.ppermute(value, 'seg', [(i, (i + turn) % size) for i in range(size)])  9.13 us
    ppermute x14, waiting for transfers between devices, flip(): return lax.ppermute(value, 'grp', [(i, i ^ peer) for i in range(size)])  7.12 us
  transfers between devices with their start and end apart: 22, of which 8 were waited for; matrix products, arithmetic and copies ran while one was open for 0% of the time, Pallas kernels for 12%

profile of v12, /device:TPU:0, one launch (start us, length us, event | category | flops | bytes accessed | tf_op | source)
XLA Modules:
  0.0 167.6 jit_solution(16086683816010346852)
XLA Ops:
  0.7 4.8 %shard_map.110 = bf16[32,2,120,128]{3,2,1,0:T(8,128)(2,1)} custom-call(bf16[32,120,128]{2,1,0:T(8,128)(2,1)} %bitcast.10, bf16[9,128,128]{2,1,0:T(8,128)(2,1)} %w_ref.3, bf16[32,120,128]{2,1,0:T(8,128)(2,1)} %bitcast.14), custom_call_target="tpu_custom_call" | custom-call | flops 1132462080 | bytes 3932160 | tf_op jit(solution)/shard_map/pallas_call | solution.py:58
  5.4 7.5 %all-to-all-start = ((bf16[32,2,120,128]{3,2,1,0:T(8,128)(2,1)}), bf16[32,2,120,128]{3,2,1,0:T(8,128)(2,1)S(1)}, u32[]{:S(2)}, u32[]{:S(2)}) async-start(bf16[32,2,120,128]{3,2,1,0:T(8,128)(2,1)} %shard_map.110), calls=%async_computation | async-start | bytes 3932160 | tf_op jit(solution)/shard_map/all_to_all | solution.py:425
  12.9 4.4 %shard_map.111.slope_hbm = bf16[28,32,120,128]{3,2,1,0:T(8,128)(2,1)} custom-call(bf16[32,120,128]{2,1,0:T(8,128)(2,1)} %bitcast.11, bf16[9,128,128]{2,1,0:T(8,128)(2,1)} %w_ref.3), custom_call_target="tpu_custom_call" | custom-call | flops 1132462080 | bytes 1966080 | tf_op jit(solution)/shard_map/pallas_call | solution.py:58
  17.3 0.0 copy-start
  17.4 41.5 %all-to-all-done.got_ref = bf16[32,2,120,128]{3,2,1,0:T(8,128)(2,1)S(1)} async-done(((bf16[32,2,120,128]{3,2,1,0:T(8,128)(2,1)}), bf16[32,2,120,128]{3,2,1,0:T(8,128)(2,1)S(1)}, u32[]{:S(2)}, u32[]{:S(2)}) %all-to-all-start) | async-done | bytes 1966112 | tf_op jit(solution)/shard_map/all_to_all | solution.py:425
  58.8 0.0 copy-start.7
  58.9 1.0 copy-done.7
  59.8 11.9 %shard_map.112 = (bf16[32,120,128]{2,1,0:T(8,128)(2,1)S(1)}, bf16[28,32,128,128]{3,2,1,0:T(8,128)(2,1)}, bf16[32,120,128]{2,1,0:T(8,128)(2,1)S(1)}) custom-call(s32[2]{0:T(128)S(1)} %copy-done.5, s32[4]{0:T(128)S(1)} %copy-done.6, bf16[32,2,120,128]{3,2,1,0:T(8,128)(2,1)S(1)} %all-to-all-done.got_ref, bf16[2,5,128,128]{3,2,1,0:T(8,128)(2,1)S(1)} %copy-done.7, ...), custom_call_target="tpu_custom_call" | custom-call | flops 2768240640 | bytes 8847360 | tf_op jit(solution)/shard_map/pallas_call | solution.py:58
  71.7 0.0 copy-start.4
  71.7 28.6 %all_to_all.15.got_ref = bf16[32,120,128]{2,1,0:T(8,128)(2,1)S(1)} all-to-all(bf16[32,120,128]{2,1,0:T(8,128)(2,1)S(1)} %get-tuple-element.54), channel_id=1, replica_groups=mesh['seg'=4,'grp'=8] {'seg','grp'}, dimensions={0} | all-to-all | bytes 1966080 | tf_op jit(solution)/shard_map/all_to_all | solution.py:425
  100.3 3.8 %all-to-all-start.2 = ((bf16[32,120,128]{2,1,0:T(8,128)(2,1)}), bf16[32,120,128]{2,1,0:T(8,128)(2,1)S(1)}, u32[]{:S(2)}, u32[]{:S(2)}) async-start(bf16[32,120,128]{2,1,0:T(8,128)(2,1)} %copy-done.4), calls=%async_computation.2 | async-start | bytes 1966080 | tf_op jit(solution)/shard_map/all_to_all | solution.py:425
  104.2 0.1 pad_add_fusion.here_ref
  104.3 1.5 copy-done.2
  105.8 8.2 %shard_map.113 = (bf16[192,128]{1,0:T(8,128)(2,1)S(1)}, bf16[192,128]{1,0:T(8,128)(2,1)S(1)}, bf16[192,128]{1,0:T(8,128)(2,1)S(1)}, bf16[192,128]{1,0:T(8,128)(2...) custom-call(s32[2]{0:T(128)S(1)} %pad_add_fusion.here_ref, ...), custom_call_target="tpu_custom_call" | custom-call | flops 1509949440 | bytes 6881280 | tf_op jit(solution)/shard_map/pallas_call | solution.py:58
  114.0 0.1 collective-permute-start
  114.1 1.7 %collective-permute-start.1 = (bf16[192,128]{1,0:T(8,128)(2,1)S(1)}, bf16[192,128]{1,0:T(8,128)(2,1)S(1)}, u32[]{:S(2)}, u32[]{:S(2)}) collective-permute-start(bf16[192,128]{1,0:T(8,128)(2,1)S(1)} %get-tuple-element.47), channel_id=1, source_target_pairs={{0,2},{1,3},{2,0},{3,1},{4,6},{5,7},{6,4},{7,5},{8,10},{9,11},{10,... | collective-permute-start | bytes 147464 | tf_op jit(solution)/shard_map/ppermute | solution.py:430
  115.8 0.2 collective-permute-start.2
  116.0 1.5 collective-permute-start.3
  117.5 0.2 collective-permute-start.4
  117.7 0.0 collective-permute-done.refs_1_
  117.7 2.5 %collective-permute-start.5 = (bf16[192,128]{1,0:T(8,128)(2,1)S(1)}, bf16[192,128]{1,0:T(8,128)(2,1)S(1)}, u32[]{:S(2)}, u32[]{:S(2)}) collective-permute-start(bf16[192,128]{1,0:T(8,128)(2,1)S(1)} %get-tuple-element.51), channel_id=1, source_target_pairs={{0,6},{1,7},{2,4},{3,5},{4,2},{5,3},{6,0},{7,1},{8,14},{9,15},{10,... | collective-permute-start | bytes 147464 | tf_op jit(solution)/shard_map/ppermute | solution.py:430
  120.2 0.0 collective-permute-done.1.refs_2_
  120.2 0.6 collective-permute-start.6
  120.8 0.0 collective-permute-done.3.refs_4_
  120.9 3.0 %collective-permute-done.4.refs_5_ = bf16[192,128]{1,0:T(8,128)(2,1)S(1)} collective-permute-done((bf16[192,128]{1,0:T(8,128)(2,1)S(1)}, bf16[192,128]{1,0:T(8,128)(2,1)S(1)}, u32[]{:S(2)}, u32[]{:S(2)}) %collective-permute-start.4) | collective-permute-done | bytes 49184 | tf_op jit(solution)/shard_map/ppermute | solution.py:430
  123.9 1.1 collective-permute-done.6.refs_7_
  125.0 0.1 shard_map.114.refs_0_
  125.1 4.5 %collective-permute-start.9 = (bf16[192,128]{1,0:T(8,128)(2,1)S(1)}, bf16[192,128]{1,0:T(8,128)(2,1)S(1)}, u32[]{:S(2)}, u32[]{:S(2)}) collective-permute-start(bf16[192,128]{1,0:T(8,128)(2,1)S(1)} %shard_map.114.refs_0_), channel_id=1, source_target_pairs={{0,24},{8,0},{16,8},{24,16},{1,25},{9,1},{17,9},{25,17},{2,26},{10... | collective-permute-start | bytes 147464 | tf_op jit(solution)/shard_map/ppermute | solution.py:435
  129.5 0.9 collective-permute-start.7
  130.4 1.2 collective-permute-done.9.refs_3_
  131.6 3.3 %collective-permute-done.8.refs_2_ = bf16[192,128]{1,0:T(8,128)(2,1)S(1)} collective-permute-done((bf16[192,128]{1,0:T(8,128)(2,1)S(1)}, bf16[192,128]{1,0:T(8,128)(2,1)S(1)}, u32[]{:S(2)}, u32[]{:S(2)}) %collective-permute-start.8) | collective-permute-done | bytes 49184 | tf_op jit(solution)/shard_map/ppermute | solution.py:435
  134.9 0.5 collective-permute-done.7.refs_1_
  135.4 3.6 %shard_map.115 = (bf16[144,128]{1,0:T(8,128)(2,1)S(1)}, bf16[144,128]{1,0:T(8,128)(2,1)S(1)}, bf16[144,128]{1,0:T(8,128)(2,1)S(1)}, bf16[144,128]{1,0:T(8,128)(2...) custom-call(s32[2]{0:T(128)S(1)} %pad_add_fusion.here_ref, ...), custom_call_target="tpu_custom_call" | custom-call | flops 1132462080 | bytes 3932160 | tf_op jit(solution)/shard_map/pallas_call | solution.py:58
  139.1 0.1 collective-permute-start.10
  139.1 0.5 collective-permute-start.11
  139.6 1.4 collective-permute-start.12
  141.0 0.2 collective-permute-start.13
  141.3 1.5 collective-permute-start.14
  142.7 1.3 collective-permute-start.15
  144.0 1.4 collective-permute-start.16
  145.4 2.1 %collective-permute-done.15.refs_6_ = bf16[144,128]{1,0:T(8,128)(2,1)S(1)} collective-permute-done((bf16[144,128]{1,0:T(8,128)(2,1)S(1)}, bf16[144,128]{1,0:T(8,128)(2,1)S(1)}, u32[]{:S(2)}, u32[]{:S(2)}) %collective-permute-start.15) | collective-permute-done | bytes 36896 | tf_op jit(solution)/shard_map/ppermute | solution.py:430
  147.6 0.8 collective-permute-done.16.refs_7_
  148.4 1.7 %collective-permute-start.19 = (bf16[144,128]{1,0:T(8,128)(2,1)S(1)}, bf16[144,128]{1,0:T(8,128)(2,1)S(1)}, u32[]{:S(2)}, u32[]{:S(2)}) collective-permute-start(bf16[144,128]{1,0:T(8,128)(2,1)S(1)} %shard_map.116.refs_4_), channel_id=1, source_target_pairs={{0,24},{8,0},{16,8},{24,16},{1,25},{9,1},{17,9},{25,17},{2,26},{10... | collective-permute-start | bytes 110600 | tf_op jit(solution)/shard_map/ppermute | solution.py:435
  150.1 0.1 collective-permute-start.18
  150.2 1.9 %collective-permute-start.17 = (bf16[144,128]{1,0:T(8,128)(2,1)S(1)}, bf16[144,128]{1,0:T(8,128)(2,1)S(1)}, u32[]{:S(2)}, u32[]{:S(2)}) collective-permute-start(bf16[144,128]{1,0:T(8,128)(2,1)S(1)} %shard_map.116.refs_4_), channel_id=1, source_target_pairs={{0,8},{8,16},{16,24},{24,0},{1,9},{9,17},{17,25},{25,1},{2,10},{10... | collective-permute-start | bytes 110600 | tf_op jit(solution)/shard_map/ppermute | solution.py:435
  152.2 4.3 %shard_map.117 = bf16[32,120,128]{2,1,0:T(8,128)(2,1)} custom-call(bf16[9,128,128]{2,1,0:T(8,128)(2,1)S(1)} %copy-done.3, bf16[32,120,128]{2,1,0:T(8,128)(2,1)S(1)} %all_to_all.15.got_ref, bf16[28,32,120,128]{3,2,1,0:T(8,128)(2,1)} %shard_map.111.slope_hbm), custom_call_target="tpu_custom_call" | custom-call | flops 1132462080 | bytes 2949120 | tf_op jit(solution)/shard_map/pallas_call | solution.py:58
  156.6 9.4 %all-gather = bf16[2688,128]{1,0:T(8,128)(2,1)S(1)} all-gather(bf16[336,128]{1,0:T(8,128)(2,1)S(1)} %shard_map.118), channel_id=2, replica_groups=mesh['seg'=4,'grp'=8] {'grp'}, dimensions={0}, use_global_device_ids=true | all-gather | bytes 774144 | tf_op jit(solution)/shard_map/all_gather | solution.py:612
  166.0 1.4 shard_map.119
  (27 shorter events, 0.2 us)
Async XLA Ops:
  0.6 58.2 %copy-start.5 = (s32[2]{0:T(128)S(1)}, s32[2]{0:T(128)}, u32[]{:S(2)}) copy-start(s32[2]{0:T(128)} %dil_ref.3) | copy-start | bytes 28
  0.6 58.2 %copy-start.6 = (s32[4]{0:T(128)S(1)}, s32[4]{0:T(128)}, u32[]{:S(2)}) copy-start(s32[4]{0:T(128)} %key_ref.3) | copy-start | bytes 52
  0.7 58.2 %copy-start.8 = (bf16[2,128,128]{2,1,0:T(8,128)(2,1)S(1)}, bf16[2,128,128]{2,1,0:T(8,128)(2,1)}, u32[]{:S(2)}) copy-start(bf16[2,128,128]{2,1,0:T(8,128)(2,1)} %uw_ref.1) | copy-start | bytes 196612
  5.4 53.4 %all-to-all-start = ((bf16[32,2,120,128]{3,2,1,0:T(8,128)(2,1)}), bf16[32,2,120,128]{3,2,1,0:T(8,128)(2,1)S(1)}, u32[]{:S(2)}, u32[]{:S(2)}) async-start(bf16[32,2,120,128]{3,2,1,0:T(8,128)(2,1)} %shard_map.110), calls=%async_computation | async-start | bytes 3932160 | tf_op jit(solution)/shard_map/all_to_all | solution.py:425
  17.3 118.1 %copy-start = (bf16[1,32,120,128]{3,2,1,0:T(8,128)(2,1)S(1)}, bf16[1,32,120,128]{3,2,1,0:T(8,128)(2,1)}, u32[]{:S(2)}) copy-start(bf16[1,32,120,128]{3,2,1,0:T(8,128)(2,1)} %param.7) | copy-start | bytes 2949124
  58.8 1.0 copy-start.7
  59.8 11.9 %copy-start.1 = (bf16[32,2,120,128]{3,2,1,0:T(8,128)(2,1)}, bf16[32,2,120,128]{3,2,1,0:T(8,128)(2,1)S(1)}, u32[]{:S(2)}) copy-start(bf16[32,2,120,128]{3,2,1,0:T(8,128)(2,1)S(1)} %all-to-all-done.got_ref) | copy-start | bytes 5898244
  71.7 28.6 %copy-start.4 = (bf16[32,120,128]{2,1,0:T(8,128)(2,1)}, bf16[32,120,128]{2,1,0:T(8,128)(2,1)S(1)}, u32[]{:S(2)}) copy-start(bf16[32,120,128]{2,1,0:T(8,128)(2,1)S(1)} %get-tuple-element.71) | copy-start | bytes 2949124
  100.3 65.6 %all-to-all-start.2 = ((bf16[32,120,128]{2,1,0:T(8,128)(2,1)}), bf16[32,120,128]{2,1,0:T(8,128)(2,1)S(1)}, u32[]{:S(2)}, u32[]{:S(2)}) async-start(bf16[32,120,128]{2,1,0:T(8,128)(2,1)} %copy-done.4), calls=%async_computation.2 | async-start | bytes 1966080 | tf_op jit(solution)/shard_map/all_to_all | solution.py:425
  104.3 1.5 copy-start.2
  105.8 46.3 %copy-start.3 = (bf16[9,128,128]{2,1,0:T(8,128)(2,1)S(1)}, bf16[9,128,128]{2,1,0:T(8,128)(2,1)}, u32[]{:S(2)}) copy-start(bf16[9,128,128]{2,1,0:T(8,128)(2,1)} %w_ref.3) | copy-start | bytes 884740
  114.0 3.6 %collective-permute-start = (bf16[192,128]{1,0:T(8,128)(2,1)S(1)}, bf16[192,128]{1,0:T(8,128)(2,1)S(1)}, u32[]{:S(2)}, u32[]{:S(2)}) collective-permute-start(bf16[192,128]{1,0:T(8,128)(2,1)S(1)} %get-tuple-element.46), channel_id=1, source_target_pairs={{0,1},{1,0},{2,3},{3,2},{4,5},{5,4},{6,7},{7,6},{8,9},{9,8},{10,11... | collective-permute-start | bytes 147464 | tf_op jit(solution)/shard_map/ppermute | solution.py:430
  114.1 6.1 %collective-permute-start.1 = (bf16[192,128]{1,0:T(8,128)(2,1)S(1)}, bf16[192,128]{1,0:T(8,128)(2,1)S(1)}, u32[]{:S(2)}, u32[]{:S(2)}) collective-permute-start(bf16[192,128]{1,0:T(8,128)(2,1)S(1)} %get-tuple-element.47), channel_id=1, source_target_pairs={{0,2},{1,3},{2,0},{3,1},{4,6},{5,7},{6,4},{7,5},{8,10},{9,11},{10,... | collective-permute-start | bytes 147464 | tf_op jit(solution)/shard_map/ppermute | solution.py:430
  115.8 5.0 %collective-permute-start.2 = (bf16[192,128]{1,0:T(8,128)(2,1)S(1)}, bf16[192,128]{1,0:T(8,128)(2,1)S(1)}, u32[]{:S(2)}, u32[]{:S(2)}) collective-permute-start(bf16[192,128]{1,0:T(8,128)(2,1)S(1)} %get-tuple-element.48), channel_id=1, source_target_pairs={{0,3},{1,2},{2,1},{3,0},{4,7},{5,6},{6,5},{7,4},{8,11},{9,10},{10,... | collective-permute-start | bytes 147464 | tf_op jit(solution)/shard_map/ppermute | solution.py:430
  116.0 4.9 %collective-permute-start.3 = (bf16[192,128]{1,0:T(8,128)(2,1)S(1)}, bf16[192,128]{1,0:T(8,128)(2,1)S(1)}, u32[]{:S(2)}, u32[]{:S(2)}) collective-permute-start(bf16[192,128]{1,0:T(8,128)(2,1)S(1)} %get-tuple-element.49), channel_id=1, source_target_pairs={{0,4},{1,5},{2,6},{3,7},{4,0},{5,1},{6,2},{7,3},{8,12},{9,13},{10,... | collective-permute-start | bytes 147464 | tf_op jit(solution)/shard_map/ppermute | solution.py:430
  117.5 6.4 %collective-permute-start.4 = (bf16[192,128]{1,0:T(8,128)(2,1)S(1)}, bf16[192,128]{1,0:T(8,128)(2,1)S(1)}, u32[]{:S(2)}, u32[]{:S(2)}) collective-permute-start(bf16[192,128]{1,0:T(8,128)(2,1)S(1)} %get-tuple-element.50), channel_id=1, source_target_pairs={{0,5},{1,4},{2,7},{3,6},{4,1},{5,0},{6,3},{7,2},{8,13},{9,12},{10,... | collective-permute-start | bytes 147464 | tf_op jit(solution)/shard_map/ppermute | solution.py:430
  117.7 6.2 %collective-permute-start.5 = (bf16[192,128]{1,0:T(8,128)(2,1)S(1)}, bf16[192,128]{1,0:T(8,128)(2,1)S(1)}, u32[]{:S(2)}, u32[]{:S(2)}) collective-permute-start(bf16[192,128]{1,0:T(8,128)(2,1)S(1)} %get-tuple-element.51), channel_id=1, source_target_pairs={{0,6},{1,7},{2,4},{3,5},{4,2},{5,3},{6,0},{7,1},{8,14},{9,15},{10,... | collective-permute-start | bytes 147464 | tf_op jit(solution)/shard_map/ppermute | solution.py:430
  120.2 4.8 %collective-permute-start.6 = (bf16[192,128]{1,0:T(8,128)(2,1)S(1)}, bf16[192,128]{1,0:T(8,128)(2,1)S(1)}, u32[]{:S(2)}, u32[]{:S(2)}) collective-permute-start(bf16[192,128]{1,0:T(8,128)(2,1)S(1)} %get-tuple-element.52), channel_id=1, source_target_pairs={{0,7},{1,6},{2,5},{3,4},{4,3},{5,2},{6,1},{7,0},{8,15},{9,14},{10,... | collective-permute-start | bytes 147464 | tf_op jit(solution)/shard_map/ppermute | solution.py:430
  125.1 6.6 %collective-permute-start.9 = (bf16[192,128]{1,0:T(8,128)(2,1)S(1)}, bf16[192,128]{1,0:T(8,128)(2,1)S(1)}, u32[]{:S(2)}, u32[]{:S(2)}) collective-permute-start(bf16[192,128]{1,0:T(8,128)(2,1)S(1)} %shard_map.114.refs_0_), channel_id=1, source_target_pairs={{0,24},{8,0},{16,8},{24,16},{1,25},{9,1},{17,9},{25,17},{2,26},{10... | collective-permute-start | bytes 147464 | tf_op jit(solution)/shard_map/ppermute | solution.py:435
  129.5 5.3 %collective-permute-start.8 = (bf16[192,128]{1,0:T(8,128)(2,1)S(1)}, bf16[192,128]{1,0:T(8,128)(2,1)S(1)}, u32[]{:S(2)}, u32[]{:S(2)}) collective-permute-start(bf16[192,128]{1,0:T(8,128)(2,1)S(1)} %shard_map.114.refs_0_), channel_id=1, source_target_pairs={{0,16},{8,24},{16,0},{24,8},{1,17},{9,25},{17,1},{25,9},{2,18},{10... | collective-permute-start | bytes 147464 | tf_op jit(solution)/shard_map/ppermute | solution.py:435
  129.5 5.9 %collective-permute-start.7 = (bf16[192,128]{1,0:T(8,128)(2,1)S(1)}, bf16[192,128]{1,0:T(8,128)(2,1)S(1)}, u32[]{:S(2)}, u32[]{:S(2)}) collective-permute-start(bf16[192,128]{1,0:T(8,128)(2,1)S(1)} %shard_map.114.refs_0_), channel_id=1, source_target_pairs={{0,8},{8,16},{16,24},{24,0},{1,9},{9,17},{17,25},{25,1},{2,10},{10... | collective-permute-start | bytes 147464 | tf_op jit(solution)/shard_map/ppermute | solution.py:435
  139.1 3.6 %collective-permute-start.10 = (bf16[144,128]{1,0:T(8,128)(2,1)S(1)}, bf16[144,128]{1,0:T(8,128)(2,1)S(1)}, u32[]{:S(2)}, u32[]{:S(2)}) collective-permute-start(bf16[144,128]{1,0:T(8,128)(2,1)S(1)} %get-tuple-element.63), channel_id=1, source_target_pairs={{0,1},{1,0},{2,3},{3,2},{4,5},{5,4},{6,7},{7,6},{8,9},{9,8},{10,11... | collective-permute-start | bytes 110600 | tf_op jit(solution)/shard_map/ppermute | solution.py:430
  139.1 4.9 %collective-permute-start.11 = (bf16[144,128]{1,0:T(8,128)(2,1)S(1)}, bf16[144,128]{1,0:T(8,128)(2,1)S(1)}, u32[]{:S(2)}, u32[]{:S(2)}) collective-permute-start(bf16[144,128]{1,0:T(8,128)(2,1)S(1)} %get-tuple-element.64), channel_id=1, source_target_pairs={{0,2},{1,3},{2,0},{3,1},{4,6},{5,7},{6,4},{7,5},{8,10},{9,11},{10,... | collective-permute-start | bytes 110600 | tf_op jit(solution)/shard_map/ppermute | solution.py:430
  139.6 5.8 %collective-permute-start.12 = (bf16[144,128]{1,0:T(8,128)(2,1)S(1)}, bf16[144,128]{1,0:T(8,128)(2,1)S(1)}, u32[]{:S(2)}, u32[]{:S(2)}) collective-permute-start(bf16[144,128]{1,0:T(8,128)(2,1)S(1)} %get-tuple-element.65), channel_id=1, source_target_pairs={{0,3},{1,2},{2,1},{3,0},{4,7},{5,6},{6,5},{7,4},{8,11},{9,10},{10,... | collective-permute-start | bytes 110600 | tf_op jit(solution)/shard_map/ppermute | solution.py:430
  141.0 4.4 %collective-permute-start.13 = (bf16[144,128]{1,0:T(8,128)(2,1)S(1)}, bf16[144,128]{1,0:T(8,128)(2,1)S(1)}, u32[]{:S(2)}, u32[]{:S(2)}) collective-permute-start(bf16[144,128]{1,0:T(8,128)(2,1)S(1)} %get-tuple-element.66), channel_id=1, source_target_pairs={{0,4},{1,5},{2,6},{3,7},{4,0},{5,1},{6,2},{7,3},{8,12},{9,13},{10,... | collective-permute-start | bytes 110600 | tf_op jit(solution)/shard_map/ppermute | solution.py:430
  141.3 4.2 %collective-permute-start.14 = (bf16[144,128]{1,0:T(8,128)(2,1)S(1)}, bf16[144,128]{1,0:T(8,128)(2,1)S(1)}, u32[]{:S(2)}, u32[]{:S(2)}) collective-permute-start(bf16[144,128]{1,0:T(8,128)(2,1)S(1)} %get-tuple-element.67), channel_id=1, source_target_pairs={{0,5},{1,4},{2,7},{3,6},{4,1},{5,0},{6,3},{7,2},{8,13},{9,12},{10,... | collective-permute-start | bytes 110600 | tf_op jit(solution)/shard_map/ppermute | solution.py:430
  142.7 4.9 %collective-permute-start.15 = (bf16[144,128]{1,0:T(8,128)(2,1)S(1)}, bf16[144,128]{1,0:T(8,128)(2,1)S(1)}, u32[]{:S(2)}, u32[]{:S(2)}) collective-permute-start(bf16[144,128]{1,0:T(8,128)(2,1)S(1)} %get-tuple-element.68), channel_id=1, source_target_pairs={{0,6},{1,7},{2,4},{3,5},{4,2},{5,3},{6,0},{7,1},{8,14},{9,15},{10,... | collective-permute-start | bytes 110600 | tf_op jit(solution)/shard_map/ppermute | solution.py:430
  144.0 4.3 %collective-permute-start.16 = (bf16[144,128]{1,0:T(8,128)(2,1)S(1)}, bf16[144,128]{1,0:T(8,128)(2,1)S(1)}, u32[]{:S(2)}, u32[]{:S(2)}) collective-permute-start(bf16[144,128]{1,0:T(8,128)(2,1)S(1)} %get-tuple-element.69), channel_id=1, source_target_pairs={{0,7},{1,6},{2,5},{3,4},{4,3},{5,2},{6,1},{7,0},{8,15},{9,14},{10,... | collective-permute-start | bytes 110600 | tf_op jit(solution)/shard_map/ppermute | solution.py:430
  148.4 8.1 %collective-permute-start.19 = (bf16[144,128]{1,0:T(8,128)(2,1)S(1)}, bf16[144,128]{1,0:T(8,128)(2,1)S(1)}, u32[]{:S(2)}, u32[]{:S(2)}) collective-permute-start(bf16[144,128]{1,0:T(8,128)(2,1)S(1)} %shard_map.116.refs_4_), channel_id=1, source_target_pairs={{0,24},{8,0},{16,8},{24,16},{1,25},{9,1},{17,9},{25,17},{2,26},{10... | collective-permute-start | bytes 110600 | tf_op jit(solution)/shard_map/ppermute | solution.py:435
  150.1 6.4 %collective-permute-start.18 = (bf16[144,128]{1,0:T(8,128)(2,1)S(1)}, bf16[144,128]{1,0:T(8,128)(2,1)S(1)}, u32[]{:S(2)}, u32[]{:S(2)}) collective-permute-start(bf16[144,128]{1,0:T(8,128)(2,1)S(1)} %shard_map.116.refs_4_), channel_id=1, source_target_pairs={{0,16},{8,24},{16,0},{24,8},{1,17},{9,25},{17,1},{25,9},{2,18},{10... | collective-permute-start | bytes 110600 | tf_op jit(solution)/shard_map/ppermute | solution.py:435
  150.2 6.3 %collective-permute-start.17 = (bf16[144,128]{1,0:T(8,128)(2,1)S(1)}, bf16[144,128]{1,0:T(8,128)(2,1)S(1)}, u32[]{:S(2)}, u32[]{:S(2)}) collective-permute-start(bf16[144,128]{1,0:T(8,128)(2,1)S(1)} %shard_map.116.refs_4_), channel_id=1, source_target_pairs={{0,8},{8,16},{16,24},{24,0},{1,9},{9,17},{17,25},{25,1},{2,10},{10... | collective-permute-start | bytes 110600 | tf_op jit(solution)/shard_map/ppermute | solution.py:435

commit v13 on v12

--- a/solution.py
+++ b/solution.py
@@ -251,12 +251,19 @@
 
 
 def temporal_kernel(
-    step_frames, dil_ref, key_ref, got_ref, tw_ref, uw_ref,
+    step_frames, dil_ref, key_ref, got_ref, tw_hbm, uw_hbm,
     grad_hbm, kept_hbm, united_hbm,
-    a0, a1, feat, cots, g0, g1, slope0, slope1, united_ref, grad_ref, sems, out_sems,
+    a0, a1, feat, cots, g0, g1, slope0, slope1, united_ref, grad_ref, tw_ref, uw_ref,
+    sems, in_sems, out_sems,
 ):
     frames, _, block, ch = got_ref.shape
     high = feat.shape[1]
+    loads = [
+        pltpu.make_async_copy(source, ref, in_sems.at[n])
+        for n, (source, ref) in enumerate(((tw_hbm, tw_ref), (uw_hbm, uw_ref)))
+    ]
+    for load in loads:
+        load.start()
     stores = [
         pltpu.make_async_copy(
             grad_ref.at[pl.ds(at, step_frames)], grad_hbm.at[pl.ds(at, step_frames)], out_sems.at[n]
@@ -285,6 +292,8 @@
         a0[HALO : HALO + frames, block:, :] = pad
         cots[:, block:, :] = pad
     a0[HALO : HALO + frames, :block, :] = got_ref[:, 0]
+    for load in loads:
+        load.wait()
     for layer, (source, target, slopes) in enumerate(((a0, a1, slope0), (a1, feat, slope1))):
         step_size = dil_ref[layer]
         weight = jnp.concatenate([tw_ref[layer, k] for k in range(TAPS)], axis=0)
@@ -467,7 +476,10 @@
     rows_step = next(n for n in (4, 2, 1) if rows % n == 0)
     steps = rows // rows_step
     parts = next(n for n in (4, 2, 1) if rows % (n * rows_step) == 0)
-    step_frames = max(n for n in range(1, frames + 1) if frames % n == 0 and n * high <= 512)
+    step_frames, narrow_step = (
+        max(n for n in range(1, frames + 1) if frames % n == 0 and n * high <= most)
+        for most in (512, 256)
+    )
     scale = float((frames * pixels) ** -0.5)
     here = jnp.stack([lax.axis_index("seg"), lax.axis_index("grp")]).astype(jnp.int32)
     space_rows, time_rows, unite_rows = (n * ch // peers for n in (9, LAYERS * TAPS, 2))
@@ -509,7 +521,7 @@
     padded = (frames + 2 * HALO, high, ch)
     whole = (frames, high, ch)
     grad_send, kept, united_send = call(
-        functools.partial(temporal_kernel, step_frames),
+        functools.partial(temporal_kernel, narrow_step),
         [
             ((frames, block, ch), BF16, HBM),
             ((SPARE,) + whole, BF16, HBM),
@@ -526,14 +538,17 @@
             pltpu.VMEM(whole, F32),
             pltpu.VMEM((frames, block, ch), BF16),
             pltpu.VMEM((frames, block, ch), BF16),
+            pltpu.VMEM(temporal_weight.shape, BF16),
+            pltpu.VMEM(uniting_weight.shape, BF16),
             pltpu.SemaphoreType.DMA((5,)),
-            pltpu.SemaphoreType.DMA((frames // step_frames,)),
+            pltpu.SemaphoreType.DMA((2,)),
+            pltpu.SemaphoreType.DMA((frames // narrow_step,)),
         ],
         2 * 22 * frames * block * ch * ch,
         frames * block * ch * 18,
         [
             (dilation, SMEM), (key_index, SMEM), (got, VMEM),
-            (temporal_weight, VMEM), (uniting_weight, VMEM),
+            (temporal_weight, HBM), (uniting_weight, HBM),
         ],
         MID_VMEM,
     )
@@ -559,9 +574,9 @@
         MID_VMEM,
     )
     time_turned = all_turns(reduce_in_grp(time_pieces))
+    *time_turned, grad_time = lax.optimization_barrier((*time_turned, grad_time))
     united_send, grad_time = lax.optimization_barrier((united_send, grad_time))
     united = exchange(united_send)
-    *time_turned, grad_time = lax.optimization_barrier((*time_turned, grad_time))
     space_pieces = call(
         functools.partial(spatial_wgrad_kernel, rows_step, scale),
         [((space_rows, ch), BF16, VMEM)] * peers,

time: 168 us -> 153 us (0.911)
  blocking collectives: 38 us -> 10.2 us
  starting transfers between devices: 33.5 us -> 39.8 us
  waiting for transfers between devices: 53.6 us -> 57.4 us
  local copies, waits for them, and re-layouts: 2.55 us -> 4.42 us
    all_to_all x1 -> x0, blocking collectives: 28.6 us -> none  [exchange(): return lax.all_to_all(blocks, AXES, split_axis=0, concat_axis=0, tiled=True)]
    all_to_all x2 -> x3, starting transfers between devices: 11.3 us -> 14.4 us  [exchange(): return lax.all_to_all(blocks, AXES, split_axis=0, concat_axis=0, tiled=True)]
    ppermute x6, waiting for transfers between devices: 5.01 us -> 7.77 us  [turn_by(): lax.ppermute(value, 'seg', [(i, (i + turn) % size) for i in range(size)])]
    ppermute x6, starting transfers between devices: 9.13 us -> 11.5 us  [turn_by(): lax.ppermute(value, 'seg', [(i, (i + turn) % size) for i in range(size)])]
    unnamed x18 -> x20, local copies, waits for them, and re-layouts: 2.55 us -> 4.42 us
    all_to_all x2 -> x3, waiting for transfers between devices: 41.5 us -> 41.5 us  [exchange(): return lax.all_to_all(blocks, AXES, split_axis=0, concat_axis=0, tiled=True)]
  transfers between devices with their start and end apart: 22 -> 23, of which waited for: 8 -> 11; matrix products, arithmetic and copies ran while one was open for 0% -> 0% of each run, Pallas kernels for 12% -> 14%
where the time goes in v13:
time: 153 us
  waiting for transfers between devices  57.4 us (38%)
  starting transfers between devices  39.8 us (26%)
  Pallas kernels  39.7 us (26%)
  blocking collectives  10.2 us (7%)
  local copies, waits for them, and re-layouts  4.42 us (3%)
    all_to_all x3, waiting for transfers between devices, exchange(): return lax.all_to_all(blocks, AXES, split_axis=0, concat_axis=0, tiled=True)  41.5 us
    pallas_call x10, Pallas kernels, call(): pl.pallas_call(kernel, out_shape=[jax.ShapeDtypeStruct(shape, kind) for s...  39.7 us
    all_to_all x3, starting transfers between devices, exchange(): return lax.all_to_all(blocks, AXES, split_axis=0, concat_axis=0, tiled=True)  14.4 us
    ppermute x14, starting transfers between devices, flip(): return lax.ppermute(value, 'grp', [(i, i ^ peer) for i in range(size)])  13.9 us
    ppermute x6, starting transfers between devices, turn_by(): lax.ppermute(value, 'seg', [(i, (i + turn) % size) for i in range(size)])  11.5 us
    all_gather x1, blocking collectives, local(): lax.all_gather(piece, 'grp', axis=0)  10.2 us
    ppermute x14, waiting for transfers between devices, flip(): return lax.ppermute(value, 'grp', [(i, i ^ peer) for i in range(size)])  8.11 us
    ppermute x6, waiting for transfers between devices, turn_by(): lax.ppermute(value, 'seg', [(i, (i + turn) % size) for i in range(size)])  7.77 us
  transfers between devices with their start and end apart: 23, of which 11 were waited for; matrix products, arithmetic and copies ran while one was open for 0% of the time, Pallas kernels for 14%

profile of v13, /device:TPU:0, one launch (start us, length us, event | category | flops | bytes accessed | tf_op | source)
XLA Modules:
  0.0 152.6 jit_solution(5736793418080368477)
XLA Ops:
  0.7 4.8 %shard_map.110 = bf16[32,2,120,128]{3,2,1,0:T(8,128)(2,1)} custom-call(bf16[32,120,128]{2,1,0:T(8,128)(2,1)} %bitcast.10, bf16[9,128,128]{2,1,0:T(8,128)(2,1)} %w_ref.3, bf16[32,120,128]{2,1,0:T(8,128)(2,1)} %bitcast.14), custom_call_target="tpu_custom_call" | custom-call | flops 1132462080 | bytes 3932160 | tf_op jit(solution)/shard_map/pallas_call | solution.py:58
  5.5 7.5 %all-to-all-start = ((bf16[32,2,120,128]{3,2,1,0:T(8,128)(2,1)}), bf16[32,2,120,128]{3,2,1,0:T(8,128)(2,1)S(1)}, u32[]{:S(2)}, u32[]{:S(2)}) async-start(bf16[32,2,120,128]{3,2,1,0:T(8,128)(2,1)} %shard_map.110), calls=%async_computation | async-start | bytes 3932160 | tf_op jit(solution)/shard_map/all_to_all | solution.py:434
  12.9 4.4 %shard_map.111.slope_hbm = bf16[28,32,120,128]{3,2,1,0:T(8,128)(2,1)} custom-call(bf16[32,120,128]{2,1,0:T(8,128)(2,1)} %bitcast.11, bf16[9,128,128]{2,1,0:T(8,128)(2,1)} %w_ref.3), custom_call_target="tpu_custom_call" | custom-call | flops 1132462080 | bytes 1966080 | tf_op jit(solution)/shard_map/pallas_call | solution.py:58
  17.3 0.0 copy-start
  17.4 41.5 %all-to-all-done.got_ref = bf16[32,2,120,128]{3,2,1,0:T(8,128)(2,1)S(1)} async-done(((bf16[32,2,120,128]{3,2,1,0:T(8,128)(2,1)}), bf16[32,2,120,128]{3,2,1,0:T(8,128)(2,1)S(1)}, u32[]{:S(2)}, u32[]{:S(2)}) %all-to-all-start) | async-done | bytes 1966112 | tf_op jit(solution)/shard_map/all_to_all | solution.py:434
  58.9 1.0 copy-done.8
  59.8 12.8 %shard_map.112 = (bf16[32,120,128]{2,1,0:T(8,128)(2,1)S(1)}, bf16[28,32,128,128]{3,2,1,0:T(8,128)(2,1)}, bf16[32,120,128]{2,1,0:T(8,128)(2,1)S(1)}) custom-call(s32[2]{0:T(128)S(1)} %copy-done.6, s32[4]{0:T(128)S(1)} %copy-done.7, bf16[32,2,120,128]{3,2,1,0:T(8,128)(2,1)S(1)} %all-to-all-done.got_ref, bf16[2,5,128,128]{3,2,1,0:T(8,128)(2,1)S(1)} %copy-done.8, ...), custom_call_target="tpu_custom_call" | custom-call | flops 2768240640 | bytes 8847360 | tf_op jit(solution)/shard_map/pallas_call | solution.py:58
  72.6 0.9 copy-done.4
  73.5 0.9 copy-done.5
  74.5 4.2 %all-to-all-start.1 = ((bf16[32,120,128]{2,1,0:T(8,128)(2,1)}), bf16[32,120,128]{2,1,0:T(8,128)(2,1)S(1)}, u32[]{:S(2)}, u32[]{:S(2)}) async-start(bf16[32,120,128]{2,1,0:T(8,128)(2,1)} %copy-done.5), calls=%async_computation.1 | async-start | bytes 1966080 | tf_op jit(solution)/shard_map/all_to_all | solution.py:434
  78.7 0.1 pad_add_fusion.here_ref
  78.8 1.5 %copy-done.2 = bf16[32,2,120,128]{3,2,1,0:T(8,128)(2,1)S(1)} copy-done((bf16[32,2,120,128]{3,2,1,0:T(8,128)(2,1)S(1)}, bf16[32,2,120,128]{3,2,1,0:T(8,128)(2,1)}, u32[]{:S(2)}) %copy-start.2) | copy-done | bytes 1966104
  80.3 8.2 %shard_map.113 = (bf16[192,128]{1,0:T(8,128)(2,1)S(1)}, bf16[192,128]{1,0:T(8,128)(2,1)S(1)}, bf16[192,128]{1,0:T(8,128)(2,1)S(1)}, bf16[192,128]{1,0:T(8,128)(2...) custom-call(s32[2]{0:T(128)S(1)} %pad_add_fusion.here_ref, ...), custom_call_target="tpu_custom_call" | custom-call | flops 1509949440 | bytes 6881280 | tf_op jit(solution)/shard_map/pallas_call | solution.py:58
  88.5 0.1 collective-permute-start
  88.6 1.7 %collective-permute-start.1 = (bf16[192,128]{1,0:T(8,128)(2,1)S(1)}, bf16[192,128]{1,0:T(8,128)(2,1)S(1)}, u32[]{:S(2)}, u32[]{:S(2)}) collective-permute-start(bf16[192,128]{1,0:T(8,128)(2,1)S(1)} %get-tuple-element.47), channel_id=1, source_target_pairs={{0,2},{1,3},{2,0},{3,1},{4,6},{5,7},{6,4},{7,5},{8,10},{9,11},{10,... | collective-permute-start | bytes 147464 | tf_op jit(solution)/shard_map/ppermute | solution.py:439
  90.3 0.2 collective-permute-start.2
  90.5 1.5 %collective-permute-start.3 = (bf16[192,128]{1,0:T(8,128)(2,1)S(1)}, bf16[192,128]{1,0:T(8,128)(2,1)S(1)}, u32[]{:S(2)}, u32[]{:S(2)}) collective-permute-start(bf16[192,128]{1,0:T(8,128)(2,1)S(1)} %get-tuple-element.49), channel_id=1, source_target_pairs={{0,4},{1,5},{2,6},{3,7},{4,0},{5,1},{6,2},{7,3},{8,12},{9,13},{10,... | collective-permute-start | bytes 147464 | tf_op jit(solution)/shard_map/ppermute | solution.py:439
  92.0 0.2 collective-permute-start.4
  92.2 2.5 %collective-permute-start.5 = (bf16[192,128]{1,0:T(8,128)(2,1)S(1)}, bf16[192,128]{1,0:T(8,128)(2,1)S(1)}, u32[]{:S(2)}, u32[]{:S(2)}) collective-permute-start(bf16[192,128]{1,0:T(8,128)(2,1)S(1)} %get-tuple-element.51), channel_id=1, source_target_pairs={{0,6},{1,7},{2,4},{3,5},{4,2},{5,3},{6,0},{7,1},{8,14},{9,15},{10,... | collective-permute-start | bytes 147464 | tf_op jit(solution)/shard_map/ppermute | solution.py:439
  94.7 0.6 collective-permute-start.6
  95.3 0.0 collective-permute-done.3.refs_4_
  95.3 3.0 %collective-permute-done.4.refs_5_ = bf16[192,128]{1,0:T(8,128)(2,1)S(1)} collective-permute-done((bf16[192,128]{1,0:T(8,128)(2,1)S(1)}, bf16[192,128]{1,0:T(8,128)(2,1)S(1)}, u32[]{:S(2)}, u32[]{:S(2)}) %collective-permute-start.4) | collective-permute-done | bytes 49184 | tf_op jit(solution)/shard_map/ppermute | solution.py:439
  98.4 1.1 collective-permute-done.6.refs_7_
  99.5 0.1 shard_map.114.refs_0_
  99.5 4.5 %collective-permute-start.9 = (bf16[192,128]{1,0:T(8,128)(2,1)S(1)}, bf16[192,128]{1,0:T(8,128)(2,1)S(1)}, u32[]{:S(2)}, u32[]{:S(2)}) collective-permute-start(bf16[192,128]{1,0:T(8,128)(2,1)S(1)} %shard_map.114.refs_0_), channel_id=1, source_target_pairs={{0,24},{8,0},{16,8},{24,16},{1,25},{9,1},{17,9},{25,17},{2,26},{10... | collective-permute-start | bytes 147464 | tf_op jit(solution)/shard_map/ppermute | solution.py:444
  104.0 0.9 collective-permute-start.7
  104.9 1.2 collective-permute-done.9.refs_3_
  106.1 3.3 %collective-permute-done.8.refs_2_ = bf16[192,128]{1,0:T(8,128)(2,1)S(1)} collective-permute-done((bf16[192,128]{1,0:T(8,128)(2,1)S(1)}, bf16[192,128]{1,0:T(8,128)(2,1)S(1)}, u32[]{:S(2)}, u32[]{:S(2)}) %collective-permute-start.8) | collective-permute-done | bytes 49184 | tf_op jit(solution)/shard_map/ppermute | solution.py:444
  109.4 0.5 collective-permute-done.7.refs_1_
  109.9 2.8 %all-to-all-start.2 = ((bf16[32,120,128]{2,1,0:T(8,128)(2,1)}), bf16[32,120,128]{2,1,0:T(8,128)(2,1)S(1)}, u32[]{:S(2)}, u32[]{:S(2)}) async-start(bf16[32,120,128]{2,1,0:T(8,128)(2,1)} %copy-done.4), calls=%async_computation.2 | async-start | bytes 1966080 | tf_op jit(solution)/shard_map/all_to_all | solution.py:434
  112.7 3.6 %shard_map.115 = (bf16[144,128]{1,0:T(8,128)(2,1)S(1)}, bf16[144,128]{1,0:T(8,128)(2,1)S(1)}, bf16[144,128]{1,0:T(8,128)(2,1)S(1)}, bf16[144,128]{1,0:T(8,128)(2...) custom-call(s32[2]{0:T(128)S(1)} %pad_add_fusion.here_ref, ...), custom_call_target="tpu_custom_call" | custom-call | flops 1132462080 | bytes 3932160 | tf_op jit(solution)/shard_map/pallas_call | solution.py:58
  116.4 0.3 collective-permute-start.10
  116.7 1.7 %collective-permute-start.11 = (bf16[144,128]{1,0:T(8,128)(2,1)S(1)}, bf16[144,128]{1,0:T(8,128)(2,1)S(1)}, u32[]{:S(2)}, u32[]{:S(2)}) collective-permute-start(bf16[144,128]{1,0:T(8,128)(2,1)S(1)} %get-tuple-element.64), channel_id=1, source_target_pairs={{0,2},{1,3},{2,0},{3,1},{4,6},{5,7},{6,4},{7,5},{8,10},{9,11},{10,... | collective-permute-start | bytes 110600 | tf_op jit(solution)/shard_map/ppermute | solution.py:439
  118.4 1.7 %collective-permute-start.13 = (bf16[144,128]{1,0:T(8,128)(2,1)S(1)}, bf16[144,128]{1,0:T(8,128)(2,1)S(1)}, u32[]{:S(2)}, u32[]{:S(2)}) collective-permute-start(bf16[144,128]{1,0:T(8,128)(2,1)S(1)} %get-tuple-element.66), channel_id=1, source_target_pairs={{0,4},{1,5},{2,6},{3,7},{4,0},{5,1},{6,2},{7,3},{8,12},{9,13},{10,... | collective-permute-start | bytes 110600 | tf_op jit(solution)/shard_map/ppermute | solution.py:439
  120.1 0.1 collective-permute-start.14
  120.2 2.6 %collective-permute-start.15 = (bf16[144,128]{1,0:T(8,128)(2,1)S(1)}, bf16[144,128]{1,0:T(8,128)(2,1)S(1)}, u32[]{:S(2)}, u32[]{:S(2)}) collective-permute-start(bf16[144,128]{1,0:T(8,128)(2,1)S(1)} %get-tuple-element.68), channel_id=1, source_target_pairs={{0,6},{1,7},{2,4},{3,5},{4,2},{5,3},{6,0},{7,1},{8,14},{9,15},{10,... | collective-permute-start | bytes 110600 | tf_op jit(solution)/shard_map/ppermute | solution.py:439
  122.8 0.7 collective-permute-start.16
  123.5 0.4 collective-permute-done.12.refs_3_
  123.9 0.0 collective-permute-done.13.refs_4_
  124.0 1.3 collective-permute-done.14.refs_5_
  125.3 1.4 collective-permute-done.15.refs_6_
  126.7 0.7 collective-permute-done.16.refs_7_
  127.4 5.5 %collective-permute-start.19 = (bf16[144,128]{1,0:T(8,128)(2,1)S(1)}, bf16[144,128]{1,0:T(8,128)(2,1)S(1)}, u32[]{:S(2)}, u32[]{:S(2)}) collective-permute-start(bf16[144,128]{1,0:T(8,128)(2,1)S(1)} %shard_map.116.refs_4_), channel_id=1, source_target_pairs={{0,24},{8,0},{16,8},{24,16},{1,25},{9,1},{17,9},{25,17},{2,26},{10... | collective-permute-start | bytes 110600 | tf_op jit(solution)/shard_map/ppermute | solution.py:444
  132.9 0.6 collective-permute-start.17
  133.6 4.3 %shard_map.117 = bf16[32,120,128]{2,1,0:T(8,128)(2,1)} custom-call(bf16[9,128,128]{2,1,0:T(8,128)(2,1)S(1)} %copy-done.3, bf16[32,120,128]{2,1,0:T(8,128)(2,1)S(1)} %all-to-all-done.1.got_ref, bf16[28,32,120,128]{3,2,1,0:T(8,128)(2,1)} %shard_map.111.slope_hbm), custom_call_target="tpu_custom_call" | custom-call | flops 1132462080 | bytes 2949120 | tf_op jit(solution)/shard_map/pallas_call | solution.py:58
  137.9 2.8 %collective-permute-done.18.refs_6_ = bf16[144,128]{1,0:T(8,128)(2,1)S(1)} collective-permute-done((bf16[144,128]{1,0:T(8,128)(2,1)S(1)}, bf16[144,128]{1,0:T(8,128)(2,1)S(1)}, u32[]{:S(2)}, u32[]{:S(2)}) %collective-permute-start.18) | collective-permute-done | bytes 36896 | tf_op jit(solution)/shard_map/ppermute | solution.py:444
  140.7 10.2 %all-gather = bf16[2688,128]{1,0:T(8,128)(2,1)S(1)} all-gather(bf16[336,128]{1,0:T(8,128)(2,1)S(1)} %shard_map.118), channel_id=2, replica_groups=mesh['seg'=4,'grp'=8] {'grp'}, dimensions={0}, use_global_device_ids=true | all-gather | bytes 774144 | tf_op jit(solution)/shard_map/all_gather | solution.py:627
  151.0 1.4 shard_map.119
  (30 shorter events, 0.2 us)
Async XLA Ops:
  0.6 58.2 %copy-start.6 = (s32[2]{0:T(128)S(1)}, s32[2]{0:T(128)}, u32[]{:S(2)}) copy-start(s32[2]{0:T(128)} %dil_ref.3) | copy-start | bytes 28
  0.6 58.2 %copy-start.7 = (s32[4]{0:T(128)S(1)}, s32[4]{0:T(128)}, u32[]{:S(2)}) copy-start(s32[4]{0:T(128)} %key_ref.3) | copy-start | bytes 52
  0.7 58.2 %copy-start.9 = (bf16[2,128,128]{2,1,0:T(8,128)(2,1)S(1)}, bf16[2,128,128]{2,1,0:T(8,128)(2,1)}, u32[]{:S(2)}) copy-start(bf16[2,128,128]{2,1,0:T(8,128)(2,1)} %uw_hbm.1) | copy-start | bytes 196612
  5.5 53.4 %all-to-all-start = ((bf16[32,2,120,128]{3,2,1,0:T(8,128)(2,1)}), bf16[32,2,120,128]{3,2,1,0:T(8,128)(2,1)S(1)}, u32[]{:S(2)}, u32[]{:S(2)}) async-start(bf16[32,2,120,128]{3,2,1,0:T(8,128)(2,1)} %shard_map.110), calls=%async_computation | async-start | bytes 3932160 | tf_op jit(solution)/shard_map/all_to_all | solution.py:434
  17.3 95.4 %copy-start = (bf16[1,32,120,128]{3,2,1,0:T(8,128)(2,1)S(1)}, bf16[1,32,120,128]{3,2,1,0:T(8,128)(2,1)}, u32[]{:S(2)}) copy-start(bf16[1,32,120,128]{3,2,1,0:T(8,128)(2,1)} %param.7) | copy-start | bytes 2949124
  58.9 1.0 copy-start.8
  59.8 14.7 %copy-start.1 = (bf16[32,2,120,128]{3,2,1,0:T(8,128)(2,1)}, bf16[32,2,120,128]{3,2,1,0:T(8,128)(2,1)S(1)}, u32[]{:S(2)}) copy-start(bf16[32,2,120,128]{3,2,1,0:T(8,128)(2,1)S(1)} %all-to-all-done.got_ref) | copy-start | bytes 5898244
  72.6 0.9 copy-start.4
  73.5 0.9 copy-start.5
  74.5 35.4 %all-to-all-start.1 = ((bf16[32,120,128]{2,1,0:T(8,128)(2,1)}), bf16[32,120,128]{2,1,0:T(8,128)(2,1)S(1)}, u32[]{:S(2)}, u32[]{:S(2)}) async-start(bf16[32,120,128]{2,1,0:T(8,128)(2,1)} %copy-done.5), calls=%async_computation.1 | async-start | bytes 1966080 | tf_op jit(solution)/shard_map/all_to_all | solution.py:434
  78.8 1.5 %copy-start.2 = (bf16[32,2,120,128]{3,2,1,0:T(8,128)(2,1)S(1)}, bf16[32,2,120,128]{3,2,1,0:T(8,128)(2,1)}, u32[]{:S(2)}) copy-start(bf16[32,2,120,128]{3,2,1,0:T(8,128)(2,1)} %copy-done.1) | copy-start | bytes 5898244
  80.3 53.3 %copy-start.3 = (bf16[9,128,128]{2,1,0:T(8,128)(2,1)S(1)}, bf16[9,128,128]{2,1,0:T(8,128)(2,1)}, u32[]{:S(2)}) copy-start(bf16[9,128,128]{2,1,0:T(8,128)(2,1)} %w_ref.3) | copy-start | bytes 884740
  88.5 3.6 %collective-permute-start = (bf16[192,128]{1,0:T(8,128)(2,1)S(1)}, bf16[192,128]{1,0:T(8,128)(2,1)S(1)}, u32[]{:S(2)}, u32[]{:S(2)}) collective-permute-start(bf16[192,128]{1,0:T(8,128)(2,1)S(1)} %get-tuple-element.46), channel_id=1, source_target_pairs={{0,1},{1,0},{2,3},{3,2},{4,5},{5,4},{6,7},{7,6},{8,9},{9,8},{10,11... | collective-permute-start | bytes 147464 | tf_op jit(solution)/shard_map/ppermute | solution.py:439
  88.6 6.1 %collective-permute-start.1 = (bf16[192,128]{1,0:T(8,128)(2,1)S(1)}, bf16[192,128]{1,0:T(8,128)(2,1)S(1)}, u32[]{:S(2)}, u32[]{:S(2)}) collective-permute-start(bf16[192,128]{1,0:T(8,128)(2,1)S(1)} %get-tuple-element.47), channel_id=1, source_target_pairs={{0,2},{1,3},{2,0},{3,1},{4,6},{5,7},{6,4},{7,5},{8,10},{9,11},{10,... | collective-permute-start | bytes 147464 | tf_op jit(solution)/shard_map/ppermute | solution.py:439
  90.3 5.0 %collective-permute-start.2 = (bf16[192,128]{1,0:T(8,128)(2,1)S(1)}, bf16[192,128]{1,0:T(8,128)(2,1)S(1)}, u32[]{:S(2)}, u32[]{:S(2)}) collective-permute-start(bf16[192,128]{1,0:T(8,128)(2,1)S(1)} %get-tuple-element.48), channel_id=1, source_target_pairs={{0,3},{1,2},{2,1},{3,0},{4,7},{5,6},{6,5},{7,4},{8,11},{9,10},{10,... | collective-permute-start | bytes 147464 | tf_op jit(solution)/shard_map/ppermute | solution.py:439
  90.5 4.9 %collective-permute-start.3 = (bf16[192,128]{1,0:T(8,128)(2,1)S(1)}, bf16[192,128]{1,0:T(8,128)(2,1)S(1)}, u32[]{:S(2)}, u32[]{:S(2)}) collective-permute-start(bf16[192,128]{1,0:T(8,128)(2,1)S(1)} %get-tuple-element.49), channel_id=1, source_target_pairs={{0,4},{1,5},{2,6},{3,7},{4,0},{5,1},{6,2},{7,3},{8,12},{9,13},{10,... | collective-permute-start | bytes 147464 | tf_op jit(solution)/shard_map/ppermute | solution.py:439
  92.0 6.4 %collective-permute-start.4 = (bf16[192,128]{1,0:T(8,128)(2,1)S(1)}, bf16[192,128]{1,0:T(8,128)(2,1)S(1)}, u32[]{:S(2)}, u32[]{:S(2)}) collective-permute-start(bf16[192,128]{1,0:T(8,128)(2,1)S(1)} %get-tuple-element.50), channel_id=1, source_target_pairs={{0,5},{1,4},{2,7},{3,6},{4,1},{5,0},{6,3},{7,2},{8,13},{9,12},{10,... | collective-permute-start | bytes 147464 | tf_op jit(solution)/shard_map/ppermute | solution.py:439
  92.2 6.2 %collective-permute-start.5 = (bf16[192,128]{1,0:T(8,128)(2,1)S(1)}, bf16[192,128]{1,0:T(8,128)(2,1)S(1)}, u32[]{:S(2)}, u32[]{:S(2)}) collective-permute-start(bf16[192,128]{1,0:T(8,128)(2,1)S(1)} %get-tuple-element.51), channel_id=1, source_target_pairs={{0,6},{1,7},{2,4},{3,5},{4,2},{5,3},{6,0},{7,1},{8,14},{9,15},{10,... | collective-permute-start | bytes 147464 | tf_op jit(solution)/shard_map/ppermute | solution.py:439
  94.7 4.8 %collective-permute-start.6 = (bf16[192,128]{1,0:T(8,128)(2,1)S(1)}, bf16[192,128]{1,0:T(8,128)(2,1)S(1)}, u32[]{:S(2)}, u32[]{:S(2)}) collective-permute-start(bf16[192,128]{1,0:T(8,128)(2,1)S(1)} %get-tuple-element.52), channel_id=1, source_target_pairs={{0,7},{1,6},{2,5},{3,4},{4,3},{5,2},{6,1},{7,0},{8,15},{9,14},{10,... | collective-permute-start | bytes 147464 | tf_op jit(solution)/shard_map/ppermute | solution.py:439
  99.5 6.6 %collective-permute-start.9 = (bf16[192,128]{1,0:T(8,128)(2,1)S(1)}, bf16[192,128]{1,0:T(8,128)(2,1)S(1)}, u32[]{:S(2)}, u32[]{:S(2)}) collective-permute-start(bf16[192,128]{1,0:T(8,128)(2,1)S(1)} %shard_map.114.refs_0_), channel_id=1, source_target_pairs={{0,24},{8,0},{16,8},{24,16},{1,25},{9,1},{17,9},{25,17},{2,26},{10... | collective-permute-start | bytes 147464 | tf_op jit(solution)/shard_map/ppermute | solution.py:444
  104.0 5.3 %collective-permute-start.8 = (bf16[192,128]{1,0:T(8,128)(2,1)S(1)}, bf16[192,128]{1,0:T(8,128)(2,1)S(1)}, u32[]{:S(2)}, u32[]{:S(2)}) collective-permute-start(bf16[192,128]{1,0:T(8,128)(2,1)S(1)} %shard_map.114.refs_0_), channel_id=1, source_target_pairs={{0,16},{8,24},{16,0},{24,8},{1,17},{9,25},{17,1},{25,9},{2,18},{10... | collective-permute-start | bytes 147464 | tf_op jit(solution)/shard_map/ppermute | solution.py:444
  104.0 5.9 %collective-permute-start.7 = (bf16[192,128]{1,0:T(8,128)(2,1)S(1)}, bf16[192,128]{1,0:T(8,128)(2,1)S(1)}, u32[]{:S(2)}, u32[]{:S(2)}) collective-permute-start(bf16[192,128]{1,0:T(8,128)(2,1)S(1)} %shard_map.114.refs_0_), channel_id=1, source_target_pairs={{0,8},{8,16},{16,24},{24,0},{1,9},{9,17},{17,25},{25,1},{2,10},{10... | collective-permute-start | bytes 147464 | tf_op jit(solution)/shard_map/ppermute | solution.py:444
  109.9 41.1 %all-to-all-start.2 = ((bf16[32,120,128]{2,1,0:T(8,128)(2,1)}), bf16[32,120,128]{2,1,0:T(8,128)(2,1)S(1)}, u32[]{:S(2)}, u32[]{:S(2)}) async-start(bf16[32,120,128]{2,1,0:T(8,128)(2,1)} %copy-done.4), calls=%async_computation.2 | async-start | bytes 1966080 | tf_op jit(solution)/shard_map/all_to_all | solution.py:434
  116.4 3.8 %collective-permute-start.10 = (bf16[144,128]{1,0:T(8,128)(2,1)S(1)}, bf16[144,128]{1,0:T(8,128)(2,1)S(1)}, u32[]{:S(2)}, u32[]{:S(2)}) collective-permute-start(bf16[144,128]{1,0:T(8,128)(2,1)S(1)} %get-tuple-element.63), channel_id=1, source_target_pairs={{0,1},{1,0},{2,3},{3,2},{4,5},{5,4},{6,7},{7,6},{8,9},{9,8},{10,11... | collective-permute-start | bytes 110600 | tf_op jit(solution)/shard_map/ppermute | solution.py:439
  116.7 6.1 %collective-permute-start.11 = (bf16[144,128]{1,0:T(8,128)(2,1)S(1)}, bf16[144,128]{1,0:T(8,128)(2,1)S(1)}, u32[]{:S(2)}, u32[]{:S(2)}) collective-permute-start(bf16[144,128]{1,0:T(8,128)(2,1)S(1)} %get-tuple-element.64), channel_id=1, source_target_pairs={{0,2},{1,3},{2,0},{3,1},{4,6},{5,7},{6,4},{7,5},{8,10},{9,11},{10,... | collective-permute-start | bytes 110600 | tf_op jit(solution)/shard_map/ppermute | solution.py:439
  118.4 5.6 %collective-permute-start.12 = (bf16[144,128]{1,0:T(8,128)(2,1)S(1)}, bf16[144,128]{1,0:T(8,128)(2,1)S(1)}, u32[]{:S(2)}, u32[]{:S(2)}) collective-permute-start(bf16[144,128]{1,0:T(8,128)(2,1)S(1)} %get-tuple-element.65), channel_id=1, source_target_pairs={{0,3},{1,2},{2,1},{3,0},{4,7},{5,6},{6,5},{7,4},{8,11},{9,10},{10,... | collective-permute-start | bytes 110600 | tf_op jit(solution)/shard_map/ppermute | solution.py:439
  118.4 5.6 %collective-permute-start.13 = (bf16[144,128]{1,0:T(8,128)(2,1)S(1)}, bf16[144,128]{1,0:T(8,128)(2,1)S(1)}, u32[]{:S(2)}, u32[]{:S(2)}) collective-permute-start(bf16[144,128]{1,0:T(8,128)(2,1)S(1)} %get-tuple-element.66), channel_id=1, source_target_pairs={{0,4},{1,5},{2,6},{3,7},{4,0},{5,1},{6,2},{7,3},{8,12},{9,13},{10,... | collective-permute-start | bytes 110600 | tf_op jit(solution)/shard_map/ppermute | solution.py:439
  120.1 5.2 %collective-permute-start.14 = (bf16[144,128]{1,0:T(8,128)(2,1)S(1)}, bf16[144,128]{1,0:T(8,128)(2,1)S(1)}, u32[]{:S(2)}, u32[]{:S(2)}) collective-permute-start(bf16[144,128]{1,0:T(8,128)(2,1)S(1)} %get-tuple-element.67), channel_id=1, source_target_pairs={{0,5},{1,4},{2,7},{3,6},{4,1},{5,0},{6,3},{7,2},{8,13},{9,12},{10,... | collective-permute-start | bytes 110600 | tf_op jit(solution)/shard_map/ppermute | solution.py:439
  120.2 6.5 %collective-permute-start.15 = (bf16[144,128]{1,0:T(8,128)(2,1)S(1)}, bf16[144,128]{1,0:T(8,128)(2,1)S(1)}, u32[]{:S(2)}, u32[]{:S(2)}) collective-permute-start(bf16[144,128]{1,0:T(8,128)(2,1)S(1)} %get-tuple-element.68), channel_id=1, source_target_pairs={{0,6},{1,7},{2,4},{3,5},{4,2},{5,3},{6,0},{7,1},{8,14},{9,15},{10,... | collective-permute-start | bytes 110600 | tf_op jit(solution)/shard_map/ppermute | solution.py:439
  122.8 4.6 %collective-permute-start.16 = (bf16[144,128]{1,0:T(8,128)(2,1)S(1)}, bf16[144,128]{1,0:T(8,128)(2,1)S(1)}, u32[]{:S(2)}, u32[]{:S(2)}) collective-permute-start(bf16[144,128]{1,0:T(8,128)(2,1)S(1)} %get-tuple-element.69), channel_id=1, source_target_pairs={{0,7},{1,6},{2,5},{3,4},{4,3},{5,2},{6,1},{7,0},{8,15},{9,14},{10,... | collective-permute-start | bytes 110600 | tf_op jit(solution)/shard_map/ppermute | solution.py:439
  127.4 10.5 %collective-permute-start.19 = (bf16[144,128]{1,0:T(8,128)(2,1)S(1)}, bf16[144,128]{1,0:T(8,128)(2,1)S(1)}, u32[]{:S(2)}, u32[]{:S(2)}) collective-permute-start(bf16[144,128]{1,0:T(8,128)(2,1)S(1)} %shard_map.116.refs_4_), channel_id=1, source_target_pairs={{0,24},{8,0},{16,8},{24,16},{1,25},{9,1},{17,9},{25,17},{2,26},{10... | collective-permute-start | bytes 110600 | tf_op jit(solution)/shard_map/ppermute | solution.py:444
  132.9 7.8 %collective-permute-start.18 = (bf16[144,128]{1,0:T(8,128)(2,1)S(1)}, bf16[144,128]{1,0:T(8,128)(2,1)S(1)}, u32[]{:S(2)}, u32[]{:S(2)}) collective-permute-start(bf16[144,128]{1,0:T(8,128)(2,1)S(1)} %shard_map.116.refs_4_), channel_id=1, source_target_pairs={{0,16},{8,24},{16,0},{24,8},{1,17},{9,25},{17,1},{25,9},{2,18},{10... | collective-permute-start | bytes 110600 | tf_op jit(solution)/shard_map/ppermute | solution.py:444
  132.9 7.8 %collective-permute-start.17 = (bf16[144,128]{1,0:T(8,128)(2,1)S(1)}, bf16[144,128]{1,0:T(8,128)(2,1)S(1)}, u32[]{:S(2)}, u32[]{:S(2)}) collective-permute-start(bf16[144,128]{1,0:T(8,128)(2,1)S(1)} %shard_map.116.refs_4_), channel_id=1, source_target_pairs={{0,8},{8,16},{16,24},{24,0},{1,9},{9,17},{17,25},{25,1},{2,10},{10... | collective-permute-start | bytes 110600 | tf_op jit(solution)/shard_map/ppermute | solution.py:444

commit v14 on v11

--- a/solution.py
+++ b/solution.py
@@ -5,13 +5,14 @@
 from jax import lax
 from jax.experimental import pallas as pl
 from jax.experimental.pallas import tpu as pltpu
-from jax.sharding import PartitionSpec as P
+from jax.sharding import Mesh, PartitionSpec as P
 
 LAYERS = 2
 TAPS = 5
 DMAX = 8
 HALO = 2 * DMAX
-AXES = ("seg", "grp")
+GRP = ("chip", "core")
+AXES = ("seg",) + GRP
 BF16 = jnp.bfloat16
 F32 = jnp.float32
 BIG_VMEM = 60 * 1024 * 1024
@@ -186,15 +187,21 @@
     load = pltpu.make_async_copy(slope_hbm.at[0], slopes, sem.at[0])
     load.start()
     pad = jnp.zeros((rows_step, wide - cols, ch), F32)
-    for at in range(0, rows, rows_step):
+
+    def columns(at):
         x = jnp.concatenate([x_ref[at : at + rows_step].astype(F32), pad], axis=1).reshape(flat, ch)
         x_cat = jnp.concatenate([roll_rows(x, 1), x, roll_rows(x, -1)], axis=1)
-        cat_ref[:, at * wide : at * wide + flat] = x_cat.T.astype(BF16)
+        return x_cat.T.astype(BF16)
+
+    early = cat_ref.shape[1] // flat
+    for n in range(early):
+        cat_ref[:, n * flat : (n + 1) * flat] = columns(n * rows_step)
     load.wait()
     fill_grads(rows_step, gs, got_ref, slopes)
     total = jnp.zeros((3 * ch, 3 * ch), F32)
-    for at in range(0, rows, rows_step):
-        total = total + mm(cat_ref[:, at * wide : at * wide + flat], taps_up(gs, at, rows_step))
+    for n, at in enumerate(range(0, rows, rows_step)):
+        cat = cat_ref[:, n * flat : (n + 1) * flat] if n < early else columns(at)
+        total = total + mm(cat, taps_up(gs, at, rows_step))
     total_ref[...] = (
         jnp.concatenate(
             [
@@ -246,8 +253,8 @@
 
 def temporal_kernel(
     step_frames, dil_ref, key_ref, got_ref, tw_hbm, uw_hbm,
-    grad_hbm, kept_hbm, united_hbm,
-    a0, a1, feat, cots, g0, g1, slope0, slope1, united_ref, grad_ref, tw_ref, uw_ref,
+    grad_hbm, kept_hbm,
+    a0, a1, feat, cots, g0, g1, slope0, slope1, grad_ref, tw_ref, uw_ref,
     sems, in_sems, out_sems,
 ):
     frames, _, block, ch = got_ref.shape
@@ -277,7 +284,6 @@
                 (g0.at[inside], kept_hbm.at[3]),
                 (a0.at[inside], kept_hbm.at[4]),
                 (cots, kept_hbm.at[5]),
-                (united_ref, united_hbm.at[0]),
             )
         )
     ]
@@ -307,12 +313,6 @@
     copies[5].start()
     for seg in range(segs):
         low, top = seg * seg_frames, (seg + 1) * seg_frames
-        here = low + key_ref[seg]
-        key_part = mm(feat[here], uw_ref[1])
-        main = mm(feat[low:top].reshape(seg_frames * high, ch), uw_ref[0]).reshape(
-            seg_frames, high, ch
-        )
-        united_ref[low:top] = (main + key_part[None]).astype(BF16)[:, :block]
         mine = cots[low:top]
         total = jnp.sum(mine.astype(F32), axis=0)
         key_term = sum(mm_nt(part, uw_ref[1]) for part in three_parts(total))
@@ -322,7 +322,6 @@
         for n in range(seg_frames):
             grad = grad_feat[n] + jnp.where(key_ref[seg] == n, key_term, 0.0)
             g1[HALO + low + n] = (grad * slope1[low + n]).astype(BF16)
-    copies[6].start()
     for layer, source in ((1, g1), (0, g0)):
         copies[3 - layer].start()
         step_size = dil_ref[layer]
@@ -346,7 +345,7 @@
 
 def temporal_wgrad_kernel(
     step_frames, scale, here_ref, dil_ref, key_ref,
-    kept_hbm, united_kept, united_hbm, *rest
+    kept_hbm, uw_ref, united_hbm, *rest
 ):
     pieces, (a0, g0, a1, g1, feat, cots, united, total_ref, sems) = rest[:-9], rest[-9:]
     frames, high, ch = feat.shape
@@ -358,13 +357,12 @@
         pltpu.make_async_copy(source, target, sems.at[n])
         for n, (source, target) in enumerate(
             (
+                (kept_hbm.at[1], feat),
                 (kept_hbm.at[4], a0.at[inside]),
                 (kept_hbm.at[3], g0),
                 (kept_hbm.at[0], a1.at[inside]),
                 (kept_hbm.at[2], g1),
-                (kept_hbm.at[1], feat),
                 (kept_hbm.at[5], cots),
-                (united_kept.at[0], united),
             )
         )
     ]
@@ -372,10 +370,21 @@
         copy.start()
     clear_halo(a0, frames)
     clear_halo(a1, frames)
+    copies[0].wait()
+    block = united.shape[1]
+    for seg in range(segs):
+        low, top = seg * seg_frames, (seg + 1) * seg_frames
+        key_part = mm(feat[low + key_ref[seg]], uw_ref[1])
+        main = mm(feat[low:top].reshape(seg_frames * high, ch), uw_ref[0]).reshape(
+            seg_frames, high, ch
+        )
+        united[low:top] = (main + key_part[None]).astype(BF16)[:, :block]
+    united_copy = pltpu.make_async_copy(united, united_hbm, sems.at[len(copies)])
+    united_copy.start()
     totals = []
     for layer, acts, grads in ((0, a0, g0), (1, a1, g1)):
-        copies[2 * layer].wait()
         copies[2 * layer + 1].wait()
+        copies[2 * layer + 2].wait()
         total = jnp.zeros((TAPS * ch, ch), F32)
         for at in range(0, frames, step_frames):
             total = total + mm_tn(
@@ -383,10 +392,7 @@
                 grads[at : at + step_frames].reshape(rows, ch),
             )
         totals.append(total)
-    for copy in copies[4:]:
-        copy.wait()
-    united_copy = pltpu.make_async_copy(united, united_hbm, sems.at[len(copies)])
-    united_copy.start()
+    copies[5].wait()
     total = jnp.zeros((ch, ch), F32)
     for at in range(0, frames, step_frames):
         total = total + mm_tn(
@@ -440,8 +446,8 @@
 
 
 def flip(value, peer):
-    size = lax.axis_size("grp")
-    return lax.ppermute(value, "grp", [(i, i ^ peer) for i in range(size)])
+    size = lax.axis_size("chip") * lax.axis_size("core")
+    return lax.ppermute(value, GRP, [(i, i ^ peer) for i in range(size)])
 
 
 def turn_by(value, turn):
@@ -471,7 +477,7 @@
     held, rows, cols, ch = frames_in.shape
     assert held == 1
     pixels = rows * cols
-    peers = lax.axis_size("grp")
+    peers = lax.axis_size("chip") * lax.axis_size("core")
     devices = lax.axis_size("seg") * peers
     frames = held * devices
     block = pixels // devices
@@ -479,13 +485,14 @@
     wide = round_up(cols + 1, 16)
     high = round_up(block, 16)
     rows_step = next(n for n in (4, 2, 1) if rows % n == 0)
+    steps = rows // rows_step
     parts = next(n for n in (4, 2, 1) if rows % (n * rows_step) == 0)
     step_frames, narrow_step = (
         max(n for n in range(1, frames + 1) if frames % n == 0 and n * high <= most)
         for most in (512, 256)
     )
     scale = float((frames * pixels) ** -0.5)
-    here = jnp.stack([lax.axis_index("seg"), lax.axis_index("grp")]).astype(jnp.int32)
+    here = jnp.stack([lax.axis_index("seg"), lax.axis_index(GRP)]).astype(jnp.int32)
     space_rows, time_rows, unite_rows = (n * ch // peers for n in (9, LAYERS * TAPS, 2))
 
     (send,) = call(
@@ -524,12 +531,11 @@
 
     padded = (frames + 2 * HALO, high, ch)
     whole = (frames, high, ch)
-    grad_send, kept, united_kept = call(
+    grad_send, kept = call(
         functools.partial(temporal_kernel, narrow_step),
         [
             ((frames, block, ch), BF16, HBM),
             ((SPARE,) + whole, BF16, HBM),
-            ((SPARE, frames, block, ch), BF16, HBM),
         ],
         [
             pltpu.VMEM(padded, BF16),
@@ -541,10 +547,9 @@
             pltpu.VMEM(whole, F32),
             pltpu.VMEM(whole, F32),
             pltpu.VMEM((frames, block, ch), BF16),
-            pltpu.VMEM((frames, block, ch), BF16),
             pltpu.VMEM(temporal_weight.shape, BF16),
             pltpu.VMEM(uniting_weight.shape, BF16),
-            pltpu.SemaphoreType.DMA((7,)),
+            pltpu.SemaphoreType.DMA((6,)),
             pltpu.SemaphoreType.DMA((2,)),
             pltpu.SemaphoreType.DMA((frames // narrow_step,)),
         ],
@@ -570,13 +575,13 @@
             pltpu.VMEM(whole, BF16),
             pltpu.VMEM((frames, block, ch), BF16),
             pltpu.VMEM((peers, time_rows + unite_rows, ch), F32),
-            pltpu.SemaphoreType.DMA((8,)),
+            pltpu.SemaphoreType.DMA((7,)),
         ],
         2 * 12 * frames * block * ch * ch,
         frames * block * ch * 14,
         [
             (here, SMEM), (dilation, SMEM), (key_index, SMEM),
-            (kept, HBM), (united_kept, HBM),
+            (kept, HBM), (uniting_weight, VMEM),
         ],
     )
     time_sum = reduce_in_grp(time_pieces)
@@ -589,7 +594,7 @@
         [
             pltpu.VMEM((rows + 2, wide, ch), BF16),
             pltpu.VMEM((rows, cols, ch), BF16),
-            pltpu.VMEM((3 * ch, rows * wide), BF16),
+            pltpu.VMEM((3 * ch, min(3, steps) * rows_step * wide), BF16),
             pltpu.VMEM((peers, space_rows, ch), F32),
             pltpu.SemaphoreType.DMA((1,)),
         ],
@@ -624,6 +629,7 @@
     turned = all_turns(plane)
     turned[0], back = lax.optimization_barrier((turned[0], back))
     piece = sum_of(turned)
+    pieces = lax.all_gather(lax.all_gather(piece, "core", axis=0), "chip", axis=0)
     *grads, united = call(
         deal_kernel,
         [((peers, count, ch), F32, HBM) for count in (time_rows, unite_rows, space_rows)]
@@ -632,7 +638,7 @@
         + [pltpu.SemaphoreType.DMA((4,))],
         0,
         6 * 21 * ch * ch,
-        [(lax.all_gather(piece, "grp", axis=0), VMEM), (united, HBM)],
+        [(pieces.reshape(peers, -1, ch), VMEM), (united, HBM)],
         SMALL_VMEM,
     )
     return (
@@ -645,10 +651,12 @@
 
 
 def solution(mesh):
+    segs, peers = (mesh.shape[name] for name in ("seg", "grp"))
+    split = Mesh(mesh.devices.reshape(segs, peers // 2, 2), AXES)
     frame_spec = P(AXES, None, None, None)
     return jax.shard_map(
         local,
-        mesh=mesh,
+        mesh=split,
         in_specs=(frame_spec, P(), P(), P(), P(), P(), frame_spec),
         out_specs=(frame_spec, frame_spec, P(), P(), P()),
         check_vma=False,

time: 146 us -> 152 us (1.041)
  blocking collectives: 10.2 us -> 13.2 us
  starting transfers between devices: 33.9 us -> 36.4 us
  local copies, waits for them, and re-layouts: 0.83 us -> 2.74 us
  waiting for transfers between devices: 58.1 us -> 56.4 us
    all_gather x1 -> x2, blocking collectives: 10.2 us -> 13.2 us  [the longest x1 11.2 us: local(): lax.all_gather(lax.all_gather(piece, 'core', axis=0), 'chip', axis=0)]
    ppermute x14, starting transfers between devices: 12.7 us -> 15.5 us  [flip(): return lax.ppermute(value, GRP, [(i, i ^ peer) for i in range(size)])]
    unnamed x16 -> x18, local copies, waits for them, and re-layouts: 0.83 us -> 2.74 us
  transfers between devices with their start and end apart: 20 -> 20, of which waited for: 10 -> 10; matrix products, arithmetic and copies ran while one was open for 0% -> 0% of each run, Pallas kernels for 16% -> 15%
where the time goes in v14:
time: 152 us; the launch traced here: 151 us
  waiting for transfers between devices  56.4 us (37%)
  Pallas kernels  40.8 us (27%)
  starting transfers between devices  36.4 us (24%)
  blocking collectives  13.2 us (9%)
  local copies, waits for them, and re-layouts  2.74 us (2%)
    all_to_all x3, waiting for transfers between devices, exchange(): return lax.all_to_all(blocks, AXES, split_axis=0, concat_axis=0, tiled=True)  42.5 us
    pallas_call x10, Pallas kernels, call(): pl.pallas_call(kernel, out_shape=[jax.ShapeDtypeStruct(shape, kind) for s...  40.8 us
    all_to_all x3, starting transfers between devices, exchange(): return lax.all_to_all(blocks, AXES, split_axis=0, concat_axis=0, tiled=True)  15.6 us
    ppermute x14, starting transfers between devices, flip(): return lax.ppermute(value, GRP, [(i, i ^ peer) for i in range(size)])  15.5 us
    all_gather x1, blocking collectives, local(): lax.all_gather(lax.all_gather(piece, 'core', axis=0), 'chip', axis=0)  11.2 us
    ppermute x14, waiting for transfers between devices, flip(): return lax.ppermute(value, GRP, [(i, i ^ peer) for i in range(size)])  9.55 us
    ppermute x3, starting transfers between devices, turn_by(): lax.ppermute(value, 'seg', [(i, (i + turn) % size) for i in range(size)])  5.42 us
    ppermute x3, waiting for transfers between devices, turn_by(): lax.ppermute(value, 'seg', [(i, (i + turn) % size) for i in range(size)])  4.31 us
  transfers between devices with their start and end apart: 20, of which 10 were waited for; matrix products, arithmetic and copies ran while one was open for 0% of the time, Pallas kernels for 15%

profile of v14, /device:TPU:0, one launch (start us, length us, event | category | flops | bytes accessed | tf_op | source)
XLA Modules:
  0.0 151.2 jit_solution(17788162422068104555)
XLA Ops:
  0.7 0.0 copy-start.6
  0.7 4.8 %shard_map.110 = bf16[32,2,120,128]{3,2,1,0:T(8,128)(2,1)} custom-call(bf16[32,120,128]{2,1,0:T(8,128)(2,1)} %bitcast.10, bf16[9,128,128]{2,1,0:T(8,128)(2,1)} %w_ref.3, bf16[32,120,128]{2,1,0:T(8,128)(2,1)} %bitcast.13), custom_call_target="tpu_custom_call" | custom-call | flops 1132462080 | bytes 3932160 | tf_op jit(solution)/shard_map/pallas_call | solution.py:59
  5.4 7.5 %all-to-all-start = ((bf16[32,2,120,128]{3,2,1,0:T(8,128)(2,1)}), bf16[32,2,120,128]{3,2,1,0:T(8,128)(2,1)S(1)}, u32[]{:S(2)}, u32[]{:S(2)}) async-start(bf16[32,2,120,128]{3,2,1,0:T(8,128)(2,1)} %shard_map.110), calls=%async_computation | async-start | bytes 3932160 | tf_op jit(solution)/shard_map/all_to_all | solution.py:445
  12.9 4.4 %shard_map.111.slope_hbm = bf16[28,32,120,128]{3,2,1,0:T(8,128)(2,1)} custom-call(bf16[32,120,128]{2,1,0:T(8,128)(2,1)} %bitcast.11, bf16[9,128,128]{2,1,0:T(8,128)(2,1)} %w_ref.3), custom_call_target="tpu_custom_call" | custom-call | flops 1132462080 | bytes 1966080 | tf_op jit(solution)/shard_map/pallas_call | solution.py:59
  17.3 0.0 copy-start
  17.3 41.5 %all-to-all-done.got_ref = bf16[32,2,120,128]{3,2,1,0:T(8,128)(2,1)S(1)} async-done(((bf16[32,2,120,128]{3,2,1,0:T(8,128)(2,1)}), bf16[32,2,120,128]{3,2,1,0:T(8,128)(2,1)S(1)}, u32[]{:S(2)}, u32[]{:S(2)}) %all-to-all-start) | async-done | bytes 1966112 | tf_op jit(solution)/shard_map/all_to_all | solution.py:445
  58.8 0.0 copy-start.8
  58.9 1.0 copy-done.8
  59.8 12.0 %shard_map.112 = (bf16[32,120,128]{2,1,0:T(8,128)(2,1)S(1)}, bf16[28,32,128,128]{3,2,1,0:T(8,128)(2,1)}) custom-call(s32[2]{0:T(128)S(1)} %copy-done.6, s32[4]{0:T(128)S(1)} %copy-done.7, bf16[32,2,120,128]{3,2,1,0:T(8,128)(2,1)S(1)} %all-to-all-done.got_ref, bf16[2,5,128,128]{3,2,1,0:T(8,128)(2,1)S(1)} %copy-done.8, bf16[2,128,128]{2,1,0:T(8,128)(2,1)S(1)} %copy-done.3), custom_call_target="tpu_custom_call" | custom-call | flops 2768240640 | bytes 8847360 | tf_op jit(solution)/shard_map/pallas_call | solution.py:59
  71.9 0.9 copy-done.2
  72.8 4.2 %all-to-all-start.1 = ((bf16[32,120,128]{2,1,0:T(8,128)(2,1)}), bf16[32,120,128]{2,1,0:T(8,128)(2,1)S(1)}, u32[]{:S(2)}, u32[]{:S(2)}) async-start(bf16[32,120,128]{2,1,0:T(8,128)(2,1)} %copy-done.2), calls=%async_computation.1 | async-start | bytes 1966080 | tf_op jit(solution)/shard_map/all_to_all | solution.py:445
  77.0 0.7 pad_add_fusion.here_ref
  77.7 10.0 %shard_map.113 = (bf16[32,120,128]{2,1,0:T(8,128)(2,1)}, bf16[192,128]{1,0:T(8,128)(2,1)}, bf16[192,128]{1,0:T(8,128)(2,1)}, bf16[192,128]{1,0:T(8,128)(2,1)}, b...) custom-call(s32[2]{0:T(128)} %pad_add_fusion.here_ref, ...), custom_call_target="tpu_custom_call" | custom-call | flops 1509949440 | bytes 6881280 | tf_op jit(solution)/shard_map/pallas_call | solution.py:59
  87.7 0.1 collective-permute-start
  87.8 1.7 %collective-permute-start.1 = (bf16[192,128]{1,0:T(8,128)(2,1)}, bf16[192,128]{1,0:T(8,128)(2,1)S(1)}, u32[]{:S(2)}, u32[]{:S(2)}) collective-permute-start(bf16[192,128]{1,0:T(8,128)(2,1)} %get-tuple-element.44), channel_id=1, source_target_pairs={{0,2},{1,3},{2,0},{3,1},{4,6},{5,7},{6,4},{7,5},{8,10},{9,11},{10,... | collective-permute-start | bytes 147464 | tf_op jit(solution)/shard_map/ppermute | solution.py:450
  89.5 0.2 collective-permute-start.2
  89.6 1.5 %collective-permute-start.3 = (bf16[192,128]{1,0:T(8,128)(2,1)}, bf16[192,128]{1,0:T(8,128)(2,1)S(1)}, u32[]{:S(2)}, u32[]{:S(2)}) collective-permute-start(bf16[192,128]{1,0:T(8,128)(2,1)} %get-tuple-element.46), channel_id=1, source_target_pairs={{0,4},{1,5},{2,6},{3,7},{4,0},{5,1},{6,2},{7,3},{8,12},{9,13},{10,... | collective-permute-start | bytes 147464 | tf_op jit(solution)/shard_map/ppermute | solution.py:450
  91.2 0.2 collective-permute-start.4
  91.3 2.5 %collective-permute-start.5 = (bf16[192,128]{1,0:T(8,128)(2,1)}, bf16[192,128]{1,0:T(8,128)(2,1)S(1)}, u32[]{:S(2)}, u32[]{:S(2)}) collective-permute-start(bf16[192,128]{1,0:T(8,128)(2,1)} %get-tuple-element.48), channel_id=1, source_target_pairs={{0,6},{1,7},{2,4},{3,5},{4,2},{5,3},{6,0},{7,1},{8,14},{9,15},{10,... | collective-permute-start | bytes 147464 | tf_op jit(solution)/shard_map/ppermute | solution.py:450
  93.9 0.2 collective-permute-start.6
  94.0 0.1 collective-permute-done.2.refs_3_
  94.2 0.0 collective-permute-done.3.refs_4_
  94.2 2.1 %collective-permute-done.4.refs_5_ = bf16[192,128]{1,0:T(8,128)(2,1)S(1)} collective-permute-done((bf16[192,128]{1,0:T(8,128)(2,1)}, bf16[192,128]{1,0:T(8,128)(2,1)S(1)}, u32[]{:S(2)}, u32[]{:S(2)}) %collective-permute-start.4) | collective-permute-done | bytes 49184 | tf_op jit(solution)/shard_map/ppermute | solution.py:450
  96.3 0.5 collective-permute-done.5.refs_6_
  96.7 3.0 %collective-permute-done.6.refs_7_ = bf16[192,128]{1,0:T(8,128)(2,1)S(1)} collective-permute-done((bf16[192,128]{1,0:T(8,128)(2,1)}, bf16[192,128]{1,0:T(8,128)(2,1)S(1)}, u32[]{:S(2)}, u32[]{:S(2)}) %collective-permute-start.6) | collective-permute-done | bytes 49184 | tf_op jit(solution)/shard_map/ppermute | solution.py:450
  99.7 0.8 copy-done.4
  100.5 0.1 shard_map.114.first_ref
  100.6 1.0 all-to-all-done.1.got_ref
  101.6 3.9 %all-to-all-start.2 = ((bf16[32,120,128]{2,1,0:T(8,128)(2,1)}), bf16[32,120,128]{2,1,0:T(8,128)(2,1)S(1)}, u32[]{:S(2)}, u32[]{:S(2)}) async-start(bf16[32,120,128]{2,1,0:T(8,128)(2,1)} %get-tuple-element.65), calls=%async_computation.2 | async-start | bytes 1966080 | tf_op jit(solution)/shard_map/all_to_all | solution.py:445
  105.5 3.6 %shard_map.115 = (bf16[144,128]{1,0:T(8,128)(2,1)S(1)}, bf16[144,128]{1,0:T(8,128)(2,1)S(1)}, bf16[144,128]{1,0:T(8,128)(2,1)S(1)}, bf16[144,128]{1,0:T(8,128)(2...) custom-call(s32[2]{0:T(128)S(1)} %copy-done.5, ...), custom_call_target="tpu_custom_call" | custom-call | flops 1132462080 | bytes 3932160 | tf_op jit(solution)/shard_map/pallas_call | solution.py:59
  109.2 1.8 %collective-permute-start.10 = (bf16[144,128]{1,0:T(8,128)(2,1)S(1)}, bf16[144,128]{1,0:T(8,128)(2,1)S(1)}, u32[]{:S(2)}, u32[]{:S(2)}) collective-permute-start(bf16[144,128]{1,0:T(8,128)(2,1)S(1)} %get-tuple-element.60), channel_id=1, source_target_pairs={{0,4},{1,5},{2,6},{3,7},{4,0},{5,1},{6,2},{7,3},{8,12},{9,13},{10,... | collective-permute-start | bytes 110600 | tf_op jit(solution)/shard_map/ppermute | solution.py:450
  111.0 2.4 %collective-permute-start.12 = (bf16[144,128]{1,0:T(8,128)(2,1)S(1)}, bf16[144,128]{1,0:T(8,128)(2,1)S(1)}, u32[]{:S(2)}, u32[]{:S(2)}) collective-permute-start(bf16[144,128]{1,0:T(8,128)(2,1)S(1)} %get-tuple-element.62), channel_id=1, source_target_pairs={{0,6},{1,7},{2,4},{3,5},{4,2},{5,3},{6,0},{7,1},{8,14},{9,15},{10,... | collective-permute-start | bytes 110600 | tf_op jit(solution)/shard_map/ppermute | solution.py:450
  113.4 0.3 collective-permute-start.13
  113.7 0.4 collective-permute-start.7
  114.1 0.1 collective-permute-done.10.refs_4_
  114.2 2.1 %collective-permute-start.8 = (bf16[144,128]{1,0:T(8,128)(2,1)S(1)}, bf16[144,128]{1,0:T(8,128)(2,1)S(1)}, u32[]{:S(2)}, u32[]{:S(2)}) collective-permute-start(bf16[144,128]{1,0:T(8,128)(2,1)S(1)} %get-tuple-element.58), channel_id=1, source_target_pairs={{0,2},{1,3},{2,0},{3,1},{4,6},{5,7},{6,4},{7,5},{8,10},{9,11},{10,... | collective-permute-start | bytes 110600 | tf_op jit(solution)/shard_map/ppermute | solution.py:450
  116.3 1.9 %collective-permute-done.11.refs_5_ = bf16[144,128]{1,0:T(8,128)(2,1)S(1)} collective-permute-done((bf16[144,128]{1,0:T(8,128)(2,1)S(1)}, bf16[144,128]{1,0:T(8,128)(2,1)S(1)}, u32[]{:S(2)}, u32[]{:S(2)}) %collective-permute-start.11) | collective-permute-done | bytes 36896 | tf_op jit(solution)/shard_map/ppermute | solution.py:450
  118.2 2.1 %collective-permute-start.9 = (bf16[144,128]{1,0:T(8,128)(2,1)S(1)}, bf16[144,128]{1,0:T(8,128)(2,1)S(1)}, u32[]{:S(2)}, u32[]{:S(2)}) collective-permute-start(bf16[144,128]{1,0:T(8,128)(2,1)S(1)} %get-tuple-element.59), channel_id=1, source_target_pairs={{0,3},{1,2},{2,1},{3,0},{4,7},{5,6},{6,5},{7,4},{8,11},{9,10},{10,... | collective-permute-start | bytes 110600 | tf_op jit(solution)/shard_map/ppermute | solution.py:450
  120.3 1.9 %collective-permute-done.9.refs_3_ = bf16[144,128]{1,0:T(8,128)(2,1)S(1)} collective-permute-done((bf16[144,128]{1,0:T(8,128)(2,1)S(1)}, bf16[144,128]{1,0:T(8,128)(2,1)S(1)}, u32[]{:S(2)}, u32[]{:S(2)}) %collective-permute-start.9) | collective-permute-done | bytes 36896 | tf_op jit(solution)/shard_map/ppermute | solution.py:450
  122.2 0.1 shard_map.116.refs_0_
  122.3 0.6 collective-permute-start.14
  122.8 4.7 %collective-permute-start.15 = (bf16[336,128]{1,0:T(8,128)(2,1)S(1)}, bf16[336,128]{1,0:T(8,128)(2,1)S(1)}, u32[]{:S(2)}, u32[]{:S(2)}) collective-permute-start(bf16[336,128]{1,0:T(8,128)(2,1)S(1)} %shard_map.116.refs_0_), channel_id=1, source_target_pairs={{0,16},{8,24},{16,0},{24,8},{1,17},{9,25},{17,1},{25,9},{2,18},{10... | collective-permute-start | bytes 258056 | tf_op jit(solution)/shard_map/ppermute | solution.py:455
  127.6 0.1 collective-permute-start.16
  127.7 4.3 %shard_map.117 = bf16[32,120,128]{2,1,0:T(8,128)(2,1)} custom-call(bf16[9,128,128]{2,1,0:T(8,128)(2,1)S(1)} %copy-done.1, bf16[32,120,128]{2,1,0:T(8,128)(2,1)S(1)} %all-to-all-done.1.got_ref, bf16[28,32,120,128]{3,2,1,0:T(8,128)(2,1)} %shard_map.111.slope_hbm), custom_call_target="tpu_custom_call" | custom-call | flops 1132462080 | bytes 2949120 | tf_op jit(solution)/shard_map/pallas_call | solution.py:59
  132.0 4.3 %collective-permute-done.15.refs_2_ = bf16[336,128]{1,0:T(8,128)(2,1)S(1)} collective-permute-done((bf16[336,128]{1,0:T(8,128)(2,1)S(1)}, bf16[336,128]{1,0:T(8,128)(2,1)S(1)}, u32[]{:S(2)}, u32[]{:S(2)}) %collective-permute-start.15) | collective-permute-done | bytes 86048 | tf_op jit(solution)/shard_map/ppermute | solution.py:455
  136.4 1.9 %all-gather = bf16[672,128]{1,0:T(8,128)(2,1)S(1)} all-gather(bf16[336,128]{1,0:T(8,128)(2,1)S(1)} %shard_map.118), channel_id=2, replica_groups=mesh['seg'=4,'chip'=4,'core'=2] {'core'}, dimensions={0}, use_global_device_ids=true | all-gather | bytes 258048 | tf_op jit(solution)/shard_map/all_gather | solution.py:632
  138.3 11.2 %all-gather.1.pieces_ref = bf16[8,336,128]{2,1,0:T(8,128)(2,1)S(1)} all-gather(bf16[2,336,128]{2,1,0:T(8,128)(2,1)S(1)} %bitcast.15), channel_id=3, replica_groups=mesh['seg'=4,'chip'=4,'core'=2] {'chip'}, dimensions={0}, use_global_device_ids=true | all-gather | bytes 860160 | tf_op jit(solution)/shard_map/all_gather | solution.py:632
  149.6 1.4 shard_map.119
  (23 shorter events, 0.1 us)
Async XLA Ops:
  0.6 58.2 %copy-start.3 = (bf16[2,128,128]{2,1,0:T(8,128)(2,1)S(1)}, bf16[2,128,128]{2,1,0:T(8,128)(2,1)}, u32[]{:S(2)}) copy-start(bf16[2,128,128]{2,1,0:T(8,128)(2,1)} %uw_ref.1) | copy-start | bytes 196612
  0.6 58.2 %copy-start.7 = (s32[4]{0:T(128)S(1)}, s32[4]{0:T(128)}, u32[]{:S(2)}) copy-start(s32[4]{0:T(128)} %key_ref.3) | copy-start | bytes 52
  0.7 58.2 %copy-start.6 = (s32[2]{0:T(128)S(1)}, s32[2]{0:T(128)}, u32[]{:S(2)}) copy-start(s32[2]{0:T(128)} %dil_ref.3) | copy-start | bytes 28
  5.4 53.4 %all-to-all-start = ((bf16[32,2,120,128]{3,2,1,0:T(8,128)(2,1)}), bf16[32,2,120,128]{3,2,1,0:T(8,128)(2,1)S(1)}, u32[]{:S(2)}, u32[]{:S(2)}) async-start(bf16[32,2,120,128]{3,2,1,0:T(8,128)(2,1)} %shard_map.110), calls=%async_computation | async-start | bytes 3932160 | tf_op jit(solution)/shard_map/all_to_all | solution.py:445
  17.3 88.2 %copy-start = (bf16[1,32,120,128]{3,2,1,0:T(8,128)(2,1)S(1)}, bf16[1,32,120,128]{3,2,1,0:T(8,128)(2,1)}, u32[]{:S(2)}) copy-start(bf16[1,32,120,128]{3,2,1,0:T(8,128)(2,1)} %param.7) | copy-start | bytes 2949124
  58.8 1.0 copy-start.8
  71.9 0.9 copy-start.2
  72.8 28.8 %all-to-all-start.1 = ((bf16[32,120,128]{2,1,0:T(8,128)(2,1)}), bf16[32,120,128]{2,1,0:T(8,128)(2,1)S(1)}, u32[]{:S(2)}, u32[]{:S(2)}) async-start(bf16[32,120,128]{2,1,0:T(8,128)(2,1)} %copy-done.2), calls=%async_computation.1 | async-start | bytes 1966080 | tf_op jit(solution)/shard_map/all_to_all | solution.py:445
  77.7 27.9 %copy-start.5 = (s32[2]{0:T(128)S(1)}, s32[2]{0:T(128)}, u32[]{:S(2)}) copy-start(s32[2]{0:T(128)} %pad_add_fusion.here_ref) | copy-start | bytes 28
  77.7 50.0 %copy-start.1 = (bf16[9,128,128]{2,1,0:T(8,128)(2,1)S(1)}, bf16[9,128,128]{2,1,0:T(8,128)(2,1)}, u32[]{:S(2)}) copy-start(bf16[9,128,128]{2,1,0:T(8,128)(2,1)} %w_ref.3) | copy-start | bytes 884740
  87.7 3.6 %collective-permute-start = (bf16[192,128]{1,0:T(8,128)(2,1)}, bf16[192,128]{1,0:T(8,128)(2,1)S(1)}, u32[]{:S(2)}, u32[]{:S(2)}) collective-permute-start(bf16[192,128]{1,0:T(8,128)(2,1)} %get-tuple-element.43), channel_id=1, source_target_pairs={{0,1},{1,0},{2,3},{3,2},{4,5},{5,4},{6,7},{7,6},{8,9},{9,8},{10,11... | collective-permute-start | bytes 147464 | tf_op jit(solution)/shard_map/ppermute | solution.py:450
  87.8 6.1 %collective-permute-start.1 = (bf16[192,128]{1,0:T(8,128)(2,1)}, bf16[192,128]{1,0:T(8,128)(2,1)S(1)}, u32[]{:S(2)}, u32[]{:S(2)}) collective-permute-start(bf16[192,128]{1,0:T(8,128)(2,1)} %get-tuple-element.44), channel_id=1, source_target_pairs={{0,2},{1,3},{2,0},{3,1},{4,6},{5,7},{6,4},{7,5},{8,10},{9,11},{10,... | collective-permute-start | bytes 147464 | tf_op jit(solution)/shard_map/ppermute | solution.py:450
  89.5 4.7 %collective-permute-start.2 = (bf16[192,128]{1,0:T(8,128)(2,1)}, bf16[192,128]{1,0:T(8,128)(2,1)S(1)}, u32[]{:S(2)}, u32[]{:S(2)}) collective-permute-start(bf16[192,128]{1,0:T(8,128)(2,1)} %get-tuple-element.45), channel_id=1, source_target_pairs={{0,3},{1,2},{2,1},{3,0},{4,7},{5,6},{6,5},{7,4},{8,11},{9,10},{10,... | collective-permute-start | bytes 147464 | tf_op jit(solution)/shard_map/ppermute | solution.py:450
  89.6 4.5 %collective-permute-start.3 = (bf16[192,128]{1,0:T(8,128)(2,1)}, bf16[192,128]{1,0:T(8,128)(2,1)S(1)}, u32[]{:S(2)}, u32[]{:S(2)}) collective-permute-start(bf16[192,128]{1,0:T(8,128)(2,1)} %get-tuple-element.46), channel_id=1, source_target_pairs={{0,4},{1,5},{2,6},{3,7},{4,0},{5,1},{6,2},{7,3},{8,12},{9,13},{10,... | collective-permute-start | bytes 147464 | tf_op jit(solution)/shard_map/ppermute | solution.py:450
  91.2 5.1 %collective-permute-start.4 = (bf16[192,128]{1,0:T(8,128)(2,1)}, bf16[192,128]{1,0:T(8,128)(2,1)S(1)}, u32[]{:S(2)}, u32[]{:S(2)}) collective-permute-start(bf16[192,128]{1,0:T(8,128)(2,1)} %get-tuple-element.47), channel_id=1, source_target_pairs={{0,5},{1,4},{2,7},{3,6},{4,1},{5,0},{6,3},{7,2},{8,13},{9,12},{10,... | collective-permute-start | bytes 147464 | tf_op jit(solution)/shard_map/ppermute | solution.py:450
  91.3 5.4 %collective-permute-start.5 = (bf16[192,128]{1,0:T(8,128)(2,1)}, bf16[192,128]{1,0:T(8,128)(2,1)S(1)}, u32[]{:S(2)}, u32[]{:S(2)}) collective-permute-start(bf16[192,128]{1,0:T(8,128)(2,1)} %get-tuple-element.48), channel_id=1, source_target_pairs={{0,6},{1,7},{2,4},{3,5},{4,2},{5,3},{6,0},{7,1},{8,14},{9,15},{10,... | collective-permute-start | bytes 147464 | tf_op jit(solution)/shard_map/ppermute | solution.py:450
  93.9 5.8 %collective-permute-start.6 = (bf16[192,128]{1,0:T(8,128)(2,1)}, bf16[192,128]{1,0:T(8,128)(2,1)S(1)}, u32[]{:S(2)}, u32[]{:S(2)}) collective-permute-start(bf16[192,128]{1,0:T(8,128)(2,1)} %get-tuple-element.49), channel_id=1, source_target_pairs={{0,7},{1,6},{2,5},{3,4},{4,3},{5,2},{6,1},{7,0},{8,15},{9,14},{10,... | collective-permute-start | bytes 147464 | tf_op jit(solution)/shard_map/ppermute | solution.py:450
  99.7 0.8 copy-start.4
  101.6 48.0 %all-to-all-start.2 = ((bf16[32,120,128]{2,1,0:T(8,128)(2,1)}), bf16[32,120,128]{2,1,0:T(8,128)(2,1)S(1)}, u32[]{:S(2)}, u32[]{:S(2)}) async-start(bf16[32,120,128]{2,1,0:T(8,128)(2,1)} %get-tuple-element.65), calls=%async_computation.2 | async-start | bytes 1966080 | tf_op jit(solution)/shard_map/all_to_all | solution.py:445
  109.2 5.0 %collective-permute-start.10 = (bf16[144,128]{1,0:T(8,128)(2,1)S(1)}, bf16[144,128]{1,0:T(8,128)(2,1)S(1)}, u32[]{:S(2)}, u32[]{:S(2)}) collective-permute-start(bf16[144,128]{1,0:T(8,128)(2,1)S(1)} %get-tuple-element.60), channel_id=1, source_target_pairs={{0,4},{1,5},{2,6},{3,7},{4,0},{5,1},{6,2},{7,3},{8,12},{9,13},{10,... | collective-permute-start | bytes 110600 | tf_op jit(solution)/shard_map/ppermute | solution.py:450
  111.0 7.2 %collective-permute-start.11 = (bf16[144,128]{1,0:T(8,128)(2,1)S(1)}, bf16[144,128]{1,0:T(8,128)(2,1)S(1)}, u32[]{:S(2)}, u32[]{:S(2)}) collective-permute-start(bf16[144,128]{1,0:T(8,128)(2,1)S(1)} %get-tuple-element.61), channel_id=1, source_target_pairs={{0,5},{1,4},{2,7},{3,6},{4,1},{5,0},{6,3},{7,2},{8,13},{9,12},{10,... | collective-permute-start | bytes 110600 | tf_op jit(solution)/shard_map/ppermute | solution.py:450
  111.0 9.3 %collective-permute-start.12 = (bf16[144,128]{1,0:T(8,128)(2,1)S(1)}, bf16[144,128]{1,0:T(8,128)(2,1)S(1)}, u32[]{:S(2)}, u32[]{:S(2)}) collective-permute-start(bf16[144,128]{1,0:T(8,128)(2,1)S(1)} %get-tuple-element.62), channel_id=1, source_target_pairs={{0,6},{1,7},{2,4},{3,5},{4,2},{5,3},{6,0},{7,1},{8,14},{9,15},{10,... | collective-permute-start | bytes 110600 | tf_op jit(solution)/shard_map/ppermute | solution.py:450
  113.4 6.9 %collective-permute-start.13 = (bf16[144,128]{1,0:T(8,128)(2,1)S(1)}, bf16[144,128]{1,0:T(8,128)(2,1)S(1)}, u32[]{:S(2)}, u32[]{:S(2)}) collective-permute-start(bf16[144,128]{1,0:T(8,128)(2,1)S(1)} %get-tuple-element.63), channel_id=1, source_target_pairs={{0,7},{1,6},{2,5},{3,4},{4,3},{5,2},{6,1},{7,0},{8,15},{9,14},{10,... | collective-permute-start | bytes 110600 | tf_op jit(solution)/shard_map/ppermute | solution.py:450
  113.7 6.6 %collective-permute-start.7 = (bf16[144,128]{1,0:T(8,128)(2,1)S(1)}, bf16[144,128]{1,0:T(8,128)(2,1)S(1)}, u32[]{:S(2)}, u32[]{:S(2)}) collective-permute-start(bf16[144,128]{1,0:T(8,128)(2,1)S(1)} %get-tuple-element.57), channel_id=1, source_target_pairs={{0,1},{1,0},{2,3},{3,2},{4,5},{5,4},{6,7},{7,6},{8,9},{9,8},{10,11... | collective-permute-start | bytes 110600 | tf_op jit(solution)/shard_map/ppermute | solution.py:450
  114.2 6.1 %collective-permute-start.8 = (bf16[144,128]{1,0:T(8,128)(2,1)S(1)}, bf16[144,128]{1,0:T(8,128)(2,1)S(1)}, u32[]{:S(2)}, u32[]{:S(2)}) collective-permute-start(bf16[144,128]{1,0:T(8,128)(2,1)S(1)} %get-tuple-element.58), channel_id=1, source_target_pairs={{0,2},{1,3},{2,0},{3,1},{4,6},{5,7},{6,4},{7,5},{8,10},{9,11},{10,... | collective-permute-start | bytes 110600 | tf_op jit(solution)/shard_map/ppermute | solution.py:450
  118.2 4.0 %collective-permute-start.9 = (bf16[144,128]{1,0:T(8,128)(2,1)S(1)}, bf16[144,128]{1,0:T(8,128)(2,1)S(1)}, u32[]{:S(2)}, u32[]{:S(2)}) collective-permute-start(bf16[144,128]{1,0:T(8,128)(2,1)S(1)} %get-tuple-element.59), channel_id=1, source_target_pairs={{0,3},{1,2},{2,1},{3,0},{4,7},{5,6},{6,5},{7,4},{8,11},{9,10},{10,... | collective-permute-start | bytes 110600 | tf_op jit(solution)/shard_map/ppermute | solution.py:450
  122.3 9.8 %collective-permute-start.14 = (bf16[336,128]{1,0:T(8,128)(2,1)S(1)}, bf16[336,128]{1,0:T(8,128)(2,1)S(1)}, u32[]{:S(2)}, u32[]{:S(2)}) collective-permute-start(bf16[336,128]{1,0:T(8,128)(2,1)S(1)} %shard_map.116.refs_0_), channel_id=1, source_target_pairs={{0,8},{8,16},{16,24},{24,0},{1,9},{9,17},{17,25},{25,1},{2,10},{10... | collective-permute-start | bytes 258056 | tf_op jit(solution)/shard_map/ppermute | solution.py:455
  122.8 13.5 %collective-permute-start.15 = (bf16[336,128]{1,0:T(8,128)(2,1)S(1)}, bf16[336,128]{1,0:T(8,128)(2,1)S(1)}, u32[]{:S(2)}, u32[]{:S(2)}) collective-permute-start(bf16[336,128]{1,0:T(8,128)(2,1)S(1)} %shard_map.116.refs_0_), channel_id=1, source_target_pairs={{0,16},{8,24},{16,0},{24,8},{1,17},{9,25},{17,1},{25,9},{2,18},{10... | collective-permute-start | bytes 258056 | tf_op jit(solution)/shard_map/ppermute | solution.py:455
  127.6 8.8 %collective-permute-start.16 = (bf16[336,128]{1,0:T(8,128)(2,1)S(1)}, bf16[336,128]{1,0:T(8,128)(2,1)S(1)}, u32[]{:S(2)}, u32[]{:S(2)}) collective-permute-start(bf16[336,128]{1,0:T(8,128)(2,1)S(1)} %shard_map.116.refs_0_), channel_id=1, source_target_pairs={{0,24},{8,0},{16,8},{24,16},{1,25},{9,1},{17,9},{25,17},{2,26},{10... | collective-permute-start | bytes 258056 | tf_op jit(solution)/shard_map/ppermute | solution.py:455

commit v15 on v11

--- a/solution.py
+++ b/solution.py
@@ -186,15 +186,21 @@
     load = pltpu.make_async_copy(slope_hbm.at[0], slopes, sem.at[0])
     load.start()
     pad = jnp.zeros((rows_step, wide - cols, ch), F32)
-    for at in range(0, rows, rows_step):
+
+    def columns(at):
         x = jnp.concatenate([x_ref[at : at + rows_step].astype(F32), pad], axis=1).reshape(flat, ch)
         x_cat = jnp.concatenate([roll_rows(x, 1), x, roll_rows(x, -1)], axis=1)
-        cat_ref[:, at * wide : at * wide + flat] = x_cat.T.astype(BF16)
+        return x_cat.T.astype(BF16)
+
+    early = cat_ref.shape[1] // flat
+    for n in range(early):
+        cat_ref[:, n * flat : (n + 1) * flat] = columns(n * rows_step)
     load.wait()
     fill_grads(rows_step, gs, got_ref, slopes)
     total = jnp.zeros((3 * ch, 3 * ch), F32)
-    for at in range(0, rows, rows_step):
-        total = total + mm(cat_ref[:, at * wide : at * wide + flat], taps_up(gs, at, rows_step))
+    for n, at in enumerate(range(0, rows, rows_step)):
+        cat = cat_ref[:, n * flat : (n + 1) * flat] if n < early else columns(at)
+        total = total + mm(cat, taps_up(gs, at, rows_step))
     total_ref[...] = (
         jnp.concatenate(
             [
@@ -305,22 +311,28 @@
         copies[layer].start()
     cots[:, :block, :] = got_ref[:, 1]
     copies[5].start()
+    keys = jnp.concatenate([feat[seg * seg_frames + key_ref[seg]] for seg in range(segs)], axis=0)
+    key_parts = mm(keys, uw_ref[1]).reshape(segs, high, ch)
+    totals = jnp.concatenate(
+        [
+            jnp.sum(cots[seg * seg_frames : (seg + 1) * seg_frames].astype(F32), axis=0)
+            for seg in range(segs)
+        ],
+        axis=0,
+    )
+    key_terms = mm_nt(jnp.concatenate(three_parts(totals), axis=0), uw_ref[1])
+    key_terms = jnp.sum(key_terms.reshape(3, segs, high, ch), axis=0)
     for seg in range(segs):
         low, top = seg * seg_frames, (seg + 1) * seg_frames
-        here = low + key_ref[seg]
-        key_part = mm(feat[here], uw_ref[1])
         main = mm(feat[low:top].reshape(seg_frames * high, ch), uw_ref[0]).reshape(
             seg_frames, high, ch
         )
-        united_ref[low:top] = (main + key_part[None]).astype(BF16)[:, :block]
-        mine = cots[low:top]
-        total = jnp.sum(mine.astype(F32), axis=0)
-        key_term = sum(mm_nt(part, uw_ref[1]) for part in three_parts(total))
-        grad_feat = mm_nt(mine.reshape(seg_frames * high, ch), uw_ref[0]).reshape(
+        united_ref[low:top] = (main + key_parts[seg][None]).astype(BF16)[:, :block]
+        grad_feat = mm_nt(cots[low:top].reshape(seg_frames * high, ch), uw_ref[0]).reshape(
             seg_frames, high, ch
         )
         for n in range(seg_frames):
-            grad = grad_feat[n] + jnp.where(key_ref[seg] == n, key_term, 0.0)
+            grad = grad_feat[n] + jnp.where(key_ref[seg] == n, key_terms[seg], 0.0)
             g1[HALO + low + n] = (grad * slope1[low + n]).astype(BF16)
     copies[6].start()
     for layer, source in ((1, g1), (0, g0)):
@@ -479,6 +491,7 @@
     wide = round_up(cols + 1, 16)
     high = round_up(block, 16)
     rows_step = next(n for n in (4, 2, 1) if rows % n == 0)
+    steps = rows // rows_step
     parts = next(n for n in (4, 2, 1) if rows % (n * rows_step) == 0)
     step_frames, narrow_step = (
         max(n for n in range(1, frames + 1) if frames % n == 0 and n * high <= most)
@@ -589,7 +602,7 @@
         [
             pltpu.VMEM((rows + 2, wide, ch), BF16),
             pltpu.VMEM((rows, cols, ch), BF16),
-            pltpu.VMEM((3 * ch, rows * wide), BF16),
+            pltpu.VMEM((3 * ch, min(3, steps) * rows_step * wide), BF16),
             pltpu.VMEM((peers, space_rows, ch), F32),
             pltpu.SemaphoreType.DMA((1,)),
         ],

time: 146 us -> 146 us (level)
  starting transfers between devices: 33.9 us -> 37.7 us
  waiting for transfers between devices: 58.1 us -> 55.1 us
    ppermute x14, starting transfers between devices: 12.7 us -> 15.5 us  [flip(): return lax.ppermute(value, 'grp', [(i, i ^ peer) for i in range(size)])]
    ppermute x3, waiting for transfers between devices: 4.35 us -> 2.76 us  [turn_by(): lax.ppermute(value, 'seg', [(i, (i + turn) % size) for i in range(size)])]
  transfers between devices with their start and end apart: 20 -> 20, of which waited for: 10 -> 9; matrix products, arithmetic and copies ran while one was open for 0% -> 0% of each run, Pallas kernels for 16% -> 15%
where the time goes in v15:
time: 146 us; the launch traced here: 145 us
  waiting for transfers between devices  55.1 us (38%)
  Pallas kernels  39.6 us (27%)
  starting transfers between devices  37.7 us (26%)
  blocking collectives  10.2 us (7%)
    all_to_all x3, waiting for transfers between devices, exchange(): return lax.all_to_all(blocks, AXES, split_axis=0, concat_axis=0, tiled=True)  43.3 us
    pallas_call x10, Pallas kernels, call(): pl.pallas_call(kernel, out_shape=[jax.ShapeDtypeStruct(shape, kind) for s...  39.6 us
    ppermute x14, starting transfers between devices, flip(): return lax.ppermute(value, 'grp', [(i, i ^ peer) for i in range(size)])  15.5 us
    all_to_all x3, starting transfers between devices, exchange(): return lax.all_to_all(blocks, AXES, split_axis=0, concat_axis=0, tiled=True)  15.3 us
    all_gather x1, blocking collectives, local(): lax.all_gather(piece, 'grp', axis=0)  10.2 us
    ppermute x14, waiting for transfers between devices, flip(): return lax.ppermute(value, 'grp', [(i, i ^ peer) for i in range(size)])  9.03 us
    ppermute x3, starting transfers between devices, turn_by(): lax.ppermute(value, 'seg', [(i, (i + turn) % size) for i in range(size)])  6.96 us
  transfers between devices with their start and end apart: 20, of which 9 were waited for; matrix products, arithmetic and copies ran while one was open for 0% of the time, Pallas kernels for 15%

profile of v15, /device:TPU:0, one launch (start us, length us, event | category | flops | bytes accessed | tf_op | source)
XLA Modules:
  0.0 145.1 jit_solution(10765154410157477376)
XLA Ops:
  0.6 0.0 copy-start.5
  0.7 0.0 copy-start.4
  0.7 4.8 %shard_map.110 = bf16[32,2,120,128]{3,2,1,0:T(8,128)(2,1)} custom-call(bf16[32,120,128]{2,1,0:T(8,128)(2,1)} %bitcast.10, bf16[9,128,128]{2,1,0:T(8,128)(2,1)} %w_ref.3, bf16[32,120,128]{2,1,0:T(8,128)(2,1)} %bitcast.14), custom_call_target="tpu_custom_call" | custom-call | flops 1132462080 | bytes 3932160 | tf_op jit(solution)/shard_map/pallas_call | solution.py:58
  5.5 7.5 %all-to-all-start = ((bf16[32,2,120,128]{3,2,1,0:T(8,128)(2,1)}), bf16[32,2,120,128]{3,2,1,0:T(8,128)(2,1)S(1)}, u32[]{:S(2)}, u32[]{:S(2)}) async-start(bf16[32,2,120,128]{3,2,1,0:T(8,128)(2,1)} %shard_map.110), calls=%async_computation | async-start | bytes 3932160 | tf_op jit(solution)/shard_map/all_to_all | solution.py:451
  13.0 4.4 %shard_map.111.slope_hbm = bf16[28,32,120,128]{3,2,1,0:T(8,128)(2,1)} custom-call(bf16[32,120,128]{2,1,0:T(8,128)(2,1)} %bitcast.11, bf16[9,128,128]{2,1,0:T(8,128)(2,1)} %w_ref.3), custom_call_target="tpu_custom_call" | custom-call | flops 1132462080 | bytes 1966080 | tf_op jit(solution)/shard_map/pallas_call | solution.py:58
  17.4 41.5 %all-to-all-done.got_ref = bf16[32,2,120,128]{3,2,1,0:T(8,128)(2,1)S(1)} async-done(((bf16[32,2,120,128]{3,2,1,0:T(8,128)(2,1)}), bf16[32,2,120,128]{3,2,1,0:T(8,128)(2,1)S(1)}, u32[]{:S(2)}, u32[]{:S(2)}) %all-to-all-start) | async-done | bytes 1966112 | tf_op jit(solution)/shard_map/all_to_all | solution.py:451
  58.9 11.1 %shard_map.112 = (bf16[32,120,128]{2,1,0:T(8,128)(2,1)}, bf16[28,32,128,128]{3,2,1,0:T(8,128)(2,1)}, bf16[28,32,120,128]{3,2,1,0:T(8,128)(2,1)}) custom-call(s32[2]{0:T(128)S(1)} %copy-done.4, s32[4]{0:T(128)S(1)} %copy-done.5, bf16[32,2,120,128]{3,2,1,0:T(8,128)(2,1)S(1)} %all-to-all-done.got_ref, bf16[2,5,128,128]{3,2,1,0:T(8,128)(2,1)S(1)} %copy-done.6, ...), custom_call_target="tpu_custom_call" | custom-call | flops 2768240640 | bytes 8847360 | tf_op jit(solution)/shard_map/pallas_call | solution.py:58
  70.0 4.2 %all-to-all-start.1 = ((bf16[32,120,128]{2,1,0:T(8,128)(2,1)}), bf16[32,120,128]{2,1,0:T(8,128)(2,1)S(1)}, u32[]{:S(2)}, u32[]{:S(2)}) async-start(bf16[32,120,128]{2,1,0:T(8,128)(2,1)} %get-tuple-element.52), calls=%async_computation.1 | async-start | bytes 1966080 | tf_op jit(solution)/shard_map/all_to_all | solution.py:451
  74.2 0.7 pad_add_fusion.here_ref
  74.8 9.8 %shard_map.113 = (bf16[32,120,128]{2,1,0:T(8,128)(2,1)}, bf16[192,128]{1,0:T(8,128)(2,1)}, bf16[192,128]{1,0:T(8,128)(2,1)}, bf16[192,128]{1,0:T(8,128)(2,1)}, b...) custom-call(s32[2]{0:T(128)} %pad_add_fusion.here_ref, ...), custom_call_target="tpu_custom_call" | custom-call | flops 1509949440 | bytes 6881280 | tf_op jit(solution)/shard_map/pallas_call | solution.py:58
  84.6 0.0 copy-start.1
  84.6 0.1 collective-permute-start
  84.7 1.7 %collective-permute-start.1 = (bf16[192,128]{1,0:T(8,128)(2,1)}, bf16[192,128]{1,0:T(8,128)(2,1)S(1)}, u32[]{:S(2)}, u32[]{:S(2)}) collective-permute-start(bf16[192,128]{1,0:T(8,128)(2,1)} %get-tuple-element.46), channel_id=1, source_target_pairs={{0,2},{1,3},{2,0},{3,1},{4,6},{5,7},{6,4},{7,5},{8,10},{9,11},{10,... | collective-permute-start | bytes 147464 | tf_op jit(solution)/shard_map/ppermute | solution.py:456
  86.4 0.2 collective-permute-start.2
  86.6 1.5 %collective-permute-start.3 = (bf16[192,128]{1,0:T(8,128)(2,1)}, bf16[192,128]{1,0:T(8,128)(2,1)S(1)}, u32[]{:S(2)}, u32[]{:S(2)}) collective-permute-start(bf16[192,128]{1,0:T(8,128)(2,1)} %get-tuple-element.48), channel_id=1, source_target_pairs={{0,4},{1,5},{2,6},{3,7},{4,0},{5,1},{6,2},{7,3},{8,12},{9,13},{10,... | collective-permute-start | bytes 147464 | tf_op jit(solution)/shard_map/ppermute | solution.py:456
  88.1 0.2 collective-permute-start.4
  88.3 2.5 %collective-permute-start.5 = (bf16[192,128]{1,0:T(8,128)(2,1)}, bf16[192,128]{1,0:T(8,128)(2,1)S(1)}, u32[]{:S(2)}, u32[]{:S(2)}) collective-permute-start(bf16[192,128]{1,0:T(8,128)(2,1)} %get-tuple-element.50), channel_id=1, source_target_pairs={{0,6},{1,7},{2,4},{3,5},{4,2},{5,3},{6,0},{7,1},{8,14},{9,15},{10,... | collective-permute-start | bytes 147464 | tf_op jit(solution)/shard_map/ppermute | solution.py:456
  90.8 0.0 collective-permute-done.1.refs_2_
  90.8 0.2 collective-permute-start.6
  91.0 0.3 collective-permute-done.2.refs_3_
  91.2 0.0 collective-permute-done.3.refs_4_
  91.2 2.4 %collective-permute-done.4.refs_5_ = bf16[192,128]{1,0:T(8,128)(2,1)S(1)} collective-permute-done((bf16[192,128]{1,0:T(8,128)(2,1)}, bf16[192,128]{1,0:T(8,128)(2,1)S(1)}, u32[]{:S(2)}, u32[]{:S(2)}) %collective-permute-start.4) | collective-permute-done | bytes 49184 | tf_op jit(solution)/shard_map/ppermute | solution.py:456
  93.6 2.5 %collective-permute-done.6.refs_7_ = bf16[192,128]{1,0:T(8,128)(2,1)S(1)} collective-permute-done((bf16[192,128]{1,0:T(8,128)(2,1)}, bf16[192,128]{1,0:T(8,128)(2,1)S(1)}, u32[]{:S(2)}, u32[]{:S(2)}) %collective-permute-start.6) | collective-permute-done | bytes 49184 | tf_op jit(solution)/shard_map/ppermute | solution.py:456
  96.1 0.8 copy-done.2
  96.9 0.1 shard_map.114.first_ref
  97.0 1.8 %all-to-all-done.1.got_ref = bf16[32,120,128]{2,1,0:T(8,128)(2,1)S(1)} async-done(((bf16[32,120,128]{2,1,0:T(8,128)(2,1)}), bf16[32,120,128]{2,1,0:T(8,128)(2,1)S(1)}, u32[]{:S(2)}, u32[]{:S(2)}) %all-to-all-start.1) | async-done | bytes 983072 | tf_op jit(solution)/shard_map/all_to_all | solution.py:451
  98.8 3.6 %all-to-all-start.2 = ((bf16[32,120,128]{2,1,0:T(8,128)(2,1)}), bf16[32,120,128]{2,1,0:T(8,128)(2,1)S(1)}, u32[]{:S(2)}, u32[]{:S(2)}) async-start(bf16[32,120,128]{2,1,0:T(8,128)(2,1)} %get-tuple-element.67), calls=%async_computation.2 | async-start | bytes 1966080 | tf_op jit(solution)/shard_map/all_to_all | solution.py:451
  102.4 3.6 %shard_map.115 = (bf16[144,128]{1,0:T(8,128)(2,1)S(1)}, bf16[144,128]{1,0:T(8,128)(2,1)S(1)}, bf16[144,128]{1,0:T(8,128)(2,1)S(1)}, bf16[144,128]{1,0:T(8,128)(2...) custom-call(s32[2]{0:T(128)S(1)} %copy-done.3, ...), custom_call_target="tpu_custom_call" | custom-call | flops 1132462080 | bytes 3932160 | tf_op jit(solution)/shard_map/pallas_call | solution.py:58
  106.1 1.8 %collective-permute-start.10 = (bf16[144,128]{1,0:T(8,128)(2,1)S(1)}, bf16[144,128]{1,0:T(8,128)(2,1)S(1)}, u32[]{:S(2)}, u32[]{:S(2)}) collective-permute-start(bf16[144,128]{1,0:T(8,128)(2,1)S(1)} %get-tuple-element.62), channel_id=1, source_target_pairs={{0,4},{1,5},{2,6},{3,7},{4,0},{5,1},{6,2},{7,3},{8,12},{9,13},{10,... | collective-permute-start | bytes 110600 | tf_op jit(solution)/shard_map/ppermute | solution.py:456
  107.9 0.0 collective-permute-start.11
  107.9 2.4 %collective-permute-start.12 = (bf16[144,128]{1,0:T(8,128)(2,1)S(1)}, bf16[144,128]{1,0:T(8,128)(2,1)S(1)}, u32[]{:S(2)}, u32[]{:S(2)}) collective-permute-start(bf16[144,128]{1,0:T(8,128)(2,1)S(1)} %get-tuple-element.64), channel_id=1, source_target_pairs={{0,6},{1,7},{2,4},{3,5},{4,2},{5,3},{6,0},{7,1},{8,14},{9,15},{10,... | collective-permute-start | bytes 110600 | tf_op jit(solution)/shard_map/ppermute | solution.py:456
  110.3 0.3 collective-permute-start.13
  110.6 0.4 collective-permute-start.7
  111.0 0.1 collective-permute-done.10.refs_4_
  111.1 2.1 %collective-permute-start.8 = (bf16[144,128]{1,0:T(8,128)(2,1)S(1)}, bf16[144,128]{1,0:T(8,128)(2,1)S(1)}, u32[]{:S(2)}, u32[]{:S(2)}) collective-permute-start(bf16[144,128]{1,0:T(8,128)(2,1)S(1)} %get-tuple-element.60), channel_id=1, source_target_pairs={{0,2},{1,3},{2,0},{3,1},{4,6},{5,7},{6,4},{7,5},{8,10},{9,11},{10,... | collective-permute-start | bytes 110600 | tf_op jit(solution)/shard_map/ppermute | solution.py:456
  113.2 1.9 %collective-permute-done.11.refs_5_ = bf16[144,128]{1,0:T(8,128)(2,1)S(1)} collective-permute-done((bf16[144,128]{1,0:T(8,128)(2,1)S(1)}, bf16[144,128]{1,0:T(8,128)(2,1)S(1)}, u32[]{:S(2)}, u32[]{:S(2)}) %collective-permute-start.11) | collective-permute-done | bytes 36896 | tf_op jit(solution)/shard_map/ppermute | solution.py:456
  115.1 2.1 %collective-permute-start.9 = (bf16[144,128]{1,0:T(8,128)(2,1)S(1)}, bf16[144,128]{1,0:T(8,128)(2,1)S(1)}, u32[]{:S(2)}, u32[]{:S(2)}) collective-permute-start(bf16[144,128]{1,0:T(8,128)(2,1)S(1)} %get-tuple-element.61), channel_id=1, source_target_pairs={{0,3},{1,2},{2,1},{3,0},{4,7},{5,6},{6,5},{7,4},{8,11},{9,10},{10,... | collective-permute-start | bytes 110600 | tf_op jit(solution)/shard_map/ppermute | solution.py:456
  117.2 0.0 collective-permute-done.12.refs_6_
  117.2 0.0 collective-permute-done.13.refs_7_
  117.2 0.0 collective-permute-done.7.refs_1_
  117.2 1.9 %collective-permute-done.9.refs_3_ = bf16[144,128]{1,0:T(8,128)(2,1)S(1)} collective-permute-done((bf16[144,128]{1,0:T(8,128)(2,1)S(1)}, bf16[144,128]{1,0:T(8,128)(2,1)S(1)}, u32[]{:S(2)}, u32[]{:S(2)}) %collective-permute-start.9) | collective-permute-done | bytes 36896 | tf_op jit(solution)/shard_map/ppermute | solution.py:456
  119.1 0.6 collective-permute-start.14
  119.7 4.7 %collective-permute-start.15 = (bf16[336,128]{1,0:T(8,128)(2,1)S(1)}, bf16[336,128]{1,0:T(8,128)(2,1)S(1)}, u32[]{:S(2)}, u32[]{:S(2)}) collective-permute-start(bf16[336,128]{1,0:T(8,128)(2,1)S(1)} %shard_map.116.refs_0_), channel_id=1, source_target_pairs={{0,16},{8,24},{16,0},{24,8},{1,17},{9,25},{17,1},{25,9},{2,18},{10... | collective-permute-start | bytes 258056 | tf_op jit(solution)/shard_map/ppermute | solution.py:461
  124.5 1.7 %collective-permute-start.16 = (bf16[336,128]{1,0:T(8,128)(2,1)S(1)}, bf16[336,128]{1,0:T(8,128)(2,1)S(1)}, u32[]{:S(2)}, u32[]{:S(2)}) collective-permute-start(bf16[336,128]{1,0:T(8,128)(2,1)S(1)} %shard_map.116.refs_0_), channel_id=1, source_target_pairs={{0,24},{8,0},{16,8},{24,16},{1,25},{9,1},{17,9},{25,17},{2,26},{10... | collective-permute-start | bytes 258056 | tf_op jit(solution)/shard_map/ppermute | solution.py:461
  126.1 4.3 %shard_map.117 = bf16[32,120,128]{2,1,0:T(8,128)(2,1)} custom-call(bf16[9,128,128]{2,1,0:T(8,128)(2,1)S(1)} %copy-done.1, bf16[32,120,128]{2,1,0:T(8,128)(2,1)S(1)} %all-to-all-done.1.got_ref, bf16[28,32,120,128]{3,2,1,0:T(8,128)(2,1)} %shard_map.111.slope_hbm), custom_call_target="tpu_custom_call" | custom-call | flops 1132462080 | bytes 2949120 | tf_op jit(solution)/shard_map/pallas_call | solution.py:58
  130.5 2.8 %collective-permute-done.15.refs_2_ = bf16[336,128]{1,0:T(8,128)(2,1)S(1)} collective-permute-done((bf16[336,128]{1,0:T(8,128)(2,1)S(1)}, bf16[336,128]{1,0:T(8,128)(2,1)S(1)}, u32[]{:S(2)}, u32[]{:S(2)}) %collective-permute-start.15) | collective-permute-done | bytes 86048 | tf_op jit(solution)/shard_map/ppermute | solution.py:461
  133.3 10.2 %all-gather = bf16[2688,128]{1,0:T(8,128)(2,1)S(1)} all-gather(bf16[336,128]{1,0:T(8,128)(2,1)S(1)} %shard_map.118), channel_id=2, replica_groups=mesh['seg'=4,'grp'=8] {'grp'}, dimensions={0}, use_global_device_ids=true | all-gather | bytes 774144 | tf_op jit(solution)/shard_map/all_gather | solution.py:648
  143.5 1.4 shard_map.119
  (20 shorter events, 0.1 us)
Async XLA Ops:
  0.6 58.2 %copy-start.7 = (bf16[2,128,128]{2,1,0:T(8,128)(2,1)S(1)}, bf16[2,128,128]{2,1,0:T(8,128)(2,1)}, u32[]{:S(2)}) copy-start(bf16[2,128,128]{2,1,0:T(8,128)(2,1)} %uw_hbm.1) | copy-start | bytes 196612
  0.6 58.2 %copy-start.5 = (s32[4]{0:T(128)S(1)}, s32[4]{0:T(128)}, u32[]{:S(2)}) copy-start(s32[4]{0:T(128)} %key_ref.3) | copy-start | bytes 52
  0.7 58.2 %copy-start.4 = (s32[2]{0:T(128)S(1)}, s32[2]{0:T(128)}, u32[]{:S(2)}) copy-start(s32[2]{0:T(128)} %dil_ref.3) | copy-start | bytes 28
  0.7 58.2 %copy-start.6 = (bf16[2,5,128,128]{3,2,1,0:T(8,128)(2,1)S(1)}, bf16[2,5,128,128]{3,2,1,0:T(8,128)(2,1)}, u32[]{:S(2)}) copy-start(bf16[2,5,128,128]{3,2,1,0:T(8,128)(2,1)} %tw_hbm.1) | copy-start | bytes 983044
  5.5 53.4 %all-to-all-start = ((bf16[32,2,120,128]{3,2,1,0:T(8,128)(2,1)}), bf16[32,2,120,128]{3,2,1,0:T(8,128)(2,1)S(1)}, u32[]{:S(2)}, u32[]{:S(2)}) async-start(bf16[32,2,120,128]{3,2,1,0:T(8,128)(2,1)} %shard_map.110), calls=%async_computation | async-start | bytes 3932160 | tf_op jit(solution)/shard_map/all_to_all | solution.py:451
  70.0 28.8 %all-to-all-start.1 = ((bf16[32,120,128]{2,1,0:T(8,128)(2,1)}), bf16[32,120,128]{2,1,0:T(8,128)(2,1)S(1)}, u32[]{:S(2)}, u32[]{:S(2)}) async-start(bf16[32,120,128]{2,1,0:T(8,128)(2,1)} %get-tuple-element.52), calls=%async_computation.1 | async-start | bytes 1966080 | tf_op jit(solution)/shard_map/all_to_all | solution.py:451
  74.8 27.6 %copy-start = (bf16[1,32,120,128]{3,2,1,0:T(8,128)(2,1)S(1)}, bf16[1,32,120,128]{3,2,1,0:T(8,128)(2,1)}, u32[]{:S(2)}) copy-start(bf16[1,32,120,128]{3,2,1,0:T(8,128)(2,1)} %param.7) | copy-start | bytes 2949124
  74.8 27.6 %copy-start.3 = (s32[2]{0:T(128)S(1)}, s32[2]{0:T(128)}, u32[]{:S(2)}) copy-start(s32[2]{0:T(128)} %pad_add_fusion.here_ref) | copy-start | bytes 28
  84.6 41.5 %copy-start.1 = (bf16[9,128,128]{2,1,0:T(8,128)(2,1)S(1)}, bf16[9,128,128]{2,1,0:T(8,128)(2,1)}, u32[]{:S(2)}) copy-start(bf16[9,128,128]{2,1,0:T(8,128)(2,1)} %w_ref.3) | copy-start | bytes 884740
  84.6 3.6 %collective-permute-start = (bf16[192,128]{1,0:T(8,128)(2,1)}, bf16[192,128]{1,0:T(8,128)(2,1)S(1)}, u32[]{:S(2)}, u32[]{:S(2)}) collective-permute-start(bf16[192,128]{1,0:T(8,128)(2,1)} %get-tuple-element.45), channel_id=1, source_target_pairs={{0,1},{1,0},{2,3},{3,2},{4,5},{5,4},{6,7},{7,6},{8,9},{9,8},{10,11... | collective-permute-start | bytes 147464 | tf_op jit(solution)/shard_map/ppermute | solution.py:456
  84.7 6.1 %collective-permute-start.1 = (bf16[192,128]{1,0:T(8,128)(2,1)}, bf16[192,128]{1,0:T(8,128)(2,1)S(1)}, u32[]{:S(2)}, u32[]{:S(2)}) collective-permute-start(bf16[192,128]{1,0:T(8,128)(2,1)} %get-tuple-element.46), channel_id=1, source_target_pairs={{0,2},{1,3},{2,0},{3,1},{4,6},{5,7},{6,4},{7,5},{8,10},{9,11},{10,... | collective-permute-start | bytes 147464 | tf_op jit(solution)/shard_map/ppermute | solution.py:456
  86.4 4.8 %collective-permute-start.2 = (bf16[192,128]{1,0:T(8,128)(2,1)}, bf16[192,128]{1,0:T(8,128)(2,1)S(1)}, u32[]{:S(2)}, u32[]{:S(2)}) collective-permute-start(bf16[192,128]{1,0:T(8,128)(2,1)} %get-tuple-element.47), channel_id=1, source_target_pairs={{0,3},{1,2},{2,1},{3,0},{4,7},{5,6},{6,5},{7,4},{8,11},{9,10},{10,... | collective-permute-start | bytes 147464 | tf_op jit(solution)/shard_map/ppermute | solution.py:456
  86.6 4.7 %collective-permute-start.3 = (bf16[192,128]{1,0:T(8,128)(2,1)}, bf16[192,128]{1,0:T(8,128)(2,1)S(1)}, u32[]{:S(2)}, u32[]{:S(2)}) collective-permute-start(bf16[192,128]{1,0:T(8,128)(2,1)} %get-tuple-element.48), channel_id=1, source_target_pairs={{0,4},{1,5},{2,6},{3,7},{4,0},{5,1},{6,2},{7,3},{8,12},{9,13},{10,... | collective-permute-start | bytes 147464 | tf_op jit(solution)/shard_map/ppermute | solution.py:456
  88.1 5.5 %collective-permute-start.4 = (bf16[192,128]{1,0:T(8,128)(2,1)}, bf16[192,128]{1,0:T(8,128)(2,1)S(1)}, u32[]{:S(2)}, u32[]{:S(2)}) collective-permute-start(bf16[192,128]{1,0:T(8,128)(2,1)} %get-tuple-element.49), channel_id=1, source_target_pairs={{0,5},{1,4},{2,7},{3,6},{4,1},{5,0},{6,3},{7,2},{8,13},{9,12},{10,... | collective-permute-start | bytes 147464 | tf_op jit(solution)/shard_map/ppermute | solution.py:456
  88.3 5.3 %collective-permute-start.5 = (bf16[192,128]{1,0:T(8,128)(2,1)}, bf16[192,128]{1,0:T(8,128)(2,1)S(1)}, u32[]{:S(2)}, u32[]{:S(2)}) collective-permute-start(bf16[192,128]{1,0:T(8,128)(2,1)} %get-tuple-element.50), channel_id=1, source_target_pairs={{0,6},{1,7},{2,4},{3,5},{4,2},{5,3},{6,0},{7,1},{8,14},{9,15},{10,... | collective-permute-start | bytes 147464 | tf_op jit(solution)/shard_map/ppermute | solution.py:456
  90.8 5.3 %collective-permute-start.6 = (bf16[192,128]{1,0:T(8,128)(2,1)}, bf16[192,128]{1,0:T(8,128)(2,1)S(1)}, u32[]{:S(2)}, u32[]{:S(2)}) collective-permute-start(bf16[192,128]{1,0:T(8,128)(2,1)} %get-tuple-element.51), channel_id=1, source_target_pairs={{0,7},{1,6},{2,5},{3,4},{4,3},{5,2},{6,1},{7,0},{8,15},{9,14},{10,... | collective-permute-start | bytes 147464 | tf_op jit(solution)/shard_map/ppermute | solution.py:456
  96.1 0.8 copy-start.2
  98.8 44.8 %all-to-all-start.2 = ((bf16[32,120,128]{2,1,0:T(8,128)(2,1)}), bf16[32,120,128]{2,1,0:T(8,128)(2,1)S(1)}, u32[]{:S(2)}, u32[]{:S(2)}) async-start(bf16[32,120,128]{2,1,0:T(8,128)(2,1)} %get-tuple-element.67), calls=%async_computation.2 | async-start | bytes 1966080 | tf_op jit(solution)/shard_map/all_to_all | solution.py:451
  106.1 5.0 %collective-permute-start.10 = (bf16[144,128]{1,0:T(8,128)(2,1)S(1)}, bf16[144,128]{1,0:T(8,128)(2,1)S(1)}, u32[]{:S(2)}, u32[]{:S(2)}) collective-permute-start(bf16[144,128]{1,0:T(8,128)(2,1)S(1)} %get-tuple-element.62), channel_id=1, source_target_pairs={{0,4},{1,5},{2,6},{3,7},{4,0},{5,1},{6,2},{7,3},{8,12},{9,13},{10,... | collective-permute-start | bytes 110600 | tf_op jit(solution)/shard_map/ppermute | solution.py:456
  107.9 7.2 %collective-permute-start.11 = (bf16[144,128]{1,0:T(8,128)(2,1)S(1)}, bf16[144,128]{1,0:T(8,128)(2,1)S(1)}, u32[]{:S(2)}, u32[]{:S(2)}) collective-permute-start(bf16[144,128]{1,0:T(8,128)(2,1)S(1)} %get-tuple-element.63), channel_id=1, source_target_pairs={{0,5},{1,4},{2,7},{3,6},{4,1},{5,0},{6,3},{7,2},{8,13},{9,12},{10,... | collective-permute-start | bytes 110600 | tf_op jit(solution)/shard_map/ppermute | solution.py:456
  107.9 9.3 %collective-permute-start.12 = (bf16[144,128]{1,0:T(8,128)(2,1)S(1)}, bf16[144,128]{1,0:T(8,128)(2,1)S(1)}, u32[]{:S(2)}, u32[]{:S(2)}) collective-permute-start(bf16[144,128]{1,0:T(8,128)(2,1)S(1)} %get-tuple-element.64), channel_id=1, source_target_pairs={{0,6},{1,7},{2,4},{3,5},{4,2},{5,3},{6,0},{7,1},{8,14},{9,15},{10,... | collective-permute-start | bytes 110600 | tf_op jit(solution)/shard_map/ppermute | solution.py:456
  110.3 6.9 %collective-permute-start.13 = (bf16[144,128]{1,0:T(8,128)(2,1)S(1)}, bf16[144,128]{1,0:T(8,128)(2,1)S(1)}, u32[]{:S(2)}, u32[]{:S(2)}) collective-permute-start(bf16[144,128]{1,0:T(8,128)(2,1)S(1)} %get-tuple-element.65), channel_id=1, source_target_pairs={{0,7},{1,6},{2,5},{3,4},{4,3},{5,2},{6,1},{7,0},{8,15},{9,14},{10,... | collective-permute-start | bytes 110600 | tf_op jit(solution)/shard_map/ppermute | solution.py:456
  110.6 6.6 %collective-permute-start.7 = (bf16[144,128]{1,0:T(8,128)(2,1)S(1)}, bf16[144,128]{1,0:T(8,128)(2,1)S(1)}, u32[]{:S(2)}, u32[]{:S(2)}) collective-permute-start(bf16[144,128]{1,0:T(8,128)(2,1)S(1)} %get-tuple-element.59), channel_id=1, source_target_pairs={{0,1},{1,0},{2,3},{3,2},{4,5},{5,4},{6,7},{7,6},{8,9},{9,8},{10,11... | collective-permute-start | bytes 110600 | tf_op jit(solution)/shard_map/ppermute | solution.py:456
  111.1 6.1 %collective-permute-start.8 = (bf16[144,128]{1,0:T(8,128)(2,1)S(1)}, bf16[144,128]{1,0:T(8,128)(2,1)S(1)}, u32[]{:S(2)}, u32[]{:S(2)}) collective-permute-start(bf16[144,128]{1,0:T(8,128)(2,1)S(1)} %get-tuple-element.60), channel_id=1, source_target_pairs={{0,2},{1,3},{2,0},{3,1},{4,6},{5,7},{6,4},{7,5},{8,10},{9,11},{10,... | collective-permute-start | bytes 110600 | tf_op jit(solution)/shard_map/ppermute | solution.py:456
  115.1 4.0 %collective-permute-start.9 = (bf16[144,128]{1,0:T(8,128)(2,1)S(1)}, bf16[144,128]{1,0:T(8,128)(2,1)S(1)}, u32[]{:S(2)}, u32[]{:S(2)}) collective-permute-start(bf16[144,128]{1,0:T(8,128)(2,1)S(1)} %get-tuple-element.61), channel_id=1, source_target_pairs={{0,3},{1,2},{2,1},{3,0},{4,7},{5,6},{6,5},{7,4},{8,11},{9,10},{10,... | collective-permute-start | bytes 110600 | tf_op jit(solution)/shard_map/ppermute | solution.py:456
  119.1 11.3 %collective-permute-start.14 = (bf16[336,128]{1,0:T(8,128)(2,1)S(1)}, bf16[336,128]{1,0:T(8,128)(2,1)S(1)}, u32[]{:S(2)}, u32[]{:S(2)}) collective-permute-start(bf16[336,128]{1,0:T(8,128)(2,1)S(1)} %shard_map.116.refs_0_), channel_id=1, source_target_pairs={{0,8},{8,16},{16,24},{24,0},{1,9},{9,17},{17,25},{25,1},{2,10},{10... | collective-permute-start | bytes 258056 | tf_op jit(solution)/shard_map/ppermute | solution.py:461
  119.7 13.5 %collective-permute-start.15 = (bf16[336,128]{1,0:T(8,128)(2,1)S(1)}, bf16[336,128]{1,0:T(8,128)(2,1)S(1)}, u32[]{:S(2)}, u32[]{:S(2)}) collective-permute-start(bf16[336,128]{1,0:T(8,128)(2,1)S(1)} %shard_map.116.refs_0_), channel_id=1, source_target_pairs={{0,16},{8,24},{16,0},{24,8},{1,17},{9,25},{17,1},{25,9},{2,18},{10... | collective-permute-start | bytes 258056 | tf_op jit(solution)/shard_map/ppermute | solution.py:461
  124.5 8.8 %collective-permute-start.16 = (bf16[336,128]{1,0:T(8,128)(2,1)S(1)}, bf16[336,128]{1,0:T(8,128)(2,1)S(1)}, u32[]{:S(2)}, u32[]{:S(2)}) collective-permute-start(bf16[336,128]{1,0:T(8,128)(2,1)S(1)} %shard_map.116.refs_0_), channel_id=1, source_target_pairs={{0,24},{8,0},{16,8},{24,16},{1,25},{9,1},{17,9},{25,17},{2,26},{10... | collective-permute-start | bytes 258056 | tf_op jit(solution)/shard_map/ppermute | solution.py:461

commit v16 on v15

--- a/solution.py
+++ b/solution.py
@@ -119,7 +119,7 @@
     ]
     w_load = pltpu.make_async_copy(w_hbm, w_ref, w_sem.at[0])
     cot_load = pltpu.make_async_copy(cot_hbm, sends.at[:, 1], cot_sem.at[0])
-    for load in [loads[0], w_load] + loads[1:] + [cot_load]:
+    for load in [loads[0], w_load] + loads[1:2]:
         load.start()
     clear_ends(xs)
 
@@ -128,6 +128,8 @@
         put_rows(xs, n * many, x_in[n * many : (n + 1) * many])
 
     bring(0)
+    for load in loads[2:] + [cot_load]:
+        load.start()
     w_load.wait()
     weight = forward_weight(w_ref)
     for n in range(parts):
@@ -380,7 +382,7 @@
             )
         )
     ]
-    for copy in copies:
+    for copy in copies[:2]:
         copy.start()
     clear_halo(a0, frames)
     clear_halo(a1, frames)
@@ -388,6 +390,8 @@
     for layer, acts, grads in ((0, a0, g0), (1, a1, g1)):
         copies[2 * layer].wait()
         copies[2 * layer + 1].wait()
+        for copy in copies[4:] if layer else copies[2:4]:
+            copy.start()
         total = jnp.zeros((TAPS * ch, ch), F32)
         for at in range(0, frames, step_frames):
             total = total + mm_tn(

time: 146 us -> 148 us (1.014)
  Pallas kernels: 39.6 us -> 42.5 us
    pallas_call x10, Pallas kernels: 39.6 us -> 42.5 us  [call(): pl.pallas_call(kernel, out_shape=[jax.ShapeDtypeStruct(shape, kind) for s...]
    all_to_all x3, waiting for transfers between devices: 43.3 us -> 41.5 us  [exchange(): return lax.all_to_all(blocks, AXES, split_axis=0, concat_axis=0, tiled=True)]
    ppermute x3, waiting for transfers between devices: 2.76 us -> 4.31 us  [turn_by(): lax.ppermute(value, 'seg', [(i, (i + turn) % size) for i in range(size)])]
    ppermute x3, starting transfers between devices: 6.96 us -> 5.42 us  [turn_by(): lax.ppermute(value, 'seg', [(i, (i + turn) % size) for i in range(size)])]
  transfers between devices with their start and end apart: 20 -> 20, of which waited for: 9 -> 8; matrix products, arithmetic and copies ran while one was open for 0% -> 0% of each run, Pallas kernels for 15% -> 17%
where the time goes in v16:
time: 148 us; the launch traced here: 147 us
  waiting for transfers between devices  55 us (37%)
  Pallas kernels  42.5 us (29%)
  starting transfers between devices  37 us (25%)
  blocking collectives  10.2 us (7%)
    pallas_call x10, Pallas kernels, call(): pl.pallas_call(kernel, out_shape=[jax.ShapeDtypeStruct(shape, kind) for s...  42.5 us
    all_to_all x3, waiting for transfers between devices, exchange(): return lax.all_to_all(blocks, AXES, split_axis=0, concat_axis=0, tiled=True)  41.5 us
    all_to_all x3, starting transfers between devices, exchange(): return lax.all_to_all(blocks, AXES, split_axis=0, concat_axis=0, tiled=True)  16.1 us
    ppermute x14, starting transfers between devices, flip(): return lax.ppermute(value, 'grp', [(i, i ^ peer) for i in range(size)])  15.5 us
    all_gather x1, blocking collectives, local(): lax.all_gather(piece, 'grp', axis=0)  10.2 us
    ppermute x14, waiting for transfers between devices, flip(): return lax.ppermute(value, 'grp', [(i, i ^ peer) for i in range(size)])  9.23 us
    ppermute x3, starting transfers between devices, turn_by(): lax.ppermute(value, 'seg', [(i, (i + turn) % size) for i in range(size)])  5.42 us
    ppermute x3, waiting for transfers between devices, turn_by(): lax.ppermute(value, 'seg', [(i, (i + turn) % size) for i in range(size)])  4.31 us
  transfers between devices with their start and end apart: 20, of which 8 were waited for; matrix products, arithmetic and copies ran while one was open for 0% of the time, Pallas kernels for 17%

profile of v16, /device:TPU:0, one launch (start us, length us, event | category | flops | bytes accessed | tf_op | source)
XLA Modules:
  0.0 147.3 jit_solution(2236305337955349850)
XLA Ops:
  0.6 0.0 copy-start.5
  0.7 0.0 copy-start.4
  0.7 5.1 %shard_map.110 = bf16[32,2,120,128]{3,2,1,0:T(8,128)(2,1)} custom-call(bf16[32,120,128]{2,1,0:T(8,128)(2,1)} %bitcast.10, bf16[9,128,128]{2,1,0:T(8,128)(2,1)} %w_ref.3, bf16[32,120,128]{2,1,0:T(8,128)(2,1)} %bitcast.14), custom_call_target="tpu_custom_call" | custom-call | flops 1132462080 | bytes 3932160 | tf_op jit(solution)/shard_map/pallas_call | solution.py:58
  5.8 7.5 %all-to-all-start = ((bf16[32,2,120,128]{3,2,1,0:T(8,128)(2,1)}), bf16[32,2,120,128]{3,2,1,0:T(8,128)(2,1)S(1)}, u32[]{:S(2)}, u32[]{:S(2)}) async-start(bf16[32,2,120,128]{3,2,1,0:T(8,128)(2,1)} %shard_map.110), calls=%async_computation | async-start | bytes 3932160 | tf_op jit(solution)/shard_map/all_to_all | solution.py:455
  13.3 4.4 %shard_map.111.slope_hbm = bf16[28,32,120,128]{3,2,1,0:T(8,128)(2,1)} custom-call(bf16[32,120,128]{2,1,0:T(8,128)(2,1)} %bitcast.11, bf16[9,128,128]{2,1,0:T(8,128)(2,1)} %w_ref.3), custom_call_target="tpu_custom_call" | custom-call | flops 1132462080 | bytes 1966080 | tf_op jit(solution)/shard_map/pallas_call | solution.py:58
  17.7 41.5 %all-to-all-done.got_ref = bf16[32,2,120,128]{3,2,1,0:T(8,128)(2,1)S(1)} async-done(((bf16[32,2,120,128]{3,2,1,0:T(8,128)(2,1)}), bf16[32,2,120,128]{3,2,1,0:T(8,128)(2,1)S(1)}, u32[]{:S(2)}, u32[]{:S(2)}) %all-to-all-start) | async-done | bytes 1966112 | tf_op jit(solution)/shard_map/all_to_all | solution.py:455
  59.3 11.1 %shard_map.112 = (bf16[32,120,128]{2,1,0:T(8,128)(2,1)}, bf16[28,32,128,128]{3,2,1,0:T(8,128)(2,1)}, bf16[28,32,120,128]{3,2,1,0:T(8,128)(2,1)}) custom-call(s32[2]{0:T(128)S(1)} %copy-done.4, s32[4]{0:T(128)S(1)} %copy-done.5, bf16[32,2,120,128]{3,2,1,0:T(8,128)(2,1)S(1)} %all-to-all-done.got_ref, bf16[2,5,128,128]{3,2,1,0:T(8,128)(2,1)S(1)} %copy-done.6, ...), custom_call_target="tpu_custom_call" | custom-call | flops 2768240640 | bytes 8847360 | tf_op jit(solution)/shard_map/pallas_call | solution.py:58
  70.3 4.2 %all-to-all-start.1 = ((bf16[32,120,128]{2,1,0:T(8,128)(2,1)}), bf16[32,120,128]{2,1,0:T(8,128)(2,1)S(1)}, u32[]{:S(2)}, u32[]{:S(2)}) async-start(bf16[32,120,128]{2,1,0:T(8,128)(2,1)} %get-tuple-element.52), calls=%async_computation.1 | async-start | bytes 1966080 | tf_op jit(solution)/shard_map/all_to_all | solution.py:455
  74.5 0.7 pad_add_fusion.here_ref
  75.2 12.4 %shard_map.113 = (bf16[32,120,128]{2,1,0:T(8,128)(2,1)}, bf16[192,128]{1,0:T(8,128)(2,1)}, bf16[192,128]{1,0:T(8,128)(2,1)}, bf16[192,128]{1,0:T(8,128)(2,1)}, b...) custom-call(s32[2]{0:T(128)} %pad_add_fusion.here_ref, ...), custom_call_target="tpu_custom_call" | custom-call | flops 1509949440 | bytes 6881280 | tf_op jit(solution)/shard_map/pallas_call | solution.py:58
  87.5 0.0 copy-start.1
  87.6 0.1 collective-permute-start
  87.7 1.7 %collective-permute-start.1 = (bf16[192,128]{1,0:T(8,128)(2,1)}, bf16[192,128]{1,0:T(8,128)(2,1)S(1)}, u32[]{:S(2)}, u32[]{:S(2)}) collective-permute-start(bf16[192,128]{1,0:T(8,128)(2,1)} %get-tuple-element.46), channel_id=1, source_target_pairs={{0,2},{1,3},{2,0},{3,1},{4,6},{5,7},{6,4},{7,5},{8,10},{9,11},{10,... | collective-permute-start | bytes 147464 | tf_op jit(solution)/shard_map/ppermute | solution.py:460
  89.3 0.2 collective-permute-start.2
  89.5 1.5 %collective-permute-start.3 = (bf16[192,128]{1,0:T(8,128)(2,1)}, bf16[192,128]{1,0:T(8,128)(2,1)S(1)}, u32[]{:S(2)}, u32[]{:S(2)}) collective-permute-start(bf16[192,128]{1,0:T(8,128)(2,1)} %get-tuple-element.48), channel_id=1, source_target_pairs={{0,4},{1,5},{2,6},{3,7},{4,0},{5,1},{6,2},{7,3},{8,12},{9,13},{10,... | collective-permute-start | bytes 147464 | tf_op jit(solution)/shard_map/ppermute | solution.py:460
  91.0 0.2 collective-permute-start.4
  91.2 0.0 collective-permute-done.refs_1_
  91.2 2.5 %collective-permute-start.5 = (bf16[192,128]{1,0:T(8,128)(2,1)}, bf16[192,128]{1,0:T(8,128)(2,1)S(1)}, u32[]{:S(2)}, u32[]{:S(2)}) collective-permute-start(bf16[192,128]{1,0:T(8,128)(2,1)} %get-tuple-element.50), channel_id=1, source_target_pairs={{0,6},{1,7},{2,4},{3,5},{4,2},{5,3},{6,0},{7,1},{8,14},{9,15},{10,... | collective-permute-start | bytes 147464 | tf_op jit(solution)/shard_map/ppermute | solution.py:460
  93.7 0.0 collective-permute-done.1.refs_2_
  93.7 0.2 collective-permute-start.6
  93.9 0.0 collective-permute-done.2.refs_3_
  93.9 1.4 collective-permute-done.4.refs_5_
  95.3 2.1 %collective-permute-done.5.refs_6_ = bf16[192,128]{1,0:T(8,128)(2,1)S(1)} collective-permute-done((bf16[192,128]{1,0:T(8,128)(2,1)}, bf16[192,128]{1,0:T(8,128)(2,1)S(1)}, u32[]{:S(2)}, u32[]{:S(2)}) %collective-permute-start.5) | collective-permute-done | bytes 49184 | tf_op jit(solution)/shard_map/ppermute | solution.py:460
  97.4 1.9 %collective-permute-done.6.refs_7_ = bf16[192,128]{1,0:T(8,128)(2,1)S(1)} collective-permute-done((bf16[192,128]{1,0:T(8,128)(2,1)}, bf16[192,128]{1,0:T(8,128)(2,1)S(1)}, u32[]{:S(2)}, u32[]{:S(2)}) %collective-permute-start.6) | collective-permute-done | bytes 49184 | tf_op jit(solution)/shard_map/ppermute | solution.py:460
  99.2 0.8 copy-done.2
  100.0 0.1 shard_map.114.first_ref
  100.1 0.0 all-to-all-done.1.got_ref
  100.1 4.4 %all-to-all-start.2 = ((bf16[32,120,128]{2,1,0:T(8,128)(2,1)}), bf16[32,120,128]{2,1,0:T(8,128)(2,1)S(1)}, u32[]{:S(2)}, u32[]{:S(2)}) async-start(bf16[32,120,128]{2,1,0:T(8,128)(2,1)} %get-tuple-element.67), calls=%async_computation.2 | async-start | bytes 1966080 | tf_op jit(solution)/shard_map/all_to_all | solution.py:455
  104.6 3.6 %shard_map.115 = (bf16[144,128]{1,0:T(8,128)(2,1)S(1)}, bf16[144,128]{1,0:T(8,128)(2,1)S(1)}, bf16[144,128]{1,0:T(8,128)(2,1)S(1)}, bf16[144,128]{1,0:T(8,128)(2...) custom-call(s32[2]{0:T(128)S(1)} %copy-done.3, ...), custom_call_target="tpu_custom_call" | custom-call | flops 1132462080 | bytes 3932160 | tf_op jit(solution)/shard_map/pallas_call | solution.py:58
  108.2 1.8 %collective-permute-start.10 = (bf16[144,128]{1,0:T(8,128)(2,1)S(1)}, bf16[144,128]{1,0:T(8,128)(2,1)S(1)}, u32[]{:S(2)}, u32[]{:S(2)}) collective-permute-start(bf16[144,128]{1,0:T(8,128)(2,1)S(1)} %get-tuple-element.62), channel_id=1, source_target_pairs={{0,4},{1,5},{2,6},{3,7},{4,0},{5,1},{6,2},{7,3},{8,12},{9,13},{10,... | collective-permute-start | bytes 110600 | tf_op jit(solution)/shard_map/ppermute | solution.py:460
  110.0 0.0 collective-permute-start.11
  110.0 2.4 %collective-permute-start.12 = (bf16[144,128]{1,0:T(8,128)(2,1)S(1)}, bf16[144,128]{1,0:T(8,128)(2,1)S(1)}, u32[]{:S(2)}, u32[]{:S(2)}) collective-permute-start(bf16[144,128]{1,0:T(8,128)(2,1)S(1)} %get-tuple-element.64), channel_id=1, source_target_pairs={{0,6},{1,7},{2,4},{3,5},{4,2},{5,3},{6,0},{7,1},{8,14},{9,15},{10,... | collective-permute-start | bytes 110600 | tf_op jit(solution)/shard_map/ppermute | solution.py:460
  112.4 0.3 collective-permute-start.13
  112.7 0.4 collective-permute-start.7
  113.1 0.1 collective-permute-done.10.refs_4_
  113.2 2.1 %collective-permute-start.8 = (bf16[144,128]{1,0:T(8,128)(2,1)S(1)}, bf16[144,128]{1,0:T(8,128)(2,1)S(1)}, u32[]{:S(2)}, u32[]{:S(2)}) collective-permute-start(bf16[144,128]{1,0:T(8,128)(2,1)S(1)} %get-tuple-element.60), channel_id=1, source_target_pairs={{0,2},{1,3},{2,0},{3,1},{4,6},{5,7},{6,4},{7,5},{8,10},{9,11},{10,... | collective-permute-start | bytes 110600 | tf_op jit(solution)/shard_map/ppermute | solution.py:460
  115.3 1.9 %collective-permute-done.11.refs_5_ = bf16[144,128]{1,0:T(8,128)(2,1)S(1)} collective-permute-done((bf16[144,128]{1,0:T(8,128)(2,1)S(1)}, bf16[144,128]{1,0:T(8,128)(2,1)S(1)}, u32[]{:S(2)}, u32[]{:S(2)}) %collective-permute-start.11) | collective-permute-done | bytes 36896 | tf_op jit(solution)/shard_map/ppermute | solution.py:460
  117.2 2.1 %collective-permute-start.9 = (bf16[144,128]{1,0:T(8,128)(2,1)S(1)}, bf16[144,128]{1,0:T(8,128)(2,1)S(1)}, u32[]{:S(2)}, u32[]{:S(2)}) collective-permute-start(bf16[144,128]{1,0:T(8,128)(2,1)S(1)} %get-tuple-element.61), channel_id=1, source_target_pairs={{0,3},{1,2},{2,1},{3,0},{4,7},{5,6},{6,5},{7,4},{8,11},{9,10},{10,... | collective-permute-start | bytes 110600 | tf_op jit(solution)/shard_map/ppermute | solution.py:460
  119.3 0.0 collective-permute-done.8.refs_2_
  119.3 1.9 %collective-permute-done.9.refs_3_ = bf16[144,128]{1,0:T(8,128)(2,1)S(1)} collective-permute-done((bf16[144,128]{1,0:T(8,128)(2,1)S(1)}, bf16[144,128]{1,0:T(8,128)(2,1)S(1)}, u32[]{:S(2)}, u32[]{:S(2)}) %collective-permute-start.9) | collective-permute-done | bytes 36896 | tf_op jit(solution)/shard_map/ppermute | solution.py:460
  121.3 0.6 collective-permute-start.14
  121.8 4.7 %collective-permute-start.15 = (bf16[336,128]{1,0:T(8,128)(2,1)S(1)}, bf16[336,128]{1,0:T(8,128)(2,1)S(1)}, u32[]{:S(2)}, u32[]{:S(2)}) collective-permute-start(bf16[336,128]{1,0:T(8,128)(2,1)S(1)} %shard_map.116.refs_0_), channel_id=1, source_target_pairs={{0,16},{8,24},{16,0},{24,8},{1,17},{9,25},{17,1},{25,9},{2,18},{10... | collective-permute-start | bytes 258056 | tf_op jit(solution)/shard_map/ppermute | solution.py:465
  126.6 0.1 collective-permute-start.16
  126.7 4.3 %shard_map.117 = bf16[32,120,128]{2,1,0:T(8,128)(2,1)} custom-call(bf16[9,128,128]{2,1,0:T(8,128)(2,1)S(1)} %copy-done.1, bf16[32,120,128]{2,1,0:T(8,128)(2,1)S(1)} %all-to-all-done.1.got_ref, bf16[28,32,120,128]{3,2,1,0:T(8,128)(2,1)} %shard_map.111.slope_hbm), custom_call_target="tpu_custom_call" | custom-call | flops 1132462080 | bytes 2949120 | tf_op jit(solution)/shard_map/pallas_call | solution.py:58
  131.0 0.0 collective-permute-done.14.refs_1_
  131.1 4.3 %collective-permute-done.15.refs_2_ = bf16[336,128]{1,0:T(8,128)(2,1)S(1)} collective-permute-done((bf16[336,128]{1,0:T(8,128)(2,1)S(1)}, bf16[336,128]{1,0:T(8,128)(2,1)S(1)}, u32[]{:S(2)}, u32[]{:S(2)}) %collective-permute-start.15) | collective-permute-done | bytes 86048 | tf_op jit(solution)/shard_map/ppermute | solution.py:465
  135.4 10.2 %all-gather = bf16[2688,128]{1,0:T(8,128)(2,1)S(1)} all-gather(bf16[336,128]{1,0:T(8,128)(2,1)S(1)} %shard_map.118), channel_id=2, replica_groups=mesh['seg'=4,'grp'=8] {'grp'}, dimensions={0}, use_global_device_ids=true | all-gather | bytes 774144 | tf_op jit(solution)/shard_map/all_gather | solution.py:652
  145.7 1.4 shard_map.119
  (20 shorter events, 0.1 us)
Async XLA Ops:
  0.6 58.6 %copy-start.7 = (bf16[2,128,128]{2,1,0:T(8,128)(2,1)S(1)}, bf16[2,128,128]{2,1,0:T(8,128)(2,1)}, u32[]{:S(2)}) copy-start(bf16[2,128,128]{2,1,0:T(8,128)(2,1)} %uw_hbm.1) | copy-start | bytes 196612
  0.6 58.6 %copy-start.5 = (s32[4]{0:T(128)S(1)}, s32[4]{0:T(128)}, u32[]{:S(2)}) copy-start(s32[4]{0:T(128)} %key_ref.3) | copy-start | bytes 52
  0.7 58.6 %copy-start.4 = (s32[2]{0:T(128)S(1)}, s32[2]{0:T(128)}, u32[]{:S(2)}) copy-start(s32[2]{0:T(128)} %dil_ref.3) | copy-start | bytes 28
  0.7 58.6 %copy-start.6 = (bf16[2,5,128,128]{3,2,1,0:T(8,128)(2,1)S(1)}, bf16[2,5,128,128]{3,2,1,0:T(8,128)(2,1)}, u32[]{:S(2)}) copy-start(bf16[2,5,128,128]{3,2,1,0:T(8,128)(2,1)} %tw_hbm.1) | copy-start | bytes 983044
  5.8 53.4 %all-to-all-start = ((bf16[32,2,120,128]{3,2,1,0:T(8,128)(2,1)}), bf16[32,2,120,128]{3,2,1,0:T(8,128)(2,1)S(1)}, u32[]{:S(2)}, u32[]{:S(2)}) async-start(bf16[32,2,120,128]{3,2,1,0:T(8,128)(2,1)} %shard_map.110), calls=%async_computation | async-start | bytes 3932160 | tf_op jit(solution)/shard_map/all_to_all | solution.py:455
  70.3 29.8 %all-to-all-start.1 = ((bf16[32,120,128]{2,1,0:T(8,128)(2,1)}), bf16[32,120,128]{2,1,0:T(8,128)(2,1)S(1)}, u32[]{:S(2)}, u32[]{:S(2)}) async-start(bf16[32,120,128]{2,1,0:T(8,128)(2,1)} %get-tuple-element.52), calls=%async_computation.1 | async-start | bytes 1966080 | tf_op jit(solution)/shard_map/all_to_all | solution.py:455
  75.2 29.4 %copy-start = (bf16[1,32,120,128]{3,2,1,0:T(8,128)(2,1)S(1)}, bf16[1,32,120,128]{3,2,1,0:T(8,128)(2,1)}, u32[]{:S(2)}) copy-start(bf16[1,32,120,128]{3,2,1,0:T(8,128)(2,1)} %param.7) | copy-start | bytes 2949124
  75.2 29.4 %copy-start.3 = (s32[2]{0:T(128)S(1)}, s32[2]{0:T(128)}, u32[]{:S(2)}) copy-start(s32[2]{0:T(128)} %pad_add_fusion.here_ref) | copy-start | bytes 28
  87.5 39.2 %copy-start.1 = (bf16[9,128,128]{2,1,0:T(8,128)(2,1)S(1)}, bf16[9,128,128]{2,1,0:T(8,128)(2,1)}, u32[]{:S(2)}) copy-start(bf16[9,128,128]{2,1,0:T(8,128)(2,1)} %w_ref.3) | copy-start | bytes 884740
  87.6 3.6 %collective-permute-start = (bf16[192,128]{1,0:T(8,128)(2,1)}, bf16[192,128]{1,0:T(8,128)(2,1)S(1)}, u32[]{:S(2)}, u32[]{:S(2)}) collective-permute-start(bf16[192,128]{1,0:T(8,128)(2,1)} %get-tuple-element.45), channel_id=1, source_target_pairs={{0,1},{1,0},{2,3},{3,2},{4,5},{5,4},{6,7},{7,6},{8,9},{9,8},{10,11... | collective-permute-start | bytes 147464 | tf_op jit(solution)/shard_map/ppermute | solution.py:460
  87.7 6.1 %collective-permute-start.1 = (bf16[192,128]{1,0:T(8,128)(2,1)}, bf16[192,128]{1,0:T(8,128)(2,1)S(1)}, u32[]{:S(2)}, u32[]{:S(2)}) collective-permute-start(bf16[192,128]{1,0:T(8,128)(2,1)} %get-tuple-element.46), channel_id=1, source_target_pairs={{0,2},{1,3},{2,0},{3,1},{4,6},{5,7},{6,4},{7,5},{8,10},{9,11},{10,... | collective-permute-start | bytes 147464 | tf_op jit(solution)/shard_map/ppermute | solution.py:460
  89.3 4.6 %collective-permute-start.2 = (bf16[192,128]{1,0:T(8,128)(2,1)}, bf16[192,128]{1,0:T(8,128)(2,1)S(1)}, u32[]{:S(2)}, u32[]{:S(2)}) collective-permute-start(bf16[192,128]{1,0:T(8,128)(2,1)} %get-tuple-element.47), channel_id=1, source_target_pairs={{0,3},{1,2},{2,1},{3,0},{4,7},{5,6},{6,5},{7,4},{8,11},{9,10},{10,... | collective-permute-start | bytes 147464 | tf_op jit(solution)/shard_map/ppermute | solution.py:460
  89.5 4.4 %collective-permute-start.3 = (bf16[192,128]{1,0:T(8,128)(2,1)}, bf16[192,128]{1,0:T(8,128)(2,1)S(1)}, u32[]{:S(2)}, u32[]{:S(2)}) collective-permute-start(bf16[192,128]{1,0:T(8,128)(2,1)} %get-tuple-element.48), channel_id=1, source_target_pairs={{0,4},{1,5},{2,6},{3,7},{4,0},{5,1},{6,2},{7,3},{8,12},{9,13},{10,... | collective-permute-start | bytes 147464 | tf_op jit(solution)/shard_map/ppermute | solution.py:460
  91.0 4.3 %collective-permute-start.4 = (bf16[192,128]{1,0:T(8,128)(2,1)}, bf16[192,128]{1,0:T(8,128)(2,1)S(1)}, u32[]{:S(2)}, u32[]{:S(2)}) collective-permute-start(bf16[192,128]{1,0:T(8,128)(2,1)} %get-tuple-element.49), channel_id=1, source_target_pairs={{0,5},{1,4},{2,7},{3,6},{4,1},{5,0},{6,3},{7,2},{8,13},{9,12},{10,... | collective-permute-start | bytes 147464 | tf_op jit(solution)/shard_map/ppermute | solution.py:460
  91.2 6.2 %collective-permute-start.5 = (bf16[192,128]{1,0:T(8,128)(2,1)}, bf16[192,128]{1,0:T(8,128)(2,1)S(1)}, u32[]{:S(2)}, u32[]{:S(2)}) collective-permute-start(bf16[192,128]{1,0:T(8,128)(2,1)} %get-tuple-element.50), channel_id=1, source_target_pairs={{0,6},{1,7},{2,4},{3,5},{4,2},{5,3},{6,0},{7,1},{8,14},{9,15},{10,... | collective-permute-start | bytes 147464 | tf_op jit(solution)/shard_map/ppermute | solution.py:460
  93.7 5.5 %collective-permute-start.6 = (bf16[192,128]{1,0:T(8,128)(2,1)}, bf16[192,128]{1,0:T(8,128)(2,1)S(1)}, u32[]{:S(2)}, u32[]{:S(2)}) collective-permute-start(bf16[192,128]{1,0:T(8,128)(2,1)} %get-tuple-element.51), channel_id=1, source_target_pairs={{0,7},{1,6},{2,5},{3,4},{4,3},{5,2},{6,1},{7,0},{8,15},{9,14},{10,... | collective-permute-start | bytes 147464 | tf_op jit(solution)/shard_map/ppermute | solution.py:460
  99.2 0.8 copy-start.2
  100.1 45.5 %all-to-all-start.2 = ((bf16[32,120,128]{2,1,0:T(8,128)(2,1)}), bf16[32,120,128]{2,1,0:T(8,128)(2,1)S(1)}, u32[]{:S(2)}, u32[]{:S(2)}) async-start(bf16[32,120,128]{2,1,0:T(8,128)(2,1)} %get-tuple-element.67), calls=%async_computation.2 | async-start | bytes 1966080 | tf_op jit(solution)/shard_map/all_to_all | solution.py:455
  108.2 5.0 %collective-permute-start.10 = (bf16[144,128]{1,0:T(8,128)(2,1)S(1)}, bf16[144,128]{1,0:T(8,128)(2,1)S(1)}, u32[]{:S(2)}, u32[]{:S(2)}) collective-permute-start(bf16[144,128]{1,0:T(8,128)(2,1)S(1)} %get-tuple-element.62), channel_id=1, source_target_pairs={{0,4},{1,5},{2,6},{3,7},{4,0},{5,1},{6,2},{7,3},{8,12},{9,13},{10,... | collective-permute-start | bytes 110600 | tf_op jit(solution)/shard_map/ppermute | solution.py:460
  110.0 7.2 %collective-permute-start.11 = (bf16[144,128]{1,0:T(8,128)(2,1)S(1)}, bf16[144,128]{1,0:T(8,128)(2,1)S(1)}, u32[]{:S(2)}, u32[]{:S(2)}) collective-permute-start(bf16[144,128]{1,0:T(8,128)(2,1)S(1)} %get-tuple-element.63), channel_id=1, source_target_pairs={{0,5},{1,4},{2,7},{3,6},{4,1},{5,0},{6,3},{7,2},{8,13},{9,12},{10,... | collective-permute-start | bytes 110600 | tf_op jit(solution)/shard_map/ppermute | solution.py:460
  110.0 9.3 %collective-permute-start.12 = (bf16[144,128]{1,0:T(8,128)(2,1)S(1)}, bf16[144,128]{1,0:T(8,128)(2,1)S(1)}, u32[]{:S(2)}, u32[]{:S(2)}) collective-permute-start(bf16[144,128]{1,0:T(8,128)(2,1)S(1)} %get-tuple-element.64), channel_id=1, source_target_pairs={{0,6},{1,7},{2,4},{3,5},{4,2},{5,3},{6,0},{7,1},{8,14},{9,15},{10,... | collective-permute-start | bytes 110600 | tf_op jit(solution)/shard_map/ppermute | solution.py:460
  112.4 6.9 %collective-permute-start.13 = (bf16[144,128]{1,0:T(8,128)(2,1)S(1)}, bf16[144,128]{1,0:T(8,128)(2,1)S(1)}, u32[]{:S(2)}, u32[]{:S(2)}) collective-permute-start(bf16[144,128]{1,0:T(8,128)(2,1)S(1)} %get-tuple-element.65), channel_id=1, source_target_pairs={{0,7},{1,6},{2,5},{3,4},{4,3},{5,2},{6,1},{7,0},{8,15},{9,14},{10,... | collective-permute-start | bytes 110600 | tf_op jit(solution)/shard_map/ppermute | solution.py:460
  112.7 6.6 %collective-permute-start.7 = (bf16[144,128]{1,0:T(8,128)(2,1)S(1)}, bf16[144,128]{1,0:T(8,128)(2,1)S(1)}, u32[]{:S(2)}, u32[]{:S(2)}) collective-permute-start(bf16[144,128]{1,0:T(8,128)(2,1)S(1)} %get-tuple-element.59), channel_id=1, source_target_pairs={{0,1},{1,0},{2,3},{3,2},{4,5},{5,4},{6,7},{7,6},{8,9},{9,8},{10,11... | collective-permute-start | bytes 110600 | tf_op jit(solution)/shard_map/ppermute | solution.py:460
  113.2 6.1 %collective-permute-start.8 = (bf16[144,128]{1,0:T(8,128)(2,1)S(1)}, bf16[144,128]{1,0:T(8,128)(2,1)S(1)}, u32[]{:S(2)}, u32[]{:S(2)}) collective-permute-start(bf16[144,128]{1,0:T(8,128)(2,1)S(1)} %get-tuple-element.60), channel_id=1, source_target_pairs={{0,2},{1,3},{2,0},{3,1},{4,6},{5,7},{6,4},{7,5},{8,10},{9,11},{10,... | collective-permute-start | bytes 110600 | tf_op jit(solution)/shard_map/ppermute | solution.py:460
  117.2 4.0 %collective-permute-start.9 = (bf16[144,128]{1,0:T(8,128)(2,1)S(1)}, bf16[144,128]{1,0:T(8,128)(2,1)S(1)}, u32[]{:S(2)}, u32[]{:S(2)}) collective-permute-start(bf16[144,128]{1,0:T(8,128)(2,1)S(1)} %get-tuple-element.61), channel_id=1, source_target_pairs={{0,3},{1,2},{2,1},{3,0},{4,7},{5,6},{6,5},{7,4},{8,11},{9,10},{10,... | collective-permute-start | bytes 110600 | tf_op jit(solution)/shard_map/ppermute | solution.py:460
  121.3 9.8 %collective-permute-start.14 = (bf16[336,128]{1,0:T(8,128)(2,1)S(1)}, bf16[336,128]{1,0:T(8,128)(2,1)S(1)}, u32[]{:S(2)}, u32[]{:S(2)}) collective-permute-start(bf16[336,128]{1,0:T(8,128)(2,1)S(1)} %shard_map.116.refs_0_), channel_id=1, source_target_pairs={{0,8},{8,16},{16,24},{24,0},{1,9},{9,17},{17,25},{25,1},{2,10},{10... | collective-permute-start | bytes 258056 | tf_op jit(solution)/shard_map/ppermute | solution.py:465
  121.8 13.5 %collective-permute-start.15 = (bf16[336,128]{1,0:T(8,128)(2,1)S(1)}, bf16[336,128]{1,0:T(8,128)(2,1)S(1)}, u32[]{:S(2)}, u32[]{:S(2)}) collective-permute-start(bf16[336,128]{1,0:T(8,128)(2,1)S(1)} %shard_map.116.refs_0_), channel_id=1, source_target_pairs={{0,16},{8,24},{16,0},{24,8},{1,17},{9,25},{17,1},{25,9},{2,18},{10... | collective-permute-start | bytes 258056 | tf_op jit(solution)/shard_map/ppermute | solution.py:465
  126.6 8.8 %collective-permute-start.16 = (bf16[336,128]{1,0:T(8,128)(2,1)S(1)}, bf16[336,128]{1,0:T(8,128)(2,1)S(1)}, u32[]{:S(2)}, u32[]{:S(2)}) collective-permute-start(bf16[336,128]{1,0:T(8,128)(2,1)S(1)} %shard_map.116.refs_0_), channel_id=1, source_target_pairs={{0,24},{8,0},{16,8},{24,16},{1,25},{9,1},{17,9},{25,17},{2,26},{10... | collective-permute-start | bytes 258056 | tf_op jit(solution)/shard_map/ppermute | solution.py:465

commit v17 on v15

--- a/solution.py
+++ b/solution.py
@@ -495,7 +495,7 @@
     parts = next(n for n in (4, 2, 1) if rows % (n * rows_step) == 0)
     step_frames, narrow_step = (
         max(n for n in range(1, frames + 1) if frames % n == 0 and n * high <= most)
-        for most in (512, 256)
+        for most in (512, 128)
     )
     scale = float((frames * pixels) ** -0.5)
     here = jnp.stack([lax.axis_index("seg"), lax.axis_index("grp")]).astype(jnp.int32)
@@ -517,6 +517,7 @@
         2 * 9 * pixels * ch * ch,
         pixels * ch * 8,
         [(frames_in[0], HBM), (spatial_weight, HBM), (cotangent[0], HBM)],
+        MID_VMEM,
     )
     send, frame = lax.optimization_barrier((send, frames_in[0]))
     send = send.reshape(rows, 2, split, block, ch).swapaxes(1, 2).reshape(devices, 2, block, ch)

time: 146 us -> 149 us (1.021)
  local copies, waits for them, and re-layouts: 0.83 us -> 4.2 us
  starting transfers between devices: 37.7 us -> 36.1 us
  waiting for transfers between devices: 55.1 us -> 56.7 us
    unnamed x16 -> x22, local copies, waits for them, and re-layouts: 0.83 us -> 4.2 us
    ppermute x3, waiting for transfers between devices: 2.76 us -> 4.33 us  [turn_by(): lax.ppermute(value, 'seg', [(i, (i + turn) % size) for i in range(size)])]
    ppermute x3, starting transfers between devices: 6.96 us -> 5.4 us  [turn_by(): lax.ppermute(value, 'seg', [(i, (i + turn) % size) for i in range(size)])]
where the time goes in v17:
time: 149 us
  waiting for transfers between devices  56.7 us (38%)
  Pallas kernels  39.9 us (27%)
  starting transfers between devices  36.1 us (24%)
  blocking collectives  10.2 us (7%)
  local copies, waits for them, and re-layouts  4.2 us (3%)
    all_to_all x3, waiting for transfers between devices, exchange(): return lax.all_to_all(blocks, AXES, split_axis=0, concat_axis=0, tiled=True)  43.3 us
    pallas_call x10, Pallas kernels, call(): pl.pallas_call(kernel, out_shape=[jax.ShapeDtypeStruct(shape, kind) for s...  39.9 us
    ppermute x14, starting transfers between devices, flip(): return lax.ppermute(value, 'grp', [(i, i ^ peer) for i in range(size)])  15.5 us
    all_to_all x3, starting transfers between devices, exchange(): return lax.all_to_all(blocks, AXES, split_axis=0, concat_axis=0, tiled=True)  15.3 us
    all_gather x1, blocking collectives, local(): lax.all_gather(piece, 'grp', axis=0)  10.2 us
    ppermute x14, waiting for transfers between devices, flip(): return lax.ppermute(value, 'grp', [(i, i ^ peer) for i in range(size)])  9.04 us
    ppermute x3, starting transfers between devices, turn_by(): lax.ppermute(value, 'seg', [(i, (i + turn) % size) for i in range(size)])  5.4 us
    ppermute x3, waiting for transfers between devices, turn_by(): lax.ppermute(value, 'seg', [(i, (i + turn) % size) for i in range(size)])  4.33 us
  transfers between devices with their start and end apart: 20, of which 9 were waited for; matrix products, arithmetic and copies ran while one was open for 0% of the time, Pallas kernels for 15%

profile of v17, /device:TPU:0, one launch (start us, length us, event | category | flops | bytes accessed | tf_op | source)
XLA Modules:
  0.0 148.8 jit_solution(11484923149600823715)
XLA Ops:
  0.6 0.0 copy-start.8
  0.6 0.0 copy-start.7
  0.7 0.0 copy-start
  0.7 1.2 copy-done
  1.9 1.0 copy-done.2
  2.8 1.2 copy-done.4
  4.0 4.8 %shard_map.110 = bf16[32,2,120,128]{3,2,1,0:T(8,128)(2,1)} custom-call(bf16[32,120,128]{2,1,0:T(8,128)(2,1)S(1)} %bitcast.11, bf16[9,128,128]{2,1,0:T(8,128)(2,1)S(1)} %copy-done.2, bf16[32,120,128]{2,1,0:T(8,128)(2,1)S(1)} %bitcast.14), custom_call_target="tpu_custom_call" | custom-call | flops 1132462080 | bytes 3932160 | tf_op jit(solution)/shard_map/pallas_call | solution.py:58
  8.9 7.5 %all-to-all-start = ((bf16[32,2,120,128]{3,2,1,0:T(8,128)(2,1)}), bf16[32,2,120,128]{3,2,1,0:T(8,128)(2,1)S(1)}, u32[]{:S(2)}, u32[]{:S(2)}) async-start(bf16[32,2,120,128]{3,2,1,0:T(8,128)(2,1)} %shard_map.110), calls=%async_computation | async-start | bytes 3932160 | tf_op jit(solution)/shard_map/all_to_all | solution.py:451
  16.4 4.4 %shard_map.111.slope_hbm = bf16[28,32,120,128]{3,2,1,0:T(8,128)(2,1)} custom-call(bf16[32,120,128]{2,1,0:T(8,128)(2,1)} %bitcast.10, bf16[9,128,128]{2,1,0:T(8,128)(2,1)} %w_ref.3), custom_call_target="tpu_custom_call" | custom-call | flops 1132462080 | bytes 1966080 | tf_op jit(solution)/shard_map/pallas_call | solution.py:58
  20.8 41.5 %all-to-all-done.got_ref = bf16[32,2,120,128]{3,2,1,0:T(8,128)(2,1)S(1)} async-done(((bf16[32,2,120,128]{3,2,1,0:T(8,128)(2,1)}), bf16[32,2,120,128]{3,2,1,0:T(8,128)(2,1)S(1)}, u32[]{:S(2)}, u32[]{:S(2)}) %all-to-all-start) | async-done | bytes 1966112 | tf_op jit(solution)/shard_map/all_to_all | solution.py:451
  62.3 11.4 %shard_map.112 = (bf16[32,120,128]{2,1,0:T(8,128)(2,1)}, bf16[28,32,128,128]{3,2,1,0:T(8,128)(2,1)}, bf16[28,32,120,128]{3,2,1,0:T(8,128)(2,1)}) custom-call(s32[2]{0:T(128)S(1)} %copy-done.7, s32[4]{0:T(128)S(1)} %copy-done.8, bf16[32,2,120,128]{3,2,1,0:T(8,128)(2,1)S(1)} %all-to-all-done.got_ref, bf16[2,5,128,128]{3,2,1,0:T(8,128)(2,1)S(1)} %copy-done.9, ...), custom_call_target="tpu_custom_call" | custom-call | flops 2768240640 | bytes 8847360 | tf_op jit(solution)/shard_map/pallas_call | solution.py:58
  73.7 4.2 %all-to-all-start.1 = ((bf16[32,120,128]{2,1,0:T(8,128)(2,1)}), bf16[32,120,128]{2,1,0:T(8,128)(2,1)S(1)}, u32[]{:S(2)}, u32[]{:S(2)}) async-start(bf16[32,120,128]{2,1,0:T(8,128)(2,1)} %get-tuple-element.52), calls=%async_computation.1 | async-start | bytes 1966080 | tf_op jit(solution)/shard_map/all_to_all | solution.py:451
  77.8 0.6 pad_add_fusion.here_ref
  78.5 9.8 %shard_map.113 = (bf16[32,120,128]{2,1,0:T(8,128)(2,1)}, bf16[192,128]{1,0:T(8,128)(2,1)}, bf16[192,128]{1,0:T(8,128)(2,1)}, bf16[192,128]{1,0:T(8,128)(2,1)}, b...) custom-call(s32[2]{0:T(128)} %pad_add_fusion.here_ref, ...), custom_call_target="tpu_custom_call" | custom-call | flops 1509949440 | bytes 6881280 | tf_op jit(solution)/shard_map/pallas_call | solution.py:58
  88.3 0.0 copy-start.3
  88.3 0.1 collective-permute-start
  88.4 1.7 %collective-permute-start.1 = (bf16[192,128]{1,0:T(8,128)(2,1)}, bf16[192,128]{1,0:T(8,128)(2,1)S(1)}, u32[]{:S(2)}, u32[]{:S(2)}) collective-permute-start(bf16[192,128]{1,0:T(8,128)(2,1)} %get-tuple-element.46), channel_id=1, source_target_pairs={{0,2},{1,3},{2,0},{3,1},{4,6},{5,7},{6,4},{7,5},{8,10},{9,11},{10,... | collective-permute-start | bytes 147464 | tf_op jit(solution)/shard_map/ppermute | solution.py:456
  90.1 0.2 collective-permute-start.2
  90.2 1.5 %collective-permute-start.3 = (bf16[192,128]{1,0:T(8,128)(2,1)}, bf16[192,128]{1,0:T(8,128)(2,1)S(1)}, u32[]{:S(2)}, u32[]{:S(2)}) collective-permute-start(bf16[192,128]{1,0:T(8,128)(2,1)} %get-tuple-element.48), channel_id=1, source_target_pairs={{0,4},{1,5},{2,6},{3,7},{4,0},{5,1},{6,2},{7,3},{8,12},{9,13},{10,... | collective-permute-start | bytes 147464 | tf_op jit(solution)/shard_map/ppermute | solution.py:456
  91.8 0.2 collective-permute-start.4
  91.9 2.5 %collective-permute-start.5 = (bf16[192,128]{1,0:T(8,128)(2,1)}, bf16[192,128]{1,0:T(8,128)(2,1)S(1)}, u32[]{:S(2)}, u32[]{:S(2)}) collective-permute-start(bf16[192,128]{1,0:T(8,128)(2,1)} %get-tuple-element.50), channel_id=1, source_target_pairs={{0,6},{1,7},{2,4},{3,5},{4,2},{5,3},{6,0},{7,1},{8,14},{9,15},{10,... | collective-permute-start | bytes 147464 | tf_op jit(solution)/shard_map/ppermute | solution.py:456
  94.5 0.0 collective-permute-done.1.refs_2_
  94.5 0.2 collective-permute-start.6
  94.6 0.3 collective-permute-done.2.refs_3_
  94.9 2.4 %collective-permute-done.4.refs_5_ = bf16[192,128]{1,0:T(8,128)(2,1)S(1)} collective-permute-done((bf16[192,128]{1,0:T(8,128)(2,1)}, bf16[192,128]{1,0:T(8,128)(2,1)S(1)}, u32[]{:S(2)}, u32[]{:S(2)}) %collective-permute-start.4) | collective-permute-done | bytes 49184 | tf_op jit(solution)/shard_map/ppermute | solution.py:456
  97.3 0.0 collective-permute-done.5.refs_6_
  97.3 2.5 %collective-permute-done.6.refs_7_ = bf16[192,128]{1,0:T(8,128)(2,1)S(1)} collective-permute-done((bf16[192,128]{1,0:T(8,128)(2,1)}, bf16[192,128]{1,0:T(8,128)(2,1)S(1)}, u32[]{:S(2)}, u32[]{:S(2)}) %collective-permute-start.6) | collective-permute-done | bytes 49184 | tf_op jit(solution)/shard_map/ppermute | solution.py:456
  99.8 0.8 copy-done.5
  100.6 0.1 shard_map.114.first_ref
  100.6 1.8 %all-to-all-done.1.got_ref = bf16[32,120,128]{2,1,0:T(8,128)(2,1)S(1)} async-done(((bf16[32,120,128]{2,1,0:T(8,128)(2,1)}), bf16[32,120,128]{2,1,0:T(8,128)(2,1)S(1)}, u32[]{:S(2)}, u32[]{:S(2)}) %all-to-all-start.1) | async-done | bytes 983072 | tf_op jit(solution)/shard_map/all_to_all | solution.py:451
  102.5 3.6 %all-to-all-start.2 = ((bf16[32,120,128]{2,1,0:T(8,128)(2,1)}), bf16[32,120,128]{2,1,0:T(8,128)(2,1)S(1)}, u32[]{:S(2)}, u32[]{:S(2)}) async-start(bf16[32,120,128]{2,1,0:T(8,128)(2,1)} %get-tuple-element.67), calls=%async_computation.2 | async-start | bytes 1966080 | tf_op jit(solution)/shard_map/all_to_all | solution.py:451
  106.1 3.6 %shard_map.115 = (bf16[144,128]{1,0:T(8,128)(2,1)S(1)}, bf16[144,128]{1,0:T(8,128)(2,1)S(1)}, bf16[144,128]{1,0:T(8,128)(2,1)S(1)}, bf16[144,128]{1,0:T(8,128)(2...) custom-call(s32[2]{0:T(128)S(1)} %copy-done.6, ...), custom_call_target="tpu_custom_call" | custom-call | flops 1132462080 | bytes 3932160 | tf_op jit(solution)/shard_map/pallas_call | solution.py:58
  109.8 1.8 %collective-permute-start.10 = (bf16[144,128]{1,0:T(8,128)(2,1)S(1)}, bf16[144,128]{1,0:T(8,128)(2,1)S(1)}, u32[]{:S(2)}, u32[]{:S(2)}) collective-permute-start(bf16[144,128]{1,0:T(8,128)(2,1)S(1)} %get-tuple-element.62), channel_id=1, source_target_pairs={{0,4},{1,5},{2,6},{3,7},{4,0},{5,1},{6,2},{7,3},{8,12},{9,13},{10,... | collective-permute-start | bytes 110600 | tf_op jit(solution)/shard_map/ppermute | solution.py:456
  111.6 2.4 %collective-permute-start.12 = (bf16[144,128]{1,0:T(8,128)(2,1)S(1)}, bf16[144,128]{1,0:T(8,128)(2,1)S(1)}, u32[]{:S(2)}, u32[]{:S(2)}) collective-permute-start(bf16[144,128]{1,0:T(8,128)(2,1)S(1)} %get-tuple-element.64), channel_id=1, source_target_pairs={{0,6},{1,7},{2,4},{3,5},{4,2},{5,3},{6,0},{7,1},{8,14},{9,15},{10,... | collective-permute-start | bytes 110600 | tf_op jit(solution)/shard_map/ppermute | solution.py:456
  114.0 0.3 collective-permute-start.13
  114.3 0.4 collective-permute-start.7
  114.7 0.1 collective-permute-done.10.refs_4_
  114.8 2.1 %collective-permute-start.8 = (bf16[144,128]{1,0:T(8,128)(2,1)S(1)}, bf16[144,128]{1,0:T(8,128)(2,1)S(1)}, u32[]{:S(2)}, u32[]{:S(2)}) collective-permute-start(bf16[144,128]{1,0:T(8,128)(2,1)S(1)} %get-tuple-element.60), channel_id=1, source_target_pairs={{0,2},{1,3},{2,0},{3,1},{4,6},{5,7},{6,4},{7,5},{8,10},{9,11},{10,... | collective-permute-start | bytes 110600 | tf_op jit(solution)/shard_map/ppermute | solution.py:456
  116.9 1.9 %collective-permute-done.11.refs_5_ = bf16[144,128]{1,0:T(8,128)(2,1)S(1)} collective-permute-done((bf16[144,128]{1,0:T(8,128)(2,1)S(1)}, bf16[144,128]{1,0:T(8,128)(2,1)S(1)}, u32[]{:S(2)}, u32[]{:S(2)}) %collective-permute-start.11) | collective-permute-done | bytes 36896 | tf_op jit(solution)/shard_map/ppermute | solution.py:456
  118.8 2.1 %collective-permute-start.9 = (bf16[144,128]{1,0:T(8,128)(2,1)S(1)}, bf16[144,128]{1,0:T(8,128)(2,1)S(1)}, u32[]{:S(2)}, u32[]{:S(2)}) collective-permute-start(bf16[144,128]{1,0:T(8,128)(2,1)S(1)} %get-tuple-element.61), channel_id=1, source_target_pairs={{0,3},{1,2},{2,1},{3,0},{4,7},{5,6},{6,5},{7,4},{8,11},{9,10},{10,... | collective-permute-start | bytes 110600 | tf_op jit(solution)/shard_map/ppermute | solution.py:456
  120.9 1.9 %collective-permute-done.9.refs_3_ = bf16[144,128]{1,0:T(8,128)(2,1)S(1)} collective-permute-done((bf16[144,128]{1,0:T(8,128)(2,1)S(1)}, bf16[144,128]{1,0:T(8,128)(2,1)S(1)}, u32[]{:S(2)}, u32[]{:S(2)}) %collective-permute-start.9) | collective-permute-done | bytes 36896 | tf_op jit(solution)/shard_map/ppermute | solution.py:456
  122.8 0.6 collective-permute-start.14
  123.4 4.7 %collective-permute-start.15 = (bf16[336,128]{1,0:T(8,128)(2,1)S(1)}, bf16[336,128]{1,0:T(8,128)(2,1)S(1)}, u32[]{:S(2)}, u32[]{:S(2)}) collective-permute-start(bf16[336,128]{1,0:T(8,128)(2,1)S(1)} %shard_map.116.refs_0_), channel_id=1, source_target_pairs={{0,16},{8,24},{16,0},{24,8},{1,17},{9,25},{17,1},{25,9},{2,18},{10... | collective-permute-start | bytes 258056 | tf_op jit(solution)/shard_map/ppermute | solution.py:461
  128.2 0.1 collective-permute-start.16
  128.2 4.3 %shard_map.117 = bf16[32,120,128]{2,1,0:T(8,128)(2,1)} custom-call(bf16[9,128,128]{2,1,0:T(8,128)(2,1)S(1)} %copy-done.3, bf16[32,120,128]{2,1,0:T(8,128)(2,1)S(1)} %all-to-all-done.1.got_ref, bf16[28,32,120,128]{3,2,1,0:T(8,128)(2,1)} %shard_map.111.slope_hbm), custom_call_target="tpu_custom_call" | custom-call | flops 1132462080 | bytes 2949120 | tf_op jit(solution)/shard_map/pallas_call | solution.py:58
  132.6 4.3 %collective-permute-done.15.refs_2_ = bf16[336,128]{1,0:T(8,128)(2,1)S(1)} collective-permute-done((bf16[336,128]{1,0:T(8,128)(2,1)S(1)}, bf16[336,128]{1,0:T(8,128)(2,1)S(1)}, u32[]{:S(2)}, u32[]{:S(2)}) %collective-permute-start.15) | collective-permute-done | bytes 86048 | tf_op jit(solution)/shard_map/ppermute | solution.py:461
  137.0 10.2 %all-gather = bf16[2688,128]{1,0:T(8,128)(2,1)S(1)} all-gather(bf16[336,128]{1,0:T(8,128)(2,1)S(1)} %shard_map.118), channel_id=2, replica_groups=mesh['seg'=4,'grp'=8] {'grp'}, dimensions={0}, use_global_device_ids=true | all-gather | bytes 774144 | tf_op jit(solution)/shard_map/all_gather | solution.py:649
  147.2 1.4 shard_map.119
  (26 shorter events, 0.1 us)
Async XLA Ops:
  0.6 61.6 %copy-start.8 = (s32[4]{0:T(128)S(1)}, s32[4]{0:T(128)}, u32[]{:S(2)}) copy-start(s32[4]{0:T(128)} %key_ref.3) | copy-start | bytes 52
  0.6 61.6 %copy-start.7 = (s32[2]{0:T(128)S(1)}, s32[2]{0:T(128)}, u32[]{:S(2)}) copy-start(s32[2]{0:T(128)} %dil_ref.3) | copy-start | bytes 28
  0.7 1.2 copy-start
  1.9 1.0 copy-start.2
  2.8 1.2 copy-start.4
  4.0 58.2 %copy-start.9 = (bf16[2,5,128,128]{3,2,1,0:T(8,128)(2,1)S(1)}, bf16[2,5,128,128]{3,2,1,0:T(8,128)(2,1)}, u32[]{:S(2)}) copy-start(bf16[2,5,128,128]{3,2,1,0:T(8,128)(2,1)} %tw_hbm.1) | copy-start | bytes 983044
  4.0 58.2 %copy-start.10 = (bf16[2,128,128]{2,1,0:T(8,128)(2,1)S(1)}, bf16[2,128,128]{2,1,0:T(8,128)(2,1)}, u32[]{:S(2)}) copy-start(bf16[2,128,128]{2,1,0:T(8,128)(2,1)} %uw_hbm.1) | copy-start | bytes 196612
  8.9 53.4 %all-to-all-start = ((bf16[32,2,120,128]{3,2,1,0:T(8,128)(2,1)}), bf16[32,2,120,128]{3,2,1,0:T(8,128)(2,1)S(1)}, u32[]{:S(2)}, u32[]{:S(2)}) async-start(bf16[32,2,120,128]{3,2,1,0:T(8,128)(2,1)} %shard_map.110), calls=%async_computation | async-start | bytes 3932160 | tf_op jit(solution)/shard_map/all_to_all | solution.py:451
  73.7 28.8 %all-to-all-start.1 = ((bf16[32,120,128]{2,1,0:T(8,128)(2,1)}), bf16[32,120,128]{2,1,0:T(8,128)(2,1)S(1)}, u32[]{:S(2)}, u32[]{:S(2)}) async-start(bf16[32,120,128]{2,1,0:T(8,128)(2,1)} %get-tuple-element.52), calls=%async_computation.1 | async-start | bytes 1966080 | tf_op jit(solution)/shard_map/all_to_all | solution.py:451
  78.5 27.6 %copy-start.1 = (bf16[1,32,120,128]{3,2,1,0:T(8,128)(2,1)S(1)}, bf16[1,32,120,128]{3,2,1,0:T(8,128)(2,1)}, u32[]{:S(2)}) copy-start(bf16[1,32,120,128]{3,2,1,0:T(8,128)(2,1)} %param.7) | copy-start | bytes 2949124
  78.5 27.6 %copy-start.6 = (s32[2]{0:T(128)S(1)}, s32[2]{0:T(128)}, u32[]{:S(2)}) copy-start(s32[2]{0:T(128)} %pad_add_fusion.here_ref) | copy-start | bytes 28
  88.3 40.0 %copy-start.3 = (bf16[9,128,128]{2,1,0:T(8,128)(2,1)S(1)}, bf16[9,128,128]{2,1,0:T(8,128)(2,1)}, u32[]{:S(2)}) copy-start(bf16[9,128,128]{2,1,0:T(8,128)(2,1)} %w_ref.3) | copy-start | bytes 884740
  88.3 3.6 %collective-permute-start = (bf16[192,128]{1,0:T(8,128)(2,1)}, bf16[192,128]{1,0:T(8,128)(2,1)S(1)}, u32[]{:S(2)}, u32[]{:S(2)}) collective-permute-start(bf16[192,128]{1,0:T(8,128)(2,1)} %get-tuple-element.45), channel_id=1, source_target_pairs={{0,1},{1,0},{2,3},{3,2},{4,5},{5,4},{6,7},{7,6},{8,9},{9,8},{10,11... | collective-permute-start | bytes 147464 | tf_op jit(solution)/shard_map/ppermute | solution.py:456
  88.4 6.1 %collective-permute-start.1 = (bf16[192,128]{1,0:T(8,128)(2,1)}, bf16[192,128]{1,0:T(8,128)(2,1)S(1)}, u32[]{:S(2)}, u32[]{:S(2)}) collective-permute-start(bf16[192,128]{1,0:T(8,128)(2,1)} %get-tuple-element.46), channel_id=1, source_target_pairs={{0,2},{1,3},{2,0},{3,1},{4,6},{5,7},{6,4},{7,5},{8,10},{9,11},{10,... | collective-permute-start | bytes 147464 | tf_op jit(solution)/shard_map/ppermute | solution.py:456
  90.1 4.9 %collective-permute-start.2 = (bf16[192,128]{1,0:T(8,128)(2,1)}, bf16[192,128]{1,0:T(8,128)(2,1)S(1)}, u32[]{:S(2)}, u32[]{:S(2)}) collective-permute-start(bf16[192,128]{1,0:T(8,128)(2,1)} %get-tuple-element.47), channel_id=1, source_target_pairs={{0,3},{1,2},{2,1},{3,0},{4,7},{5,6},{6,5},{7,4},{8,11},{9,10},{10,... | collective-permute-start | bytes 147464 | tf_op jit(solution)/shard_map/ppermute | solution.py:456
  90.2 4.7 %collective-permute-start.3 = (bf16[192,128]{1,0:T(8,128)(2,1)}, bf16[192,128]{1,0:T(8,128)(2,1)S(1)}, u32[]{:S(2)}, u32[]{:S(2)}) collective-permute-start(bf16[192,128]{1,0:T(8,128)(2,1)} %get-tuple-element.48), channel_id=1, source_target_pairs={{0,4},{1,5},{2,6},{3,7},{4,0},{5,1},{6,2},{7,3},{8,12},{9,13},{10,... | collective-permute-start | bytes 147464 | tf_op jit(solution)/shard_map/ppermute | solution.py:456
  91.8 5.5 %collective-permute-start.4 = (bf16[192,128]{1,0:T(8,128)(2,1)}, bf16[192,128]{1,0:T(8,128)(2,1)S(1)}, u32[]{:S(2)}, u32[]{:S(2)}) collective-permute-start(bf16[192,128]{1,0:T(8,128)(2,1)} %get-tuple-element.49), channel_id=1, source_target_pairs={{0,5},{1,4},{2,7},{3,6},{4,1},{5,0},{6,3},{7,2},{8,13},{9,12},{10,... | collective-permute-start | bytes 147464 | tf_op jit(solution)/shard_map/ppermute | solution.py:456
  91.9 5.4 %collective-permute-start.5 = (bf16[192,128]{1,0:T(8,128)(2,1)}, bf16[192,128]{1,0:T(8,128)(2,1)S(1)}, u32[]{:S(2)}, u32[]{:S(2)}) collective-permute-start(bf16[192,128]{1,0:T(8,128)(2,1)} %get-tuple-element.50), channel_id=1, source_target_pairs={{0,6},{1,7},{2,4},{3,5},{4,2},{5,3},{6,0},{7,1},{8,14},{9,15},{10,... | collective-permute-start | bytes 147464 | tf_op jit(solution)/shard_map/ppermute | solution.py:456
  94.5 5.3 %collective-permute-start.6 = (bf16[192,128]{1,0:T(8,128)(2,1)}, bf16[192,128]{1,0:T(8,128)(2,1)S(1)}, u32[]{:S(2)}, u32[]{:S(2)}) collective-permute-start(bf16[192,128]{1,0:T(8,128)(2,1)} %get-tuple-element.51), channel_id=1, source_target_pairs={{0,7},{1,6},{2,5},{3,4},{4,3},{5,2},{6,1},{7,0},{8,15},{9,14},{10,... | collective-permute-start | bytes 147464 | tf_op jit(solution)/shard_map/ppermute | solution.py:456
  99.8 0.8 copy-start.5
  102.5 44.8 %all-to-all-start.2 = ((bf16[32,120,128]{2,1,0:T(8,128)(2,1)}), bf16[32,120,128]{2,1,0:T(8,128)(2,1)S(1)}, u32[]{:S(2)}, u32[]{:S(2)}) async-start(bf16[32,120,128]{2,1,0:T(8,128)(2,1)} %get-tuple-element.67), calls=%async_computation.2 | async-start | bytes 1966080 | tf_op jit(solution)/shard_map/all_to_all | solution.py:451
  109.8 5.0 %collective-permute-start.10 = (bf16[144,128]{1,0:T(8,128)(2,1)S(1)}, bf16[144,128]{1,0:T(8,128)(2,1)S(1)}, u32[]{:S(2)}, u32[]{:S(2)}) collective-permute-start(bf16[144,128]{1,0:T(8,128)(2,1)S(1)} %get-tuple-element.62), channel_id=1, source_target_pairs={{0,4},{1,5},{2,6},{3,7},{4,0},{5,1},{6,2},{7,3},{8,12},{9,13},{10,... | collective-permute-start | bytes 110600 | tf_op jit(solution)/shard_map/ppermute | solution.py:456
  111.6 7.2 %collective-permute-start.11 = (bf16[144,128]{1,0:T(8,128)(2,1)S(1)}, bf16[144,128]{1,0:T(8,128)(2,1)S(1)}, u32[]{:S(2)}, u32[]{:S(2)}) collective-permute-start(bf16[144,128]{1,0:T(8,128)(2,1)S(1)} %get-tuple-element.63), channel_id=1, source_target_pairs={{0,5},{1,4},{2,7},{3,6},{4,1},{5,0},{6,3},{7,2},{8,13},{9,12},{10,... | collective-permute-start | bytes 110600 | tf_op jit(solution)/shard_map/ppermute | solution.py:456
  111.6 9.3 %collective-permute-start.12 = (bf16[144,128]{1,0:T(8,128)(2,1)S(1)}, bf16[144,128]{1,0:T(8,128)(2,1)S(1)}, u32[]{:S(2)}, u32[]{:S(2)}) collective-permute-start(bf16[144,128]{1,0:T(8,128)(2,1)S(1)} %get-tuple-element.64), channel_id=1, source_target_pairs={{0,6},{1,7},{2,4},{3,5},{4,2},{5,3},{6,0},{7,1},{8,14},{9,15},{10,... | collective-permute-start | bytes 110600 | tf_op jit(solution)/shard_map/ppermute | solution.py:456
  114.0 6.9 %collective-permute-start.13 = (bf16[144,128]{1,0:T(8,128)(2,1)S(1)}, bf16[144,128]{1,0:T(8,128)(2,1)S(1)}, u32[]{:S(2)}, u32[]{:S(2)}) collective-permute-start(bf16[144,128]{1,0:T(8,128)(2,1)S(1)} %get-tuple-element.65), channel_id=1, source_target_pairs={{0,7},{1,6},{2,5},{3,4},{4,3},{5,2},{6,1},{7,0},{8,15},{9,14},{10,... | collective-permute-start | bytes 110600 | tf_op jit(solution)/shard_map/ppermute | solution.py:456
  114.3 6.6 %collective-permute-start.7 = (bf16[144,128]{1,0:T(8,128)(2,1)S(1)}, bf16[144,128]{1,0:T(8,128)(2,1)S(1)}, u32[]{:S(2)}, u32[]{:S(2)}) collective-permute-start(bf16[144,128]{1,0:T(8,128)(2,1)S(1)} %get-tuple-element.59), channel_id=1, source_target_pairs={{0,1},{1,0},{2,3},{3,2},{4,5},{5,4},{6,7},{7,6},{8,9},{9,8},{10,11... | collective-permute-start | bytes 110600 | tf_op jit(solution)/shard_map/ppermute | solution.py:456
  114.8 6.1 %collective-permute-start.8 = (bf16[144,128]{1,0:T(8,128)(2,1)S(1)}, bf16[144,128]{1,0:T(8,128)(2,1)S(1)}, u32[]{:S(2)}, u32[]{:S(2)}) collective-permute-start(bf16[144,128]{1,0:T(8,128)(2,1)S(1)} %get-tuple-element.60), channel_id=1, source_target_pairs={{0,2},{1,3},{2,0},{3,1},{4,6},{5,7},{6,4},{7,5},{8,10},{9,11},{10,... | collective-permute-start | bytes 110600 | tf_op jit(solution)/shard_map/ppermute | solution.py:456
  118.8 4.0 %collective-permute-start.9 = (bf16[144,128]{1,0:T(8,128)(2,1)S(1)}, bf16[144,128]{1,0:T(8,128)(2,1)S(1)}, u32[]{:S(2)}, u32[]{:S(2)}) collective-permute-start(bf16[144,128]{1,0:T(8,128)(2,1)S(1)} %get-tuple-element.61), channel_id=1, source_target_pairs={{0,3},{1,2},{2,1},{3,0},{4,7},{5,6},{6,5},{7,4},{8,11},{9,10},{10,... | collective-permute-start | bytes 110600 | tf_op jit(solution)/shard_map/ppermute | solution.py:456
  122.8 9.7 %collective-permute-start.14 = (bf16[336,128]{1,0:T(8,128)(2,1)S(1)}, bf16[336,128]{1,0:T(8,128)(2,1)S(1)}, u32[]{:S(2)}, u32[]{:S(2)}) collective-permute-start(bf16[336,128]{1,0:T(8,128)(2,1)S(1)} %shard_map.116.refs_0_), channel_id=1, source_target_pairs={{0,8},{8,16},{16,24},{24,0},{1,9},{9,17},{17,25},{25,1},{2,10},{10... | collective-permute-start | bytes 258056 | tf_op jit(solution)/shard_map/ppermute | solution.py:461
  123.4 13.5 %collective-permute-start.15 = (bf16[336,128]{1,0:T(8,128)(2,1)S(1)}, bf16[336,128]{1,0:T(8,128)(2,1)S(1)}, u32[]{:S(2)}, u32[]{:S(2)}) collective-permute-start(bf16[336,128]{1,0:T(8,128)(2,1)S(1)} %shard_map.116.refs_0_), channel_id=1, source_target_pairs={{0,16},{8,24},{16,0},{24,8},{1,17},{9,25},{17,1},{25,9},{2,18},{10... | collective-permute-start | bytes 258056 | tf_op jit(solution)/shard_map/ppermute | solution.py:461
  128.2 8.8 %collective-permute-start.16 = (bf16[336,128]{1,0:T(8,128)(2,1)S(1)}, bf16[336,128]{1,0:T(8,128)(2,1)S(1)}, u32[]{:S(2)}, u32[]{:S(2)}) collective-permute-start(bf16[336,128]{1,0:T(8,128)(2,1)S(1)} %shard_map.116.refs_0_), channel_id=1, source_target_pairs={{0,24},{8,0},{16,8},{24,16},{1,25},{9,1},{17,9},{25,17},{2,26},{10... | collective-permute-start | bytes 258056 | tf_op jit(solution)/shard_map/ppermute | solution.py:461

commit v18 on v15

--- a/solution.py
+++ b/solution.py
@@ -456,9 +456,9 @@
     return lax.ppermute(value, "grp", [(i, i ^ peer) for i in range(size)])
 
 
-def turn_by(value, turn):
+def meet_in_seg(value, bit):
     size = lax.axis_size("seg")
-    return lax.ppermute(value, "seg", [(i, (i + turn) % size) for i in range(size)])
+    return lax.ppermute(value, "seg", [(i, i ^ bit) for i in range(size)])
 
 
 def sum_of(parts):
@@ -471,10 +471,6 @@
 
 def reduce_in_grp(pieces):
     return sum_of([flip(piece, peer) if peer else piece for peer, piece in enumerate(pieces)])
-
-
-def all_turns(value):
-    return [turn_by(value, turn) if turn else value for turn in range(lax.axis_size("seg"))]
 
 
 def local(
@@ -484,7 +480,8 @@
     assert held == 1
     pixels = rows * cols
     peers = lax.axis_size("grp")
-    devices = lax.axis_size("seg") * peers
+    segs = lax.axis_size("seg")
+    devices = segs * peers
     frames = held * devices
     block = pixels // devices
     split = cols // block
@@ -634,9 +631,13 @@
         [(time_sum, VMEM)] + [(part, VMEM) for part in space_parts],
         SMALL_VMEM,
     )
-    turned = all_turns(plane)
-    turned[0], back = lax.optimization_barrier((turned[0], back))
-    piece = sum_of(turned)
+    piece = plane
+    bits = [1 << n for n in range((segs - 1).bit_length())]
+    for bit in bits:
+        other = meet_in_seg(piece, bit)
+        if bit == bits[-1]:
+            other, back = lax.optimization_barrier((other, back))
+        piece = sum_of([piece, other])
     *grads, united = call(
         deal_kernel,
         [((peers, count, ch), F32, HBM) for count in (time_rows, unite_rows, space_rows)]

time: 146 us -> 146 us (level)
  starting transfers between devices: 37.7 us -> 33.3 us
  waiting for transfers between devices: 55.1 us -> 58.5 us
    ppermute x3 -> x2, starting transfers between devices: 6.96 us -> 2.61 us  [meet_in_seg(): return lax.ppermute(value, 'seg', [(i, i ^ bit) for i in range(size)])]
    ppermute x3 -> x2, waiting for transfers between devices: 2.76 us -> 6.11 us  [meet_in_seg(): return lax.ppermute(value, 'seg', [(i, i ^ bit) for i in range(size)])]
    pallas_call x10 -> x11, Pallas kernels: 39.6 us -> 39.6 us  [call(): pl.pallas_call(kernel, out_shape=[jax.ShapeDtypeStruct(shape, kind) for s...]
  transfers between devices with their start and end apart: 20 -> 19, of which waited for: 9 -> 9; matrix products, arithmetic and copies ran while one was open for 0% -> 0% of each run, Pallas kernels for 15% -> 15%
where the time goes in v18:
time: 146 us; the launch traced here: 145 us
  waiting for transfers between devices  58.5 us (40%)
  Pallas kernels  39.6 us (27%)
  starting transfers between devices  33.3 us (23%)
  blocking collectives  11.1 us (8%)
    all_to_all x3, waiting for transfers between devices, exchange(): return lax.all_to_all(blocks, AXES, split_axis=0, concat_axis=0, tiled=True)  43.3 us
    pallas_call x11, Pallas kernels, call(): pl.pallas_call(kernel, out_shape=[jax.ShapeDtypeStruct(shape, kind) for s...  39.6 us
    ppermute x14, starting transfers between devices, flip(): return lax.ppermute(value, 'grp', [(i, i ^ peer) for i in range(size)])  15.5 us
    all_to_all x3, starting transfers between devices, exchange(): return lax.all_to_all(blocks, AXES, split_axis=0, concat_axis=0, tiled=True)  15.3 us
    all_gather x1, blocking collectives, local(): lax.all_gather(piece, 'grp', axis=0)  11.1 us
    ppermute x14, waiting for transfers between devices, flip(): return lax.ppermute(value, 'grp', [(i, i ^ peer) for i in range(size)])  9.04 us
    ppermute x2, waiting for transfers between devices, meet_in_seg(): return lax.ppermute(value, 'seg', [(i, i ^ bit) for i in range(size)])  6.11 us
  transfers between devices with their start and end apart: 19, of which 9 were waited for; matrix products, arithmetic and copies ran while one was open for 0% of the time, Pallas kernels for 15%

profile of v18, /device:TPU:0, one launch (start us, length us, event | category | flops | bytes accessed | tf_op | source)
XLA Modules:
  0.0 145.0 jit_solution(4182576829140568248)
XLA Ops:
  0.6 0.0 copy-start.5
  0.7 0.0 copy-start.4
  0.7 4.8 %shard_map.110 = bf16[32,2,120,128]{3,2,1,0:T(8,128)(2,1)} custom-call(bf16[32,120,128]{2,1,0:T(8,128)(2,1)} %bitcast.10, bf16[9,128,128]{2,1,0:T(8,128)(2,1)} %w_ref.3, bf16[32,120,128]{2,1,0:T(8,128)(2,1)} %bitcast.14), custom_call_target="tpu_custom_call" | custom-call | flops 1132462080 | bytes 3932160 | tf_op jit(solution)/shard_map/pallas_call | solution.py:58
  5.5 7.5 %all-to-all-start = ((bf16[32,2,120,128]{3,2,1,0:T(8,128)(2,1)}), bf16[32,2,120,128]{3,2,1,0:T(8,128)(2,1)S(1)}, u32[]{:S(2)}, u32[]{:S(2)}) async-start(bf16[32,2,120,128]{3,2,1,0:T(8,128)(2,1)} %shard_map.110), calls=%async_computation | async-start | bytes 3932160 | tf_op jit(solution)/shard_map/all_to_all | solution.py:451
  13.0 4.4 %shard_map.111.slope_hbm = bf16[28,32,120,128]{3,2,1,0:T(8,128)(2,1)} custom-call(bf16[32,120,128]{2,1,0:T(8,128)(2,1)} %bitcast.11, bf16[9,128,128]{2,1,0:T(8,128)(2,1)} %w_ref.3), custom_call_target="tpu_custom_call" | custom-call | flops 1132462080 | bytes 1966080 | tf_op jit(solution)/shard_map/pallas_call | solution.py:58
  17.4 41.5 %all-to-all-done.got_ref = bf16[32,2,120,128]{3,2,1,0:T(8,128)(2,1)S(1)} async-done(((bf16[32,2,120,128]{3,2,1,0:T(8,128)(2,1)}), bf16[32,2,120,128]{3,2,1,0:T(8,128)(2,1)S(1)}, u32[]{:S(2)}, u32[]{:S(2)}) %all-to-all-start) | async-done | bytes 1966112 | tf_op jit(solution)/shard_map/all_to_all | solution.py:451
  58.9 11.0 %shard_map.112 = (bf16[32,120,128]{2,1,0:T(8,128)(2,1)}, bf16[28,32,128,128]{3,2,1,0:T(8,128)(2,1)}, bf16[28,32,120,128]{3,2,1,0:T(8,128)(2,1)}) custom-call(s32[2]{0:T(128)S(1)} %copy-done.4, s32[4]{0:T(128)S(1)} %copy-done.5, bf16[32,2,120,128]{3,2,1,0:T(8,128)(2,1)S(1)} %all-to-all-done.got_ref, bf16[2,5,128,128]{3,2,1,0:T(8,128)(2,1)S(1)} %copy-done.6, ...), custom_call_target="tpu_custom_call" | custom-call | flops 2768240640 | bytes 8847360 | tf_op jit(solution)/shard_map/pallas_call | solution.py:58
  69.9 4.2 %all-to-all-start.1 = ((bf16[32,120,128]{2,1,0:T(8,128)(2,1)}), bf16[32,120,128]{2,1,0:T(8,128)(2,1)S(1)}, u32[]{:S(2)}, u32[]{:S(2)}) async-start(bf16[32,120,128]{2,1,0:T(8,128)(2,1)} %get-tuple-element.52), calls=%async_computation.1 | async-start | bytes 1966080 | tf_op jit(solution)/shard_map/all_to_all | solution.py:451
  74.1 0.6 pad_add_fusion.here_ref
  74.8 9.8 %shard_map.113 = (bf16[32,120,128]{2,1,0:T(8,128)(2,1)}, bf16[192,128]{1,0:T(8,128)(2,1)}, bf16[192,128]{1,0:T(8,128)(2,1)}, bf16[192,128]{1,0:T(8,128)(2,1)}, b...) custom-call(s32[2]{0:T(128)} %pad_add_fusion.here_ref, ...), custom_call_target="tpu_custom_call" | custom-call | flops 1509949440 | bytes 6881280 | tf_op jit(solution)/shard_map/pallas_call | solution.py:58
  84.6 0.0 copy-start.1
  84.6 0.1 collective-permute-start
  84.7 1.7 %collective-permute-start.1 = (bf16[192,128]{1,0:T(8,128)(2,1)}, bf16[192,128]{1,0:T(8,128)(2,1)S(1)}, u32[]{:S(2)}, u32[]{:S(2)}) collective-permute-start(bf16[192,128]{1,0:T(8,128)(2,1)} %get-tuple-element.46), channel_id=1, source_target_pairs={{0,2},{1,3},{2,0},{3,1},{4,6},{5,7},{6,4},{7,5},{8,10},{9,11},{10,... | collective-permute-start | bytes 147464 | tf_op jit(solution)/shard_map/ppermute | solution.py:456
  86.4 0.2 collective-permute-start.2
  86.5 1.5 %collective-permute-start.3 = (bf16[192,128]{1,0:T(8,128)(2,1)}, bf16[192,128]{1,0:T(8,128)(2,1)S(1)}, u32[]{:S(2)}, u32[]{:S(2)}) collective-permute-start(bf16[192,128]{1,0:T(8,128)(2,1)} %get-tuple-element.48), channel_id=1, source_target_pairs={{0,4},{1,5},{2,6},{3,7},{4,0},{5,1},{6,2},{7,3},{8,12},{9,13},{10,... | collective-permute-start | bytes 147464 | tf_op jit(solution)/shard_map/ppermute | solution.py:456
  88.1 0.2 collective-permute-start.4
  88.2 0.0 collective-permute-done.refs_1_
  88.2 2.5 %collective-permute-start.5 = (bf16[192,128]{1,0:T(8,128)(2,1)}, bf16[192,128]{1,0:T(8,128)(2,1)S(1)}, u32[]{:S(2)}, u32[]{:S(2)}) collective-permute-start(bf16[192,128]{1,0:T(8,128)(2,1)} %get-tuple-element.50), channel_id=1, source_target_pairs={{0,6},{1,7},{2,4},{3,5},{4,2},{5,3},{6,0},{7,1},{8,14},{9,15},{10,... | collective-permute-start | bytes 147464 | tf_op jit(solution)/shard_map/ppermute | solution.py:456
  90.8 0.2 collective-permute-start.6
  90.9 0.3 collective-permute-done.2.refs_3_
  91.2 0.0 collective-permute-done.3.refs_4_
  91.2 2.4 %collective-permute-done.4.refs_5_ = bf16[192,128]{1,0:T(8,128)(2,1)S(1)} collective-permute-done((bf16[192,128]{1,0:T(8,128)(2,1)}, bf16[192,128]{1,0:T(8,128)(2,1)S(1)}, u32[]{:S(2)}, u32[]{:S(2)}) %collective-permute-start.4) | collective-permute-done | bytes 49184 | tf_op jit(solution)/shard_map/ppermute | solution.py:456
  93.6 0.0 collective-permute-done.5.refs_6_
  93.6 2.4 %collective-permute-done.6.refs_7_ = bf16[192,128]{1,0:T(8,128)(2,1)S(1)} collective-permute-done((bf16[192,128]{1,0:T(8,128)(2,1)}, bf16[192,128]{1,0:T(8,128)(2,1)S(1)}, u32[]{:S(2)}, u32[]{:S(2)}) %collective-permute-start.6) | collective-permute-done | bytes 49184 | tf_op jit(solution)/shard_map/ppermute | solution.py:456
  96.1 0.8 copy-done.2
  96.9 0.1 shard_map.114.first_ref
  96.9 1.8 %all-to-all-done.1.got_ref = bf16[32,120,128]{2,1,0:T(8,128)(2,1)S(1)} async-done(((bf16[32,120,128]{2,1,0:T(8,128)(2,1)}), bf16[32,120,128]{2,1,0:T(8,128)(2,1)S(1)}, u32[]{:S(2)}, u32[]{:S(2)}) %all-to-all-start.1) | async-done | bytes 983072 | tf_op jit(solution)/shard_map/all_to_all | solution.py:451
  98.7 3.6 %all-to-all-start.2 = ((bf16[32,120,128]{2,1,0:T(8,128)(2,1)}), bf16[32,120,128]{2,1,0:T(8,128)(2,1)S(1)}, u32[]{:S(2)}, u32[]{:S(2)}) async-start(bf16[32,120,128]{2,1,0:T(8,128)(2,1)} %get-tuple-element.67), calls=%async_computation.2 | async-start | bytes 1966080 | tf_op jit(solution)/shard_map/all_to_all | solution.py:451
  102.4 3.6 %shard_map.115 = (bf16[144,128]{1,0:T(8,128)(2,1)S(1)}, bf16[144,128]{1,0:T(8,128)(2,1)S(1)}, bf16[144,128]{1,0:T(8,128)(2,1)S(1)}, bf16[144,128]{1,0:T(8,128)(2...) custom-call(s32[2]{0:T(128)S(1)} %copy-done.3, ...), custom_call_target="tpu_custom_call" | custom-call | flops 1132462080 | bytes 3932160 | tf_op jit(solution)/shard_map/pallas_call | solution.py:58
  106.0 1.8 %collective-permute-start.10 = (bf16[144,128]{1,0:T(8,128)(2,1)S(1)}, bf16[144,128]{1,0:T(8,128)(2,1)S(1)}, u32[]{:S(2)}, u32[]{:S(2)}) collective-permute-start(bf16[144,128]{1,0:T(8,128)(2,1)S(1)} %get-tuple-element.62), channel_id=1, source_target_pairs={{0,4},{1,5},{2,6},{3,7},{4,0},{5,1},{6,2},{7,3},{8,12},{9,13},{10,... | collective-permute-start | bytes 110600 | tf_op jit(solution)/shard_map/ppermute | solution.py:456
  107.9 2.4 %collective-permute-start.12 = (bf16[144,128]{1,0:T(8,128)(2,1)S(1)}, bf16[144,128]{1,0:T(8,128)(2,1)S(1)}, u32[]{:S(2)}, u32[]{:S(2)}) collective-permute-start(bf16[144,128]{1,0:T(8,128)(2,1)S(1)} %get-tuple-element.64), channel_id=1, source_target_pairs={{0,6},{1,7},{2,4},{3,5},{4,2},{5,3},{6,0},{7,1},{8,14},{9,15},{10,... | collective-permute-start | bytes 110600 | tf_op jit(solution)/shard_map/ppermute | solution.py:456
  110.3 0.3 collective-permute-start.13
  110.6 0.4 collective-permute-start.7
  110.9 0.1 collective-permute-done.10.refs_4_
  111.1 2.1 %collective-permute-start.8 = (bf16[144,128]{1,0:T(8,128)(2,1)S(1)}, bf16[144,128]{1,0:T(8,128)(2,1)S(1)}, u32[]{:S(2)}, u32[]{:S(2)}) collective-permute-start(bf16[144,128]{1,0:T(8,128)(2,1)S(1)} %get-tuple-element.60), channel_id=1, source_target_pairs={{0,2},{1,3},{2,0},{3,1},{4,6},{5,7},{6,4},{7,5},{8,10},{9,11},{10,... | collective-permute-start | bytes 110600 | tf_op jit(solution)/shard_map/ppermute | solution.py:456
  113.2 1.9 %collective-permute-done.11.refs_5_ = bf16[144,128]{1,0:T(8,128)(2,1)S(1)} collective-permute-done((bf16[144,128]{1,0:T(8,128)(2,1)S(1)}, bf16[144,128]{1,0:T(8,128)(2,1)S(1)}, u32[]{:S(2)}, u32[]{:S(2)}) %collective-permute-start.11) | collective-permute-done | bytes 36896 | tf_op jit(solution)/shard_map/ppermute | solution.py:456
  115.0 2.1 %collective-permute-start.9 = (bf16[144,128]{1,0:T(8,128)(2,1)S(1)}, bf16[144,128]{1,0:T(8,128)(2,1)S(1)}, u32[]{:S(2)}, u32[]{:S(2)}) collective-permute-start(bf16[144,128]{1,0:T(8,128)(2,1)S(1)} %get-tuple-element.61), channel_id=1, source_target_pairs={{0,3},{1,2},{2,1},{3,0},{4,7},{5,6},{6,5},{7,4},{8,11},{9,10},{10,... | collective-permute-start | bytes 110600 | tf_op jit(solution)/shard_map/ppermute | solution.py:456
  117.2 0.0 collective-permute-done.12.refs_6_
  117.2 0.0 collective-permute-done.13.refs_7_
  117.2 0.0 collective-permute-done.7.refs_1_
  117.2 1.9 %collective-permute-done.9.refs_3_ = bf16[144,128]{1,0:T(8,128)(2,1)S(1)} collective-permute-done((bf16[144,128]{1,0:T(8,128)(2,1)S(1)}, bf16[144,128]{1,0:T(8,128)(2,1)S(1)}, u32[]{:S(2)}, u32[]{:S(2)}) %collective-permute-start.9) | collective-permute-done | bytes 36896 | tf_op jit(solution)/shard_map/ppermute | solution.py:456
  119.1 0.1 shard_map.116.refs_0_
  119.1 0.6 collective-permute-start.14
  119.7 6.1 %collective-permute-done.14.refs_1_ = bf16[336,128]{1,0:T(8,128)(2,1)S(1)} collective-permute-done((bf16[336,128]{1,0:T(8,128)(2,1)S(1)}, bf16[336,128]{1,0:T(8,128)(2,1)S(1)}, u32[]{:S(2)}, u32[]{:S(2)}) %collective-permute-start.14) | collective-permute-done | bytes 86048 | tf_op jit(solution)/shard_map/ppermute | solution.py:461
  125.8 2.0 %collective-permute-start.15 = (bf16[336,128]{1,0:T(8,128)(2,1)S(1)}, bf16[336,128]{1,0:T(8,128)(2,1)S(1)}, u32[]{:S(2)}, u32[]{:S(2)}) collective-permute-start(bf16[336,128]{1,0:T(8,128)(2,1)S(1)} %shard_map.117.refs_0_), channel_id=1, source_target_pairs={{0,16},{8,24},{16,0},{24,8},{1,17},{9,25},{17,1},{25,9},{2,18},{10... | collective-permute-start | bytes 258056 | tf_op jit(solution)/shard_map/ppermute | solution.py:461
  127.9 4.3 %shard_map.118 = bf16[32,120,128]{2,1,0:T(8,128)(2,1)} custom-call(bf16[9,128,128]{2,1,0:T(8,128)(2,1)S(1)} %copy-done.1, bf16[32,120,128]{2,1,0:T(8,128)(2,1)S(1)} %all-to-all-done.1.got_ref, bf16[28,32,120,128]{3,2,1,0:T(8,128)(2,1)} %shard_map.111.slope_hbm), custom_call_target="tpu_custom_call" | custom-call | flops 1132462080 | bytes 2949120 | tf_op jit(solution)/shard_map/pallas_call | solution.py:58
  132.3 11.1 %all-gather = bf16[2688,128]{1,0:T(8,128)(2,1)S(1)} all-gather(bf16[336,128]{1,0:T(8,128)(2,1)S(1)} %shard_map.119), channel_id=2, replica_groups=mesh['seg'=4,'grp'=8] {'grp'}, dimensions={0}, use_global_device_ids=true | all-gather | bytes 774144 | tf_op jit(solution)/shard_map/all_gather | solution.py:649
  143.4 1.4 shard_map.120
  (19 shorter events, 0.1 us)
Async XLA Ops:
  0.6 58.2 %copy-start.7 = (bf16[2,128,128]{2,1,0:T(8,128)(2,1)S(1)}, bf16[2,128,128]{2,1,0:T(8,128)(2,1)}, u32[]{:S(2)}) copy-start(bf16[2,128,128]{2,1,0:T(8,128)(2,1)} %uw_hbm.1) | copy-start | bytes 196612
  0.6 58.2 %copy-start.5 = (s32[4]{0:T(128)S(1)}, s32[4]{0:T(128)}, u32[]{:S(2)}) copy-start(s32[4]{0:T(128)} %key_ref.3) | copy-start | bytes 52
  0.7 58.2 %copy-start.4 = (s32[2]{0:T(128)S(1)}, s32[2]{0:T(128)}, u32[]{:S(2)}) copy-start(s32[2]{0:T(128)} %dil_ref.3) | copy-start | bytes 28
  0.7 58.2 %copy-start.6 = (bf16[2,5,128,128]{3,2,1,0:T(8,128)(2,1)S(1)}, bf16[2,5,128,128]{3,2,1,0:T(8,128)(2,1)}, u32[]{:S(2)}) copy-start(bf16[2,5,128,128]{3,2,1,0:T(8,128)(2,1)} %tw_hbm.1) | copy-start | bytes 983044
  5.5 53.4 %all-to-all-start = ((bf16[32,2,120,128]{3,2,1,0:T(8,128)(2,1)}), bf16[32,2,120,128]{3,2,1,0:T(8,128)(2,1)S(1)}, u32[]{:S(2)}, u32[]{:S(2)}) async-start(bf16[32,2,120,128]{3,2,1,0:T(8,128)(2,1)} %shard_map.110), calls=%async_computation | async-start | bytes 3932160 | tf_op jit(solution)/shard_map/all_to_all | solution.py:451
  69.9 28.8 %all-to-all-start.1 = ((bf16[32,120,128]{2,1,0:T(8,128)(2,1)}), bf16[32,120,128]{2,1,0:T(8,128)(2,1)S(1)}, u32[]{:S(2)}, u32[]{:S(2)}) async-start(bf16[32,120,128]{2,1,0:T(8,128)(2,1)} %get-tuple-element.52), calls=%async_computation.1 | async-start | bytes 1966080 | tf_op jit(solution)/shard_map/all_to_all | solution.py:451
  74.7 27.6 %copy-start = (bf16[1,32,120,128]{3,2,1,0:T(8,128)(2,1)S(1)}, bf16[1,32,120,128]{3,2,1,0:T(8,128)(2,1)}, u32[]{:S(2)}) copy-start(bf16[1,32,120,128]{3,2,1,0:T(8,128)(2,1)} %param.7) | copy-start | bytes 2949124
  74.7 27.6 %copy-start.3 = (s32[2]{0:T(128)S(1)}, s32[2]{0:T(128)}, u32[]{:S(2)}) copy-start(s32[2]{0:T(128)} %pad_add_fusion.here_ref) | copy-start | bytes 28
  84.6 43.3 %copy-start.1 = (bf16[9,128,128]{2,1,0:T(8,128)(2,1)S(1)}, bf16[9,128,128]{2,1,0:T(8,128)(2,1)}, u32[]{:S(2)}) copy-start(bf16[9,128,128]{2,1,0:T(8,128)(2,1)} %w_ref.3) | copy-start | bytes 884740
  84.6 3.6 %collective-permute-start = (bf16[192,128]{1,0:T(8,128)(2,1)}, bf16[192,128]{1,0:T(8,128)(2,1)S(1)}, u32[]{:S(2)}, u32[]{:S(2)}) collective-permute-start(bf16[192,128]{1,0:T(8,128)(2,1)} %get-tuple-element.45), channel_id=1, source_target_pairs={{0,1},{1,0},{2,3},{3,2},{4,5},{5,4},{6,7},{7,6},{8,9},{9,8},{10,11... | collective-permute-start | bytes 147464 | tf_op jit(solution)/shard_map/ppermute | solution.py:456
  84.7 6.1 %collective-permute-start.1 = (bf16[192,128]{1,0:T(8,128)(2,1)}, bf16[192,128]{1,0:T(8,128)(2,1)S(1)}, u32[]{:S(2)}, u32[]{:S(2)}) collective-permute-start(bf16[192,128]{1,0:T(8,128)(2,1)} %get-tuple-element.46), channel_id=1, source_target_pairs={{0,2},{1,3},{2,0},{3,1},{4,6},{5,7},{6,4},{7,5},{8,10},{9,11},{10,... | collective-permute-start | bytes 147464 | tf_op jit(solution)/shard_map/ppermute | solution.py:456
  86.4 4.9 %collective-permute-start.2 = (bf16[192,128]{1,0:T(8,128)(2,1)}, bf16[192,128]{1,0:T(8,128)(2,1)S(1)}, u32[]{:S(2)}, u32[]{:S(2)}) collective-permute-start(bf16[192,128]{1,0:T(8,128)(2,1)} %get-tuple-element.47), channel_id=1, source_target_pairs={{0,3},{1,2},{2,1},{3,0},{4,7},{5,6},{6,5},{7,4},{8,11},{9,10},{10,... | collective-permute-start | bytes 147464 | tf_op jit(solution)/shard_map/ppermute | solution.py:456
  86.5 4.7 %collective-permute-start.3 = (bf16[192,128]{1,0:T(8,128)(2,1)}, bf16[192,128]{1,0:T(8,128)(2,1)S(1)}, u32[]{:S(2)}, u32[]{:S(2)}) collective-permute-start(bf16[192,128]{1,0:T(8,128)(2,1)} %get-tuple-element.48), channel_id=1, source_target_pairs={{0,4},{1,5},{2,6},{3,7},{4,0},{5,1},{6,2},{7,3},{8,12},{9,13},{10,... | collective-permute-start | bytes 147464 | tf_op jit(solution)/shard_map/ppermute | solution.py:456
  88.1 5.6 %collective-permute-start.4 = (bf16[192,128]{1,0:T(8,128)(2,1)}, bf16[192,128]{1,0:T(8,128)(2,1)S(1)}, u32[]{:S(2)}, u32[]{:S(2)}) collective-permute-start(bf16[192,128]{1,0:T(8,128)(2,1)} %get-tuple-element.49), channel_id=1, source_target_pairs={{0,5},{1,4},{2,7},{3,6},{4,1},{5,0},{6,3},{7,2},{8,13},{9,12},{10,... | collective-permute-start | bytes 147464 | tf_op jit(solution)/shard_map/ppermute | solution.py:456
  88.2 5.4 %collective-permute-start.5 = (bf16[192,128]{1,0:T(8,128)(2,1)}, bf16[192,128]{1,0:T(8,128)(2,1)S(1)}, u32[]{:S(2)}, u32[]{:S(2)}) collective-permute-start(bf16[192,128]{1,0:T(8,128)(2,1)} %get-tuple-element.50), channel_id=1, source_target_pairs={{0,6},{1,7},{2,4},{3,5},{4,2},{5,3},{6,0},{7,1},{8,14},{9,15},{10,... | collective-permute-start | bytes 147464 | tf_op jit(solution)/shard_map/ppermute | solution.py:456
  90.8 5.3 %collective-permute-start.6 = (bf16[192,128]{1,0:T(8,128)(2,1)}, bf16[192,128]{1,0:T(8,128)(2,1)S(1)}, u32[]{:S(2)}, u32[]{:S(2)}) collective-permute-start(bf16[192,128]{1,0:T(8,128)(2,1)} %get-tuple-element.51), channel_id=1, source_target_pairs={{0,7},{1,6},{2,5},{3,4},{4,3},{5,2},{6,1},{7,0},{8,15},{9,14},{10,... | collective-permute-start | bytes 147464 | tf_op jit(solution)/shard_map/ppermute | solution.py:456
  96.1 0.8 copy-start.2
  98.7 44.6 %all-to-all-start.2 = ((bf16[32,120,128]{2,1,0:T(8,128)(2,1)}), bf16[32,120,128]{2,1,0:T(8,128)(2,1)S(1)}, u32[]{:S(2)}, u32[]{:S(2)}) async-start(bf16[32,120,128]{2,1,0:T(8,128)(2,1)} %get-tuple-element.67), calls=%async_computation.2 | async-start | bytes 1966080 | tf_op jit(solution)/shard_map/all_to_all | solution.py:451
  106.0 5.0 %collective-permute-start.10 = (bf16[144,128]{1,0:T(8,128)(2,1)S(1)}, bf16[144,128]{1,0:T(8,128)(2,1)S(1)}, u32[]{:S(2)}, u32[]{:S(2)}) collective-permute-start(bf16[144,128]{1,0:T(8,128)(2,1)S(1)} %get-tuple-element.62), channel_id=1, source_target_pairs={{0,4},{1,5},{2,6},{3,7},{4,0},{5,1},{6,2},{7,3},{8,12},{9,13},{10,... | collective-permute-start | bytes 110600 | tf_op jit(solution)/shard_map/ppermute | solution.py:456
  107.9 7.2 %collective-permute-start.11 = (bf16[144,128]{1,0:T(8,128)(2,1)S(1)}, bf16[144,128]{1,0:T(8,128)(2,1)S(1)}, u32[]{:S(2)}, u32[]{:S(2)}) collective-permute-start(bf16[144,128]{1,0:T(8,128)(2,1)S(1)} %get-tuple-element.63), channel_id=1, source_target_pairs={{0,5},{1,4},{2,7},{3,6},{4,1},{5,0},{6,3},{7,2},{8,13},{9,12},{10,... | collective-permute-start | bytes 110600 | tf_op jit(solution)/shard_map/ppermute | solution.py:456
  107.9 9.3 %collective-permute-start.12 = (bf16[144,128]{1,0:T(8,128)(2,1)S(1)}, bf16[144,128]{1,0:T(8,128)(2,1)S(1)}, u32[]{:S(2)}, u32[]{:S(2)}) collective-permute-start(bf16[144,128]{1,0:T(8,128)(2,1)S(1)} %get-tuple-element.64), channel_id=1, source_target_pairs={{0,6},{1,7},{2,4},{3,5},{4,2},{5,3},{6,0},{7,1},{8,14},{9,15},{10,... | collective-permute-start | bytes 110600 | tf_op jit(solution)/shard_map/ppermute | solution.py:456
  110.3 6.9 %collective-permute-start.13 = (bf16[144,128]{1,0:T(8,128)(2,1)S(1)}, bf16[144,128]{1,0:T(8,128)(2,1)S(1)}, u32[]{:S(2)}, u32[]{:S(2)}) collective-permute-start(bf16[144,128]{1,0:T(8,128)(2,1)S(1)} %get-tuple-element.65), channel_id=1, source_target_pairs={{0,7},{1,6},{2,5},{3,4},{4,3},{5,2},{6,1},{7,0},{8,15},{9,14},{10,... | collective-permute-start | bytes 110600 | tf_op jit(solution)/shard_map/ppermute | solution.py:456
  110.6 6.6 %collective-permute-start.7 = (bf16[144,128]{1,0:T(8,128)(2,1)S(1)}, bf16[144,128]{1,0:T(8,128)(2,1)S(1)}, u32[]{:S(2)}, u32[]{:S(2)}) collective-permute-start(bf16[144,128]{1,0:T(8,128)(2,1)S(1)} %get-tuple-element.59), channel_id=1, source_target_pairs={{0,1},{1,0},{2,3},{3,2},{4,5},{5,4},{6,7},{7,6},{8,9},{9,8},{10,11... | collective-permute-start | bytes 110600 | tf_op jit(solution)/shard_map/ppermute | solution.py:456
  111.1 6.1 %collective-permute-start.8 = (bf16[144,128]{1,0:T(8,128)(2,1)S(1)}, bf16[144,128]{1,0:T(8,128)(2,1)S(1)}, u32[]{:S(2)}, u32[]{:S(2)}) collective-permute-start(bf16[144,128]{1,0:T(8,128)(2,1)S(1)} %get-tuple-element.60), channel_id=1, source_target_pairs={{0,2},{1,3},{2,0},{3,1},{4,6},{5,7},{6,4},{7,5},{8,10},{9,11},{10,... | collective-permute-start | bytes 110600 | tf_op jit(solution)/shard_map/ppermute | solution.py:456
  115.0 4.0 %collective-permute-start.9 = (bf16[144,128]{1,0:T(8,128)(2,1)S(1)}, bf16[144,128]{1,0:T(8,128)(2,1)S(1)}, u32[]{:S(2)}, u32[]{:S(2)}) collective-permute-start(bf16[144,128]{1,0:T(8,128)(2,1)S(1)} %get-tuple-element.61), channel_id=1, source_target_pairs={{0,3},{1,2},{2,1},{3,0},{4,7},{5,6},{6,5},{7,4},{8,11},{9,10},{10,... | collective-permute-start | bytes 110600 | tf_op jit(solution)/shard_map/ppermute | solution.py:456
  119.1 6.7 %collective-permute-start.14 = (bf16[336,128]{1,0:T(8,128)(2,1)S(1)}, bf16[336,128]{1,0:T(8,128)(2,1)S(1)}, u32[]{:S(2)}, u32[]{:S(2)}) collective-permute-start(bf16[336,128]{1,0:T(8,128)(2,1)S(1)} %shard_map.116.refs_0_), channel_id=1, source_target_pairs={{0,8},{8,0},{16,24},{24,16},{1,9},{9,1},{17,25},{25,17},{2,10},{10... | collective-permute-start | bytes 258056 | tf_op jit(solution)/shard_map/ppermute | solution.py:461
  125.8 6.4 %collective-permute-start.15 = (bf16[336,128]{1,0:T(8,128)(2,1)S(1)}, bf16[336,128]{1,0:T(8,128)(2,1)S(1)}, u32[]{:S(2)}, u32[]{:S(2)}) collective-permute-start(bf16[336,128]{1,0:T(8,128)(2,1)S(1)} %shard_map.117.refs_0_), channel_id=1, source_target_pairs={{0,16},{8,24},{16,0},{24,8},{1,17},{9,25},{17,1},{25,9},{2,18},{10... | collective-permute-start | bytes 258056 | tf_op jit(solution)/shard_map/ppermute | solution.py:461

commit v19 on v18

--- a/solution.py
+++ b/solution.py
@@ -635,7 +635,7 @@
     bits = [1 << n for n in range((segs - 1).bit_length())]
     for bit in bits:
         other = meet_in_seg(piece, bit)
-        if bit == bits[-1]:
+        if bit == bits[0]:
             other, back = lax.optimization_barrier((other, back))
         piece = sum_of([piece, other])
     *grads, united = call(

time: 146 us -> 146 us (level)
  transfers between devices with their start and end apart: 19 -> 19, of which waited for: 9 -> 10; matrix products, arithmetic and copies ran while one was open for 0% -> 0% of each run, Pallas kernels for 15% -> 15%
where the time goes in v19:
time: 146 us; the launch traced here: 145 us
  waiting for transfers between devices  58.3 us (40%)
  Pallas kernels  39.6 us (27%)
  starting transfers between devices  34.4 us (24%)
  blocking collectives  10.3 us (7%)
    all_to_all x3, waiting for transfers between devices, exchange(): return lax.all_to_all(blocks, AXES, split_axis=0, concat_axis=0, tiled=True)  43.3 us
    pallas_call x11, Pallas kernels, call(): pl.pallas_call(kernel, out_shape=[jax.ShapeDtypeStruct(shape, kind) for s...  39.6 us
    ppermute x14, starting transfers between devices, flip(): return lax.ppermute(value, 'grp', [(i, i ^ peer) for i in range(size)])  15.5 us
    all_to_all x3, starting transfers between devices, exchange(): return lax.all_to_all(blocks, AXES, split_axis=0, concat_axis=0, tiled=True)  15.3 us
    all_gather x1, blocking collectives, local(): lax.all_gather(piece, 'grp', axis=0)  10.3 us
    ppermute x14, waiting for transfers between devices, flip(): return lax.ppermute(value, 'grp', [(i, i ^ peer) for i in range(size)])  9.04 us
    ppermute x2, waiting for transfers between devices, meet_in_seg(): return lax.ppermute(value, 'seg', [(i, i ^ bit) for i in range(size)])  5.92 us
    ppermute x2, starting transfers between devices, meet_in_seg(): return lax.ppermute(value, 'seg', [(i, i ^ bit) for i in range(size)])  3.65 us
  transfers between devices with their start and end apart: 19, of which 10 were waited for; matrix products, arithmetic and copies ran while one was open for 0% of the time, Pallas kernels for 15%

profile of v19, /device:TPU:0, one launch (start us, length us, event | category | flops | bytes accessed | tf_op | source)
XLA Modules:
  0.0 145.0 jit_solution(6330089798411979280)
XLA Ops:
  0.6 0.0 copy-start.5
  0.7 0.0 copy-start.4
  0.7 4.8 %shard_map.110 = bf16[32,2,120,128]{3,2,1,0:T(8,128)(2,1)} custom-call(bf16[32,120,128]{2,1,0:T(8,128)(2,1)} %bitcast.10, bf16[9,128,128]{2,1,0:T(8,128)(2,1)} %w_ref.3, bf16[32,120,128]{2,1,0:T(8,128)(2,1)} %bitcast.14), custom_call_target="tpu_custom_call" | custom-call | flops 1132462080 | bytes 3932160 | tf_op jit(solution)/shard_map/pallas_call | solution.py:58
  5.5 7.5 %all-to-all-start = ((bf16[32,2,120,128]{3,2,1,0:T(8,128)(2,1)}), bf16[32,2,120,128]{3,2,1,0:T(8,128)(2,1)S(1)}, u32[]{:S(2)}, u32[]{:S(2)}) async-start(bf16[32,2,120,128]{3,2,1,0:T(8,128)(2,1)} %shard_map.110), calls=%async_computation | async-start | bytes 3932160 | tf_op jit(solution)/shard_map/all_to_all | solution.py:451
  13.0 4.4 %shard_map.111.slope_hbm = bf16[28,32,120,128]{3,2,1,0:T(8,128)(2,1)} custom-call(bf16[32,120,128]{2,1,0:T(8,128)(2,1)} %bitcast.11, bf16[9,128,128]{2,1,0:T(8,128)(2,1)} %w_ref.3), custom_call_target="tpu_custom_call" | custom-call | flops 1132462080 | bytes 1966080 | tf_op jit(solution)/shard_map/pallas_call | solution.py:58
  17.4 41.5 %all-to-all-done.got_ref = bf16[32,2,120,128]{3,2,1,0:T(8,128)(2,1)S(1)} async-done(((bf16[32,2,120,128]{3,2,1,0:T(8,128)(2,1)}), bf16[32,2,120,128]{3,2,1,0:T(8,128)(2,1)S(1)}, u32[]{:S(2)}, u32[]{:S(2)}) %all-to-all-start) | async-done | bytes 1966112 | tf_op jit(solution)/shard_map/all_to_all | solution.py:451
  58.9 11.0 %shard_map.112 = (bf16[32,120,128]{2,1,0:T(8,128)(2,1)}, bf16[28,32,128,128]{3,2,1,0:T(8,128)(2,1)}, bf16[28,32,120,128]{3,2,1,0:T(8,128)(2,1)}) custom-call(s32[2]{0:T(128)S(1)} %copy-done.4, s32[4]{0:T(128)S(1)} %copy-done.5, bf16[32,2,120,128]{3,2,1,0:T(8,128)(2,1)S(1)} %all-to-all-done.got_ref, bf16[2,5,128,128]{3,2,1,0:T(8,128)(2,1)S(1)} %copy-done.6, ...), custom_call_target="tpu_custom_call" | custom-call | flops 2768240640 | bytes 8847360 | tf_op jit(solution)/shard_map/pallas_call | solution.py:58
  69.9 4.2 %all-to-all-start.1 = ((bf16[32,120,128]{2,1,0:T(8,128)(2,1)}), bf16[32,120,128]{2,1,0:T(8,128)(2,1)S(1)}, u32[]{:S(2)}, u32[]{:S(2)}) async-start(bf16[32,120,128]{2,1,0:T(8,128)(2,1)} %get-tuple-element.52), calls=%async_computation.1 | async-start | bytes 1966080 | tf_op jit(solution)/shard_map/all_to_all | solution.py:451
  74.1 0.6 pad_add_fusion.here_ref
  74.8 9.8 %shard_map.113 = (bf16[32,120,128]{2,1,0:T(8,128)(2,1)}, bf16[192,128]{1,0:T(8,128)(2,1)}, bf16[192,128]{1,0:T(8,128)(2,1)}, bf16[192,128]{1,0:T(8,128)(2,1)}, b...) custom-call(s32[2]{0:T(128)} %pad_add_fusion.here_ref, ...), custom_call_target="tpu_custom_call" | custom-call | flops 1509949440 | bytes 6881280 | tf_op jit(solution)/shard_map/pallas_call | solution.py:58
  84.6 0.0 copy-start.1
  84.6 0.1 collective-permute-start
  84.7 1.7 %collective-permute-start.1 = (bf16[192,128]{1,0:T(8,128)(2,1)}, bf16[192,128]{1,0:T(8,128)(2,1)S(1)}, u32[]{:S(2)}, u32[]{:S(2)}) collective-permute-start(bf16[192,128]{1,0:T(8,128)(2,1)} %get-tuple-element.46), channel_id=1, source_target_pairs={{0,2},{1,3},{2,0},{3,1},{4,6},{5,7},{6,4},{7,5},{8,10},{9,11},{10,... | collective-permute-start | bytes 147464 | tf_op jit(solution)/shard_map/ppermute | solution.py:456
  86.4 0.2 collective-permute-start.2
  86.5 1.5 %collective-permute-start.3 = (bf16[192,128]{1,0:T(8,128)(2,1)}, bf16[192,128]{1,0:T(8,128)(2,1)S(1)}, u32[]{:S(2)}, u32[]{:S(2)}) collective-permute-start(bf16[192,128]{1,0:T(8,128)(2,1)} %get-tuple-element.48), channel_id=1, source_target_pairs={{0,4},{1,5},{2,6},{3,7},{4,0},{5,1},{6,2},{7,3},{8,12},{9,13},{10,... | collective-permute-start | bytes 147464 | tf_op jit(solution)/shard_map/ppermute | solution.py:456
  88.1 0.2 collective-permute-start.4
  88.2 0.0 collective-permute-done.refs_1_
  88.2 2.5 %collective-permute-start.5 = (bf16[192,128]{1,0:T(8,128)(2,1)}, bf16[192,128]{1,0:T(8,128)(2,1)S(1)}, u32[]{:S(2)}, u32[]{:S(2)}) collective-permute-start(bf16[192,128]{1,0:T(8,128)(2,1)} %get-tuple-element.50), channel_id=1, source_target_pairs={{0,6},{1,7},{2,4},{3,5},{4,2},{5,3},{6,0},{7,1},{8,14},{9,15},{10,... | collective-permute-start | bytes 147464 | tf_op jit(solution)/shard_map/ppermute | solution.py:456
  90.8 0.2 collective-permute-start.6
  90.9 0.3 collective-permute-done.2.refs_3_
  91.2 0.0 collective-permute-done.3.refs_4_
  91.2 2.4 %collective-permute-done.4.refs_5_ = bf16[192,128]{1,0:T(8,128)(2,1)S(1)} collective-permute-done((bf16[192,128]{1,0:T(8,128)(2,1)}, bf16[192,128]{1,0:T(8,128)(2,1)S(1)}, u32[]{:S(2)}, u32[]{:S(2)}) %collective-permute-start.4) | collective-permute-done | bytes 49184 | tf_op jit(solution)/shard_map/ppermute | solution.py:456
  93.6 0.0 collective-permute-done.5.refs_6_
  93.6 2.4 %collective-permute-done.6.refs_7_ = bf16[192,128]{1,0:T(8,128)(2,1)S(1)} collective-permute-done((bf16[192,128]{1,0:T(8,128)(2,1)}, bf16[192,128]{1,0:T(8,128)(2,1)S(1)}, u32[]{:S(2)}, u32[]{:S(2)}) %collective-permute-start.6) | collective-permute-done | bytes 49184 | tf_op jit(solution)/shard_map/ppermute | solution.py:456
  96.1 0.8 copy-done.2
  96.9 0.1 shard_map.114.first_ref
  96.9 1.8 %all-to-all-done.1.got_ref = bf16[32,120,128]{2,1,0:T(8,128)(2,1)S(1)} async-done(((bf16[32,120,128]{2,1,0:T(8,128)(2,1)}), bf16[32,120,128]{2,1,0:T(8,128)(2,1)S(1)}, u32[]{:S(2)}, u32[]{:S(2)}) %all-to-all-start.1) | async-done | bytes 983072 | tf_op jit(solution)/shard_map/all_to_all | solution.py:451
  98.7 3.6 %all-to-all-start.2 = ((bf16[32,120,128]{2,1,0:T(8,128)(2,1)}), bf16[32,120,128]{2,1,0:T(8,128)(2,1)S(1)}, u32[]{:S(2)}, u32[]{:S(2)}) async-start(bf16[32,120,128]{2,1,0:T(8,128)(2,1)} %get-tuple-element.67), calls=%async_computation.2 | async-start | bytes 1966080 | tf_op jit(solution)/shard_map/all_to_all | solution.py:451
  102.4 3.6 %shard_map.115 = (bf16[144,128]{1,0:T(8,128)(2,1)S(1)}, bf16[144,128]{1,0:T(8,128)(2,1)S(1)}, bf16[144,128]{1,0:T(8,128)(2,1)S(1)}, bf16[144,128]{1,0:T(8,128)(2...) custom-call(s32[2]{0:T(128)S(1)} %copy-done.3, ...), custom_call_target="tpu_custom_call" | custom-call | flops 1132462080 | bytes 3932160 | tf_op jit(solution)/shard_map/pallas_call | solution.py:58
  106.0 1.8 %collective-permute-start.10 = (bf16[144,128]{1,0:T(8,128)(2,1)S(1)}, bf16[144,128]{1,0:T(8,128)(2,1)S(1)}, u32[]{:S(2)}, u32[]{:S(2)}) collective-permute-start(bf16[144,128]{1,0:T(8,128)(2,1)S(1)} %get-tuple-element.62), channel_id=1, source_target_pairs={{0,4},{1,5},{2,6},{3,7},{4,0},{5,1},{6,2},{7,3},{8,12},{9,13},{10,... | collective-permute-start | bytes 110600 | tf_op jit(solution)/shard_map/ppermute | solution.py:456
  107.9 2.4 %collective-permute-start.12 = (bf16[144,128]{1,0:T(8,128)(2,1)S(1)}, bf16[144,128]{1,0:T(8,128)(2,1)S(1)}, u32[]{:S(2)}, u32[]{:S(2)}) collective-permute-start(bf16[144,128]{1,0:T(8,128)(2,1)S(1)} %get-tuple-element.64), channel_id=1, source_target_pairs={{0,6},{1,7},{2,4},{3,5},{4,2},{5,3},{6,0},{7,1},{8,14},{9,15},{10,... | collective-permute-start | bytes 110600 | tf_op jit(solution)/shard_map/ppermute | solution.py:456
  110.3 0.3 collective-permute-start.13
  110.6 0.4 collective-permute-start.7
  110.9 0.1 collective-permute-done.10.refs_4_
  111.1 2.1 %collective-permute-start.8 = (bf16[144,128]{1,0:T(8,128)(2,1)S(1)}, bf16[144,128]{1,0:T(8,128)(2,1)S(1)}, u32[]{:S(2)}, u32[]{:S(2)}) collective-permute-start(bf16[144,128]{1,0:T(8,128)(2,1)S(1)} %get-tuple-element.60), channel_id=1, source_target_pairs={{0,2},{1,3},{2,0},{3,1},{4,6},{5,7},{6,4},{7,5},{8,10},{9,11},{10,... | collective-permute-start | bytes 110600 | tf_op jit(solution)/shard_map/ppermute | solution.py:456
  113.2 1.9 %collective-permute-done.11.refs_5_ = bf16[144,128]{1,0:T(8,128)(2,1)S(1)} collective-permute-done((bf16[144,128]{1,0:T(8,128)(2,1)S(1)}, bf16[144,128]{1,0:T(8,128)(2,1)S(1)}, u32[]{:S(2)}, u32[]{:S(2)}) %collective-permute-start.11) | collective-permute-done | bytes 36896 | tf_op jit(solution)/shard_map/ppermute | solution.py:456
  115.0 2.1 %collective-permute-start.9 = (bf16[144,128]{1,0:T(8,128)(2,1)S(1)}, bf16[144,128]{1,0:T(8,128)(2,1)S(1)}, u32[]{:S(2)}, u32[]{:S(2)}) collective-permute-start(bf16[144,128]{1,0:T(8,128)(2,1)S(1)} %get-tuple-element.61), channel_id=1, source_target_pairs={{0,3},{1,2},{2,1},{3,0},{4,7},{5,6},{6,5},{7,4},{8,11},{9,10},{10,... | collective-permute-start | bytes 110600 | tf_op jit(solution)/shard_map/ppermute | solution.py:456
  117.2 0.0 collective-permute-done.12.refs_6_
  117.2 0.0 collective-permute-done.13.refs_7_
  117.2 1.9 %collective-permute-done.9.refs_3_ = bf16[144,128]{1,0:T(8,128)(2,1)S(1)} collective-permute-done((bf16[144,128]{1,0:T(8,128)(2,1)S(1)}, bf16[144,128]{1,0:T(8,128)(2,1)S(1)}, u32[]{:S(2)}, u32[]{:S(2)}) %collective-permute-start.9) | collective-permute-done | bytes 36896 | tf_op jit(solution)/shard_map/ppermute | solution.py:456
  119.1 0.1 shard_map.116.refs_0_
  119.1 0.6 collective-permute-start.14
  119.7 4.3 %shard_map.117 = bf16[32,120,128]{2,1,0:T(8,128)(2,1)} custom-call(bf16[9,128,128]{2,1,0:T(8,128)(2,1)S(1)} %copy-done.1, bf16[32,120,128]{2,1,0:T(8,128)(2,1)S(1)} %all-to-all-done.1.got_ref, bf16[28,32,120,128]{3,2,1,0:T(8,128)(2,1)} %shard_map.111.slope_hbm), custom_call_target="tpu_custom_call" | custom-call | flops 1132462080 | bytes 2949120 | tf_op jit(solution)/shard_map/pallas_call | solution.py:58
  124.1 1.8 %collective-permute-done.14.refs_1_ = bf16[336,128]{1,0:T(8,128)(2,1)S(1)} collective-permute-done((bf16[336,128]{1,0:T(8,128)(2,1)S(1)}, bf16[336,128]{1,0:T(8,128)(2,1)S(1)}, u32[]{:S(2)}, u32[]{:S(2)}) %collective-permute-start.14) | collective-permute-done | bytes 86048 | tf_op jit(solution)/shard_map/ppermute | solution.py:461
  125.8 3.1 %collective-permute-start.15 = (bf16[336,128]{1,0:T(8,128)(2,1)S(1)}, bf16[336,128]{1,0:T(8,128)(2,1)S(1)}, u32[]{:S(2)}, u32[]{:S(2)}) collective-permute-start(bf16[336,128]{1,0:T(8,128)(2,1)S(1)} %shard_map.118.refs_0_), channel_id=1, source_target_pairs={{0,16},{8,24},{16,0},{24,8},{1,17},{9,25},{17,1},{25,9},{2,18},{10... | collective-permute-start | bytes 258056 | tf_op jit(solution)/shard_map/ppermute | solution.py:461
  128.9 4.2 %collective-permute-done.15.refs_1_ = bf16[336,128]{1,0:T(8,128)(2,1)S(1)} collective-permute-done((bf16[336,128]{1,0:T(8,128)(2,1)S(1)}, bf16[336,128]{1,0:T(8,128)(2,1)S(1)}, u32[]{:S(2)}, u32[]{:S(2)}) %collective-permute-start.15) | collective-permute-done | bytes 86048 | tf_op jit(solution)/shard_map/ppermute | solution.py:461
  133.1 10.3 %all-gather = bf16[2688,128]{1,0:T(8,128)(2,1)S(1)} all-gather(bf16[336,128]{1,0:T(8,128)(2,1)S(1)} %shard_map.119), channel_id=2, replica_groups=mesh['seg'=4,'grp'=8] {'grp'}, dimensions={0}, use_global_device_ids=true | all-gather | bytes 774144 | tf_op jit(solution)/shard_map/all_gather | solution.py:649
  143.4 1.4 shard_map.120
  (19 shorter events, 0.1 us)
Async XLA Ops:
  0.6 58.2 %copy-start.7 = (bf16[2,128,128]{2,1,0:T(8,128)(2,1)S(1)}, bf16[2,128,128]{2,1,0:T(8,128)(2,1)}, u32[]{:S(2)}) copy-start(bf16[2,128,128]{2,1,0:T(8,128)(2,1)} %uw_hbm.1) | copy-start | bytes 196612
  0.6 58.2 %copy-start.5 = (s32[4]{0:T(128)S(1)}, s32[4]{0:T(128)}, u32[]{:S(2)}) copy-start(s32[4]{0:T(128)} %key_ref.3) | copy-start | bytes 52
  0.7 58.2 %copy-start.4 = (s32[2]{0:T(128)S(1)}, s32[2]{0:T(128)}, u32[]{:S(2)}) copy-start(s32[2]{0:T(128)} %dil_ref.3) | copy-start | bytes 28
  0.7 58.2 %copy-start.6 = (bf16[2,5,128,128]{3,2,1,0:T(8,128)(2,1)S(1)}, bf16[2,5,128,128]{3,2,1,0:T(8,128)(2,1)}, u32[]{:S(2)}) copy-start(bf16[2,5,128,128]{3,2,1,0:T(8,128)(2,1)} %tw_hbm.1) | copy-start | bytes 983044
  5.5 53.4 %all-to-all-start = ((bf16[32,2,120,128]{3,2,1,0:T(8,128)(2,1)}), bf16[32,2,120,128]{3,2,1,0:T(8,128)(2,1)S(1)}, u32[]{:S(2)}, u32[]{:S(2)}) async-start(bf16[32,2,120,128]{3,2,1,0:T(8,128)(2,1)} %shard_map.110), calls=%async_computation | async-start | bytes 3932160 | tf_op jit(solution)/shard_map/all_to_all | solution.py:451
  69.9 28.8 %all-to-all-start.1 = ((bf16[32,120,128]{2,1,0:T(8,128)(2,1)}), bf16[32,120,128]{2,1,0:T(8,128)(2,1)S(1)}, u32[]{:S(2)}, u32[]{:S(2)}) async-start(bf16[32,120,128]{2,1,0:T(8,128)(2,1)} %get-tuple-element.52), calls=%async_computation.1 | async-start | bytes 1966080 | tf_op jit(solution)/shard_map/all_to_all | solution.py:451
  74.7 27.6 %copy-start = (bf16[1,32,120,128]{3,2,1,0:T(8,128)(2,1)S(1)}, bf16[1,32,120,128]{3,2,1,0:T(8,128)(2,1)}, u32[]{:S(2)}) copy-start(bf16[1,32,120,128]{3,2,1,0:T(8,128)(2,1)} %param.7) | copy-start | bytes 2949124
  74.7 27.6 %copy-start.3 = (s32[2]{0:T(128)S(1)}, s32[2]{0:T(128)}, u32[]{:S(2)}) copy-start(s32[2]{0:T(128)} %pad_add_fusion.here_ref) | copy-start | bytes 28
  84.6 35.1 %copy-start.1 = (bf16[9,128,128]{2,1,0:T(8,128)(2,1)S(1)}, bf16[9,128,128]{2,1,0:T(8,128)(2,1)}, u32[]{:S(2)}) copy-start(bf16[9,128,128]{2,1,0:T(8,128)(2,1)} %w_ref.3) | copy-start | bytes 884740
  84.6 3.6 %collective-permute-start = (bf16[192,128]{1,0:T(8,128)(2,1)}, bf16[192,128]{1,0:T(8,128)(2,1)S(1)}, u32[]{:S(2)}, u32[]{:S(2)}) collective-permute-start(bf16[192,128]{1,0:T(8,128)(2,1)} %get-tuple-element.45), channel_id=1, source_target_pairs={{0,1},{1,0},{2,3},{3,2},{4,5},{5,4},{6,7},{7,6},{8,9},{9,8},{10,11... | collective-permute-start | bytes 147464 | tf_op jit(solution)/shard_map/ppermute | solution.py:456
  84.7 6.1 %collective-permute-start.1 = (bf16[192,128]{1,0:T(8,128)(2,1)}, bf16[192,128]{1,0:T(8,128)(2,1)S(1)}, u32[]{:S(2)}, u32[]{:S(2)}) collective-permute-start(bf16[192,128]{1,0:T(8,128)(2,1)} %get-tuple-element.46), channel_id=1, source_target_pairs={{0,2},{1,3},{2,0},{3,1},{4,6},{5,7},{6,4},{7,5},{8,10},{9,11},{10,... | collective-permute-start | bytes 147464 | tf_op jit(solution)/shard_map/ppermute | solution.py:456
  86.4 4.9 %collective-permute-start.2 = (bf16[192,128]{1,0:T(8,128)(2,1)}, bf16[192,128]{1,0:T(8,128)(2,1)S(1)}, u32[]{:S(2)}, u32[]{:S(2)}) collective-permute-start(bf16[192,128]{1,0:T(8,128)(2,1)} %get-tuple-element.47), channel_id=1, source_target_pairs={{0,3},{1,2},{2,1},{3,0},{4,7},{5,6},{6,5},{7,4},{8,11},{9,10},{10,... | collective-permute-start | bytes 147464 | tf_op jit(solution)/shard_map/ppermute | solution.py:456
  86.5 4.7 %collective-permute-start.3 = (bf16[192,128]{1,0:T(8,128)(2,1)}, bf16[192,128]{1,0:T(8,128)(2,1)S(1)}, u32[]{:S(2)}, u32[]{:S(2)}) collective-permute-start(bf16[192,128]{1,0:T(8,128)(2,1)} %get-tuple-element.48), channel_id=1, source_target_pairs={{0,4},{1,5},{2,6},{3,7},{4,0},{5,1},{6,2},{7,3},{8,12},{9,13},{10,... | collective-permute-start | bytes 147464 | tf_op jit(solution)/shard_map/ppermute | solution.py:456
  88.1 5.6 %collective-permute-start.4 = (bf16[192,128]{1,0:T(8,128)(2,1)}, bf16[192,128]{1,0:T(8,128)(2,1)S(1)}, u32[]{:S(2)}, u32[]{:S(2)}) collective-permute-start(bf16[192,128]{1,0:T(8,128)(2,1)} %get-tuple-element.49), channel_id=1, source_target_pairs={{0,5},{1,4},{2,7},{3,6},{4,1},{5,0},{6,3},{7,2},{8,13},{9,12},{10,... | collective-permute-start | bytes 147464 | tf_op jit(solution)/shard_map/ppermute | solution.py:456
  88.2 5.4 %collective-permute-start.5 = (bf16[192,128]{1,0:T(8,128)(2,1)}, bf16[192,128]{1,0:T(8,128)(2,1)S(1)}, u32[]{:S(2)}, u32[]{:S(2)}) collective-permute-start(bf16[192,128]{1,0:T(8,128)(2,1)} %get-tuple-element.50), channel_id=1, source_target_pairs={{0,6},{1,7},{2,4},{3,5},{4,2},{5,3},{6,0},{7,1},{8,14},{9,15},{10,... | collective-permute-start | bytes 147464 | tf_op jit(solution)/shard_map/ppermute | solution.py:456
  90.8 5.3 %collective-permute-start.6 = (bf16[192,128]{1,0:T(8,128)(2,1)}, bf16[192,128]{1,0:T(8,128)(2,1)S(1)}, u32[]{:S(2)}, u32[]{:S(2)}) collective-permute-start(bf16[192,128]{1,0:T(8,128)(2,1)} %get-tuple-element.51), channel_id=1, source_target_pairs={{0,7},{1,6},{2,5},{3,4},{4,3},{5,2},{6,1},{7,0},{8,15},{9,14},{10,... | collective-permute-start | bytes 147464 | tf_op jit(solution)/shard_map/ppermute | solution.py:456
  96.1 0.8 copy-start.2
  98.7 44.6 %all-to-all-start.2 = ((bf16[32,120,128]{2,1,0:T(8,128)(2,1)}), bf16[32,120,128]{2,1,0:T(8,128)(2,1)S(1)}, u32[]{:S(2)}, u32[]{:S(2)}) async-start(bf16[32,120,128]{2,1,0:T(8,128)(2,1)} %get-tuple-element.67), calls=%async_computation.2 | async-start | bytes 1966080 | tf_op jit(solution)/shard_map/all_to_all | solution.py:451
  106.0 5.0 %collective-permute-start.10 = (bf16[144,128]{1,0:T(8,128)(2,1)S(1)}, bf16[144,128]{1,0:T(8,128)(2,1)S(1)}, u32[]{:S(2)}, u32[]{:S(2)}) collective-permute-start(bf16[144,128]{1,0:T(8,128)(2,1)S(1)} %get-tuple-element.62), channel_id=1, source_target_pairs={{0,4},{1,5},{2,6},{3,7},{4,0},{5,1},{6,2},{7,3},{8,12},{9,13},{10,... | collective-permute-start | bytes 110600 | tf_op jit(solution)/shard_map/ppermute | solution.py:456
  107.9 7.2 %collective-permute-start.11 = (bf16[144,128]{1,0:T(8,128)(2,1)S(1)}, bf16[144,128]{1,0:T(8,128)(2,1)S(1)}, u32[]{:S(2)}, u32[]{:S(2)}) collective-permute-start(bf16[144,128]{1,0:T(8,128)(2,1)S(1)} %get-tuple-element.63), channel_id=1, source_target_pairs={{0,5},{1,4},{2,7},{3,6},{4,1},{5,0},{6,3},{7,2},{8,13},{9,12},{10,... | collective-permute-start | bytes 110600 | tf_op jit(solution)/shard_map/ppermute | solution.py:456
  107.9 9.3 %collective-permute-start.12 = (bf16[144,128]{1,0:T(8,128)(2,1)S(1)}, bf16[144,128]{1,0:T(8,128)(2,1)S(1)}, u32[]{:S(2)}, u32[]{:S(2)}) collective-permute-start(bf16[144,128]{1,0:T(8,128)(2,1)S(1)} %get-tuple-element.64), channel_id=1, source_target_pairs={{0,6},{1,7},{2,4},{3,5},{4,2},{5,3},{6,0},{7,1},{8,14},{9,15},{10,... | collective-permute-start | bytes 110600 | tf_op jit(solution)/shard_map/ppermute | solution.py:456
  110.3 6.9 %collective-permute-start.13 = (bf16[144,128]{1,0:T(8,128)(2,1)S(1)}, bf16[144,128]{1,0:T(8,128)(2,1)S(1)}, u32[]{:S(2)}, u32[]{:S(2)}) collective-permute-start(bf16[144,128]{1,0:T(8,128)(2,1)S(1)} %get-tuple-element.65), channel_id=1, source_target_pairs={{0,7},{1,6},{2,5},{3,4},{4,3},{5,2},{6,1},{7,0},{8,15},{9,14},{10,... | collective-permute-start | bytes 110600 | tf_op jit(solution)/shard_map/ppermute | solution.py:456
  110.6 6.6 %collective-permute-start.7 = (bf16[144,128]{1,0:T(8,128)(2,1)S(1)}, bf16[144,128]{1,0:T(8,128)(2,1)S(1)}, u32[]{:S(2)}, u32[]{:S(2)}) collective-permute-start(bf16[144,128]{1,0:T(8,128)(2,1)S(1)} %get-tuple-element.59), channel_id=1, source_target_pairs={{0,1},{1,0},{2,3},{3,2},{4,5},{5,4},{6,7},{7,6},{8,9},{9,8},{10,11... | collective-permute-start | bytes 110600 | tf_op jit(solution)/shard_map/ppermute | solution.py:456
  111.1 6.1 %collective-permute-start.8 = (bf16[144,128]{1,0:T(8,128)(2,1)S(1)}, bf16[144,128]{1,0:T(8,128)(2,1)S(1)}, u32[]{:S(2)}, u32[]{:S(2)}) collective-permute-start(bf16[144,128]{1,0:T(8,128)(2,1)S(1)} %get-tuple-element.60), channel_id=1, source_target_pairs={{0,2},{1,3},{2,0},{3,1},{4,6},{5,7},{6,4},{7,5},{8,10},{9,11},{10,... | collective-permute-start | bytes 110600 | tf_op jit(solution)/shard_map/ppermute | solution.py:456
  115.0 4.0 %collective-permute-start.9 = (bf16[144,128]{1,0:T(8,128)(2,1)S(1)}, bf16[144,128]{1,0:T(8,128)(2,1)S(1)}, u32[]{:S(2)}, u32[]{:S(2)}) collective-permute-start(bf16[144,128]{1,0:T(8,128)(2,1)S(1)} %get-tuple-element.61), channel_id=1, source_target_pairs={{0,3},{1,2},{2,1},{3,0},{4,7},{5,6},{6,5},{7,4},{8,11},{9,10},{10,... | collective-permute-start | bytes 110600 | tf_op jit(solution)/shard_map/ppermute | solution.py:456
  119.1 6.7 %collective-permute-start.14 = (bf16[336,128]{1,0:T(8,128)(2,1)S(1)}, bf16[336,128]{1,0:T(8,128)(2,1)S(1)}, u32[]{:S(2)}, u32[]{:S(2)}) collective-permute-start(bf16[336,128]{1,0:T(8,128)(2,1)S(1)} %shard_map.116.refs_0_), channel_id=1, source_target_pairs={{0,8},{8,0},{16,24},{24,16},{1,9},{9,1},{17,25},{25,17},{2,10},{10... | collective-permute-start | bytes 258056 | tf_op jit(solution)/shard_map/ppermute | solution.py:461
  125.8 7.2 %collective-permute-start.15 = (bf16[336,128]{1,0:T(8,128)(2,1)S(1)}, bf16[336,128]{1,0:T(8,128)(2,1)S(1)}, u32[]{:S(2)}, u32[]{:S(2)}) collective-permute-start(bf16[336,128]{1,0:T(8,128)(2,1)S(1)} %shard_map.118.refs_0_), channel_id=1, source_target_pairs={{0,16},{8,24},{16,0},{24,8},{1,17},{9,25},{17,1},{25,9},{2,18},{10... | collective-permute-start | bytes 258056 | tf_op jit(solution)/shard_map/ppermute | solution.py:461

commit v20 on v18

--- a/solution.py
+++ b/solution.py
@@ -264,11 +264,13 @@
     ]
     for load in loads:
         load.start()
+    parts = out_sems.shape[0]
+    many = frames // parts
     stores = [
         pltpu.make_async_copy(
-            grad_ref.at[pl.ds(at, step_frames)], grad_hbm.at[pl.ds(at, step_frames)], out_sems.at[n]
-        )
-        for n, at in enumerate(range(0, frames, step_frames))
+            grad_ref.at[pl.ds(n * many, many)], grad_hbm.at[pl.ds(n * many, many)], out_sems.at[n]
+        )
+        for n in range(parts)
     ]
     segs = key_ref.shape[0]
     seg_frames = frames // segs
@@ -341,7 +343,7 @@
         weight = jnp.concatenate(
             [tw_ref[layer, k].astype(F32).T.astype(BF16) for k in range(TAPS)], axis=0
         )
-        for n, at in enumerate(range(0, frames, step_frames)):
+        for at in range(0, frames, step_frames):
             grad = mm(taps_of(source, at, step_frames, step_size, -1), weight).reshape(
                 step_frames, high, ch
             )
@@ -351,7 +353,8 @@
                 ).astype(BF16)
             else:
                 grad_ref[at : at + step_frames] = grad.astype(BF16)[:, :block]
-                stores[n].start()
+                if (at + step_frames) % many == 0:
+                    stores[at // many].start()
     for copy in copies + stores:
         copy.wait()
 
@@ -494,6 +497,7 @@
         max(n for n in range(1, frames + 1) if frames % n == 0 and n * high <= most)
         for most in (512, 256)
     )
+    grad_parts = 4 if frames % (4 * narrow_step) == 0 else frames // narrow_step
     scale = float((frames * pixels) ** -0.5)
     here = jnp.stack([lax.axis_index("seg"), lax.axis_index("grp")]).astype(jnp.int32)
     space_rows, time_rows, unite_rows = (n * ch // peers for n in (9, LAYERS * TAPS, 2))
@@ -556,7 +560,7 @@
             pltpu.VMEM(uniting_weight.shape, BF16),
             pltpu.SemaphoreType.DMA((7,)),
             pltpu.SemaphoreType.DMA((2,)),
-            pltpu.SemaphoreType.DMA((frames // narrow_step,)),
+            pltpu.SemaphoreType.DMA((grad_parts,)),
         ],
         2 * 22 * frames * block * ch * ch,
         frames * block * ch * 18,

time: 146 us -> 145 us (level)
  no operation moved by 1% of the time
where the time goes in v20:
time: 145 us
  waiting for transfers between devices  58.5 us (40%)
  Pallas kernels  39.4 us (27%)
  starting transfers between devices  33.4 us (23%)
  blocking collectives  11.1 us (8%)
    all_to_all x3, waiting for transfers between devices, exchange(): return lax.all_to_all(blocks, AXES, split_axis=0, concat_axis=0, tiled=True)  43.3 us
    pallas_call x11, Pallas kernels, call(): pl.pallas_call(kernel, out_shape=[jax.ShapeDtypeStruct(shape, kind) for s...  39.4 us
    ppermute x14, starting transfers between devices, flip(): return lax.ppermute(value, 'grp', [(i, i ^ peer) for i in range(size)])  15.5 us
    all_to_all x3, starting transfers between devices, exchange(): return lax.all_to_all(blocks, AXES, split_axis=0, concat_axis=0, tiled=True)  15.3 us
    all_gather x1, blocking collectives, local(): lax.all_gather(piece, 'grp', axis=0)  11.1 us
    ppermute x14, waiting for transfers between devices, flip(): return lax.ppermute(value, 'grp', [(i, i ^ peer) for i in range(size)])  9.03 us
    ppermute x2, waiting for transfers between devices, meet_in_seg(): return lax.ppermute(value, 'seg', [(i, i ^ bit) for i in range(size)])  6.11 us
  transfers between devices with their start and end apart: 19, of which 9 were waited for; matrix products, arithmetic and copies ran while one was open for 0% of the time, Pallas kernels for 15%

profile of v20, /device:TPU:0, one launch (start us, length us, event | category | flops | bytes accessed | tf_op | source)
XLA Modules:
  0.0 144.7 jit_solution(18105943639325156951)
XLA Ops:
  0.6 0.0 copy-start.5
  0.7 0.0 copy-start.4
  0.7 4.8 %shard_map.110 = bf16[32,2,120,128]{3,2,1,0:T(8,128)(2,1)} custom-call(bf16[32,120,128]{2,1,0:T(8,128)(2,1)} %bitcast.10, bf16[9,128,128]{2,1,0:T(8,128)(2,1)} %w_ref.3, bf16[32,120,128]{2,1,0:T(8,128)(2,1)} %bitcast.14), custom_call_target="tpu_custom_call" | custom-call | flops 1132462080 | bytes 3932160 | tf_op jit(solution)/shard_map/pallas_call | solution.py:58
  5.5 7.5 %all-to-all-start = ((bf16[32,2,120,128]{3,2,1,0:T(8,128)(2,1)}), bf16[32,2,120,128]{3,2,1,0:T(8,128)(2,1)S(1)}, u32[]{:S(2)}, u32[]{:S(2)}) async-start(bf16[32,2,120,128]{3,2,1,0:T(8,128)(2,1)} %shard_map.110), calls=%async_computation | async-start | bytes 3932160 | tf_op jit(solution)/shard_map/all_to_all | solution.py:454
  13.0 4.4 %shard_map.111.slope_hbm = bf16[28,32,120,128]{3,2,1,0:T(8,128)(2,1)} custom-call(bf16[32,120,128]{2,1,0:T(8,128)(2,1)} %bitcast.11, bf16[9,128,128]{2,1,0:T(8,128)(2,1)} %w_ref.3), custom_call_target="tpu_custom_call" | custom-call | flops 1132462080 | bytes 1966080 | tf_op jit(solution)/shard_map/pallas_call | solution.py:58
  17.4 41.5 %all-to-all-done.got_ref = bf16[32,2,120,128]{3,2,1,0:T(8,128)(2,1)S(1)} async-done(((bf16[32,2,120,128]{3,2,1,0:T(8,128)(2,1)}), bf16[32,2,120,128]{3,2,1,0:T(8,128)(2,1)S(1)}, u32[]{:S(2)}, u32[]{:S(2)}) %all-to-all-start) | async-done | bytes 1966112 | tf_op jit(solution)/shard_map/all_to_all | solution.py:454
  58.9 10.8 %shard_map.112 = (bf16[32,120,128]{2,1,0:T(8,128)(2,1)}, bf16[28,32,128,128]{3,2,1,0:T(8,128)(2,1)}, bf16[28,32,120,128]{3,2,1,0:T(8,128)(2,1)}) custom-call(s32[2]{0:T(128)S(1)} %copy-done.4, s32[4]{0:T(128)S(1)} %copy-done.5, bf16[32,2,120,128]{3,2,1,0:T(8,128)(2,1)S(1)} %all-to-all-done.got_ref, bf16[2,5,128,128]{3,2,1,0:T(8,128)(2,1)S(1)} %copy-done.6, ...), custom_call_target="tpu_custom_call" | custom-call | flops 2768240640 | bytes 8847360 | tf_op jit(solution)/shard_map/pallas_call | solution.py:58
  69.7 4.2 %all-to-all-start.1 = ((bf16[32,120,128]{2,1,0:T(8,128)(2,1)}), bf16[32,120,128]{2,1,0:T(8,128)(2,1)S(1)}, u32[]{:S(2)}, u32[]{:S(2)}) async-start(bf16[32,120,128]{2,1,0:T(8,128)(2,1)} %get-tuple-element.52), calls=%async_computation.1 | async-start | bytes 1966080 | tf_op jit(solution)/shard_map/all_to_all | solution.py:454
  73.9 0.6 pad_add_fusion.here_ref
  74.5 9.8 %shard_map.113 = (bf16[32,120,128]{2,1,0:T(8,128)(2,1)}, bf16[192,128]{1,0:T(8,128)(2,1)}, bf16[192,128]{1,0:T(8,128)(2,1)}, bf16[192,128]{1,0:T(8,128)(2,1)}, b...) custom-call(s32[2]{0:T(128)} %pad_add_fusion.here_ref, ...), custom_call_target="tpu_custom_call" | custom-call | flops 1509949440 | bytes 6881280 | tf_op jit(solution)/shard_map/pallas_call | solution.py:58
  84.3 0.0 copy-start.1
  84.3 0.1 collective-permute-start
  84.4 1.7 %collective-permute-start.1 = (bf16[192,128]{1,0:T(8,128)(2,1)}, bf16[192,128]{1,0:T(8,128)(2,1)S(1)}, u32[]{:S(2)}, u32[]{:S(2)}) collective-permute-start(bf16[192,128]{1,0:T(8,128)(2,1)} %get-tuple-element.46), channel_id=1, source_target_pairs={{0,2},{1,3},{2,0},{3,1},{4,6},{5,7},{6,4},{7,5},{8,10},{9,11},{10,... | collective-permute-start | bytes 147464 | tf_op jit(solution)/shard_map/ppermute | solution.py:459
  86.1 0.2 collective-permute-start.2
  86.3 1.5 %collective-permute-start.3 = (bf16[192,128]{1,0:T(8,128)(2,1)}, bf16[192,128]{1,0:T(8,128)(2,1)S(1)}, u32[]{:S(2)}, u32[]{:S(2)}) collective-permute-start(bf16[192,128]{1,0:T(8,128)(2,1)} %get-tuple-element.48), channel_id=1, source_target_pairs={{0,4},{1,5},{2,6},{3,7},{4,0},{5,1},{6,2},{7,3},{8,12},{9,13},{10,... | collective-permute-start | bytes 147464 | tf_op jit(solution)/shard_map/ppermute | solution.py:459
  87.8 0.2 collective-permute-start.4
  88.0 2.5 %collective-permute-start.5 = (bf16[192,128]{1,0:T(8,128)(2,1)}, bf16[192,128]{1,0:T(8,128)(2,1)S(1)}, u32[]{:S(2)}, u32[]{:S(2)}) collective-permute-start(bf16[192,128]{1,0:T(8,128)(2,1)} %get-tuple-element.50), channel_id=1, source_target_pairs={{0,6},{1,7},{2,4},{3,5},{4,2},{5,3},{6,0},{7,1},{8,14},{9,15},{10,... | collective-permute-start | bytes 147464 | tf_op jit(solution)/shard_map/ppermute | solution.py:459
  90.5 0.2 collective-permute-start.6
  90.7 0.3 collective-permute-done.2.refs_3_
  91.0 2.4 %collective-permute-done.4.refs_5_ = bf16[192,128]{1,0:T(8,128)(2,1)S(1)} collective-permute-done((bf16[192,128]{1,0:T(8,128)(2,1)}, bf16[192,128]{1,0:T(8,128)(2,1)S(1)}, u32[]{:S(2)}, u32[]{:S(2)}) %collective-permute-start.4) | collective-permute-done | bytes 49184 | tf_op jit(solution)/shard_map/ppermute | solution.py:459
  93.4 0.0 collective-permute-done.5.refs_6_
  93.4 2.4 %collective-permute-done.6.refs_7_ = bf16[192,128]{1,0:T(8,128)(2,1)S(1)} collective-permute-done((bf16[192,128]{1,0:T(8,128)(2,1)}, bf16[192,128]{1,0:T(8,128)(2,1)S(1)}, u32[]{:S(2)}, u32[]{:S(2)}) %collective-permute-start.6) | collective-permute-done | bytes 49184 | tf_op jit(solution)/shard_map/ppermute | solution.py:459
  95.8 0.8 copy-done.2
  96.6 0.1 shard_map.114.first_ref
  96.7 1.8 %all-to-all-done.1.got_ref = bf16[32,120,128]{2,1,0:T(8,128)(2,1)S(1)} async-done(((bf16[32,120,128]{2,1,0:T(8,128)(2,1)}), bf16[32,120,128]{2,1,0:T(8,128)(2,1)S(1)}, u32[]{:S(2)}, u32[]{:S(2)}) %all-to-all-start.1) | async-done | bytes 983072 | tf_op jit(solution)/shard_map/all_to_all | solution.py:454
  98.5 3.6 %all-to-all-start.2 = ((bf16[32,120,128]{2,1,0:T(8,128)(2,1)}), bf16[32,120,128]{2,1,0:T(8,128)(2,1)S(1)}, u32[]{:S(2)}, u32[]{:S(2)}) async-start(bf16[32,120,128]{2,1,0:T(8,128)(2,1)} %get-tuple-element.67), calls=%async_computation.2 | async-start | bytes 1966080 | tf_op jit(solution)/shard_map/all_to_all | solution.py:454
  102.2 3.6 %shard_map.115 = (bf16[144,128]{1,0:T(8,128)(2,1)S(1)}, bf16[144,128]{1,0:T(8,128)(2,1)S(1)}, bf16[144,128]{1,0:T(8,128)(2,1)S(1)}, bf16[144,128]{1,0:T(8,128)(2...) custom-call(s32[2]{0:T(128)S(1)} %copy-done.3, ...), custom_call_target="tpu_custom_call" | custom-call | flops 1132462080 | bytes 3932160 | tf_op jit(solution)/shard_map/pallas_call | solution.py:58
  105.8 1.8 %collective-permute-start.10 = (bf16[144,128]{1,0:T(8,128)(2,1)S(1)}, bf16[144,128]{1,0:T(8,128)(2,1)S(1)}, u32[]{:S(2)}, u32[]{:S(2)}) collective-permute-start(bf16[144,128]{1,0:T(8,128)(2,1)S(1)} %get-tuple-element.62), channel_id=1, source_target_pairs={{0,4},{1,5},{2,6},{3,7},{4,0},{5,1},{6,2},{7,3},{8,12},{9,13},{10,... | collective-permute-start | bytes 110600 | tf_op jit(solution)/shard_map/ppermute | solution.py:459
  107.6 2.4 %collective-permute-start.12 = (bf16[144,128]{1,0:T(8,128)(2,1)S(1)}, bf16[144,128]{1,0:T(8,128)(2,1)S(1)}, u32[]{:S(2)}, u32[]{:S(2)}) collective-permute-start(bf16[144,128]{1,0:T(8,128)(2,1)S(1)} %get-tuple-element.64), channel_id=1, source_target_pairs={{0,6},{1,7},{2,4},{3,5},{4,2},{5,3},{6,0},{7,1},{8,14},{9,15},{10,... | collective-permute-start | bytes 110600 | tf_op jit(solution)/shard_map/ppermute | solution.py:459
  110.0 0.3 collective-permute-start.13
  110.3 0.4 collective-permute-start.7
  110.7 0.1 collective-permute-done.10.refs_4_
  110.8 2.1 %collective-permute-start.8 = (bf16[144,128]{1,0:T(8,128)(2,1)S(1)}, bf16[144,128]{1,0:T(8,128)(2,1)S(1)}, u32[]{:S(2)}, u32[]{:S(2)}) collective-permute-start(bf16[144,128]{1,0:T(8,128)(2,1)S(1)} %get-tuple-element.60), channel_id=1, source_target_pairs={{0,2},{1,3},{2,0},{3,1},{4,6},{5,7},{6,4},{7,5},{8,10},{9,11},{10,... | collective-permute-start | bytes 110600 | tf_op jit(solution)/shard_map/ppermute | solution.py:459
  113.0 1.9 %collective-permute-done.11.refs_5_ = bf16[144,128]{1,0:T(8,128)(2,1)S(1)} collective-permute-done((bf16[144,128]{1,0:T(8,128)(2,1)S(1)}, bf16[144,128]{1,0:T(8,128)(2,1)S(1)}, u32[]{:S(2)}, u32[]{:S(2)}) %collective-permute-start.11) | collective-permute-done | bytes 36896 | tf_op jit(solution)/shard_map/ppermute | solution.py:459
  114.8 2.1 %collective-permute-start.9 = (bf16[144,128]{1,0:T(8,128)(2,1)S(1)}, bf16[144,128]{1,0:T(8,128)(2,1)S(1)}, u32[]{:S(2)}, u32[]{:S(2)}) collective-permute-start(bf16[144,128]{1,0:T(8,128)(2,1)S(1)} %get-tuple-element.61), channel_id=1, source_target_pairs={{0,3},{1,2},{2,1},{3,0},{4,7},{5,6},{6,5},{7,4},{8,11},{9,10},{10,... | collective-permute-start | bytes 110600 | tf_op jit(solution)/shard_map/ppermute | solution.py:459
  116.9 0.0 collective-permute-done.12.refs_6_
  116.9 0.0 collective-permute-done.13.refs_7_
  116.9 0.0 collective-permute-done.7.refs_1_
  116.9 0.0 collective-permute-done.8.refs_2_
  117.0 1.9 %collective-permute-done.9.refs_3_ = bf16[144,128]{1,0:T(8,128)(2,1)S(1)} collective-permute-done((bf16[144,128]{1,0:T(8,128)(2,1)S(1)}, bf16[144,128]{1,0:T(8,128)(2,1)S(1)}, u32[]{:S(2)}, u32[]{:S(2)}) %collective-permute-start.9) | collective-permute-done | bytes 36896 | tf_op jit(solution)/shard_map/ppermute | solution.py:459
  118.8 0.1 shard_map.116.refs_0_
  118.9 0.6 collective-permute-start.14
  119.5 6.1 %collective-permute-done.14.refs_1_ = bf16[336,128]{1,0:T(8,128)(2,1)S(1)} collective-permute-done((bf16[336,128]{1,0:T(8,128)(2,1)S(1)}, bf16[336,128]{1,0:T(8,128)(2,1)S(1)}, u32[]{:S(2)}, u32[]{:S(2)}) %collective-permute-start.14) | collective-permute-done | bytes 86048 | tf_op jit(solution)/shard_map/ppermute | solution.py:464
  125.6 2.0 %collective-permute-start.15 = (bf16[336,128]{1,0:T(8,128)(2,1)S(1)}, bf16[336,128]{1,0:T(8,128)(2,1)S(1)}, u32[]{:S(2)}, u32[]{:S(2)}) collective-permute-start(bf16[336,128]{1,0:T(8,128)(2,1)S(1)} %shard_map.117.refs_0_), channel_id=1, source_target_pairs={{0,16},{8,24},{16,0},{24,8},{1,17},{9,25},{17,1},{25,9},{2,18},{10... | collective-permute-start | bytes 258056 | tf_op jit(solution)/shard_map/ppermute | solution.py:464
  127.6 4.3 %shard_map.118 = bf16[32,120,128]{2,1,0:T(8,128)(2,1)} custom-call(bf16[9,128,128]{2,1,0:T(8,128)(2,1)S(1)} %copy-done.1, bf16[32,120,128]{2,1,0:T(8,128)(2,1)S(1)} %all-to-all-done.1.got_ref, bf16[28,32,120,128]{3,2,1,0:T(8,128)(2,1)} %shard_map.111.slope_hbm), custom_call_target="tpu_custom_call" | custom-call | flops 1132462080 | bytes 2949120 | tf_op jit(solution)/shard_map/pallas_call | solution.py:58
  132.0 0.0 collective-permute-done.15.refs_1_
  132.0 11.1 %all-gather = bf16[2688,128]{1,0:T(8,128)(2,1)S(1)} all-gather(bf16[336,128]{1,0:T(8,128)(2,1)S(1)} %shard_map.119), channel_id=2, replica_groups=mesh['seg'=4,'grp'=8] {'grp'}, dimensions={0}, use_global_device_ids=true | all-gather | bytes 774144 | tf_op jit(solution)/shard_map/all_gather | solution.py:653
  143.1 1.4 shard_map.120
  (19 shorter events, 0.1 us)
Async XLA Ops:
  0.6 58.2 %copy-start.7 = (bf16[2,128,128]{2,1,0:T(8,128)(2,1)S(1)}, bf16[2,128,128]{2,1,0:T(8,128)(2,1)}, u32[]{:S(2)}) copy-start(bf16[2,128,128]{2,1,0:T(8,128)(2,1)} %uw_hbm.1) | copy-start | bytes 196612
  0.6 58.2 %copy-start.5 = (s32[4]{0:T(128)S(1)}, s32[4]{0:T(128)}, u32[]{:S(2)}) copy-start(s32[4]{0:T(128)} %key_ref.3) | copy-start | bytes 52
  0.7 58.2 %copy-start.4 = (s32[2]{0:T(128)S(1)}, s32[2]{0:T(128)}, u32[]{:S(2)}) copy-start(s32[2]{0:T(128)} %dil_ref.3) | copy-start | bytes 28
  0.7 58.2 %copy-start.6 = (bf16[2,5,128,128]{3,2,1,0:T(8,128)(2,1)S(1)}, bf16[2,5,128,128]{3,2,1,0:T(8,128)(2,1)}, u32[]{:S(2)}) copy-start(bf16[2,5,128,128]{3,2,1,0:T(8,128)(2,1)} %tw_hbm.1) | copy-start | bytes 983044
  5.5 53.4 %all-to-all-start = ((bf16[32,2,120,128]{3,2,1,0:T(8,128)(2,1)}), bf16[32,2,120,128]{3,2,1,0:T(8,128)(2,1)S(1)}, u32[]{:S(2)}, u32[]{:S(2)}) async-start(bf16[32,2,120,128]{3,2,1,0:T(8,128)(2,1)} %shard_map.110), calls=%async_computation | async-start | bytes 3932160 | tf_op jit(solution)/shard_map/all_to_all | solution.py:454
  69.7 28.8 %all-to-all-start.1 = ((bf16[32,120,128]{2,1,0:T(8,128)(2,1)}), bf16[32,120,128]{2,1,0:T(8,128)(2,1)S(1)}, u32[]{:S(2)}, u32[]{:S(2)}) async-start(bf16[32,120,128]{2,1,0:T(8,128)(2,1)} %get-tuple-element.52), calls=%async_computation.1 | async-start | bytes 1966080 | tf_op jit(solution)/shard_map/all_to_all | solution.py:454
  74.5 27.6 %copy-start = (bf16[1,32,120,128]{3,2,1,0:T(8,128)(2,1)S(1)}, bf16[1,32,120,128]{3,2,1,0:T(8,128)(2,1)}, u32[]{:S(2)}) copy-start(bf16[1,32,120,128]{3,2,1,0:T(8,128)(2,1)} %param.7) | copy-start | bytes 2949124
  74.5 27.6 %copy-start.3 = (s32[2]{0:T(128)S(1)}, s32[2]{0:T(128)}, u32[]{:S(2)}) copy-start(s32[2]{0:T(128)} %pad_add_fusion.here_ref) | copy-start | bytes 28
  84.3 43.3 %copy-start.1 = (bf16[9,128,128]{2,1,0:T(8,128)(2,1)S(1)}, bf16[9,128,128]{2,1,0:T(8,128)(2,1)}, u32[]{:S(2)}) copy-start(bf16[9,128,128]{2,1,0:T(8,128)(2,1)} %w_ref.3) | copy-start | bytes 884740
  84.3 3.6 %collective-permute-start = (bf16[192,128]{1,0:T(8,128)(2,1)}, bf16[192,128]{1,0:T(8,128)(2,1)S(1)}, u32[]{:S(2)}, u32[]{:S(2)}) collective-permute-start(bf16[192,128]{1,0:T(8,128)(2,1)} %get-tuple-element.45), channel_id=1, source_target_pairs={{0,1},{1,0},{2,3},{3,2},{4,5},{5,4},{6,7},{7,6},{8,9},{9,8},{10,11... | collective-permute-start | bytes 147464 | tf_op jit(solution)/shard_map/ppermute | solution.py:459
  84.4 6.1 %collective-permute-start.1 = (bf16[192,128]{1,0:T(8,128)(2,1)}, bf16[192,128]{1,0:T(8,128)(2,1)S(1)}, u32[]{:S(2)}, u32[]{:S(2)}) collective-permute-start(bf16[192,128]{1,0:T(8,128)(2,1)} %get-tuple-element.46), channel_id=1, source_target_pairs={{0,2},{1,3},{2,0},{3,1},{4,6},{5,7},{6,4},{7,5},{8,10},{9,11},{10,... | collective-permute-start | bytes 147464 | tf_op jit(solution)/shard_map/ppermute | solution.py:459
  86.1 4.9 %collective-permute-start.2 = (bf16[192,128]{1,0:T(8,128)(2,1)}, bf16[192,128]{1,0:T(8,128)(2,1)S(1)}, u32[]{:S(2)}, u32[]{:S(2)}) collective-permute-start(bf16[192,128]{1,0:T(8,128)(2,1)} %get-tuple-element.47), channel_id=1, source_target_pairs={{0,3},{1,2},{2,1},{3,0},{4,7},{5,6},{6,5},{7,4},{8,11},{9,10},{10,... | collective-permute-start | bytes 147464 | tf_op jit(solution)/shard_map/ppermute | solution.py:459
  86.3 4.7 %collective-permute-start.3 = (bf16[192,128]{1,0:T(8,128)(2,1)}, bf16[192,128]{1,0:T(8,128)(2,1)S(1)}, u32[]{:S(2)}, u32[]{:S(2)}) collective-permute-start(bf16[192,128]{1,0:T(8,128)(2,1)} %get-tuple-element.48), channel_id=1, source_target_pairs={{0,4},{1,5},{2,6},{3,7},{4,0},{5,1},{6,2},{7,3},{8,12},{9,13},{10,... | collective-permute-start | bytes 147464 | tf_op jit(solution)/shard_map/ppermute | solution.py:459
  87.8 5.6 %collective-permute-start.4 = (bf16[192,128]{1,0:T(8,128)(2,1)}, bf16[192,128]{1,0:T(8,128)(2,1)S(1)}, u32[]{:S(2)}, u32[]{:S(2)}) collective-permute-start(bf16[192,128]{1,0:T(8,128)(2,1)} %get-tuple-element.49), channel_id=1, source_target_pairs={{0,5},{1,4},{2,7},{3,6},{4,1},{5,0},{6,3},{7,2},{8,13},{9,12},{10,... | collective-permute-start | bytes 147464 | tf_op jit(solution)/shard_map/ppermute | solution.py:459
  88.0 5.4 %collective-permute-start.5 = (bf16[192,128]{1,0:T(8,128)(2,1)}, bf16[192,128]{1,0:T(8,128)(2,1)S(1)}, u32[]{:S(2)}, u32[]{:S(2)}) collective-permute-start(bf16[192,128]{1,0:T(8,128)(2,1)} %get-tuple-element.50), channel_id=1, source_target_pairs={{0,6},{1,7},{2,4},{3,5},{4,2},{5,3},{6,0},{7,1},{8,14},{9,15},{10,... | collective-permute-start | bytes 147464 | tf_op jit(solution)/shard_map/ppermute | solution.py:459
  90.5 5.3 %collective-permute-start.6 = (bf16[192,128]{1,0:T(8,128)(2,1)}, bf16[192,128]{1,0:T(8,128)(2,1)S(1)}, u32[]{:S(2)}, u32[]{:S(2)}) collective-permute-start(bf16[192,128]{1,0:T(8,128)(2,1)} %get-tuple-element.51), channel_id=1, source_target_pairs={{0,7},{1,6},{2,5},{3,4},{4,3},{5,2},{6,1},{7,0},{8,15},{9,14},{10,... | collective-permute-start | bytes 147464 | tf_op jit(solution)/shard_map/ppermute | solution.py:459
  95.8 0.8 copy-start.2
  98.5 44.6 %all-to-all-start.2 = ((bf16[32,120,128]{2,1,0:T(8,128)(2,1)}), bf16[32,120,128]{2,1,0:T(8,128)(2,1)S(1)}, u32[]{:S(2)}, u32[]{:S(2)}) async-start(bf16[32,120,128]{2,1,0:T(8,128)(2,1)} %get-tuple-element.67), calls=%async_computation.2 | async-start | bytes 1966080 | tf_op jit(solution)/shard_map/all_to_all | solution.py:454
  105.8 5.0 %collective-permute-start.10 = (bf16[144,128]{1,0:T(8,128)(2,1)S(1)}, bf16[144,128]{1,0:T(8,128)(2,1)S(1)}, u32[]{:S(2)}, u32[]{:S(2)}) collective-permute-start(bf16[144,128]{1,0:T(8,128)(2,1)S(1)} %get-tuple-element.62), channel_id=1, source_target_pairs={{0,4},{1,5},{2,6},{3,7},{4,0},{5,1},{6,2},{7,3},{8,12},{9,13},{10,... | collective-permute-start | bytes 110600 | tf_op jit(solution)/shard_map/ppermute | solution.py:459
  107.6 7.2 %collective-permute-start.11 = (bf16[144,128]{1,0:T(8,128)(2,1)S(1)}, bf16[144,128]{1,0:T(8,128)(2,1)S(1)}, u32[]{:S(2)}, u32[]{:S(2)}) collective-permute-start(bf16[144,128]{1,0:T(8,128)(2,1)S(1)} %get-tuple-element.63), channel_id=1, source_target_pairs={{0,5},{1,4},{2,7},{3,6},{4,1},{5,0},{6,3},{7,2},{8,13},{9,12},{10,... | collective-permute-start | bytes 110600 | tf_op jit(solution)/shard_map/ppermute | solution.py:459
  107.6 9.3 %collective-permute-start.12 = (bf16[144,128]{1,0:T(8,128)(2,1)S(1)}, bf16[144,128]{1,0:T(8,128)(2,1)S(1)}, u32[]{:S(2)}, u32[]{:S(2)}) collective-permute-start(bf16[144,128]{1,0:T(8,128)(2,1)S(1)} %get-tuple-element.64), channel_id=1, source_target_pairs={{0,6},{1,7},{2,4},{3,5},{4,2},{5,3},{6,0},{7,1},{8,14},{9,15},{10,... | collective-permute-start | bytes 110600 | tf_op jit(solution)/shard_map/ppermute | solution.py:459
  110.0 6.9 %collective-permute-start.13 = (bf16[144,128]{1,0:T(8,128)(2,1)S(1)}, bf16[144,128]{1,0:T(8,128)(2,1)S(1)}, u32[]{:S(2)}, u32[]{:S(2)}) collective-permute-start(bf16[144,128]{1,0:T(8,128)(2,1)S(1)} %get-tuple-element.65), channel_id=1, source_target_pairs={{0,7},{1,6},{2,5},{3,4},{4,3},{5,2},{6,1},{7,0},{8,15},{9,14},{10,... | collective-permute-start | bytes 110600 | tf_op jit(solution)/shard_map/ppermute | solution.py:459
  110.3 6.6 %collective-permute-start.7 = (bf16[144,128]{1,0:T(8,128)(2,1)S(1)}, bf16[144,128]{1,0:T(8,128)(2,1)S(1)}, u32[]{:S(2)}, u32[]{:S(2)}) collective-permute-start(bf16[144,128]{1,0:T(8,128)(2,1)S(1)} %get-tuple-element.59), channel_id=1, source_target_pairs={{0,1},{1,0},{2,3},{3,2},{4,5},{5,4},{6,7},{7,6},{8,9},{9,8},{10,11... | collective-permute-start | bytes 110600 | tf_op jit(solution)/shard_map/ppermute | solution.py:459
  110.8 6.1 %collective-permute-start.8 = (bf16[144,128]{1,0:T(8,128)(2,1)S(1)}, bf16[144,128]{1,0:T(8,128)(2,1)S(1)}, u32[]{:S(2)}, u32[]{:S(2)}) collective-permute-start(bf16[144,128]{1,0:T(8,128)(2,1)S(1)} %get-tuple-element.60), channel_id=1, source_target_pairs={{0,2},{1,3},{2,0},{3,1},{4,6},{5,7},{6,4},{7,5},{8,10},{9,11},{10,... | collective-permute-start | bytes 110600 | tf_op jit(solution)/shard_map/ppermute | solution.py:459
  114.8 4.0 %collective-permute-start.9 = (bf16[144,128]{1,0:T(8,128)(2,1)S(1)}, bf16[144,128]{1,0:T(8,128)(2,1)S(1)}, u32[]{:S(2)}, u32[]{:S(2)}) collective-permute-start(bf16[144,128]{1,0:T(8,128)(2,1)S(1)} %get-tuple-element.61), channel_id=1, source_target_pairs={{0,3},{1,2},{2,1},{3,0},{4,7},{5,6},{6,5},{7,4},{8,11},{9,10},{10,... | collective-permute-start | bytes 110600 | tf_op jit(solution)/shard_map/ppermute | solution.py:459
  118.9 6.7 %collective-permute-start.14 = (bf16[336,128]{1,0:T(8,128)(2,1)S(1)}, bf16[336,128]{1,0:T(8,128)(2,1)S(1)}, u32[]{:S(2)}, u32[]{:S(2)}) collective-permute-start(bf16[336,128]{1,0:T(8,128)(2,1)S(1)} %shard_map.116.refs_0_), channel_id=1, source_target_pairs={{0,8},{8,0},{16,24},{24,16},{1,9},{9,1},{17,25},{25,17},{2,10},{10... | collective-permute-start | bytes 258056 | tf_op jit(solution)/shard_map/ppermute | solution.py:464
  125.6 6.4 %collective-permute-start.15 = (bf16[336,128]{1,0:T(8,128)(2,1)S(1)}, bf16[336,128]{1,0:T(8,128)(2,1)S(1)}, u32[]{:S(2)}, u32[]{:S(2)}) collective-permute-start(bf16[336,128]{1,0:T(8,128)(2,1)S(1)} %shard_map.117.refs_0_), channel_id=1, source_target_pairs={{0,16},{8,24},{16,0},{24,8},{1,17},{9,25},{17,1},{25,9},{2,18},{10... | collective-permute-start | bytes 258056 | tf_op jit(solution)/shard_map/ppermute | solution.py:464
